TPU v7x, 32 devices: a whole 2x2x4 slice. The times are simulated.
32 devices in a mesh: seg: 8 (over y, x, core), fsdp: 4 (over z).
Axes of the slice: x: 2, y: 2, z: 4, core: 2. Of those that a mesh axis runs over, the one named last changes fastest.
Arguments:
- tokens: bfloat16 [4, 2048, 4096], P('fsdp', 'seg')
- w_query: bfloat16 [4096, 2048], P(('seg', 'fsdp'))
- w_key: bfloat16 [4096, 512], P(('seg', 'fsdp'))
- value_weight: bfloat16 [4096, 512], P(('seg', 'fsdp')), may hold values from -0.09375 to 0.09375
- gate_bias: float32 [16], replicated, may hold values from -2 to 2
- block_mask: int32 [4, 8, 2, 2], P('fsdp', 'seg'), may hold values from 0 to 1, as said below
- valid_len: int32 [4, 8], P('fsdp', 'seg'), may hold values from 1 to 256, as said below
Outputs:
- attended: bfloat16 [4, 2048, 2048], P('fsdp', 'seg')
Inputs may be any that keep to these rules, and one draw needn't show every extreme that they name: block_mask[b, s] is 1 on its diagonal, 0 above it, and 0 or 1 below it. `valid_len`: the first segment of every book is full.
All inputs are finite; a program needn't handle non-finite values.
Results may differ from a plain program's by a relative error of at most 0.0095.
Values may be sent and summed in bfloat16 or wider, within the bound.
No kernel may reach another device: no remote copies, remote signals or barrier semaphores. Data moves between devices by JAX's collectives and lax.ppermute only.
A program may use at most 128 MiB of HBM per device.

v0:
```python
import jax
import jax.numpy as jnp
from jax import lax
from jax.sharding import PartitionSpec as P

HEAD_SIZE = 128
BLK = 128


def carried_in(array, axis, combine, identity):
    length, here = (lax.axis_size(axis), lax.axis_index(axis))
    everything = jax.tree.map(
        lambda part, kind: lax.all_gather(part.astype(kind), axis),
        array,
        (jnp.bfloat16, jnp.bfloat16),
    )
    start = jax.tree.map(
        lambda part, zero: jnp.broadcast_to(jnp.asarray(zero, part.dtype), part.shape),
        array,
        identity,
    )

    def lap(k, before):
        reached = k < here
        new = combine(
            before, jax.tree.map(lambda part, own: part[k].astype(own.dtype), everything, array)
        )
        return jax.tree.map(lambda a, b: jnp.where(reached, a, b), new, before)

    return lax.fori_loop(0, length, lap, start)


def sigma_plus(values):
    return jax.nn.elu(values) + 1.0


def segment_delta(keys, values, valid):
    length = keys.shape[0]
    heads_kv = keys.shape[1] // HEAD_SIZE
    live = (jnp.arange(length, dtype=jnp.int32) < valid)[:, None, None]
    sig_keys = jnp.where(
        live, sigma_plus(keys.reshape(length, heads_kv, HEAD_SIZE).astype(jnp.float32)), 0.0
    )
    delta_m = jnp.einsum(
        "jgd,jge->gde",
        sig_keys,
        values.reshape(length, heads_kv, HEAD_SIZE).astype(jnp.float32),
        precision=lax.Precision.HIGHEST,
    )
    delta_z = jnp.sum(sig_keys, axis=0)
    return (delta_m, delta_z)


def memory_before(keys, values, valid):
    delta_m, delta_z = segment_delta(keys, values, valid)

    def combine(earlier, later):
        return (earlier[0] + later[0], earlier[1] + later[1])

    identity = (jnp.zeros_like(delta_m), jnp.zeros_like(delta_z))
    memory, normalizer = carried_in((delta_m, delta_z), "seg", combine, identity)
    return (memory, normalizer)


def segment_output(queries, keys, values, gate_bias, mask_blocks, valid, memory, normalizer):
    length = queries.shape[0]
    heads_kv = memory.shape[0]
    group = queries.shape[1] // (heads_kv * HEAD_SIZE)
    nblocks = mask_blocks.shape[0]
    q_heads = queries.reshape(length, heads_kv, group, HEAD_SIZE)
    k_heads = keys.reshape(length, heads_kv, HEAD_SIZE)
    v_heads = values.reshape(length, heads_kv, HEAD_SIZE)
    scores = jnp.einsum(
        "igxd,jgd->gxij", q_heads, k_heads, preferred_element_type=jnp.float32
    ) * HEAD_SIZE ** (-0.5)
    full = jnp.broadcast_to(mask_blocks[:, None, :, None], (nblocks, BLK, nblocks, BLK)).reshape(
        length, length
    )
    pos = jnp.arange(length, dtype=jnp.int32)
    allowed = (full > 0) & (pos[None, :] <= pos[:, None]) & (pos[None, :] < valid)
    masked = jnp.where(allowed, scores, -1e30)
    top = jnp.max(masked, axis=-1, keepdims=True)
    expo = jnp.where(allowed, jnp.exp(masked - top), 0.0)
    total = jnp.maximum(jnp.sum(expo, axis=-1, keepdims=True), 1.0)
    weights = (expo / total).astype(jnp.bfloat16)
    local = jnp.einsum("gxij,jgd->igxd", weights, v_heads, preferred_element_type=jnp.float32)
    sig_q = sigma_plus(q_heads.astype(jnp.float32))
    numer = jnp.einsum("igxd,gde->igxe", sig_q, memory, precision=lax.Precision.HIGHEST)
    denom = jnp.einsum("igxd,gd->igx", sig_q, normalizer, precision=lax.Precision.HIGHEST) + 1.0
    gate = jax.nn.sigmoid(gate_bias).reshape(heads_kv, group)[None, :, :, None]
    mixed = gate * (numer / denom[..., None]) + (1.0 - gate) * local
    live = (pos < valid)[:, None, None, None]
    return jnp.where(live, mixed, 0.0).reshape(length, -1).astype(jnp.bfloat16)


def shards(tokens, w_query, w_key, value_weight, gate_bias, block_mask, valid_len):
    seg_tokens = tokens[0]
    mask_blocks = block_mask[0, 0]
    valid = valid_len[0, 0]

    def add_rows(piece):
        return jnp.dot(seg_tokens, piece, preferred_element_type=jnp.float32)

    q_sum = add_rows(lax.all_gather(w_query, ("seg", "fsdp"), axis=0, tiled=True))
    k_sum = add_rows(lax.all_gather(w_key, ("seg", "fsdp"), axis=0, tiled=True))
    v_sum = add_rows(lax.all_gather(value_weight, ("seg", "fsdp"), axis=0, tiled=True))
    keys = k_sum.astype(jnp.bfloat16)
    values = v_sum.astype(jnp.bfloat16)
    queries = q_sum.astype(jnp.bfloat16)
    memory, normalizer = memory_before(keys, values, valid)
    output = segment_output(
        queries, keys, values, gate_bias, mask_blocks, valid, memory, normalizer
    )
    return output[None]


def solution(mesh):
    in_specs = (
        P("fsdp", "seg", None),
        P(("seg", "fsdp"), None),
        P(("seg", "fsdp"), None),
        P(("seg", "fsdp"), None),
        P(),
        P("fsdp", "seg", None, None),
        P("fsdp", "seg"),
    )
    out_specs = P("fsdp", "seg", None)
    return jax.shard_map(shards, mesh=mesh, in_specs=in_specs, out_specs=out_specs, check_vma=False)
```

profile of v0, /device:TPU:9, one launch (start us, length us, event | category | flops | bytes accessed | tf_op | source)
XLA Modules:
  0.0 319.9 jit_solution(5439529996035667825)
XLA Ops:
  6.5 0.0 copy-start
  6.5 0.0 all-gather.6.cloned.1.call-start
  6.5 0.7 all-gather.6.cloned.1.call-update
  7.3 0.0 all-gather.8.cloned.1.call-start
  7.3 0.7 all-gather.8.cloned.1.call-update
  8.0 0.0 all-gather.12.cloned.1.call-start
  8.7 65.3 %all-gather.6.cloned.1.call-done = bf16[4096,512]{1,0:T(8,128)(2,1)} async-done(((bf16[128,512]{1,0:T(8,128)(2,1)}), bf16[4096,512]{1,0:T(8,128)(2,1)}) %all-gather.6.cloned.1.call-update) | async-done | bytes 4194320 | tf_op jit(solution)/shard_map/all_gather | solution.py:105
  74.0 0.0 copy-done
  74.0 3.6 %fusion.42 = (bf16[512]{0:T(512)(128)(2,1)S(1)}, bf16[256,512]{1,0:T(8,128)(2,1)S(1)}) fusion(pred[256]{0:T(512)(128)(4,1)S(1)} %iota_compare_fusion.1, bf16[4096,512]{1,0:T(8,128)(2,1)} %all-gather.6.cloned.1.call-done, bf16[1,256,4096]{2,1,0:T(8,128)(2,1)S(1)} %copy-done), kind=kOutput, calls=%fused_computation.46 | convolution fusion | flops 1074789888 | bytes 6554880 | tf_op jit(solution)/shard_map/dot_general | solution.py:102
  77.7 0.1 reshape.73
  77.7 0.0 copy-start.1
  77.7 0.2 copy.30
  77.9 59.8 %all-gather.8.cloned.1.call-done = bf16[4096,512]{1,0:T(8,128)(2,1)} async-done(((bf16[128,512]{1,0:T(8,128)(2,1)}), bf16[4096,512]{1,0:T(8,128)(2,1)}) %all-gather.8.cloned.1.call-update) | async-done | bytes 4194320 | tf_op jit(solution)/shard_map/all_gather | solution.py:106
  137.7 3.4 %fusion.28 = bf16[256,512]{1,0:T(8,128)(2,1)S(1)} fusion(bf16[4096,512]{1,0:T(8,128)(2,1)} %all-gather.8.cloned.1.call-done, bf16[1,256,4096]{2,1,0:T(8,128)(2,1)S(1)} %copy-done), kind=kOutput, calls=%fused_computation.34 | convolution fusion | flops 1073872896 | bytes 6553600 | tf_op jit(solution)/shard_map/dot_general | solution.py:102
  141.1 0.0 copy-done.1
  141.1 0.0 copy-start.3
  141.1 0.0 copy-start.2
  141.1 1.3 convolution_convert_fusion.1
  142.4 0.0 all-gather.12.cloned.1.call-update
  142.4 0.0 all-gather.10.cloned.1.call-start
  142.5 0.5 all-gather.10.cloned.1.call-update
  143.0 0.0 copy-done.3
  143.1 0.1 mul.30
  143.1 0.0 copy-done.2
  143.2 0.1 broadcast_in_dim.65
  143.3 0.1 fusion.52
  143.4 0.2 copy.35
  143.6 0.8 reshape.74
  144.3 9.1 %all_gather.23 = bf16[8,4,128]{2,1,0:T(4,128)(2,1)S(1)} all-gather(bf16[1,4,128]{2,1,0:T(4,128)(2,1)S(1)} %bitcast.97), channel_id=1, replica_groups=mesh['seg'=8,'fsdp'=4] {'seg'}, dimensions={0}, use_global_device_ids=true | all-gather | bytes 9216 | tf_op jit(solution)/shard_map/all_gather | solution.py:13
  153.4 11.3 %all-gather.12.cloned.1.call-done = bf16[32,128,128]{2,1,0:T(8,128)(2,1)} async-done(((bf16[4,128,128]{2,1,0:T(8,128)(2,1)}), bf16[32,128,128]{2,1,0:T(8,128)(2,1)}) %all-gather.12.cloned.1.call-update) | async-done | bytes 1048592 | tf_op jit(solution)/shard_map/all_gather | solution.py:13
  164.7 8.6 %while.16 = (s32[]{:T(128)}, f32[4,128,128]{2,1,0:T(8,128)S(1)}, f32[4,128]{1,0:T(4,128)S(1)}, s32[]{:T(128)}, bf16[8,4,128,128]{3,2,1,0:T(8,128)(2,1)}, /*index...) while((s32[]{:T(128)}, f32[4,128,128]{2,1,0:T(8,128)S(1)}, f32[4,128]{1,0:T(4,128)S(1)}, ...), condition=%wide.region_2.3_spmd.clone, body=%wide.region_1.2_spmd.clone.sunk | while | flops 264196 | bytes 660603 | solution.py:30
  164.7 1.0 add_select_fusion.4
  165.8 1.0 add_select_fusion.4
  166.9 1.0 add_select_fusion.4
  167.9 1.0 add_select_fusion.4
  169.0 1.0 add_select_fusion.4
  170.1 1.0 add_select_fusion.4
  171.2 1.0 add_select_fusion.4
  172.3 1.0 add_select_fusion.4
  173.3 108.0 %all-gather.10.cloned.1.call-done = bf16[4096,2048]{1,0:T(8,128)(2,1)} async-done(((bf16[128,2048]{1,0:T(8,128)(2,1)}), bf16[4096,2048]{1,0:T(8,128)(2,1)}) %all-gather.10.cloned.1.call-update) | async-done | bytes 16777232 | tf_op jit(solution)/shard_map/all_gather | solution.py:104
  281.4 9.2 %convolution_convert_fusion = bf16[256,2048]{1,0:T(8,128)(2,1)} fusion(bf16[4096,2048]{1,0:T(8,128)(2,1)} %all-gather.10.cloned.1.call-done, bf16[1,256,4096]{2,1,0:T(8,128)(2,1)S(1)} %copy-done), kind=kOutput, calls=%fused_computation.9 | convolution fusion | flops 4295491584 | bytes 19922944 | tf_op jit(solution)/shard_map/dot_general | solution.py:102
  290.6 1.5 copy.54
  292.0 5.2 %fusion.20 = f32[4,1,256,4]{1,2,3,0:T(8,128)} fusion(f32[4,128,1,1]{1,2,3,0:T(1,128)S(1)} %bitcast.96, bf16[256,4,4,128]{0,3,2,1:T(8,128)(2,1)S(1)} %bitcast.88), kind=kOutput, calls=%fused_computation.32 | convolution fusion | flops 8916992 | bytes 1067008 | tf_op jit(solution)/shard_map/igxd,gd->igx/dot_general | solution.py:89
  297.3 2.2 copy.57
  299.5 4.7 %fusion.69 = (f32[4,4,256]{2,1,0:T(4,128)S(1)}, f32[4,4,256,256]{2,3,1,0:T(8,128)}) fusion(pred[256,256]{0,1:T(8,128)(4,1)S(1)} %copy.35, bf16[256,4,4,128]{0,3,2,1:T(8,128)(2,1)S(1)} %bitcast.89, bf16[256,4,128,1]{2,1,0,3:T(4,128)(2,1)} %bitcast.92), kind=kOutput, calls=%fused_computation.76 | convolution fusion | flops 273678592 | bytes 5586944 | tf_op jit(solution)/shard_map/sub | solution.py:83
  304.2 2.8 fusion.14
  307.0 4.1 %fusion.5 = bf16[256,4,4,128]{0,3,2,1:T(8,128)(2,1)} fusion(f32[4,128,4,256]{3,1,2,0:T(8,128)S(1)} %fusion.14, bf16[256,4,4,128]{0,3,2,1:T(8,128)(2,1)S(1)} %bitcast.90, f32[4,4]{1,0:T(4,128)S(1)} %broadcast_subtract_fusion, f32[256,4,4]{0,2,1:T(4,128)S(1)} %bitcast_bitcast_fusion, f32[4,4]{1,0:T(4,128)S(1)} %mul.30, ...), kind=kOutput, calls=%fused_computation.14 | convolution fusion | flops 811073536 | bytes 4473216 | tf_op jit(solution)/shard_map/igxd,gde->igxe/dot_general | solution.py:88
  311.1 2.3 copy.40
  (16 shorter events, 0.2 us)
Async XLA Ops:
  6.5 67.5 %copy-start = (bf16[1,256,4096]{2,1,0:T(8,128)(2,1)S(1)}, bf16[1,256,4096]{2,1,0:T(8,128)(2,1)}, u32[]{:S(2)}) copy-start(bf16[1,256,4096]{2,1,0:T(8,128)(2,1)} %param.9) | copy-start | bytes 6291460
  6.5 67.5 %all-gather.6.cloned.1.call-start = ((), (), s32[]{:S(2)}) async-start(), calls=%async_computation | async-start | bytes 4325376 | tf_op jit(solution)/shard_map/all_gather | solution.py:105
  7.3 130.4 %all-gather.8.cloned.1.call-start = ((), (), s32[]{:S(2)}) async-start(), calls=%async_computation.1 | async-start | bytes 4325376 | tf_op jit(solution)/shard_map/all_gather | solution.py:106
  8.0 156.7 %all-gather.12.cloned.1.call-start = ((), (), s32[]{:S(2)}) async-start(), calls=%async_computation.3 | async-start | bytes 1179648 | tf_op jit(solution)/shard_map/all_gather | solution.py:13
  77.7 63.4 %copy-start.1 = (bf16[256,4,128]{2,1,0:T(4,128)(2,1)}, bf16[256,4,128]{2,1,0:T(4,128)(2,1)S(1)}, u32[]{:S(2)}) copy-start(bf16[256,4,128]{2,1,0:T(4,128)(2,1)S(1)} %reshape.73) | copy-start | bytes 786436
  141.1 1.9 copy-start.3
  141.1 2.0 copy-start.2
  142.4 138.9 %all-gather.10.cloned.1.call-start = ((), (), s32[]{:S(2)}) async-start(), calls=%async_computation.2 | async-start | bytes 17301504 | tf_op jit(solution)/shard_map/all_gather | solution.py:104
Sparse Core Ops, SparseCore 0:
  10.4 63.6 all-gather.5
  77.0 60.6 all-gather.7
  142.6 22.0 all-gather.11
  167.5 113.7 all-gather.9
where the time goes:
time: 323 us; the launch traced here: 320 us
  waiting for transfers between devices  246 us (76%)
  matrix products  34.3 us (11%)
  between operations  13.9 us (4%)
  blocking collectives  9.07 us (3%)
  other arithmetic  8.53 us (3%)
  local copies, waits for them, and re-layouts  7.38 us (2%)
    all_gather x1, waiting for transfers between devices, shards(): lax.all_gather(w_query, ('seg', 'fsdp'), axis=0, tiled=True)  108 us
    all_gather x1, waiting for transfers between devices, shards(): k_sum = add_rows(lax.all_gather(w_key, ('seg', 'fsdp'), axis=0, tiled=True))  65.3 us
    all_gather x1, waiting for transfers between devices, shards(): lax.all_gather(value_weight, ('seg', 'fsdp'), axis=0, tiled=True)  59.8 us
    dot_general x3, matrix products, add_rows(): return jnp.dot(seg_tokens, piece, preferred_element_type=jnp.float32)  16.3 us
    all_gather x1, waiting for transfers between devices, carried_in(): lax.all_gather(part.astype(kind), axis)  11.3 us
    all_gather x1, blocking collectives, carried_in(): lax.all_gather(part.astype(kind), axis)  9.07 us
    select_n x16, other arithmetic, lap(): return jax.tree.map(lambda a, b: jnp.where(reached, a, b), new, before)  8.44 us
  transfers between devices with their start and end apart: 4, of which 4 were waited for; matrix products, arithmetic and copies ran while one was open for 4% of the time, Pallas kernels for 0%

commit v1 on v0

v1 whole, which is shorter than its diff:
```python
import functools

import jax
import jax.numpy as jnp
from jax import lax
from jax.experimental import pallas as pl
from jax.experimental.pallas import tpu as pltpu
from jax.sharding import PartitionSpec as P

HEAD_SIZE = 128
BLK = 128
MEMBERS = 4
META_ROWS = 16
AXES = ("seg", "fsdp")

VMEM = pl.BlockSpec(memory_space=pltpu.VMEM)
SMEM = pl.BlockSpec(memory_space=pltpu.SMEM)


def call(body, outs, n_smem, n_vmem, flops=0, scratch=(), limit=48 << 20):
    return pl.pallas_call(
        body,
        out_shape=outs,
        in_specs=[SMEM] * n_smem + [VMEM] * n_vmem,
        out_specs=[VMEM] * len(outs),
        scratch_shapes=list(scratch),
        compiler_params=pltpu.CompilerParams(vmem_limit_bytes=limit),
        cost_estimate=pl.CostEstimate(flops=flops, bytes_accessed=8 << 20, transcendentals=0),
    )


def aligned(offset):
    return pl.multiple_of(offset, HEAD_SIZE)


def pack_body(group, here_ref, meta_ref, wq_ref, wk_ref, wv_ref, *outs):
    rows = wk_ref.shape[0]
    half = group * HEAD_SIZE // 2
    lane = lax.broadcasted_iota(jnp.int32, (META_ROWS, 2 * HEAD_SIZE), 1)
    facts = jnp.zeros((META_ROWS, 2 * HEAD_SIZE), jnp.float32)
    for place in range(5):
        facts = jnp.where(lane == place, meta_ref[place].astype(jnp.float32), facts)
    for k in range(MEMBERS):
        head = here_ref[0] ^ k
        kv, q0, q1 = outs[3 * k : 3 * k + 3]
        at = aligned(head * HEAD_SIZE)
        kv[0:rows, 0:HEAD_SIZE] = wk_ref[:, pl.ds(at, HEAD_SIZE)]
        kv[0:rows, HEAD_SIZE:] = wv_ref[:, pl.ds(at, HEAD_SIZE)]
        kv[rows:, :] = facts.astype(jnp.bfloat16)
        q0[...] = wq_ref[:, pl.ds(aligned(head * 2 * half), half)]
        q1[...] = wq_ref[:, pl.ds(aligned(head * 2 * half + half), half)]


def project(tokens_ref, pieces, offs_ref):
    total = None
    for p, piece in enumerate(pieces):
        parts = [
            tokens_ref[:, pl.ds(aligned(offs_ref[p * MEMBERS + k]), HEAD_SIZE)]
            for k in range(MEMBERS)
        ]
        term = jnp.dot(
            jnp.concatenate(parts, axis=1), piece[...], preferred_element_type=jnp.float32
        )
        total = term if total is None else total + term
    return total


def sigma_plus(v):
    return jnp.where(v > 0, v + 1.0, jnp.exp(jnp.minimum(v, 0.0)))


def kv_body(n_pieces, segs, offs_ref, meta_ref, *refs):
    tokens, pieces, outs = refs[: len(segs)], refs[len(segs) : len(segs) + n_pieces], refs[len(segs) + n_pieces :]
    for n, seg in enumerate(segs):
        kv = project(tokens[n], pieces, offs_ref).astype(jnp.bfloat16)
        outs[2 * n][...] = kv
        length = kv.shape[0]
        row = lax.broadcasted_iota(jnp.int32, (length, HEAD_SIZE), 0)
        keys = kv[:, :HEAD_SIZE].astype(jnp.float32)
        sig = jnp.where(row < meta_ref[5 * seg], sigma_plus(keys), 0.0)
        wide = jnp.concatenate(
            [kv[:, HEAD_SIZE:], jnp.ones((length, HEAD_SIZE), jnp.bfloat16)], axis=1
        )
        high = sig.astype(jnp.bfloat16)
        low = (sig - high.astype(jnp.float32)).astype(jnp.bfloat16)
        over = (((0,), (0,)), ((), ()))
        delta = lax.dot_general(high, wide, over, preferred_element_type=jnp.float32)
        delta += lax.dot_general(low, wide, over, preferred_element_type=jnp.float32)
        outs[2 * n + 1][...] = delta


def attend_body(
    n_pieces, heads, first_head, group, here_ref, offs_ref, meta_ref, gate_ref, *refs
):
    tokens = refs[:MEMBERS]
    pieces = refs[MEMBERS : MEMBERS + n_pieces]
    rest = refs[MEMBERS + n_pieces :]
    kvs, deltas, base = rest[:MEMBERS], rest[MEMBERS : 2 * MEMBERS], rest[2 * MEMBERS]
    outs = rest[2 * MEMBERS + 1 :]
    me = here_ref[0]
    for seg in range(MEMBERS):
        queries = project(tokens[seg], pieces, offs_ref).astype(jnp.bfloat16)
        length = queries.shape[0]
        stacked = jnp.concatenate(
            [queries[:, h * HEAD_SIZE : (h + 1) * HEAD_SIZE] for h in range(heads)], axis=0
        )
        rows = heads * length
        keys = kvs[seg][:, :HEAD_SIZE]
        values = kvs[seg][:, HEAD_SIZE:]
        scores = lax.dot_general(
            stacked, keys, (((1,), (1,)), ((), ())), preferred_element_type=jnp.float32
        ) * HEAD_SIZE ** (-0.5)
        i = lax.broadcasted_iota(jnp.int32, (rows, length), 0) % length
        j = lax.broadcasted_iota(jnp.int32, (rows, length), 1)
        valid = meta_ref[5 * seg]
        top_block, left_block = i < BLK, j < BLK
        seen = jnp.where(
            top_block,
            jnp.where(left_block, meta_ref[5 * seg + 1], meta_ref[5 * seg + 2]),
            jnp.where(left_block, meta_ref[5 * seg + 3], meta_ref[5 * seg + 4]),
        )
        allowed = (seen == 1) & (j <= i) & (j < valid)
        masked = jnp.where(allowed, scores, -1e30)
        top = jnp.max(masked, axis=-1, keepdims=True)
        expo = jnp.where(allowed, jnp.exp(masked - top), 0.0)
        total = jnp.maximum(jnp.sum(expo, axis=-1, keepdims=True), 1.0)
        weights = (expo / total).astype(jnp.bfloat16)
        local = jnp.dot(weights, values, preferred_element_type=jnp.float32)

        memory = base[...].astype(jnp.float32)
        for other in range(MEMBERS):
            earlier = jnp.where((me ^ other) < (me ^ seg), 1.0, 0.0)
            if other != seg:
                memory = memory + earlier * deltas[other][...]
        sig = sigma_plus(stacked.astype(jnp.float32))
        high = sig.astype(jnp.bfloat16)
        low = (sig - high.astype(jnp.float32)).astype(jnp.bfloat16)
        mem_high = memory.astype(jnp.bfloat16)
        mem_low = (memory - mem_high.astype(jnp.float32)).astype(jnp.bfloat16)
        numer = jnp.dot(high, mem_high, preferred_element_type=jnp.float32)
        numer += jnp.dot(high, mem_low, preferred_element_type=jnp.float32)
        numer += jnp.dot(low, mem_high, preferred_element_type=jnp.float32)
        retrieved = numer[:, :HEAD_SIZE] / (numer[:, HEAD_SIZE:] + 1.0)
        live = lax.broadcasted_iota(jnp.int32, (length, HEAD_SIZE), 0) < valid
        for h in range(heads):
            span = slice(h * length, (h + 1) * length)
            logit = jnp.full((1, HEAD_SIZE), gate_ref[me * group + first_head + h], jnp.float32)
            gate = 1.0 / (1.0 + jnp.exp(-logit))
            mixed = gate * retrieved[span] + (1.0 - gate) * local[span]
            outs[seg][:, h * HEAD_SIZE : (h + 1) * HEAD_SIZE] = jnp.where(live, mixed, 0.0).astype(
                jnp.bfloat16
            )


def assemble_body(group, here_ref, *refs):
    parts, out = refs[:-1], refs[-1]
    half = group * HEAD_SIZE // 2
    for k in range(MEMBERS):
        at = (here_ref[0] ^ k) * 2 * half
        for c in range(2):
            out[:, pl.ds(aligned(at + c * half), half)] = parts[2 * k + c][...]


def shards(sizes, tokens, w_query, w_key, value_weight, gate_bias, block_mask, valid_len):
    n_seg, n_z = sizes
    n_groups = n_seg // MEMBERS
    heads_kv = w_key.shape[1] // HEAD_SIZE
    group = w_query.shape[1] // w_key.shape[1]
    half = group * HEAD_SIZE // 2
    rows = w_query.shape[0]
    length, width = tokens.shape[1], tokens.shape[2]
    assert heads_kv == MEMBERS and group % 2 == 0
    seg = lax.axis_index("seg")
    z = lax.axis_index("fsdp")
    g, m = seg // MEMBERS, seg % MEMBERS
    here = jnp.reshape(m, (1,)).astype(jnp.int32)

    def permute(array, to):
        pairs = []
        for gg in range(n_groups):
            for mm in range(MEMBERS):
                for zz in range(n_z):
                    target = to(gg, mm, zz)
                    if target is not None:
                        index = lambda t: (t[0] * MEMBERS + t[1]) * n_z + t[2]
                        pairs.append((index((gg, mm, zz)), index(target)))
        return lax.ppermute(array, AXES, pairs)

    def to_member(array, k):
        return permute(array, lambda gg, mm, zz: (gg, mm ^ k, zz))

    bf16 = jnp.bfloat16
    shape = jax.ShapeDtypeStruct
    mine = jnp.concatenate([valid_len.reshape(1), block_mask.reshape(4)]).astype(jnp.int32)
    packed = call(
        functools.partial(pack_body, group),
        [shape((rows + META_ROWS, 2 * HEAD_SIZE), bf16), shape((rows, half), bf16), shape((rows, half), bf16)]
        * MEMBERS,
        2,
        3,
    )(here, mine, w_query, w_key, value_weight)
    received = [packed[:3]] + [
        [to_member(part, k) for part in packed[3 * k : 3 * k + 3]] for k in range(1, MEMBERS)
    ]
    meta = jnp.concatenate([part[0][rows, :5] for part in received]).astype(jnp.int32)

    own = tokens[0]
    sibling = to_member(own, 1)
    across = to_member(own, 2)
    diagonal = to_member(across, 1)
    books = [own, sibling, across, diagonal]

    def gathered(piece):
        if n_groups == 2 and n_z == 4:
            flip = lambda b: lambda gg, mm, zz: (gg, mm, zz ^ b)
            one = permute(piece, flip(1))
            two = permute(piece, flip(2))
            inner = permute(piece, lambda gg, mm, zz: (gg, mm, zz ^ 3) if zz in (1, 2) else None)
            outer = permute(two, lambda gg, mm, zz: (gg, mm, zz ^ 1) if zz in (1, 2) else None)
            three = jnp.where((z == 1) | (z == 2), inner, outer)
            line = [piece, one, two, three]
            return line + [permute(part, lambda gg, mm, zz: (gg ^ 1, mm, zz)) for part in line]
        index = lambda gg, mm, zz: (gg * MEMBERS + mm) * n_z + zz
        everything = lax.all_gather(
            piece,
            AXES,
            axis_index_groups=[
                [index(gg, mm, zz) for gg in range(n_groups) for zz in range(n_z)]
                for mm in range(MEMBERS)
            ],
        )
        columns = piece.shape[1]
        natural = everything.reshape(n_groups, n_z, MEMBERS, rows, columns)
        members = jnp.arange(MEMBERS, dtype=jnp.int32) ^ m
        natural = jnp.take(natural, members, axis=2).transpose(0, 2, 1, 3, 4)
        return list(natural.reshape(-1, MEMBERS * HEAD_SIZE, columns))

    if n_groups == 2 and n_z == 4:
        assert rows == HEAD_SIZE
        n_pieces = n_groups * n_z
        a, b, k = jnp.meshgrid(
            jnp.arange(n_groups), jnp.arange(n_z), jnp.arange(MEMBERS), indexing="ij"
        )
        offs = ((((g ^ a) * MEMBERS + (m ^ k)) * n_z + (z ^ b)) * rows).reshape(-1).astype(jnp.int32)
    else:
        n_pieces = width // (MEMBERS * HEAD_SIZE)
        offs = jnp.arange(n_pieces * MEMBERS, dtype=jnp.int32) * HEAD_SIZE

    chunks = [
        gathered(jnp.concatenate([part[c][:rows] for part in received], axis=0)) for c in range(3)
    ]

    kvs, deltas = [], []
    for segs in ((0, 1), (2, 3)):
        found = call(
            functools.partial(kv_body, n_pieces, segs),
            [shape((length, 2 * HEAD_SIZE), bf16), shape((HEAD_SIZE, 2 * HEAD_SIZE), jnp.float32)] * 2,
            2,
            2 + n_pieces,
            flops=2 * 2 * length * width * 2 * HEAD_SIZE,
        )(offs, meta, *[books[s] for s in segs], *chunks[0])
        kvs += found[0::2]
        deltas += found[1::2]

    total = (deltas[0] + deltas[1] + deltas[2] + deltas[3]).astype(bf16)
    base = None
    for a in range(1, n_groups):
        term = permute(total, lambda gg, mm, zz: (gg ^ a, mm, zz) if gg < gg ^ a else None)
        base = term if base is None else base.astype(jnp.float32) + term.astype(jnp.float32)

    sent = []
    for c in range(2):
        attended = call(
            functools.partial(attend_body, n_pieces, group // 2, c * (group // 2), group),
            [shape((length, half), bf16)] * MEMBERS,
            4,
            3 * MEMBERS + 1 + n_pieces,
            flops=2 * MEMBERS * length * width * half,
        )(here, offs, meta, gate_bias, *books, *chunks[1 + c], *kvs, *deltas, base)
        sent.append([attended[0]] + [to_member(attended[k], k) for k in range(1, MEMBERS)])

    (output,) = call(
        functools.partial(assemble_body, group),
        [shape((length, w_query.shape[1]), bf16)],
        1,
        2 * MEMBERS,
    )(here, *[sent[c][k] for k in range(MEMBERS) for c in range(2)])
    return output[None]


def solution(mesh):
    in_specs = (
        P("fsdp", "seg", None),
        P(("seg", "fsdp"), None),
        P(("seg", "fsdp"), None),
        P(("seg", "fsdp"), None),
        P(),
        P("fsdp", "seg", None, None),
        P("fsdp", "seg"),
    )
    out_specs = P("fsdp", "seg", None)
    body = functools.partial(shards, (mesh.shape["seg"], mesh.shape["fsdp"]))
    return jax.shard_map(body, mesh=mesh, in_specs=in_specs, out_specs=out_specs, check_vma=False)
```

time: 323 us -> 204 us (0.63)
  waiting for transfers between devices: 246 us -> 97.1 us
  starting transfers between devices: 0.12 us -> 60.2 us
  Pallas kernels: 0 us -> 34.5 us
  matrix products: 34.3 us -> 0 us
  between operations: 13.9 us -> 0.93 us
  blocking collectives: 9.07 us -> 0 us
  other arithmetic: 8.53 us -> 0.39 us
    all_gather x4 -> x0, waiting for transfers between devices: 244 us -> none  [the longest x1 108 us: shards(): lax.all_gather(w_query, ('seg', 'fsdp'), axis=0, tiled=True)]
    ppermute x0 -> x43, waiting for transfers between devices: none -> 97.1 us  [permute(): return lax.ppermute(array, AXES, pairs)]
    ppermute x0 -> x43, starting transfers between devices: none -> 60.2 us  [permute(): return lax.ppermute(array, AXES, pairs)]
    pallas_call x0 -> x6, Pallas kernels: none -> 34.5 us  [the longest x2 22.6 us: shards(): call(functools.partial(attend_body, n_pieces, group // 2, c * (group // 2...]
    dot_general x7 -> x0, matrix products: 29.6 us -> none  [the longest x3 16.3 us: add_rows(): return jnp.dot(seg_tokens, piece, preferred_element_type=jnp.float32)]
    all_gather x1 -> x0, blocking collectives: 9.07 us -> none  [carried_in(): lax.all_gather(part.astype(kind), axis)]
    select_n x16 -> x3, other arithmetic: 8.44 us -> 0.09 us  [gathered(): three = jnp.where((z == 1) | (z == 2), inner, outer)]
    sub x1 -> x0, matrix products: 4.7 us -> none  [segment_output(): expo = jnp.where(allowed, jnp.exp(masked - top), 0.0)]
  transfers between devices with their start and end apart: 4 -> 43, of which waited for: 4 -> 18; matrix products, arithmetic and copies ran while one was open for 4% -> 2% of each run, Pallas kernels for 0% -> 16%
where the time goes in v1:
time: 204 us; the launch traced here: 203 us
  waiting for transfers between devices  97.1 us (48%)
  starting transfers between devices  60.2 us (30%)
  Pallas kernels  34.5 us (17%)
  local copies, waits for them, and re-layouts  9.69 us (5%)
    ppermute x43, waiting for transfers between devices, permute(): return lax.ppermute(array, AXES, pairs)  97.1 us
    ppermute x43, starting transfers between devices, permute(): return lax.ppermute(array, AXES, pairs)  60.2 us
    pallas_call x2, Pallas kernels, shards(): call(functools.partial(attend_body, n_pieces, group // 2, c * (group // 2...  22.6 us
    pallas_call x2, Pallas kernels, shards(): call(functools.partial(kv_body, n_pieces, segs), [shape((length, 2 * HEAD...  9.45 us
    unnamed x30, local copies, waits for them, and re-layouts  6.79 us
  transfers between devices with their start and end apart: 43, of which 18 were waited for; matrix products, arithmetic and copies ran while one was open for 2% of the time, Pallas kernels for 16%

profile of v1, /device:TPU:9, one launch (start us, length us, event | category | flops | bytes accessed | tf_op | source)
XLA Modules:
  0.0 202.8 jit_solution(6988417185281364273)
XLA Ops:
  0.0 1.2 collective-permute-start.4
  1.2 1.0 collective-permute-start.3
  2.8 0.8 reshape.21
  3.7 1.0 copy-done.1
  4.7 0.9 copy-done.2
  5.6 0.9 copy-done.3
  6.5 1.3 shard_map.73
  7.8 0.6 copy-done.5
  8.4 0.6 copy-done.7
  9.1 0.6 copy-done.8
  10.0 0.8 collective-permute-start.26
  10.8 1.0 collective-permute-done.26
  11.8 1.2 collective-permute-start.27
  13.1 36.6 %collective-permute-done.27 = bf16[128,256]{1,0:T(8,128)(2,1)S(1)} collective-permute-done((bf16[128,256]{1,0:T(8,128)(2,1)}, bf16[128,256]{1,0:T(8,128)(2,1)S(1)}, u32[]{:S(2)}, u32[]{:S(2)}) %collective-permute-start.27) | collective-permute-done | bytes 65568 | tf_op jit(solution)/shard_map/ppermute | solution.py:187
  49.7 2.6 %collective-permute-start.28 = (bf16[128,256]{1,0:T(8,128)(2,1)}, bf16[128,256]{1,0:T(8,128)(2,1)S(1)}, u32[]{:S(2)}, u32[]{:S(2)}) collective-permute-start(bf16[128,256]{1,0:T(8,128)(2,1)} %copy-done.7), channel_id=1, source_target_pairs={{0,12},{1,13},{2,14},{3,15},{4,8},{5,9},{6,10},{7,11},{8,4},{9,5},... | collective-permute-start | bytes 196616 | tf_op jit(solution)/shard_map/ppermute | solution.py:187
  52.4 3.1 %collective-permute-done.28 = bf16[128,256]{1,0:T(8,128)(2,1)S(1)} collective-permute-done((bf16[128,256]{1,0:T(8,128)(2,1)}, bf16[128,256]{1,0:T(8,128)(2,1)S(1)}, u32[]{:S(2)}, u32[]{:S(2)}) %collective-permute-start.28) | collective-permute-done | bytes 65568 | tf_op jit(solution)/shard_map/ppermute | solution.py:187
  55.4 0.8 collective-permute-start.2
  56.9 2.3 %collective-permute-start.30 = (bf16[512,256]{1,0:T(8,128)(2,1)S(1)}, bf16[512,256]{1,0:T(8,128)(2,1)S(1)}, u32[]{:S(2)}, u32[]{:S(2)}) collective-permute-start(bf16[512,256]{1,0:T(8,128)(2,1)S(1)} %constant_dynamic-update-slice_fusion.4.refs_4_), channel_id=1, source_target_pairs={{0,2},{1,3},{2,0},{3,1},{4,6},{5,7},{6,4},{7,5},{8,10},{9,11},{10,... | collective-permute-start | bytes 786440 | tf_op jit(solution)/shard_map/ppermute | solution.py:187
  59.7 0.6 copy-done.11
  60.3 2.4 %collective-permute-start.18 = (bf16[512,256]{1,0:T(8,128)(2,1)S(1)}, bf16[512,256]{1,0:T(8,128)(2,1)S(1)}, u32[]{:S(2)}, u32[]{:S(2)}) collective-permute-start(bf16[512,256]{1,0:T(8,128)(2,1)S(1)} %pad_maximum_fusion.refs_2_), channel_id=1, source_target_pairs={{0,2},{1,3},{2,0},{3,1},{4,6},{5,7},{6,4},{7,5},{8,10},{9,11},{10,... | collective-permute-start | bytes 786440 | tf_op jit(solution)/shard_map/ppermute | solution.py:187
  63.2 0.8 constant_dynamic-update-slice_fusion.2
  64.1 2.4 %collective-permute-done.7 = bf16[128,256]{1,0:T(8,128)(2,1)S(1)} collective-permute-done((bf16[128,256]{1,0:T(8,128)(2,1)}, bf16[128,256]{1,0:T(8,128)(2,1)S(1)}, u32[]{:S(2)}, u32[]{:S(2)}) %collective-permute-start.7) | collective-permute-done | bytes 65568 | tf_op jit(solution)/shard_map/ppermute | solution.py:187
  66.5 2.0 collective-permute-start.8
  68.5 2.4 %collective-permute-done.8 = bf16[128,256]{1,0:T(8,128)(2,1)S(1)} collective-permute-done((bf16[128,256]{1,0:T(8,128)(2,1)S(1)}, bf16[128,256]{1,0:T(8,128)(2,1)S(1)}, u32[]{:S(2)}, u32[]{:S(2)}) %collective-permute-start.8) | collective-permute-done | bytes 65568 | tf_op jit(solution)/shard_map/ppermute | solution.py:187
  70.9 1.9 collective-permute-start.31
  72.9 3.5 %collective-permute-done.30.refs_6_ = bf16[512,256]{1,0:T(8,128)(2,1)S(1)} collective-permute-done((bf16[512,256]{1,0:T(8,128)(2,1)S(1)}, bf16[512,256]{1,0:T(8,128)(2,1)S(1)}, u32[]{:S(2)}, u32[]{:S(2)}) %collective-permute-start.30) | collective-permute-done | bytes 262176 | tf_op jit(solution)/shard_map/ppermute | solution.py:187
  76.4 1.9 collective-permute-start.19
  78.3 3.7 %collective-permute-done.18.refs_4_ = bf16[512,256]{1,0:T(8,128)(2,1)S(1)} collective-permute-done((bf16[512,256]{1,0:T(8,128)(2,1)S(1)}, bf16[512,256]{1,0:T(8,128)(2,1)S(1)}, u32[]{:S(2)}, u32[]{:S(2)}) %collective-permute-start.18) | collective-permute-done | bytes 262176 | tf_op jit(solution)/shard_map/ppermute | solution.py:187
  82.0 2.6 %collective-permute-start.20 = (bf16[512,256]{1,0:T(8,128)(2,1)S(1)}, bf16[512,256]{1,0:T(8,128)(2,1)S(1)}, u32[]{:S(2)}, u32[]{:S(2)}) collective-permute-start(bf16[512,256]{1,0:T(8,128)(2,1)S(1)} %collective-permute-done.18.refs_4_), channel_id=1, source_target_pairs={{1,0},{2,3},{5,4},{6,7},{9,8},{10,11},{13,12},{14,15},{17,16},{18,... | collective-permute-start | bytes 786440 | tf_op jit(solution)/shard_map/ppermute | solution.py:187
  84.6 0.7 slice_bitcast_fusion
  85.3 2.3 %collective-permute-done.31 = bf16[512,256]{1,0:T(8,128)(2,1)S(1)} collective-permute-done((bf16[512,256]{1,0:T(8,128)(2,1)S(1)}, bf16[512,256]{1,0:T(8,128)(2,1)S(1)}, u32[]{:S(2)}, u32[]{:S(2)}) %collective-permute-start.31) | collective-permute-done | bytes 262176 | tf_op jit(solution)/shard_map/ppermute | solution.py:187
  87.6 5.6 %collective-permute-done.19 = bf16[512,256]{1,0:T(8,128)(2,1)S(1)} collective-permute-done((bf16[512,256]{1,0:T(8,128)(2,1)S(1)}, bf16[512,256]{1,0:T(8,128)(2,1)S(1)}, u32[]{:S(2)}, u32[]{:S(2)}) %collective-permute-start.19) | collective-permute-done | bytes 262176 | tf_op jit(solution)/shard_map/ppermute | solution.py:187
  93.3 1.2 collective-permute-start.21
  94.5 1.3 collective-permute-start.32
  95.8 0.7 slice_bitcast_fusion.1
  96.8 3.9 %collective-permute-done.21.refs_6_ = bf16[512,256]{1,0:T(8,128)(2,1)S(1)} collective-permute-done((bf16[512,256]{1,0:T(8,128)(2,1)S(1)}, bf16[512,256]{1,0:T(8,128)(2,1)S(1)}, u32[]{:S(2)}, u32[]{:S(2)}) %collective-permute-start.21) | collective-permute-done | bytes 262176 | tf_op jit(solution)/shard_map/ppermute | solution.py:187
  100.7 1.2 collective-permute-start.22
  102.1 0.7 slice_bitcast_fusion.2
  102.9 9.0 %collective-permute-done.22.refs_7_ = bf16[512,256]{1,0:T(8,128)(2,1)S(1)} collective-permute-done((bf16[512,256]{1,0:T(8,128)(2,1)S(1)}, bf16[512,256]{1,0:T(8,128)(2,1)S(1)}, u32[]{:S(2)}, u32[]{:S(2)}) %collective-permute-start.22) | collective-permute-done | bytes 262176 | tf_op jit(solution)/shard_map/ppermute | solution.py:187
  111.9 1.2 collective-permute-start.33
  113.2 4.4 %collective-permute-done.24.refs_9_ = bf16[512,256]{1,0:T(8,128)(2,1)S(1)} collective-permute-done((bf16[512,256]{1,0:T(8,128)(2,1)S(1)}, bf16[512,256]{1,0:T(8,128)(2,1)S(1)}, u32[]{:S(2)}, u32[]{:S(2)}) %collective-permute-start.24) | collective-permute-done | bytes 262176 | tf_op jit(solution)/shard_map/ppermute | solution.py:187
  117.5 4.1 %collective-permute-start.11 = (bf16[512,256]{1,0:T(8,128)(2,1)S(1)}, bf16[512,256]{1,0:T(8,128)(2,1)S(1)}, u32[]{:S(2)}, u32[]{:S(2)}) collective-permute-start(bf16[512,256]{1,0:T(8,128)(2,1)S(1)} %constant_dynamic-update-slice_fusion.refs_4_), channel_id=1, source_target_pairs={{1,2},{2,1},{5,6},{6,5},{9,10},{10,9},{13,14},{14,13},{17,18},{18,... | collective-permute-start | bytes 786440 | tf_op jit(solution)/shard_map/ppermute | solution.py:187
  121.7 4.4 %shard_map.74 = (bf16[256,256]{1,0:T(8,128)(2,1)S(1)}, f32[128,256]{1,0:T(8,128)S(1)}, bf16[256,256]{1,0:T(8,128)(2,1)S(1)}, f32[128,256]{1,0:T(8,128)S(1)}) custom-call(s32[32]{0:T(128)S(1)} %reshape.23.offs_ref, s32[20]{0:T(128)S(1)} %maximum_convert_fusion.meta_ref, bf16[256,4096]{1,0:T(8,128)(2,1)S(1)} %bitcast.15, ...), custom_call_target="tpu_custom_call" | custom-call | flops 1073741824 | bytes 8388608 | tf_op jit(solution)/shard_map/pallas_call | solution.py:255
  126.1 5.9 %collective-permute-start.9 = (bf16[512,256]{1,0:T(8,128)(2,1)S(1)}, bf16[512,256]{1,0:T(8,128)(2,1)S(1)}, u32[]{:S(2)}, u32[]{:S(2)}) collective-permute-start(bf16[512,256]{1,0:T(8,128)(2,1)S(1)} %constant_dynamic-update-slice_fusion.refs_4_), channel_id=1, source_target_pairs={{0,1},{1,0},{2,3},{3,2},{4,5},{5,4},{6,7},{7,6},{8,9},{9,8},{10,11... | collective-permute-start | bytes 786440 | tf_op jit(solution)/shard_map/ppermute | solution.py:187
  132.1 1.9 collective-permute-start.12
  134.0 5.0 %shard_map.75 = (bf16[256,256]{1,0:T(8,128)(2,1)S(1)}, f32[128,256]{1,0:T(8,128)S(1)}, bf16[256,256]{1,0:T(8,128)(2,1)S(1)}, f32[128,256]{1,0:T(8,128)S(1)}) custom-call(s32[32]{0:T(128)S(1)} %reshape.23.offs_ref, s32[20]{0:T(128)S(1)} %maximum_convert_fusion.meta_ref, bf16[256,4096]{1,0:T(8,128)(2,1)} %collective-permute-done.4.refs_0_.refs_2_, ...), custom_call_target="tpu_custom_call" | custom-call | flops 1073741824 | bytes 8388608 | tf_op jit(solution)/shard_map/pallas_call | solution.py:255
  139.1 1.3 collective-permute-start.35
  140.6 1.2 collective-permute-start.36
  142.2 3.3 %collective-permute-start.25 = (bf16[128,256]{1,0:T(8,128)(2,1)S(1)}, bf16[128,256]{1,0:T(8,128)(2,1)S(1)}, u32[]{:S(2)}, u32[]{:S(2)}) collective-permute-start(bf16[128,256]{1,0:T(8,128)(2,1)S(1)} %add_convert_fusion), channel_id=1, source_target_pairs={{0,16},{1,17},{2,18},{3,19},{4,20},{5,21},{6,22},{7,23},{8,24},{9,... | collective-permute-start | bytes 196616 | tf_op jit(solution)/shard_map/ppermute | solution.py:187
  145.5 3.6 %collective-permute-done.34.refs_9_ = bf16[512,256]{1,0:T(8,128)(2,1)S(1)} collective-permute-done((bf16[512,256]{1,0:T(8,128)(2,1)S(1)}, bf16[512,256]{1,0:T(8,128)(2,1)S(1)}, u32[]{:S(2)}, u32[]{:S(2)}) %collective-permute-start.34) | collective-permute-done | bytes 262176 | tf_op jit(solution)/shard_map/ppermute | solution.py:187
  149.2 1.2 collective-permute-start.14
  150.6 4.1 %collective-permute-done.36.refs_11_ = bf16[512,256]{1,0:T(8,128)(2,1)S(1)} collective-permute-done((bf16[512,256]{1,0:T(8,128)(2,1)S(1)}, bf16[512,256]{1,0:T(8,128)(2,1)S(1)}, u32[]{:S(2)}, u32[]{:S(2)}) %collective-permute-start.36) | collective-permute-done | bytes 262176 | tf_op jit(solution)/shard_map/ppermute | solution.py:187
  154.8 1.2 collective-permute-start.16
  156.0 4.8 %collective-permute-done.25.refs_20_ = bf16[128,256]{1,0:T(8,128)(2,1)S(1)} collective-permute-done((bf16[128,256]{1,0:T(8,128)(2,1)S(1)}, bf16[128,256]{1,0:T(8,128)(2,1)S(1)}, u32[]{:S(2)}, u32[]{:S(2)}) %collective-permute-start.25) | collective-permute-done | bytes 65568 | tf_op jit(solution)/shard_map/ppermute | solution.py:187
  160.8 11.3 %shard_map.77 = (bf16[256,256]{1,0:T(8,128)(2,1)S(1)}, bf16[256,256]{1,0:T(8,128)(2,1)S(1)}, bf16[256,256]{1,0:T(8,128)(2,1)S(1)}, bf16[256,256]{1,0:T(8,128)(2,1)S(1)}) custom-call(s32[1]{0:T(128)} %bitcast.here_ref, s32[32]{0:T(128)S(1)} %reshape.23.offs_ref, s32[20]{0:T(128)S(1)} %maximum_convert_fusion.meta_ref, f32[16]{0:T(128)S(1)} %copy-done.4, ...), custom_call_target="tpu_custom_call" | custom-call | flops 2147483648 | bytes 8388608 | tf_op jit(solution)/shard_map/pallas_call | solution.py:273
  172.1 8.3 %collective-permute-start.38 = (bf16[256,256]{1,0:T(8,128)(2,1)S(1)}, bf16[256,256]{1,0:T(8,128)(2,1)S(1)}, u32[]{:S(2)}, u32[]{:S(2)}) collective-permute-start(bf16[256,256]{1,0:T(8,128)(2,1)S(1)} %get-tuple-element.56), channel_id=1, source_target_pairs={{0,4},{1,5},{2,6},{3,7},{4,0},{5,1},{6,2},{7,3},{8,12},{9,13},{10,... | collective-permute-start | bytes 393224 | tf_op jit(solution)/shard_map/ppermute | solution.py:187
  180.4 1.0 collective-permute-start.40
  181.4 0.8 collective-permute-start.42
  182.1 11.3 %shard_map.76 = (bf16[256,256]{1,0:T(8,128)(2,1)S(1)}, bf16[256,256]{1,0:T(8,128)(2,1)S(1)}, bf16[256,256]{1,0:T(8,128)(2,1)S(1)}, bf16[256,256]{1,0:T(8,128)(2,1)S(1)}) custom-call(s32[1]{0:T(128)} %bitcast.here_ref, s32[32]{0:T(128)S(1)} %reshape.23.offs_ref, s32[20]{0:T(128)S(1)} %maximum_convert_fusion.meta_ref, f32[16]{0:T(128)S(1)} %copy-done.4, ...), custom_call_target="tpu_custom_call" | custom-call | flops 2147483648 | bytes 8388608 | tf_op jit(solution)/shard_map/pallas_call | solution.py:273
  193.7 0.9 collective-permute-start.39
  194.6 1.0 collective-permute-start.41
  195.7 2.7 %collective-permute-done.39.refs_4_ = bf16[256,256]{1,0:T(8,128)(2,1)S(1)} collective-permute-done((bf16[256,256]{1,0:T(8,128)(2,1)S(1)}, bf16[256,256]{1,0:T(8,128)(2,1)S(1)}, u32[]{:S(2)}, u32[]{:S(2)}) %collective-permute-start.39) | collective-permute-done | bytes 131104 | tf_op jit(solution)/shard_map/ppermute | solution.py:187
  198.4 3.3 %collective-permute-done.41.refs_6_ = bf16[256,256]{1,0:T(8,128)(2,1)S(1)} collective-permute-done((bf16[256,256]{1,0:T(8,128)(2,1)S(1)}, bf16[256,256]{1,0:T(8,128)(2,1)S(1)}, u32[]{:S(2)}, u32[]{:S(2)}) %collective-permute-start.41) | collective-permute-done | bytes 131104 | tf_op jit(solution)/shard_map/ppermute | solution.py:187
  201.7 1.1 shard_map.78
  (80 shorter events, 3.9 us)
Async XLA Ops:
  0.0 52.3 %collective-permute-start.4 = (bf16[256,4096]{1,0:T(8,128)(2,1)}, bf16[256,4096]{1,0:T(8,128)(2,1)}, u32[]{:S(2)}, u32[]{:S(2)}) collective-permute-start(bf16[256,4096]{1,0:T(8,128)(2,1)} %bitcast.13), channel_id=1, source_target_pairs={{0,8},{1,9},{2,10},{3,11},{4,12},{5,13},{6,14},{7,15},{8,0},{9,1},... | collective-permute-start | bytes 6291464 | tf_op jit(solution)/shard_map/ppermute | solution.py:187
  1.2 116.3 %collective-permute-start.3 = (bf16[256,4096]{1,0:T(8,128)(2,1)}, bf16[256,4096]{1,0:T(8,128)(2,1)}, u32[]{:S(2)}, u32[]{:S(2)}) collective-permute-start(bf16[256,4096]{1,0:T(8,128)(2,1)} %bitcast.14), channel_id=1, source_target_pairs={{0,4},{1,5},{2,6},{3,7},{4,0},{5,1},{6,2},{7,3},{8,12},{9,13},{10,... | collective-permute-start | bytes 6291464 | tf_op jit(solution)/shard_map/ppermute | solution.py:187
  3.7 1.0 copy-start.1
  4.7 0.9 copy-start.2
  5.6 0.9 copy-start.3
  6.5 115.2 %copy-start = (bf16[1,256,4096]{2,1,0:T(8,128)(2,1)S(1)}, bf16[1,256,4096]{2,1,0:T(8,128)(2,1)}, u32[]{:S(2)}) copy-start(bf16[1,256,4096]{2,1,0:T(8,128)(2,1)} %param.7) | copy-start | bytes 6291460
  7.8 0.6 copy-start.5
  8.4 0.6 copy-start.7
  9.1 0.6 copy-start.8
  9.7 1.1 copy-start.6
  9.7 46.5 %collective-permute-start = (bf16[144,256]{1,0:T(8,128)(2,1)S(1)}, bf16[144,256]{1,0:T(8,128)(2,1)S(1)}, u32[]{:S(2)}, u32[]{:S(2)}) collective-permute-start(bf16[144,256]{1,0:T(8,128)(2,1)S(1)} %get-tuple-element.34), channel_id=1, source_target_pairs={{0,4},{1,5},{2,6},{3,7},{4,0},{5,1},{6,2},{7,3},{8,12},{9,13},{10,... | collective-permute-start | bytes 221192 | tf_op jit(solution)/shard_map/ppermute | solution.py:187
  9.7 47.2 %collective-permute-start.1 = (bf16[144,256]{1,0:T(8,128)(2,1)S(1)}, bf16[144,256]{1,0:T(8,128)(2,1)S(1)}, u32[]{:S(2)}, u32[]{:S(2)}) collective-permute-start(bf16[144,256]{1,0:T(8,128)(2,1)S(1)} %get-tuple-element.35), channel_id=1, source_target_pairs={{0,8},{1,9},{2,10},{3,11},{4,12},{5,13},{6,14},{7,15},{8,0},{9,1},... | collective-permute-start | bytes 221192 | tf_op jit(solution)/shard_map/ppermute | solution.py:187
  10.0 1.9 collective-permute-start.26
  11.8 37.9 %collective-permute-start.27 = (bf16[128,256]{1,0:T(8,128)(2,1)}, bf16[128,256]{1,0:T(8,128)(2,1)S(1)}, u32[]{:S(2)}, u32[]{:S(2)}) collective-permute-start(bf16[128,256]{1,0:T(8,128)(2,1)} %copy-done.8), channel_id=1, source_target_pairs={{0,8},{1,9},{2,10},{3,11},{4,12},{5,13},{6,14},{7,15},{8,0},{9,1},... | collective-permute-start | bytes 196616 | tf_op jit(solution)/shard_map/ppermute | solution.py:187
  49.7 5.7 %collective-permute-start.28 = (bf16[128,256]{1,0:T(8,128)(2,1)}, bf16[128,256]{1,0:T(8,128)(2,1)S(1)}, u32[]{:S(2)}, u32[]{:S(2)}) collective-permute-start(bf16[128,256]{1,0:T(8,128)(2,1)} %copy-done.7), channel_id=1, source_target_pairs={{0,12},{1,13},{2,14},{3,15},{4,8},{5,9},{6,10},{7,11},{8,4},{9,5},... | collective-permute-start | bytes 196616 | tf_op jit(solution)/shard_map/ppermute | solution.py:187
  52.3 79.7 %collective-permute-start.5 = (bf16[256,4096]{1,0:T(8,128)(2,1)}, bf16[256,4096]{1,0:T(8,128)(2,1)}, u32[]{:S(2)}, u32[]{:S(2)}) collective-permute-start(bf16[256,4096]{1,0:T(8,128)(2,1)} %collective-permute-done.4.refs_0_.refs_2_), channel_id=1, source_target_pairs={{0,4},{1,5},{2,6},{3,7},{4,0},{5,1},{6,2},{7,3},{8,12},{9,13},{10,... | collective-permute-start | bytes 6291464 | tf_op jit(solution)/shard_map/ppermute | solution.py:187
  55.4 4.3 %collective-permute-start.2 = (bf16[144,256]{1,0:T(8,128)(2,1)S(1)}, bf16[144,256]{1,0:T(8,128)(2,1)S(1)}, u32[]{:S(2)}, u32[]{:S(2)}) collective-permute-start(bf16[144,256]{1,0:T(8,128)(2,1)S(1)} %get-tuple-element.36), channel_id=1, source_target_pairs={{0,12},{1,13},{2,14},{3,15},{4,8},{5,9},{6,10},{7,11},{8,4},{9,5},... | collective-permute-start | bytes 221192 | tf_op jit(solution)/shard_map/ppermute | solution.py:187
  56.3 0.6 copy-start.9
  56.3 6.5 %collective-permute-start.6 = (bf16[128,256]{1,0:T(8,128)(2,1)}, bf16[128,256]{1,0:T(8,128)(2,1)}, u32[]{:S(2)}, u32[]{:S(2)}) collective-permute-start(bf16[128,256]{1,0:T(8,128)(2,1)} %copy-done.6), channel_id=1, source_target_pairs={{0,4},{1,5},{2,6},{3,7},{4,0},{5,1},{6,2},{7,3},{8,12},{9,13},{10,... | collective-permute-start | bytes 196616 | tf_op jit(solution)/shard_map/ppermute | solution.py:187
  56.9 2.8 %copy-start.10 = (bf16[144,256]{1,0:T(8,128)(2,1)}, bf16[144,256]{1,0:T(8,128)(2,1)S(1)}, u32[]{:S(2)}) copy-start(bf16[144,256]{1,0:T(8,128)(2,1)S(1)} %collective-permute-done.1) | copy-start | bytes 221188
  56.9 19.5 %collective-permute-start.30 = (bf16[512,256]{1,0:T(8,128)(2,1)S(1)}, bf16[512,256]{1,0:T(8,128)(2,1)S(1)}, u32[]{:S(2)}, u32[]{:S(2)}) collective-permute-start(bf16[512,256]{1,0:T(8,128)(2,1)S(1)} %constant_dynamic-update-slice_fusion.4.refs_4_), channel_id=1, source_target_pairs={{0,2},{1,3},{2,0},{3,1},{4,6},{5,7},{6,4},{7,5},{8,10},{9,11},{10,... | collective-permute-start | bytes 786440 | tf_op jit(solution)/shard_map/ppermute | solution.py:187
  59.7 0.6 copy-start.11
  60.3 21.7 %collective-permute-start.18 = (bf16[512,256]{1,0:T(8,128)(2,1)S(1)}, bf16[512,256]{1,0:T(8,128)(2,1)S(1)}, u32[]{:S(2)}, u32[]{:S(2)}) collective-permute-start(bf16[512,256]{1,0:T(8,128)(2,1)S(1)} %pad_maximum_fusion.refs_2_), channel_id=1, source_target_pairs={{0,2},{1,3},{2,0},{3,1},{4,6},{5,7},{6,4},{7,5},{8,10},{9,11},{10,... | collective-permute-start | bytes 786440 | tf_op jit(solution)/shard_map/ppermute | solution.py:187
  62.8 3.7 %collective-permute-start.7 = (bf16[128,256]{1,0:T(8,128)(2,1)}, bf16[128,256]{1,0:T(8,128)(2,1)S(1)}, u32[]{:S(2)}, u32[]{:S(2)}) collective-permute-start(bf16[128,256]{1,0:T(8,128)(2,1)} %copy-done.5), channel_id=1, source_target_pairs={{0,8},{1,9},{2,10},{3,11},{4,12},{5,13},{6,14},{7,15},{8,0},{9,1},... | collective-permute-start | bytes 196616 | tf_op jit(solution)/shard_map/ppermute | solution.py:187
  66.5 4.4 %collective-permute-start.8 = (bf16[128,256]{1,0:T(8,128)(2,1)S(1)}, bf16[128,256]{1,0:T(8,128)(2,1)S(1)}, u32[]{:S(2)}, u32[]{:S(2)}) collective-permute-start(bf16[128,256]{1,0:T(8,128)(2,1)S(1)} %get-tuple-element.40), channel_id=1, source_target_pairs={{0,12},{1,13},{2,14},{3,15},{4,8},{5,9},{6,10},{7,11},{8,4},{9,5},... | collective-permute-start | bytes 196616 | tf_op jit(solution)/shard_map/ppermute | solution.py:187
  70.9 16.7 %collective-permute-start.31 = (bf16[512,256]{1,0:T(8,128)(2,1)S(1)}, bf16[512,256]{1,0:T(8,128)(2,1)S(1)}, u32[]{:S(2)}, u32[]{:S(2)}) collective-permute-start(bf16[512,256]{1,0:T(8,128)(2,1)S(1)} %constant_dynamic-update-slice_fusion.4.refs_4_), channel_id=1, source_target_pairs={{1,2},{2,1},{5,6},{6,5},{9,10},{10,9},{13,14},{14,13},{17,18},{18,... | collective-permute-start | bytes 786440 | tf_op jit(solution)/shard_map/ppermute | solution.py:187
  76.4 16.9 %collective-permute-start.19 = (bf16[512,256]{1,0:T(8,128)(2,1)S(1)}, bf16[512,256]{1,0:T(8,128)(2,1)S(1)}, u32[]{:S(2)}, u32[]{:S(2)}) collective-permute-start(bf16[512,256]{1,0:T(8,128)(2,1)S(1)} %pad_maximum_fusion.refs_2_), channel_id=1, source_target_pairs={{1,2},{2,1},{5,6},{6,5},{9,10},{10,9},{13,14},{14,13},{17,18},{18,... | collective-permute-start | bytes 786440 | tf_op jit(solution)/shard_map/ppermute | solution.py:187
  82.0 12.5 %collective-permute-start.20 = (bf16[512,256]{1,0:T(8,128)(2,1)S(1)}, bf16[512,256]{1,0:T(8,128)(2,1)S(1)}, u32[]{:S(2)}, u32[]{:S(2)}) collective-permute-start(bf16[512,256]{1,0:T(8,128)(2,1)S(1)} %collective-permute-done.18.refs_4_), channel_id=1, source_target_pairs={{1,0},{2,3},{5,4},{6,7},{9,8},{10,11},{13,12},{14,15},{17,16},{18,... | collective-permute-start | bytes 786440 | tf_op jit(solution)/shard_map/ppermute | solution.py:187
  87.6 8.9 %collective-permute-start.17 = (bf16[512,256]{1,0:T(8,128)(2,1)S(1)}, bf16[512,256]{1,0:T(8,128)(2,1)S(1)}, u32[]{:S(2)}, u32[]{:S(2)}) collective-permute-start(bf16[512,256]{1,0:T(8,128)(2,1)S(1)} %pad_maximum_fusion.refs_2_), channel_id=1, source_target_pairs={{0,1},{1,0},{2,3},{3,2},{4,5},{5,4},{6,7},{7,6},{8,9},{9,8},{10,11... | collective-permute-start | bytes 786440 | tf_op jit(solution)/shard_map/ppermute | solution.py:187
  93.3 7.4 %collective-permute-start.21 = (bf16[512,256]{1,0:T(8,128)(2,1)S(1)}, bf16[512,256]{1,0:T(8,128)(2,1)S(1)}, u32[]{:S(2)}, u32[]{:S(2)}) collective-permute-start(bf16[512,256]{1,0:T(8,128)(2,1)S(1)} %pad_maximum_fusion.refs_2_), channel_id=1, source_target_pairs={{0,16},{1,17},{2,18},{3,19},{4,20},{5,21},{6,22},{7,23},{8,24},{9,... | collective-permute-start | bytes 786440 | tf_op jit(solution)/shard_map/ppermute | solution.py:187
  94.5 7.4 %collective-permute-start.32 = (bf16[512,256]{1,0:T(8,128)(2,1)S(1)}, bf16[512,256]{1,0:T(8,128)(2,1)S(1)}, u32[]{:S(2)}, u32[]{:S(2)}) collective-permute-start(bf16[512,256]{1,0:T(8,128)(2,1)S(1)} %collective-permute-done.30.refs_6_), channel_id=1, source_target_pairs={{1,0},{2,3},{5,4},{6,7},{9,8},{10,11},{13,12},{14,15},{17,16},{18,... | collective-permute-start | bytes 786440 | tf_op jit(solution)/shard_map/ppermute | solution.py:187
  96.5 15.4 %collective-permute-start.23 = (bf16[512,256]{1,0:T(8,128)(2,1)S(1)}, bf16[512,256]{1,0:T(8,128)(2,1)S(1)}, u32[]{:S(2)}, u32[]{:S(2)}) collective-permute-start(bf16[512,256]{1,0:T(8,128)(2,1)S(1)} %collective-permute-done.18.refs_4_), channel_id=1, source_target_pairs={{0,16},{1,17},{2,18},{3,19},{4,20},{5,21},{6,22},{7,23},{8,24},{9,... | collective-permute-start | bytes 786440 | tf_op jit(solution)/shard_map/ppermute | solution.py:187
  100.7 11.2 %collective-permute-start.22 = (bf16[512,256]{1,0:T(8,128)(2,1)S(1)}, bf16[512,256]{1,0:T(8,128)(2,1)S(1)}, u32[]{:S(2)}, u32[]{:S(2)}) collective-permute-start(bf16[512,256]{1,0:T(8,128)(2,1)S(1)} %collective-permute-done.17.refs_3_), channel_id=1, source_target_pairs={{0,16},{1,17},{2,18},{3,19},{4,20},{5,21},{6,22},{7,23},{8,24},{9,... | collective-permute-start | bytes 786440 | tf_op jit(solution)/shard_map/ppermute | solution.py:187
  101.9 15.6 %collective-permute-start.24 = (bf16[512,256]{1,0:T(8,128)(2,1)S(1)}, bf16[512,256]{1,0:T(8,128)(2,1)S(1)}, u32[]{:S(2)}, u32[]{:S(2)}) collective-permute-start(bf16[512,256]{1,0:T(8,128)(2,1)S(1)} %broadcast_select_fusion.1.refs_5_), channel_id=1, source_target_pairs={{0,16},{1,17},{2,18},{3,19},{4,20},{5,21},{6,22},{7,23},{8,24},{9,... | collective-permute-start | bytes 786440 | tf_op jit(solution)/shard_map/ppermute | solution.py:187
  111.9 27.1 %collective-permute-start.29 = (bf16[512,256]{1,0:T(8,128)(2,1)S(1)}, bf16[512,256]{1,0:T(8,128)(2,1)S(1)}, u32[]{:S(2)}, u32[]{:S(2)}) collective-permute-start(bf16[512,256]{1,0:T(8,128)(2,1)S(1)} %constant_dynamic-update-slice_fusion.4.refs_4_), channel_id=1, source_target_pairs={{0,1},{1,0},{2,3},{3,2},{4,5},{5,4},{6,7},{7,6},{8,9},{9,8},{10,11... | collective-permute-start | bytes 786440 | tf_op jit(solution)/shard_map/ppermute | solution.py:187
  111.9 28.4 %collective-permute-start.33 = (bf16[512,256]{1,0:T(8,128)(2,1)S(1)}, bf16[512,256]{1,0:T(8,128)(2,1)S(1)}, u32[]{:S(2)}, u32[]{:S(2)}) collective-permute-start(bf16[512,256]{1,0:T(8,128)(2,1)S(1)} %constant_dynamic-update-slice_fusion.4.refs_4_), channel_id=1, source_target_pairs={{0,16},{1,17},{2,18},{3,19},{4,20},{5,21},{6,22},{7,23},{8,24},{9,... | collective-permute-start | bytes 786440 | tf_op jit(solution)/shard_map/ppermute | solution.py:187
  117.5 8.6 %collective-permute-start.10 = (bf16[512,256]{1,0:T(8,128)(2,1)S(1)}, bf16[512,256]{1,0:T(8,128)(2,1)S(1)}, u32[]{:S(2)}, u32[]{:S(2)}) collective-permute-start(bf16[512,256]{1,0:T(8,128)(2,1)S(1)} %constant_dynamic-update-slice_fusion.refs_4_), channel_id=1, source_target_pairs={{0,2},{1,3},{2,0},{3,1},{4,6},{5,7},{6,4},{7,5},{8,10},{9,11},{10,... | collective-permute-start | bytes 786440 | tf_op jit(solution)/shard_map/ppermute | solution.py:187
  117.5 23.1 %collective-permute-start.11 = (bf16[512,256]{1,0:T(8,128)(2,1)S(1)}, bf16[512,256]{1,0:T(8,128)(2,1)S(1)}, u32[]{:S(2)}, u32[]{:S(2)}) collective-permute-start(bf16[512,256]{1,0:T(8,128)(2,1)S(1)} %constant_dynamic-update-slice_fusion.refs_4_), channel_id=1, source_target_pairs={{1,2},{2,1},{5,6},{6,5},{9,10},{10,9},{13,14},{14,13},{17,18},{18,... | collective-permute-start | bytes 786440 | tf_op jit(solution)/shard_map/ppermute | solution.py:187
  126.1 34.7 %copy-start.4 = (f32[16]{0:T(128)S(1)}, f32[16]{0:T(128)}, u32[]{:S(2)}) copy-start(f32[16]{0:T(128)} %gate_ref.3) | copy-start | bytes 196
  126.1 15.7 %collective-permute-start.9 = (bf16[512,256]{1,0:T(8,128)(2,1)S(1)}, bf16[512,256]{1,0:T(8,128)(2,1)S(1)}, u32[]{:S(2)}, u32[]{:S(2)}) collective-permute-start(bf16[512,256]{1,0:T(8,128)(2,1)S(1)} %constant_dynamic-update-slice_fusion.refs_4_), channel_id=1, source_target_pairs={{0,1},{1,0},{2,3},{3,2},{4,5},{5,4},{6,7},{7,6},{8,9},{9,8},{10,11... | collective-permute-start | bytes 786440 | tf_op jit(solution)/shard_map/ppermute | solution.py:187
  132.1 10.1 %collective-permute-start.12 = (bf16[512,256]{1,0:T(8,128)(2,1)S(1)}, bf16[512,256]{1,0:T(8,128)(2,1)S(1)}, u32[]{:S(2)}, u32[]{:S(2)}) collective-permute-start(bf16[512,256]{1,0:T(8,128)(2,1)S(1)} %collective-permute-done.10.refs_6_), channel_id=1, source_target_pairs={{1,0},{2,3},{5,4},{6,7},{9,8},{10,11},{13,12},{14,15},{17,16},{18,... | collective-permute-start | bytes 786440 | tf_op jit(solution)/shard_map/ppermute | solution.py:187
  139.1 11.3 %collective-permute-start.35 = (bf16[512,256]{1,0:T(8,128)(2,1)S(1)}, bf16[512,256]{1,0:T(8,128)(2,1)S(1)}, u32[]{:S(2)}, u32[]{:S(2)}) collective-permute-start(bf16[512,256]{1,0:T(8,128)(2,1)S(1)} %collective-permute-done.30.refs_6_), channel_id=1, source_target_pairs={{0,16},{1,17},{2,18},{3,19},{4,20},{5,21},{6,22},{7,23},{8,24},{9,... | collective-permute-start | bytes 786440 | tf_op jit(solution)/shard_map/ppermute | solution.py:187
  140.4 8.8 %collective-permute-start.34 = (bf16[512,256]{1,0:T(8,128)(2,1)S(1)}, bf16[512,256]{1,0:T(8,128)(2,1)S(1)}, u32[]{:S(2)}, u32[]{:S(2)}) collective-permute-start(bf16[512,256]{1,0:T(8,128)(2,1)S(1)} %collective-permute-done.29.refs_5_), channel_id=1, source_target_pairs={{0,16},{1,17},{2,18},{3,19},{4,20},{5,21},{6,22},{7,23},{8,24},{9,... | collective-permute-start | bytes 786440 | tf_op jit(solution)/shard_map/ppermute | solution.py:187
  140.6 14.2 %collective-permute-start.36 = (bf16[512,256]{1,0:T(8,128)(2,1)S(1)}, bf16[512,256]{1,0:T(8,128)(2,1)S(1)}, u32[]{:S(2)}, u32[]{:S(2)}) collective-permute-start(bf16[512,256]{1,0:T(8,128)(2,1)S(1)} %broadcast_select_fusion.refs_7_), channel_id=1, source_target_pairs={{0,16},{1,17},{2,18},{3,19},{4,20},{5,21},{6,22},{7,23},{8,24},{9,... | collective-permute-start | bytes 786440 | tf_op jit(solution)/shard_map/ppermute | solution.py:187
  141.9 38.5 %collective-permute-start.13 = (bf16[512,256]{1,0:T(8,128)(2,1)S(1)}, bf16[512,256]{1,0:T(8,128)(2,1)S(1)}, u32[]{:S(2)}, u32[]{:S(2)}) collective-permute-start(bf16[512,256]{1,0:T(8,128)(2,1)S(1)} %constant_dynamic-update-slice_fusion.refs_4_), channel_id=1, source_target_pairs={{0,16},{1,17},{2,18},{3,19},{4,20},{5,21},{6,22},{7,23},{8,24},{9,... | collective-permute-start | bytes 786440 | tf_op jit(solution)/shard_map/ppermute | solution.py:187
  142.2 18.7 %collective-permute-start.25 = (bf16[128,256]{1,0:T(8,128)(2,1)S(1)}, bf16[128,256]{1,0:T(8,128)(2,1)S(1)}, u32[]{:S(2)}, u32[]{:S(2)}) collective-permute-start(bf16[128,256]{1,0:T(8,128)(2,1)S(1)} %add_convert_fusion), channel_id=1, source_target_pairs={{0,16},{1,17},{2,18},{3,19},{4,20},{5,21},{6,22},{7,23},{8,24},{9,... | collective-permute-start | bytes 196616 | tf_op jit(solution)/shard_map/ppermute | solution.py:187
  149.2 32.2 %collective-permute-start.14 = (bf16[512,256]{1,0:T(8,128)(2,1)S(1)}, bf16[512,256]{1,0:T(8,128)(2,1)S(1)}, u32[]{:S(2)}, u32[]{:S(2)}) collective-permute-start(bf16[512,256]{1,0:T(8,128)(2,1)S(1)} %collective-permute-done.9.refs_5_), channel_id=1, source_target_pairs={{0,16},{1,17},{2,18},{3,19},{4,20},{5,21},{6,22},{7,23},{8,24},{9,... | collective-permute-start | bytes 786440 | tf_op jit(solution)/shard_map/ppermute | solution.py:187
  150.4 31.7 %collective-permute-start.15 = (bf16[512,256]{1,0:T(8,128)(2,1)S(1)}, bf16[512,256]{1,0:T(8,128)(2,1)S(1)}, u32[]{:S(2)}, u32[]{:S(2)}) collective-permute-start(bf16[512,256]{1,0:T(8,128)(2,1)S(1)} %collective-permute-done.10.refs_6_), channel_id=1, source_target_pairs={{0,16},{1,17},{2,18},{3,19},{4,20},{5,21},{6,22},{7,23},{8,24},{9,... | collective-permute-start | bytes 786440 | tf_op jit(solution)/shard_map/ppermute | solution.py:187
  154.8 27.4 %collective-permute-start.16 = (bf16[512,256]{1,0:T(8,128)(2,1)S(1)}, bf16[512,256]{1,0:T(8,128)(2,1)S(1)}, u32[]{:S(2)}, u32[]{:S(2)}) collective-permute-start(bf16[512,256]{1,0:T(8,128)(2,1)S(1)} %broadcast_select_fusion.2.refs_7_), channel_id=1, source_target_pairs={{0,16},{1,17},{2,18},{3,19},{4,20},{5,21},{6,22},{7,23},{8,24},{9,... | collective-permute-start | bytes 786440 | tf_op jit(solution)/shard_map/ppermute | solution.py:187
  172.1 22.5 %collective-permute-start.38 = (bf16[256,256]{1,0:T(8,128)(2,1)S(1)}, bf16[256,256]{1,0:T(8,128)(2,1)S(1)}, u32[]{:S(2)}, u32[]{:S(2)}) collective-permute-start(bf16[256,256]{1,0:T(8,128)(2,1)S(1)} %get-tuple-element.56), channel_id=1, source_target_pairs={{0,4},{1,5},{2,6},{3,7},{4,0},{5,1},{6,2},{7,3},{8,12},{9,13},{10,... | collective-permute-start | bytes 393224 | tf_op jit(solution)/shard_map/ppermute | solution.py:187
  180.4 15.3 %collective-permute-start.40 = (bf16[256,256]{1,0:T(8,128)(2,1)S(1)}, bf16[256,256]{1,0:T(8,128)(2,1)S(1)}, u32[]{:S(2)}, u32[]{:S(2)}) collective-permute-start(bf16[256,256]{1,0:T(8,128)(2,1)S(1)} %get-tuple-element.58), channel_id=1, source_target_pairs={{0,8},{1,9},{2,10},{3,11},{4,12},{5,13},{6,14},{7,15},{8,0},{9,1},... | collective-permute-start | bytes 393224 | tf_op jit(solution)/shard_map/ppermute | solution.py:187
  181.4 14.3 %collective-permute-start.42 = (bf16[256,256]{1,0:T(8,128)(2,1)S(1)}, bf16[256,256]{1,0:T(8,128)(2,1)S(1)}, u32[]{:S(2)}, u32[]{:S(2)}) collective-permute-start(bf16[256,256]{1,0:T(8,128)(2,1)S(1)} %get-tuple-element.60), channel_id=1, source_target_pairs={{0,12},{1,13},{2,14},{3,15},{4,8},{5,9},{6,10},{7,11},{8,4},{9,5},... | collective-permute-start | bytes 393224 | tf_op jit(solution)/shard_map/ppermute | solution.py:187
  193.5 2.2 %collective-permute-start.37 = (bf16[256,256]{1,0:T(8,128)(2,1)S(1)}, bf16[256,256]{1,0:T(8,128)(2,1)S(1)}, u32[]{:S(2)}, u32[]{:S(2)}) collective-permute-start(bf16[256,256]{1,0:T(8,128)(2,1)S(1)} %get-tuple-element.55), channel_id=1, source_target_pairs={{0,4},{1,5},{2,6},{3,7},{4,0},{5,1},{6,2},{7,3},{8,12},{9,13},{10,... | collective-permute-start | bytes 393224 | tf_op jit(solution)/shard_map/ppermute | solution.py:187
  193.7 4.7 %collective-permute-start.39 = (bf16[256,256]{1,0:T(8,128)(2,1)S(1)}, bf16[256,256]{1,0:T(8,128)(2,1)S(1)}, u32[]{:S(2)}, u32[]{:S(2)}) collective-permute-start(bf16[256,256]{1,0:T(8,128)(2,1)S(1)} %get-tuple-element.57), channel_id=1, source_target_pairs={{0,8},{1,9},{2,10},{3,11},{4,12},{5,13},{6,14},{7,15},{8,0},{9,1},... | collective-permute-start | bytes 393224 | tf_op jit(solution)/shard_map/ppermute | solution.py:187
  194.6 7.1 %collective-permute-start.41 = (bf16[256,256]{1,0:T(8,128)(2,1)S(1)}, bf16[256,256]{1,0:T(8,128)(2,1)S(1)}, u32[]{:S(2)}, u32[]{:S(2)}) collective-permute-start(bf16[256,256]{1,0:T(8,128)(2,1)S(1)} %get-tuple-element.59), channel_id=1, source_target_pairs={{0,12},{1,13},{2,14},{3,15},{4,8},{5,9},{6,10},{7,11},{8,4},{9,5},... | collective-permute-start | bytes 393224 | tf_op jit(solution)/shard_map/ppermute | solution.py:187

commit v2 on v1

v2 whole, which is shorter than its diff:
```python
import functools

import jax
import jax.numpy as jnp
from jax import lax
from jax.experimental import pallas as pl
from jax.experimental.pallas import tpu as pltpu
from jax.sharding import PartitionSpec as P

HEAD_SIZE = 128
BLK = 128
MEMBERS = 4
META_ROWS = 16
FACTS = 2
AXES = ("seg", "fsdp")

VMEM = pl.BlockSpec(memory_space=pltpu.VMEM)
SMEM = pl.BlockSpec(memory_space=pltpu.SMEM)
HBM = pl.BlockSpec(memory_space=pl.ANY)


def call(body, outs, in_specs, flops=0, scratch=(), out_spec=VMEM, limit=28 << 20):
    return pl.pallas_call(
        body,
        out_shape=outs,
        in_specs=in_specs,
        out_specs=[out_spec] * len(outs),
        scratch_shapes=list(scratch),
        compiler_params=pltpu.CompilerParams(vmem_limit_bytes=limit),
        cost_estimate=pl.CostEstimate(flops=flops, bytes_accessed=4 << 20, transcendentals=0),
    )


def aligned(offset):
    return pl.multiple_of(offset, HEAD_SIZE)


def pack_body(
    group, early, here_ref, valid_ref, mask_ref, wq_ref, wk_ref, wv_ref, *refs
):
    outs, facts_ref, sems = refs[: 2 * MEMBERS], refs[-2], refs[-1]
    rows = wk_ref.shape[0]
    lane = lax.broadcasted_iota(jnp.int32, facts_ref.shape, 1)
    facts = jnp.where(lane == 0, valid_ref[0, 0], mask_ref[0, 0, 1, 0])
    facts_ref[...] = facts.astype(jnp.float32).astype(jnp.bfloat16)
    copies = []

    def copy(source, target):
        copies.append(pltpu.make_async_copy(source, target, sems.at[len(copies)]))
        copies[-1].start()

    for k in range(MEMBERS):
        head = here_ref[0] ^ k
        first, second = outs[2 * k : 2 * k + 2]
        at = aligned(head * HEAD_SIZE)
        wide = group * HEAD_SIZE
        copy(wk_ref.at[:, pl.ds(at, HEAD_SIZE)], first.at[pl.ds(0, rows), pl.ds(0, HEAD_SIZE)])
        copy(wv_ref.at[:, pl.ds(at, HEAD_SIZE)], first.at[pl.ds(0, rows), pl.ds(HEAD_SIZE, HEAD_SIZE)])
        if early:
            copy(
                wq_ref.at[:, pl.ds(aligned(head * wide), early * HEAD_SIZE)],
                first.at[pl.ds(0, rows), pl.ds(2 * HEAD_SIZE, early * HEAD_SIZE)],
            )
        copy(facts_ref, first.at[pl.ds(rows, META_ROWS), :])
        copy(
            wq_ref.at[:, pl.ds(aligned(head * wide + early * HEAD_SIZE), (group - early) * HEAD_SIZE)],
            second,
        )
    for one in copies:
        one.wait()


def columns_of(tokens_ref, offs_ref, piece):
    parts = [
        tokens_ref[:, pl.ds(aligned(offs_ref[piece * MEMBERS + k]), HEAD_SIZE)]
        for k in range(MEMBERS)
    ]
    return jnp.concatenate(parts, axis=1)


def project_body(n_segs, n_pieces, keep_last, offs_ref, *refs):
    tokens, pieces = refs[:n_segs], refs[n_segs : n_segs + n_pieces - 1]
    outs = refs[n_segs + n_pieces - 1 :]
    for n in range(n_segs):
        total = None
        for p in range(n_pieces - 1):
            term = jnp.dot(
                columns_of(tokens[n], offs_ref, p), pieces[p][...], preferred_element_type=jnp.float32
            )
            total = term if total is None else total + term
        outs[n][...] = total
        if keep_last:
            outs[n_segs + n][...] = columns_of(tokens[n], offs_ref, n_pieces - 1)


def sigma_plus(v):
    return jnp.where(v > 0, v + 1.0, jnp.exp(jnp.minimum(v, 0.0)))


def split(values):
    high = values.astype(jnp.bfloat16)
    return high, (values - high.astype(jnp.float32)).astype(jnp.bfloat16)


def kv_body(meta_ref, piece_ref, *refs):
    sums, lasts = refs[:MEMBERS], refs[MEMBERS : 2 * MEMBERS]
    outs = refs[2 * MEMBERS :]
    whole = None
    for seg in range(MEMBERS):
        total = sums[seg][...] + jnp.dot(
            lasts[seg][...], piece_ref[...], preferred_element_type=jnp.float32
        )
        kvq = total.astype(jnp.bfloat16)
        outs[2 * seg][...] = kvq
        length = kvq.shape[0]
        row = lax.broadcasted_iota(jnp.int32, (length, HEAD_SIZE), 0)
        keys = kvq[:, :HEAD_SIZE].astype(jnp.float32)
        sig = jnp.where(row < meta_ref[FACTS * seg], sigma_plus(keys), 0.0)
        wide = jnp.concatenate(
            [kvq[:, HEAD_SIZE : 2 * HEAD_SIZE], jnp.ones((length, HEAD_SIZE), jnp.bfloat16)], axis=1
        )
        high, low = split(sig)
        over = (((0,), (0,)), ((), ()))
        delta = lax.dot_general(high, wide, over, preferred_element_type=jnp.float32)
        delta += lax.dot_general(low, wide, over, preferred_element_type=jnp.float32)
        outs[2 * seg + 1][...] = delta
        whole = delta if whole is None else whole + delta
    outs[-1][...] = whole.astype(jnp.bfloat16)


def attend_body(
    segs, heads, first_head, group, ready, here_ref, meta_ref, gate_ref, base_ref, *refs
):
    kvqs, deltas = refs[:MEMBERS], refs[MEMBERS : 2 * MEMBERS]
    rest = refs[2 * MEMBERS :]
    n = len(segs)
    if not ready:
        piece, sums, lasts = rest[0], rest[1 : 1 + n], rest[1 + n : 1 + 2 * n]
        rest = rest[1 + 2 * n :]
    outs = rest
    me = here_ref[0]
    for at, seg in enumerate(segs):
        if ready:
            queries = kvqs[seg][:, 2 * HEAD_SIZE : (2 + heads) * HEAD_SIZE]
        else:
            queries = (
                sums[at][...]
                + jnp.dot(lasts[at][...], piece[...], preferred_element_type=jnp.float32)
            ).astype(jnp.bfloat16)
        length = queries.shape[0]
        blocks = length // BLK
        valid = meta_ref[FACTS * seg]
        seen = meta_ref[FACTS * seg + 1] == 1

        memory = base_ref[...].astype(jnp.float32)
        for other in range(MEMBERS):
            if other != seg:
                earlier = jnp.where((me ^ other) < (me ^ seg), 1.0, 0.0)
                memory = memory + earlier * deltas[other][...]
        mem_high, mem_low = split(memory)

        for block in range(blocks):
            span = slice(block * BLK, (block + 1) * BLK)
            stacked = jnp.concatenate(
                [queries[span, h * HEAD_SIZE : (h + 1) * HEAD_SIZE] for h in range(heads)], axis=0
            )
            width = (block + 1) * BLK
            keys = kvqs[seg][0:width, :HEAD_SIZE]
            values = kvqs[seg][0:width, HEAD_SIZE : 2 * HEAD_SIZE]
            scores = lax.dot_general(
                stacked, keys, (((1,), (1,)), ((), ())), preferred_element_type=jnp.float32
            ) * HEAD_SIZE ** (-0.5)
            i = lax.broadcasted_iota(jnp.int32, (BLK, width), 0) + block * BLK
            j = lax.broadcasted_iota(jnp.int32, (BLK, width), 1)
            allowed = (j <= i) & (j < valid)
            if block:
                allowed = allowed & ((j >= block * BLK) | seen)
            allowed = jnp.concatenate([jnp.where(allowed, 0.0, -1e30)] * heads, axis=0)
            masked = jnp.where(allowed < 0, -1e30, scores)
            top = jnp.max(masked, axis=-1, keepdims=True)
            expo = jnp.exp(masked - top)
            total = jnp.maximum(jnp.sum(expo, axis=-1, keepdims=True), 1.0)
            weights = (expo / total).astype(jnp.bfloat16)
            local = jnp.dot(weights, values, preferred_element_type=jnp.float32)

            high, low = split(sigma_plus(stacked.astype(jnp.float32)))
            numer = jnp.dot(high, mem_high, preferred_element_type=jnp.float32)
            numer += jnp.dot(high, mem_low, preferred_element_type=jnp.float32)
            numer += jnp.dot(low, mem_high, preferred_element_type=jnp.float32)
            retrieved = numer[:, :HEAD_SIZE] / (numer[:, HEAD_SIZE:] + 1.0)
            live = lax.broadcasted_iota(jnp.int32, (BLK, HEAD_SIZE), 0) + block * BLK < valid
            for h in range(heads):
                part = slice(h * BLK, (h + 1) * BLK)
                logit = jnp.full((1, HEAD_SIZE), gate_ref[me * group + first_head + h], jnp.float32)
                gate = 1.0 / (1.0 + jnp.exp(-logit))
                mixed = gate * retrieved[part] + (1.0 - gate) * local[part]
                outs[at][span, h * HEAD_SIZE : (h + 1) * HEAD_SIZE] = jnp.where(
                    live, mixed, 0.0
                ).astype(jnp.bfloat16)


def assemble_body(group, widths, here_ref, *refs):
    parts, out = refs[:-1], refs[-1]
    for k in range(MEMBERS):
        at = (here_ref[0] ^ k) * group * HEAD_SIZE
        for c, width in enumerate(widths):
            out[:, pl.ds(aligned(at), width)] = parts[len(widths) * k + c][...]
            at = at + width


def after(array, *others):
    return lax.optimization_barrier((array,) + others)[0]


def shards(sizes, tokens, w_query, w_key, value_weight, gate_bias, block_mask, valid_len):
    n_seg, n_z = sizes
    n_groups = n_seg // MEMBERS
    heads_kv = w_key.shape[1] // HEAD_SIZE
    group = w_query.shape[1] // w_key.shape[1]
    early = group // 2
    rows = w_query.shape[0]
    length, width = tokens.shape[1], tokens.shape[2]
    assert heads_kv == MEMBERS and length == 2 * BLK
    seg = lax.axis_index("seg")
    z = lax.axis_index("fsdp")
    g, m = seg // MEMBERS, seg % MEMBERS
    here = jnp.reshape(m, (1,)).astype(jnp.int32)
    bf16, f32 = jnp.bfloat16, jnp.float32
    shape = jax.ShapeDtypeStruct

    def permute(array, to):
        pairs = []
        for gg in range(n_groups):
            for mm in range(MEMBERS):
                for zz in range(n_z):
                    target = to(gg, mm, zz)
                    if target is not None:
                        index = lambda t: (t[0] * MEMBERS + t[1]) * n_z + t[2]
                        pairs.append((index((gg, mm, zz)), index(target)))
        return lax.ppermute(array, AXES, pairs)

    def to_member(array, k):
        return permute(array, lambda gg, mm, zz: (gg, mm ^ k, zz))

    wide = [(2 + early) * HEAD_SIZE, (group - early) * HEAD_SIZE]
    packed = call(
        functools.partial(pack_body, group, early),
        [shape((rows + META_ROWS, wide[0]), bf16), shape((rows, wide[1]), bf16)] * MEMBERS,
        [SMEM] * 3 + [HBM] * 3,
        scratch=[pltpu.VMEM((META_ROWS, wide[0]), bf16), pltpu.SemaphoreType.DMA((5 * MEMBERS,))],
        out_spec=HBM,
    )(here, valid_len, block_mask, w_query, w_key, value_weight)
    order = (2, 3, 1)
    first = {0: packed[0]}
    second = {0: packed[1]}
    for k in order:
        first[k] = to_member(packed[2 * k], k)
    for k in order:
        second[k] = to_member(packed[2 * k + 1], k)
    meta = jnp.concatenate([first[k][rows, :FACTS] for k in range(MEMBERS)]).astype(jnp.int32)

    own = after(tokens[0], first[2], first[3])
    across = to_member(own, 2)
    sibling = to_member(own, 1)
    diagonal = to_member(across, 1)
    books = [tokens[0], sibling, across, diagonal]

    def gathered(piece):
        if n_groups == 2 and n_z == 4:
            inside = (z == 1) | (z == 2)
            over = lambda part: permute(part, lambda gg, mm, zz: (gg ^ 1, mm, zz))
            outward = lambda part: permute(
                part, lambda gg, mm, zz: (gg, mm, zz ^ 1) if zz in (1, 2) else None
            )
            inward = lambda part: permute(
                part, lambda gg, mm, zz: (gg, mm, zz ^ 3) if zz in (1, 2) else None
            )
            one = permute(piece, lambda gg, mm, zz: (gg, mm, zz ^ 1))
            inner = inward(piece)
            far = [over(piece)]
            middle = inward(one)
            outer = outward(inner)
            far.append(over(one))
            two = jnp.where(inside, inner, outer)
            last = outward(middle)
            far.append(over(two))
            three = jnp.where(inside, middle, last)
            far.append(over(three))
            return [piece, one, two, three] + far
        index = lambda gg, mm, zz: (gg * MEMBERS + mm) * n_z + zz
        everything = lax.all_gather(
            piece,
            AXES,
            axis_index_groups=[
                [index(gg, mm, zz) for gg in range(n_groups) for zz in range(n_z)]
                for mm in range(MEMBERS)
            ],
        )
        columns = piece.shape[1]
        natural = everything.reshape(n_groups, n_z, MEMBERS, rows, columns)
        members = jnp.arange(MEMBERS, dtype=jnp.int32) ^ m
        natural = jnp.take(natural, members, axis=2).transpose(0, 2, 1, 3, 4)
        return list(natural.reshape(-1, MEMBERS * HEAD_SIZE, columns))

    if n_groups == 2 and n_z == 4:
        assert rows == HEAD_SIZE
        n_pieces = n_groups * n_z
        inside = (z == 1) | (z == 2)
        steps = jnp.stack([z, z ^ 1, jnp.where(inside, z ^ 3, z ^ 2), jnp.where(inside, z ^ 2, z ^ 3)])
        a, b, k = jnp.meshgrid(
            jnp.arange(n_groups), jnp.arange(n_z), jnp.arange(MEMBERS), indexing="ij"
        )
        offs = ((((g ^ a) * MEMBERS + (m ^ k)) * n_z + steps[b]) * rows).reshape(-1).astype(jnp.int32)
    else:
        n_pieces = width // (MEMBERS * HEAD_SIZE)
        offs = jnp.arange(n_pieces * MEMBERS, dtype=jnp.int32) * HEAD_SIZE

    chunks = [
        gathered(jnp.concatenate([part[k][:rows] for k in range(MEMBERS)], axis=0))
        for part in (first, second)
    ]

    sums, lasts = [[], []], []
    for c in range(2):
        for segs in ((0, 1), (2, 3)):
            n = len(segs)
            found = call(
                functools.partial(project_body, n, n_pieces, c == 0),
                [shape((length, wide[c]), f32)] * n
                + [shape((length, MEMBERS * HEAD_SIZE), bf16)] * (n if c == 0 else 0),
                [SMEM] + [VMEM] * (n + n_pieces - 1),
                flops=2 * n * length * width * wide[c],
            )(offs, *[books[s] for s in segs], *chunks[c][:-1])
            sums[c] += found[:n]
            lasts += found[n:]

    found = call(
        kv_body,
        [shape((length, wide[0]), bf16), shape((HEAD_SIZE, 2 * HEAD_SIZE), f32)] * MEMBERS
        + [shape((HEAD_SIZE, 2 * HEAD_SIZE), bf16)],
        [SMEM] + [VMEM] * (1 + 2 * MEMBERS),
        flops=2 * MEMBERS * length * MEMBERS * HEAD_SIZE * wide[0],
    )(meta, chunks[0][-1], *sums[0], *lasts)
    kvqs, deltas, total = found[0:-1:2], found[1:-1:2], found[-1]

    base = None
    for a in range(1, n_groups):
        term = permute(total, lambda gg, mm, zz: (gg ^ a, mm, zz) if gg < gg ^ a else None)
        base = term if base is None else base.astype(f32) + term.astype(f32)

    sent = {}

    def attend(c, segs):
        heads = wide[c] // HEAD_SIZE - (0 if c else 2)
        extra = [] if c == 0 else [chunks[1][-1], *[sums[1][s] for s in segs], *[lasts[s] for s in segs]]
        attended = call(
            functools.partial(attend_body, segs, heads, c * early, group, c == 0),
            [shape((length, heads * HEAD_SIZE), bf16)] * len(segs),
            [SMEM] * 3 + [VMEM] * (1 + 2 * MEMBERS + len(extra)),
            flops=2 * len(segs) * length * length * HEAD_SIZE * heads * 3,
        )(here, meta, gate_bias, base, *kvqs, *deltas, *extra)
        for seg_at, part in zip(segs, attended):
            sent[c, seg_at] = to_member(part, seg_at) if seg_at else part

    attend(0, (2, 3))
    attend(0, (1, 0))
    attend(1, (2, 3))
    attend(1, (1, 0))
    (output,) = call(
        functools.partial(assemble_body, group, (early * HEAD_SIZE, wide[1])),
        [shape((length, w_query.shape[1]), bf16)],
        [SMEM] + [VMEM] * (2 * MEMBERS),
    )(here, *[sent[c, k] for k in range(MEMBERS) for c in range(2)])
    return output[None]


def solution(mesh):
    in_specs = (
        P("fsdp", "seg", None),
        P(("seg", "fsdp"), None),
        P(("seg", "fsdp"), None),
        P(("seg", "fsdp"), None),
        P(),
        P("fsdp", "seg", None, None),
        P("fsdp", "seg"),
    )
    out_specs = P("fsdp", "seg", None)
    body = functools.partial(shards, (mesh.shape["seg"], mesh.shape["fsdp"]))
    return jax.shard_map(body, mesh=mesh, in_specs=in_specs, out_specs=out_specs, check_vma=False)
```

time: 204 us -> 204 us (level); the launches traced: 203 us -> 200 us
  waiting for transfers between devices: 97.1 us -> 111 us
  starting transfers between devices: 60.2 us -> 47.6 us
  Pallas kernels: 34.5 us -> 27.3 us
  other arithmetic: 0.39 us -> 4.08 us
    ppermute x43 -> x34, waiting for transfers between devices: 97.1 us -> 111 us  [permute(): return lax.ppermute(array, AXES, pairs)]
    ppermute x43 -> x34, starting transfers between devices: 60.2 us -> 47.6 us  [permute(): return lax.ppermute(array, AXES, pairs)]
    pallas_call x6 -> x11, Pallas kernels: 34.5 us -> 27.3 us  [the longest x4 14.6 us: shards(): call(functools.partial(project_body, n, n_pieces, c == 0), [shape((length...]
    unnamed x30 -> x19, local copies, waits for them, and re-layouts: 6.79 us -> 3.55 us
  transfers between devices with their start and end apart: 43 -> 34, of which waited for: 18 -> 19; matrix products, arithmetic and copies ran while one was open for 2% -> 5% of each run, Pallas kernels for 16% -> 11%
where the time goes in v2:
time: 204 us; the launch traced here: 200 us
  waiting for transfers between devices  111 us (54%)
  starting transfers between devices  47.6 us (23%)
  Pallas kernels  27.3 us (13%)
  local copies, waits for them, and re-layouts  9.37 us (5%)
  other arithmetic  4.08 us (2%)
    ppermute x34, waiting for transfers between devices, permute(): return lax.ppermute(array, AXES, pairs)  111 us
    ppermute x34, starting transfers between devices, permute(): return lax.ppermute(array, AXES, pairs)  47.6 us
    pallas_call x4, Pallas kernels, shards(): call(functools.partial(project_body, n, n_pieces, c == 0), [shape((length...  14.6 us
    pallas_call x4, Pallas kernels, attend(): call(functools.partial(attend_body, segs, heads, c * early, group, c == 0...  8.81 us
  transfers between devices with their start and end apart: 34, of which 19 were waited for; matrix products, arithmetic and copies ran while one was open for 5% of the time, Pallas kernels for 11%

profile of v2, /device:TPU:9, one launch (start us, length us, event | category | flops | bytes accessed | tf_op | source)
XLA Modules:
  0.0 200.3 jit_solution(11128066260460832383)
XLA Ops:
  0.7 1.0 copy-done.1
  1.7 0.9 copy-done.2
  2.6 0.9 copy-done.3
  4.2 1.0 shard_map.73
  5.2 1.3 collective-permute-start.1
  6.5 1.1 collective-permute-start.2
  7.6 2.4 %collective-permute-done.1 = bf16[144,512]{1,0:T(8,128)(2,1)S(1)} collective-permute-done((bf16[144,512]{1,0:T(8,128)(2,1)S(1)}, bf16[144,512]{1,0:T(8,128)(2,1)S(1)}, u32[]{:S(2)}, u32[]{:S(2)}) %collective-permute-start.1) | collective-permute-done | bytes 147488 | tf_op jit(solution)/shard_map/ppermute | solution.py:240
  10.0 4.0 %collective-permute-done.2 = bf16[144,512]{1,0:T(8,128)(2,1)S(1)} collective-permute-done((bf16[144,512]{1,0:T(8,128)(2,1)S(1)}, bf16[144,512]{1,0:T(8,128)(2,1)S(1)}, u32[]{:S(2)}, u32[]{:S(2)}) %collective-permute-start.2) | collective-permute-done | bytes 147488 | tf_op jit(solution)/shard_map/ppermute | solution.py:240
  14.0 1.2 collective-permute-start.13
  15.5 1.9 collective-permute-start.18
  18.1 45.0 %collective-permute-done.17 = bf16[128,256]{1,0:T(8,128)(2,1)S(1)} collective-permute-done((bf16[128,256]{1,0:T(8,128)(2,1)S(1)}, bf16[128,256]{1,0:T(8,128)(2,1)S(1)}, u32[]{:S(2)}, u32[]{:S(2)}) %collective-permute-start.17) | collective-permute-done | bytes 65568 | tf_op jit(solution)/shard_map/ppermute | solution.py:240
  63.1 1.4 collective-permute-done.18
  64.6 0.7 gather_fusion
  65.3 0.7 reshape.17
  66.1 0.9 slice.37
  67.1 1.5 collective-permute-start.3
  68.6 3.2 %collective-permute-start.23 = (bf16[512,256]{1,0:T(8,128)(2,1)S(1)}, bf16[512,256]{1,0:T(8,128)(2,1)S(1)}, u32[]{:S(2)}, u32[]{:S(2)}) collective-permute-start(bf16[512,256]{1,0:T(8,128)(2,1)S(1)} %constant_dynamic-update-slice_fusion.refs_2_), channel_id=1, source_target_pairs={{1,2},{2,1},{5,6},{6,5},{9,10},{10,9},{13,14},{14,13},{17,18},{18,... | collective-permute-start | bytes 786440 | tf_op jit(solution)/shard_map/ppermute | solution.py:240
  71.8 2.1 %collective-permute-start.8 = (bf16[512,512]{1,0:T(8,128)(2,1)S(1)}, bf16[512,512]{1,0:T(8,128)(2,1)}, u32[]{:S(2)}, u32[]{:S(2)}) collective-permute-start(bf16[512,512]{1,0:T(8,128)(2,1)S(1)} %pad_maximum_fusion.refs_2_), channel_id=1, source_target_pairs={{1,2},{2,1},{5,6},{6,5},{9,10},{10,9},{13,14},{14,13},{17,18},{18,... | collective-permute-start | bytes 1572872 | tf_op jit(solution)/shard_map/ppermute | solution.py:240
  73.9 1.6 collective-permute-start.7
  75.5 1.4 add_multiply_fusion
  77.4 0.8 reshape.15.offs_ref
  78.2 3.2 %collective-permute-start.20 = (bf16[512,256]{1,0:T(8,128)(2,1)S(1)}, bf16[512,256]{1,0:T(8,128)(2,1)S(1)}, u32[]{:S(2)}, u32[]{:S(2)}) collective-permute-start(bf16[512,256]{1,0:T(8,128)(2,1)S(1)} %collective-permute-done.19.refs_3_), channel_id=1, source_target_pairs={{1,2},{2,1},{5,6},{6,5},{9,10},{10,9},{13,14},{14,13},{17,18},{18,... | collective-permute-start | bytes 786440 | tf_op jit(solution)/shard_map/ppermute | solution.py:240
  81.4 2.0 collective-permute-done.3.refs_3_
  83.4 3.2 %collective-permute-start.4 = (bf16[512,512]{1,0:T(8,128)(2,1)}, bf16[512,512]{1,0:T(8,128)(2,1)S(1)}, u32[]{:S(2)}, u32[]{:S(2)}) collective-permute-start(bf16[512,512]{1,0:T(8,128)(2,1)} %collective-permute-done.3.refs_3_), channel_id=1, source_target_pairs={{1,2},{2,1},{5,6},{6,5},{9,10},{10,9},{13,14},{14,13},{17,18},{18,... | collective-permute-start | bytes 1572872 | tf_op jit(solution)/shard_map/ppermute | solution.py:240
  86.6 0.7 slice_bitcast_fusion
  87.2 1.4 collective-permute-done.8
  88.7 1.3 collective-permute-start.9
  90.0 0.7 slice_bitcast_fusion.1
  90.7 3.5 %collective-permute-done.20 = bf16[512,256]{1,0:T(8,128)(2,1)S(1)} collective-permute-done((bf16[512,256]{1,0:T(8,128)(2,1)S(1)}, bf16[512,256]{1,0:T(8,128)(2,1)S(1)}, u32[]{:S(2)}, u32[]{:S(2)}) %collective-permute-start.20) | collective-permute-done | bytes 262176 | tf_op jit(solution)/shard_map/ppermute | solution.py:240
  94.2 1.2 collective-permute-start.10
  95.4 0.7 slice_bitcast_fusion.2
  96.1 9.3 %collective-permute-done.4 = bf16[512,512]{1,0:T(8,128)(2,1)S(1)} collective-permute-done((bf16[512,512]{1,0:T(8,128)(2,1)}, bf16[512,512]{1,0:T(8,128)(2,1)S(1)}, u32[]{:S(2)}, u32[]{:S(2)}) %collective-permute-start.4) | collective-permute-done | bytes 524320 | tf_op jit(solution)/shard_map/ppermute | solution.py:240
  105.4 1.3 collective-permute-start.5
  106.7 0.7 maximum_convert_fusion.meta_ref
  107.5 1.3 collective-permute-start.24
  108.8 1.1 broadcast_select_fusion.refs_4_
  109.9 12.0 %collective-permute-done.24 = bf16[512,256]{1,0:T(8,128)(2,1)S(1)} collective-permute-done((bf16[512,256]{1,0:T(8,128)(2,1)S(1)}, bf16[512,256]{1,0:T(8,128)(2,1)S(1)}, u32[]{:S(2)}, u32[]{:S(2)}) %collective-permute-start.24) | collective-permute-done | bytes 262176 | tf_op jit(solution)/shard_map/ppermute | solution.py:240
  121.9 1.2 collective-permute-start.11
  123.4 4.1 %collective-permute-start.21 = (bf16[512,256]{1,0:T(8,128)(2,1)S(1)}, bf16[512,256]{1,0:T(8,128)(2,1)S(1)}, u32[]{:S(2)}, u32[]{:S(2)}) collective-permute-start(bf16[512,256]{1,0:T(8,128)(2,1)S(1)} %collective-permute-done.20), channel_id=1, source_target_pairs={{1,0},{2,3},{5,4},{6,7},{9,8},{10,11},{13,12},{14,15},{17,16},{18,... | collective-permute-start | bytes 786440 | tf_op jit(solution)/shard_map/ppermute | solution.py:240
  127.6 3.2 %collective-permute-done.21 = bf16[512,256]{1,0:T(8,128)(2,1)S(1)} collective-permute-done((bf16[512,256]{1,0:T(8,128)(2,1)S(1)}, bf16[512,256]{1,0:T(8,128)(2,1)S(1)}, u32[]{:S(2)}, u32[]{:S(2)}) %collective-permute-start.21) | collective-permute-done | bytes 262176 | tf_op jit(solution)/shard_map/ppermute | solution.py:240
  130.9 1.2 collective-permute-start.6
  132.1 0.9 collective-permute-done.11.refs_7_
  133.0 1.2 collective-permute-start.25
  134.3 10.0 %collective-permute-done.12.refs_8_ = bf16[512,512]{1,0:T(8,128)(2,1)S(1)} collective-permute-done((bf16[512,512]{1,0:T(8,128)(2,1)S(1)}, bf16[512,512]{1,0:T(8,128)(2,1)S(1)}, u32[]{:S(2)}, u32[]{:S(2)}) %collective-permute-start.12) | collective-permute-done | bytes 524320 | tf_op jit(solution)/shard_map/ppermute | solution.py:240
  144.3 1.2 collective-permute-start.26
  145.8 3.9 %shard_map.74 = (f32[256,512]{1,0:T(8,128)S(1)}, f32[256,512]{1,0:T(8,128)S(1)}, bf16[256,512]{1,0:T(8,128)(2,1)S(1)}, bf16[256,512]{1,0:T(8,128)(2,1)S(1)}) custom-call(s32[32]{0:T(128)S(1)} %reshape.15.offs_ref, bf16[256,4096]{1,0:T(8,128)(2,1)S(1)} %bitcast.17, bf16[256,4096]{1,0:T(8,128)(2,1)} %collective-permute-done.7.refs_1_, ...), custom_call_target="tpu_custom_call" | custom-call | flops 2147483648 | bytes 4194304 | tf_op jit(solution)/shard_map/pallas_call | solution.py:327
  149.6 1.3 collective-permute-start.22
  150.9 4.5 %shard_map.75 = (f32[256,512]{1,0:T(8,128)S(1)}, f32[256,512]{1,0:T(8,128)S(1)}, bf16[256,512]{1,0:T(8,128)(2,1)S(1)}, bf16[256,512]{1,0:T(8,128)(2,1)S(1)}) custom-call(s32[32]{0:T(128)S(1)} %reshape.15.offs_ref, bf16[256,4096]{1,0:T(8,128)(2,1)} %collective-permute-done.13.refs_0_, bf16[256,4096]{1,0:T(8,128)(2,1)} %collective-permute-done.14.refs_1_, ...), custom_call_target="tpu_custom_call" | custom-call | flops 2147483648 | bytes 4194304 | tf_op jit(solution)/shard_map/pallas_call | solution.py:327
  155.5 1.8 shard_map.76
  157.3 3.3 %collective-permute-start.15 = (bf16[128,256]{1,0:T(8,128)(2,1)S(1)}, bf16[128,256]{1,0:T(8,128)(2,1)S(1)}, u32[]{:S(2)}, u32[]{:S(2)}) collective-permute-start(bf16[128,256]{1,0:T(8,128)(2,1)S(1)} %get-tuple-element.56), channel_id=1, source_target_pairs={{0,16},{1,17},{2,18},{3,19},{4,20},{5,21},{6,22},{7,23},{8,24},{9,... | collective-permute-start | bytes 196616 | tf_op jit(solution)/shard_map/ppermute | solution.py:240
  161.1 5.6 %collective-permute-done.26.refs_7_ = bf16[512,256]{1,0:T(8,128)(2,1)S(1)} collective-permute-done((bf16[512,256]{1,0:T(8,128)(2,1)S(1)}, bf16[512,256]{1,0:T(8,128)(2,1)S(1)}, u32[]{:S(2)}, u32[]{:S(2)}) %collective-permute-start.26) | collective-permute-done | bytes 262176 | tf_op jit(solution)/shard_map/ppermute | solution.py:240
  166.8 5.6 %collective-permute-done.27.refs_8_ = bf16[512,256]{1,0:T(8,128)(2,1)S(1)} collective-permute-done((bf16[512,256]{1,0:T(8,128)(2,1)S(1)}, bf16[512,256]{1,0:T(8,128)(2,1)S(1)}, u32[]{:S(2)}, u32[]{:S(2)}) %collective-permute-start.27) | collective-permute-done | bytes 262176 | tf_op jit(solution)/shard_map/ppermute | solution.py:240
  172.4 3.4 %shard_map.81 = (f32[256,256]{1,0:T(8,128)S(1)}, f32[256,256]{1,0:T(8,128)S(1)}) custom-call(s32[32]{0:T(128)S(1)} %reshape.15.offs_ref, bf16[256,4096]{1,0:T(8,128)(2,1)} %collective-permute-done.13.refs_0_, bf16[256,4096]{1,0:T(8,128)(2,1)} %collective-permute-done.14.refs_1_, bf16[512,256]{1,0:T(8,128)(2,1)S(1)} %constant_dynamic-update-slice_fusion.refs_2_, ...), custom_call_target="tpu_custom_call" | custom-call | flops 1073741824 | bytes 4194304 | tf_op jit(solution)/shard_map/pallas_call | solution.py:327
  175.8 2.2 %collective-permute-done.22.refs_8_ = bf16[512,256]{1,0:T(8,128)(2,1)S(1)} collective-permute-done((bf16[512,256]{1,0:T(8,128)(2,1)S(1)}, bf16[512,256]{1,0:T(8,128)(2,1)S(1)}, u32[]{:S(2)}, u32[]{:S(2)}) %collective-permute-start.22) | collective-permute-done | bytes 262176 | tf_op jit(solution)/shard_map/ppermute | solution.py:240
  178.4 2.5 %shard_map.82 = (bf16[256,256]{1,0:T(8,128)(2,1)S(1)}, bf16[256,256]{1,0:T(8,128)(2,1)S(1)}) custom-call(s32[1]{0:T(128)} %bitcast.here_ref, s32[8]{0:T(128)S(1)} %maximum_convert_fusion.meta_ref, f32[16]{0:T(128)S(1)} %copy-done.4, bf16[128,256]{1,0:T(8,128)(2,1)S(1)} %collective-permute-done.15.base_ref, bf16[256,512]{1,0:T(8,128)(2,1)S(1)} %get-tuple-element.57.refs_0_, ...), custom_call_target="tpu_custom_call" | custom-call | flops 201326592 | bytes 4194304 | tf_op jit(solution)/shard_map/pallas_call | solution.py:356
  181.0 1.4 collective-permute-start.31
  182.4 2.8 %shard_map.78 = (f32[256,256]{1,0:T(8,128)S(1)}, f32[256,256]{1,0:T(8,128)S(1)}) custom-call(s32[32]{0:T(128)S(1)} %reshape.15.offs_ref, bf16[256,4096]{1,0:T(8,128)(2,1)S(1)} %bitcast.18, bf16[256,4096]{1,0:T(8,128)(2,1)} %collective-permute-done.7.refs_1_, bf16[512,256]{1,0:T(8,128)(2,1)S(1)} %constant_dynamic-update-slice_fusion.refs_2_, ...), custom_call_target="tpu_custom_call" | custom-call | flops 1073741824 | bytes 4194304 | tf_op jit(solution)/shard_map/pallas_call | solution.py:327
  185.2 4.0 %collective-permute-start.33 = (bf16[256,256]{1,0:T(8,128)(2,1)S(1)}, bf16[256,256]{1,0:T(8,128)(2,1)S(1)}, u32[]{:S(2)}, u32[]{:S(2)}) collective-permute-start(bf16[256,256]{1,0:T(8,128)(2,1)S(1)} %get-tuple-element.80), channel_id=1, source_target_pairs={{0,12},{1,13},{2,14},{3,15},{4,8},{5,9},{6,10},{7,11},{8,4},{9,5},... | collective-permute-start | bytes 393224 | tf_op jit(solution)/shard_map/ppermute | solution.py:240
  189.2 1.9 shard_map.80
  191.1 1.4 collective-permute-start.30
  192.8 2.5 %shard_map.79 = (bf16[256,256]{1,0:T(8,128)(2,1)S(1)}, bf16[256,256]{1,0:T(8,128)(2,1)S(1)}) custom-call(s32[1]{0:T(128)} %bitcast.here_ref, s32[8]{0:T(128)S(1)} %maximum_convert_fusion.meta_ref, f32[16]{0:T(128)S(1)} %copy-done.4, bf16[128,256]{1,0:T(8,128)(2,1)S(1)} %collective-permute-done.15.base_ref, bf16[256,512]{1,0:T(8,128)(2,1)S(1)} %get-tuple-element.57.refs_0_, ...), custom_call_target="tpu_custom_call" | custom-call | flops 201326592 | bytes 4194304 | tf_op jit(solution)/shard_map/pallas_call | solution.py:356
  195.6 1.9 shard_map.77
  197.9 1.3 collective-permute-done.32.refs_6_
  199.2 1.1 shard_map.83
  (59 shorter events, 5.0 us)
Async XLA Ops:
  0.7 1.0 copy-start.1
  1.7 0.9 copy-start.2
  2.6 0.9 copy-start.3
  3.5 0.7 copy-start.5
  5.2 4.8 %collective-permute-start.1 = (bf16[144,512]{1,0:T(8,128)(2,1)S(1)}, bf16[144,512]{1,0:T(8,128)(2,1)S(1)}, u32[]{:S(2)}, u32[]{:S(2)}) collective-permute-start(bf16[144,512]{1,0:T(8,128)(2,1)S(1)} %get-tuple-element.45), channel_id=1, source_target_pairs={{0,8},{1,9},{2,10},{3,11},{4,12},{5,13},{6,14},{7,15},{8,0},{9,1},... | collective-permute-start | bytes 442376 | tf_op jit(solution)/shard_map/ppermute | solution.py:240
  6.5 7.5 %collective-permute-start.2 = (bf16[144,512]{1,0:T(8,128)(2,1)S(1)}, bf16[144,512]{1,0:T(8,128)(2,1)S(1)}, u32[]{:S(2)}, u32[]{:S(2)}) collective-permute-start(bf16[144,512]{1,0:T(8,128)(2,1)S(1)} %get-tuple-element.46), channel_id=1, source_target_pairs={{0,12},{1,13},{2,14},{3,15},{4,8},{5,9},{6,10},{7,11},{8,4},{9,5},... | collective-permute-start | bytes 442376 | tf_op jit(solution)/shard_map/ppermute | solution.py:240
  10.0 56.0 %copy-start.6 = (bf16[144,512]{1,0:T(8,128)(2,1)}, bf16[144,512]{1,0:T(8,128)(2,1)S(1)}, u32[]{:S(2)}) copy-start(bf16[144,512]{1,0:T(8,128)(2,1)S(1)} %collective-permute-done.1) | copy-start | bytes 442372
  14.0 52.0 %copy-start.7 = (bf16[144,512]{1,0:T(8,128)(2,1)}, bf16[144,512]{1,0:T(8,128)(2,1)S(1)}, u32[]{:S(2)}) copy-start(bf16[144,512]{1,0:T(8,128)(2,1)S(1)} %collective-permute-done.2) | copy-start | bytes 442372
  14.0 62.8 %collective-permute-start.13 = (bf16[256,4096]{1,0:T(8,128)(2,1)}, bf16[256,4096]{1,0:T(8,128)(2,1)}, u32[]{:S(2)}, u32[]{:S(2)}) collective-permute-start(bf16[256,4096]{1,0:T(8,128)(2,1)} %bitcast.15), channel_id=1, source_target_pairs={{0,8},{1,9},{2,10},{3,11},{4,12},{5,13},{6,14},{7,15},{8,0},{9,1},... | collective-permute-start | bytes 6291464 | tf_op jit(solution)/shard_map/ppermute | solution.py:240
  15.2 2.9 %collective-permute-start.16 = (bf16[128,256]{1,0:T(8,128)(2,1)S(1)}, bf16[128,256]{1,0:T(8,128)(2,1)S(1)}, u32[]{:S(2)}, u32[]{:S(2)}) collective-permute-start(bf16[128,256]{1,0:T(8,128)(2,1)S(1)} %get-tuple-element.67), channel_id=1, source_target_pairs={{0,4},{1,5},{2,6},{3,7},{4,0},{5,1},{6,2},{7,3},{8,12},{9,13},{10,... | collective-permute-start | bytes 196616 | tf_op jit(solution)/shard_map/ppermute | solution.py:240
  15.2 47.9 %collective-permute-start.17 = (bf16[128,256]{1,0:T(8,128)(2,1)S(1)}, bf16[128,256]{1,0:T(8,128)(2,1)S(1)}, u32[]{:S(2)}, u32[]{:S(2)}) collective-permute-start(bf16[128,256]{1,0:T(8,128)(2,1)S(1)} %get-tuple-element.68), channel_id=1, source_target_pairs={{0,8},{1,9},{2,10},{3,11},{4,12},{5,13},{6,14},{7,15},{8,0},{9,1},... | collective-permute-start | bytes 196616 | tf_op jit(solution)/shard_map/ppermute | solution.py:240
  15.5 49.0 %collective-permute-start.18 = (bf16[128,256]{1,0:T(8,128)(2,1)S(1)}, bf16[128,256]{1,0:T(8,128)(2,1)S(1)}, u32[]{:S(2)}, u32[]{:S(2)}) collective-permute-start(bf16[128,256]{1,0:T(8,128)(2,1)S(1)} %get-tuple-element.69), channel_id=1, source_target_pairs={{0,12},{1,13},{2,14},{3,15},{4,8},{5,9},{6,10},{7,11},{8,4},{9,5},... | collective-permute-start | bytes 196616 | tf_op jit(solution)/shard_map/ppermute | solution.py:240
  17.4 48.7 %collective-permute-start = (bf16[144,512]{1,0:T(8,128)(2,1)S(1)}, bf16[144,512]{1,0:T(8,128)(2,1)}, u32[]{:S(2)}, u32[]{:S(2)}) collective-permute-start(bf16[144,512]{1,0:T(8,128)(2,1)S(1)} %get-tuple-element.44), channel_id=1, source_target_pairs={{0,4},{1,5},{2,6},{3,7},{4,0},{5,1},{6,2},{7,3},{8,12},{9,13},{10,... | collective-permute-start | bytes 442376 | tf_op jit(solution)/shard_map/ppermute | solution.py:240
  64.5 9.3 %collective-permute-start.19 = (bf16[512,256]{1,0:T(8,128)(2,1)S(1)}, bf16[512,256]{1,0:T(8,128)(2,1)S(1)}, u32[]{:S(2)}, u32[]{:S(2)}) collective-permute-start(bf16[512,256]{1,0:T(8,128)(2,1)S(1)} %constant_dynamic-update-slice_fusion.refs_2_), channel_id=1, source_target_pairs={{0,1},{1,0},{2,3},{3,2},{4,5},{5,4},{6,7},{7,6},{8,9},{9,8},{10,11... | collective-permute-start | bytes 786440 | tf_op jit(solution)/shard_map/ppermute | solution.py:240
  65.3 8.6 %copy-start = (bf16[1,256,4096]{2,1,0:T(8,128)(2,1)S(1)}, bf16[1,256,4096]{2,1,0:T(8,128)(2,1)}, u32[]{:S(2)}) copy-start(bf16[1,256,4096]{2,1,0:T(8,128)(2,1)} %param.7) | copy-start | bytes 6291460
  67.1 16.3 %collective-permute-start.3 = (bf16[512,512]{1,0:T(8,128)(2,1)S(1)}, bf16[512,512]{1,0:T(8,128)(2,1)}, u32[]{:S(2)}, u32[]{:S(2)}) collective-permute-start(bf16[512,512]{1,0:T(8,128)(2,1)S(1)} %pad_maximum_fusion.refs_2_), channel_id=1, source_target_pairs={{0,1},{1,0},{2,3},{3,2},{4,5},{5,4},{6,7},{7,6},{8,9},{9,8},{10,11... | collective-permute-start | bytes 1572872 | tf_op jit(solution)/shard_map/ppermute | solution.py:240
  68.6 9.6 %collective-permute-start.23 = (bf16[512,256]{1,0:T(8,128)(2,1)S(1)}, bf16[512,256]{1,0:T(8,128)(2,1)S(1)}, u32[]{:S(2)}, u32[]{:S(2)}) collective-permute-start(bf16[512,256]{1,0:T(8,128)(2,1)S(1)} %constant_dynamic-update-slice_fusion.refs_2_), channel_id=1, source_target_pairs={{1,2},{2,1},{5,6},{6,5},{9,10},{10,9},{13,14},{14,13},{17,18},{18,... | collective-permute-start | bytes 786440 | tf_op jit(solution)/shard_map/ppermute | solution.py:240
  71.8 16.9 %collective-permute-start.8 = (bf16[512,512]{1,0:T(8,128)(2,1)S(1)}, bf16[512,512]{1,0:T(8,128)(2,1)}, u32[]{:S(2)}, u32[]{:S(2)}) collective-permute-start(bf16[512,512]{1,0:T(8,128)(2,1)S(1)} %pad_maximum_fusion.refs_2_), channel_id=1, source_target_pairs={{1,2},{2,1},{5,6},{6,5},{9,10},{10,9},{13,14},{14,13},{17,18},{18,... | collective-permute-start | bytes 1572872 | tf_op jit(solution)/shard_map/ppermute | solution.py:240
  73.9 71.6 %collective-permute-start.7 = (bf16[256,4096]{1,0:T(8,128)(2,1)S(1)}, bf16[256,4096]{1,0:T(8,128)(2,1)}, u32[]{:S(2)}, u32[]{:S(2)}) collective-permute-start(bf16[256,4096]{1,0:T(8,128)(2,1)S(1)} %bitcast.16), channel_id=1, source_target_pairs={{0,4},{1,5},{2,6},{3,7},{4,0},{5,1},{6,2},{7,3},{8,12},{9,13},{10,... | collective-permute-start | bytes 6291464 | tf_op jit(solution)/shard_map/ppermute | solution.py:240
  76.8 72.8 %collective-permute-start.14 = (bf16[256,4096]{1,0:T(8,128)(2,1)}, bf16[256,4096]{1,0:T(8,128)(2,1)}, u32[]{:S(2)}, u32[]{:S(2)}) collective-permute-start(bf16[256,4096]{1,0:T(8,128)(2,1)} %collective-permute-done.13.refs_0_), channel_id=1, source_target_pairs={{0,4},{1,5},{2,6},{3,7},{4,0},{5,1},{6,2},{7,3},{8,12},{9,13},{10,... | collective-permute-start | bytes 6291464 | tf_op jit(solution)/shard_map/ppermute | solution.py:240
  78.2 16.0 %collective-permute-start.20 = (bf16[512,256]{1,0:T(8,128)(2,1)S(1)}, bf16[512,256]{1,0:T(8,128)(2,1)S(1)}, u32[]{:S(2)}, u32[]{:S(2)}) collective-permute-start(bf16[512,256]{1,0:T(8,128)(2,1)S(1)} %collective-permute-done.19.refs_3_), channel_id=1, source_target_pairs={{1,2},{2,1},{5,6},{6,5},{9,10},{10,9},{13,14},{14,13},{17,18},{18,... | collective-permute-start | bytes 786440 | tf_op jit(solution)/shard_map/ppermute | solution.py:240
  83.4 22.1 %collective-permute-start.4 = (bf16[512,512]{1,0:T(8,128)(2,1)}, bf16[512,512]{1,0:T(8,128)(2,1)S(1)}, u32[]{:S(2)}, u32[]{:S(2)}) collective-permute-start(bf16[512,512]{1,0:T(8,128)(2,1)} %collective-permute-done.3.refs_3_), channel_id=1, source_target_pairs={{1,2},{2,1},{5,6},{6,5},{9,10},{10,9},{13,14},{14,13},{17,18},{18,... | collective-permute-start | bytes 1572872 | tf_op jit(solution)/shard_map/ppermute | solution.py:240
  88.7 18.8 %collective-permute-start.9 = (bf16[512,512]{1,0:T(8,128)(2,1)}, bf16[512,512]{1,0:T(8,128)(2,1)S(1)}, u32[]{:S(2)}, u32[]{:S(2)}) collective-permute-start(bf16[512,512]{1,0:T(8,128)(2,1)} %collective-permute-done.8), channel_id=1, source_target_pairs={{1,0},{2,3},{5,4},{6,7},{9,8},{10,11},{13,12},{14,15},{17,16},{18,... | collective-permute-start | bytes 1572872 | tf_op jit(solution)/shard_map/ppermute | solution.py:240
  94.2 29.0 %collective-permute-start.10 = (bf16[512,512]{1,0:T(8,128)(2,1)S(1)}, bf16[512,512]{1,0:T(8,128)(2,1)S(1)}, u32[]{:S(2)}, u32[]{:S(2)}) collective-permute-start(bf16[512,512]{1,0:T(8,128)(2,1)S(1)} %pad_maximum_fusion.refs_2_), channel_id=1, source_target_pairs={{0,16},{1,17},{2,18},{3,19},{4,20},{5,21},{6,22},{7,23},{8,24},{9,... | collective-permute-start | bytes 1572872 | tf_op jit(solution)/shard_map/ppermute | solution.py:240
  105.4 18.0 %collective-permute-start.5 = (bf16[512,512]{1,0:T(8,128)(2,1)S(1)}, bf16[512,512]{1,0:T(8,128)(2,1)S(1)}, u32[]{:S(2)}, u32[]{:S(2)}) collective-permute-start(bf16[512,512]{1,0:T(8,128)(2,1)S(1)} %collective-permute-done.4), channel_id=1, source_target_pairs={{1,0},{2,3},{5,4},{6,7},{9,8},{10,11},{13,12},{14,15},{17,16},{18,... | collective-permute-start | bytes 1572872 | tf_op jit(solution)/shard_map/ppermute | solution.py:240
  107.5 14.5 %collective-permute-start.24 = (bf16[512,256]{1,0:T(8,128)(2,1)S(1)}, bf16[512,256]{1,0:T(8,128)(2,1)S(1)}, u32[]{:S(2)}, u32[]{:S(2)}) collective-permute-start(bf16[512,256]{1,0:T(8,128)(2,1)S(1)} %collective-permute-done.23), channel_id=1, source_target_pairs={{1,0},{2,3},{5,4},{6,7},{9,8},{10,11},{13,12},{14,15},{17,16},{18,... | collective-permute-start | bytes 786440 | tf_op jit(solution)/shard_map/ppermute | solution.py:240
  121.9 11.1 %collective-permute-start.11 = (bf16[512,512]{1,0:T(8,128)(2,1)}, bf16[512,512]{1,0:T(8,128)(2,1)S(1)}, u32[]{:S(2)}, u32[]{:S(2)}) collective-permute-start(bf16[512,512]{1,0:T(8,128)(2,1)} %collective-permute-done.3.refs_3_), channel_id=1, source_target_pairs={{0,16},{1,17},{2,18},{3,19},{4,20},{5,21},{6,22},{7,23},{8,24},{9,... | collective-permute-start | bytes 1572872 | tf_op jit(solution)/shard_map/ppermute | solution.py:240
  123.2 21.1 %collective-permute-start.12 = (bf16[512,512]{1,0:T(8,128)(2,1)S(1)}, bf16[512,512]{1,0:T(8,128)(2,1)S(1)}, u32[]{:S(2)}, u32[]{:S(2)}) collective-permute-start(bf16[512,512]{1,0:T(8,128)(2,1)S(1)} %broadcast_select_fusion.refs_4_), channel_id=1, source_target_pairs={{0,16},{1,17},{2,18},{3,19},{4,20},{5,21},{6,22},{7,23},{8,24},{9,... | collective-permute-start | bytes 1572872 | tf_op jit(solution)/shard_map/ppermute | solution.py:240
  123.4 7.4 %collective-permute-start.21 = (bf16[512,256]{1,0:T(8,128)(2,1)S(1)}, bf16[512,256]{1,0:T(8,128)(2,1)S(1)}, u32[]{:S(2)}, u32[]{:S(2)}) collective-permute-start(bf16[512,256]{1,0:T(8,128)(2,1)S(1)} %collective-permute-done.20), channel_id=1, source_target_pairs={{1,0},{2,3},{5,4},{6,7},{9,8},{10,11},{13,12},{14,15},{17,16},{18,... | collective-permute-start | bytes 786440 | tf_op jit(solution)/shard_map/ppermute | solution.py:240
  130.9 24.7 %collective-permute-start.6 = (bf16[512,512]{1,0:T(8,128)(2,1)S(1)}, bf16[512,512]{1,0:T(8,128)(2,1)S(1)}, u32[]{:S(2)}, u32[]{:S(2)}) collective-permute-start(bf16[512,512]{1,0:T(8,128)(2,1)S(1)} %broadcast_select_fusion.1.refs_5_), channel_id=1, source_target_pairs={{0,16},{1,17},{2,18},{3,19},{4,20},{5,21},{6,22},{7,23},{8,24},{9,... | collective-permute-start | bytes 1572872 | tf_op jit(solution)/shard_map/ppermute | solution.py:240
  133.0 28.1 %collective-permute-start.25 = (bf16[512,256]{1,0:T(8,128)(2,1)S(1)}, bf16[512,256]{1,0:T(8,128)(2,1)S(1)}, u32[]{:S(2)}, u32[]{:S(2)}) collective-permute-start(bf16[512,256]{1,0:T(8,128)(2,1)S(1)} %constant_dynamic-update-slice_fusion.refs_2_), channel_id=1, source_target_pairs={{0,16},{1,17},{2,18},{3,19},{4,20},{5,21},{6,22},{7,23},{8,24},{9,... | collective-permute-start | bytes 786440 | tf_op jit(solution)/shard_map/ppermute | solution.py:240
  144.3 22.5 %collective-permute-start.26 = (bf16[512,256]{1,0:T(8,128)(2,1)S(1)}, bf16[512,256]{1,0:T(8,128)(2,1)S(1)}, u32[]{:S(2)}, u32[]{:S(2)}) collective-permute-start(bf16[512,256]{1,0:T(8,128)(2,1)S(1)} %collective-permute-done.19.refs_3_), channel_id=1, source_target_pairs={{0,16},{1,17},{2,18},{3,19},{4,20},{5,21},{6,22},{7,23},{8,24},{9,... | collective-permute-start | bytes 786440 | tf_op jit(solution)/shard_map/ppermute | solution.py:240
  145.5 26.8 %collective-permute-start.27 = (bf16[512,256]{1,0:T(8,128)(2,1)S(1)}, bf16[512,256]{1,0:T(8,128)(2,1)S(1)}, u32[]{:S(2)}, u32[]{:S(2)}) collective-permute-start(bf16[512,256]{1,0:T(8,128)(2,1)S(1)} %broadcast_select_fusion.2.refs_4_), channel_id=1, source_target_pairs={{0,16},{1,17},{2,18},{3,19},{4,20},{5,21},{6,22},{7,23},{8,24},{9,... | collective-permute-start | bytes 786440 | tf_op jit(solution)/shard_map/ppermute | solution.py:240
  149.6 28.4 %collective-permute-start.22 = (bf16[512,256]{1,0:T(8,128)(2,1)S(1)}, bf16[512,256]{1,0:T(8,128)(2,1)S(1)}, u32[]{:S(2)}, u32[]{:S(2)}) collective-permute-start(bf16[512,256]{1,0:T(8,128)(2,1)S(1)} %broadcast_select_fusion.3.refs_5_), channel_id=1, source_target_pairs={{0,16},{1,17},{2,18},{3,19},{4,20},{5,21},{6,22},{7,23},{8,24},{9,... | collective-permute-start | bytes 786440 | tf_op jit(solution)/shard_map/ppermute | solution.py:240
  157.3 21.1 %copy-start.4 = (f32[16]{0:T(128)S(1)}, f32[16]{0:T(128)}, u32[]{:S(2)}) copy-start(f32[16]{0:T(128)} %gate_ref.7) | copy-start | bytes 196
  157.3 21.1 %collective-permute-start.15 = (bf16[128,256]{1,0:T(8,128)(2,1)S(1)}, bf16[128,256]{1,0:T(8,128)(2,1)S(1)}, u32[]{:S(2)}, u32[]{:S(2)}) collective-permute-start(bf16[128,256]{1,0:T(8,128)(2,1)S(1)} %get-tuple-element.56), channel_id=1, source_target_pairs={{0,16},{1,17},{2,18},{3,19},{4,20},{5,21},{6,22},{7,23},{8,24},{9,... | collective-permute-start | bytes 196616 | tf_op jit(solution)/shard_map/ppermute | solution.py:240
  181.0 16.5 %collective-permute-start.31 = (bf16[256,256]{1,0:T(8,128)(2,1)S(1)}, bf16[256,256]{1,0:T(8,128)(2,1)S(1)}, u32[]{:S(2)}, u32[]{:S(2)}) collective-permute-start(bf16[256,256]{1,0:T(8,128)(2,1)S(1)} %get-tuple-element.78), channel_id=1, source_target_pairs={{0,8},{1,9},{2,10},{3,11},{4,12},{5,13},{6,14},{7,15},{8,0},{9,1},... | collective-permute-start | bytes 393224 | tf_op jit(solution)/shard_map/ppermute | solution.py:240
  185.2 12.7 %collective-permute-start.33 = (bf16[256,256]{1,0:T(8,128)(2,1)S(1)}, bf16[256,256]{1,0:T(8,128)(2,1)S(1)}, u32[]{:S(2)}, u32[]{:S(2)}) collective-permute-start(bf16[256,256]{1,0:T(8,128)(2,1)S(1)} %get-tuple-element.80), channel_id=1, source_target_pairs={{0,12},{1,13},{2,14},{3,15},{4,8},{5,9},{6,10},{7,11},{8,4},{9,5},... | collective-permute-start | bytes 393224 | tf_op jit(solution)/shard_map/ppermute | solution.py:240
  191.1 6.8 %collective-permute-start.30 = (bf16[256,256]{1,0:T(8,128)(2,1)S(1)}, bf16[256,256]{1,0:T(8,128)(2,1)S(1)}, u32[]{:S(2)}, u32[]{:S(2)}) collective-permute-start(bf16[256,256]{1,0:T(8,128)(2,1)S(1)} %get-tuple-element.75), channel_id=1, source_target_pairs={{0,8},{1,9},{2,10},{3,11},{4,12},{5,13},{6,14},{7,15},{8,0},{9,1},... | collective-permute-start | bytes 393224 | tf_op jit(solution)/shard_map/ppermute | solution.py:240
  192.5 6.7 %collective-permute-start.32 = (bf16[256,256]{1,0:T(8,128)(2,1)S(1)}, bf16[256,256]{1,0:T(8,128)(2,1)S(1)}, u32[]{:S(2)}, u32[]{:S(2)}) collective-permute-start(bf16[256,256]{1,0:T(8,128)(2,1)S(1)} %get-tuple-element.79), channel_id=1, source_target_pairs={{0,12},{1,13},{2,14},{3,15},{4,8},{5,9},{6,10},{7,11},{8,4},{9,5},... | collective-permute-start | bytes 393224 | tf_op jit(solution)/shard_map/ppermute | solution.py:240
  195.3 3.9 %collective-permute-start.29 = (bf16[256,256]{1,0:T(8,128)(2,1)S(1)}, bf16[256,256]{1,0:T(8,128)(2,1)S(1)}, u32[]{:S(2)}, u32[]{:S(2)}) collective-permute-start(bf16[256,256]{1,0:T(8,128)(2,1)S(1)} %get-tuple-element.74), channel_id=1, source_target_pairs={{0,4},{1,5},{2,6},{3,7},{4,0},{5,1},{6,2},{7,3},{8,12},{9,13},{10,... | collective-permute-start | bytes 393224 | tf_op jit(solution)/shard_map/ppermute | solution.py:240
  197.5 1.7 collective-permute-start.28

commit v3 on v2

v3 whole, which is shorter than its diff:
```python
import functools

import jax
import jax.numpy as jnp
from jax import lax
from jax.experimental import pallas as pl
from jax.experimental.pallas import tpu as pltpu
from jax.sharding import PartitionSpec as P

HEAD_SIZE = 128
BLK = 128
MEMBERS = 4
META_ROWS = 16
HALF = META_ROWS // 2
AXES = ("seg", "fsdp")

VMEM = pl.BlockSpec(memory_space=pltpu.VMEM)
SMEM = pl.BlockSpec(memory_space=pltpu.SMEM)
ANY = pl.BlockSpec(memory_space=pl.ANY)
HBM = pl.BlockSpec(memory_space=pltpu.HBM)


def call(body, outs, in_specs, flops=0, scratch=(), out_spec=VMEM, limit=28 << 20):
    return pl.pallas_call(
        body,
        out_shape=outs,
        in_specs=in_specs,
        out_specs=[out_spec] * len(outs),
        scratch_shapes=list(scratch),
        compiler_params=pltpu.CompilerParams(vmem_limit_bytes=limit),
        cost_estimate=pl.CostEstimate(flops=flops, bytes_accessed=4 << 20, transcendentals=0),
    )


def aligned(offset):
    return pl.multiple_of(offset, HEAD_SIZE)


def pack_body(
    group, early, here_ref, valid_ref, mask_ref, wq_ref, wk_ref, wv_ref, *refs
):
    outs, facts_ref, sems = refs[: 2 * MEMBERS], refs[-2], refs[-1]
    rows = wk_ref.shape[0]
    row = lax.broadcasted_iota(jnp.int32, facts_ref.shape, 0)
    facts = jnp.where(row < HALF, valid_ref[0, 0], mask_ref[0, 0, 1, 0])
    facts_ref[...] = facts.astype(jnp.float32).astype(jnp.bfloat16)
    copies = []

    def copy(source, target):
        copies.append(pltpu.make_async_copy(source, target, sems.at[len(copies)]))
        copies[-1].start()

    for k in range(MEMBERS):
        head = here_ref[1] ^ k
        first, second = outs[2 * k : 2 * k + 2]
        at = aligned(head * HEAD_SIZE)
        wide = group * HEAD_SIZE
        copy(wk_ref.at[:, pl.ds(at, HEAD_SIZE)], first.at[pl.ds(0, rows), pl.ds(0, HEAD_SIZE)])
        copy(wv_ref.at[:, pl.ds(at, HEAD_SIZE)], first.at[pl.ds(0, rows), pl.ds(HEAD_SIZE, HEAD_SIZE)])
        if early:
            copy(
                wq_ref.at[:, pl.ds(aligned(head * wide), early * HEAD_SIZE)],
                first.at[pl.ds(0, rows), pl.ds(2 * HEAD_SIZE, early * HEAD_SIZE)],
            )
        copy(facts_ref, first.at[pl.ds(rows, META_ROWS), :])
        copy(
            wq_ref.at[:, pl.ds(aligned(head * wide + early * HEAD_SIZE), (group - early) * HEAD_SIZE)],
            second,
        )
    for one in copies:
        one.wait()


def columns_of(tokens_ref, here_ref, piece, line):
    if not line:
        return tokens_ref[:, pl.ds(piece * MEMBERS * HEAD_SIZE, MEMBERS * HEAD_SIZE)]
    g, m, z = here_ref[0] ^ (piece // line), here_ref[1], here_ref[2]
    inside = (z == 1) | (z == 2)
    step = piece % line
    if step < 2:
        z = z ^ step
    else:
        z = jnp.where(inside, z ^ (5 - step), z ^ step)
    parts = [
        tokens_ref[:, pl.ds(aligned(((g * MEMBERS + (m ^ k)) * line + z) * HEAD_SIZE), HEAD_SIZE)]
        for k in range(MEMBERS)
    ]
    return jnp.concatenate(parts, axis=1)


def facts_of(message_ref):
    rows = message_ref.shape[0] - META_ROWS
    facts = message_ref[rows:, : 2 * HEAD_SIZE].astype(jnp.float32)
    return facts[0:1, :], facts[HALF : HALF + 1, :]


def iota(shape, dimension):
    return lax.broadcasted_iota(jnp.int32, shape, dimension).astype(jnp.float32)


def project_body(n_segs, n_pieces, keep_last, line, here_ref, *refs):
    tokens, pieces = refs[:n_segs], refs[n_segs : n_segs + n_pieces - 1]
    outs = refs[n_segs + n_pieces - 1 :]
    for n in range(n_segs):
        total = None
        for p in range(n_pieces - 1):
            term = jnp.dot(
                columns_of(tokens[n], here_ref, p, line), pieces[p][...], preferred_element_type=jnp.float32
            )
            total = term if total is None else total + term
        outs[n][...] = total
        if keep_last:
            outs[n_segs + n][...] = columns_of(tokens[n], here_ref, n_pieces - 1, line)


def sigma_plus(v):
    return jnp.where(v > 0, v + 1.0, jnp.exp(jnp.minimum(v, 0.0)))


def split(values):
    high = values.astype(jnp.bfloat16)
    return high, (values - high.astype(jnp.float32)).astype(jnp.bfloat16)


def kv_body(piece_ref, *refs):
    sums, lasts, messages = refs[:MEMBERS], refs[MEMBERS : 2 * MEMBERS], refs[2 * MEMBERS : 3 * MEMBERS]
    outs = refs[3 * MEMBERS :]
    whole = None
    for seg in range(MEMBERS):
        total = sums[seg][...] + jnp.dot(
            lasts[seg][...], piece_ref[...], preferred_element_type=jnp.float32
        )
        kvq = total.astype(jnp.bfloat16)
        outs[2 * seg][...] = kvq
        length = kvq.shape[0]
        valid, _ = facts_of(messages[seg])
        keys = kvq[:, :HEAD_SIZE].astype(jnp.float32)
        live = iota((length, HEAD_SIZE), 0) < valid[:, :HEAD_SIZE]
        sig = jnp.where(live, sigma_plus(keys), 0.0)
        wide = jnp.concatenate(
            [kvq[:, HEAD_SIZE : 2 * HEAD_SIZE], jnp.ones((length, HEAD_SIZE), jnp.bfloat16)], axis=1
        )
        high, low = split(sig)
        over = (((0,), (0,)), ((), ()))
        delta = lax.dot_general(high, wide, over, preferred_element_type=jnp.float32)
        delta += lax.dot_general(low, wide, over, preferred_element_type=jnp.float32)
        outs[2 * seg + 1][...] = delta
        whole = delta if whole is None else whole + delta
    outs[-1][...] = whole.astype(jnp.bfloat16)


def attend_body(segs, early, late, first_head, group, here_ref, gate_ref, base_ref, *refs):
    kvqs, deltas, messages = refs[:MEMBERS], refs[MEMBERS : 2 * MEMBERS], refs[2 * MEMBERS : 3 * MEMBERS]
    rest = refs[3 * MEMBERS :]
    n = len(segs)
    piece, sums, lasts, outs = rest[0], rest[1 : 1 + n], rest[1 + n : 1 + 2 * n], rest[1 + 2 * n :]
    me = here_ref[1]
    heads = early + late[1] - late[0]
    at_late = slice(late[0] * HEAD_SIZE, late[1] * HEAD_SIZE)
    for at, seg in enumerate(segs):
        queries = (
            sums[at][:, at_late]
            + jnp.dot(lasts[at][...], piece[:, at_late], preferred_element_type=jnp.float32)
        ).astype(jnp.bfloat16)
        if early:
            queries = jnp.concatenate(
                [kvqs[seg][:, 2 * HEAD_SIZE : (2 + early) * HEAD_SIZE], queries], axis=1
            )
        length = queries.shape[0]
        blocks = length // BLK
        valid, seen = facts_of(messages[seg])

        memory = base_ref[...].astype(jnp.float32)
        for other in range(MEMBERS):
            if other != seg:
                earlier = jnp.where((me ^ other) < (me ^ seg), 1.0, 0.0)
                memory = memory + earlier * deltas[other][...]
        mem_high, mem_low = split(memory)

        for block in range(blocks):
            span = slice(block * BLK, (block + 1) * BLK)
            stacked = jnp.concatenate(
                [queries[span, h * HEAD_SIZE : (h + 1) * HEAD_SIZE] for h in range(heads)], axis=0
            )
            width = (block + 1) * BLK
            keys = kvqs[seg][0:width, :HEAD_SIZE]
            values = kvqs[seg][0:width, HEAD_SIZE : 2 * HEAD_SIZE]
            scores = lax.dot_general(
                stacked, keys, (((1,), (1,)), ((), ())), preferred_element_type=jnp.float32
            ) * HEAD_SIZE ** (-0.5)
            i, j = iota((BLK, width), 0) + block * BLK, iota((BLK, width), 1)
            limit = valid[:, :width]
            if block:
                limit = jnp.where((j[0:1] >= block * BLK) | (seen[:, :width] > 0), limit, 0.0)
            allowed = (j <= i) & (j < limit)
            masked = jnp.concatenate(
                [
                    jnp.where(allowed, scores[h * BLK : (h + 1) * BLK], -1e30)
                    for h in range(heads)
                ],
                axis=0,
            )
            top = jnp.max(masked, axis=-1, keepdims=True)
            expo = jnp.exp(masked - top)
            total = jnp.maximum(jnp.sum(expo, axis=-1, keepdims=True), 1.0)
            weights = (expo / total).astype(jnp.bfloat16)
            local = jnp.dot(weights, values, preferred_element_type=jnp.float32)

            high, low = split(sigma_plus(stacked.astype(jnp.float32)))
            numer = jnp.dot(high, mem_high, preferred_element_type=jnp.float32)
            numer += jnp.dot(high, mem_low, preferred_element_type=jnp.float32)
            numer += jnp.dot(low, mem_high, preferred_element_type=jnp.float32)
            retrieved = numer[:, :HEAD_SIZE] / (numer[:, HEAD_SIZE:] + 1.0)
            live = iota((BLK, HEAD_SIZE), 0) + block * BLK < valid[:, :HEAD_SIZE]
            for h in range(heads):
                part = slice(h * BLK, (h + 1) * BLK)
                logit = jnp.full((1, HEAD_SIZE), gate_ref[me * group + first_head + h], jnp.float32)
                gate = 1.0 / (1.0 + jnp.exp(-logit))
                mixed = gate * retrieved[part] + (1.0 - gate) * local[part]
                outs[at][span, h * HEAD_SIZE : (h + 1) * HEAD_SIZE] = jnp.where(
                    live, mixed, 0.0
                ).astype(jnp.bfloat16)


def assemble_body(group, widths, here_ref, *refs):
    parts, out = refs[:-1], refs[-1]
    for k in range(MEMBERS):
        at = (here_ref[1] ^ k) * group * HEAD_SIZE
        for c, width in enumerate(widths):
            out[:, pl.ds(aligned(at), width)] = parts[len(widths) * k + c][...]
            at = at + width


def after(array, *others):
    return lax.optimization_barrier((array,) + others)[0]


def shards(sizes, tokens, w_query, w_key, value_weight, gate_bias, block_mask, valid_len):
    n_seg, n_z = sizes
    n_groups = n_seg // MEMBERS
    heads_kv = w_key.shape[1] // HEAD_SIZE
    group = w_query.shape[1] // w_key.shape[1]
    early = 1
    rows = w_query.shape[0]
    length, width = tokens.shape[1], tokens.shape[2]
    assert heads_kv == MEMBERS and length == 2 * BLK
    seg = lax.axis_index("seg")
    z = lax.axis_index("fsdp")
    g, m = seg // MEMBERS, seg % MEMBERS
    here = jnp.stack([g, m, z]).astype(jnp.int32)
    bf16, f32 = jnp.bfloat16, jnp.float32
    shape = jax.ShapeDtypeStruct

    def permute(array, to):
        pairs = []
        for gg in range(n_groups):
            for mm in range(MEMBERS):
                for zz in range(n_z):
                    target = to(gg, mm, zz)
                    if target is not None:
                        index = lambda t: (t[0] * MEMBERS + t[1]) * n_z + t[2]
                        pairs.append((index((gg, mm, zz)), index(target)))
        return lax.ppermute(array, AXES, pairs)

    def to_member(array, k):
        return permute(array, lambda gg, mm, zz: (gg, mm ^ k, zz))

    wide = [(2 + early) * HEAD_SIZE, (group - early) * HEAD_SIZE]
    packed = call(
        functools.partial(pack_body, group, early),
        [shape((rows + META_ROWS, wide[0]), bf16), shape((rows, wide[1]), bf16)] * MEMBERS,
        [SMEM] * 3 + [HBM] * 3,
        scratch=[pltpu.VMEM((META_ROWS, wide[0]), bf16), pltpu.SemaphoreType.DMA((5 * MEMBERS,))],
        out_spec=ANY,
    )(here, valid_len, block_mask, w_query, w_key, value_weight)
    order = (2, 3, 1)
    first = {0: packed[0]}
    second = {0: packed[1]}
    for k in order:
        first[k] = to_member(packed[2 * k], k)
    for k in order:
        second[k] = to_member(packed[2 * k + 1], k)
    messages = [first[k] for k in range(MEMBERS)]

    own = after(tokens[0], first[2], first[3], second[2], second[3])
    across = to_member(own, 2)
    sibling = to_member(own, 1)
    diagonal = to_member(across, 1)
    books = [tokens[0], sibling, across, diagonal]

    def lines(pieces):
        inside = (z == 1) | (z == 2)
        over = lambda part: permute(part, lambda gg, mm, zz: (gg ^ 1, mm, zz))
        pair = lambda part: permute(part, lambda gg, mm, zz: (gg, mm, zz ^ 1))
        outward = lambda part: permute(
            part, lambda gg, mm, zz: (gg, mm, zz ^ 1) if zz in (1, 2) else None
        )
        inward = lambda part: permute(
            part, lambda gg, mm, zz: (gg, mm, zz ^ 3) if zz in (1, 2) else None
        )
        locked = lambda *parts: lax.optimization_barrier(parts)
        states = [(pair(piece), inward(piece), over(piece)) for piece in pieces]
        found = [[] for _ in pieces]
        for n, piece in enumerate(pieces):
            one, inner, far0 = locked(*states[n])
            found[n] = [piece, one, far0]
            states[n] = (inward(one), outward(inner), over(one), inner)
        for n in range(len(pieces)):
            middle, outer, far1, inner = locked(*states[n])
            two = jnp.where(inside, inner, outer)
            states[n] = (outward(middle), over(two), middle, two, far1)
        for n in range(len(pieces)):
            last, far2, middle, two, far1 = locked(*states[n])
            three = jnp.where(inside, middle, last)
            piece, one, far0 = found[n]
            found[n] = [piece, one, two, three, far0, far1, far2, over(three)]
        return found

    def gathered(piece):
        index = lambda gg, mm, zz: (gg * MEMBERS + mm) * n_z + zz
        everything = lax.all_gather(
            piece,
            AXES,
            axis_index_groups=[
                [index(gg, mm, zz) for gg in range(n_groups) for zz in range(n_z)]
                for mm in range(MEMBERS)
            ],
        )
        columns = piece.shape[1]
        natural = everything.reshape(n_groups, n_z, MEMBERS, rows, columns)
        members = jnp.arange(MEMBERS, dtype=jnp.int32) ^ m
        natural = jnp.take(natural, members, axis=2).transpose(0, 2, 1, 3, 4)
        return list(natural.reshape(-1, MEMBERS * HEAD_SIZE, columns))

    pieces = [
        jnp.concatenate([part[k][:rows] for k in range(MEMBERS)], axis=0) for part in (first, second)
    ]
    if n_groups == 2 and n_z == 4:
        assert rows == HEAD_SIZE
        line, chunks = n_z, lines(pieces)
    else:
        line, chunks = 0, [gathered(piece) for piece in pieces]
    n_pieces = width // (MEMBERS * HEAD_SIZE)

    sums, lasts = [[], []], []
    for c in range(2):
        for segs in ((0, 1), (2, 3)):
            n = len(segs)
            found = call(
                functools.partial(project_body, n, n_pieces, c == 0, line),
                [shape((length, wide[c]), f32)] * n
                + [shape((length, MEMBERS * HEAD_SIZE), bf16)] * (n if c == 0 else 0),
                [SMEM] + [VMEM] * (n + n_pieces - 1),
                flops=2 * n * length * width * wide[c],
            )(here, *[books[s] for s in segs], *chunks[c][:-1])
            sums[c] += found[:n]
            lasts += found[n:]

    found = call(
        kv_body,
        [shape((length, wide[0]), bf16), shape((HEAD_SIZE, 2 * HEAD_SIZE), f32)] * MEMBERS
        + [shape((HEAD_SIZE, 2 * HEAD_SIZE), bf16)],
        [VMEM] * (1 + 3 * MEMBERS),
        flops=2 * MEMBERS * length * MEMBERS * HEAD_SIZE * wide[0],
    )(chunks[0][-1], *sums[0], *lasts, *messages)
    kvqs, deltas, total = found[0:-1:2], found[1:-1:2], found[-1]

    base = None
    for a in range(1, n_groups):
        term = permute(total, lambda gg, mm, zz: (gg ^ a, mm, zz) if gg < gg ^ a else None)
        base = term if base is None else base.astype(f32) + term.astype(f32)

    sent = {}
    half = group // 2
    picks = [(early, (0, half - early)), (0, (half - early, group - early))]

    def attend(c, segs, base):
        attended = call(
            functools.partial(attend_body, segs, *picks[c], c * half, group),
            [shape((length, half * HEAD_SIZE), bf16)] * len(segs),
            [SMEM] * 2 + [VMEM] * (2 + 3 * MEMBERS + 2 * len(segs)),
            flops=2 * len(segs) * length * length * HEAD_SIZE * half * 3,
        )(
            here, gate_bias, base, *kvqs, *deltas, *messages, chunks[1][-1],
            *[sums[1][s] for s in segs], *[lasts[s] for s in segs],
        )
        for seg_at, part in zip(segs, attended):
            sent[c, seg_at] = to_member(part, seg_at) if seg_at else part
        return attended

    far = attend(0, (2, 3), base)
    far = attend(1, (2, 3), after(base, *far))
    near = attend(0, (1, 0), after(base, *far))
    attend(1, (1, 0), after(base, *near))
    (output,) = call(
        functools.partial(assemble_body, group, (half * HEAD_SIZE,) * 2),
        [shape((length, w_query.shape[1]), bf16)],
        [SMEM] + [VMEM] * (2 * MEMBERS),
    )(here, *[sent[c, k] for k in range(MEMBERS) for c in range(2)])
    return output[None]


def solution(mesh):
    in_specs = (
        P("fsdp", "seg", None),
        P(("seg", "fsdp"), None),
        P(("seg", "fsdp"), None),
        P(("seg", "fsdp"), None),
        P(),
        P("fsdp", "seg", None, None),
        P("fsdp", "seg"),
    )
    out_specs = P("fsdp", "seg", None)
    body = functools.partial(shards, (mesh.shape["seg"], mesh.shape["fsdp"]))
    return jax.shard_map(body, mesh=mesh, in_specs=in_specs, out_specs=out_specs, check_vma=False)
```

time: 204 us -> 163 us (0.80); the launches traced: 200 us -> 161 us
  waiting for transfers between devices: 111 us -> 64.8 us
  starting transfers between devices: 47.6 us -> 55.2 us
  local copies, waits for them, and re-layouts: 9.37 us -> 5.22 us
  Pallas kernels: 27.3 us -> 30.5 us
    ppermute x34, waiting for transfers between devices: 111 us -> 64.8 us  [permute(): return lax.ppermute(array, AXES, pairs)]
    ppermute x34, starting transfers between devices: 47.6 us -> 55.2 us  [permute(): return lax.ppermute(array, AXES, pairs)]
    pallas_call x9, Pallas kernels: 24.5 us -> 28.3 us  [the longest x4 16.7 us: shards(): call(functools.partial(project_body, n, n_pieces, c == 0, line), [shape((...]
    select_n x4, other arithmetic: 1.25 us -> 4.25 us  [the longest x2 2.15 us: lines(): three = jnp.where(inside, middle, last)]
    squeeze x4 -> x0, local copies, waits for them, and re-layouts: 2.62 us -> none  [shards(): first[k][rows, :FACTS]]
    unnamed x19 -> x25, local copies, waits for them, and re-layouts: 3.55 us -> 5.16 us
  transfers between devices with their start and end apart: 34 -> 34, of which waited for: 19 -> 18; matrix products, arithmetic and copies ran while one was open for 5% -> 3% of each run, Pallas kernels for 11% -> 11%
where the time goes in v3:
time: 163 us; the launch traced here: 161 us
  waiting for transfers between devices  64.8 us (40%)
  starting transfers between devices  55.2 us (34%)
  Pallas kernels  30.5 us (19%)
  local copies, waits for them, and re-layouts  5.22 us (3%)
  other arithmetic  4.37 us (3%)
    ppermute x34, waiting for transfers between devices, permute(): return lax.ppermute(array, AXES, pairs)  64.8 us
    ppermute x34, starting transfers between devices, permute(): return lax.ppermute(array, AXES, pairs)  55.2 us
    pallas_call x4, Pallas kernels, shards(): call(functools.partial(project_body, n, n_pieces, c == 0, line), [shape((...  16.7 us
    pallas_call x4, Pallas kernels, attend(): call(functools.partial(attend_body, segs, *picks[c], c * half, group), [s...  9.97 us
    unnamed x25, local copies, waits for them, and re-layouts  5.16 us
  transfers between devices with their start and end apart: 34, of which 18 were waited for; matrix products, arithmetic and copies ran while one was open for 3% of the time, Pallas kernels for 11%

profile of v3, /device:TPU:9, one launch (start us, length us, event | category | flops | bytes accessed | tf_op | source)
XLA Modules:
  0.0 161.3 jit_solution(11517857626050300612)
XLA Ops:
  0.9 1.0 copy-done.5
  1.9 0.9 copy-done.6
  2.8 0.9 copy-done.7
  3.7 0.7 copy-done.9
  4.4 1.0 shard_map.73
  5.4 1.3 collective-permute-start.1
  6.7 1.1 collective-permute-start.2
  7.8 1.2 collective-permute-start.12
  9.3 5.4 %collective-permute-done.12 = bf16[128,384]{1,0:T(8,128)(2,1)S(1)} collective-permute-done((bf16[128,384]{1,0:T(8,128)(2,1)S(1)}, bf16[128,384]{1,0:T(8,128)(2,1)S(1)}, u32[]{:S(2)}, u32[]{:S(2)}) %collective-permute-start.12) | collective-permute-done | bytes 98336 | tf_op jit(solution)/shard_map/ppermute | solution.py:263
  14.7 2.1 %collective-permute-done.13 = bf16[128,384]{1,0:T(8,128)(2,1)S(1)} collective-permute-done((bf16[128,384]{1,0:T(8,128)(2,1)S(1)}, bf16[128,384]{1,0:T(8,128)(2,1)S(1)}, u32[]{:S(2)}, u32[]{:S(2)}) %collective-permute-start.13) | collective-permute-done | bytes 98336 | tf_op jit(solution)/shard_map/ppermute | solution.py:263
  16.9 1.2 collective-permute-start.15
  18.1 1.3 collective-permute-done.18
  19.7 4.3 %collective-permute-start.20 = (bf16[512,384]{1,0:T(8,128)(2,1)S(1)}, bf16[512,384]{1,0:T(8,128)(2,1)}, u32[]{:S(2)}, u32[]{:S(2)}) collective-permute-start(bf16[512,384]{1,0:T(8,128)(2,1)S(1)} %constant_dynamic-update-slice_fusion.refs_2_), channel_id=1, source_target_pairs={{1,2},{2,1},{5,6},{6,5},{9,10},{10,9},{13,14},{14,13},{17,18},{18,... | collective-permute-start | bytes 1179656 | tf_op jit(solution)/shard_map/ppermute | solution.py:263
  24.0 1.3 collective-permute-start.21
  25.3 1.0 collective-permute-start
  26.4 0.9 collective-permute-done.refs_9_
  27.4 2.7 %collective-permute-done.19.refs_3_ = bf16[512,384]{1,0:T(8,128)(2,1)} collective-permute-done((bf16[512,384]{1,0:T(8,128)(2,1)S(1)}, bf16[512,384]{1,0:T(8,128)(2,1)}, u32[]{:S(2)}, u32[]{:S(2)}) %collective-permute-start.19) | collective-permute-done | bytes 393248 | tf_op jit(solution)/shard_map/ppermute | solution.py:263
  30.2 1.4 collective-permute-start.14
  31.6 1.6 collective-permute-done.20
  33.2 3.0 %collective-permute-start.4 = (bf16[512,384]{1,0:T(8,128)(2,1)S(1)}, bf16[512,384]{1,0:T(8,128)(2,1)S(1)}, u32[]{:S(2)}, u32[]{:S(2)}) collective-permute-start(bf16[512,384]{1,0:T(8,128)(2,1)S(1)} %pad_maximum_fusion.refs_2_), channel_id=1, source_target_pairs={{1,2},{2,1},{5,6},{6,5},{9,10},{10,9},{13,14},{14,13},{17,18},{18,... | collective-permute-start | bytes 1179656 | tf_op jit(solution)/shard_map/ppermute | solution.py:263
  36.3 0.8 copy-done.1
  37.0 1.2 collective-permute-start.5
  38.7 3.1 %collective-permute-start.22 = (bf16[512,384]{1,0:T(8,128)(2,1)}, bf16[512,384]{1,0:T(8,128)(2,1)}, u32[]{:S(2)}, u32[]{:S(2)}) collective-permute-start(bf16[512,384]{1,0:T(8,128)(2,1)} %collective-permute-done.19.refs_3_), channel_id=1, source_target_pairs={{1,2},{2,1},{5,6},{6,5},{9,10},{10,9},{13,14},{14,13},{17,18},{18,... | collective-permute-start | bytes 1179656 | tf_op jit(solution)/shard_map/ppermute | solution.py:263
  41.8 22.2 %collective-permute-done.15.refs_0_ = bf16[256,4096]{1,0:T(8,128)(2,1)} collective-permute-done((bf16[256,4096]{1,0:T(8,128)(2,1)}, bf16[256,4096]{1,0:T(8,128)(2,1)}, u32[]{:S(2)}, u32[]{:S(2)}) %collective-permute-start.15) | collective-permute-done | bytes 2097184 | tf_op jit(solution)/shard_map/ppermute | solution.py:263
  64.1 1.2 collective-permute-start.16
  65.2 2.9 %collective-permute-start.23 = (bf16[512,384]{1,0:T(8,128)(2,1)}, bf16[512,384]{1,0:T(8,128)(2,1)}, u32[]{:S(2)}, u32[]{:S(2)}) collective-permute-start(bf16[512,384]{1,0:T(8,128)(2,1)} %collective-permute-done.20), channel_id=1, source_target_pairs={{1,0},{2,3},{5,4},{6,7},{9,8},{10,11},{13,12},{14,15},{17,16},{18,... | collective-permute-start | bytes 1179656 | tf_op jit(solution)/shard_map/ppermute | solution.py:263
  68.1 0.8 copy-done.3
  68.9 1.2 collective-permute-start.24
  70.1 4.3 %collective-permute-start.6 = (bf16[512,384]{1,0:T(8,128)(2,1)}, bf16[512,384]{1,0:T(8,128)(2,1)}, u32[]{:S(2)}, u32[]{:S(2)}) collective-permute-start(bf16[512,384]{1,0:T(8,128)(2,1)} %collective-permute-done.3.refs_3_), channel_id=1, source_target_pairs={{1,2},{2,1},{5,6},{6,5},{9,10},{10,9},{13,14},{14,13},{17,18},{18,... | collective-permute-start | bytes 1179656 | tf_op jit(solution)/shard_map/ppermute | solution.py:263
  74.4 1.7 %collective-permute-done.23 = bf16[512,384]{1,0:T(8,128)(2,1)} collective-permute-done((bf16[512,384]{1,0:T(8,128)(2,1)}, bf16[512,384]{1,0:T(8,128)(2,1)}, u32[]{:S(2)}, u32[]{:S(2)}) %collective-permute-start.23) | collective-permute-done | bytes 393248 | tf_op jit(solution)/shard_map/ppermute | solution.py:263
  76.2 4.9 %collective-permute-start.7 = (bf16[512,384]{1,0:T(8,128)(2,1)}, bf16[512,384]{1,0:T(8,128)(2,1)}, u32[]{:S(2)}, u32[]{:S(2)}) collective-permute-start(bf16[512,384]{1,0:T(8,128)(2,1)} %copy-done.10), channel_id=1, source_target_pairs={{1,0},{2,3},{5,4},{6,7},{9,8},{10,11},{13,12},{14,15},{17,16},{18,... | collective-permute-start | bytes 1179656 | tf_op jit(solution)/shard_map/ppermute | solution.py:263
  81.1 1.2 collective-permute-start.8
  82.3 1.0 broadcast_select_fusion.1.refs_4_
  83.9 4.3 %collective-permute-done.7 = bf16[512,384]{1,0:T(8,128)(2,1)} collective-permute-done((bf16[512,384]{1,0:T(8,128)(2,1)}, bf16[512,384]{1,0:T(8,128)(2,1)}, u32[]{:S(2)}, u32[]{:S(2)}) %collective-permute-start.7) | collective-permute-done | bytes 393248 | tf_op jit(solution)/shard_map/ppermute | solution.py:263
  88.2 4.1 %collective-permute-start.25 = (bf16[512,384]{1,0:T(8,128)(2,1)}, bf16[512,384]{1,0:T(8,128)(2,1)S(1)}, u32[]{:S(2)}, u32[]{:S(2)}) collective-permute-start(bf16[512,384]{1,0:T(8,128)(2,1)} %collective-permute-done.22), channel_id=1, source_target_pairs={{1,0},{2,3},{5,4},{6,7},{9,8},{10,11},{13,12},{14,15},{17,16},{18,... | collective-permute-start | bytes 1179656 | tf_op jit(solution)/shard_map/ppermute | solution.py:263
  92.4 1.1 broadcast_select_fusion.3.refs_4_
  93.4 1.3 collective-permute-start.10
  94.7 4.5 %collective-permute-done.26.refs_8_ = bf16[512,384]{1,0:T(8,128)(2,1)S(1)} collective-permute-done((bf16[512,384]{1,0:T(8,128)(2,1)S(1)}, bf16[512,384]{1,0:T(8,128)(2,1)S(1)}, u32[]{:S(2)}, u32[]{:S(2)}) %collective-permute-start.26) | collective-permute-done | bytes 393248 | tf_op jit(solution)/shard_map/ppermute | solution.py:263
  99.2 1.3 collective-permute-start.9
  100.6 1.1 broadcast_select_fusion.refs_5_
  101.6 1.3 collective-permute-start.27
  102.9 4.8 %collective-permute-done.10.refs_8_ = bf16[512,384]{1,0:T(8,128)(2,1)S(1)} collective-permute-done((bf16[512,384]{1,0:T(8,128)(2,1)S(1)}, bf16[512,384]{1,0:T(8,128)(2,1)S(1)}, u32[]{:S(2)}, u32[]{:S(2)}) %collective-permute-start.10) | collective-permute-done | bytes 393248 | tf_op jit(solution)/shard_map/ppermute | solution.py:263
  107.7 1.1 broadcast_select_fusion.2.refs_5_
  108.8 1.3 collective-permute-start.11
  110.0 3.9 %shard_map.80 = (f32[256,384]{1,0:T(8,128)S(1)}, f32[256,384]{1,0:T(8,128)S(1)}) custom-call(s32[3]{0:T(128)S(1)} %pad_add_fusion.here_ref, bf16[256,4096]{1,0:T(8,128)(2,1)S(1)} %bitcast.7, bf16[256,4096]{1,0:T(8,128)(2,1)} %collective-permute-done.14.refs_1_, bf16[512,384]{1,0:T(8,128)(2,1)S(1)} %constant_dynamic-update-slice_fusion.refs_2_, ...), custom_call_target="tpu_custom_call" | custom-call | flops 1610612736 | bytes 4194304 | tf_op jit(solution)/shard_map/pallas_call | solution.py:349
  113.9 3.8 %shard_map.74 = (f32[256,384]{1,0:T(8,128)S(1)}, f32[256,384]{1,0:T(8,128)S(1)}, bf16[256,512]{1,0:T(8,128)(2,1)S(1)}, bf16[256,512]{1,0:T(8,128)(2,1)S(1)}) custom-call(s32[3]{0:T(128)S(1)} %pad_add_fusion.here_ref, bf16[256,4096]{1,0:T(8,128)(2,1)S(1)} %bitcast.8, bf16[256,4096]{1,0:T(8,128)(2,1)} %collective-permute-done.14.refs_1_, ...), custom_call_target="tpu_custom_call" | custom-call | flops 1610612736 | bytes 4194304 | tf_op jit(solution)/shard_map/pallas_call | solution.py:349
  117.8 4.5 %shard_map.75 = (f32[256,384]{1,0:T(8,128)S(1)}, f32[256,384]{1,0:T(8,128)S(1)}, bf16[256,512]{1,0:T(8,128)(2,1)S(1)}, bf16[256,512]{1,0:T(8,128)(2,1)S(1)}) custom-call(s32[3]{0:T(128)S(1)} %pad_add_fusion.here_ref, bf16[256,4096]{1,0:T(8,128)(2,1)} %collective-permute-done.15.refs_0_, bf16[256,4096]{1,0:T(8,128)(2,1)} %collective-permute-done.16.refs_1_, ...), custom_call_target="tpu_custom_call" | custom-call | flops 1610612736 | bytes 4194304 | tf_op jit(solution)/shard_map/pallas_call | solution.py:349
  122.2 2.3 %collective-permute-done.11.piece_ref = bf16[512,384]{1,0:T(8,128)(2,1)S(1)} collective-permute-done((bf16[512,384]{1,0:T(8,128)(2,1)S(1)}, bf16[512,384]{1,0:T(8,128)(2,1)S(1)}, u32[]{:S(2)}, u32[]{:S(2)}) %collective-permute-start.11) | collective-permute-done | bytes 393248 | tf_op jit(solution)/shard_map/ppermute | solution.py:263
  124.5 1.2 shard_map.76
  125.8 3.3 %collective-permute-start.17 = (bf16[128,256]{1,0:T(8,128)(2,1)S(1)}, bf16[128,256]{1,0:T(8,128)(2,1)S(1)}, u32[]{:S(2)}, u32[]{:S(2)}) collective-permute-start(bf16[128,256]{1,0:T(8,128)(2,1)S(1)} %get-tuple-element.97), channel_id=1, source_target_pairs={{0,16},{1,17},{2,18},{3,19},{4,20},{5,21},{6,22},{7,23},{8,24},{9,... | collective-permute-start | bytes 196616 | tf_op jit(solution)/shard_map/ppermute | solution.py:263
  129.1 4.5 %shard_map.77 = (f32[256,384]{1,0:T(8,128)S(1)}, f32[256,384]{1,0:T(8,128)S(1)}) custom-call(s32[3]{0:T(128)S(1)} %pad_add_fusion.here_ref, bf16[256,4096]{1,0:T(8,128)(2,1)} %collective-permute-done.15.refs_0_, bf16[256,4096]{1,0:T(8,128)(2,1)} %collective-permute-done.16.refs_1_, bf16[512,384]{1,0:T(8,128)(2,1)S(1)} %constant_dynamic-update-slice_fusion.refs_2_, ...), custom_call_target="tpu_custom_call" | custom-call | flops 1610612736 | bytes 4194304 | tf_op jit(solution)/shard_map/pallas_call | solution.py:349
  133.6 2.5 %shard_map.78 = (bf16[256,256]{1,0:T(8,128)(2,1)S(1)}, bf16[256,256]{1,0:T(8,128)(2,1)S(1)}) custom-call(s32[3]{0:T(128)S(1)} %pad_add_fusion.here_ref, f32[16]{0:T(128)S(1)} %copy-done.8, bf16[128,256]{1,0:T(8,128)(2,1)S(1)} %collective-permute-done.17.base_ref, bf16[256,384]{1,0:T(8,128)(2,1)S(1)} %get-tuple-element.98.refs_0_, ...), custom_call_target="tpu_custom_call" | custom-call | flops 201326592 | bytes 4194304 | tf_op jit(solution)/shard_map/pallas_call | solution.py:378
  136.1 2.5 %shard_map.79 = (bf16[256,256]{1,0:T(8,128)(2,1)S(1)}, bf16[256,256]{1,0:T(8,128)(2,1)S(1)}) custom-call(s32[3]{0:T(128)S(1)} %pad_add_fusion.here_ref, f32[16]{0:T(128)S(1)} %copy-done.8, bf16[128,256]{1,0:T(8,128)(2,1)S(1)} %collective-permute-done.17.base_ref, bf16[256,384]{1,0:T(8,128)(2,1)S(1)} %get-tuple-element.98.refs_0_, ...), custom_call_target="tpu_custom_call" | custom-call | flops 201326592 | bytes 4194304 | tf_op jit(solution)/shard_map/pallas_call | solution.py:378
  138.6 2.5 %shard_map.81 = (bf16[256,256]{1,0:T(8,128)(2,1)S(1)}, bf16[256,256]{1,0:T(8,128)(2,1)S(1)}) custom-call(s32[3]{0:T(128)S(1)} %pad_add_fusion.here_ref, f32[16]{0:T(128)S(1)} %copy-done.8, bf16[128,256]{1,0:T(8,128)(2,1)S(1)} %collective-permute-done.17.base_ref, bf16[256,384]{1,0:T(8,128)(2,1)S(1)} %get-tuple-element.98.refs_0_, ...), custom_call_target="tpu_custom_call" | custom-call | flops 201326592 | bytes 4194304 | tf_op jit(solution)/shard_map/pallas_call | solution.py:378
  141.1 2.5 %shard_map.82 = (bf16[256,256]{1,0:T(8,128)(2,1)S(1)}, bf16[256,256]{1,0:T(8,128)(2,1)S(1)}) custom-call(s32[3]{0:T(128)S(1)} %pad_add_fusion.here_ref, f32[16]{0:T(128)S(1)} %copy-done.8, bf16[128,256]{1,0:T(8,128)(2,1)S(1)} %collective-permute-done.17.base_ref, bf16[256,384]{1,0:T(8,128)(2,1)S(1)} %get-tuple-element.98.refs_0_, ...), custom_call_target="tpu_custom_call" | custom-call | flops 201326592 | bytes 4194304 | tf_op jit(solution)/shard_map/pallas_call | solution.py:378
  143.6 2.3 %collective-permute-start.29 = (bf16[256,256]{1,0:T(8,128)(2,1)S(1)}, bf16[256,256]{1,0:T(8,128)(2,1)S(1)}, u32[]{:S(2)}, u32[]{:S(2)}) collective-permute-start(bf16[256,256]{1,0:T(8,128)(2,1)S(1)} %get-tuple-element.134), channel_id=1, source_target_pairs={{0,4},{1,5},{2,6},{3,7},{4,0},{5,1},{6,2},{7,3},{8,12},{9,13},{10,... | collective-permute-start | bytes 393224 | tf_op jit(solution)/shard_map/ppermute | solution.py:263
  146.0 1.2 collective-permute-start.31
  147.2 0.9 collective-permute-start.33
  148.1 1.2 collective-permute-start.30
  149.6 1.1 collective-permute-done.31.refs_5_
  150.7 4.3 %collective-permute-done.33.refs_7_ = bf16[256,256]{1,0:T(8,128)(2,1)S(1)} collective-permute-done((bf16[256,256]{1,0:T(8,128)(2,1)S(1)}, bf16[256,256]{1,0:T(8,128)(2,1)S(1)}, u32[]{:S(2)}, u32[]{:S(2)}) %collective-permute-start.33) | collective-permute-done | bytes 131104 | tf_op jit(solution)/shard_map/ppermute | solution.py:263
  154.9 1.4 collective-permute-done.30.refs_4_
  156.3 3.4 %collective-permute-done.32.refs_6_ = bf16[256,256]{1,0:T(8,128)(2,1)S(1)} collective-permute-done((bf16[256,256]{1,0:T(8,128)(2,1)S(1)}, bf16[256,256]{1,0:T(8,128)(2,1)S(1)}, u32[]{:S(2)}, u32[]{:S(2)}) %collective-permute-start.32) | collective-permute-done | bytes 131104 | tf_op jit(solution)/shard_map/ppermute | solution.py:263
  159.7 1.6 %shard_map.83 = bf16[256,2048]{1,0:T(8,128)(2,1)} custom-call(s32[3]{0:T(128)S(1)} %pad_add_fusion.here_ref, bf16[256,256]{1,0:T(8,128)(2,1)S(1)} %get-tuple-element.130.refs_0_, bf16[256,256]{1,0:T(8,128)(2,1)S(1)} %get-tuple-element.133.refs_1_, bf16[256,256]{1,0:T(8,128)(2,1)S(1)} %collective-permute-done.28.refs_2_, ...), custom_call_target="tpu_custom_call" | custom-call | bytes 4194304 | tf_op jit(solution)/shard_map/pallas_call | solution.py:395
  (51 shorter events, 2.4 us)
Async XLA Ops:
  0.0 30.2 %copy-start = (bf16[1,256,4096]{2,1,0:T(8,128)(2,1)S(1)}, bf16[1,256,4096]{2,1,0:T(8,128)(2,1)}, u32[]{:S(2)}) copy-start(bf16[1,256,4096]{2,1,0:T(8,128)(2,1)} %param.7) | copy-start | bytes 6291460
  0.9 1.0 copy-start.5
  1.9 0.9 copy-start.6
  2.8 0.9 copy-start.7
  3.7 0.7 copy-start.9
  5.4 11.4 %collective-permute-start.1 = (bf16[144,384]{1,0:T(8,128)(2,1)S(1)}, bf16[144,384]{1,0:T(8,128)(2,1)S(1)}, u32[]{:S(2)}, u32[]{:S(2)}) collective-permute-start(bf16[144,384]{1,0:T(8,128)(2,1)S(1)} %get-tuple-element.72), channel_id=1, source_target_pairs={{0,8},{1,9},{2,10},{3,11},{4,12},{5,13},{6,14},{7,15},{8,0},{9,1},... | collective-permute-start | bytes 331784 | tf_op jit(solution)/shard_map/ppermute | solution.py:263
  6.7 10.2 %collective-permute-start.2 = (bf16[144,384]{1,0:T(8,128)(2,1)S(1)}, bf16[144,384]{1,0:T(8,128)(2,1)S(1)}, u32[]{:S(2)}, u32[]{:S(2)}) collective-permute-start(bf16[144,384]{1,0:T(8,128)(2,1)S(1)} %get-tuple-element.73), channel_id=1, source_target_pairs={{0,12},{1,13},{2,14},{3,15},{4,8},{5,9},{6,10},{7,11},{8,4},{9,5},... | collective-permute-start | bytes 331784 | tf_op jit(solution)/shard_map/ppermute | solution.py:263
  7.8 6.9 %collective-permute-start.12 = (bf16[128,384]{1,0:T(8,128)(2,1)S(1)}, bf16[128,384]{1,0:T(8,128)(2,1)S(1)}, u32[]{:S(2)}, u32[]{:S(2)}) collective-permute-start(bf16[128,384]{1,0:T(8,128)(2,1)S(1)} %get-tuple-element.82), channel_id=1, source_target_pairs={{0,8},{1,9},{2,10},{3,11},{4,12},{5,13},{6,14},{7,15},{8,0},{9,1},... | collective-permute-start | bytes 294920 | tf_op jit(solution)/shard_map/ppermute | solution.py:263
  9.0 7.8 %collective-permute-start.13 = (bf16[128,384]{1,0:T(8,128)(2,1)S(1)}, bf16[128,384]{1,0:T(8,128)(2,1)S(1)}, u32[]{:S(2)}, u32[]{:S(2)}) collective-permute-start(bf16[128,384]{1,0:T(8,128)(2,1)S(1)} %get-tuple-element.83), channel_id=1, source_target_pairs={{0,12},{1,13},{2,14},{3,15},{4,8},{5,9},{6,10},{7,11},{8,4},{9,5},... | collective-permute-start | bytes 294920 | tf_op jit(solution)/shard_map/ppermute | solution.py:263
  16.9 47.2 %collective-permute-start.15 = (bf16[256,4096]{1,0:T(8,128)(2,1)}, bf16[256,4096]{1,0:T(8,128)(2,1)}, u32[]{:S(2)}, u32[]{:S(2)}) collective-permute-start(bf16[256,4096]{1,0:T(8,128)(2,1)} %bitcast.5), channel_id=1, source_target_pairs={{0,8},{1,9},{2,10},{3,11},{4,12},{5,13},{6,14},{7,15},{8,0},{9,1},... | collective-permute-start | bytes 6291464 | tf_op jit(solution)/shard_map/ppermute | solution.py:263
  18.1 1.3 collective-permute-start.18
  19.5 10.7 %collective-permute-start.19 = (bf16[512,384]{1,0:T(8,128)(2,1)S(1)}, bf16[512,384]{1,0:T(8,128)(2,1)}, u32[]{:S(2)}, u32[]{:S(2)}) collective-permute-start(bf16[512,384]{1,0:T(8,128)(2,1)S(1)} %constant_dynamic-update-slice_fusion.refs_2_), channel_id=1, source_target_pairs={{0,1},{1,0},{2,3},{3,2},{4,5},{5,4},{6,7},{7,6},{8,9},{9,8},{10,11... | collective-permute-start | bytes 1179656 | tf_op jit(solution)/shard_map/ppermute | solution.py:263
  19.7 13.5 %collective-permute-start.20 = (bf16[512,384]{1,0:T(8,128)(2,1)S(1)}, bf16[512,384]{1,0:T(8,128)(2,1)}, u32[]{:S(2)}, u32[]{:S(2)}) collective-permute-start(bf16[512,384]{1,0:T(8,128)(2,1)S(1)} %constant_dynamic-update-slice_fusion.refs_2_), channel_id=1, source_target_pairs={{1,2},{2,1},{5,6},{6,5},{9,10},{10,9},{13,14},{14,13},{17,18},{18,... | collective-permute-start | bytes 1179656 | tf_op jit(solution)/shard_map/ppermute | solution.py:263
  24.0 12.2 %collective-permute-start.21 = (bf16[512,384]{1,0:T(8,128)(2,1)S(1)}, bf16[512,384]{1,0:T(8,128)(2,1)S(1)}, u32[]{:S(2)}, u32[]{:S(2)}) collective-permute-start(bf16[512,384]{1,0:T(8,128)(2,1)S(1)} %constant_dynamic-update-slice_fusion.refs_2_), channel_id=1, source_target_pairs={{0,16},{1,17},{2,18},{3,19},{4,20},{5,21},{6,22},{7,23},{8,24},{9,... | collective-permute-start | bytes 1179656 | tf_op jit(solution)/shard_map/ppermute | solution.py:263
  25.3 2.0 %collective-permute-start = (bf16[144,384]{1,0:T(8,128)(2,1)S(1)}, bf16[144,384]{1,0:T(8,128)(2,1)S(1)}, u32[]{:S(2)}, u32[]{:S(2)}) collective-permute-start(bf16[144,384]{1,0:T(8,128)(2,1)S(1)} %get-tuple-element.71), channel_id=1, source_target_pairs={{0,4},{1,5},{2,6},{3,7},{4,0},{5,1},{6,2},{7,3},{8,12},{9,13},{10,... | collective-permute-start | bytes 331784 | tf_op jit(solution)/shard_map/ppermute | solution.py:263
  27.4 11.4 %collective-permute-start.3 = (bf16[512,384]{1,0:T(8,128)(2,1)S(1)}, bf16[512,384]{1,0:T(8,128)(2,1)}, u32[]{:S(2)}, u32[]{:S(2)}) collective-permute-start(bf16[512,384]{1,0:T(8,128)(2,1)S(1)} %pad_maximum_fusion.refs_2_), channel_id=1, source_target_pairs={{0,1},{1,0},{2,3},{3,2},{4,5},{5,4},{6,7},{7,6},{8,9},{9,8},{10,11... | collective-permute-start | bytes 1179656 | tf_op jit(solution)/shard_map/ppermute | solution.py:263
  30.2 79.8 %collective-permute-start.14 = (bf16[256,4096]{1,0:T(8,128)(2,1)S(1)}, bf16[256,4096]{1,0:T(8,128)(2,1)}, u32[]{:S(2)}, u32[]{:S(2)}) collective-permute-start(bf16[256,4096]{1,0:T(8,128)(2,1)S(1)} %bitcast.6), channel_id=1, source_target_pairs={{0,4},{1,5},{2,6},{3,7},{4,0},{5,1},{6,2},{7,3},{8,12},{9,13},{10,... | collective-permute-start | bytes 6291464 | tf_op jit(solution)/shard_map/ppermute | solution.py:263
  33.2 32.0 %collective-permute-start.4 = (bf16[512,384]{1,0:T(8,128)(2,1)S(1)}, bf16[512,384]{1,0:T(8,128)(2,1)S(1)}, u32[]{:S(2)}, u32[]{:S(2)}) collective-permute-start(bf16[512,384]{1,0:T(8,128)(2,1)S(1)} %pad_maximum_fusion.refs_2_), channel_id=1, source_target_pairs={{1,2},{2,1},{5,6},{6,5},{9,10},{10,9},{13,14},{14,13},{17,18},{18,... | collective-permute-start | bytes 1179656 | tf_op jit(solution)/shard_map/ppermute | solution.py:263
  36.3 0.8 copy-start.1
  37.0 31.1 %collective-permute-start.5 = (bf16[512,384]{1,0:T(8,128)(2,1)S(1)}, bf16[512,384]{1,0:T(8,128)(2,1)S(1)}, u32[]{:S(2)}, u32[]{:S(2)}) collective-permute-start(bf16[512,384]{1,0:T(8,128)(2,1)S(1)} %pad_maximum_fusion.refs_2_), channel_id=1, source_target_pairs={{0,16},{1,17},{2,18},{3,19},{4,20},{5,21},{6,22},{7,23},{8,24},{9,... | collective-permute-start | bytes 1179656 | tf_op jit(solution)/shard_map/ppermute | solution.py:263
  38.7 31.4 %collective-permute-start.22 = (bf16[512,384]{1,0:T(8,128)(2,1)}, bf16[512,384]{1,0:T(8,128)(2,1)}, u32[]{:S(2)}, u32[]{:S(2)}) collective-permute-start(bf16[512,384]{1,0:T(8,128)(2,1)} %collective-permute-done.19.refs_3_), channel_id=1, source_target_pairs={{1,2},{2,1},{5,6},{6,5},{9,10},{10,9},{13,14},{14,13},{17,18},{18,... | collective-permute-start | bytes 1179656 | tf_op jit(solution)/shard_map/ppermute | solution.py:263
  64.1 53.7 %collective-permute-start.16 = (bf16[256,4096]{1,0:T(8,128)(2,1)}, bf16[256,4096]{1,0:T(8,128)(2,1)}, u32[]{:S(2)}, u32[]{:S(2)}) collective-permute-start(bf16[256,4096]{1,0:T(8,128)(2,1)} %collective-permute-done.15.refs_0_), channel_id=1, source_target_pairs={{0,4},{1,5},{2,6},{3,7},{4,0},{5,1},{6,2},{7,3},{8,12},{9,13},{10,... | collective-permute-start | bytes 6291464 | tf_op jit(solution)/shard_map/ppermute | solution.py:263
  65.2 2.9 %copy-start.10 = (bf16[512,384]{1,0:T(8,128)(2,1)}, bf16[512,384]{1,0:T(8,128)(2,1)S(1)}, u32[]{:S(2)}) copy-start(bf16[512,384]{1,0:T(8,128)(2,1)S(1)} %collective-permute-done.4) | copy-start | bytes 1179652
  65.2 10.9 %collective-permute-start.23 = (bf16[512,384]{1,0:T(8,128)(2,1)}, bf16[512,384]{1,0:T(8,128)(2,1)}, u32[]{:S(2)}, u32[]{:S(2)}) collective-permute-start(bf16[512,384]{1,0:T(8,128)(2,1)} %collective-permute-done.20), channel_id=1, source_target_pairs={{1,0},{2,3},{5,4},{6,7},{9,8},{10,11},{13,12},{14,15},{17,16},{18,... | collective-permute-start | bytes 1179656 | tf_op jit(solution)/shard_map/ppermute | solution.py:263
  68.1 0.8 copy-start.3
  68.9 12.2 %collective-permute-start.24 = (bf16[512,384]{1,0:T(8,128)(2,1)}, bf16[512,384]{1,0:T(8,128)(2,1)}, u32[]{:S(2)}, u32[]{:S(2)}) collective-permute-start(bf16[512,384]{1,0:T(8,128)(2,1)} %collective-permute-done.19.refs_3_), channel_id=1, source_target_pairs={{0,16},{1,17},{2,18},{3,19},{4,20},{5,21},{6,22},{7,23},{8,24},{9,... | collective-permute-start | bytes 1179656 | tf_op jit(solution)/shard_map/ppermute | solution.py:263
  70.1 13.6 %collective-permute-start.6 = (bf16[512,384]{1,0:T(8,128)(2,1)}, bf16[512,384]{1,0:T(8,128)(2,1)}, u32[]{:S(2)}, u32[]{:S(2)}) collective-permute-start(bf16[512,384]{1,0:T(8,128)(2,1)} %collective-permute-done.3.refs_3_), channel_id=1, source_target_pairs={{1,2},{2,1},{5,6},{6,5},{9,10},{10,9},{13,14},{14,13},{17,18},{18,... | collective-permute-start | bytes 1179656 | tf_op jit(solution)/shard_map/ppermute | solution.py:263
  76.2 12.0 %collective-permute-start.7 = (bf16[512,384]{1,0:T(8,128)(2,1)}, bf16[512,384]{1,0:T(8,128)(2,1)}, u32[]{:S(2)}, u32[]{:S(2)}) collective-permute-start(bf16[512,384]{1,0:T(8,128)(2,1)} %copy-done.10), channel_id=1, source_target_pairs={{1,0},{2,3},{5,4},{6,7},{9,8},{10,11},{13,12},{14,15},{17,16},{18,... | collective-permute-start | bytes 1179656 | tf_op jit(solution)/shard_map/ppermute | solution.py:263
  81.1 29.0 %copy-start.2 = (bf16[512,384]{1,0:T(8,128)(2,1)S(1)}, bf16[512,384]{1,0:T(8,128)(2,1)}, u32[]{:S(2)}) copy-start(bf16[512,384]{1,0:T(8,128)(2,1)} %copy-done.1) | copy-start | bytes 1179652
  81.1 11.3 %collective-permute-start.8 = (bf16[512,384]{1,0:T(8,128)(2,1)}, bf16[512,384]{1,0:T(8,128)(2,1)S(1)}, u32[]{:S(2)}, u32[]{:S(2)}) collective-permute-start(bf16[512,384]{1,0:T(8,128)(2,1)} %collective-permute-done.3.refs_3_), channel_id=1, source_target_pairs={{0,16},{1,17},{2,18},{3,19},{4,20},{5,21},{6,22},{7,23},{8,24},{9,... | collective-permute-start | bytes 1179656 | tf_op jit(solution)/shard_map/ppermute | solution.py:263
  83.7 15.5 %collective-permute-start.26 = (bf16[512,384]{1,0:T(8,128)(2,1)S(1)}, bf16[512,384]{1,0:T(8,128)(2,1)S(1)}, u32[]{:S(2)}, u32[]{:S(2)}) collective-permute-start(bf16[512,384]{1,0:T(8,128)(2,1)S(1)} %broadcast_select_fusion.1.refs_4_), channel_id=1, source_target_pairs={{0,16},{1,17},{2,18},{3,19},{4,20},{5,21},{6,22},{7,23},{8,24},{9,... | collective-permute-start | bytes 1179656 | tf_op jit(solution)/shard_map/ppermute | solution.py:263
  88.2 12.3 %collective-permute-start.25 = (bf16[512,384]{1,0:T(8,128)(2,1)}, bf16[512,384]{1,0:T(8,128)(2,1)S(1)}, u32[]{:S(2)}, u32[]{:S(2)}) collective-permute-start(bf16[512,384]{1,0:T(8,128)(2,1)} %collective-permute-done.22), channel_id=1, source_target_pairs={{1,0},{2,3},{5,4},{6,7},{9,8},{10,11},{13,12},{14,15},{17,16},{18,... | collective-permute-start | bytes 1179656 | tf_op jit(solution)/shard_map/ppermute | solution.py:263
  93.4 14.2 %collective-permute-start.10 = (bf16[512,384]{1,0:T(8,128)(2,1)S(1)}, bf16[512,384]{1,0:T(8,128)(2,1)S(1)}, u32[]{:S(2)}, u32[]{:S(2)}) collective-permute-start(bf16[512,384]{1,0:T(8,128)(2,1)S(1)} %broadcast_select_fusion.3.refs_4_), channel_id=1, source_target_pairs={{0,16},{1,17},{2,18},{3,19},{4,20},{5,21},{6,22},{7,23},{8,24},{9,... | collective-permute-start | bytes 1179656 | tf_op jit(solution)/shard_map/ppermute | solution.py:263
  99.2 8.4 %collective-permute-start.9 = (bf16[512,384]{1,0:T(8,128)(2,1)}, bf16[512,384]{1,0:T(8,128)(2,1)S(1)}, u32[]{:S(2)}, u32[]{:S(2)}) collective-permute-start(bf16[512,384]{1,0:T(8,128)(2,1)} %collective-permute-done.6), channel_id=1, source_target_pairs={{1,0},{2,3},{5,4},{6,7},{9,8},{10,11},{13,12},{14,15},{17,16},{18,... | collective-permute-start | bytes 1179656 | tf_op jit(solution)/shard_map/ppermute | solution.py:263
  101.6 32.0 %collective-permute-start.27 = (bf16[512,384]{1,0:T(8,128)(2,1)S(1)}, bf16[512,384]{1,0:T(8,128)(2,1)S(1)}, u32[]{:S(2)}, u32[]{:S(2)}) collective-permute-start(bf16[512,384]{1,0:T(8,128)(2,1)S(1)} %broadcast_select_fusion.refs_5_), channel_id=1, source_target_pairs={{0,16},{1,17},{2,18},{3,19},{4,20},{5,21},{6,22},{7,23},{8,24},{9,... | collective-permute-start | bytes 1179656 | tf_op jit(solution)/shard_map/ppermute | solution.py:263
  108.7 5.2 %copy-start.4 = (bf16[512,384]{1,0:T(8,128)(2,1)S(1)}, bf16[512,384]{1,0:T(8,128)(2,1)}, u32[]{:S(2)}) copy-start(bf16[512,384]{1,0:T(8,128)(2,1)} %copy-done.3) | copy-start | bytes 1179652
  108.8 15.8 %collective-permute-start.11 = (bf16[512,384]{1,0:T(8,128)(2,1)S(1)}, bf16[512,384]{1,0:T(8,128)(2,1)S(1)}, u32[]{:S(2)}, u32[]{:S(2)}) collective-permute-start(bf16[512,384]{1,0:T(8,128)(2,1)S(1)} %broadcast_select_fusion.2.refs_5_), channel_id=1, source_target_pairs={{0,16},{1,17},{2,18},{3,19},{4,20},{5,21},{6,22},{7,23},{8,24},{9,... | collective-permute-start | bytes 1179656 | tf_op jit(solution)/shard_map/ppermute | solution.py:263
  125.8 7.9 %copy-start.8 = (f32[16]{0:T(128)S(1)}, f32[16]{0:T(128)}, u32[]{:S(2)}) copy-start(f32[16]{0:T(128)} %gate_ref.7) | copy-start | bytes 196
  125.8 7.8 %collective-permute-start.17 = (bf16[128,256]{1,0:T(8,128)(2,1)S(1)}, bf16[128,256]{1,0:T(8,128)(2,1)S(1)}, u32[]{:S(2)}, u32[]{:S(2)}) collective-permute-start(bf16[128,256]{1,0:T(8,128)(2,1)S(1)} %get-tuple-element.97), channel_id=1, source_target_pairs={{0,16},{1,17},{2,18},{3,19},{4,20},{5,21},{6,22},{7,23},{8,24},{9,... | collective-permute-start | bytes 196616 | tf_op jit(solution)/shard_map/ppermute | solution.py:263
  143.6 5.7 %collective-permute-start.29 = (bf16[256,256]{1,0:T(8,128)(2,1)S(1)}, bf16[256,256]{1,0:T(8,128)(2,1)S(1)}, u32[]{:S(2)}, u32[]{:S(2)}) collective-permute-start(bf16[256,256]{1,0:T(8,128)(2,1)S(1)} %get-tuple-element.134), channel_id=1, source_target_pairs={{0,4},{1,5},{2,6},{3,7},{4,0},{5,1},{6,2},{7,3},{8,12},{9,13},{10,... | collective-permute-start | bytes 393224 | tf_op jit(solution)/shard_map/ppermute | solution.py:263
  146.0 3.7 %collective-permute-start.28 = (bf16[256,256]{1,0:T(8,128)(2,1)S(1)}, bf16[256,256]{1,0:T(8,128)(2,1)S(1)}, u32[]{:S(2)}, u32[]{:S(2)}) collective-permute-start(bf16[256,256]{1,0:T(8,128)(2,1)S(1)} %get-tuple-element.131), channel_id=1, source_target_pairs={{0,4},{1,5},{2,6},{3,7},{4,0},{5,1},{6,2},{7,3},{8,12},{9,13},{10,... | collective-permute-start | bytes 393224 | tf_op jit(solution)/shard_map/ppermute | solution.py:263
  146.0 4.6 %collective-permute-start.31 = (bf16[256,256]{1,0:T(8,128)(2,1)S(1)}, bf16[256,256]{1,0:T(8,128)(2,1)S(1)}, u32[]{:S(2)}, u32[]{:S(2)}) collective-permute-start(bf16[256,256]{1,0:T(8,128)(2,1)S(1)} %get-tuple-element.125), channel_id=1, source_target_pairs={{0,8},{1,9},{2,10},{3,11},{4,12},{5,13},{6,14},{7,15},{8,0},{9,1},... | collective-permute-start | bytes 393224 | tf_op jit(solution)/shard_map/ppermute | solution.py:263
  147.2 7.7 %collective-permute-start.33 = (bf16[256,256]{1,0:T(8,128)(2,1)S(1)}, bf16[256,256]{1,0:T(8,128)(2,1)S(1)}, u32[]{:S(2)}, u32[]{:S(2)}) collective-permute-start(bf16[256,256]{1,0:T(8,128)(2,1)S(1)} %get-tuple-element.126), channel_id=1, source_target_pairs={{0,12},{1,13},{2,14},{3,15},{4,8},{5,9},{6,10},{7,11},{8,4},{9,5},... | collective-permute-start | bytes 393224 | tf_op jit(solution)/shard_map/ppermute | solution.py:263
  148.1 8.2 %collective-permute-start.30 = (bf16[256,256]{1,0:T(8,128)(2,1)S(1)}, bf16[256,256]{1,0:T(8,128)(2,1)S(1)}, u32[]{:S(2)}, u32[]{:S(2)}) collective-permute-start(bf16[256,256]{1,0:T(8,128)(2,1)S(1)} %get-tuple-element.122), channel_id=1, source_target_pairs={{0,8},{1,9},{2,10},{3,11},{4,12},{5,13},{6,14},{7,15},{8,0},{9,1},... | collective-permute-start | bytes 393224 | tf_op jit(solution)/shard_map/ppermute | solution.py:263
  149.3 10.4 %collective-permute-start.32 = (bf16[256,256]{1,0:T(8,128)(2,1)S(1)}, bf16[256,256]{1,0:T(8,128)(2,1)S(1)}, u32[]{:S(2)}, u32[]{:S(2)}) collective-permute-start(bf16[256,256]{1,0:T(8,128)(2,1)S(1)} %get-tuple-element.123), channel_id=1, source_target_pairs={{0,12},{1,13},{2,14},{3,15},{4,8},{5,9},{6,10},{7,11},{8,4},{9,5},... | collective-permute-start | bytes 393224 | tf_op jit(solution)/shard_map/ppermute | solution.py:263

commit v4 on v3

--- a/solution.py
+++ b/solution.py
@@ -36,10 +36,8 @@
     return pl.multiple_of(offset, HEAD_SIZE)
 
 
-def pack_body(
-    group, early, here_ref, valid_ref, mask_ref, wq_ref, wk_ref, wv_ref, *refs
-):
-    outs, facts_ref, sems = refs[: 2 * MEMBERS], refs[-2], refs[-1]
+def pack_body(group, here_ref, valid_ref, mask_ref, wq_ref, wk_ref, wv_ref, *refs):
+    outs, facts_ref, sems = refs[:MEMBERS], refs[-2], refs[-1]
     rows = wk_ref.shape[0]
     row = lax.broadcasted_iota(jnp.int32, facts_ref.shape, 0)
     facts = jnp.where(row < HALF, valid_ref[0, 0], mask_ref[0, 0, 1, 0])
@@ -50,30 +48,23 @@
         copies.append(pltpu.make_async_copy(source, target, sems.at[len(copies)]))
         copies[-1].start()
 
-    for k in range(MEMBERS):
-        head = here_ref[1] ^ k
-        first, second = outs[2 * k : 2 * k + 2]
+    for k in (2, 3, 1, 0):
+        head, out = here_ref[1] ^ k, outs[k]
         at = aligned(head * HEAD_SIZE)
+        top = pl.ds(0, rows)
+        copy(wk_ref.at[:, pl.ds(at, HEAD_SIZE)], out.at[top, pl.ds(0, HEAD_SIZE)])
+        copy(wv_ref.at[:, pl.ds(at, HEAD_SIZE)], out.at[top, pl.ds(HEAD_SIZE, HEAD_SIZE)])
         wide = group * HEAD_SIZE
-        copy(wk_ref.at[:, pl.ds(at, HEAD_SIZE)], first.at[pl.ds(0, rows), pl.ds(0, HEAD_SIZE)])
-        copy(wv_ref.at[:, pl.ds(at, HEAD_SIZE)], first.at[pl.ds(0, rows), pl.ds(HEAD_SIZE, HEAD_SIZE)])
-        if early:
-            copy(
-                wq_ref.at[:, pl.ds(aligned(head * wide), early * HEAD_SIZE)],
-                first.at[pl.ds(0, rows), pl.ds(2 * HEAD_SIZE, early * HEAD_SIZE)],
-            )
-        copy(facts_ref, first.at[pl.ds(rows, META_ROWS), :])
-        copy(
-            wq_ref.at[:, pl.ds(aligned(head * wide + early * HEAD_SIZE), (group - early) * HEAD_SIZE)],
-            second,
-        )
+        copy(wq_ref.at[:, pl.ds(aligned(head * wide), wide)], out.at[top, pl.ds(2 * HEAD_SIZE, wide)])
+        copy(facts_ref, out.at[pl.ds(rows, META_ROWS), :])
     for one in copies:
         one.wait()
 
 
-def columns_of(tokens_ref, here_ref, piece, line):
+def columns_of(tokens_ref, here_ref, piece, members, line):
     if not line:
-        return tokens_ref[:, pl.ds(piece * MEMBERS * HEAD_SIZE, MEMBERS * HEAD_SIZE)]
+        first = (piece * MEMBERS + members[0]) * HEAD_SIZE
+        return tokens_ref[:, pl.ds(first, len(members) * HEAD_SIZE)]
     g, m, z = here_ref[0] ^ (piece // line), here_ref[1], here_ref[2]
     inside = (z == 1) | (z == 2)
     step = piece % line
@@ -83,7 +74,7 @@
         z = jnp.where(inside, z ^ (5 - step), z ^ step)
     parts = [
         tokens_ref[:, pl.ds(aligned(((g * MEMBERS + (m ^ k)) * line + z) * HEAD_SIZE), HEAD_SIZE)]
-        for k in range(MEMBERS)
+        for k in members
     ]
     return jnp.concatenate(parts, axis=1)
 
@@ -98,19 +89,24 @@
     return lax.broadcasted_iota(jnp.int32, shape, dimension).astype(jnp.float32)
 
 
-def project_body(n_segs, n_pieces, keep_last, line, here_ref, *refs):
-    tokens, pieces = refs[:n_segs], refs[n_segs : n_segs + n_pieces - 1]
-    outs = refs[n_segs + n_pieces - 1 :]
-    for n in range(n_segs):
-        total = None
-        for p in range(n_pieces - 1):
-            term = jnp.dot(
-                columns_of(tokens[n], here_ref, p, line), pieces[p][...], preferred_element_type=jnp.float32
+def project_body(places, line, n_pieces, first, here_ref, *refs):
+    tokens, pieces = refs[:2], refs[2 : 2 + 2 * len(places)]
+    rest = refs[2 + 2 * len(places) :]
+    length = tokens[0].shape[0]
+    total = None if first else jnp.concatenate([rest[0][...], rest[1][...]], axis=0)
+    outs = rest if first else rest[2:]
+    for half in range(2):
+        members = (0, 1) if half == 0 else (2, 3)
+        for n, place in enumerate(places):
+            columns = jnp.concatenate(
+                [columns_of(one, here_ref, place, members, line) for one in tokens], axis=0
             )
+            term = jnp.dot(columns, pieces[2 * n + half][...], preferred_element_type=jnp.float32)
             total = term if total is None else total + term
-        outs[n][...] = total
-        if keep_last:
-            outs[n_segs + n][...] = columns_of(tokens[n], here_ref, n_pieces - 1, line)
+    for n in range(2):
+        outs[n][...] = total[n * length : (n + 1) * length]
+        if first:
+            outs[2 + n][...] = columns_of(tokens[n], here_ref, n_pieces - 1, range(MEMBERS), line)
 
 
 def sigma_plus(v):
@@ -122,23 +118,30 @@
     return high, (values - high.astype(jnp.float32)).astype(jnp.bfloat16)
 
 
-def kv_body(piece_ref, *refs):
+def last_piece(columns_ref, upper_ref, lower_ref, start, width):
+    half = upper_ref.shape[0]
+    at = slice(start, start + width)
+    lost = 2 * HEAD_SIZE if start else 0
+    term = jnp.dot(columns_ref[:, :half], upper_ref[:, at], preferred_element_type=jnp.float32)
+    return term + jnp.dot(columns_ref[:, half:], lower_ref[:, start - lost : start - lost + width], preferred_element_type=jnp.float32)
+
+
+def kv_body(upper_ref, lower_ref, *refs):
     sums, lasts, messages = refs[:MEMBERS], refs[MEMBERS : 2 * MEMBERS], refs[2 * MEMBERS : 3 * MEMBERS]
     outs = refs[3 * MEMBERS :]
     whole = None
     for seg in range(MEMBERS):
-        total = sums[seg][...] + jnp.dot(
-            lasts[seg][...], piece_ref[...], preferred_element_type=jnp.float32
-        )
-        kvq = total.astype(jnp.bfloat16)
-        outs[2 * seg][...] = kvq
-        length = kvq.shape[0]
+        at = 2 * HEAD_SIZE
+        total = sums[seg][:, :at] + last_piece(lasts[seg], upper_ref, lower_ref, 0, at)
+        kv = total.astype(jnp.bfloat16)
+        outs[2 * seg][...] = kv
+        length = kv.shape[0]
         valid, _ = facts_of(messages[seg])
-        keys = kvq[:, :HEAD_SIZE].astype(jnp.float32)
+        keys = kv[:, :HEAD_SIZE].astype(jnp.float32)
         live = iota((length, HEAD_SIZE), 0) < valid[:, :HEAD_SIZE]
         sig = jnp.where(live, sigma_plus(keys), 0.0)
         wide = jnp.concatenate(
-            [kvq[:, HEAD_SIZE : 2 * HEAD_SIZE], jnp.ones((length, HEAD_SIZE), jnp.bfloat16)], axis=1
+            [kv[:, HEAD_SIZE:], jnp.ones((length, HEAD_SIZE), jnp.bfloat16)], axis=1
         )
         high, low = split(sig)
         over = (((0,), (0,)), ((), ()))
@@ -149,23 +152,17 @@
     outs[-1][...] = whole.astype(jnp.bfloat16)
 
 
-def attend_body(segs, early, late, first_head, group, here_ref, gate_ref, base_ref, *refs):
-    kvqs, deltas, messages = refs[:MEMBERS], refs[MEMBERS : 2 * MEMBERS], refs[2 * MEMBERS : 3 * MEMBERS]
+def attend_body(segs, heads, first_head, group, here_ref, gate_ref, base_ref, upper_ref, lower_ref, *refs):
+    kvs, deltas, messages = refs[:MEMBERS], refs[MEMBERS : 2 * MEMBERS], refs[2 * MEMBERS : 3 * MEMBERS]
     rest = refs[3 * MEMBERS :]
     n = len(segs)
-    piece, sums, lasts, outs = rest[0], rest[1 : 1 + n], rest[1 + n : 1 + 2 * n], rest[1 + 2 * n :]
+    sums, lasts, outs = rest[:n], rest[n : 2 * n], rest[2 * n :]
     me = here_ref[1]
-    heads = early + late[1] - late[0]
-    at_late = slice(late[0] * HEAD_SIZE, late[1] * HEAD_SIZE)
+    start, across = (2 + first_head) * HEAD_SIZE, heads * HEAD_SIZE
     for at, seg in enumerate(segs):
-        queries = (
-            sums[at][:, at_late]
-            + jnp.dot(lasts[at][...], piece[:, at_late], preferred_element_type=jnp.float32)
-        ).astype(jnp.bfloat16)
-        if early:
-            queries = jnp.concatenate(
-                [kvqs[seg][:, 2 * HEAD_SIZE : (2 + early) * HEAD_SIZE], queries], axis=1
-            )
+        queries = sums[at][:, start : start + across]
+        queries += last_piece(lasts[at], upper_ref, lower_ref, start, across)
+        queries = queries.astype(jnp.bfloat16)
         length = queries.shape[0]
         blocks = length // BLK
         valid, seen = facts_of(messages[seg])
@@ -183,8 +180,8 @@
                 [queries[span, h * HEAD_SIZE : (h + 1) * HEAD_SIZE] for h in range(heads)], axis=0
             )
             width = (block + 1) * BLK
-            keys = kvqs[seg][0:width, :HEAD_SIZE]
-            values = kvqs[seg][0:width, HEAD_SIZE : 2 * HEAD_SIZE]
+            keys = kvs[seg][0:width, :HEAD_SIZE]
+            values = kvs[seg][0:width, HEAD_SIZE:]
             scores = lax.dot_general(
                 stacked, keys, (((1,), (1,)), ((), ())), preferred_element_type=jnp.float32
             ) * HEAD_SIZE ** (-0.5)
@@ -240,7 +237,7 @@
     n_groups = n_seg // MEMBERS
     heads_kv = w_key.shape[1] // HEAD_SIZE
     group = w_query.shape[1] // w_key.shape[1]
-    early = 1
+    half = group // 2
     rows = w_query.shape[0]
     length, width = tokens.shape[1], tokens.shape[2]
     assert heads_kv == MEMBERS and length == 2 * BLK
@@ -265,28 +262,19 @@
     def to_member(array, k):
         return permute(array, lambda gg, mm, zz: (gg, mm ^ k, zz))
 
-    wide = [(2 + early) * HEAD_SIZE, (group - early) * HEAD_SIZE]
+    wide = (2 + group) * HEAD_SIZE
     packed = call(
-        functools.partial(pack_body, group, early),
-        [shape((rows + META_ROWS, wide[0]), bf16), shape((rows, wide[1]), bf16)] * MEMBERS,
+        functools.partial(pack_body, group),
+        [shape((rows + META_ROWS, wide), bf16)] * MEMBERS,
         [SMEM] * 3 + [HBM] * 3,
-        scratch=[pltpu.VMEM((META_ROWS, wide[0]), bf16), pltpu.SemaphoreType.DMA((5 * MEMBERS,))],
+        scratch=[pltpu.VMEM((META_ROWS, wide), bf16), pltpu.SemaphoreType.DMA((4 * MEMBERS,))],
         out_spec=ANY,
     )(here, valid_len, block_mask, w_query, w_key, value_weight)
-    order = (2, 3, 1)
-    first = {0: packed[0]}
-    second = {0: packed[1]}
-    for k in order:
-        first[k] = to_member(packed[2 * k], k)
-    for k in order:
-        second[k] = to_member(packed[2 * k + 1], k)
-    messages = [first[k] for k in range(MEMBERS)]
-
-    own = after(tokens[0], first[2], first[3], second[2], second[3])
+    messages = [packed[0], *[to_member(packed[k], k) for k in (1, 2, 3)]]
+
+    own = after(tokens[0], *messages)
     across = to_member(own, 2)
     sibling = to_member(own, 1)
-    diagonal = to_member(across, 1)
-    books = [tokens[0], sibling, across, diagonal]
 
     def lines(pieces):
         inside = (z == 1) | (z == 2)
@@ -300,21 +288,28 @@
         )
         locked = lambda *parts: lax.optimization_barrier(parts)
         states = [(pair(piece), inward(piece), over(piece)) for piece in pieces]
-        found = [[] for _ in pieces]
+        found, marks = [[] for _ in pieces], []
         for n, piece in enumerate(pieces):
             one, inner, far0 = locked(*states[n])
             found[n] = [piece, one, far0]
             states[n] = (inward(one), outward(inner), over(one), inner)
         for n in range(len(pieces)):
             middle, outer, far1, inner = locked(*states[n])
+            marks.append(far1)
             two = jnp.where(inside, inner, outer)
             states[n] = (outward(middle), over(two), middle, two, far1)
         for n in range(len(pieces)):
             last, far2, middle, two, far1 = locked(*states[n])
             three = jnp.where(inside, middle, last)
             piece, one, far0 = found[n]
-            found[n] = [piece, one, two, three, far0, far1, far2, over(three)]
-        return found
+            found[n] = [piece, one, two, three, far0, far1, far2]
+            if n == 0:
+                final = over(three)
+                found[n] += [final, final]
+            else:
+                at = 2 * HEAD_SIZE
+                found[n] += [over(jnp.where(inside, middle[:, cut], last[:, cut])) for cut in (slice(0, at), slice(at, None))]
+        return found, marks[-1]
 
     def gathered(piece):
         index = lambda gg, mm, zz: (gg * MEMBERS + mm) * n_z + zz
@@ -333,37 +328,55 @@
         return list(natural.reshape(-1, MEMBERS * HEAD_SIZE, columns))
 
     pieces = [
-        jnp.concatenate([part[k][:rows] for k in range(MEMBERS)], axis=0) for part in (first, second)
+        jnp.concatenate([messages[k][:rows] for k in members], axis=0) for members in ((0, 1), (2, 3))
     ]
+    n_pieces = width // (MEMBERS * HEAD_SIZE)
     if n_groups == 2 and n_z == 4:
         assert rows == HEAD_SIZE
-        line, chunks = n_z, lines(pieces)
+        line = n_z
+        (upper, lower), mark = lines(pieces)
+        across_late = after(across, mark)
+        parts = [(0, 1, 4, 5), (2, 3, 6)]
     else:
-        line, chunks = 0, [gathered(piece) for piece in pieces]
-    n_pieces = width // (MEMBERS * HEAD_SIZE)
-
-    sums, lasts = [[], []], []
-    for c in range(2):
+        line = 0
+        full = gathered(jnp.concatenate(pieces, axis=0))
+        cut = MEMBERS * HEAD_SIZE // 2
+        upper, lower = [part[:cut] for part in full], [part[cut:] for part in full]
+        upper.append(upper[-1])
+        lower[-1:] = [lower[-1][:, : 2 * HEAD_SIZE], lower[-1][:, 2 * HEAD_SIZE :]]
+        across_late = across
+        parts = [tuple(range(n_pieces - 1))]
+    diagonal = to_member(across_late, 1)
+    books = [tokens[0], sibling, across, diagonal]
+
+    sums, lasts = [None] * MEMBERS, [None] * MEMBERS
+    for c, places in enumerate(parts):
         for segs in ((0, 1), (2, 3)):
-            n = len(segs)
             found = call(
-                functools.partial(project_body, n, n_pieces, c == 0, line),
-                [shape((length, wide[c]), f32)] * n
-                + [shape((length, MEMBERS * HEAD_SIZE), bf16)] * (n if c == 0 else 0),
-                [SMEM] + [VMEM] * (n + n_pieces - 1),
-                flops=2 * n * length * width * wide[c],
-            )(here, *[books[s] for s in segs], *chunks[c][:-1])
-            sums[c] += found[:n]
-            lasts += found[n:]
+                functools.partial(project_body, places, line, n_pieces, c == 0),
+                [shape((length, wide), f32)] * 2
+                + [shape((length, MEMBERS * HEAD_SIZE), bf16)] * (2 if c == 0 else 0),
+                [SMEM] + [VMEM] * (2 + 2 * len(places) + (0 if c == 0 else 2)),
+                flops=2 * 2 * length * len(places) * MEMBERS * HEAD_SIZE * wide,
+            )(
+                here,
+                *[books[s] for s in segs],
+                *[part[p] for p in places for part in (upper, lower)],
+                *([] if c == 0 else [sums[s] for s in segs]),
+            )
+            for at, s in enumerate(segs):
+                sums[s] = found[at]
+                if c == 0:
+                    lasts[s] = found[2 + at]
 
     found = call(
         kv_body,
-        [shape((length, wide[0]), bf16), shape((HEAD_SIZE, 2 * HEAD_SIZE), f32)] * MEMBERS
+        [shape((length, 2 * HEAD_SIZE), bf16), shape((HEAD_SIZE, 2 * HEAD_SIZE), f32)] * MEMBERS
         + [shape((HEAD_SIZE, 2 * HEAD_SIZE), bf16)],
-        [VMEM] * (1 + 3 * MEMBERS),
-        flops=2 * MEMBERS * length * MEMBERS * HEAD_SIZE * wide[0],
-    )(chunks[0][-1], *sums[0], *lasts, *messages)
-    kvqs, deltas, total = found[0:-1:2], found[1:-1:2], found[-1]
+        [VMEM] * (2 + 3 * MEMBERS),
+        flops=2 * MEMBERS * length * MEMBERS * HEAD_SIZE * 2 * HEAD_SIZE,
+    )(upper[-2], lower[-2], *sums, *lasts, *messages)
+    kvs, deltas, total = found[0:-1:2], found[1:-1:2], found[-1]
 
     base = None
     for a in range(1, n_groups):
@@ -371,18 +384,16 @@
         base = term if base is None else base.astype(f32) + term.astype(f32)
 
     sent = {}
-    half = group // 2
-    picks = [(early, (0, half - early)), (0, (half - early, group - early))]
 
     def attend(c, segs, base):
         attended = call(
-            functools.partial(attend_body, segs, *picks[c], c * half, group),
+            functools.partial(attend_body, segs, half, c * half, group),
             [shape((length, half * HEAD_SIZE), bf16)] * len(segs),
-            [SMEM] * 2 + [VMEM] * (2 + 3 * MEMBERS + 2 * len(segs)),
+            [SMEM] * 2 + [VMEM] * (3 + 3 * MEMBERS + 2 * len(segs)),
             flops=2 * len(segs) * length * length * HEAD_SIZE * half * 3,
         )(
-            here, gate_bias, base, *kvqs, *deltas, *messages, chunks[1][-1],
-            *[sums[1][s] for s in segs], *[lasts[s] for s in segs],
+            here, gate_bias, base, upper[-1], lower[-1], *kvs, *deltas, *messages,
+            *[sums[s] for s in segs], *[lasts[s] for s in segs],
         )
         for seg_at, part in zip(segs, attended):
             sent[c, seg_at] = to_member(part, seg_at) if seg_at else part

time: 163 us -> 146 us (0.90)
  waiting for transfers between devices: 64.8 us -> 49.8 us
  starting transfers between devices: 55.2 us -> 52.9 us
    ppermute x34 -> x32, waiting for transfers between devices: 64.8 us -> 49.8 us  [permute(): return lax.ppermute(array, AXES, pairs)]
    ppermute x34 -> x32, starting transfers between devices: 55.2 us -> 52.9 us  [permute(): return lax.ppermute(array, AXES, pairs)]
    unnamed x25 -> x40, local copies, waits for them, and re-layouts: 5.16 us -> 6.63 us
  transfers between devices with their start and end apart: 34 -> 32, of which waited for: 18 -> 15; matrix products, arithmetic and copies ran while one was open for 3% -> 2% of each run, Pallas kernels for 11% -> 15%
where the time goes in v4:
time: 146 us; the launch traced here: 143 us
  starting transfers between devices  52.9 us (36%)
  waiting for transfers between devices  49.8 us (34%)
  Pallas kernels  29.1 us (20%)
  local copies, waits for them, and re-layouts  6.68 us (5%)
  other arithmetic  3.42 us (2%)
    ppermute x32, starting transfers between devices, permute(): return lax.ppermute(array, AXES, pairs)  52.9 us
    ppermute x32, waiting for transfers between devices, permute(): return lax.ppermute(array, AXES, pairs)  49.8 us
    pallas_call x4, Pallas kernels, shards(): call(functools.partial(project_body, places, line, n_pieces, c == 0), [sh...  14.7 us
    pallas_call x4, Pallas kernels, attend(): call(functools.partial(attend_body, segs, half, c * half, group), [shape(...  10.1 us
    unnamed x40, local copies, waits for them, and re-layouts  6.63 us
  transfers between devices with their start and end apart: 32, of which 15 were waited for; matrix products, arithmetic and copies ran while one was open for 2% of the time, Pallas kernels for 15%

profile of v4, /device:TPU:9, one launch (start us, length us, event | category | flops | bytes accessed | tf_op | source)
XLA Modules:
  0.0 143.2 jit_solution(12968209523985660558)
XLA Ops:
  0.9 1.0 copy-done.11
  1.9 0.9 copy-done.12
  2.8 0.9 copy-done.13
  3.7 0.7 copy-done.15
  4.4 1.0 shard_map.73
  5.4 0.7 collective-permute-start
  6.2 1.2 collective-permute-start.10
  7.4 0.5 collective-permute-start.11
  7.9 5.3 %collective-permute-done.10.refs_10_ = bf16[144,768]{1,0:T(8,128)(2,1)S(1)} collective-permute-done((bf16[144,768]{1,0:T(8,128)(2,1)S(1)}, bf16[144,768]{1,0:T(8,128)(2,1)S(1)}, u32[]{:S(2)}, u32[]{:S(2)}) %collective-permute-start.10) | collective-permute-done | bytes 221216 | tf_op jit(solution)/shard_map/ppermute | solution.py:260
  13.2 4.9 %collective-permute-done.11.refs_11_ = bf16[144,768]{1,0:T(8,128)(2,1)S(1)} collective-permute-done((bf16[144,768]{1,0:T(8,128)(2,1)S(1)}, bf16[144,768]{1,0:T(8,128)(2,1)S(1)}, u32[]{:S(2)}, u32[]{:S(2)}) %collective-permute-start.11) | collective-permute-done | bytes 221216 | tf_op jit(solution)/shard_map/ppermute | solution.py:260
  18.1 1.2 collective-permute-start.22
  19.4 1.3 collective-permute-start.14
  20.7 3.2 %collective-permute-start.13 = (bf16[256,768]{1,0:T(8,128)(2,1)S(1)}, bf16[256,768]{1,0:T(8,128)(2,1)S(1)}, u32[]{:S(2)}, u32[]{:S(2)}) collective-permute-start(bf16[256,768]{1,0:T(8,128)(2,1)S(1)} %pad_maximum_fusion.1.refs_3_), channel_id=1, source_target_pairs={{1,2},{2,1},{5,6},{6,5},{9,10},{10,9},{13,14},{14,13},{17,18},{18,... | collective-permute-start | bytes 1179656 | tf_op jit(solution)/shard_map/ppermute | solution.py:260
  24.0 5.8 %collective-permute-done.14.refs_7_ = bf16[256,768]{1,0:T(8,128)(2,1)S(1)} collective-permute-done((bf16[256,768]{1,0:T(8,128)(2,1)S(1)}, bf16[256,768]{1,0:T(8,128)(2,1)S(1)}, u32[]{:S(2)}, u32[]{:S(2)}) %collective-permute-start.14) | collective-permute-done | bytes 393248 | tf_op jit(solution)/shard_map/ppermute | solution.py:260
  29.7 0.8 copy-done.3
  30.5 2.0 %collective-permute-done.13 = bf16[256,768]{1,0:T(8,128)(2,1)S(1)} collective-permute-done((bf16[256,768]{1,0:T(8,128)(2,1)S(1)}, bf16[256,768]{1,0:T(8,128)(2,1)S(1)}, u32[]{:S(2)}, u32[]{:S(2)}) %collective-permute-start.13) | collective-permute-done | bytes 393248 | tf_op jit(solution)/shard_map/ppermute | solution.py:260
  32.5 1.1 collective-permute-done.12.refs_5_
  33.6 2.2 %collective-permute-start.16 = (bf16[256,768]{1,0:T(8,128)(2,1)S(1)}, bf16[256,768]{1,0:T(8,128)(2,1)S(1)}, u32[]{:S(2)}, u32[]{:S(2)}) collective-permute-start(bf16[256,768]{1,0:T(8,128)(2,1)S(1)} %collective-permute-done.13), channel_id=1, source_target_pairs={{1,0},{2,3},{5,4},{6,7},{9,8},{10,11},{13,12},{14,15},{17,16},{18,... | collective-permute-start | bytes 1179656 | tf_op jit(solution)/shard_map/ppermute | solution.py:260
  35.8 0.3 collective-permute-start.17
  36.1 2.1 %collective-permute-start.15 = (bf16[256,768]{1,0:T(8,128)(2,1)S(1)}, bf16[256,768]{1,0:T(8,128)(2,1)S(1)}, u32[]{:S(2)}, u32[]{:S(2)}) collective-permute-start(bf16[256,768]{1,0:T(8,128)(2,1)S(1)} %collective-permute-done.12.refs_5_), channel_id=1, source_target_pairs={{1,2},{2,1},{5,6},{6,5},{9,10},{10,9},{13,14},{14,13},{17,18},{18,... | collective-permute-start | bytes 1179656 | tf_op jit(solution)/shard_map/ppermute | solution.py:260
  38.3 1.3 collective-permute-start.3
  39.6 3.0 %collective-permute-done.16 = bf16[256,768]{1,0:T(8,128)(2,1)S(1)} collective-permute-done((bf16[256,768]{1,0:T(8,128)(2,1)S(1)}, bf16[256,768]{1,0:T(8,128)(2,1)S(1)}, u32[]{:S(2)}, u32[]{:S(2)}) %collective-permute-start.16) | collective-permute-done | bytes 393248 | tf_op jit(solution)/shard_map/ppermute | solution.py:260
  42.6 2.1 %collective-permute-start.2 = (bf16[256,768]{1,0:T(8,128)(2,1)S(1)}, bf16[256,768]{1,0:T(8,128)(2,1)}, u32[]{:S(2)}, u32[]{:S(2)}) collective-permute-start(bf16[256,768]{1,0:T(8,128)(2,1)S(1)} %pad_maximum_fusion.refs_2_), channel_id=1, source_target_pairs={{1,2},{2,1},{5,6},{6,5},{9,10},{10,9},{13,14},{14,13},{17,18},{18,... | collective-permute-start | bytes 1179656 | tf_op jit(solution)/shard_map/ppermute | solution.py:260
  44.7 0.8 copy-done.7
  45.5 1.6 %collective-permute-start.1 = (bf16[256,768]{1,0:T(8,128)(2,1)S(1)}, bf16[256,768]{1,0:T(8,128)(2,1)}, u32[]{:S(2)}, u32[]{:S(2)}) collective-permute-start(bf16[256,768]{1,0:T(8,128)(2,1)S(1)} %pad_maximum_fusion.refs_2_), channel_id=1, source_target_pairs={{0,1},{1,0},{2,3},{3,2},{4,5},{5,4},{6,7},{7,6},{8,9},{9,8},{10,11... | collective-permute-start | bytes 1179656 | tf_op jit(solution)/shard_map/ppermute | solution.py:260
  47.1 0.7 copy-done.1
  47.9 3.5 %collective-permute-start.21 = (bf16[256,4096]{1,0:T(8,128)(2,1)S(1)}, bf16[256,4096]{1,0:T(8,128)(2,1)}, u32[]{:S(2)}, u32[]{:S(2)}) collective-permute-start(bf16[256,4096]{1,0:T(8,128)(2,1)S(1)} %bitcast.6), channel_id=1, source_target_pairs={{0,4},{1,5},{2,6},{3,7},{4,0},{5,1},{6,2},{7,3},{8,12},{9,13},{10,... | collective-permute-start | bytes 6291464 | tf_op jit(solution)/shard_map/ppermute | solution.py:260
  51.4 14.0 %collective-permute-done.22.refs_0_ = bf16[256,4096]{1,0:T(8,128)(2,1)} collective-permute-done((bf16[256,4096]{1,0:T(8,128)(2,1)}, bf16[256,4096]{1,0:T(8,128)(2,1)}, u32[]{:S(2)}, u32[]{:S(2)}) %collective-permute-start.22) | collective-permute-done | bytes 2097184 | tf_op jit(solution)/shard_map/ppermute | solution.py:260
  65.4 1.0 collective-permute-start.23
  66.4 0.7 copy-done.9
  67.2 2.6 %collective-permute-start.5 = (bf16[256,768]{1,0:T(8,128)(2,1)}, bf16[256,768]{1,0:T(8,128)(2,1)}, u32[]{:S(2)}, u32[]{:S(2)}) collective-permute-start(bf16[256,768]{1,0:T(8,128)(2,1)} %collective-permute-done.2), channel_id=1, source_target_pairs={{1,0},{2,3},{5,4},{6,7},{9,8},{10,11},{13,12},{14,15},{17,16},{18,... | collective-permute-start | bytes 1179656 | tf_op jit(solution)/shard_map/ppermute | solution.py:260
  69.8 1.5 %collective-permute-start.6 = (bf16[256,768]{1,0:T(8,128)(2,1)}, bf16[256,768]{1,0:T(8,128)(2,1)}, u32[]{:S(2)}, u32[]{:S(2)}) collective-permute-start(bf16[256,768]{1,0:T(8,128)(2,1)} %collective-permute-done.1.refs_4_), channel_id=1, source_target_pairs={{0,16},{1,17},{2,18},{3,19},{4,20},{5,21},{6,22},{7,23},{8,24},{9,... | collective-permute-start | bytes 1179656 | tf_op jit(solution)/shard_map/ppermute | solution.py:260
  71.3 4.3 %collective-permute-start.4 = (bf16[256,768]{1,0:T(8,128)(2,1)}, bf16[256,768]{1,0:T(8,128)(2,1)}, u32[]{:S(2)}, u32[]{:S(2)}) collective-permute-start(bf16[256,768]{1,0:T(8,128)(2,1)} %collective-permute-done.1.refs_4_), channel_id=1, source_target_pairs={{1,2},{2,1},{5,6},{6,5},{9,10},{10,9},{13,14},{14,13},{17,18},{18,... | collective-permute-start | bytes 1179656 | tf_op jit(solution)/shard_map/ppermute | solution.py:260
  75.6 1.1 broadcast_select_fusion.1.refs_3_
  76.8 1.1 collective-permute-done.5
  77.9 1.5 %collective-permute-start.19 = (bf16[256,768]{1,0:T(8,128)(2,1)S(1)}, bf16[256,768]{1,0:T(8,128)(2,1)S(1)}, u32[]{:S(2)}, u32[]{:S(2)}) collective-permute-start(bf16[256,768]{1,0:T(8,128)(2,1)S(1)} %broadcast_select_fusion.1.refs_3_), channel_id=1, source_target_pairs={{0,16},{1,17},{2,18},{3,19},{4,20},{5,21},{6,22},{7,23},{8,24},{9,... | collective-permute-start | bytes 1179656 | tf_op jit(solution)/shard_map/ppermute | solution.py:260
  79.4 1.2 collective-permute-done.6.refs_8_
  80.6 2.9 %collective-permute-start.18 = (bf16[256,768]{1,0:T(8,128)(2,1)}, bf16[256,768]{1,0:T(8,128)(2,1)S(1)}, u32[]{:S(2)}, u32[]{:S(2)}) collective-permute-start(bf16[256,768]{1,0:T(8,128)(2,1)} %copy-done.16), channel_id=1, source_target_pairs={{1,0},{2,3},{5,4},{6,7},{9,8},{10,11},{13,12},{14,15},{17,16},{18,... | collective-permute-start | bytes 1179656 | tf_op jit(solution)/shard_map/ppermute | solution.py:260
  83.5 1.4 collective-permute-done.4
  84.9 1.0 broadcast_select_fusion.3.refs_2_
  86.2 2.7 %collective-permute-done.19.refs_7_ = bf16[256,768]{1,0:T(8,128)(2,1)S(1)} collective-permute-done((bf16[256,768]{1,0:T(8,128)(2,1)S(1)}, bf16[256,768]{1,0:T(8,128)(2,1)S(1)}, u32[]{:S(2)}, u32[]{:S(2)}) %collective-permute-start.19) | collective-permute-done | bytes 393248 | tf_op jit(solution)/shard_map/ppermute | solution.py:260
  88.9 3.0 %collective-permute-start.7 = (bf16[256,768]{1,0:T(8,128)(2,1)}, bf16[256,768]{1,0:T(8,128)(2,1)S(1)}, u32[]{:S(2)}, u32[]{:S(2)}) collective-permute-start(bf16[256,768]{1,0:T(8,128)(2,1)} %collective-permute-done.4), channel_id=1, source_target_pairs={{1,0},{2,3},{5,4},{6,7},{9,8},{10,11},{13,12},{14,15},{17,16},{18,... | collective-permute-start | bytes 1179656 | tf_op jit(solution)/shard_map/ppermute | solution.py:260
  91.9 1.5 %collective-permute-start.20 = (bf16[256,256]{1,0:T(8,128)(2,1)S(1)}, bf16[256,256]{1,0:T(8,128)(2,1)S(1)}, u32[]{:S(2)}, u32[]{:S(2)}) collective-permute-start(bf16[256,256]{1,0:T(8,128)(2,1)S(1)} %slice_select_fusion.1), channel_id=1, source_target_pairs={{0,16},{1,17},{2,18},{3,19},{4,20},{5,21},{6,22},{7,23},{8,24},{9,... | collective-permute-start | bytes 393224 | tf_op jit(solution)/shard_map/ppermute | solution.py:260
  93.5 3.8 %collective-permute-done.8.refs_6_ = bf16[256,768]{1,0:T(8,128)(2,1)S(1)} collective-permute-done((bf16[256,768]{1,0:T(8,128)(2,1)S(1)}, bf16[256,768]{1,0:T(8,128)(2,1)S(1)}, u32[]{:S(2)}, u32[]{:S(2)}) %collective-permute-start.8) | collective-permute-done | bytes 393248 | tf_op jit(solution)/shard_map/ppermute | solution.py:260
  97.3 1.5 %collective-permute-start.25 = (bf16[256,512]{1,0:T(8,128)(2,1)S(1)}, bf16[256,512]{1,0:T(8,128)(2,1)S(1)}, u32[]{:S(2)}, u32[]{:S(2)}) collective-permute-start(bf16[256,512]{1,0:T(8,128)(2,1)S(1)} %slice_select_fusion), channel_id=1, source_target_pairs={{0,16},{1,17},{2,18},{3,19},{4,20},{5,21},{6,22},{7,23},{8,24},{9,... | collective-permute-start | bytes 786440 | tf_op jit(solution)/shard_map/ppermute | solution.py:260
  98.8 1.1 broadcast_select_fusion.2.refs_4_
  99.8 0.4 collective-permute-start.9
  100.3 3.7 %shard_map.74 = (f32[256,768]{1,0:T(8,128)S(1)}, f32[256,768]{1,0:T(8,128)S(1)}, bf16[256,512]{1,0:T(8,128)(2,1)S(1)}, bf16[256,512]{1,0:T(8,128)(2,1)S(1)}) custom-call(s32[3]{0:T(128)S(1)} %pad_add_fusion.here_ref, bf16[256,4096]{1,0:T(8,128)(2,1)S(1)} %bitcast.7, bf16[256,4096]{1,0:T(8,128)(2,1)} %collective-permute-done.21.refs_1_, ...), custom_call_target="tpu_custom_call" | custom-call | flops 1610612736 | bytes 4194304 | tf_op jit(solution)/shard_map/pallas_call | solution.py:355
  104.0 3.0 %shard_map.75 = (f32[256,768]{1,0:T(8,128)S(1)}, f32[256,768]{1,0:T(8,128)S(1)}) custom-call(s32[3]{0:T(128)S(1)} %pad_add_fusion.here_ref, bf16[256,4096]{1,0:T(8,128)(2,1)S(1)} %bitcast.8, bf16[256,4096]{1,0:T(8,128)(2,1)} %collective-permute-done.21.refs_1_, bf16[256,768]{1,0:T(8,128)(2,1)S(1)} %broadcast_select_fusion.3.refs_2_, ...), custom_call_target="tpu_custom_call" | custom-call | flops 1207959552 | bytes 4194304 | tf_op jit(solution)/shard_map/pallas_call | solution.py:355
  107.1 4.3 %shard_map.76 = (f32[256,768]{1,0:T(8,128)S(1)}, f32[256,768]{1,0:T(8,128)S(1)}, bf16[256,512]{1,0:T(8,128)(2,1)S(1)}, bf16[256,512]{1,0:T(8,128)(2,1)S(1)}) custom-call(s32[3]{0:T(128)S(1)} %pad_add_fusion.here_ref, bf16[256,4096]{1,0:T(8,128)(2,1)} %collective-permute-done.22.refs_0_, bf16[256,4096]{1,0:T(8,128)(2,1)} %collective-permute-done.23.refs_1_, ...), custom_call_target="tpu_custom_call" | custom-call | flops 1610612736 | bytes 4194304 | tf_op jit(solution)/shard_map/pallas_call | solution.py:355
  111.4 3.7 %shard_map.77 = (f32[256,768]{1,0:T(8,128)S(1)}, f32[256,768]{1,0:T(8,128)S(1)}) custom-call(s32[3]{0:T(128)S(1)} %pad_add_fusion.here_ref, bf16[256,4096]{1,0:T(8,128)(2,1)} %collective-permute-done.22.refs_0_, bf16[256,4096]{1,0:T(8,128)(2,1)} %collective-permute-done.23.refs_1_, bf16[256,768]{1,0:T(8,128)(2,1)S(1)} %broadcast_select_fusion.3.refs_2_, ...), custom_call_target="tpu_custom_call" | custom-call | flops 1207959552 | bytes 4194304 | tf_op jit(solution)/shard_map/pallas_call | solution.py:355
  115.1 1.7 %shard_map.78 = (bf16[256,256]{1,0:T(8,128)(2,1)S(1)}, f32[128,256]{1,0:T(8,128)S(1)}, bf16[256,256]{1,0:T(8,128)(2,1)S(1)}, f32[128,256]{1,0:T(8,128)S(1)}, bf1...) custom-call(bf16[256,768]{1,0:T(8,128)(2,1)S(1)} %collective-permute, ...), custom_call_target="tpu_custom_call" | custom-call | flops 268435456 | bytes 4194304 | tf_op jit(solution)/shard_map/pallas_call | solution.py:372
  116.8 3.3 %collective-permute-start.24 = (bf16[128,256]{1,0:T(8,128)(2,1)S(1)}, bf16[128,256]{1,0:T(8,128)(2,1)S(1)}, u32[]{:S(2)}, u32[]{:S(2)}) collective-permute-start(bf16[128,256]{1,0:T(8,128)(2,1)S(1)} %get-tuple-element.109), channel_id=1, source_target_pairs={{0,16},{1,17},{2,18},{3,19},{4,20},{5,21},{6,22},{7,23},{8,24},{9,... | collective-permute-start | bytes 196616 | tf_op jit(solution)/shard_map/ppermute | solution.py:260
  120.1 1.1 collective-permute-done.24.base_ref
  121.2 2.5 %shard_map.79 = (bf16[256,256]{1,0:T(8,128)(2,1)S(1)}, bf16[256,256]{1,0:T(8,128)(2,1)S(1)}) custom-call(s32[3]{0:T(128)S(1)} %pad_add_fusion.here_ref, f32[16]{0:T(128)S(1)} %copy-done.14, bf16[128,256]{1,0:T(8,128)(2,1)S(1)} %collective-permute-done.24.base_ref, bf16[256,768]{1,0:T(8,128)(2,1)S(1)} %collective-permute-done.9.upper_ref, ...), custom_call_target="tpu_custom_call" | custom-call | flops 201326592 | bytes 4194304 | tf_op jit(solution)/shard_map/pallas_call | solution.py:389
  123.7 2.5 %shard_map.80 = (bf16[256,256]{1,0:T(8,128)(2,1)S(1)}, bf16[256,256]{1,0:T(8,128)(2,1)S(1)}) custom-call(s32[3]{0:T(128)S(1)} %pad_add_fusion.here_ref, f32[16]{0:T(128)S(1)} %copy-done.14, bf16[128,256]{1,0:T(8,128)(2,1)S(1)} %collective-permute-done.24.base_ref, bf16[256,768]{1,0:T(8,128)(2,1)S(1)} %collective-permute-done.9.upper_ref, ...), custom_call_target="tpu_custom_call" | custom-call | flops 201326592 | bytes 4194304 | tf_op jit(solution)/shard_map/pallas_call | solution.py:389
  126.3 1.2 collective-permute-start.29
  127.5 0.3 collective-permute-start.28
  127.8 5.7 %collective-permute-start.30 = (bf16[256,256]{1,0:T(8,128)(2,1)S(1)}, bf16[256,256]{1,0:T(8,128)(2,1)S(1)}, u32[]{:S(2)}, u32[]{:S(2)}) collective-permute-start(bf16[256,256]{1,0:T(8,128)(2,1)S(1)} %get-tuple-element.119), channel_id=1, source_target_pairs={{0,12},{1,13},{2,14},{3,15},{4,8},{5,9},{6,10},{7,11},{8,4},{9,5},... | collective-permute-start | bytes 393224 | tf_op jit(solution)/shard_map/ppermute | solution.py:260
  133.5 2.5 %shard_map.81 = (bf16[256,256]{1,0:T(8,128)(2,1)S(1)}, bf16[256,256]{1,0:T(8,128)(2,1)S(1)}) custom-call(s32[3]{0:T(128)S(1)} %pad_add_fusion.here_ref, f32[16]{0:T(128)S(1)} %copy-done.14, bf16[128,256]{1,0:T(8,128)(2,1)S(1)} %collective-permute-done.24.base_ref, bf16[256,768]{1,0:T(8,128)(2,1)S(1)} %collective-permute-done.9.upper_ref, ...), custom_call_target="tpu_custom_call" | custom-call | flops 201326592 | bytes 4194304 | tf_op jit(solution)/shard_map/pallas_call | solution.py:389
  136.0 2.5 %shard_map.82 = (bf16[256,256]{1,0:T(8,128)(2,1)S(1)}, bf16[256,256]{1,0:T(8,128)(2,1)S(1)}) custom-call(s32[3]{0:T(128)S(1)} %pad_add_fusion.here_ref, f32[16]{0:T(128)S(1)} %copy-done.14, bf16[128,256]{1,0:T(8,128)(2,1)S(1)} %collective-permute-done.24.base_ref, bf16[256,768]{1,0:T(8,128)(2,1)S(1)} %collective-permute-done.9.upper_ref, ...), custom_call_target="tpu_custom_call" | custom-call | flops 201326592 | bytes 4194304 | tf_op jit(solution)/shard_map/pallas_call | solution.py:389
  138.6 0.5 collective-permute-start.27
  139.2 2.3 %collective-permute-done.31.refs_7_ = bf16[256,256]{1,0:T(8,128)(2,1)S(1)} collective-permute-done((bf16[256,256]{1,0:T(8,128)(2,1)S(1)}, bf16[256,256]{1,0:T(8,128)(2,1)S(1)}, u32[]{:S(2)}, u32[]{:S(2)}) %collective-permute-start.31) | collective-permute-done | bytes 131104 | tf_op jit(solution)/shard_map/ppermute | solution.py:260
  141.5 1.6 %shard_map.83 = bf16[256,2048]{1,0:T(8,128)(2,1)} custom-call(s32[3]{0:T(128)S(1)} %pad_add_fusion.here_ref, bf16[256,256]{1,0:T(8,128)(2,1)S(1)} %get-tuple-element.124.refs_0_, bf16[256,256]{1,0:T(8,128)(2,1)S(1)} %get-tuple-element.127.refs_1_, bf16[256,256]{1,0:T(8,128)(2,1)S(1)} %collective-permute-done.26.refs_2_, ...), custom_call_target="tpu_custom_call" | custom-call | bytes 4194304 | tf_op jit(solution)/shard_map/pallas_call | solution.py:406
  (64 shorter events, 0.9 us)
Async XLA Ops:
  0.0 47.9 %copy-start = (bf16[1,256,4096]{2,1,0:T(8,128)(2,1)S(1)}, bf16[1,256,4096]{2,1,0:T(8,128)(2,1)}, u32[]{:S(2)}) copy-start(bf16[1,256,4096]{2,1,0:T(8,128)(2,1)} %param.7) | copy-start | bytes 6291460
  0.9 1.0 copy-start.11
  1.9 0.9 copy-start.12
  2.8 0.9 copy-start.13
  3.7 0.7 copy-start.15
  5.4 2.5 %collective-permute-start = (bf16[144,768]{1,0:T(8,128)(2,1)S(1)}, bf16[144,768]{1,0:T(8,128)(2,1)S(1)}, u32[]{:S(2)}, u32[]{:S(2)}) collective-permute-start(bf16[144,768]{1,0:T(8,128)(2,1)S(1)} %get-tuple-element.68), channel_id=1, source_target_pairs={{0,4},{1,5},{2,6},{3,7},{4,0},{5,1},{6,2},{7,3},{8,12},{9,13},{10,... | collective-permute-start | bytes 663560 | tf_op jit(solution)/shard_map/ppermute | solution.py:260
  6.2 7.0 %collective-permute-start.10 = (bf16[144,768]{1,0:T(8,128)(2,1)S(1)}, bf16[144,768]{1,0:T(8,128)(2,1)S(1)}, u32[]{:S(2)}, u32[]{:S(2)}) collective-permute-start(bf16[144,768]{1,0:T(8,128)(2,1)S(1)} %get-tuple-element.77), channel_id=1, source_target_pairs={{0,8},{1,9},{2,10},{3,11},{4,12},{5,13},{6,14},{7,15},{8,0},{9,1},... | collective-permute-start | bytes 663560 | tf_op jit(solution)/shard_map/ppermute | solution.py:260
  7.4 10.7 %collective-permute-start.11 = (bf16[144,768]{1,0:T(8,128)(2,1)S(1)}, bf16[144,768]{1,0:T(8,128)(2,1)S(1)}, u32[]{:S(2)}, u32[]{:S(2)}) collective-permute-start(bf16[144,768]{1,0:T(8,128)(2,1)S(1)} %get-tuple-element.78), channel_id=1, source_target_pairs={{0,12},{1,13},{2,14},{3,15},{4,8},{5,9},{6,10},{7,11},{8,4},{9,5},... | collective-permute-start | bytes 663560 | tf_op jit(solution)/shard_map/ppermute | solution.py:260
  18.1 47.3 %collective-permute-start.22 = (bf16[256,4096]{1,0:T(8,128)(2,1)}, bf16[256,4096]{1,0:T(8,128)(2,1)}, u32[]{:S(2)}, u32[]{:S(2)}) collective-permute-start(bf16[256,4096]{1,0:T(8,128)(2,1)} %bitcast.5), channel_id=1, source_target_pairs={{0,8},{1,9},{2,10},{3,11},{4,12},{5,13},{6,14},{7,15},{8,0},{9,1},... | collective-permute-start | bytes 6291464 | tf_op jit(solution)/shard_map/ppermute | solution.py:260
  19.4 10.3 %collective-permute-start.14 = (bf16[256,768]{1,0:T(8,128)(2,1)S(1)}, bf16[256,768]{1,0:T(8,128)(2,1)S(1)}, u32[]{:S(2)}, u32[]{:S(2)}) collective-permute-start(bf16[256,768]{1,0:T(8,128)(2,1)S(1)} %pad_maximum_fusion.1.refs_3_), channel_id=1, source_target_pairs={{0,16},{1,17},{2,18},{3,19},{4,20},{5,21},{6,22},{7,23},{8,24},{9,... | collective-permute-start | bytes 1179656 | tf_op jit(solution)/shard_map/ppermute | solution.py:260
  20.7 11.8 %collective-permute-start.13 = (bf16[256,768]{1,0:T(8,128)(2,1)S(1)}, bf16[256,768]{1,0:T(8,128)(2,1)S(1)}, u32[]{:S(2)}, u32[]{:S(2)}) collective-permute-start(bf16[256,768]{1,0:T(8,128)(2,1)S(1)} %pad_maximum_fusion.1.refs_3_), channel_id=1, source_target_pairs={{1,2},{2,1},{5,6},{6,5},{9,10},{10,9},{13,14},{14,13},{17,18},{18,... | collective-permute-start | bytes 1179656 | tf_op jit(solution)/shard_map/ppermute | solution.py:260
  23.9 9.7 %collective-permute-start.12 = (bf16[256,768]{1,0:T(8,128)(2,1)S(1)}, bf16[256,768]{1,0:T(8,128)(2,1)S(1)}, u32[]{:S(2)}, u32[]{:S(2)}) collective-permute-start(bf16[256,768]{1,0:T(8,128)(2,1)S(1)} %pad_maximum_fusion.1.refs_3_), channel_id=1, source_target_pairs={{0,1},{1,0},{2,3},{3,2},{4,5},{5,4},{6,7},{7,6},{8,9},{9,8},{10,11... | collective-permute-start | bytes 1179656 | tf_op jit(solution)/shard_map/ppermute | solution.py:260
  29.7 0.8 copy-start.3
  32.5 37.3 %copy-start.18 = (bf16[256,768]{1,0:T(8,128)(2,1)}, bf16[256,768]{1,0:T(8,128)(2,1)S(1)}, u32[]{:S(2)}) copy-start(bf16[256,768]{1,0:T(8,128)(2,1)S(1)} %collective-permute-done.13) | copy-start | bytes 1179652
  33.6 33.6 %copy-start.5 = (bf16[256,768]{1,0:T(8,128)(2,1)}, bf16[256,768]{1,0:T(8,128)(2,1)S(1)}, u32[]{:S(2)}) copy-start(bf16[256,768]{1,0:T(8,128)(2,1)S(1)} %collective-permute-done.12.refs_5_) | copy-start | bytes 1179652
  33.6 9.0 %collective-permute-start.16 = (bf16[256,768]{1,0:T(8,128)(2,1)S(1)}, bf16[256,768]{1,0:T(8,128)(2,1)S(1)}, u32[]{:S(2)}, u32[]{:S(2)}) collective-permute-start(bf16[256,768]{1,0:T(8,128)(2,1)S(1)} %collective-permute-done.13), channel_id=1, source_target_pairs={{1,0},{2,3},{5,4},{6,7},{9,8},{10,11},{13,12},{14,15},{17,16},{18,... | collective-permute-start | bytes 1179656 | tf_op jit(solution)/shard_map/ppermute | solution.py:260
  35.8 8.9 %collective-permute-start.17 = (bf16[256,768]{1,0:T(8,128)(2,1)S(1)}, bf16[256,768]{1,0:T(8,128)(2,1)S(1)}, u32[]{:S(2)}, u32[]{:S(2)}) collective-permute-start(bf16[256,768]{1,0:T(8,128)(2,1)S(1)} %collective-permute-done.12.refs_5_), channel_id=1, source_target_pairs={{0,16},{1,17},{2,18},{3,19},{4,20},{5,21},{6,22},{7,23},{8,24},{9,... | collective-permute-start | bytes 1179656 | tf_op jit(solution)/shard_map/ppermute | solution.py:260
  36.1 11.8 %collective-permute-start.15 = (bf16[256,768]{1,0:T(8,128)(2,1)S(1)}, bf16[256,768]{1,0:T(8,128)(2,1)S(1)}, u32[]{:S(2)}, u32[]{:S(2)}) collective-permute-start(bf16[256,768]{1,0:T(8,128)(2,1)S(1)} %collective-permute-done.12.refs_5_), channel_id=1, source_target_pairs={{1,2},{2,1},{5,6},{6,5},{9,10},{10,9},{13,14},{14,13},{17,18},{18,... | collective-permute-start | bytes 1179656 | tf_op jit(solution)/shard_map/ppermute | solution.py:260
  38.3 28.1 %collective-permute-start.3 = (bf16[256,768]{1,0:T(8,128)(2,1)S(1)}, bf16[256,768]{1,0:T(8,128)(2,1)S(1)}, u32[]{:S(2)}, u32[]{:S(2)}) collective-permute-start(bf16[256,768]{1,0:T(8,128)(2,1)S(1)} %pad_maximum_fusion.refs_2_), channel_id=1, source_target_pairs={{0,16},{1,17},{2,18},{3,19},{4,20},{5,21},{6,22},{7,23},{8,24},{9,... | collective-permute-start | bytes 1179656 | tf_op jit(solution)/shard_map/ppermute | solution.py:260
  42.6 27.2 %copy-start.19 = (bf16[256,768]{1,0:T(8,128)(2,1)}, bf16[256,768]{1,0:T(8,128)(2,1)S(1)}, u32[]{:S(2)}) copy-start(bf16[256,768]{1,0:T(8,128)(2,1)S(1)} %collective-permute-done.16) | copy-start | bytes 1179652
  42.6 24.6 %collective-permute-start.2 = (bf16[256,768]{1,0:T(8,128)(2,1)S(1)}, bf16[256,768]{1,0:T(8,128)(2,1)}, u32[]{:S(2)}, u32[]{:S(2)}) collective-permute-start(bf16[256,768]{1,0:T(8,128)(2,1)S(1)} %pad_maximum_fusion.refs_2_), channel_id=1, source_target_pairs={{1,2},{2,1},{5,6},{6,5},{9,10},{10,9},{13,14},{14,13},{17,18},{18,... | collective-permute-start | bytes 1179656 | tf_op jit(solution)/shard_map/ppermute | solution.py:260
  44.7 0.8 copy-start.7
  45.5 21.7 %collective-permute-start.1 = (bf16[256,768]{1,0:T(8,128)(2,1)S(1)}, bf16[256,768]{1,0:T(8,128)(2,1)}, u32[]{:S(2)}, u32[]{:S(2)}) collective-permute-start(bf16[256,768]{1,0:T(8,128)(2,1)S(1)} %pad_maximum_fusion.refs_2_), channel_id=1, source_target_pairs={{0,1},{1,0},{2,3},{3,2},{4,5},{5,4},{6,7},{7,6},{8,9},{9,8},{10,11... | collective-permute-start | bytes 1179656 | tf_op jit(solution)/shard_map/ppermute | solution.py:260
  47.1 0.7 copy-start.1
  47.9 21.9 %copy-start.16 = (bf16[256,768]{1,0:T(8,128)(2,1)}, bf16[256,768]{1,0:T(8,128)(2,1)S(1)}, u32[]{:S(2)}) copy-start(bf16[256,768]{1,0:T(8,128)(2,1)S(1)} %collective-permute-done.15) | copy-start | bytes 1179652
  47.9 52.4 %collective-permute-start.21 = (bf16[256,4096]{1,0:T(8,128)(2,1)S(1)}, bf16[256,4096]{1,0:T(8,128)(2,1)}, u32[]{:S(2)}, u32[]{:S(2)}) collective-permute-start(bf16[256,4096]{1,0:T(8,128)(2,1)S(1)} %bitcast.6), channel_id=1, source_target_pairs={{0,4},{1,5},{2,6},{3,7},{4,0},{5,1},{6,2},{7,3},{8,12},{9,13},{10,... | collective-permute-start | bytes 6291464 | tf_op jit(solution)/shard_map/ppermute | solution.py:260
  65.4 41.7 %collective-permute-start.23 = (bf16[256,4096]{1,0:T(8,128)(2,1)}, bf16[256,4096]{1,0:T(8,128)(2,1)}, u32[]{:S(2)}, u32[]{:S(2)}) collective-permute-start(bf16[256,4096]{1,0:T(8,128)(2,1)} %collective-permute-done.22.refs_0_), channel_id=1, source_target_pairs={{0,4},{1,5},{2,6},{3,7},{4,0},{5,1},{6,2},{7,3},{8,12},{9,13},{10,... | collective-permute-start | bytes 6291464 | tf_op jit(solution)/shard_map/ppermute | solution.py:260
  66.4 0.7 copy-start.9
  67.2 10.7 %collective-permute-start.5 = (bf16[256,768]{1,0:T(8,128)(2,1)}, bf16[256,768]{1,0:T(8,128)(2,1)}, u32[]{:S(2)}, u32[]{:S(2)}) collective-permute-start(bf16[256,768]{1,0:T(8,128)(2,1)} %collective-permute-done.2), channel_id=1, source_target_pairs={{1,0},{2,3},{5,4},{6,7},{9,8},{10,11},{13,12},{14,15},{17,16},{18,... | collective-permute-start | bytes 1179656 | tf_op jit(solution)/shard_map/ppermute | solution.py:260
  69.8 10.8 %collective-permute-start.6 = (bf16[256,768]{1,0:T(8,128)(2,1)}, bf16[256,768]{1,0:T(8,128)(2,1)}, u32[]{:S(2)}, u32[]{:S(2)}) collective-permute-start(bf16[256,768]{1,0:T(8,128)(2,1)} %collective-permute-done.1.refs_4_), channel_id=1, source_target_pairs={{0,16},{1,17},{2,18},{3,19},{4,20},{5,21},{6,22},{7,23},{8,24},{9,... | collective-permute-start | bytes 1179656 | tf_op jit(solution)/shard_map/ppermute | solution.py:260
  71.3 13.6 %collective-permute-start.4 = (bf16[256,768]{1,0:T(8,128)(2,1)}, bf16[256,768]{1,0:T(8,128)(2,1)}, u32[]{:S(2)}, u32[]{:S(2)}) collective-permute-start(bf16[256,768]{1,0:T(8,128)(2,1)} %collective-permute-done.1.refs_4_), channel_id=1, source_target_pairs={{1,2},{2,1},{5,6},{6,5},{9,10},{10,9},{13,14},{14,13},{17,18},{18,... | collective-permute-start | bytes 1179656 | tf_op jit(solution)/shard_map/ppermute | solution.py:260
  75.6 16.3 %copy-start.17 = (bf16[256,768]{1,0:T(8,128)(2,1)S(1)}, bf16[256,768]{1,0:T(8,128)(2,1)}, u32[]{:S(2)}) copy-start(bf16[256,768]{1,0:T(8,128)(2,1)} %copy-done.16) | copy-start | bytes 1179652
  76.7 23.5 %copy-start.2 = (bf16[256,768]{1,0:T(8,128)(2,1)S(1)}, bf16[256,768]{1,0:T(8,128)(2,1)}, u32[]{:S(2)}) copy-start(bf16[256,768]{1,0:T(8,128)(2,1)} %copy-done.1) | copy-start | bytes 1179652
  76.7 23.5 %copy-start.4 = (bf16[256,768]{1,0:T(8,128)(2,1)S(1)}, bf16[256,768]{1,0:T(8,128)(2,1)}, u32[]{:S(2)}) copy-start(bf16[256,768]{1,0:T(8,128)(2,1)} %copy-done.3) | copy-start | bytes 1179652
  76.7 23.5 %copy-start.6 = (bf16[256,768]{1,0:T(8,128)(2,1)S(1)}, bf16[256,768]{1,0:T(8,128)(2,1)}, u32[]{:S(2)}) copy-start(bf16[256,768]{1,0:T(8,128)(2,1)} %copy-done.5) | copy-start | bytes 1179652
  76.8 23.5 %copy-start.8 = (bf16[256,768]{1,0:T(8,128)(2,1)S(1)}, bf16[256,768]{1,0:T(8,128)(2,1)}, u32[]{:S(2)}) copy-start(bf16[256,768]{1,0:T(8,128)(2,1)} %copy-done.7) | copy-start | bytes 1179652
  76.8 23.5 %copy-start.10 = (bf16[256,768]{1,0:T(8,128)(2,1)S(1)}, bf16[256,768]{1,0:T(8,128)(2,1)}, u32[]{:S(2)}) copy-start(bf16[256,768]{1,0:T(8,128)(2,1)} %copy-done.9) | copy-start | bytes 1179652
  77.9 11.0 %collective-permute-start.19 = (bf16[256,768]{1,0:T(8,128)(2,1)S(1)}, bf16[256,768]{1,0:T(8,128)(2,1)S(1)}, u32[]{:S(2)}, u32[]{:S(2)}) collective-permute-start(bf16[256,768]{1,0:T(8,128)(2,1)S(1)} %broadcast_select_fusion.1.refs_3_), channel_id=1, source_target_pairs={{0,16},{1,17},{2,18},{3,19},{4,20},{5,21},{6,22},{7,23},{8,24},{9,... | collective-permute-start | bytes 1179656 | tf_op jit(solution)/shard_map/ppermute | solution.py:260
  80.6 11.3 %collective-permute-start.18 = (bf16[256,768]{1,0:T(8,128)(2,1)}, bf16[256,768]{1,0:T(8,128)(2,1)S(1)}, u32[]{:S(2)}, u32[]{:S(2)}) collective-permute-start(bf16[256,768]{1,0:T(8,128)(2,1)} %copy-done.16), channel_id=1, source_target_pairs={{1,0},{2,3},{5,4},{6,7},{9,8},{10,11},{13,12},{14,15},{17,16},{18,... | collective-permute-start | bytes 1179656 | tf_op jit(solution)/shard_map/ppermute | solution.py:260
  85.9 11.4 %collective-permute-start.8 = (bf16[256,768]{1,0:T(8,128)(2,1)S(1)}, bf16[256,768]{1,0:T(8,128)(2,1)S(1)}, u32[]{:S(2)}, u32[]{:S(2)}) collective-permute-start(bf16[256,768]{1,0:T(8,128)(2,1)S(1)} %broadcast_select_fusion.3.refs_2_), channel_id=1, source_target_pairs={{0,16},{1,17},{2,18},{3,19},{4,20},{5,21},{6,22},{7,23},{8,24},{9,... | collective-permute-start | bytes 1179656 | tf_op jit(solution)/shard_map/ppermute | solution.py:260
  88.9 9.9 %collective-permute-start.7 = (bf16[256,768]{1,0:T(8,128)(2,1)}, bf16[256,768]{1,0:T(8,128)(2,1)S(1)}, u32[]{:S(2)}, u32[]{:S(2)}) collective-permute-start(bf16[256,768]{1,0:T(8,128)(2,1)} %collective-permute-done.4), channel_id=1, source_target_pairs={{1,0},{2,3},{5,4},{6,7},{9,8},{10,11},{13,12},{14,15},{17,16},{18,... | collective-permute-start | bytes 1179656 | tf_op jit(solution)/shard_map/ppermute | solution.py:260
  91.9 23.1 %collective-permute-start.20 = (bf16[256,256]{1,0:T(8,128)(2,1)S(1)}, bf16[256,256]{1,0:T(8,128)(2,1)S(1)}, u32[]{:S(2)}, u32[]{:S(2)}) collective-permute-start(bf16[256,256]{1,0:T(8,128)(2,1)S(1)} %slice_select_fusion.1), channel_id=1, source_target_pairs={{0,16},{1,17},{2,18},{3,19},{4,20},{5,21},{6,22},{7,23},{8,24},{9,... | collective-permute-start | bytes 393224 | tf_op jit(solution)/shard_map/ppermute | solution.py:260
  97.3 22.8 %collective-permute-start.25 = (bf16[256,512]{1,0:T(8,128)(2,1)S(1)}, bf16[256,512]{1,0:T(8,128)(2,1)S(1)}, u32[]{:S(2)}, u32[]{:S(2)}) collective-permute-start(bf16[256,512]{1,0:T(8,128)(2,1)S(1)} %slice_select_fusion), channel_id=1, source_target_pairs={{0,16},{1,17},{2,18},{3,19},{4,20},{5,21},{6,22},{7,23},{8,24},{9,... | collective-permute-start | bytes 786440 | tf_op jit(solution)/shard_map/ppermute | solution.py:260
  99.8 15.3 %collective-permute-start.9 = (bf16[256,768]{1,0:T(8,128)(2,1)S(1)}, bf16[256,768]{1,0:T(8,128)(2,1)S(1)}, u32[]{:S(2)}, u32[]{:S(2)}) collective-permute-start(bf16[256,768]{1,0:T(8,128)(2,1)S(1)} %broadcast_select_fusion.2.refs_4_), channel_id=1, source_target_pairs={{0,16},{1,17},{2,18},{3,19},{4,20},{5,21},{6,22},{7,23},{8,24},{9,... | collective-permute-start | bytes 1179656 | tf_op jit(solution)/shard_map/ppermute | solution.py:260
  115.1 6.1 %copy-start.14 = (f32[16]{0:T(128)S(1)}, f32[16]{0:T(128)}, u32[]{:S(2)}) copy-start(f32[16]{0:T(128)} %gate_ref.7) | copy-start | bytes 196
  116.8 4.4 %collective-permute-start.24 = (bf16[128,256]{1,0:T(8,128)(2,1)S(1)}, bf16[128,256]{1,0:T(8,128)(2,1)S(1)}, u32[]{:S(2)}, u32[]{:S(2)}) collective-permute-start(bf16[128,256]{1,0:T(8,128)(2,1)S(1)} %get-tuple-element.109), channel_id=1, source_target_pairs={{0,16},{1,17},{2,18},{3,19},{4,20},{5,21},{6,22},{7,23},{8,24},{9,... | collective-permute-start | bytes 196616 | tf_op jit(solution)/shard_map/ppermute | solution.py:260
  126.3 12.8 %collective-permute-start.29 = (bf16[256,256]{1,0:T(8,128)(2,1)S(1)}, bf16[256,256]{1,0:T(8,128)(2,1)S(1)}, u32[]{:S(2)}, u32[]{:S(2)}) collective-permute-start(bf16[256,256]{1,0:T(8,128)(2,1)S(1)} %get-tuple-element.121), channel_id=1, source_target_pairs={{0,8},{1,9},{2,10},{3,11},{4,12},{5,13},{6,14},{7,15},{8,0},{9,1},... | collective-permute-start | bytes 393224 | tf_op jit(solution)/shard_map/ppermute | solution.py:260
  127.5 14.0 %collective-permute-start.28 = (bf16[256,256]{1,0:T(8,128)(2,1)S(1)}, bf16[256,256]{1,0:T(8,128)(2,1)S(1)}, u32[]{:S(2)}, u32[]{:S(2)}) collective-permute-start(bf16[256,256]{1,0:T(8,128)(2,1)S(1)} %get-tuple-element.118), channel_id=1, source_target_pairs={{0,8},{1,9},{2,10},{3,11},{4,12},{5,13},{6,14},{7,15},{8,0},{9,1},... | collective-permute-start | bytes 393224 | tf_op jit(solution)/shard_map/ppermute | solution.py:260
  127.8 13.7 %collective-permute-start.30 = (bf16[256,256]{1,0:T(8,128)(2,1)S(1)}, bf16[256,256]{1,0:T(8,128)(2,1)S(1)}, u32[]{:S(2)}, u32[]{:S(2)}) collective-permute-start(bf16[256,256]{1,0:T(8,128)(2,1)S(1)} %get-tuple-element.119), channel_id=1, source_target_pairs={{0,12},{1,13},{2,14},{3,15},{4,8},{5,9},{6,10},{7,11},{8,4},{9,5},... | collective-permute-start | bytes 393224 | tf_op jit(solution)/shard_map/ppermute | solution.py:260
  133.5 8.0 %collective-permute-start.31 = (bf16[256,256]{1,0:T(8,128)(2,1)S(1)}, bf16[256,256]{1,0:T(8,128)(2,1)S(1)}, u32[]{:S(2)}, u32[]{:S(2)}) collective-permute-start(bf16[256,256]{1,0:T(8,128)(2,1)S(1)} %get-tuple-element.122), channel_id=1, source_target_pairs={{0,12},{1,13},{2,14},{3,15},{4,8},{5,9},{6,10},{7,11},{8,4},{9,5},... | collective-permute-start | bytes 393224 | tf_op jit(solution)/shard_map/ppermute | solution.py:260
  138.6 3.0 %collective-permute-start.27 = (bf16[256,256]{1,0:T(8,128)(2,1)S(1)}, bf16[256,256]{1,0:T(8,128)(2,1)S(1)}, u32[]{:S(2)}, u32[]{:S(2)}) collective-permute-start(bf16[256,256]{1,0:T(8,128)(2,1)S(1)} %get-tuple-element.128), channel_id=1, source_target_pairs={{0,4},{1,5},{2,6},{3,7},{4,0},{5,1},{6,2},{7,3},{8,12},{9,13},{10,... | collective-permute-start | bytes 393224 | tf_op jit(solution)/shard_map/ppermute | solution.py:260
  139.1 2.4 %collective-permute-start.26 = (bf16[256,256]{1,0:T(8,128)(2,1)S(1)}, bf16[256,256]{1,0:T(8,128)(2,1)S(1)}, u32[]{:S(2)}, u32[]{:S(2)}) collective-permute-start(bf16[256,256]{1,0:T(8,128)(2,1)S(1)} %get-tuple-element.125), channel_id=1, source_target_pairs={{0,4},{1,5},{2,6},{3,7},{4,0},{5,1},{6,2},{7,3},{8,12},{9,13},{10,... | collective-permute-start | bytes 393224 | tf_op jit(solution)/shard_map/ppermute | solution.py:260

commit v5 on v4

--- a/solution.py
+++ b/solution.py
@@ -272,45 +272,6 @@
     )(here, valid_len, block_mask, w_query, w_key, value_weight)
     messages = [packed[0], *[to_member(packed[k], k) for k in (1, 2, 3)]]
 
-    own = after(tokens[0], *messages)
-    across = to_member(own, 2)
-    sibling = to_member(own, 1)
-
-    def lines(pieces):
-        inside = (z == 1) | (z == 2)
-        over = lambda part: permute(part, lambda gg, mm, zz: (gg ^ 1, mm, zz))
-        pair = lambda part: permute(part, lambda gg, mm, zz: (gg, mm, zz ^ 1))
-        outward = lambda part: permute(
-            part, lambda gg, mm, zz: (gg, mm, zz ^ 1) if zz in (1, 2) else None
-        )
-        inward = lambda part: permute(
-            part, lambda gg, mm, zz: (gg, mm, zz ^ 3) if zz in (1, 2) else None
-        )
-        locked = lambda *parts: lax.optimization_barrier(parts)
-        states = [(pair(piece), inward(piece), over(piece)) for piece in pieces]
-        found, marks = [[] for _ in pieces], []
-        for n, piece in enumerate(pieces):
-            one, inner, far0 = locked(*states[n])
-            found[n] = [piece, one, far0]
-            states[n] = (inward(one), outward(inner), over(one), inner)
-        for n in range(len(pieces)):
-            middle, outer, far1, inner = locked(*states[n])
-            marks.append(far1)
-            two = jnp.where(inside, inner, outer)
-            states[n] = (outward(middle), over(two), middle, two, far1)
-        for n in range(len(pieces)):
-            last, far2, middle, two, far1 = locked(*states[n])
-            three = jnp.where(inside, middle, last)
-            piece, one, far0 = found[n]
-            found[n] = [piece, one, two, three, far0, far1, far2]
-            if n == 0:
-                final = over(three)
-                found[n] += [final, final]
-            else:
-                at = 2 * HEAD_SIZE
-                found[n] += [over(jnp.where(inside, middle[:, cut], last[:, cut])) for cut in (slice(0, at), slice(at, None))]
-        return found, marks[-1]
-
     def gathered(piece):
         index = lambda gg, mm, zz: (gg * MEMBERS + mm) * n_z + zz
         everything = lax.all_gather(
@@ -331,43 +292,83 @@
         jnp.concatenate([messages[k][:rows] for k in members], axis=0) for members in ((0, 1), (2, 3))
     ]
     n_pieces = width // (MEMBERS * HEAD_SIZE)
+    sums, lasts = [None] * MEMBERS, [None] * MEMBERS
+
+    def project(segs, places, upper, lower, line, first):
+        found = call(
+            functools.partial(project_body, places, line, n_pieces, first),
+            [shape((length, wide), f32)] * 2
+            + [shape((length, MEMBERS * HEAD_SIZE), bf16)] * (2 if first else 0),
+            [SMEM] + [VMEM] * (2 + 2 * len(places) + (0 if first else 2)),
+            flops=2 * 2 * length * len(places) * MEMBERS * HEAD_SIZE * wide,
+        )(
+            here,
+            *[books[s] for s in segs],
+            *[part[p] for p in places for part in (upper, lower)],
+            *([] if first else [sums[s] for s in segs]),
+        )
+        for at, s in enumerate(segs):
+            sums[s] = found[at]
+            if first:
+                lasts[s] = found[2 + at]
+
+    cut = 2 * HEAD_SIZE
     if n_groups == 2 and n_z == 4:
         assert rows == HEAD_SIZE
-        line = n_z
-        (upper, lower), mark = lines(pieces)
-        across_late = after(across, mark)
-        parts = [(0, 1, 4, 5), (2, 3, 6)]
+        inside = (z == 1) | (z == 2)
+        over = lambda part: permute(part, lambda gg, mm, zz: (gg ^ 1, mm, zz))
+        pair = lambda part: permute(part, lambda gg, mm, zz: (gg, mm, zz ^ 1))
+        outward = lambda part: permute(
+            part, lambda gg, mm, zz: (gg, mm, zz ^ 1) if zz in (1, 2) else None
+        )
+        inward = lambda part: permute(
+            part, lambda gg, mm, zz: (gg, mm, zz ^ 3) if zz in (1, 2) else None
+        )
+        locked = lambda *parts: lax.optimization_barrier(parts)
+        stage1 = lambda piece: (pair(piece), inward(piece), over(piece))
+        stage2 = lambda one, inner: (inward(one), outward(inner), over(one))
+        stage3 = lambda middle, two: (outward(middle), over(two))
+
+        a, b, own, sibling = locked(*pieces, tokens[0], to_member(tokens[0], 1))
+        across = to_member(own, 2)
+        a_one, a_inner, a_far0 = locked(*stage1(a))
+        b_one, b_inner, b_far0 = locked(*stage1(b))
+        a_middle, a_outer, a_far1 = locked(*stage2(a_one, a_inner))
+        b_middle, b_outer, b_far1 = locked(*stage2(b_one, b_inner))
+        a_two = jnp.where(inside, a_inner, a_outer)
+        a_last, a_far2 = stage3(a_middle, a_two)
+        b_two = jnp.where(inside, b_inner, b_outer)
+        b_last, b_far2 = stage3(b_middle, b_two)
+        (
+            a_last, a_far2, a_middle, a_two, a_far1, b_last, b_middle, b_two, b_far1, across, sibling, own
+        ) = locked(
+            a_last, a_far2, a_middle, a_two, a_far1, b_last, b_middle, b_two, b_far1, across, sibling, own
+        )
+        diagonal = to_member(across, 1)
+        a_three = jnp.where(inside, a_middle, a_last)
+        a_far3 = over(a_three)
+        b_three = jnp.where(inside, b_middle, b_last)
+        b_far3 = [
+            over(jnp.where(inside, b_middle[:, at], b_last[:, at]))
+            for at in (slice(0, cut), slice(cut, None))
+        ]
+        books = [own, sibling, across, diagonal]
+        upper = [a, a_one, a_two, a_three, a_far0, a_far1, a_far2, a_far3, a_far3]
+        lower = [b, b_one, b_two, b_three, b_far0, b_far1, b_far2] + b_far3
+        project((0, 1), (0, 1, 4, 5), upper, lower, n_z, True)
+        project((0, 1), (2, 3, 6), upper, lower, n_z, False)
+        project((2, 3), (0, 1, 4, 5), upper, lower, n_z, True)
+        project((2, 3), (2, 3, 6), upper, lower, n_z, False)
     else:
-        line = 0
+        across, sibling = to_member(tokens[0], 2), to_member(tokens[0], 1)
+        books = [tokens[0], sibling, across, to_member(across, 1)]
         full = gathered(jnp.concatenate(pieces, axis=0))
-        cut = MEMBERS * HEAD_SIZE // 2
-        upper, lower = [part[:cut] for part in full], [part[cut:] for part in full]
+        deep = MEMBERS * HEAD_SIZE // 2
+        upper, lower = [part[:deep] for part in full], [part[deep:] for part in full]
         upper.append(upper[-1])
-        lower[-1:] = [lower[-1][:, : 2 * HEAD_SIZE], lower[-1][:, 2 * HEAD_SIZE :]]
-        across_late = across
-        parts = [tuple(range(n_pieces - 1))]
-    diagonal = to_member(across_late, 1)
-    books = [tokens[0], sibling, across, diagonal]
-
-    sums, lasts = [None] * MEMBERS, [None] * MEMBERS
-    for c, places in enumerate(parts):
+        lower[-1:] = [lower[-1][:, :cut], lower[-1][:, cut:]]
         for segs in ((0, 1), (2, 3)):
-            found = call(
-                functools.partial(project_body, places, line, n_pieces, c == 0),
-                [shape((length, wide), f32)] * 2
-                + [shape((length, MEMBERS * HEAD_SIZE), bf16)] * (2 if c == 0 else 0),
-                [SMEM] + [VMEM] * (2 + 2 * len(places) + (0 if c == 0 else 2)),
-                flops=2 * 2 * length * len(places) * MEMBERS * HEAD_SIZE * wide,
-            )(
-                here,
-                *[books[s] for s in segs],
-                *[part[p] for p in places for part in (upper, lower)],
-                *([] if c == 0 else [sums[s] for s in segs]),
-            )
-            for at, s in enumerate(segs):
-                sums[s] = found[at]
-                if c == 0:
-                    lasts[s] = found[2 + at]
+            project(segs, tuple(range(n_pieces - 1)), upper, lower, 0, True)
 
     found = call(
         kv_body,

time: 146 us -> 138 us (0.945)
  the two profiles are of different devices: /device:TPU:9 before, /device:TPU:1 now
where the time goes in v5:
time: 138 us; the launch traced here: 137 us
  waiting for transfers between devices  55.2 us (40%)
  starting transfers between devices  41.9 us (30%)
  Pallas kernels  28.1 us (20%)
  local copies, waits for them, and re-layouts  6.63 us (5%)
  other arithmetic  4.27 us (3%)
    ppermute x32, waiting for transfers between devices, permute(): return lax.ppermute(array, AXES, pairs)  55.2 us
    ppermute x32, starting transfers between devices, permute(): return lax.ppermute(array, AXES, pairs)  41.9 us
    pallas_call x4, Pallas kernels, project(): call(functools.partial(project_body, places, line, n_pieces, first), [sha...  13.7 us
    pallas_call x4, Pallas kernels, attend(): call(functools.partial(attend_body, segs, half, c * half, group), [shape(...  10.1 us
    unnamed x32, local copies, waits for them, and re-layouts  6.58 us
  transfers between devices with their start and end apart: 32, of which 14 were waited for; matrix products, arithmetic and copies ran while one was open for 3% of the time, Pallas kernels for 16%

profile of v5, /device:TPU:1, one launch (start us, length us, event | category | flops | bytes accessed | tf_op | source)
XLA Modules:
  0.0 137.2 jit_solution(18253180849237979221)
XLA Ops:
  0.9 1.0 copy-done.9
  2.0 0.9 copy-done.10
  2.9 0.9 copy-done.11
  3.8 0.7 copy-done.13
  4.5 1.0 shard_map.73
  5.5 0.6 collective-permute-start
  6.0 2.2 %collective-permute-start.1 = (bf16[144,768]{1,0:T(8,128)(2,1)S(1)}, bf16[144,768]{1,0:T(8,128)(2,1)S(1)}, u32[]{:S(2)}, u32[]{:S(2)}) collective-permute-start(bf16[144,768]{1,0:T(8,128)(2,1)S(1)} %get-tuple-element.71), channel_id=1, source_target_pairs={{0,8},{1,9},{2,10},{3,11},{4,12},{5,13},{6,14},{7,15},{8,0},{9,1},... | collective-permute-start | bytes 663560 | tf_op jit(solution)/shard_map/ppermute | solution.py:260
  8.5 5.2 %collective-permute-done.1.refs_10_ = bf16[144,768]{1,0:T(8,128)(2,1)S(1)} collective-permute-done((bf16[144,768]{1,0:T(8,128)(2,1)S(1)}, bf16[144,768]{1,0:T(8,128)(2,1)S(1)}, u32[]{:S(2)}, u32[]{:S(2)}) %collective-permute-start.1) | collective-permute-done | bytes 221216 | tf_op jit(solution)/shard_map/ppermute | solution.py:260
  13.7 4.9 %collective-permute-done.2.refs_11_ = bf16[144,768]{1,0:T(8,128)(2,1)S(1)} collective-permute-done((bf16[144,768]{1,0:T(8,128)(2,1)S(1)}, bf16[144,768]{1,0:T(8,128)(2,1)S(1)}, u32[]{:S(2)}, u32[]{:S(2)}) %collective-permute-start.2) | collective-permute-done | bytes 221216 | tf_op jit(solution)/shard_map/ppermute | solution.py:260
  18.8 1.5 %collective-permute-start.19 = (bf16[256,4096]{1,0:T(8,128)(2,1)S(1)}, bf16[256,4096]{1,0:T(8,128)(2,1)}, u32[]{:S(2)}, u32[]{:S(2)}) collective-permute-start(bf16[256,4096]{1,0:T(8,128)(2,1)S(1)} %bitcast.6), channel_id=1, source_target_pairs={{0,8},{1,9},{2,10},{3,11},{4,12},{5,13},{6,14},{7,15},{8,0},{9,1},... | collective-permute-start | bytes 6291464 | tf_op jit(solution)/shard_map/ppermute | solution.py:260
  20.3 1.2 collective-permute-start.6
  21.5 0.7 collective-permute-start.5
  22.2 3.9 %collective-permute-start.4 = (bf16[256,768]{1,0:T(8,128)(2,1)S(1)}, bf16[256,768]{1,0:T(8,128)(2,1)}, u32[]{:S(2)}, u32[]{:S(2)}) collective-permute-start(bf16[256,768]{1,0:T(8,128)(2,1)S(1)} %pad_maximum_fusion.refs_2_), channel_id=1, source_target_pairs={{0,1},{1,0},{2,3},{3,2},{4,5},{5,4},{6,7},{7,6},{8,9},{9,8},{10,11... | collective-permute-start | bytes 1179656 | tf_op jit(solution)/shard_map/ppermute | solution.py:260
  26.3 4.6 %collective-permute-done.6.refs_6_ = bf16[256,768]{1,0:T(8,128)(2,1)S(1)} collective-permute-done((bf16[256,768]{1,0:T(8,128)(2,1)S(1)}, bf16[256,768]{1,0:T(8,128)(2,1)S(1)}, u32[]{:S(2)}, u32[]{:S(2)}) %collective-permute-start.6) | collective-permute-done | bytes 393248 | tf_op jit(solution)/shard_map/ppermute | solution.py:260
  30.9 0.8 copy-done.3
  31.7 1.4 %collective-permute-start.13 = (bf16[256,768]{1,0:T(8,128)(2,1)S(1)}, bf16[256,768]{1,0:T(8,128)(2,1)}, u32[]{:S(2)}, u32[]{:S(2)}) collective-permute-start(bf16[256,768]{1,0:T(8,128)(2,1)S(1)} %pad_maximum_fusion.1.refs_3_), channel_id=1, source_target_pairs={{1,2},{2,1},{5,6},{6,5},{9,10},{10,9},{13,14},{14,13},{17,18},{18,... | collective-permute-start | bytes 1179656 | tf_op jit(solution)/shard_map/ppermute | solution.py:260
  33.1 3.2 %collective-permute-start.12 = (bf16[256,768]{1,0:T(8,128)(2,1)S(1)}, bf16[256,768]{1,0:T(8,128)(2,1)}, u32[]{:S(2)}, u32[]{:S(2)}) collective-permute-start(bf16[256,768]{1,0:T(8,128)(2,1)S(1)} %pad_maximum_fusion.1.refs_3_), channel_id=1, source_target_pairs={{0,1},{1,0},{2,3},{3,2},{4,5},{5,4},{6,7},{7,6},{8,9},{9,8},{10,11... | collective-permute-start | bytes 1179656 | tf_op jit(solution)/shard_map/ppermute | solution.py:260
  36.3 0.8 copy-done.1
  37.1 1.3 collective-permute-start.8
  38.3 1.0 collective-permute-done.14.refs_7_
  39.4 0.8 copy-done.5
  40.1 1.2 collective-permute-start.9
  41.4 1.5 %collective-permute-start.7 = (bf16[256,768]{1,0:T(8,128)(2,1)}, bf16[256,768]{1,0:T(8,128)(2,1)}, u32[]{:S(2)}, u32[]{:S(2)}) collective-permute-start(bf16[256,768]{1,0:T(8,128)(2,1)} %collective-permute-done.4.refs_4_), channel_id=1, source_target_pairs={{1,2},{2,1},{5,6},{6,5},{9,10},{10,9},{13,14},{14,13},{17,18},{18,... | collective-permute-start | bytes 1179656 | tf_op jit(solution)/shard_map/ppermute | solution.py:260
  42.8 1.3 collective-permute-done.12.refs_5_
  44.1 1.3 collective-permute-start.16
  45.4 7.1 %collective-permute-done.8 = bf16[256,768]{1,0:T(8,128)(2,1)S(1)} collective-permute-done((bf16[256,768]{1,0:T(8,128)(2,1)S(1)}, bf16[256,768]{1,0:T(8,128)(2,1)S(1)}, u32[]{:S(2)}, u32[]{:S(2)}) %collective-permute-start.8) | collective-permute-done | bytes 393248 | tf_op jit(solution)/shard_map/ppermute | solution.py:260
  52.5 1.2 collective-permute-start.17
  53.8 0.7 copy-done.7
  54.5 1.4 %collective-permute-start.15 = (bf16[256,768]{1,0:T(8,128)(2,1)}, bf16[256,768]{1,0:T(8,128)(2,1)}, u32[]{:S(2)}, u32[]{:S(2)}) collective-permute-start(bf16[256,768]{1,0:T(8,128)(2,1)} %collective-permute-done.12.refs_5_), channel_id=1, source_target_pairs={{1,2},{2,1},{5,6},{6,5},{9,10},{10,9},{13,14},{14,13},{17,18},{18,... | collective-permute-start | bytes 1179656 | tf_op jit(solution)/shard_map/ppermute | solution.py:260
  56.0 1.0 broadcast_select_fusion.3.refs_2_
  57.0 0.8 collective-permute-start.11
  57.8 3.1 %collective-permute-done.16 = bf16[256,768]{1,0:T(8,128)(2,1)} collective-permute-done((bf16[256,768]{1,0:T(8,128)(2,1)}, bf16[256,768]{1,0:T(8,128)(2,1)}, u32[]{:S(2)}, u32[]{:S(2)}) %collective-permute-start.16) | collective-permute-done | bytes 393248 | tf_op jit(solution)/shard_map/ppermute | solution.py:260
  60.9 1.3 collective-permute-start.10
  62.3 1.3 collective-permute-start.18
  63.6 1.1 broadcast_select_fusion.2.refs_3_
  64.6 3.4 %collective-permute-done.11.refs_6_ = bf16[256,768]{1,0:T(8,128)(2,1)S(1)} collective-permute-done((bf16[256,768]{1,0:T(8,128)(2,1)S(1)}, bf16[256,768]{1,0:T(8,128)(2,1)S(1)}, u32[]{:S(2)}, u32[]{:S(2)}) %collective-permute-start.11) | collective-permute-done | bytes 393248 | tf_op jit(solution)/shard_map/ppermute | solution.py:260
  68.0 3.2 %collective-permute-done.10 = bf16[256,768]{1,0:T(8,128)(2,1)S(1)} collective-permute-done((bf16[256,768]{1,0:T(8,128)(2,1)}, bf16[256,768]{1,0:T(8,128)(2,1)S(1)}, u32[]{:S(2)}, u32[]{:S(2)}) %collective-permute-start.10) | collective-permute-done | bytes 393248 | tf_op jit(solution)/shard_map/ppermute | solution.py:260
  71.3 8.4 %collective-permute-done.18 = bf16[256,768]{1,0:T(8,128)(2,1)S(1)} collective-permute-done((bf16[256,768]{1,0:T(8,128)(2,1)}, bf16[256,768]{1,0:T(8,128)(2,1)S(1)}, u32[]{:S(2)}, u32[]{:S(2)}) %collective-permute-start.18) | collective-permute-done | bytes 393248 | tf_op jit(solution)/shard_map/ppermute | solution.py:260
  79.7 3.3 %collective-permute-start.23 = (bf16[256,4096]{1,0:T(8,128)(2,1)}, bf16[256,4096]{1,0:T(8,128)(2,1)S(1)}, u32[]{:S(2)}, u32[]{:S(2)}) collective-permute-start(bf16[256,4096]{1,0:T(8,128)(2,1)} %collective-permute-done.19.refs_0_), channel_id=1, source_target_pairs={{0,4},{1,5},{2,6},{3,7},{4,0},{5,1},{6,2},{7,3},{8,12},{9,13},{10,... | collective-permute-start | bytes 6291464 | tf_op jit(solution)/shard_map/ppermute | solution.py:260
  83.0 1.2 collective-permute-start.22
  84.2 0.9 slice_select_fusion.1
  85.2 0.3 collective-permute-start.21
  85.5 1.0 slice_select_fusion
  86.4 1.3 collective-permute-start.25
  87.8 0.3 collective-permute-start.20
  88.2 3.8 %shard_map.74 = (f32[256,768]{1,0:T(8,128)S(1)}, f32[256,768]{1,0:T(8,128)S(1)}, bf16[256,512]{1,0:T(8,128)(2,1)S(1)}, bf16[256,512]{1,0:T(8,128)(2,1)S(1)}) custom-call(s32[3]{0:T(128)S(1)} %pad_add_fusion.here_ref, bf16[256,4096]{1,0:T(8,128)(2,1)S(1)} %bitcast.7, bf16[256,4096]{1,0:T(8,128)(2,1)} %collective-permute-done.3.refs_1_, ...), custom_call_target="tpu_custom_call" | custom-call | flops 1610612736 | bytes 4194304 | tf_op jit(solution)/shard_map/pallas_call | solution.py:298
  92.0 1.7 %collective-permute-done.22.refs_7_ = bf16[256,768]{1,0:T(8,128)(2,1)S(1)} collective-permute-done((bf16[256,768]{1,0:T(8,128)(2,1)S(1)}, bf16[256,768]{1,0:T(8,128)(2,1)S(1)}, u32[]{:S(2)}, u32[]{:S(2)}) %collective-permute-start.22) | collective-permute-done | bytes 393248 | tf_op jit(solution)/shard_map/ppermute | solution.py:260
  93.7 3.1 %shard_map.75 = (f32[256,768]{1,0:T(8,128)S(1)}, f32[256,768]{1,0:T(8,128)S(1)}) custom-call(s32[3]{0:T(128)S(1)} %pad_add_fusion.here_ref, bf16[256,4096]{1,0:T(8,128)(2,1)S(1)} %bitcast.8, bf16[256,4096]{1,0:T(8,128)(2,1)} %collective-permute-done.3.refs_1_, bf16[256,768]{1,0:T(8,128)(2,1)S(1)} %broadcast_select_fusion.3.refs_2_, ...), custom_call_target="tpu_custom_call" | custom-call | flops 1207959552 | bytes 4194304 | tf_op jit(solution)/shard_map/pallas_call | solution.py:298
  96.8 3.8 %shard_map.76 = (f32[256,768]{1,0:T(8,128)S(1)}, f32[256,768]{1,0:T(8,128)S(1)}, bf16[256,512]{1,0:T(8,128)(2,1)S(1)}, bf16[256,512]{1,0:T(8,128)(2,1)S(1)}) custom-call(s32[3]{0:T(128)S(1)} %pad_add_fusion.here_ref, bf16[256,4096]{1,0:T(8,128)(2,1)} %collective-permute-done.19.refs_0_, bf16[256,4096]{1,0:T(8,128)(2,1)S(1)} %collective-permute-done.23.refs_1_, ...), custom_call_target="tpu_custom_call" | custom-call | flops 1610612736 | bytes 4194304 | tf_op jit(solution)/shard_map/pallas_call | solution.py:298
  100.6 3.1 %shard_map.77 = (f32[256,768]{1,0:T(8,128)S(1)}, f32[256,768]{1,0:T(8,128)S(1)}) custom-call(s32[3]{0:T(128)S(1)} %pad_add_fusion.here_ref, bf16[256,4096]{1,0:T(8,128)(2,1)} %collective-permute-done.19.refs_0_, bf16[256,4096]{1,0:T(8,128)(2,1)S(1)} %collective-permute-done.23.refs_1_, bf16[256,768]{1,0:T(8,128)(2,1)S(1)} %broadcast_select_fusion.3.refs_2_, ...), custom_call_target="tpu_custom_call" | custom-call | flops 1207959552 | bytes 4194304 | tf_op jit(solution)/shard_map/pallas_call | solution.py:298
  103.7 6.9 %collective-permute-done.20.upper_ref = bf16[256,768]{1,0:T(8,128)(2,1)S(1)} collective-permute-done((bf16[256,768]{1,0:T(8,128)(2,1)S(1)}, bf16[256,768]{1,0:T(8,128)(2,1)S(1)}, u32[]{:S(2)}, u32[]{:S(2)}) %collective-permute-start.20) | collective-permute-done | bytes 393248 | tf_op jit(solution)/shard_map/ppermute | solution.py:260
  110.6 1.6 %shard_map.78 = (bf16[256,256]{1,0:T(8,128)(2,1)S(1)}, f32[128,256]{1,0:T(8,128)S(1)}, bf16[256,256]{1,0:T(8,128)(2,1)S(1)}, f32[128,256]{1,0:T(8,128)S(1)}, bf1...) custom-call(bf16[256,768]{1,0:T(8,128)(2,1)S(1)} %collective-permute, ...), custom_call_target="tpu_custom_call" | custom-call | flops 268435456 | bytes 4194304 | tf_op jit(solution)/shard_map/pallas_call | solution.py:373
  112.3 3.3 %collective-permute-start.24 = (bf16[128,256]{1,0:T(8,128)(2,1)S(1)}, bf16[128,256]{1,0:T(8,128)(2,1)S(1)}, u32[]{:S(2)}, u32[]{:S(2)}) collective-permute-start(bf16[128,256]{1,0:T(8,128)(2,1)S(1)} %get-tuple-element.113), channel_id=1, source_target_pairs={{0,16},{1,17},{2,18},{3,19},{4,20},{5,21},{6,22},{7,23},{8,24},{9,... | collective-permute-start | bytes 196616 | tf_op jit(solution)/shard_map/ppermute | solution.py:260
  115.6 1.1 collective-permute-done.24.base_ref
  116.7 2.5 %shard_map.79 = (bf16[256,256]{1,0:T(8,128)(2,1)S(1)}, bf16[256,256]{1,0:T(8,128)(2,1)S(1)}) custom-call(s32[3]{0:T(128)S(1)} %pad_add_fusion.here_ref, f32[16]{0:T(128)S(1)} %copy-done.12, bf16[128,256]{1,0:T(8,128)(2,1)S(1)} %collective-permute-done.24.base_ref, bf16[256,768]{1,0:T(8,128)(2,1)S(1)} %collective-permute-done.20.upper_ref, ...), custom_call_target="tpu_custom_call" | custom-call | flops 201326592 | bytes 4194304 | tf_op jit(solution)/shard_map/pallas_call | solution.py:390
  119.3 2.5 %shard_map.80 = (bf16[256,256]{1,0:T(8,128)(2,1)S(1)}, bf16[256,256]{1,0:T(8,128)(2,1)S(1)}) custom-call(s32[3]{0:T(128)S(1)} %pad_add_fusion.here_ref, f32[16]{0:T(128)S(1)} %copy-done.12, bf16[128,256]{1,0:T(8,128)(2,1)S(1)} %collective-permute-done.24.base_ref, bf16[256,768]{1,0:T(8,128)(2,1)S(1)} %collective-permute-done.20.upper_ref, ...), custom_call_target="tpu_custom_call" | custom-call | flops 201326592 | bytes 4194304 | tf_op jit(solution)/shard_map/pallas_call | solution.py:390
  121.8 0.3 collective-permute-start.29
  122.1 1.2 collective-permute-start.28
  123.3 2.3 %collective-permute-start.30 = (bf16[256,256]{1,0:T(8,128)(2,1)S(1)}, bf16[256,256]{1,0:T(8,128)(2,1)S(1)}, u32[]{:S(2)}, u32[]{:S(2)}) collective-permute-start(bf16[256,256]{1,0:T(8,128)(2,1)S(1)} %get-tuple-element.123), channel_id=1, source_target_pairs={{0,12},{1,13},{2,14},{3,15},{4,8},{5,9},{6,10},{7,11},{8,4},{9,5},... | collective-permute-start | bytes 393224 | tf_op jit(solution)/shard_map/ppermute | solution.py:260
  125.7 2.5 %shard_map.81 = (bf16[256,256]{1,0:T(8,128)(2,1)S(1)}, bf16[256,256]{1,0:T(8,128)(2,1)S(1)}) custom-call(s32[3]{0:T(128)S(1)} %pad_add_fusion.here_ref, f32[16]{0:T(128)S(1)} %copy-done.12, bf16[128,256]{1,0:T(8,128)(2,1)S(1)} %collective-permute-done.24.base_ref, bf16[256,768]{1,0:T(8,128)(2,1)S(1)} %collective-permute-done.20.upper_ref, ...), custom_call_target="tpu_custom_call" | custom-call | flops 201326592 | bytes 4194304 | tf_op jit(solution)/shard_map/pallas_call | solution.py:390
  128.2 2.5 %shard_map.82 = (bf16[256,256]{1,0:T(8,128)(2,1)S(1)}, bf16[256,256]{1,0:T(8,128)(2,1)S(1)}) custom-call(s32[3]{0:T(128)S(1)} %pad_add_fusion.here_ref, f32[16]{0:T(128)S(1)} %copy-done.12, bf16[128,256]{1,0:T(8,128)(2,1)S(1)} %collective-permute-done.24.base_ref, bf16[256,768]{1,0:T(8,128)(2,1)S(1)} %collective-permute-done.20.upper_ref, ...), custom_call_target="tpu_custom_call" | custom-call | flops 201326592 | bytes 4194304 | tf_op jit(solution)/shard_map/pallas_call | solution.py:390
  130.8 1.6 %collective-permute-start.27 = (bf16[256,256]{1,0:T(8,128)(2,1)S(1)}, bf16[256,256]{1,0:T(8,128)(2,1)S(1)}, u32[]{:S(2)}, u32[]{:S(2)}) collective-permute-start(bf16[256,256]{1,0:T(8,128)(2,1)S(1)} %get-tuple-element.132), channel_id=1, source_target_pairs={{0,4},{1,5},{2,6},{3,7},{4,0},{5,1},{6,2},{7,3},{8,12},{9,13},{10,... | collective-permute-start | bytes 393224 | tf_op jit(solution)/shard_map/ppermute | solution.py:260
  132.5 3.0 %collective-permute-done.31.refs_7_ = bf16[256,256]{1,0:T(8,128)(2,1)S(1)} collective-permute-done((bf16[256,256]{1,0:T(8,128)(2,1)S(1)}, bf16[256,256]{1,0:T(8,128)(2,1)S(1)}, u32[]{:S(2)}, u32[]{:S(2)}) %collective-permute-start.31) | collective-permute-done | bytes 131104 | tf_op jit(solution)/shard_map/ppermute | solution.py:260
  135.5 1.6 %shard_map.83 = bf16[256,2048]{1,0:T(8,128)(2,1)} custom-call(s32[3]{0:T(128)S(1)} %pad_add_fusion.here_ref, bf16[256,256]{1,0:T(8,128)(2,1)S(1)} %get-tuple-element.128.refs_0_, bf16[256,256]{1,0:T(8,128)(2,1)S(1)} %get-tuple-element.131.refs_1_, bf16[256,256]{1,0:T(8,128)(2,1)S(1)} %collective-permute-done.26.refs_2_, ...), custom_call_target="tpu_custom_call" | custom-call | bytes 4194304 | tf_op jit(solution)/shard_map/pallas_call | solution.py:407
  (56 shorter events, 1.1 us)
Async XLA Ops:
  0.0 18.8 %copy-start = (bf16[1,256,4096]{2,1,0:T(8,128)(2,1)S(1)}, bf16[1,256,4096]{2,1,0:T(8,128)(2,1)}, u32[]{:S(2)}) copy-start(bf16[1,256,4096]{2,1,0:T(8,128)(2,1)} %param.7) | copy-start | bytes 6291460
  0.0 18.7 %collective-permute-start.3 = (bf16[256,4096]{1,0:T(8,128)(2,1)}, bf16[256,4096]{1,0:T(8,128)(2,1)}, u32[]{:S(2)}, u32[]{:S(2)}) collective-permute-start(bf16[256,4096]{1,0:T(8,128)(2,1)} %bitcast.5), channel_id=1, source_target_pairs={{0,4},{1,5},{2,6},{3,7},{4,0},{5,1},{6,2},{7,3},{8,12},{9,13},{10,... | collective-permute-start | bytes 6291464 | tf_op jit(solution)/shard_map/ppermute | solution.py:260
  0.9 1.0 copy-start.9
  2.0 0.9 copy-start.10
  2.9 0.9 copy-start.11
  3.8 0.7 copy-start.13
  5.5 3.0 %collective-permute-start = (bf16[144,768]{1,0:T(8,128)(2,1)S(1)}, bf16[144,768]{1,0:T(8,128)(2,1)S(1)}, u32[]{:S(2)}, u32[]{:S(2)}) collective-permute-start(bf16[144,768]{1,0:T(8,128)(2,1)S(1)} %get-tuple-element.70), channel_id=1, source_target_pairs={{0,4},{1,5},{2,6},{3,7},{4,0},{5,1},{6,2},{7,3},{8,12},{9,13},{10,... | collective-permute-start | bytes 663560 | tf_op jit(solution)/shard_map/ppermute | solution.py:260
  6.0 7.7 %collective-permute-start.1 = (bf16[144,768]{1,0:T(8,128)(2,1)S(1)}, bf16[144,768]{1,0:T(8,128)(2,1)S(1)}, u32[]{:S(2)}, u32[]{:S(2)}) collective-permute-start(bf16[144,768]{1,0:T(8,128)(2,1)S(1)} %get-tuple-element.71), channel_id=1, source_target_pairs={{0,8},{1,9},{2,10},{3,11},{4,12},{5,13},{6,14},{7,15},{8,0},{9,1},... | collective-permute-start | bytes 663560 | tf_op jit(solution)/shard_map/ppermute | solution.py:260
  8.2 10.4 %collective-permute-start.2 = (bf16[144,768]{1,0:T(8,128)(2,1)S(1)}, bf16[144,768]{1,0:T(8,128)(2,1)S(1)}, u32[]{:S(2)}, u32[]{:S(2)}) collective-permute-start(bf16[144,768]{1,0:T(8,128)(2,1)S(1)} %get-tuple-element.72), channel_id=1, source_target_pairs={{0,12},{1,13},{2,14},{3,15},{4,8},{5,9},{6,10},{7,11},{8,4},{9,5},... | collective-permute-start | bytes 663560 | tf_op jit(solution)/shard_map/ppermute | solution.py:260
  18.8 61.0 %collective-permute-start.19 = (bf16[256,4096]{1,0:T(8,128)(2,1)S(1)}, bf16[256,4096]{1,0:T(8,128)(2,1)}, u32[]{:S(2)}, u32[]{:S(2)}) collective-permute-start(bf16[256,4096]{1,0:T(8,128)(2,1)S(1)} %bitcast.6), channel_id=1, source_target_pairs={{0,8},{1,9},{2,10},{3,11},{4,12},{5,13},{6,14},{7,15},{8,0},{9,1},... | collective-permute-start | bytes 6291464 | tf_op jit(solution)/shard_map/ppermute | solution.py:260
  20.3 10.7 %collective-permute-start.6 = (bf16[256,768]{1,0:T(8,128)(2,1)S(1)}, bf16[256,768]{1,0:T(8,128)(2,1)S(1)}, u32[]{:S(2)}, u32[]{:S(2)}) collective-permute-start(bf16[256,768]{1,0:T(8,128)(2,1)S(1)} %pad_maximum_fusion.refs_2_), channel_id=1, source_target_pairs={{0,16},{1,17},{2,18},{3,19},{4,20},{5,21},{6,22},{7,23},{8,24},{9,... | collective-permute-start | bytes 1179656 | tf_op jit(solution)/shard_map/ppermute | solution.py:260
  21.5 11.6 %collective-permute-start.5 = (bf16[256,768]{1,0:T(8,128)(2,1)S(1)}, bf16[256,768]{1,0:T(8,128)(2,1)S(1)}, u32[]{:S(2)}, u32[]{:S(2)}) collective-permute-start(bf16[256,768]{1,0:T(8,128)(2,1)S(1)} %pad_maximum_fusion.refs_2_), channel_id=1, source_target_pairs={{1,2},{2,1},{5,6},{6,5},{9,10},{10,9},{13,14},{14,13},{17,18},{18,... | collective-permute-start | bytes 1179656 | tf_op jit(solution)/shard_map/ppermute | solution.py:260
  22.2 14.8 %collective-permute-start.4 = (bf16[256,768]{1,0:T(8,128)(2,1)S(1)}, bf16[256,768]{1,0:T(8,128)(2,1)}, u32[]{:S(2)}, u32[]{:S(2)}) collective-permute-start(bf16[256,768]{1,0:T(8,128)(2,1)S(1)} %pad_maximum_fusion.refs_2_), channel_id=1, source_target_pairs={{0,1},{1,0},{2,3},{3,2},{4,5},{5,4},{6,7},{7,6},{8,9},{9,8},{10,11... | collective-permute-start | bytes 1179656 | tf_op jit(solution)/shard_map/ppermute | solution.py:260
  26.1 13.3 %collective-permute-start.14 = (bf16[256,768]{1,0:T(8,128)(2,1)S(1)}, bf16[256,768]{1,0:T(8,128)(2,1)S(1)}, u32[]{:S(2)}, u32[]{:S(2)}) collective-permute-start(bf16[256,768]{1,0:T(8,128)(2,1)S(1)} %pad_maximum_fusion.1.refs_3_), channel_id=1, source_target_pairs={{0,16},{1,17},{2,18},{3,19},{4,20},{5,21},{6,22},{7,23},{8,24},{9,... | collective-permute-start | bytes 1179656 | tf_op jit(solution)/shard_map/ppermute | solution.py:260
  30.9 0.8 copy-start.3
  31.7 9.7 %collective-permute-start.13 = (bf16[256,768]{1,0:T(8,128)(2,1)S(1)}, bf16[256,768]{1,0:T(8,128)(2,1)}, u32[]{:S(2)}, u32[]{:S(2)}) collective-permute-start(bf16[256,768]{1,0:T(8,128)(2,1)S(1)} %pad_maximum_fusion.1.refs_3_), channel_id=1, source_target_pairs={{1,2},{2,1},{5,6},{6,5},{9,10},{10,9},{13,14},{14,13},{17,18},{18,... | collective-permute-start | bytes 1179656 | tf_op jit(solution)/shard_map/ppermute | solution.py:260
  33.1 20.7 %copy-start.14 = (bf16[256,768]{1,0:T(8,128)(2,1)}, bf16[256,768]{1,0:T(8,128)(2,1)S(1)}, u32[]{:S(2)}) copy-start(bf16[256,768]{1,0:T(8,128)(2,1)S(1)} %collective-permute-done.5) | copy-start | bytes 1179652
  33.1 11.0 %collective-permute-start.12 = (bf16[256,768]{1,0:T(8,128)(2,1)S(1)}, bf16[256,768]{1,0:T(8,128)(2,1)}, u32[]{:S(2)}, u32[]{:S(2)}) collective-permute-start(bf16[256,768]{1,0:T(8,128)(2,1)S(1)} %pad_maximum_fusion.1.refs_3_), channel_id=1, source_target_pairs={{0,1},{1,0},{2,3},{3,2},{4,5},{5,4},{6,7},{7,6},{8,9},{9,8},{10,11... | collective-permute-start | bytes 1179656 | tf_op jit(solution)/shard_map/ppermute | solution.py:260
  36.3 0.8 copy-start.1
  37.1 15.5 %collective-permute-start.8 = (bf16[256,768]{1,0:T(8,128)(2,1)S(1)}, bf16[256,768]{1,0:T(8,128)(2,1)S(1)}, u32[]{:S(2)}, u32[]{:S(2)}) collective-permute-start(bf16[256,768]{1,0:T(8,128)(2,1)S(1)} %collective-permute-done.5), channel_id=1, source_target_pairs={{1,0},{2,3},{5,4},{6,7},{9,8},{10,11},{13,12},{14,15},{17,16},{18,... | collective-permute-start | bytes 1179656 | tf_op jit(solution)/shard_map/ppermute | solution.py:260
  39.4 0.8 copy-start.5
  40.1 13.6 %collective-permute-start.9 = (bf16[256,768]{1,0:T(8,128)(2,1)}, bf16[256,768]{1,0:T(8,128)(2,1)S(1)}, u32[]{:S(2)}, u32[]{:S(2)}) collective-permute-start(bf16[256,768]{1,0:T(8,128)(2,1)} %collective-permute-done.4.refs_4_), channel_id=1, source_target_pairs={{0,16},{1,17},{2,18},{3,19},{4,20},{5,21},{6,22},{7,23},{8,24},{9,... | collective-permute-start | bytes 1179656 | tf_op jit(solution)/shard_map/ppermute | solution.py:260
  41.4 14.6 %collective-permute-start.7 = (bf16[256,768]{1,0:T(8,128)(2,1)}, bf16[256,768]{1,0:T(8,128)(2,1)}, u32[]{:S(2)}, u32[]{:S(2)}) collective-permute-start(bf16[256,768]{1,0:T(8,128)(2,1)} %collective-permute-done.4.refs_4_), channel_id=1, source_target_pairs={{1,2},{2,1},{5,6},{6,5},{9,10},{10,9},{13,14},{14,13},{17,18},{18,... | collective-permute-start | bytes 1179656 | tf_op jit(solution)/shard_map/ppermute | solution.py:260
  44.1 16.9 %collective-permute-start.16 = (bf16[256,768]{1,0:T(8,128)(2,1)}, bf16[256,768]{1,0:T(8,128)(2,1)}, u32[]{:S(2)}, u32[]{:S(2)}) collective-permute-start(bf16[256,768]{1,0:T(8,128)(2,1)} %collective-permute-done.13), channel_id=1, source_target_pairs={{1,0},{2,3},{5,4},{6,7},{9,8},{10,11},{13,12},{14,15},{17,16},{18,... | collective-permute-start | bytes 1179656 | tf_op jit(solution)/shard_map/ppermute | solution.py:260
  52.5 1.2 copy-start.15
  52.5 9.7 %collective-permute-start.17 = (bf16[256,768]{1,0:T(8,128)(2,1)}, bf16[256,768]{1,0:T(8,128)(2,1)}, u32[]{:S(2)}, u32[]{:S(2)}) collective-permute-start(bf16[256,768]{1,0:T(8,128)(2,1)} %collective-permute-done.12.refs_5_), channel_id=1, source_target_pairs={{0,16},{1,17},{2,18},{3,19},{4,20},{5,21},{6,22},{7,23},{8,24},{9,... | collective-permute-start | bytes 1179656 | tf_op jit(solution)/shard_map/ppermute | solution.py:260
  53.8 0.7 copy-start.7
  54.5 7.7 %collective-permute-start.15 = (bf16[256,768]{1,0:T(8,128)(2,1)}, bf16[256,768]{1,0:T(8,128)(2,1)}, u32[]{:S(2)}, u32[]{:S(2)}) collective-permute-start(bf16[256,768]{1,0:T(8,128)(2,1)} %collective-permute-done.12.refs_5_), channel_id=1, source_target_pairs={{1,2},{2,1},{5,6},{6,5},{9,10},{10,9},{13,14},{14,13},{17,18},{18,... | collective-permute-start | bytes 1179656 | tf_op jit(solution)/shard_map/ppermute | solution.py:260
  57.0 31.2 %copy-start.2 = (bf16[256,768]{1,0:T(8,128)(2,1)S(1)}, bf16[256,768]{1,0:T(8,128)(2,1)}, u32[]{:S(2)}) copy-start(bf16[256,768]{1,0:T(8,128)(2,1)} %copy-done.1) | copy-start | bytes 1179652
  57.0 31.2 %copy-start.4 = (bf16[256,768]{1,0:T(8,128)(2,1)S(1)}, bf16[256,768]{1,0:T(8,128)(2,1)}, u32[]{:S(2)}) copy-start(bf16[256,768]{1,0:T(8,128)(2,1)} %copy-done.3) | copy-start | bytes 1179652
  57.0 31.2 %copy-start.6 = (bf16[256,768]{1,0:T(8,128)(2,1)S(1)}, bf16[256,768]{1,0:T(8,128)(2,1)}, u32[]{:S(2)}) copy-start(bf16[256,768]{1,0:T(8,128)(2,1)} %copy-done.5) | copy-start | bytes 1179652
  57.0 31.2 %copy-start.8 = (bf16[256,768]{1,0:T(8,128)(2,1)S(1)}, bf16[256,768]{1,0:T(8,128)(2,1)}, u32[]{:S(2)}) copy-start(bf16[256,768]{1,0:T(8,128)(2,1)} %copy-done.7) | copy-start | bytes 1179652
  57.0 11.0 %collective-permute-start.11 = (bf16[256,768]{1,0:T(8,128)(2,1)S(1)}, bf16[256,768]{1,0:T(8,128)(2,1)S(1)}, u32[]{:S(2)}, u32[]{:S(2)}) collective-permute-start(bf16[256,768]{1,0:T(8,128)(2,1)S(1)} %broadcast_select_fusion.3.refs_2_), channel_id=1, source_target_pairs={{0,16},{1,17},{2,18},{3,19},{4,20},{5,21},{6,22},{7,23},{8,24},{9,... | collective-permute-start | bytes 1179656 | tf_op jit(solution)/shard_map/ppermute | solution.py:260
  60.9 10.3 %collective-permute-start.10 = (bf16[256,768]{1,0:T(8,128)(2,1)}, bf16[256,768]{1,0:T(8,128)(2,1)S(1)}, u32[]{:S(2)}, u32[]{:S(2)}) collective-permute-start(bf16[256,768]{1,0:T(8,128)(2,1)} %collective-permute-done.7), channel_id=1, source_target_pairs={{1,0},{2,3},{5,4},{6,7},{9,8},{10,11},{13,12},{14,15},{17,16},{18,... | collective-permute-start | bytes 1179656 | tf_op jit(solution)/shard_map/ppermute | solution.py:260
  62.3 17.4 %collective-permute-start.18 = (bf16[256,768]{1,0:T(8,128)(2,1)}, bf16[256,768]{1,0:T(8,128)(2,1)S(1)}, u32[]{:S(2)}, u32[]{:S(2)}) collective-permute-start(bf16[256,768]{1,0:T(8,128)(2,1)} %collective-permute-done.15), channel_id=1, source_target_pairs={{1,0},{2,3},{5,4},{6,7},{9,8},{10,11},{13,12},{14,15},{17,16},{18,... | collective-permute-start | bytes 1179656 | tf_op jit(solution)/shard_map/ppermute | solution.py:260
  79.7 17.1 %collective-permute-start.23 = (bf16[256,4096]{1,0:T(8,128)(2,1)}, bf16[256,4096]{1,0:T(8,128)(2,1)S(1)}, u32[]{:S(2)}, u32[]{:S(2)}) collective-permute-start(bf16[256,4096]{1,0:T(8,128)(2,1)} %collective-permute-done.19.refs_0_), channel_id=1, source_target_pairs={{0,4},{1,5},{2,6},{3,7},{4,0},{5,1},{6,2},{7,3},{8,12},{9,13},{10,... | collective-permute-start | bytes 6291464 | tf_op jit(solution)/shard_map/ppermute | solution.py:260
  83.0 10.7 %collective-permute-start.22 = (bf16[256,768]{1,0:T(8,128)(2,1)S(1)}, bf16[256,768]{1,0:T(8,128)(2,1)S(1)}, u32[]{:S(2)}, u32[]{:S(2)}) collective-permute-start(bf16[256,768]{1,0:T(8,128)(2,1)S(1)} %broadcast_select_fusion.2.refs_3_), channel_id=1, source_target_pairs={{0,16},{1,17},{2,18},{3,19},{4,20},{5,21},{6,22},{7,23},{8,24},{9,... | collective-permute-start | bytes 1179656 | tf_op jit(solution)/shard_map/ppermute | solution.py:260
  85.2 18.5 %collective-permute-start.21 = (bf16[256,256]{1,0:T(8,128)(2,1)S(1)}, bf16[256,256]{1,0:T(8,128)(2,1)S(1)}, u32[]{:S(2)}, u32[]{:S(2)}) collective-permute-start(bf16[256,256]{1,0:T(8,128)(2,1)S(1)} %slice_select_fusion.1), channel_id=1, source_target_pairs={{0,16},{1,17},{2,18},{3,19},{4,20},{5,21},{6,22},{7,23},{8,24},{9,... | collective-permute-start | bytes 393224 | tf_op jit(solution)/shard_map/ppermute | solution.py:260
  86.4 29.2 %collective-permute-start.25 = (bf16[256,512]{1,0:T(8,128)(2,1)S(1)}, bf16[256,512]{1,0:T(8,128)(2,1)S(1)}, u32[]{:S(2)}, u32[]{:S(2)}) collective-permute-start(bf16[256,512]{1,0:T(8,128)(2,1)S(1)} %slice_select_fusion), channel_id=1, source_target_pairs={{0,16},{1,17},{2,18},{3,19},{4,20},{5,21},{6,22},{7,23},{8,24},{9,... | collective-permute-start | bytes 786440 | tf_op jit(solution)/shard_map/ppermute | solution.py:260
  87.8 22.8 %collective-permute-start.20 = (bf16[256,768]{1,0:T(8,128)(2,1)S(1)}, bf16[256,768]{1,0:T(8,128)(2,1)S(1)}, u32[]{:S(2)}, u32[]{:S(2)}) collective-permute-start(bf16[256,768]{1,0:T(8,128)(2,1)S(1)} %broadcast_select_fusion.1.refs_4_), channel_id=1, source_target_pairs={{0,16},{1,17},{2,18},{3,19},{4,20},{5,21},{6,22},{7,23},{8,24},{9,... | collective-permute-start | bytes 1179656 | tf_op jit(solution)/shard_map/ppermute | solution.py:260
  110.6 6.1 %copy-start.12 = (f32[16]{0:T(128)S(1)}, f32[16]{0:T(128)}, u32[]{:S(2)}) copy-start(f32[16]{0:T(128)} %gate_ref.7) | copy-start | bytes 196
  112.3 4.5 %collective-permute-start.24 = (bf16[128,256]{1,0:T(8,128)(2,1)S(1)}, bf16[128,256]{1,0:T(8,128)(2,1)S(1)}, u32[]{:S(2)}, u32[]{:S(2)}) collective-permute-start(bf16[128,256]{1,0:T(8,128)(2,1)S(1)} %get-tuple-element.113), channel_id=1, source_target_pairs={{0,16},{1,17},{2,18},{3,19},{4,20},{5,21},{6,22},{7,23},{8,24},{9,... | collective-permute-start | bytes 196616 | tf_op jit(solution)/shard_map/ppermute | solution.py:260
  121.8 10.6 %collective-permute-start.29 = (bf16[256,256]{1,0:T(8,128)(2,1)S(1)}, bf16[256,256]{1,0:T(8,128)(2,1)S(1)}, u32[]{:S(2)}, u32[]{:S(2)}) collective-permute-start(bf16[256,256]{1,0:T(8,128)(2,1)S(1)} %get-tuple-element.125), channel_id=1, source_target_pairs={{0,8},{1,9},{2,10},{3,11},{4,12},{5,13},{6,14},{7,15},{8,0},{9,1},... | collective-permute-start | bytes 393224 | tf_op jit(solution)/shard_map/ppermute | solution.py:260
  122.1 13.4 %collective-permute-start.28 = (bf16[256,256]{1,0:T(8,128)(2,1)S(1)}, bf16[256,256]{1,0:T(8,128)(2,1)S(1)}, u32[]{:S(2)}, u32[]{:S(2)}) collective-permute-start(bf16[256,256]{1,0:T(8,128)(2,1)S(1)} %get-tuple-element.122), channel_id=1, source_target_pairs={{0,8},{1,9},{2,10},{3,11},{4,12},{5,13},{6,14},{7,15},{8,0},{9,1},... | collective-permute-start | bytes 393224 | tf_op jit(solution)/shard_map/ppermute | solution.py:260
  123.3 12.2 %collective-permute-start.30 = (bf16[256,256]{1,0:T(8,128)(2,1)S(1)}, bf16[256,256]{1,0:T(8,128)(2,1)S(1)}, u32[]{:S(2)}, u32[]{:S(2)}) collective-permute-start(bf16[256,256]{1,0:T(8,128)(2,1)S(1)} %get-tuple-element.123), channel_id=1, source_target_pairs={{0,12},{1,13},{2,14},{3,15},{4,8},{5,9},{6,10},{7,11},{8,4},{9,5},... | collective-permute-start | bytes 393224 | tf_op jit(solution)/shard_map/ppermute | solution.py:260
  125.7 9.8 %collective-permute-start.31 = (bf16[256,256]{1,0:T(8,128)(2,1)S(1)}, bf16[256,256]{1,0:T(8,128)(2,1)S(1)}, u32[]{:S(2)}, u32[]{:S(2)}) collective-permute-start(bf16[256,256]{1,0:T(8,128)(2,1)S(1)} %get-tuple-element.126), channel_id=1, source_target_pairs={{0,12},{1,13},{2,14},{3,15},{4,8},{5,9},{6,10},{7,11},{8,4},{9,5},... | collective-permute-start | bytes 393224 | tf_op jit(solution)/shard_map/ppermute | solution.py:260
  130.8 4.7 %collective-permute-start.27 = (bf16[256,256]{1,0:T(8,128)(2,1)S(1)}, bf16[256,256]{1,0:T(8,128)(2,1)S(1)}, u32[]{:S(2)}, u32[]{:S(2)}) collective-permute-start(bf16[256,256]{1,0:T(8,128)(2,1)S(1)} %get-tuple-element.132), channel_id=1, source_target_pairs={{0,4},{1,5},{2,6},{3,7},{4,0},{5,1},{6,2},{7,3},{8,12},{9,13},{10,... | collective-permute-start | bytes 393224 | tf_op jit(solution)/shard_map/ppermute | solution.py:260
  132.4 3.1 %collective-permute-start.26 = (bf16[256,256]{1,0:T(8,128)(2,1)S(1)}, bf16[256,256]{1,0:T(8,128)(2,1)S(1)}, u32[]{:S(2)}, u32[]{:S(2)}) collective-permute-start(bf16[256,256]{1,0:T(8,128)(2,1)S(1)} %get-tuple-element.129), channel_id=1, source_target_pairs={{0,4},{1,5},{2,6},{3,7},{4,0},{5,1},{6,2},{7,3},{8,12},{9,13},{10,... | collective-permute-start | bytes 393224 | tf_op jit(solution)/shard_map/ppermute | solution.py:260

commit v6 on v5

--- a/solution.py
+++ b/solution.py
@@ -20,7 +20,7 @@
 HBM = pl.BlockSpec(memory_space=pltpu.HBM)
 
 
-def call(body, outs, in_specs, flops=0, scratch=(), out_spec=VMEM, limit=28 << 20):
+def call(body, outs, in_specs, flops=0, scratch=(), out_spec=VMEM, limit=16 << 20):
     return pl.pallas_call(
         body,
         out_shape=outs,
@@ -152,36 +152,25 @@
     outs[-1][...] = whole.astype(jnp.bfloat16)
 
 
-def attend_body(segs, heads, first_head, group, here_ref, gate_ref, base_ref, upper_ref, lower_ref, *refs):
-    kvs, deltas, messages = refs[:MEMBERS], refs[MEMBERS : 2 * MEMBERS], refs[2 * MEMBERS : 3 * MEMBERS]
-    rest = refs[3 * MEMBERS :]
+def local_body(segs, heads, upper_ref, lower_ref, *refs):
     n = len(segs)
-    sums, lasts, outs = rest[:n], rest[n : 2 * n], rest[2 * n :]
-    me = here_ref[1]
-    start, across = (2 + first_head) * HEAD_SIZE, heads * HEAD_SIZE
-    for at, seg in enumerate(segs):
-        queries = sums[at][:, start : start + across]
-        queries += last_piece(lasts[at], upper_ref, lower_ref, start, across)
+    kvs, messages, sums, lasts = refs[:n], refs[n : 2 * n], refs[2 * n : 3 * n], refs[3 * n : 4 * n]
+    outs = refs[4 * n :]
+    start, across = 2 * HEAD_SIZE, heads * HEAD_SIZE
+    for at in range(n):
+        queries = sums[at][:, start:] + last_piece(lasts[at], upper_ref, lower_ref, start, across)
         queries = queries.astype(jnp.bfloat16)
-        length = queries.shape[0]
-        blocks = length // BLK
-        valid, seen = facts_of(messages[seg])
-
-        memory = base_ref[...].astype(jnp.float32)
-        for other in range(MEMBERS):
-            if other != seg:
-                earlier = jnp.where((me ^ other) < (me ^ seg), 1.0, 0.0)
-                memory = memory + earlier * deltas[other][...]
-        mem_high, mem_low = split(memory)
-
+        outs[2 * at][...] = queries
+        blocks = queries.shape[0] // BLK
+        valid, seen = facts_of(messages[at])
         for block in range(blocks):
             span = slice(block * BLK, (block + 1) * BLK)
             stacked = jnp.concatenate(
                 [queries[span, h * HEAD_SIZE : (h + 1) * HEAD_SIZE] for h in range(heads)], axis=0
             )
             width = (block + 1) * BLK
-            keys = kvs[seg][0:width, :HEAD_SIZE]
-            values = kvs[seg][0:width, HEAD_SIZE:]
+            keys = kvs[at][0:width, :HEAD_SIZE]
+            values = kvs[at][0:width, HEAD_SIZE:]
             scores = lax.dot_general(
                 stacked, keys, (((1,), (1,)), ((), ())), preferred_element_type=jnp.float32
             ) * HEAD_SIZE ** (-0.5)
@@ -202,30 +191,45 @@
             total = jnp.maximum(jnp.sum(expo, axis=-1, keepdims=True), 1.0)
             weights = (expo / total).astype(jnp.bfloat16)
             local = jnp.dot(weights, values, preferred_element_type=jnp.float32)
-
-            high, low = split(sigma_plus(stacked.astype(jnp.float32)))
+            for h in range(heads):
+                outs[2 * at + 1][span, h * HEAD_SIZE : (h + 1) * HEAD_SIZE] = local[
+                    h * BLK : (h + 1) * BLK
+                ]
+
+
+def mix_body(segs, heads, here_ref, gate_ref, base_ref, *refs):
+    n = len(segs)
+    deltas, rest = refs[:MEMBERS], refs[MEMBERS:]
+    messages, queries, locals_, outs = rest[:n], rest[n : 2 * n], rest[2 * n : 3 * n], rest[3 * n :]
+    me = here_ref[1]
+    for at, seg in enumerate(segs):
+        memory = base_ref[...].astype(jnp.float32)
+        for other in range(MEMBERS):
+            if other != seg:
+                earlier = jnp.where((me ^ other) < (me ^ seg), 1.0, 0.0)
+                memory = memory + earlier * deltas[other][...]
+        mem_high, mem_low = split(memory)
+        valid, _ = facts_of(messages[at])
+        length = queries[at].shape[0]
+        live = iota((length, HEAD_SIZE), 0) < valid[:, :HEAD_SIZE]
+        for h in range(heads):
+            columns = slice(h * HEAD_SIZE, (h + 1) * HEAD_SIZE)
+            high, low = split(sigma_plus(queries[at][:, columns].astype(jnp.float32)))
             numer = jnp.dot(high, mem_high, preferred_element_type=jnp.float32)
             numer += jnp.dot(high, mem_low, preferred_element_type=jnp.float32)
             numer += jnp.dot(low, mem_high, preferred_element_type=jnp.float32)
             retrieved = numer[:, :HEAD_SIZE] / (numer[:, HEAD_SIZE:] + 1.0)
-            live = iota((BLK, HEAD_SIZE), 0) + block * BLK < valid[:, :HEAD_SIZE]
-            for h in range(heads):
-                part = slice(h * BLK, (h + 1) * BLK)
-                logit = jnp.full((1, HEAD_SIZE), gate_ref[me * group + first_head + h], jnp.float32)
-                gate = 1.0 / (1.0 + jnp.exp(-logit))
-                mixed = gate * retrieved[part] + (1.0 - gate) * local[part]
-                outs[at][span, h * HEAD_SIZE : (h + 1) * HEAD_SIZE] = jnp.where(
-                    live, mixed, 0.0
-                ).astype(jnp.bfloat16)
-
-
-def assemble_body(group, widths, here_ref, *refs):
+            logit = jnp.full((1, HEAD_SIZE), gate_ref[me * heads + h], jnp.float32)
+            gate = 1.0 / (1.0 + jnp.exp(-logit))
+            mixed = gate * retrieved + (1.0 - gate) * locals_[at][:, columns]
+            outs[at][:, columns] = jnp.where(live, mixed, 0.0).astype(jnp.bfloat16)
+
+
+def assemble_body(here_ref, *refs):
     parts, out = refs[:-1], refs[-1]
+    width = parts[0].shape[1]
     for k in range(MEMBERS):
-        at = (here_ref[1] ^ k) * group * HEAD_SIZE
-        for c, width in enumerate(widths):
-            out[:, pl.ds(aligned(at), width)] = parts[len(widths) * k + c][...]
-            at = at + width
+        out[:, pl.ds(aligned((here_ref[1] ^ k) * width), width)] = parts[k][...]
 
 
 def after(array, *others):
@@ -237,7 +241,6 @@
     n_groups = n_seg // MEMBERS
     heads_kv = w_key.shape[1] // HEAD_SIZE
     group = w_query.shape[1] // w_key.shape[1]
-    half = group // 2
     rows = w_query.shape[0]
     length, width = tokens.shape[1], tokens.shape[2]
     assert heads_kv == MEMBERS and length == 2 * BLK
@@ -269,6 +272,7 @@
         [SMEM] * 3 + [HBM] * 3,
         scratch=[pltpu.VMEM((META_ROWS, wide), bf16), pltpu.SemaphoreType.DMA((4 * MEMBERS,))],
         out_spec=ANY,
+        limit=60 << 20,
     )(here, valid_len, block_mask, w_query, w_key, value_weight)
     messages = [packed[0], *[to_member(packed[k], k) for k in (1, 2, 3)]]
 
@@ -339,23 +343,23 @@
         a_last, a_far2 = stage3(a_middle, a_two)
         b_two = jnp.where(inside, b_inner, b_outer)
         b_last, b_far2 = stage3(b_middle, b_two)
-        (
-            a_last, a_far2, a_middle, a_two, a_far1, b_last, b_middle, b_two, b_far1, across, sibling, own
-        ) = locked(
-            a_last, a_far2, a_middle, a_two, a_far1, b_last, b_middle, b_two, b_far1, across, sibling, own
-        )
-        diagonal = to_member(across, 1)
+        a_last, a_far2, a_middle = locked(a_last, a_far2, a_middle)
         a_three = jnp.where(inside, a_middle, a_last)
         a_far3 = over(a_three)
-        b_three = jnp.where(inside, b_middle, b_last)
+        books = [own, sibling]
+        upper = [a, a_one, a_two, a_three, a_far0, a_far1, a_far2, a_far3, a_far3]
+        lower = [b, b_one, b_two, None, b_far0, b_far1]
+        project((0, 1), (0, 1, 4, 5), upper, lower, n_z, True)
+        b_last, b_far2, b_middle, a_far3, across, sums[0], sums[1] = locked(
+            b_last, b_far2, b_middle, a_far3, across, sums[0], sums[1]
+        )
         b_far3 = [
             over(jnp.where(inside, b_middle[:, at], b_last[:, at]))
             for at in (slice(0, cut), slice(cut, None))
         ]
-        books = [own, sibling, across, diagonal]
-        upper = [a, a_one, a_two, a_three, a_far0, a_far1, a_far2, a_far3, a_far3]
-        lower = [b, b_one, b_two, b_three, b_far0, b_far1, b_far2] + b_far3
-        project((0, 1), (0, 1, 4, 5), upper, lower, n_z, True)
+        books += [across, to_member(across, 1)]
+        upper[7:] = [a_far3, a_far3]
+        lower[3:] = [jnp.where(inside, b_middle, b_last), b_far0, b_far1, b_far2] + b_far3
         project((0, 1), (2, 3, 6), upper, lower, n_z, False)
         project((2, 3), (0, 1, 4, 5), upper, lower, n_z, True)
         project((2, 3), (2, 3, 6), upper, lower, n_z, False)
@@ -384,31 +388,37 @@
         term = permute(total, lambda gg, mm, zz: (gg ^ a, mm, zz) if gg < gg ^ a else None)
         base = term if base is None else base.astype(f32) + term.astype(f32)
 
-    sent = {}
-
-    def attend(c, segs, base):
-        attended = call(
-            functools.partial(attend_body, segs, half, c * half, group),
-            [shape((length, half * HEAD_SIZE), bf16)] * len(segs),
-            [SMEM] * 2 + [VMEM] * (3 + 3 * MEMBERS + 2 * len(segs)),
-            flops=2 * len(segs) * length * length * HEAD_SIZE * half * 3,
-        )(
-            here, gate_bias, base, upper[-1], lower[-1], *kvs, *deltas, *messages,
-            *[sums[s] for s in segs], *[lasts[s] for s in segs],
-        )
-        for seg_at, part in zip(segs, attended):
-            sent[c, seg_at] = to_member(part, seg_at) if seg_at else part
-        return attended
-
-    far = attend(0, (2, 3), base)
-    far = attend(1, (2, 3), after(base, *far))
-    near = attend(0, (1, 0), after(base, *far))
-    attend(1, (1, 0), after(base, *near))
+    heads_wide = group * HEAD_SIZE
+
+    def local(segs, piece):
+        found = call(
+            functools.partial(local_body, segs, group),
+            [shape((length, heads_wide), bf16), shape((length, heads_wide), f32)] * len(segs),
+            [VMEM] * (2 + 4 * len(segs)),
+            flops=4 * len(segs) * length * length * heads_wide,
+        )(piece, lower[-1], *[one[s] for one in (kvs, messages, sums, lasts) for s in segs])
+        return found[0::2], found[1::2]
+
+    def mix(segs, base, queries, locals_):
+        return call(
+            functools.partial(mix_body, segs, group),
+            [shape((length, heads_wide), bf16)] * len(segs),
+            [SMEM] * 2 + [VMEM] * (1 + MEMBERS + 3 * len(segs)),
+            flops=0,
+        )(here, gate_bias, base, *deltas, *[messages[s] for s in segs], *queries, *locals_)
+
+    queries, locals_ = local((2, 3), upper[-1])
+    near = local((1, 0), after(upper[-1], *queries))
+    base = after(base, *near[0])
+    (two,) = mix((2,), base, queries[:1], locals_[:1])
+    (three,) = mix((3,), after(base, two), queries[1:], locals_[1:])
+    near = mix((1, 0), after(base, three), *near)
+    sent = [near[1], to_member(near[0], 1), to_member(two, 2), to_member(three, 3)]
     (output,) = call(
-        functools.partial(assemble_body, group, (half * HEAD_SIZE,) * 2),
+        assemble_body,
         [shape((length, w_query.shape[1]), bf16)],
-        [SMEM] + [VMEM] * (2 * MEMBERS),
-    )(here, *[sent[c, k] for k in range(MEMBERS) for c in range(2)])
+        [SMEM] + [VMEM] * MEMBERS,
+    )(here, *sent)
     return output[None]
 
 

time: 138 us -> 153 us (1.11)
  the two profiles are of different devices: /device:TPU:1 before, /device:TPU:0 now
where the time goes in v6:
time: 153 us; the launch traced here: 152 us
  waiting for transfers between devices  55.6 us (36%)
  Pallas kernels  49.9 us (33%)
  starting transfers between devices  39.2 us (26%)
  local copies, waits for them, and re-layouts  3.27 us (2%)
  other arithmetic  2.96 us (2%)
    ppermute x29, waiting for transfers between devices, permute(): return lax.ppermute(array, AXES, pairs)  55.6 us
    ppermute x29, starting transfers between devices, permute(): return lax.ppermute(array, AXES, pairs)  39.2 us
    pallas_call x1, Pallas kernels, shards(): call(functools.partial(pack_body, group), [shape((rows + META_ROWS, wide)...  25.8 us
    pallas_call x4, Pallas kernels, project(): call(functools.partial(project_body, places, line, n_pieces, first), [sha...  13.5 us
    pallas_call x3, Pallas kernels, mix(): call(functools.partial(mix_body, segs, group), [shape((length, heads_wide...  3.93 us
    pallas_call x2, Pallas kernels, local(): call(functools.partial(local_body, segs, group), [shape((length, heads_wi...  3.42 us
  transfers between devices with their start and end apart: 29, of which 14 were waited for; matrix products, arithmetic and copies ran while one was open for 3% of the time, Pallas kernels for 29%

profile of v6, /device:TPU:0, one launch (start us, length us, event | category | flops | bytes accessed | tf_op | source)
XLA Modules:
  0.0 152.1 jit_solution(6106808587937278095)
XLA Ops:
  0.0 0.5 collective-permute-start.3
  1.3 0.7 pad_add_fusion.here_ref
  1.9 25.8 %shard_map.73 = (bf16[144,768]{1,0:T(8,128)(2,1)}, bf16[144,768]{1,0:T(8,128)(2,1)}, bf16[144,768]{1,0:T(8,128)(2,1)}, bf16[144,768]{1,0:T(8,128)(2,1)}) custom-call(s32[3]{0:T(128)} %pad_add_fusion.here_ref, s32[1,1]{1,0:T(1,128)S(6)} %copy.8.valid_ref, s32[1,1,2,2]{3,2,1,0:T(2,128)} %mask_ref.1, bf16[128,2048]{1,0:T(8,128)(2,1)} %wq_ref.1, ...), custom_call_target="tpu_custom_call" | custom-call | bytes 4194304 | tf_op jit(solution)/shard_map/pallas_call | solution.py:269
  27.7 0.1 collective-permute-start
  27.8 2.8 %collective-permute-start.1 = (bf16[144,768]{1,0:T(8,128)(2,1)}, bf16[144,768]{1,0:T(8,128)(2,1)S(1)}, u32[]{:S(2)}, u32[]{:S(2)}) collective-permute-start(bf16[144,768]{1,0:T(8,128)(2,1)} %get-tuple-element.72), channel_id=1, source_target_pairs={{0,8},{1,9},{2,10},{3,11},{4,12},{5,13},{6,14},{7,15},{8,0},{9,1},... | collective-permute-start | bytes 663560 | tf_op jit(solution)/shard_map/ppermute | solution.py:263
  30.6 0.0 collective-permute-start.2
  30.6 0.9 slice.24
  31.6 5.4 %collective-permute-done.1.refs_10_.refs_2_.refs_4_ = bf16[144,768]{1,0:T(8,128)(2,1)S(1)} collective-permute-done((bf16[144,768]{1,0:T(8,128)(2,1)}, bf16[144,768]{1,0:T(8,128)(2,1)S(1)}, u32[]{:S(2)}, u32[]{:S(2)}) %collective-permute-start.1) | collective-permute-done | bytes 221216 | tf_op jit(solution)/shard_map/ppermute | solution.py:263
  37.0 3.8 %collective-permute-done.2.refs_11_.refs_3_.refs_4_ = bf16[144,768]{1,0:T(8,128)(2,1)S(1)} collective-permute-done((bf16[144,768]{1,0:T(8,128)(2,1)}, bf16[144,768]{1,0:T(8,128)(2,1)S(1)}, u32[]{:S(2)}, u32[]{:S(2)}) %collective-permute-start.2) | collective-permute-done | bytes 221216 | tf_op jit(solution)/shard_map/ppermute | solution.py:263
  40.9 1.5 collective-permute-start.14
  42.5 1.4 collective-permute-start.13
  43.9 1.5 collective-permute-start.21
  45.4 3.7 %collective-permute-start.12 = (bf16[256,768]{1,0:T(8,128)(2,1)S(1)}, bf16[256,768]{1,0:T(8,128)(2,1)}, u32[]{:S(2)}, u32[]{:S(2)}) collective-permute-start(bf16[256,768]{1,0:T(8,128)(2,1)S(1)} %pad_maximum_fusion.refs_2_), channel_id=1, source_target_pairs={{0,1},{1,0},{2,3},{3,2},{4,5},{5,4},{6,7},{7,6},{8,9},{9,8},{10,11... | collective-permute-start | bytes 1179656 | tf_op jit(solution)/shard_map/ppermute | solution.py:263
  49.1 0.5 collective-permute-start.6
  49.6 3.3 %collective-permute-done.14.refs_6_ = bf16[256,768]{1,0:T(8,128)(2,1)S(1)} collective-permute-done((bf16[256,768]{1,0:T(8,128)(2,1)S(1)}, bf16[256,768]{1,0:T(8,128)(2,1)S(1)}, u32[]{:S(2)}, u32[]{:S(2)}) %collective-permute-start.14) | collective-permute-done | bytes 393248 | tf_op jit(solution)/shard_map/ppermute | solution.py:263
  52.9 0.8 copy-done.2
  53.7 1.4 collective-permute-start.5
  55.1 3.6 %collective-permute-start.4 = (bf16[256,768]{1,0:T(8,128)(2,1)S(1)}, bf16[256,768]{1,0:T(8,128)(2,1)S(1)}, u32[]{:S(2)}, u32[]{:S(2)}) collective-permute-start(bf16[256,768]{1,0:T(8,128)(2,1)S(1)} %pad_maximum_fusion.1.refs_3_), channel_id=1, source_target_pairs={{0,1},{1,0},{2,3},{3,2},{4,5},{5,4},{6,7},{7,6},{8,9},{9,8},{10,11... | collective-permute-start | bytes 1179656 | tf_op jit(solution)/shard_map/ppermute | solution.py:263
  58.7 1.3 collective-permute-start.16
  60.0 0.8 collective-permute-done.6.refs_7_
  60.8 0.7 copy-done.4
  61.5 1.7 %collective-permute-start.17 = (bf16[256,768]{1,0:T(8,128)(2,1)}, bf16[256,768]{1,0:T(8,128)(2,1)}, u32[]{:S(2)}, u32[]{:S(2)}) collective-permute-start(bf16[256,768]{1,0:T(8,128)(2,1)} %collective-permute-done.12.refs_4_), channel_id=1, source_target_pairs={{0,16},{1,17},{2,18},{3,19},{4,20},{5,21},{6,22},{7,23},{8,24},{9,... | collective-permute-start | bytes 1179656 | tf_op jit(solution)/shard_map/ppermute | solution.py:263
  63.3 1.4 collective-permute-start.15
  64.7 4.1 %collective-permute-done.4.refs_5_ = bf16[256,768]{1,0:T(8,128)(2,1)S(1)} collective-permute-done((bf16[256,768]{1,0:T(8,128)(2,1)S(1)}, bf16[256,768]{1,0:T(8,128)(2,1)S(1)}, u32[]{:S(2)}, u32[]{:S(2)}) %collective-permute-start.4) | collective-permute-done | bytes 393248 | tf_op jit(solution)/shard_map/ppermute | solution.py:263
  68.7 0.7 copy-done.6
  69.5 1.3 collective-permute-start.8
  70.8 0.0 copy-start.7
  70.8 6.5 %collective-permute-done.16 = bf16[256,768]{1,0:T(8,128)(2,1)} collective-permute-done((bf16[256,768]{1,0:T(8,128)(2,1)}, bf16[256,768]{1,0:T(8,128)(2,1)}, u32[]{:S(2)}, u32[]{:S(2)}) %collective-permute-start.16) | collective-permute-done | bytes 393248 | tf_op jit(solution)/shard_map/ppermute | solution.py:263
  77.3 1.5 collective-permute-start.9
  78.8 0.7 collective-permute-start.7
  79.5 1.1 broadcast_select_fusion.2.refs_2_
  80.5 0.6 collective-permute-start.19
  81.1 3.3 %collective-permute-done.8 = bf16[256,768]{1,0:T(8,128)(2,1)} collective-permute-done((bf16[256,768]{1,0:T(8,128)(2,1)}, bf16[256,768]{1,0:T(8,128)(2,1)}, u32[]{:S(2)}, u32[]{:S(2)}) %collective-permute-start.8) | collective-permute-done | bytes 393248 | tf_op jit(solution)/shard_map/ppermute | solution.py:263
  84.4 1.3 collective-permute-start.18
  85.7 3.8 %collective-permute-done.9.refs_9_ = bf16[256,768]{1,0:T(8,128)(2,1)S(1)} collective-permute-done((bf16[256,768]{1,0:T(8,128)(2,1)}, bf16[256,768]{1,0:T(8,128)(2,1)S(1)}, u32[]{:S(2)}, u32[]{:S(2)}) %collective-permute-start.9) | collective-permute-done | bytes 393248 | tf_op jit(solution)/shard_map/ppermute | solution.py:263
  89.5 1.0 broadcast_select_fusion.3.refs_3_
  90.6 1.6 %collective-permute-start.11 = (bf16[256,768]{1,0:T(8,128)(2,1)S(1)}, bf16[256,768]{1,0:T(8,128)(2,1)S(1)}, u32[]{:S(2)}, u32[]{:S(2)}) collective-permute-start(bf16[256,768]{1,0:T(8,128)(2,1)S(1)} %broadcast_select_fusion.3.refs_3_), channel_id=1, source_target_pairs={{0,16},{1,17},{2,18},{3,19},{4,20},{5,21},{6,22},{7,23},{8,24},{9,... | collective-permute-start | bytes 1179656 | tf_op jit(solution)/shard_map/ppermute | solution.py:263
  92.2 1.3 collective-permute-start.10
  93.4 4.5 %collective-permute-done.19.refs_6_ = bf16[256,768]{1,0:T(8,128)(2,1)S(1)} collective-permute-done((bf16[256,768]{1,0:T(8,128)(2,1)S(1)}, bf16[256,768]{1,0:T(8,128)(2,1)S(1)}, u32[]{:S(2)}, u32[]{:S(2)}) %collective-permute-start.19) | collective-permute-done | bytes 393248 | tf_op jit(solution)/shard_map/ppermute | solution.py:263
  97.9 0.6 collective-permute-done.18
  98.5 0.1 broadcast_select_fusion.1.refs_4_
  98.6 1.6 %collective-permute-start.20 = (bf16[256,768]{1,0:T(8,128)(2,1)S(1)}, bf16[256,768]{1,0:T(8,128)(2,1)S(1)}, u32[]{:S(2)}, u32[]{:S(2)}) collective-permute-start(bf16[256,768]{1,0:T(8,128)(2,1)S(1)} %broadcast_select_fusion.1.refs_4_), channel_id=1, source_target_pairs={{0,16},{1,17},{2,18},{3,19},{4,20},{5,21},{6,22},{7,23},{8,24},{9,... | collective-permute-start | bytes 1179656 | tf_op jit(solution)/shard_map/ppermute | solution.py:263
  100.2 3.7 %shard_map.74 = (f32[256,768]{1,0:T(8,128)S(1)}, f32[256,768]{1,0:T(8,128)S(1)}, bf16[256,512]{1,0:T(8,128)(2,1)S(1)}, bf16[256,512]{1,0:T(8,128)(2,1)S(1)}) custom-call(s32[3]{0:T(128)S(1)} %copy-done.8, bf16[256,4096]{1,0:T(8,128)(2,1)S(1)} %bitcast.7, bf16[256,4096]{1,0:T(8,128)(2,1)} %collective-permute-done.3.refs_1_, ...), custom_call_target="tpu_custom_call" | custom-call | flops 1610612736 | bytes 4194304 | tf_op jit(solution)/shard_map/pallas_call | solution.py:302
  103.9 2.5 %collective-permute-done.11.refs_7_ = bf16[256,768]{1,0:T(8,128)(2,1)S(1)} collective-permute-done((bf16[256,768]{1,0:T(8,128)(2,1)S(1)}, bf16[256,768]{1,0:T(8,128)(2,1)S(1)}, u32[]{:S(2)}, u32[]{:S(2)}) %collective-permute-start.11) | collective-permute-done | bytes 393248 | tf_op jit(solution)/shard_map/ppermute | solution.py:263
  106.4 4.9 %collective-permute-done.20.upper_ref = bf16[256,768]{1,0:T(8,128)(2,1)S(1)} collective-permute-done((bf16[256,768]{1,0:T(8,128)(2,1)S(1)}, bf16[256,768]{1,0:T(8,128)(2,1)S(1)}, u32[]{:S(2)}, u32[]{:S(2)}) %collective-permute-start.20) | collective-permute-done | bytes 393248 | tf_op jit(solution)/shard_map/ppermute | solution.py:263
  111.3 1.6 %collective-permute-start.22 = (bf16[256,256]{1,0:T(8,128)(2,1)S(1)}, bf16[256,256]{1,0:T(8,128)(2,1)S(1)}, u32[]{:S(2)}, u32[]{:S(2)}) collective-permute-start(bf16[256,256]{1,0:T(8,128)(2,1)S(1)} %slice_select_fusion.1), channel_id=1, source_target_pairs={{0,16},{1,17},{2,18},{3,19},{4,20},{5,21},{6,22},{7,23},{8,24},{9,... | collective-permute-start | bytes 393224 | tf_op jit(solution)/shard_map/ppermute | solution.py:263
  112.9 0.6 collective-permute-start.25
  113.5 3.0 %shard_map.75 = (f32[256,768]{1,0:T(8,128)S(1)}, f32[256,768]{1,0:T(8,128)S(1)}) custom-call(s32[3]{0:T(128)S(1)} %copy-done.8, bf16[256,4096]{1,0:T(8,128)(2,1)S(1)} %bitcast.8, bf16[256,4096]{1,0:T(8,128)(2,1)} %collective-permute-done.3.refs_1_, bf16[256,768]{1,0:T(8,128)(2,1)S(1)} %broadcast_select_fusion.2.refs_2_, ...), custom_call_target="tpu_custom_call" | custom-call | flops 1207959552 | bytes 4194304 | tf_op jit(solution)/shard_map/pallas_call | solution.py:302
  116.6 3.7 %shard_map.76 = (f32[256,768]{1,0:T(8,128)S(1)}, f32[256,768]{1,0:T(8,128)S(1)}, bf16[256,512]{1,0:T(8,128)(2,1)S(1)}, bf16[256,512]{1,0:T(8,128)(2,1)S(1)}) custom-call(s32[3]{0:T(128)S(1)} %copy-done.8, bf16[256,4096]{1,0:T(8,128)(2,1)} %collective-permute-done.21.refs_0_, bf16[256,4096]{1,0:T(8,128)(2,1)S(1)} %collective-permute-done.23.refs_1_, ...), custom_call_target="tpu_custom_call" | custom-call | flops 1610612736 | bytes 4194304 | tf_op jit(solution)/shard_map/pallas_call | solution.py:302
  120.3 3.1 %shard_map.77 = (f32[256,768]{1,0:T(8,128)S(1)}, f32[256,768]{1,0:T(8,128)S(1)}) custom-call(s32[3]{0:T(128)S(1)} %copy-done.8, bf16[256,4096]{1,0:T(8,128)(2,1)} %collective-permute-done.21.refs_0_, bf16[256,4096]{1,0:T(8,128)(2,1)S(1)} %collective-permute-done.23.refs_1_, bf16[256,768]{1,0:T(8,128)(2,1)S(1)} %broadcast_select_fusion.2.refs_2_, ...), custom_call_target="tpu_custom_call" | custom-call | flops 1207959552 | bytes 4194304 | tf_op jit(solution)/shard_map/pallas_call | solution.py:302
  123.4 1.7 %shard_map.78 = (bf16[256,256]{1,0:T(8,128)(2,1)S(1)}, f32[128,256]{1,0:T(8,128)S(1)}, bf16[256,256]{1,0:T(8,128)(2,1)S(1)}, f32[128,256]{1,0:T(8,128)S(1)}, bf1...) custom-call(bf16[256,768]{1,0:T(8,128)(2,1)S(1)} %collective-permute, ...), custom_call_target="tpu_custom_call" | custom-call | flops 268435456 | bytes 4194304 | tf_op jit(solution)/shard_map/pallas_call | solution.py:377
  125.1 3.6 %collective-permute-start.24 = (bf16[128,256]{1,0:T(8,128)(2,1)S(1)}, bf16[128,256]{1,0:T(8,128)(2,1)S(1)}, u32[]{:S(2)}, u32[]{:S(2)}) collective-permute-start(bf16[128,256]{1,0:T(8,128)(2,1)S(1)} %get-tuple-element.112), channel_id=1, source_target_pairs={{0,16},{1,17},{2,18},{3,19},{4,20},{5,21},{6,22},{7,23},{8,24},{9,... | collective-permute-start | bytes 196616 | tf_op jit(solution)/shard_map/ppermute | solution.py:263
  128.7 1.7 %shard_map.79 = (bf16[256,512]{1,0:T(8,128)(2,1)S(1)}, f32[256,512]{1,0:T(8,128)S(1)}, bf16[256,512]{1,0:T(8,128)(2,1)S(1)}, f32[256,512]{1,0:T(8,128)S(1)}) custom-call(bf16[256,768]{1,0:T(8,128)(2,1)S(1)} %collective-permute-done.20.upper_ref, bf16[256,512]{1,0:T(8,128)(2,1)S(1)} %collective-permute-done.25.lower_ref, ...), custom_call_target="tpu_custom_call" | custom-call | flops 268435456 | bytes 4194304 | tf_op jit(solution)/shard_map/pallas_call | solution.py:394
  130.5 0.0 copy-start.9
  130.5 1.7 %shard_map.80 = (bf16[256,512]{1,0:T(8,128)(2,1)S(1)}, f32[256,512]{1,0:T(8,128)S(1)}, bf16[256,512]{1,0:T(8,128)(2,1)S(1)}, f32[256,512]{1,0:T(8,128)S(1)}) custom-call(bf16[256,768]{1,0:T(8,128)(2,1)S(1)} %collective-permute-done.20.upper_ref, bf16[256,512]{1,0:T(8,128)(2,1)S(1)} %collective-permute-done.25.lower_ref, ...), custom_call_target="tpu_custom_call" | custom-call | flops 268435456 | bytes 4194304 | tf_op jit(solution)/shard_map/pallas_call | solution.py:394
  132.2 1.2 shard_map.81
  133.4 1.2 shard_map.82
  134.6 1.6 %shard_map.83 = (bf16[256,512]{1,0:T(8,128)(2,1)S(1)}, bf16[256,512]{1,0:T(8,128)(2,1)S(1)}) custom-call(s32[3]{0:T(128)S(1)} %copy-done.8, f32[16]{0:T(128)S(1)} %copy-done.9, bf16[128,256]{1,0:T(8,128)(2,1)S(1)} %collective-permute-done.24.base_ref, f32[128,256]{1,0:T(8,128)S(1)} %get-tuple-element.123.refs_0_, f32[128,256]{1,0:T(8,128)S(1)} %get-tuple-element.124.refs_1_, ...), custom_call_target="tpu_custom_call" | custom-call | bytes 4194304 | tf_op jit(solution)/shard_map/pallas_call | solution.py:403
  136.2 0.1 collective-permute-start.26
  136.2 1.6 %collective-permute-start.28 = (bf16[256,512]{1,0:T(8,128)(2,1)S(1)}, bf16[256,512]{1,0:T(8,128)(2,1)S(1)}, u32[]{:S(2)}, u32[]{:S(2)}) collective-permute-start(bf16[256,512]{1,0:T(8,128)(2,1)S(1)} %shard_map.82), channel_id=1, source_target_pairs={{0,12},{1,13},{2,14},{3,15},{4,8},{5,9},{6,10},{7,11},{8,4},{9,5},... | collective-permute-start | bytes 786440 | tf_op jit(solution)/shard_map/ppermute | solution.py:263
  137.8 0.5 collective-permute-start.27
  138.4 6.1 %collective-permute-done.28.refs_3_ = bf16[256,512]{1,0:T(8,128)(2,1)S(1)} collective-permute-done((bf16[256,512]{1,0:T(8,128)(2,1)S(1)}, bf16[256,512]{1,0:T(8,128)(2,1)S(1)}, u32[]{:S(2)}, u32[]{:S(2)}) %collective-permute-start.28) | collective-permute-done | bytes 262176 | tf_op jit(solution)/shard_map/ppermute | solution.py:263
  144.5 6.0 %collective-permute-done.27.refs_2_ = bf16[256,512]{1,0:T(8,128)(2,1)S(1)} collective-permute-done((bf16[256,512]{1,0:T(8,128)(2,1)S(1)}, bf16[256,512]{1,0:T(8,128)(2,1)S(1)}, u32[]{:S(2)}, u32[]{:S(2)}) %collective-permute-start.27) | collective-permute-done | bytes 262176 | tf_op jit(solution)/shard_map/ppermute | solution.py:263
  150.5 1.6 %shard_map.84 = bf16[256,2048]{1,0:T(8,128)(2,1)} custom-call(s32[3]{0:T(128)S(1)} %copy-done.8, bf16[256,512]{1,0:T(8,128)(2,1)S(1)} %get-tuple-element.133.refs_0_, bf16[256,512]{1,0:T(8,128)(2,1)S(1)} %collective-permute-done.26.refs_1_, bf16[256,512]{1,0:T(8,128)(2,1)S(1)} %collective-permute-done.27.refs_2_, ...), custom_call_target="tpu_custom_call" | custom-call | bytes 4194304 | tf_op jit(solution)/shard_map/pallas_call | solution.py:417
  (39 shorter events, 0.3 us)
Async XLA Ops:
  0.0 43.9 %copy-start = (bf16[1,256,4096]{2,1,0:T(8,128)(2,1)S(1)}, bf16[1,256,4096]{2,1,0:T(8,128)(2,1)}, u32[]{:S(2)}) copy-start(bf16[1,256,4096]{2,1,0:T(8,128)(2,1)} %param.7) | copy-start | bytes 6291460
  0.0 40.9 %collective-permute-start.3 = (bf16[256,4096]{1,0:T(8,128)(2,1)}, bf16[256,4096]{1,0:T(8,128)(2,1)}, u32[]{:S(2)}, u32[]{:S(2)}) collective-permute-start(bf16[256,4096]{1,0:T(8,128)(2,1)} %bitcast.5), channel_id=1, source_target_pairs={{0,4},{1,5},{2,6},{3,7},{4,0},{5,1},{6,2},{7,3},{8,12},{9,13},{10,... | collective-permute-start | bytes 6291464 | tf_op jit(solution)/shard_map/ppermute | solution.py:263
  27.7 3.8 %collective-permute-start = (bf16[144,768]{1,0:T(8,128)(2,1)}, bf16[144,768]{1,0:T(8,128)(2,1)S(1)}, u32[]{:S(2)}, u32[]{:S(2)}) collective-permute-start(bf16[144,768]{1,0:T(8,128)(2,1)} %get-tuple-element.71), channel_id=1, source_target_pairs={{0,4},{1,5},{2,6},{3,7},{4,0},{5,1},{6,2},{7,3},{8,12},{9,13},{10,... | collective-permute-start | bytes 663560 | tf_op jit(solution)/shard_map/ppermute | solution.py:263
  27.8 9.2 %collective-permute-start.1 = (bf16[144,768]{1,0:T(8,128)(2,1)}, bf16[144,768]{1,0:T(8,128)(2,1)S(1)}, u32[]{:S(2)}, u32[]{:S(2)}) collective-permute-start(bf16[144,768]{1,0:T(8,128)(2,1)} %get-tuple-element.72), channel_id=1, source_target_pairs={{0,8},{1,9},{2,10},{3,11},{4,12},{5,13},{6,14},{7,15},{8,0},{9,1},... | collective-permute-start | bytes 663560 | tf_op jit(solution)/shard_map/ppermute | solution.py:263
  30.6 10.2 %collective-permute-start.2 = (bf16[144,768]{1,0:T(8,128)(2,1)}, bf16[144,768]{1,0:T(8,128)(2,1)S(1)}, u32[]{:S(2)}, u32[]{:S(2)}) collective-permute-start(bf16[144,768]{1,0:T(8,128)(2,1)} %get-tuple-element.73), channel_id=1, source_target_pairs={{0,12},{1,13},{2,14},{3,15},{4,8},{5,9},{6,10},{7,11},{8,4},{9,5},... | collective-permute-start | bytes 663560 | tf_op jit(solution)/shard_map/ppermute | solution.py:263
  40.9 59.3 %copy-start.8 = (s32[3]{0:T(128)S(1)}, s32[3]{0:T(128)}, u32[]{:S(2)}) copy-start(s32[3]{0:T(128)} %pad_add_fusion.here_ref) | copy-start | bytes 40
  40.9 12.0 %collective-permute-start.14 = (bf16[256,768]{1,0:T(8,128)(2,1)S(1)}, bf16[256,768]{1,0:T(8,128)(2,1)S(1)}, u32[]{:S(2)}, u32[]{:S(2)}) collective-permute-start(bf16[256,768]{1,0:T(8,128)(2,1)S(1)} %pad_maximum_fusion.refs_2_), channel_id=1, source_target_pairs={{0,16},{1,17},{2,18},{3,19},{4,20},{5,21},{6,22},{7,23},{8,24},{9,... | collective-permute-start | bytes 1179656 | tf_op jit(solution)/shard_map/ppermute | solution.py:263
  42.5 12.7 %collective-permute-start.13 = (bf16[256,768]{1,0:T(8,128)(2,1)S(1)}, bf16[256,768]{1,0:T(8,128)(2,1)}, u32[]{:S(2)}, u32[]{:S(2)}) collective-permute-start(bf16[256,768]{1,0:T(8,128)(2,1)S(1)} %pad_maximum_fusion.refs_2_), channel_id=1, source_target_pairs={{1,2},{2,1},{5,6},{6,5},{9,10},{10,9},{13,14},{14,13},{17,18},{18,... | collective-permute-start | bytes 1179656 | tf_op jit(solution)/shard_map/ppermute | solution.py:263
  43.9 67.4 %collective-permute-start.21 = (bf16[256,4096]{1,0:T(8,128)(2,1)S(1)}, bf16[256,4096]{1,0:T(8,128)(2,1)}, u32[]{:S(2)}, u32[]{:S(2)}) collective-permute-start(bf16[256,4096]{1,0:T(8,128)(2,1)S(1)} %bitcast.6), channel_id=1, source_target_pairs={{0,8},{1,9},{2,10},{3,11},{4,12},{5,13},{6,14},{7,15},{8,0},{9,1},... | collective-permute-start | bytes 6291464 | tf_op jit(solution)/shard_map/ppermute | solution.py:263
  45.4 13.4 %collective-permute-start.12 = (bf16[256,768]{1,0:T(8,128)(2,1)S(1)}, bf16[256,768]{1,0:T(8,128)(2,1)}, u32[]{:S(2)}, u32[]{:S(2)}) collective-permute-start(bf16[256,768]{1,0:T(8,128)(2,1)S(1)} %pad_maximum_fusion.refs_2_), channel_id=1, source_target_pairs={{0,1},{1,0},{2,3},{3,2},{4,5},{5,4},{6,7},{7,6},{8,9},{9,8},{10,11... | collective-permute-start | bytes 1179656 | tf_op jit(solution)/shard_map/ppermute | solution.py:263
  49.1 11.7 %collective-permute-start.6 = (bf16[256,768]{1,0:T(8,128)(2,1)S(1)}, bf16[256,768]{1,0:T(8,128)(2,1)S(1)}, u32[]{:S(2)}, u32[]{:S(2)}) collective-permute-start(bf16[256,768]{1,0:T(8,128)(2,1)S(1)} %pad_maximum_fusion.1.refs_3_), channel_id=1, source_target_pairs={{0,16},{1,17},{2,18},{3,19},{4,20},{5,21},{6,22},{7,23},{8,24},{9,... | collective-permute-start | bytes 1179656 | tf_op jit(solution)/shard_map/ppermute | solution.py:263
  52.9 0.8 copy-start.2
  53.7 9.6 %collective-permute-start.5 = (bf16[256,768]{1,0:T(8,128)(2,1)S(1)}, bf16[256,768]{1,0:T(8,128)(2,1)}, u32[]{:S(2)}, u32[]{:S(2)}) collective-permute-start(bf16[256,768]{1,0:T(8,128)(2,1)S(1)} %pad_maximum_fusion.1.refs_3_), channel_id=1, source_target_pairs={{1,2},{2,1},{5,6},{6,5},{9,10},{10,9},{13,14},{14,13},{17,18},{18,... | collective-permute-start | bytes 1179656 | tf_op jit(solution)/shard_map/ppermute | solution.py:263
  55.1 13.6 %collective-permute-start.4 = (bf16[256,768]{1,0:T(8,128)(2,1)S(1)}, bf16[256,768]{1,0:T(8,128)(2,1)S(1)}, u32[]{:S(2)}, u32[]{:S(2)}) collective-permute-start(bf16[256,768]{1,0:T(8,128)(2,1)S(1)} %pad_maximum_fusion.1.refs_3_), channel_id=1, source_target_pairs={{0,1},{1,0},{2,3},{3,2},{4,5},{5,4},{6,7},{7,6},{8,9},{9,8},{10,11... | collective-permute-start | bytes 1179656 | tf_op jit(solution)/shard_map/ppermute | solution.py:263
  58.7 18.5 %collective-permute-start.16 = (bf16[256,768]{1,0:T(8,128)(2,1)}, bf16[256,768]{1,0:T(8,128)(2,1)}, u32[]{:S(2)}, u32[]{:S(2)}) collective-permute-start(bf16[256,768]{1,0:T(8,128)(2,1)} %collective-permute-done.13), channel_id=1, source_target_pairs={{1,0},{2,3},{5,4},{6,7},{9,8},{10,11},{13,12},{14,15},{17,16},{18,... | collective-permute-start | bytes 1179656 | tf_op jit(solution)/shard_map/ppermute | solution.py:263
  60.8 0.7 copy-start.4
  61.5 17.3 %collective-permute-start.17 = (bf16[256,768]{1,0:T(8,128)(2,1)}, bf16[256,768]{1,0:T(8,128)(2,1)}, u32[]{:S(2)}, u32[]{:S(2)}) collective-permute-start(bf16[256,768]{1,0:T(8,128)(2,1)} %collective-permute-done.12.refs_4_), channel_id=1, source_target_pairs={{0,16},{1,17},{2,18},{3,19},{4,20},{5,21},{6,22},{7,23},{8,24},{9,... | collective-permute-start | bytes 1179656 | tf_op jit(solution)/shard_map/ppermute | solution.py:263
  63.3 16.2 %collective-permute-start.15 = (bf16[256,768]{1,0:T(8,128)(2,1)}, bf16[256,768]{1,0:T(8,128)(2,1)}, u32[]{:S(2)}, u32[]{:S(2)}) collective-permute-start(bf16[256,768]{1,0:T(8,128)(2,1)} %collective-permute-done.12.refs_4_), channel_id=1, source_target_pairs={{1,2},{2,1},{5,6},{6,5},{9,10},{10,9},{13,14},{14,13},{17,18},{18,... | collective-permute-start | bytes 1179656 | tf_op jit(solution)/shard_map/ppermute | solution.py:263
  68.7 0.7 copy-start.6
  69.5 14.9 %collective-permute-start.8 = (bf16[256,768]{1,0:T(8,128)(2,1)}, bf16[256,768]{1,0:T(8,128)(2,1)}, u32[]{:S(2)}, u32[]{:S(2)}) collective-permute-start(bf16[256,768]{1,0:T(8,128)(2,1)} %collective-permute-done.5), channel_id=1, source_target_pairs={{1,0},{2,3},{5,4},{6,7},{9,8},{10,11},{13,12},{14,15},{17,16},{18,... | collective-permute-start | bytes 1179656 | tf_op jit(solution)/shard_map/ppermute | solution.py:263
  70.8 29.4 %copy-start.3 = (bf16[256,768]{1,0:T(8,128)(2,1)S(1)}, bf16[256,768]{1,0:T(8,128)(2,1)}, u32[]{:S(2)}) copy-start(bf16[256,768]{1,0:T(8,128)(2,1)} %copy-done.2) | copy-start | bytes 1179652
  70.8 29.4 %copy-start.5 = (bf16[256,768]{1,0:T(8,128)(2,1)S(1)}, bf16[256,768]{1,0:T(8,128)(2,1)}, u32[]{:S(2)}) copy-start(bf16[256,768]{1,0:T(8,128)(2,1)} %copy-done.4) | copy-start | bytes 1179652
  70.8 29.4 %copy-start.7 = (bf16[256,768]{1,0:T(8,128)(2,1)S(1)}, bf16[256,768]{1,0:T(8,128)(2,1)}, u32[]{:S(2)}) copy-start(bf16[256,768]{1,0:T(8,128)(2,1)} %copy-done.6) | copy-start | bytes 1179652
  77.3 12.3 %collective-permute-start.9 = (bf16[256,768]{1,0:T(8,128)(2,1)}, bf16[256,768]{1,0:T(8,128)(2,1)S(1)}, u32[]{:S(2)}, u32[]{:S(2)}) collective-permute-start(bf16[256,768]{1,0:T(8,128)(2,1)} %copy-done.6), channel_id=1, source_target_pairs={{0,16},{1,17},{2,18},{3,19},{4,20},{5,21},{6,22},{7,23},{8,24},{9,... | collective-permute-start | bytes 1179656 | tf_op jit(solution)/shard_map/ppermute | solution.py:263
  78.8 10.7 %collective-permute-start.7 = (bf16[256,768]{1,0:T(8,128)(2,1)}, bf16[256,768]{1,0:T(8,128)(2,1)S(1)}, u32[]{:S(2)}, u32[]{:S(2)}) collective-permute-start(bf16[256,768]{1,0:T(8,128)(2,1)} %copy-done.6), channel_id=1, source_target_pairs={{1,2},{2,1},{5,6},{6,5},{9,10},{10,9},{13,14},{14,13},{17,18},{18,... | collective-permute-start | bytes 1179656 | tf_op jit(solution)/shard_map/ppermute | solution.py:263
  80.5 17.4 %collective-permute-start.19 = (bf16[256,768]{1,0:T(8,128)(2,1)S(1)}, bf16[256,768]{1,0:T(8,128)(2,1)S(1)}, u32[]{:S(2)}, u32[]{:S(2)}) collective-permute-start(bf16[256,768]{1,0:T(8,128)(2,1)S(1)} %broadcast_select_fusion.2.refs_2_), channel_id=1, source_target_pairs={{0,16},{1,17},{2,18},{3,19},{4,20},{5,21},{6,22},{7,23},{8,24},{9,... | collective-permute-start | bytes 1179656 | tf_op jit(solution)/shard_map/ppermute | solution.py:263
  84.4 14.1 %collective-permute-start.18 = (bf16[256,768]{1,0:T(8,128)(2,1)}, bf16[256,768]{1,0:T(8,128)(2,1)S(1)}, u32[]{:S(2)}, u32[]{:S(2)}) collective-permute-start(bf16[256,768]{1,0:T(8,128)(2,1)} %collective-permute-done.15), channel_id=1, source_target_pairs={{1,0},{2,3},{5,4},{6,7},{9,8},{10,11},{13,12},{14,15},{17,16},{18,... | collective-permute-start | bytes 1179656 | tf_op jit(solution)/shard_map/ppermute | solution.py:263
  90.6 15.8 %collective-permute-start.11 = (bf16[256,768]{1,0:T(8,128)(2,1)S(1)}, bf16[256,768]{1,0:T(8,128)(2,1)S(1)}, u32[]{:S(2)}, u32[]{:S(2)}) collective-permute-start(bf16[256,768]{1,0:T(8,128)(2,1)S(1)} %broadcast_select_fusion.3.refs_3_), channel_id=1, source_target_pairs={{0,16},{1,17},{2,18},{3,19},{4,20},{5,21},{6,22},{7,23},{8,24},{9,... | collective-permute-start | bytes 1179656 | tf_op jit(solution)/shard_map/ppermute | solution.py:263
  92.2 14.2 %collective-permute-start.10 = (bf16[256,768]{1,0:T(8,128)(2,1)S(1)}, bf16[256,768]{1,0:T(8,128)(2,1)S(1)}, u32[]{:S(2)}, u32[]{:S(2)}) collective-permute-start(bf16[256,768]{1,0:T(8,128)(2,1)S(1)} %collective-permute-done.7), channel_id=1, source_target_pairs={{1,0},{2,3},{5,4},{6,7},{9,8},{10,11},{13,12},{14,15},{17,16},{18,... | collective-permute-start | bytes 1179656 | tf_op jit(solution)/shard_map/ppermute | solution.py:263
  98.6 12.7 %collective-permute-start.20 = (bf16[256,768]{1,0:T(8,128)(2,1)S(1)}, bf16[256,768]{1,0:T(8,128)(2,1)S(1)}, u32[]{:S(2)}, u32[]{:S(2)}) collective-permute-start(bf16[256,768]{1,0:T(8,128)(2,1)S(1)} %broadcast_select_fusion.1.refs_4_), channel_id=1, source_target_pairs={{0,16},{1,17},{2,18},{3,19},{4,20},{5,21},{6,22},{7,23},{8,24},{9,... | collective-permute-start | bytes 1179656 | tf_op jit(solution)/shard_map/ppermute | solution.py:263
  111.3 5.3 %collective-permute-start.23 = (bf16[256,4096]{1,0:T(8,128)(2,1)}, bf16[256,4096]{1,0:T(8,128)(2,1)S(1)}, u32[]{:S(2)}, u32[]{:S(2)}) collective-permute-start(bf16[256,4096]{1,0:T(8,128)(2,1)} %collective-permute-done.21.refs_0_), channel_id=1, source_target_pairs={{0,4},{1,5},{2,6},{3,7},{4,0},{5,1},{6,2},{7,3},{8,12},{9,13},{10,... | collective-permute-start | bytes 6291464 | tf_op jit(solution)/shard_map/ppermute | solution.py:263
  111.3 12.1 %collective-permute-start.22 = (bf16[256,256]{1,0:T(8,128)(2,1)S(1)}, bf16[256,256]{1,0:T(8,128)(2,1)S(1)}, u32[]{:S(2)}, u32[]{:S(2)}) collective-permute-start(bf16[256,256]{1,0:T(8,128)(2,1)S(1)} %slice_select_fusion.1), channel_id=1, source_target_pairs={{0,16},{1,17},{2,18},{3,19},{4,20},{5,21},{6,22},{7,23},{8,24},{9,... | collective-permute-start | bytes 393224 | tf_op jit(solution)/shard_map/ppermute | solution.py:263
  112.9 15.8 %collective-permute-start.25 = (bf16[256,512]{1,0:T(8,128)(2,1)S(1)}, bf16[256,512]{1,0:T(8,128)(2,1)S(1)}, u32[]{:S(2)}, u32[]{:S(2)}) collective-permute-start(bf16[256,512]{1,0:T(8,128)(2,1)S(1)} %slice_select_fusion), channel_id=1, source_target_pairs={{0,16},{1,17},{2,18},{3,19},{4,20},{5,21},{6,22},{7,23},{8,24},{9,... | collective-permute-start | bytes 786440 | tf_op jit(solution)/shard_map/ppermute | solution.py:263
  120.3 3.1 %copy-start.1 = (bf16[144,768]{1,0:T(8,128)(2,1)S(1)}, bf16[144,768]{1,0:T(8,128)(2,1)}, u32[]{:S(2)}) copy-start(bf16[144,768]{1,0:T(8,128)(2,1)} %get-tuple-element.70.refs_8_.refs_3_.refs_5_) | copy-start | bytes 663556
  125.1 7.1 %collective-permute-start.24 = (bf16[128,256]{1,0:T(8,128)(2,1)S(1)}, bf16[128,256]{1,0:T(8,128)(2,1)S(1)}, u32[]{:S(2)}, u32[]{:S(2)}) collective-permute-start(bf16[128,256]{1,0:T(8,128)(2,1)S(1)} %get-tuple-element.112), channel_id=1, source_target_pairs={{0,16},{1,17},{2,18},{3,19},{4,20},{5,21},{6,22},{7,23},{8,24},{9,... | collective-permute-start | bytes 196616 | tf_op jit(solution)/shard_map/ppermute | solution.py:263
  130.5 1.7 %copy-start.9 = (f32[16]{0:T(128)S(1)}, f32[16]{0:T(128)}, u32[]{:S(2)}) copy-start(f32[16]{0:T(128)} %gate_ref.5) | copy-start | bytes 196
  136.2 2.2 %collective-permute-start.26 = (bf16[256,512]{1,0:T(8,128)(2,1)S(1)}, bf16[256,512]{1,0:T(8,128)(2,1)S(1)}, u32[]{:S(2)}, u32[]{:S(2)}) collective-permute-start(bf16[256,512]{1,0:T(8,128)(2,1)S(1)} %get-tuple-element.134), channel_id=1, source_target_pairs={{0,4},{1,5},{2,6},{3,7},{4,0},{5,1},{6,2},{7,3},{8,12},{9,13},{10,... | collective-permute-start | bytes 786440 | tf_op jit(solution)/shard_map/ppermute | solution.py:263
  136.2 8.2 %collective-permute-start.28 = (bf16[256,512]{1,0:T(8,128)(2,1)S(1)}, bf16[256,512]{1,0:T(8,128)(2,1)S(1)}, u32[]{:S(2)}, u32[]{:S(2)}) collective-permute-start(bf16[256,512]{1,0:T(8,128)(2,1)S(1)} %shard_map.82), channel_id=1, source_target_pairs={{0,12},{1,13},{2,14},{3,15},{4,8},{5,9},{6,10},{7,11},{8,4},{9,5},... | collective-permute-start | bytes 786440 | tf_op jit(solution)/shard_map/ppermute | solution.py:263
  137.8 12.7 %collective-permute-start.27 = (bf16[256,512]{1,0:T(8,128)(2,1)S(1)}, bf16[256,512]{1,0:T(8,128)(2,1)S(1)}, u32[]{:S(2)}, u32[]{:S(2)}) collective-permute-start(bf16[256,512]{1,0:T(8,128)(2,1)S(1)} %shard_map.81), channel_id=1, source_target_pairs={{0,8},{1,9},{2,10},{3,11},{4,12},{5,13},{6,14},{7,15},{8,0},{9,1},... | collective-permute-start | bytes 786440 | tf_op jit(solution)/shard_map/ppermute | solution.py:263

commit v7 on v5

--- a/solution.py
+++ b/solution.py
@@ -20,7 +20,7 @@
 HBM = pl.BlockSpec(memory_space=pltpu.HBM)
 
 
-def call(body, outs, in_specs, flops=0, scratch=(), out_spec=VMEM, limit=28 << 20):
+def call(body, outs, in_specs, flops=0, scratch=(), out_spec=VMEM, limit=16 << 20):
     return pl.pallas_call(
         body,
         out_shape=outs,
@@ -36,35 +36,23 @@
     return pl.multiple_of(offset, HEAD_SIZE)
 
 
-def pack_body(group, here_ref, valid_ref, mask_ref, wq_ref, wk_ref, wv_ref, *refs):
-    outs, facts_ref, sems = refs[:MEMBERS], refs[-2], refs[-1]
-    rows = wk_ref.shape[0]
-    row = lax.broadcasted_iota(jnp.int32, facts_ref.shape, 0)
+def pack_body(group, here_ref, valid_ref, mask_ref, wq_ref, wk_ref, wv_ref, *outs):
+    rows, wide = wk_ref.shape[0], group * HEAD_SIZE
+    row = lax.broadcasted_iota(jnp.int32, (META_ROWS, outs[0].shape[1]), 0)
     facts = jnp.where(row < HALF, valid_ref[0, 0], mask_ref[0, 0, 1, 0])
-    facts_ref[...] = facts.astype(jnp.float32).astype(jnp.bfloat16)
-    copies = []
-
-    def copy(source, target):
-        copies.append(pltpu.make_async_copy(source, target, sems.at[len(copies)]))
-        copies[-1].start()
-
-    for k in (2, 3, 1, 0):
+    facts = facts.astype(jnp.float32).astype(jnp.bfloat16)
+    for k in range(MEMBERS):
         head, out = here_ref[1] ^ k, outs[k]
         at = aligned(head * HEAD_SIZE)
-        top = pl.ds(0, rows)
-        copy(wk_ref.at[:, pl.ds(at, HEAD_SIZE)], out.at[top, pl.ds(0, HEAD_SIZE)])
-        copy(wv_ref.at[:, pl.ds(at, HEAD_SIZE)], out.at[top, pl.ds(HEAD_SIZE, HEAD_SIZE)])
-        wide = group * HEAD_SIZE
-        copy(wq_ref.at[:, pl.ds(aligned(head * wide), wide)], out.at[top, pl.ds(2 * HEAD_SIZE, wide)])
-        copy(facts_ref, out.at[pl.ds(rows, META_ROWS), :])
-    for one in copies:
-        one.wait()
-
-
-def columns_of(tokens_ref, here_ref, piece, members, line):
+        out[:rows, :HEAD_SIZE] = wk_ref[:, pl.ds(at, HEAD_SIZE)]
+        out[:rows, HEAD_SIZE : 2 * HEAD_SIZE] = wv_ref[:, pl.ds(at, HEAD_SIZE)]
+        out[:rows, 2 * HEAD_SIZE :] = wq_ref[:, pl.ds(aligned(head * wide), wide)]
+        out[rows:, :] = facts
+
+
+def spans_of(here_ref, piece, line):
     if not line:
-        first = (piece * MEMBERS + members[0]) * HEAD_SIZE
-        return tokens_ref[:, pl.ds(first, len(members) * HEAD_SIZE)]
+        return [(piece * MEMBERS * HEAD_SIZE, MEMBERS * HEAD_SIZE)]
     g, m, z = here_ref[0] ^ (piece // line), here_ref[1], here_ref[2]
     inside = (z == 1) | (z == 2)
     step = piece % line
@@ -72,11 +60,9 @@
         z = z ^ step
     else:
         z = jnp.where(inside, z ^ (5 - step), z ^ step)
-    parts = [
-        tokens_ref[:, pl.ds(aligned(((g * MEMBERS + (m ^ k)) * line + z) * HEAD_SIZE), HEAD_SIZE)]
-        for k in members
+    return [
+        (aligned(((g * MEMBERS + (m ^ k)) * line + z) * HEAD_SIZE), HEAD_SIZE) for k in range(MEMBERS)
     ]
-    return jnp.concatenate(parts, axis=1)
 
 
 def facts_of(message_ref):
@@ -91,22 +77,50 @@
 
 def project_body(places, line, n_pieces, first, here_ref, *refs):
     tokens, pieces = refs[:2], refs[2 : 2 + 2 * len(places)]
-    rest = refs[2 + 2 * len(places) :]
+    rest = refs[2 + 2 * len(places) : -2]
+    columns_ref, sems = refs[-2:]
     length = tokens[0].shape[0]
+    deep = MEMBERS * HEAD_SIZE
+    outs = rest if first else rest[2:]
+    copies = []
+
+    def bring(n, piece, target, rows, at):
+        for start, width in spans_of(here_ref, piece, line):
+            one = pltpu.make_async_copy(
+                tokens[n].at[:, pl.ds(start, width)],
+                target.at[rows, pl.ds(at, width)],
+                sems.at[len(copies)],
+            )
+            one.start()
+            copies.append(one)
+            at += width
+
+    marks = []
+    for p, place in enumerate(places):
+        for n in range(2):
+            bring(n, place, columns_ref, pl.ds(n * length, length), p * deep)
+        marks.append(len(copies))
+    if first:
+        for n in range(2):
+            bring(n, n_pieces - 1, outs[2 + n], pl.ds(0, length), 0)
     total = None if first else jnp.concatenate([rest[0][...], rest[1][...]], axis=0)
-    outs = rest if first else rest[2:]
-    for half in range(2):
-        members = (0, 1) if half == 0 else (2, 3)
-        for n, place in enumerate(places):
-            columns = jnp.concatenate(
-                [columns_of(one, here_ref, place, members, line) for one in tokens], axis=0
+    done = 0
+    for p in range(len(places)):
+        for one in copies[done : marks[p]]:
+            one.wait()
+        done = marks[p]
+        for half in range(2):
+            at = p * deep + half * deep // 2
+            term = jnp.dot(
+                columns_ref[:, at : at + deep // 2],
+                pieces[2 * p + half][...],
+                preferred_element_type=jnp.float32,
             )
-            term = jnp.dot(columns, pieces[2 * n + half][...], preferred_element_type=jnp.float32)
             total = term if total is None else total + term
     for n in range(2):
         outs[n][...] = total[n * length : (n + 1) * length]
-        if first:
-            outs[2 + n][...] = columns_of(tokens[n], here_ref, n_pieces - 1, range(MEMBERS), line)
+    for one in copies[done:]:
+        one.wait()
 
 
 def sigma_plus(v):
@@ -118,12 +132,12 @@
     return high, (values - high.astype(jnp.float32)).astype(jnp.bfloat16)
 
 
-def last_piece(columns_ref, upper_ref, lower_ref, start, width):
-    half = upper_ref.shape[0]
-    at = slice(start, start + width)
-    lost = 2 * HEAD_SIZE if start else 0
-    term = jnp.dot(columns_ref[:, :half], upper_ref[:, at], preferred_element_type=jnp.float32)
-    return term + jnp.dot(columns_ref[:, half:], lower_ref[:, start - lost : start - lost + width], preferred_element_type=jnp.float32)
+def last_piece(columns_ref, upper_ref, lower_ref, start):
+    half, width = upper_ref.shape[0], lower_ref.shape[1]
+    term = jnp.dot(
+        columns_ref[:, :half], upper_ref[:, start : start + width], preferred_element_type=jnp.float32
+    )
+    return term + jnp.dot(columns_ref[:, half:], lower_ref[...], preferred_element_type=jnp.float32)
 
 
 def kv_body(upper_ref, lower_ref, *refs):
@@ -132,7 +146,7 @@
     whole = None
     for seg in range(MEMBERS):
         at = 2 * HEAD_SIZE
-        total = sums[seg][:, :at] + last_piece(lasts[seg], upper_ref, lower_ref, 0, at)
+        total = sums[seg][:, :at] + last_piece(lasts[seg], upper_ref, lower_ref, 0)
         kv = total.astype(jnp.bfloat16)
         outs[2 * seg][...] = kv
         length = kv.shape[0]
@@ -152,20 +166,25 @@
     outs[-1][...] = whole.astype(jnp.bfloat16)
 
 
-def attend_body(segs, heads, first_head, group, here_ref, gate_ref, base_ref, upper_ref, lower_ref, *refs):
-    kvs, deltas, messages = refs[:MEMBERS], refs[MEMBERS : 2 * MEMBERS], refs[2 * MEMBERS : 3 * MEMBERS]
-    rest = refs[3 * MEMBERS :]
+def attend_body(
+    segs, parts, heads, here_ref, gate_ref, base_ref, upper_ref, *refs
+):
     n = len(segs)
-    sums, lasts, outs = rest[:n], rest[n : 2 * n], rest[2 * n :]
+    lowers, refs = refs[: len(parts)], refs[len(parts) :]
+    deltas, refs = refs[:MEMBERS], refs[MEMBERS:]
+    kvs, messages, sums, lasts, outs = [refs[k * n : (k + 1) * n] for k in range(5)]
+    all_heads = upper_ref.shape[1] // HEAD_SIZE - 2
     me = here_ref[1]
-    start, across = (2 + first_head) * HEAD_SIZE, heads * HEAD_SIZE
+    across = len(parts) * heads * HEAD_SIZE
+    first = 2 * HEAD_SIZE + parts[0] * heads * HEAD_SIZE
+    heads = len(parts) * heads
+    first_head = first // HEAD_SIZE - 2
     for at, seg in enumerate(segs):
-        queries = sums[at][:, start : start + across]
-        queries += last_piece(lasts[at], upper_ref, lower_ref, start, across)
+        terms = []
+        for p, lower_ref in enumerate(lowers):
+            terms.append(last_piece(lasts[at], upper_ref, lower_ref, first + p * lower_ref.shape[1]))
+        queries = sums[at][:, first : first + across] + jnp.concatenate(terms, axis=1)
         queries = queries.astype(jnp.bfloat16)
-        length = queries.shape[0]
-        blocks = length // BLK
-        valid, seen = facts_of(messages[seg])
 
         memory = base_ref[...].astype(jnp.float32)
         for other in range(MEMBERS):
@@ -173,15 +192,16 @@
                 earlier = jnp.where((me ^ other) < (me ^ seg), 1.0, 0.0)
                 memory = memory + earlier * deltas[other][...]
         mem_high, mem_low = split(memory)
-
+        blocks = queries.shape[0] // BLK
+        valid, seen = facts_of(messages[at])
         for block in range(blocks):
             span = slice(block * BLK, (block + 1) * BLK)
             stacked = jnp.concatenate(
                 [queries[span, h * HEAD_SIZE : (h + 1) * HEAD_SIZE] for h in range(heads)], axis=0
             )
             width = (block + 1) * BLK
-            keys = kvs[seg][0:width, :HEAD_SIZE]
-            values = kvs[seg][0:width, HEAD_SIZE:]
+            keys = kvs[at][0:width, :HEAD_SIZE]
+            values = kvs[at][0:width, HEAD_SIZE:]
             scores = lax.dot_general(
                 stacked, keys, (((1,), (1,)), ((), ())), preferred_element_type=jnp.float32
             ) * HEAD_SIZE ** (-0.5)
@@ -211,7 +231,7 @@
             live = iota((BLK, HEAD_SIZE), 0) + block * BLK < valid[:, :HEAD_SIZE]
             for h in range(heads):
                 part = slice(h * BLK, (h + 1) * BLK)
-                logit = jnp.full((1, HEAD_SIZE), gate_ref[me * group + first_head + h], jnp.float32)
+                logit = jnp.full((1, HEAD_SIZE), gate_ref[me * all_heads + first_head + h], jnp.float32)
                 gate = 1.0 / (1.0 + jnp.exp(-logit))
                 mixed = gate * retrieved[part] + (1.0 - gate) * local[part]
                 outs[at][span, h * HEAD_SIZE : (h + 1) * HEAD_SIZE] = jnp.where(
@@ -219,13 +239,13 @@
                 ).astype(jnp.bfloat16)
 
 
-def assemble_body(group, widths, here_ref, *refs):
-    parts, out = refs[:-1], refs[-1]
-    for k in range(MEMBERS):
-        at = (here_ref[1] ^ k) * group * HEAD_SIZE
-        for c, width in enumerate(widths):
-            out[:, pl.ds(aligned(at), width)] = parts[len(widths) * k + c][...]
-            at = at + width
+def assemble_body(counts, here_ref, *refs):
+    parts, out = list(refs[:-1]), refs[-1]
+    width = out.shape[1] // MEMBERS
+    for k, count in enumerate(counts):
+        for c in range(count):
+            at = (here_ref[1] ^ k) * width + c * (width // count)
+            out[:, pl.ds(aligned(at), width // count)] = parts.pop(0)[...]
 
 
 def after(array, *others):
@@ -237,10 +257,9 @@
     n_groups = n_seg // MEMBERS
     heads_kv = w_key.shape[1] // HEAD_SIZE
     group = w_query.shape[1] // w_key.shape[1]
-    half = group // 2
     rows = w_query.shape[0]
     length, width = tokens.shape[1], tokens.shape[2]
-    assert heads_kv == MEMBERS and length == 2 * BLK
+    assert heads_kv == MEMBERS and group == 4 and length == 2 * BLK
     seg = lax.axis_index("seg")
     z = lax.axis_index("fsdp")
     g, m = seg // MEMBERS, seg % MEMBERS
@@ -266,9 +285,7 @@
     packed = call(
         functools.partial(pack_body, group),
         [shape((rows + META_ROWS, wide), bf16)] * MEMBERS,
-        [SMEM] * 3 + [HBM] * 3,
-        scratch=[pltpu.VMEM((META_ROWS, wide), bf16), pltpu.SemaphoreType.DMA((4 * MEMBERS,))],
-        out_spec=ANY,
+        [SMEM] * 3 + [VMEM] * 3,
     )(here, valid_len, block_mask, w_query, w_key, value_weight)
     messages = [packed[0], *[to_member(packed[k], k) for k in (1, 2, 3)]]
 
@@ -299,8 +316,12 @@
             functools.partial(project_body, places, line, n_pieces, first),
             [shape((length, wide), f32)] * 2
             + [shape((length, MEMBERS * HEAD_SIZE), bf16)] * (2 if first else 0),
-            [SMEM] + [VMEM] * (2 + 2 * len(places) + (0 if first else 2)),
+            [SMEM] + [ANY] * 2 + [VMEM] * (2 * len(places) + (0 if first else 2)),
             flops=2 * 2 * length * len(places) * MEMBERS * HEAD_SIZE * wide,
+            scratch=[
+                pltpu.VMEM((2 * length, len(places) * MEMBERS * HEAD_SIZE), bf16),
+                pltpu.SemaphoreType.DMA((2 * MEMBERS * (len(places) + 1),)),
+            ],
         )(
             here,
             *[books[s] for s in segs],
@@ -312,7 +333,6 @@
             if first:
                 lasts[s] = found[2 + at]
 
-    cut = 2 * HEAD_SIZE
     if n_groups == 2 and n_z == 4:
         assert rows == HEAD_SIZE
         inside = (z == 1) | (z == 2)
@@ -339,25 +359,22 @@
         a_last, a_far2 = stage3(a_middle, a_two)
         b_two = jnp.where(inside, b_inner, b_outer)
         b_last, b_far2 = stage3(b_middle, b_two)
-        (
-            a_last, a_far2, a_middle, a_two, a_far1, b_last, b_middle, b_two, b_far1, across, sibling, own
-        ) = locked(
-            a_last, a_far2, a_middle, a_two, a_far1, b_last, b_middle, b_two, b_far1, across, sibling, own
-        )
-        diagonal = to_member(across, 1)
+        a_last, a_far2, a_middle, across, b_middle, b_two, b_far1 = locked(
+            a_last, a_far2, a_middle, across, b_middle, b_two, b_far1
+        )
         a_three = jnp.where(inside, a_middle, a_last)
         a_far3 = over(a_three)
+        books = [own, sibling, across, to_member(across, 1)]
+        upper = [a, a_one, a_two, a_three, a_far0, a_far1, a_far2, a_far3]
+        lower = [b, b_one, b_two, None, b_far0, b_far1]
+        project((0, 1), (0, 1, 4, 5), upper, lower, n_z, True)
+        project((2, 3), (0, 1, 4, 5), upper, lower, n_z, True)
+        b_last, b_far2, b_middle, a_far3, *sums = locked(b_last, b_far2, b_middle, a_far3, *sums)
         b_three = jnp.where(inside, b_middle, b_last)
-        b_far3 = [
-            over(jnp.where(inside, b_middle[:, at], b_last[:, at]))
-            for at in (slice(0, cut), slice(cut, None))
-        ]
-        books = [own, sibling, across, diagonal]
-        upper = [a, a_one, a_two, a_three, a_far0, a_far1, a_far2, a_far3, a_far3]
-        lower = [b, b_one, b_two, b_three, b_far0, b_far1, b_far2] + b_far3
-        project((0, 1), (0, 1, 4, 5), upper, lower, n_z, True)
+        upper[7] = a_far3
+        lower[3:] = [b_three, b_far0, b_far1, b_far2]
+        finish = lambda at, *others: over(after(b_three[:, at], *others))
         project((0, 1), (2, 3, 6), upper, lower, n_z, False)
-        project((2, 3), (0, 1, 4, 5), upper, lower, n_z, True)
         project((2, 3), (2, 3, 6), upper, lower, n_z, False)
     else:
         across, sibling = to_member(tokens[0], 2), to_member(tokens[0], 1)
@@ -365,18 +382,19 @@
         full = gathered(jnp.concatenate(pieces, axis=0))
         deep = MEMBERS * HEAD_SIZE // 2
         upper, lower = [part[:deep] for part in full], [part[deep:] for part in full]
-        upper.append(upper[-1])
-        lower[-1:] = [lower[-1][:, :cut], lower[-1][:, cut:]]
+        finish = lambda at, *others: lower[n_pieces - 1][:, at]
         for segs in ((0, 1), (2, 3)):
             project(segs, tuple(range(n_pieces - 1)), upper, lower, 0, True)
 
+    halves = [slice(k * HEAD_SIZE, (k + 2) * HEAD_SIZE) for k in (0, 2, 4)]
+    lower_kv, lower_q0 = finish(halves[0]), finish(halves[1])
     found = call(
         kv_body,
         [shape((length, 2 * HEAD_SIZE), bf16), shape((HEAD_SIZE, 2 * HEAD_SIZE), f32)] * MEMBERS
         + [shape((HEAD_SIZE, 2 * HEAD_SIZE), bf16)],
         [VMEM] * (2 + 3 * MEMBERS),
         flops=2 * MEMBERS * length * MEMBERS * HEAD_SIZE * 2 * HEAD_SIZE,
-    )(upper[-2], lower[-2], *sums, *lasts, *messages)
+    )(upper[-1], lower_kv, *sums, *lasts, *messages)
     kvs, deltas, total = found[0:-1:2], found[1:-1:2], found[-1]
 
     base = None
@@ -384,31 +402,32 @@
         term = permute(total, lambda gg, mm, zz: (gg ^ a, mm, zz) if gg < gg ^ a else None)
         base = term if base is None else base.astype(f32) + term.astype(f32)
 
-    sent = {}
-
-    def attend(c, segs, base):
-        attended = call(
-            functools.partial(attend_body, segs, half, c * half, group),
-            [shape((length, half * HEAD_SIZE), bf16)] * len(segs),
-            [SMEM] * 2 + [VMEM] * (3 + 3 * MEMBERS + 2 * len(segs)),
-            flops=2 * len(segs) * length * length * HEAD_SIZE * half * 3,
+    lower_q1 = finish(halves[2], total)
+
+    def attend(segs, parts, base, *lowers):
+        across = len(parts) * 2 * HEAD_SIZE
+        return call(
+            functools.partial(attend_body, segs, parts, 2),
+            [shape((length, across), bf16)] * len(segs),
+            [SMEM] * 2 + [VMEM] * (2 + len(lowers) + MEMBERS + 4 * len(segs)),
+            flops=4 * len(segs) * length * length * across,
         )(
-            here, gate_bias, base, upper[-1], lower[-1], *kvs, *deltas, *messages,
-            *[sums[s] for s in segs], *[lasts[s] for s in segs],
-        )
-        for seg_at, part in zip(segs, attended):
-            sent[c, seg_at] = to_member(part, seg_at) if seg_at else part
-        return attended
-
-    far = attend(0, (2, 3), base)
-    far = attend(1, (2, 3), after(base, *far))
-    near = attend(0, (1, 0), after(base, *far))
-    attend(1, (1, 0), after(base, *near))
+            here, gate_bias, base, upper[-1], *lowers, *deltas,
+            *[one[s] for one in (kvs, messages, sums, lasts) for s in segs],
+        )
+
+    two0, three0 = attend((2, 3), (0,), base, lower_q0)
+    two1, three1 = attend((2, 3), (1,), after(base, two0, three0), lower_q1)
+    one0, mine0 = attend((1, 0), (0,), after(base, two1, three1), lower_q0)
+    one1, mine1 = attend((1, 0), (1,), after(base, one0), lower_q1)
+    sent = [mine0, mine1]
+    for k, parts in ((1, (one0, one1)), (2, (two0, two1)), (3, (three0, three1))):
+        sent += [to_member(part, k) for part in parts]
     (output,) = call(
-        functools.partial(assemble_body, group, (half * HEAD_SIZE,) * 2),
+        functools.partial(assemble_body, (2,) * MEMBERS),
         [shape((length, w_query.shape[1]), bf16)],
-        [SMEM] + [VMEM] * (2 * MEMBERS),
-    )(here, *[sent[c, k] for k in range(MEMBERS) for c in range(2)])
+        [SMEM] + [VMEM] * len(sent),
+    )(here, *sent)
     return output[None]
 
 

time: 138 us -> 133 us (0.964)
  the two profiles are of different devices: /device:TPU:1 before, /device:TPU:9 now
where the time goes in v7:
time: 133 us; the launch traced here: 131 us
  starting transfers between devices  50.6 us (38%)
  waiting for transfers between devices  36.5 us (27%)
  Pallas kernels  32.7 us (25%)
  local copies, waits for them, and re-layouts  5.81 us (4%)
  other arithmetic  4.33 us (3%)
    ppermute x33, starting transfers between devices, permute(): return lax.ppermute(array, AXES, pairs)  50.6 us
    ppermute x33, waiting for transfers between devices, permute(): return lax.ppermute(array, AXES, pairs)  36.5 us
    pallas_call x4, Pallas kernels, project(): call(functools.partial(project_body, places, line, n_pieces, first), [sha...  18.6 us
    pallas_call x4, Pallas kernels, attend(): call(functools.partial(attend_body, segs, parts, 2), [shape((length, acro...  10.1 us
    unnamed x26, local copies, waits for them, and re-layouts  5.73 us
  transfers between devices with their start and end apart: 33, of which 12 were waited for; matrix products, arithmetic and copies ran while one was open for 3% of the time, Pallas kernels for 24%

profile of v7, /device:TPU:9, one launch (start us, length us, event | category | flops | bytes accessed | tf_op | source)
XLA Modules:
  0.0 131.0 jit_solution(153226799854213159)
XLA Ops:
  0.0 0.7 collective-permute-start.3
  1.3 0.1 pad_add_fusion.here_ref
  1.4 1.0 copy-done.7
  2.5 0.9 copy-done.8
  3.4 0.9 copy-done.9
  4.3 0.7 copy-done.11
  4.9 0.6 shard_map.73
  5.6 1.3 collective-permute-start.1
  6.9 0.6 collective-permute-start.2
  7.5 5.0 %collective-permute-done.1.refs_10_.refs_7_ = bf16[144,768]{1,0:T(8,128)(2,1)S(1)} collective-permute-done((bf16[144,768]{1,0:T(8,128)(2,1)S(1)}, bf16[144,768]{1,0:T(8,128)(2,1)S(1)}, u32[]{:S(2)}, u32[]{:S(2)}) %collective-permute-start.1) | collective-permute-done | bytes 221216 | tf_op jit(solution)/shard_map/ppermute | solution.py:279
  12.5 5.0 %collective-permute-done.2.refs_11_.refs_8_ = bf16[144,768]{1,0:T(8,128)(2,1)S(1)} collective-permute-done((bf16[144,768]{1,0:T(8,128)(2,1)S(1)}, bf16[144,768]{1,0:T(8,128)(2,1)S(1)}, u32[]{:S(2)}, u32[]{:S(2)}) %collective-permute-start.2) | collective-permute-done | bytes 221216 | tf_op jit(solution)/shard_map/ppermute | solution.py:279
  17.6 0.7 copy-done.1
  18.3 1.3 collective-permute-start.20
  19.6 0.2 collective-permute-start.12
  19.8 4.3 %collective-permute-start.13 = (bf16[256,768]{1,0:T(8,128)(2,1)S(1)}, bf16[256,768]{1,0:T(8,128)(2,1)}, u32[]{:S(2)}, u32[]{:S(2)}) collective-permute-start(bf16[256,768]{1,0:T(8,128)(2,1)S(1)} %pad_maximum_fusion.refs_2_), channel_id=1, source_target_pairs={{1,2},{2,1},{5,6},{6,5},{9,10},{10,9},{13,14},{14,13},{17,18},{18,... | collective-permute-start | bytes 1179656 | tf_op jit(solution)/shard_map/ppermute | solution.py:279
  24.1 1.3 collective-permute-start.14
  25.5 4.6 %collective-permute-done.12.refs_4_ = bf16[256,768]{1,0:T(8,128)(2,1)} collective-permute-done((bf16[256,768]{1,0:T(8,128)(2,1)S(1)}, bf16[256,768]{1,0:T(8,128)(2,1)}, u32[]{:S(2)}, u32[]{:S(2)}) %collective-permute-start.12) | collective-permute-done | bytes 393248 | tf_op jit(solution)/shard_map/ppermute | solution.py:279
  30.1 3.2 %collective-permute-start.5 = (bf16[256,768]{1,0:T(8,128)(2,1)S(1)}, bf16[256,768]{1,0:T(8,128)(2,1)S(1)}, u32[]{:S(2)}, u32[]{:S(2)}) collective-permute-start(bf16[256,768]{1,0:T(8,128)(2,1)S(1)} %pad_maximum_fusion.1.refs_3_), channel_id=1, source_target_pairs={{1,2},{2,1},{5,6},{6,5},{9,10},{10,9},{13,14},{14,13},{17,18},{18,... | collective-permute-start | bytes 1179656 | tf_op jit(solution)/shard_map/ppermute | solution.py:279
  33.3 1.3 collective-permute-start.6
  34.6 0.8 copy-done.3
  35.4 2.8 %collective-permute-start.15 = (bf16[256,768]{1,0:T(8,128)(2,1)}, bf16[256,768]{1,0:T(8,128)(2,1)}, u32[]{:S(2)}, u32[]{:S(2)}) collective-permute-start(bf16[256,768]{1,0:T(8,128)(2,1)} %collective-permute-done.12.refs_4_), channel_id=1, source_target_pairs={{1,2},{2,1},{5,6},{6,5},{9,10},{10,9},{13,14},{14,13},{17,18},{18,... | collective-permute-start | bytes 1179656 | tf_op jit(solution)/shard_map/ppermute | solution.py:279
  38.2 0.4 collective-permute-done.4.refs_5_
  38.5 2.9 %collective-permute-start.16 = (bf16[256,768]{1,0:T(8,128)(2,1)}, bf16[256,768]{1,0:T(8,128)(2,1)}, u32[]{:S(2)}, u32[]{:S(2)}) collective-permute-start(bf16[256,768]{1,0:T(8,128)(2,1)} %collective-permute-done.13), channel_id=1, source_target_pairs={{1,0},{2,3},{5,4},{6,7},{9,8},{10,11},{13,12},{14,15},{17,16},{18,... | collective-permute-start | bytes 1179656 | tf_op jit(solution)/shard_map/ppermute | solution.py:279
  41.4 1.2 collective-permute-start.17
  42.7 0.8 copy-done.5
  43.4 4.3 %collective-permute-start.7 = (bf16[256,768]{1,0:T(8,128)(2,1)}, bf16[256,768]{1,0:T(8,128)(2,1)}, u32[]{:S(2)}, u32[]{:S(2)}) collective-permute-start(bf16[256,768]{1,0:T(8,128)(2,1)} %collective-permute-done.4.refs_5_), channel_id=1, source_target_pairs={{1,2},{2,1},{5,6},{6,5},{9,10},{10,9},{13,14},{14,13},{17,18},{18,... | collective-permute-start | bytes 1179656 | tf_op jit(solution)/shard_map/ppermute | solution.py:279
  47.8 1.4 %collective-permute-done.15 = bf16[256,768]{1,0:T(8,128)(2,1)} collective-permute-done((bf16[256,768]{1,0:T(8,128)(2,1)}, bf16[256,768]{1,0:T(8,128)(2,1)}, u32[]{:S(2)}, u32[]{:S(2)}) %collective-permute-start.15) | collective-permute-done | bytes 393248 | tf_op jit(solution)/shard_map/ppermute | solution.py:279
  49.1 1.2 collective-permute-start.9
  50.4 1.8 %collective-permute-start.8 = (bf16[256,768]{1,0:T(8,128)(2,1)}, bf16[256,768]{1,0:T(8,128)(2,1)S(1)}, u32[]{:S(2)}, u32[]{:S(2)}) collective-permute-start(bf16[256,768]{1,0:T(8,128)(2,1)} %copy-done.12), channel_id=1, source_target_pairs={{1,0},{2,3},{5,4},{6,7},{9,8},{10,11},{13,12},{14,15},{17,16},{18,... | collective-permute-start | bytes 1179656 | tf_op jit(solution)/shard_map/ppermute | solution.py:279
  52.2 1.1 broadcast_select_fusion.2.refs_2_
  53.3 1.3 collective-permute-start.19
  54.6 3.2 %collective-permute-done.7 = bf16[256,768]{1,0:T(8,128)(2,1)} collective-permute-done((bf16[256,768]{1,0:T(8,128)(2,1)}, bf16[256,768]{1,0:T(8,128)(2,1)}, u32[]{:S(2)}, u32[]{:S(2)}) %collective-permute-start.7) | collective-permute-done | bytes 393248 | tf_op jit(solution)/shard_map/ppermute | solution.py:279
  57.8 1.3 collective-permute-start.18
  59.1 1.0 broadcast_select_fusion.3.refs_3_
  60.2 6.1 %collective-permute-done.19.refs_6_ = bf16[256,768]{1,0:T(8,128)(2,1)S(1)} collective-permute-done((bf16[256,768]{1,0:T(8,128)(2,1)S(1)}, bf16[256,768]{1,0:T(8,128)(2,1)S(1)}, u32[]{:S(2)}, u32[]{:S(2)}) %collective-permute-start.19) | collective-permute-done | bytes 393248 | tf_op jit(solution)/shard_map/ppermute | solution.py:279
  66.3 2.1 %collective-permute-done.18 = bf16[256,768]{1,0:T(8,128)(2,1)S(1)} collective-permute-done((bf16[256,768]{1,0:T(8,128)(2,1)}, bf16[256,768]{1,0:T(8,128)(2,1)S(1)}, u32[]{:S(2)}, u32[]{:S(2)}) %collective-permute-start.18) | collective-permute-done | bytes 393248 | tf_op jit(solution)/shard_map/ppermute | solution.py:279
  68.4 3.0 %collective-permute-start.22 = (bf16[256,4096]{1,0:T(8,128)(2,1)}, bf16[256,4096]{1,0:T(8,128)(2,1)S(1)}, u32[]{:S(2)}, u32[]{:S(2)}) collective-permute-start(bf16[256,4096]{1,0:T(8,128)(2,1)} %collective-permute-done.20.refs_0_), channel_id=1, source_target_pairs={{0,4},{1,5},{2,6},{3,7},{4,0},{5,1},{6,2},{7,3},{8,12},{9,13},{10,... | collective-permute-start | bytes 6291464 | tf_op jit(solution)/shard_map/ppermute | solution.py:279
  71.4 0.7 collective-permute-start.11
  72.1 3.6 %collective-permute-start.10 = (bf16[256,768]{1,0:T(8,128)(2,1)}, bf16[256,768]{1,0:T(8,128)(2,1)S(1)}, u32[]{:S(2)}, u32[]{:S(2)}) collective-permute-start(bf16[256,768]{1,0:T(8,128)(2,1)} %collective-permute-done.7), channel_id=1, source_target_pairs={{1,0},{2,3},{5,4},{6,7},{9,8},{10,11},{13,12},{14,15},{17,16},{18,... | collective-permute-start | bytes 1179656 | tf_op jit(solution)/shard_map/ppermute | solution.py:279
  75.7 1.1 broadcast_select_fusion.1.refs_4_
  76.8 1.4 %collective-permute-start.21 = (bf16[256,768]{1,0:T(8,128)(2,1)S(1)}, bf16[256,768]{1,0:T(8,128)(2,1)S(1)}, u32[]{:S(2)}, u32[]{:S(2)}) collective-permute-start(bf16[256,768]{1,0:T(8,128)(2,1)S(1)} %broadcast_select_fusion.1.refs_4_), channel_id=1, source_target_pairs={{0,16},{1,17},{2,18},{3,19},{4,20},{5,21},{6,22},{7,23},{8,24},{9,... | collective-permute-start | bytes 1179656 | tf_op jit(solution)/shard_map/ppermute | solution.py:279
  78.2 5.5 %shard_map.74 = (f32[256,768]{1,0:T(8,128)S(1)}, f32[256,768]{1,0:T(8,128)S(1)}, bf16[256,512]{1,0:T(8,128)(2,1)S(1)}, bf16[256,512]{1,0:T(8,128)(2,1)S(1)}) custom-call(s32[3]{0:T(128)S(1)} %pad_add_fusion.here_ref, bf16[256,4096]{1,0:T(8,128)(2,1)S(1)} %bitcast.7, bf16[256,4096]{1,0:T(8,128)(2,1)} %collective-permute-done.3.refs_1_, ...), custom_call_target="tpu_custom_call" | custom-call | flops 1610612736 | bytes 4194304 | tf_op jit(solution)/shard_map/pallas_call | solution.py:315
  83.7 5.4 %shard_map.75 = (f32[256,768]{1,0:T(8,128)S(1)}, f32[256,768]{1,0:T(8,128)S(1)}, bf16[256,512]{1,0:T(8,128)(2,1)S(1)}, bf16[256,512]{1,0:T(8,128)(2,1)S(1)}) custom-call(s32[3]{0:T(128)S(1)} %pad_add_fusion.here_ref, bf16[256,4096]{1,0:T(8,128)(2,1)} %collective-permute-done.20.refs_0_, bf16[256,4096]{1,0:T(8,128)(2,1)S(1)} %collective-permute-done.22.refs_1_, ...), custom_call_target="tpu_custom_call" | custom-call | flops 1610612736 | bytes 4194304 | tf_op jit(solution)/shard_map/pallas_call | solution.py:315
  89.1 1.4 %collective-permute-done.21.upper_ref = bf16[256,768]{1,0:T(8,128)(2,1)S(1)} collective-permute-done((bf16[256,768]{1,0:T(8,128)(2,1)S(1)}, bf16[256,768]{1,0:T(8,128)(2,1)S(1)}, u32[]{:S(2)}, u32[]{:S(2)}) %collective-permute-start.21) | collective-permute-done | bytes 393248 | tf_op jit(solution)/shard_map/ppermute | solution.py:279
  90.5 1.0 broadcast_select_fusion.refs_5_
  91.6 0.7 collective-permute-start.23
  92.3 0.8 collective-permute-start.25
  93.2 3.9 %shard_map.76 = (f32[256,768]{1,0:T(8,128)S(1)}, f32[256,768]{1,0:T(8,128)S(1)}) custom-call(s32[3]{0:T(128)S(1)} %pad_add_fusion.here_ref, bf16[256,4096]{1,0:T(8,128)(2,1)S(1)} %bitcast.8, bf16[256,4096]{1,0:T(8,128)(2,1)} %collective-permute-done.3.refs_1_, bf16[256,768]{1,0:T(8,128)(2,1)S(1)} %broadcast_select_fusion.2.refs_2_, ...), custom_call_target="tpu_custom_call" | custom-call | flops 1207959552 | bytes 4194304 | tf_op jit(solution)/shard_map/pallas_call | solution.py:315
  97.1 3.8 %shard_map.77 = (f32[256,768]{1,0:T(8,128)S(1)}, f32[256,768]{1,0:T(8,128)S(1)}) custom-call(s32[3]{0:T(128)S(1)} %pad_add_fusion.here_ref, bf16[256,4096]{1,0:T(8,128)(2,1)} %collective-permute-done.20.refs_0_, bf16[256,4096]{1,0:T(8,128)(2,1)S(1)} %collective-permute-done.22.refs_1_, bf16[256,768]{1,0:T(8,128)(2,1)S(1)} %broadcast_select_fusion.2.refs_2_, ...), custom_call_target="tpu_custom_call" | custom-call | flops 1207959552 | bytes 4194304 | tf_op jit(solution)/shard_map/pallas_call | solution.py:315
  100.9 1.7 %shard_map.78 = (bf16[256,256]{1,0:T(8,128)(2,1)S(1)}, f32[128,256]{1,0:T(8,128)S(1)}, bf16[256,256]{1,0:T(8,128)(2,1)S(1)}, f32[128,256]{1,0:T(8,128)S(1)}, bf1...) custom-call(bf16[256,768]{1,0:T(8,128)(2,1)S(1)} %collective-permute, ...), custom_call_target="tpu_custom_call" | custom-call | flops 268435456 | bytes 4194304 | tf_op jit(solution)/shard_map/pallas_call | solution.py:391
  102.6 2.8 %collective-permute-start.24 = (bf16[128,256]{1,0:T(8,128)(2,1)S(1)}, bf16[128,256]{1,0:T(8,128)(2,1)S(1)}, u32[]{:S(2)}, u32[]{:S(2)}) collective-permute-start(bf16[128,256]{1,0:T(8,128)(2,1)S(1)} %get-tuple-element.120), channel_id=1, source_target_pairs={{0,16},{1,17},{2,18},{3,19},{4,20},{5,21},{6,22},{7,23},{8,24},{9,... | collective-permute-start | bytes 196616 | tf_op jit(solution)/shard_map/ppermute | solution.py:279
  105.5 1.0 collective-permute-done.24.base_ref
  106.5 2.5 %shard_map.79 = (bf16[256,256]{1,0:T(8,128)(2,1)S(1)}, bf16[256,256]{1,0:T(8,128)(2,1)S(1)}) custom-call(s32[3]{0:T(128)S(1)} %pad_add_fusion.here_ref, f32[16]{0:T(128)S(1)} %copy-done.10, bf16[128,256]{1,0:T(8,128)(2,1)S(1)} %collective-permute-done.24.base_ref, bf16[256,768]{1,0:T(8,128)(2,1)S(1)} %collective-permute-done.21.upper_ref, ...), custom_call_target="tpu_custom_call" | custom-call | flops 134217728 | bytes 4194304 | tf_op jit(solution)/shard_map/pallas_call | solution.py:409
  109.0 0.3 collective-permute-start.29
  109.3 3.8 %collective-permute-start.31 = (bf16[256,256]{1,0:T(8,128)(2,1)S(1)}, bf16[256,256]{1,0:T(8,128)(2,1)S(1)}, u32[]{:S(2)}, u32[]{:S(2)}) collective-permute-start(bf16[256,256]{1,0:T(8,128)(2,1)S(1)} %get-tuple-element.128), channel_id=1, source_target_pairs={{0,12},{1,13},{2,14},{3,15},{4,8},{5,9},{6,10},{7,11},{8,4},{9,5},... | collective-permute-start | bytes 393224 | tf_op jit(solution)/shard_map/ppermute | solution.py:279
  113.1 2.5 %shard_map.80 = (bf16[256,256]{1,0:T(8,128)(2,1)S(1)}, bf16[256,256]{1,0:T(8,128)(2,1)S(1)}) custom-call(s32[3]{0:T(128)S(1)} %pad_add_fusion.here_ref, f32[16]{0:T(128)S(1)} %copy-done.10, bf16[128,256]{1,0:T(8,128)(2,1)S(1)} %collective-permute-done.24.base_ref, bf16[256,768]{1,0:T(8,128)(2,1)S(1)} %collective-permute-done.21.upper_ref, ...), custom_call_target="tpu_custom_call" | custom-call | flops 134217728 | bytes 4194304 | tf_op jit(solution)/shard_map/pallas_call | solution.py:409
  115.6 2.5 %shard_map.81 = (bf16[256,256]{1,0:T(8,128)(2,1)S(1)}, bf16[256,256]{1,0:T(8,128)(2,1)S(1)}) custom-call(s32[3]{0:T(128)S(1)} %pad_add_fusion.here_ref, f32[16]{0:T(128)S(1)} %copy-done.10, bf16[128,256]{1,0:T(8,128)(2,1)S(1)} %collective-permute-done.24.base_ref, bf16[256,768]{1,0:T(8,128)(2,1)S(1)} %collective-permute-done.21.upper_ref, ...), custom_call_target="tpu_custom_call" | custom-call | flops 134217728 | bytes 4194304 | tf_op jit(solution)/shard_map/pallas_call | solution.py:409
  118.2 2.5 %shard_map.82 = (bf16[256,256]{1,0:T(8,128)(2,1)S(1)}, bf16[256,256]{1,0:T(8,128)(2,1)S(1)}) custom-call(s32[3]{0:T(128)S(1)} %pad_add_fusion.here_ref, f32[16]{0:T(128)S(1)} %copy-done.10, bf16[128,256]{1,0:T(8,128)(2,1)S(1)} %collective-permute-done.24.base_ref, bf16[256,768]{1,0:T(8,128)(2,1)S(1)} %collective-permute-done.21.upper_ref, ...), custom_call_target="tpu_custom_call" | custom-call | flops 134217728 | bytes 4194304 | tf_op jit(solution)/shard_map/pallas_call | solution.py:409
  120.7 0.5 collective-permute-start.28
  121.3 0.3 collective-permute-start.30
  121.6 1.4 %collective-permute-start.32 = (bf16[256,256]{1,0:T(8,128)(2,1)S(1)}, bf16[256,256]{1,0:T(8,128)(2,1)S(1)}, u32[]{:S(2)}, u32[]{:S(2)}) collective-permute-start(bf16[256,256]{1,0:T(8,128)(2,1)S(1)} %get-tuple-element.132), channel_id=1, source_target_pairs={{0,12},{1,13},{2,14},{3,15},{4,8},{5,9},{6,10},{7,11},{8,4},{9,5},... | collective-permute-start | bytes 393224 | tf_op jit(solution)/shard_map/ppermute | solution.py:279
  123.0 3.4 %collective-permute-done.30.refs_5_ = bf16[256,256]{1,0:T(8,128)(2,1)S(1)} collective-permute-done((bf16[256,256]{1,0:T(8,128)(2,1)S(1)}, bf16[256,256]{1,0:T(8,128)(2,1)S(1)}, u32[]{:S(2)}, u32[]{:S(2)}) %collective-permute-start.30) | collective-permute-done | bytes 131104 | tf_op jit(solution)/shard_map/ppermute | solution.py:279
  126.4 3.0 %collective-permute-done.32.refs_7_ = bf16[256,256]{1,0:T(8,128)(2,1)S(1)} collective-permute-done((bf16[256,256]{1,0:T(8,128)(2,1)S(1)}, bf16[256,256]{1,0:T(8,128)(2,1)S(1)}, u32[]{:S(2)}, u32[]{:S(2)}) %collective-permute-start.32) | collective-permute-done | bytes 131104 | tf_op jit(solution)/shard_map/ppermute | solution.py:279
  129.3 1.6 %shard_map.83 = bf16[256,2048]{1,0:T(8,128)(2,1)} custom-call(s32[3]{0:T(128)S(1)} %pad_add_fusion.here_ref, bf16[256,256]{1,0:T(8,128)(2,1)S(1)} %get-tuple-element.136.refs_0_, bf16[256,256]{1,0:T(8,128)(2,1)S(1)} %get-tuple-element.139.refs_1_, bf16[256,256]{1,0:T(8,128)(2,1)S(1)} %collective-permute-done.27.refs_2_, ...), custom_call_target="tpu_custom_call" | custom-call | bytes 4194304 | tf_op jit(solution)/shard_map/pallas_call | solution.py:426
  (51 shorter events, 0.4 us)
Async XLA Ops:
  0.0 18.3 %copy-start = (bf16[1,256,4096]{2,1,0:T(8,128)(2,1)S(1)}, bf16[1,256,4096]{2,1,0:T(8,128)(2,1)}, u32[]{:S(2)}) copy-start(bf16[1,256,4096]{2,1,0:T(8,128)(2,1)} %param.7) | copy-start | bytes 6291460
  0.0 18.3 %collective-permute-start.3 = (bf16[256,4096]{1,0:T(8,128)(2,1)}, bf16[256,4096]{1,0:T(8,128)(2,1)}, u32[]{:S(2)}, u32[]{:S(2)}) collective-permute-start(bf16[256,4096]{1,0:T(8,128)(2,1)} %bitcast.5), channel_id=1, source_target_pairs={{0,4},{1,5},{2,6},{3,7},{4,0},{5,1},{6,2},{7,3},{8,12},{9,13},{10,... | collective-permute-start | bytes 6291464 | tf_op jit(solution)/shard_map/ppermute | solution.py:279
  1.4 1.0 copy-start.7
  2.5 0.9 copy-start.8
  3.4 0.9 copy-start.9
  4.3 0.7 copy-start.11
  5.6 6.9 %collective-permute-start.1 = (bf16[144,768]{1,0:T(8,128)(2,1)S(1)}, bf16[144,768]{1,0:T(8,128)(2,1)S(1)}, u32[]{:S(2)}, u32[]{:S(2)}) collective-permute-start(bf16[144,768]{1,0:T(8,128)(2,1)S(1)} %get-tuple-element.75), channel_id=1, source_target_pairs={{0,8},{1,9},{2,10},{3,11},{4,12},{5,13},{6,14},{7,15},{8,0},{9,1},... | collective-permute-start | bytes 663560 | tf_op jit(solution)/shard_map/ppermute | solution.py:279
  6.9 10.7 %collective-permute-start.2 = (bf16[144,768]{1,0:T(8,128)(2,1)S(1)}, bf16[144,768]{1,0:T(8,128)(2,1)S(1)}, u32[]{:S(2)}, u32[]{:S(2)}) collective-permute-start(bf16[144,768]{1,0:T(8,128)(2,1)S(1)} %get-tuple-element.76), channel_id=1, source_target_pairs={{0,12},{1,13},{2,14},{3,15},{4,8},{5,9},{6,10},{7,11},{8,4},{9,5},... | collective-permute-start | bytes 663560 | tf_op jit(solution)/shard_map/ppermute | solution.py:279
  7.5 10.1 %collective-permute-start = (bf16[144,768]{1,0:T(8,128)(2,1)S(1)}, bf16[144,768]{1,0:T(8,128)(2,1)S(1)}, u32[]{:S(2)}, u32[]{:S(2)}) collective-permute-start(bf16[144,768]{1,0:T(8,128)(2,1)S(1)} %get-tuple-element.74), channel_id=1, source_target_pairs={{0,4},{1,5},{2,6},{3,7},{4,0},{5,1},{6,2},{7,3},{8,12},{9,13},{10,... | collective-permute-start | bytes 663560 | tf_op jit(solution)/shard_map/ppermute | solution.py:279
  17.5 0.7 copy-start.1
  18.3 50.0 %collective-permute-start.20 = (bf16[256,4096]{1,0:T(8,128)(2,1)S(1)}, bf16[256,4096]{1,0:T(8,128)(2,1)}, u32[]{:S(2)}, u32[]{:S(2)}) collective-permute-start(bf16[256,4096]{1,0:T(8,128)(2,1)S(1)} %bitcast.6), channel_id=1, source_target_pairs={{0,8},{1,9},{2,10},{3,11},{4,12},{5,13},{6,14},{7,15},{8,0},{9,1},... | collective-permute-start | bytes 6291464 | tf_op jit(solution)/shard_map/ppermute | solution.py:279
  19.6 10.4 %collective-permute-start.12 = (bf16[256,768]{1,0:T(8,128)(2,1)S(1)}, bf16[256,768]{1,0:T(8,128)(2,1)}, u32[]{:S(2)}, u32[]{:S(2)}) collective-permute-start(bf16[256,768]{1,0:T(8,128)(2,1)S(1)} %pad_maximum_fusion.refs_2_), channel_id=1, source_target_pairs={{0,1},{1,0},{2,3},{3,2},{4,5},{5,4},{6,7},{7,6},{8,9},{9,8},{10,11... | collective-permute-start | bytes 1179656 | tf_op jit(solution)/shard_map/ppermute | solution.py:279
  19.8 13.5 %collective-permute-start.13 = (bf16[256,768]{1,0:T(8,128)(2,1)S(1)}, bf16[256,768]{1,0:T(8,128)(2,1)}, u32[]{:S(2)}, u32[]{:S(2)}) collective-permute-start(bf16[256,768]{1,0:T(8,128)(2,1)S(1)} %pad_maximum_fusion.refs_2_), channel_id=1, source_target_pairs={{1,2},{2,1},{5,6},{6,5},{9,10},{10,9},{13,14},{14,13},{17,18},{18,... | collective-permute-start | bytes 1179656 | tf_op jit(solution)/shard_map/ppermute | solution.py:279
  24.1 10.5 %collective-permute-start.14 = (bf16[256,768]{1,0:T(8,128)(2,1)S(1)}, bf16[256,768]{1,0:T(8,128)(2,1)S(1)}, u32[]{:S(2)}, u32[]{:S(2)}) collective-permute-start(bf16[256,768]{1,0:T(8,128)(2,1)S(1)} %pad_maximum_fusion.refs_2_), channel_id=1, source_target_pairs={{0,16},{1,17},{2,18},{3,19},{4,20},{5,21},{6,22},{7,23},{8,24},{9,... | collective-permute-start | bytes 1179656 | tf_op jit(solution)/shard_map/ppermute | solution.py:279
  25.5 13.1 %collective-permute-start.4 = (bf16[256,768]{1,0:T(8,128)(2,1)S(1)}, bf16[256,768]{1,0:T(8,128)(2,1)}, u32[]{:S(2)}, u32[]{:S(2)}) collective-permute-start(bf16[256,768]{1,0:T(8,128)(2,1)S(1)} %pad_maximum_fusion.1.refs_3_), channel_id=1, source_target_pairs={{0,1},{1,0},{2,3},{3,2},{4,5},{5,4},{6,7},{7,6},{8,9},{9,8},{10,11... | collective-permute-start | bytes 1179656 | tf_op jit(solution)/shard_map/ppermute | solution.py:279
  30.1 11.3 %collective-permute-start.5 = (bf16[256,768]{1,0:T(8,128)(2,1)S(1)}, bf16[256,768]{1,0:T(8,128)(2,1)S(1)}, u32[]{:S(2)}, u32[]{:S(2)}) collective-permute-start(bf16[256,768]{1,0:T(8,128)(2,1)S(1)} %pad_maximum_fusion.1.refs_3_), channel_id=1, source_target_pairs={{1,2},{2,1},{5,6},{6,5},{9,10},{10,9},{13,14},{14,13},{17,18},{18,... | collective-permute-start | bytes 1179656 | tf_op jit(solution)/shard_map/ppermute | solution.py:279
  33.3 9.4 %collective-permute-start.6 = (bf16[256,768]{1,0:T(8,128)(2,1)S(1)}, bf16[256,768]{1,0:T(8,128)(2,1)S(1)}, u32[]{:S(2)}, u32[]{:S(2)}) collective-permute-start(bf16[256,768]{1,0:T(8,128)(2,1)S(1)} %pad_maximum_fusion.1.refs_3_), channel_id=1, source_target_pairs={{0,16},{1,17},{2,18},{3,19},{4,20},{5,21},{6,22},{7,23},{8,24},{9,... | collective-permute-start | bytes 1179656 | tf_op jit(solution)/shard_map/ppermute | solution.py:279
  34.6 0.8 copy-start.3
  35.4 13.8 %collective-permute-start.15 = (bf16[256,768]{1,0:T(8,128)(2,1)}, bf16[256,768]{1,0:T(8,128)(2,1)}, u32[]{:S(2)}, u32[]{:S(2)}) collective-permute-start(bf16[256,768]{1,0:T(8,128)(2,1)} %collective-permute-done.12.refs_4_), channel_id=1, source_target_pairs={{1,2},{2,1},{5,6},{6,5},{9,10},{10,9},{13,14},{14,13},{17,18},{18,... | collective-permute-start | bytes 1179656 | tf_op jit(solution)/shard_map/ppermute | solution.py:279
  38.5 11.9 %collective-permute-start.16 = (bf16[256,768]{1,0:T(8,128)(2,1)}, bf16[256,768]{1,0:T(8,128)(2,1)}, u32[]{:S(2)}, u32[]{:S(2)}) collective-permute-start(bf16[256,768]{1,0:T(8,128)(2,1)} %collective-permute-done.13), channel_id=1, source_target_pairs={{1,0},{2,3},{5,4},{6,7},{9,8},{10,11},{13,12},{14,15},{17,16},{18,... | collective-permute-start | bytes 1179656 | tf_op jit(solution)/shard_map/ppermute | solution.py:279
  41.4 1.2 copy-start.12
  41.4 10.8 %collective-permute-start.17 = (bf16[256,768]{1,0:T(8,128)(2,1)}, bf16[256,768]{1,0:T(8,128)(2,1)}, u32[]{:S(2)}, u32[]{:S(2)}) collective-permute-start(bf16[256,768]{1,0:T(8,128)(2,1)} %collective-permute-done.12.refs_4_), channel_id=1, source_target_pairs={{0,16},{1,17},{2,18},{3,19},{4,20},{5,21},{6,22},{7,23},{8,24},{9,... | collective-permute-start | bytes 1179656 | tf_op jit(solution)/shard_map/ppermute | solution.py:279
  42.7 0.8 copy-start.5
  43.4 14.4 %collective-permute-start.7 = (bf16[256,768]{1,0:T(8,128)(2,1)}, bf16[256,768]{1,0:T(8,128)(2,1)}, u32[]{:S(2)}, u32[]{:S(2)}) collective-permute-start(bf16[256,768]{1,0:T(8,128)(2,1)} %collective-permute-done.4.refs_5_), channel_id=1, source_target_pairs={{1,2},{2,1},{5,6},{6,5},{9,10},{10,9},{13,14},{14,13},{17,18},{18,... | collective-permute-start | bytes 1179656 | tf_op jit(solution)/shard_map/ppermute | solution.py:279
  47.8 30.4 %copy-start.4 = (bf16[256,768]{1,0:T(8,128)(2,1)S(1)}, bf16[256,768]{1,0:T(8,128)(2,1)}, u32[]{:S(2)}) copy-start(bf16[256,768]{1,0:T(8,128)(2,1)} %copy-done.3) | copy-start | bytes 1179652
  47.8 30.4 %copy-start.6 = (bf16[256,768]{1,0:T(8,128)(2,1)S(1)}, bf16[256,768]{1,0:T(8,128)(2,1)}, u32[]{:S(2)}) copy-start(bf16[256,768]{1,0:T(8,128)(2,1)} %copy-done.5) | copy-start | bytes 1179652
  49.1 10.0 %collective-permute-start.9 = (bf16[256,768]{1,0:T(8,128)(2,1)}, bf16[256,768]{1,0:T(8,128)(2,1)S(1)}, u32[]{:S(2)}, u32[]{:S(2)}) collective-permute-start(bf16[256,768]{1,0:T(8,128)(2,1)} %collective-permute-done.4.refs_5_), channel_id=1, source_target_pairs={{0,16},{1,17},{2,18},{3,19},{4,20},{5,21},{6,22},{7,23},{8,24},{9,... | collective-permute-start | bytes 1179656 | tf_op jit(solution)/shard_map/ppermute | solution.py:279
  50.4 8.7 %collective-permute-start.8 = (bf16[256,768]{1,0:T(8,128)(2,1)}, bf16[256,768]{1,0:T(8,128)(2,1)S(1)}, u32[]{:S(2)}, u32[]{:S(2)}) collective-permute-start(bf16[256,768]{1,0:T(8,128)(2,1)} %copy-done.12), channel_id=1, source_target_pairs={{1,0},{2,3},{5,4},{6,7},{9,8},{10,11},{13,12},{14,15},{17,16},{18,... | collective-permute-start | bytes 1179656 | tf_op jit(solution)/shard_map/ppermute | solution.py:279
  53.3 13.0 %collective-permute-start.19 = (bf16[256,768]{1,0:T(8,128)(2,1)S(1)}, bf16[256,768]{1,0:T(8,128)(2,1)S(1)}, u32[]{:S(2)}, u32[]{:S(2)}) collective-permute-start(bf16[256,768]{1,0:T(8,128)(2,1)S(1)} %broadcast_select_fusion.2.refs_2_), channel_id=1, source_target_pairs={{0,16},{1,17},{2,18},{3,19},{4,20},{5,21},{6,22},{7,23},{8,24},{9,... | collective-permute-start | bytes 1179656 | tf_op jit(solution)/shard_map/ppermute | solution.py:279
  57.8 10.6 %collective-permute-start.18 = (bf16[256,768]{1,0:T(8,128)(2,1)}, bf16[256,768]{1,0:T(8,128)(2,1)S(1)}, u32[]{:S(2)}, u32[]{:S(2)}) collective-permute-start(bf16[256,768]{1,0:T(8,128)(2,1)} %collective-permute-done.15), channel_id=1, source_target_pairs={{1,0},{2,3},{5,4},{6,7},{9,8},{10,11},{13,12},{14,15},{17,16},{18,... | collective-permute-start | bytes 1179656 | tf_op jit(solution)/shard_map/ppermute | solution.py:279
  68.4 15.3 %collective-permute-start.22 = (bf16[256,4096]{1,0:T(8,128)(2,1)}, bf16[256,4096]{1,0:T(8,128)(2,1)S(1)}, u32[]{:S(2)}, u32[]{:S(2)}) collective-permute-start(bf16[256,4096]{1,0:T(8,128)(2,1)} %collective-permute-done.20.refs_0_), channel_id=1, source_target_pairs={{0,4},{1,5},{2,6},{3,7},{4,0},{5,1},{6,2},{7,3},{8,12},{9,13},{10,... | collective-permute-start | bytes 6291464 | tf_op jit(solution)/shard_map/ppermute | solution.py:279
  71.4 17.8 %collective-permute-start.11 = (bf16[256,768]{1,0:T(8,128)(2,1)S(1)}, bf16[256,768]{1,0:T(8,128)(2,1)S(1)}, u32[]{:S(2)}, u32[]{:S(2)}) collective-permute-start(bf16[256,768]{1,0:T(8,128)(2,1)S(1)} %broadcast_select_fusion.3.refs_3_), channel_id=1, source_target_pairs={{0,16},{1,17},{2,18},{3,19},{4,20},{5,21},{6,22},{7,23},{8,24},{9,... | collective-permute-start | bytes 1179656 | tf_op jit(solution)/shard_map/ppermute | solution.py:279
  72.1 17.0 %collective-permute-start.10 = (bf16[256,768]{1,0:T(8,128)(2,1)}, bf16[256,768]{1,0:T(8,128)(2,1)S(1)}, u32[]{:S(2)}, u32[]{:S(2)}) collective-permute-start(bf16[256,768]{1,0:T(8,128)(2,1)} %collective-permute-done.7), channel_id=1, source_target_pairs={{1,0},{2,3},{5,4},{6,7},{9,8},{10,11},{13,12},{14,15},{17,16},{18,... | collective-permute-start | bytes 1179656 | tf_op jit(solution)/shard_map/ppermute | solution.py:279
  76.8 13.8 %collective-permute-start.21 = (bf16[256,768]{1,0:T(8,128)(2,1)S(1)}, bf16[256,768]{1,0:T(8,128)(2,1)S(1)}, u32[]{:S(2)}, u32[]{:S(2)}) collective-permute-start(bf16[256,768]{1,0:T(8,128)(2,1)S(1)} %broadcast_select_fusion.1.refs_4_), channel_id=1, source_target_pairs={{0,16},{1,17},{2,18},{3,19},{4,20},{5,21},{6,22},{7,23},{8,24},{9,... | collective-permute-start | bytes 1179656 | tf_op jit(solution)/shard_map/ppermute | solution.py:279
  91.6 9.3 %collective-permute-start.23 = (bf16[256,256]{1,0:T(8,128)(2,1)S(1)}, bf16[256,256]{1,0:T(8,128)(2,1)S(1)}, u32[]{:S(2)}, u32[]{:S(2)}) collective-permute-start(bf16[256,256]{1,0:T(8,128)(2,1)S(1)} %get-tuple-element.143), channel_id=1, source_target_pairs={{0,16},{1,17},{2,18},{3,19},{4,20},{5,21},{6,22},{7,23},{8,24},{9,... | collective-permute-start | bytes 393224 | tf_op jit(solution)/shard_map/ppermute | solution.py:279
  92.3 13.1 %collective-permute-start.25 = (bf16[256,256]{1,0:T(8,128)(2,1)S(1)}, bf16[256,256]{1,0:T(8,128)(2,1)S(1)}, u32[]{:S(2)}, u32[]{:S(2)}) collective-permute-start(bf16[256,256]{1,0:T(8,128)(2,1)S(1)} %get-tuple-element.142), channel_id=1, source_target_pairs={{0,16},{1,17},{2,18},{3,19},{4,20},{5,21},{6,22},{7,23},{8,24},{9,... | collective-permute-start | bytes 393224 | tf_op jit(solution)/shard_map/ppermute | solution.py:279
  97.1 3.8 %copy-start.2 = (bf16[144,768]{1,0:T(8,128)(2,1)S(1)}, bf16[144,768]{1,0:T(8,128)(2,1)}, u32[]{:S(2)}) copy-start(bf16[144,768]{1,0:T(8,128)(2,1)} %copy-done.1) | copy-start | bytes 663556
  100.9 5.6 %copy-start.10 = (f32[16]{0:T(128)S(1)}, f32[16]{0:T(128)}, u32[]{:S(2)}) copy-start(f32[16]{0:T(128)} %gate_ref.7) | copy-start | bytes 196
  102.6 3.9 %collective-permute-start.24 = (bf16[128,256]{1,0:T(8,128)(2,1)S(1)}, bf16[128,256]{1,0:T(8,128)(2,1)S(1)}, u32[]{:S(2)}, u32[]{:S(2)}) collective-permute-start(bf16[128,256]{1,0:T(8,128)(2,1)S(1)} %get-tuple-element.120), channel_id=1, source_target_pairs={{0,16},{1,17},{2,18},{3,19},{4,20},{5,21},{6,22},{7,23},{8,24},{9,... | collective-permute-start | bytes 196616 | tf_op jit(solution)/shard_map/ppermute | solution.py:279
  105.4 7.7 %collective-permute-start.26 = (bf16[256,256]{1,0:T(8,128)(2,1)S(1)}, bf16[256,256]{1,0:T(8,128)(2,1)S(1)}, u32[]{:S(2)}, u32[]{:S(2)}) collective-permute-start(bf16[256,256]{1,0:T(8,128)(2,1)S(1)} %get-tuple-element.130), channel_id=1, source_target_pairs={{0,16},{1,17},{2,18},{3,19},{4,20},{5,21},{6,22},{7,23},{8,24},{9,... | collective-permute-start | bytes 393224 | tf_op jit(solution)/shard_map/ppermute | solution.py:279
  109.0 12.6 %collective-permute-start.29 = (bf16[256,256]{1,0:T(8,128)(2,1)S(1)}, bf16[256,256]{1,0:T(8,128)(2,1)S(1)}, u32[]{:S(2)}, u32[]{:S(2)}) collective-permute-start(bf16[256,256]{1,0:T(8,128)(2,1)S(1)} %get-tuple-element.127), channel_id=1, source_target_pairs={{0,8},{1,9},{2,10},{3,11},{4,12},{5,13},{6,14},{7,15},{8,0},{9,1},... | collective-permute-start | bytes 393224 | tf_op jit(solution)/shard_map/ppermute | solution.py:279
  109.3 13.7 %collective-permute-start.31 = (bf16[256,256]{1,0:T(8,128)(2,1)S(1)}, bf16[256,256]{1,0:T(8,128)(2,1)S(1)}, u32[]{:S(2)}, u32[]{:S(2)}) collective-permute-start(bf16[256,256]{1,0:T(8,128)(2,1)S(1)} %get-tuple-element.128), channel_id=1, source_target_pairs={{0,12},{1,13},{2,14},{3,15},{4,8},{5,9},{6,10},{7,11},{8,4},{9,5},... | collective-permute-start | bytes 393224 | tf_op jit(solution)/shard_map/ppermute | solution.py:279
  118.1 4.9 %collective-permute-start.27 = (bf16[256,256]{1,0:T(8,128)(2,1)S(1)}, bf16[256,256]{1,0:T(8,128)(2,1)S(1)}, u32[]{:S(2)}, u32[]{:S(2)}) collective-permute-start(bf16[256,256]{1,0:T(8,128)(2,1)S(1)} %get-tuple-element.137), channel_id=1, source_target_pairs={{0,4},{1,5},{2,6},{3,7},{4,0},{5,1},{6,2},{7,3},{8,12},{9,13},{10,... | collective-permute-start | bytes 393224 | tf_op jit(solution)/shard_map/ppermute | solution.py:279
  120.7 2.3 %collective-permute-start.28 = (bf16[256,256]{1,0:T(8,128)(2,1)S(1)}, bf16[256,256]{1,0:T(8,128)(2,1)S(1)}, u32[]{:S(2)}, u32[]{:S(2)}) collective-permute-start(bf16[256,256]{1,0:T(8,128)(2,1)S(1)} %get-tuple-element.140), channel_id=1, source_target_pairs={{0,4},{1,5},{2,6},{3,7},{4,0},{5,1},{6,2},{7,3},{8,12},{9,13},{10,... | collective-permute-start | bytes 393224 | tf_op jit(solution)/shard_map/ppermute | solution.py:279
  121.3 5.1 %collective-permute-start.30 = (bf16[256,256]{1,0:T(8,128)(2,1)S(1)}, bf16[256,256]{1,0:T(8,128)(2,1)S(1)}, u32[]{:S(2)}, u32[]{:S(2)}) collective-permute-start(bf16[256,256]{1,0:T(8,128)(2,1)S(1)} %get-tuple-element.131), channel_id=1, source_target_pairs={{0,8},{1,9},{2,10},{3,11},{4,12},{5,13},{6,14},{7,15},{8,0},{9,1},... | collective-permute-start | bytes 393224 | tf_op jit(solution)/shard_map/ppermute | solution.py:279
  121.6 7.8 %collective-permute-start.32 = (bf16[256,256]{1,0:T(8,128)(2,1)S(1)}, bf16[256,256]{1,0:T(8,128)(2,1)S(1)}, u32[]{:S(2)}, u32[]{:S(2)}) collective-permute-start(bf16[256,256]{1,0:T(8,128)(2,1)S(1)} %get-tuple-element.132), channel_id=1, source_target_pairs={{0,12},{1,13},{2,14},{3,15},{4,8},{5,9},{6,10},{7,11},{8,4},{9,5},... | collective-permute-start | bytes 393224 | tf_op jit(solution)/shard_map/ppermute | solution.py:279

commit v8 on v7

v8 whole, which is shorter than its diff:
```python
import functools

import jax
import jax.numpy as jnp
from jax import lax
from jax.experimental import pallas as pl
from jax.experimental.pallas import tpu as pltpu
from jax.sharding import PartitionSpec as P

HEAD_SIZE = 128
BLK = 128
MEMBERS = 4
META_ROWS = 16
HALF = META_ROWS // 2
AXES = ("seg", "fsdp")

VMEM = pl.BlockSpec(memory_space=pltpu.VMEM)
SMEM = pl.BlockSpec(memory_space=pltpu.SMEM)
ANY = pl.BlockSpec(memory_space=pl.ANY)
HBM = pl.BlockSpec(memory_space=pltpu.HBM)


def call(body, outs, in_specs, flops=0, scratch=(), out_spec=VMEM, limit=16 << 20):
    return pl.pallas_call(
        body,
        out_shape=outs,
        in_specs=in_specs,
        out_specs=[out_spec] * len(outs),
        scratch_shapes=list(scratch),
        compiler_params=pltpu.CompilerParams(vmem_limit_bytes=limit),
        cost_estimate=pl.CostEstimate(flops=flops, bytes_accessed=4 << 20, transcendentals=0),
    )


def aligned(offset):
    return pl.multiple_of(offset, HEAD_SIZE)


def pack_body(group, here_ref, valid_ref, mask_ref, wq_ref, wk_ref, wv_ref, *outs):
    rows, wide = wk_ref.shape[0], group * HEAD_SIZE
    row = lax.broadcasted_iota(jnp.int32, (META_ROWS, outs[0].shape[1]), 0)
    facts = jnp.where(row < HALF, valid_ref[0, 0], mask_ref[0, 0, 1, 0])
    facts = facts.astype(jnp.float32).astype(jnp.bfloat16)
    for k in range(MEMBERS):
        head, out = here_ref[1] ^ k, outs[k]
        at = aligned(head * HEAD_SIZE)
        out[:rows, :HEAD_SIZE] = wk_ref[:, pl.ds(at, HEAD_SIZE)]
        out[:rows, HEAD_SIZE : 2 * HEAD_SIZE] = wv_ref[:, pl.ds(at, HEAD_SIZE)]
        out[:rows, 2 * HEAD_SIZE :] = wq_ref[:, pl.ds(aligned(head * wide), wide)]
        out[rows:, :] = facts


def columns_of(tokens_ref, here_ref, piece, half, line):
    deep = MEMBERS * HEAD_SIZE // 2
    if not line:
        return tokens_ref[:, pl.ds((2 * piece + half) * deep, deep)]
    g, m, z = here_ref[0] ^ (piece // line), here_ref[1], here_ref[2]
    inside = (z == 1) | (z == 2)
    step = piece % line
    if step < 2:
        z = z ^ step
    else:
        z = jnp.where(inside, z ^ (5 - step), z ^ step)
    parts = [
        tokens_ref[:, pl.ds(aligned(((g * MEMBERS + (m ^ k)) * line + z) * HEAD_SIZE), HEAD_SIZE)]
        for k in (2 * half, 2 * half + 1)
    ]
    return jnp.concatenate(parts, axis=1)


def facts_of(message_ref):
    rows = message_ref.shape[0] - META_ROWS
    facts = message_ref[rows:, : 2 * HEAD_SIZE].astype(jnp.float32)
    return facts[0:1, :], facts[HALF : HALF + 1, :]


def iota(shape, dimension):
    return lax.broadcasted_iota(jnp.int32, shape, dimension).astype(jnp.float32)


def project_body(early, late, line, here_ref, *refs):
    tokens, pieces, outs = refs[:2], refs[2 : 2 + len(early)], refs[2 + len(early) :]
    length = tokens[0].shape[0]
    total = None
    for place, piece in zip(early, pieces):
        columns = jnp.concatenate([columns_of(one, here_ref, *place, line) for one in tokens], axis=0)
        term = jnp.dot(columns, piece[...], preferred_element_type=jnp.float32)
        total = term if total is None else total + term
    for n in range(2):
        outs[n][...] = total[n * length : (n + 1) * length]
        for k, place in enumerate(late):
            columns = columns_of(tokens[n], here_ref, *place, line)
            deep = columns.shape[1]
            outs[2 + n][:, k * deep : (k + 1) * deep] = columns


def sigma_plus(v):
    return jnp.where(v > 0, v + 1.0, jnp.exp(jnp.minimum(v, 0.0)))


def split(values):
    high = values.astype(jnp.bfloat16)
    return high, (values - high.astype(jnp.float32)).astype(jnp.bfloat16)


def late_rows(pieces, start):
    width = pieces[-1].shape[1]
    rows = [piece[:, start : start + width] for piece in pieces[:-1]]
    return jnp.concatenate(rows + [pieces[-1][...]], axis=0)


def kv_body(n_late, *refs):
    pieces, refs = refs[:n_late], refs[n_late:]
    sums, lates, messages = refs[:MEMBERS], refs[MEMBERS : 2 * MEMBERS], refs[2 * MEMBERS : 3 * MEMBERS]
    outs = refs[3 * MEMBERS :]
    rows = late_rows(pieces, 0)
    kvs = []
    for seg in range(MEMBERS):
        total = sums[seg][:, : 2 * HEAD_SIZE]
        total += jnp.dot(lates[seg][...], rows, preferred_element_type=jnp.float32)
        kvs.append(total.astype(jnp.bfloat16))
        outs[2 * seg][...] = kvs[seg]
    whole = None
    for seg, kv in enumerate(kvs):
        length = kv.shape[0]
        valid, _ = facts_of(messages[seg])
        keys = kv[:, :HEAD_SIZE].astype(jnp.float32)
        live = iota((length, HEAD_SIZE), 0) < valid[:, :HEAD_SIZE]
        sig = jnp.where(live, sigma_plus(keys), 0.0)
        wide = jnp.concatenate(
            [kv[:, HEAD_SIZE:], jnp.ones((length, HEAD_SIZE), jnp.bfloat16)], axis=1
        )
        high, low = split(sig)
        over = (((0,), (0,)), ((), ()))
        delta = lax.dot_general(high, wide, over, preferred_element_type=jnp.float32)
        delta += lax.dot_general(low, wide, over, preferred_element_type=jnp.float32)
        outs[2 * seg + 1][...] = delta
        whole = delta if whole is None else whole + delta
    outs[-1][...] = whole.astype(jnp.bfloat16)


def local_body(n, n_late, start, heads, *refs):
    pieces, refs = refs[:n_late], refs[n_late:]
    kvs, messages, sums, lates, outs = [refs[k * n : (k + 1) * n] for k in range(4)] + [refs[4 * n :]]
    rows = late_rows(pieces, start)
    columns = slice(start, start + heads * HEAD_SIZE)
    queries = []
    for at in range(n):
        total = sums[at][:, columns] + jnp.dot(
            lates[at][...], rows, preferred_element_type=jnp.float32
        )
        queries.append(total.astype(jnp.bfloat16))
        outs[2 * at][...] = queries[at]
    work = [(at, block) for at in range(n) for block in range(queries[0].shape[0] // BLK)]
    span = lambda block: slice(block * BLK, (block + 1) * BLK)
    scores = []
    for at, block in work:
        stacked = jnp.concatenate(
            [queries[at][span(block), h * HEAD_SIZE : (h + 1) * HEAD_SIZE] for h in range(heads)], axis=0
        )
        keys = kvs[at][0 : (block + 1) * BLK, :HEAD_SIZE]
        scores.append(
            lax.dot_general(
                stacked, keys, (((1,), (1,)), ((), ())), preferred_element_type=jnp.float32
            )
        )
    weights = []
    for (at, block), score in zip(work, scores):
        width = (block + 1) * BLK
        valid, seen = facts_of(messages[at])
        i, j = iota((BLK, width), 0) + block * BLK, iota((BLK, width), 1)
        limit = valid[:, :width]
        if block:
            limit = jnp.where((j[0:1] >= block * BLK) | (seen[:, :width] > 0), limit, 0.0)
        allowed = (j <= i) & (j < limit)
        masked = jnp.concatenate(
            [jnp.where(allowed, score[span(h)] * HEAD_SIZE ** (-0.5), -1e30) for h in range(heads)],
            axis=0,
        )
        top = jnp.max(masked, axis=-1, keepdims=True)
        expo = jnp.exp(masked - top)
        total = jnp.maximum(jnp.sum(expo, axis=-1, keepdims=True), 1.0)
        weights.append((expo * (1.0 / total)).astype(jnp.bfloat16))
    for (at, block), weight in zip(work, weights):
        values = kvs[at][0 : (block + 1) * BLK, HEAD_SIZE:]
        local = jnp.dot(weight, values, preferred_element_type=jnp.float32)
        for h in range(heads):
            outs[2 * at + 1][span(block), h * HEAD_SIZE : (h + 1) * HEAD_SIZE] = local[span(h)]


def mix_body(segs, parts, group, here_ref, gate_ref, base_ref, *refs):
    deltas, messages, refs = refs[:MEMBERS], refs[MEMBERS : MEMBERS + len(segs)], refs[MEMBERS + len(segs) :]
    n = len(segs) * len(parts)
    queries, locals_, outs = refs[:n], refs[n : 2 * n], refs[2 * n :]
    me = here_ref[1]
    heads = queries[0].shape[1] // HEAD_SIZE
    length = queries[0].shape[0]
    work = [(at, p, h) for at in range(len(segs)) for p in range(len(parts)) for h in range(heads)]
    memories = []
    for seg in segs:
        memory = base_ref[...].astype(jnp.float32)
        for other in range(MEMBERS):
            if other != seg:
                earlier = jnp.where((me ^ other) < (me ^ seg), 1.0, 0.0)
                memory = memory + earlier * deltas[other][...]
        memories.append(split(memory))
    columns = lambda h: slice(h * HEAD_SIZE, (h + 1) * HEAD_SIZE)
    numers = []
    for at, p, h in work:
        mem_high, mem_low = memories[at]
        high, low = split(sigma_plus(queries[at * len(parts) + p][:, columns(h)].astype(jnp.float32)))
        numer = jnp.dot(high, mem_high, preferred_element_type=jnp.float32)
        numer += jnp.dot(high, mem_low, preferred_element_type=jnp.float32)
        numer += jnp.dot(low, mem_high, preferred_element_type=jnp.float32)
        numers.append(numer)
    for (at, p, h), numer in zip(work, numers):
        valid, _ = facts_of(messages[at])
        live = iota((length, HEAD_SIZE), 0) < valid[:, :HEAD_SIZE]
        retrieved = numer[:, :HEAD_SIZE] / (numer[:, HEAD_SIZE:] + 1.0)
        logit = jnp.full((1, HEAD_SIZE), gate_ref[me * group + parts[p] * heads + h], jnp.float32)
        gate = 1.0 / (1.0 + jnp.exp(-logit))
        mixed = gate * retrieved + (1.0 - gate) * locals_[at * len(parts) + p][:, columns(h)]
        outs[at * len(parts) + p][:, columns(h)] = jnp.where(live, mixed, 0.0).astype(jnp.bfloat16)


def assemble_body(counts, here_ref, *refs):
    parts, out = list(refs[:-1]), refs[-1]
    width = out.shape[1] // MEMBERS
    for k, count in enumerate(counts):
        for c in range(count):
            at = (here_ref[1] ^ k) * width + c * (width // count)
            out[:, pl.ds(aligned(at), width // count)] = parts.pop(0)[...]


def after(array, *others):
    return lax.optimization_barrier((array,) + others)[0]


def shards(sizes, tokens, w_query, w_key, value_weight, gate_bias, block_mask, valid_len):
    n_seg, n_z = sizes
    n_groups = n_seg // MEMBERS
    heads_kv = w_key.shape[1] // HEAD_SIZE
    group = w_query.shape[1] // w_key.shape[1]
    rows = w_query.shape[0]
    length, width = tokens.shape[1], tokens.shape[2]
    assert heads_kv == MEMBERS and group == 4 and length == 2 * BLK
    seg = lax.axis_index("seg")
    z = lax.axis_index("fsdp")
    g, m = seg // MEMBERS, seg % MEMBERS
    here = jnp.stack([g, m, z]).astype(jnp.int32)
    bf16, f32 = jnp.bfloat16, jnp.float32
    shape = jax.ShapeDtypeStruct

    def permute(array, to):
        pairs = []
        for gg in range(n_groups):
            for mm in range(MEMBERS):
                for zz in range(n_z):
                    target = to(gg, mm, zz)
                    if target is not None:
                        index = lambda t: (t[0] * MEMBERS + t[1]) * n_z + t[2]
                        pairs.append((index((gg, mm, zz)), index(target)))
        return lax.ppermute(array, AXES, pairs)

    def to_member(array, k):
        return permute(array, lambda gg, mm, zz: (gg, mm ^ k, zz))

    wide = (2 + group) * HEAD_SIZE
    packed = call(
        functools.partial(pack_body, group),
        [shape((rows + META_ROWS, wide), bf16)] * MEMBERS,
        [SMEM] * 3 + [VMEM] * 3,
    )(here, valid_len, block_mask, w_query, w_key, value_weight)
    messages = [packed[0], *[to_member(packed[k], k) for k in (1, 2, 3)]]

    def gathered(piece):
        index = lambda gg, mm, zz: (gg * MEMBERS + mm) * n_z + zz
        everything = lax.all_gather(
            piece,
            AXES,
            axis_index_groups=[
                [index(gg, mm, zz) for gg in range(n_groups) for zz in range(n_z)]
                for mm in range(MEMBERS)
            ],
        )
        columns = piece.shape[1]
        natural = everything.reshape(n_groups, n_z, MEMBERS, rows, columns)
        members = jnp.arange(MEMBERS, dtype=jnp.int32) ^ m
        natural = jnp.take(natural, members, axis=2).transpose(0, 2, 1, 3, 4)
        return list(natural.reshape(-1, MEMBERS * HEAD_SIZE, columns))

    pieces = [
        jnp.concatenate([messages[k][:rows] for k in members], axis=0) for members in ((0, 1), (2, 3))
    ]
    n_pieces = width // (MEMBERS * HEAD_SIZE)
    sums, lates = [None] * MEMBERS, [None] * MEMBERS

    def project(segs, early, late, halves, line):
        deep = MEMBERS * HEAD_SIZE // 2
        found = call(
            functools.partial(project_body, early, late, line),
            [shape((length, wide), f32)] * 2 + [shape((length, len(late) * deep), bf16)] * 2,
            [SMEM] + [VMEM] * (2 + len(early)),
            flops=2 * 2 * length * len(early) * deep * wide,
        )(here, *[books[s] for s in segs], *[halves[half][piece] for piece, half in early])
        for at, s in enumerate(segs):
            sums[s], lates[s] = found[at], found[2 + at]

    if n_groups == 2 and n_z == 4:
        assert rows == HEAD_SIZE
        inside = (z == 1) | (z == 2)
        over = lambda part: permute(part, lambda gg, mm, zz: (gg ^ 1, mm, zz))
        pair = lambda part: permute(part, lambda gg, mm, zz: (gg, mm, zz ^ 1))
        outward = lambda part: permute(
            part, lambda gg, mm, zz: (gg, mm, zz ^ 1) if zz in (1, 2) else None
        )
        inward = lambda part: permute(
            part, lambda gg, mm, zz: (gg, mm, zz ^ 3) if zz in (1, 2) else None
        )
        locked = lambda *parts: lax.optimization_barrier(parts)
        stage1 = lambda piece: (pair(piece), inward(piece), over(piece))
        stage2 = lambda one, inner: (inward(one), outward(inner), over(one))
        stage3 = lambda middle, two: (outward(middle), over(two))

        a, b, own, sibling = locked(*pieces, tokens[0], to_member(tokens[0], 1))
        across = to_member(own, 2)
        a_one, a_inner, a_far0 = locked(*stage1(a))
        b_one, b_inner, b_far0 = locked(*stage1(b))
        a_middle, a_outer, a_far1 = locked(*stage2(a_one, a_inner))
        b_middle, b_outer, b_far1 = locked(*stage2(b_one, b_inner))
        a_two = jnp.where(inside, a_inner, a_outer)
        a_last, a_far2 = stage3(a_middle, a_two)
        b_two = jnp.where(inside, b_inner, b_outer)
        b_last, b_far2 = stage3(b_middle, b_two)
        a_last, a_far2, a_middle = locked(a_last, a_far2, a_middle)
        a_three = jnp.where(inside, a_middle, a_last)
        a_far3 = over(a_three)
        books = [own, sibling]
        upper = [a, a_one, a_two, a_three, a_far0, a_far1, a_far2]
        lower = [b, b_one, b_two, None, b_far0, b_far1]
        late = [(7, 0), (3, 1), (6, 1), (7, 1)]
        early = [(k, half) for half in range(2) for k in range(8) if (k, half) not in late]
        project((0, 1), early, late, (upper, lower), n_z)
        b_last, b_far2, b_middle, sums[0], sums[1], across = locked(
            b_last, b_far2, b_middle, sums[0], sums[1], after(across, a_last, a_far2)
        )
        books += [across, to_member(across, 1)]
        project((2, 3), early, late, (upper, lower), n_z)
        b_three = jnp.where(inside, b_middle, b_last)
        pieces = [a_far3, b_three, b_far2]
        finish = lambda at, *others: over(after(b_three[:, at], *others))
    else:
        across, sibling = to_member(tokens[0], 2), to_member(tokens[0], 1)
        books = [tokens[0], sibling, across, to_member(across, 1)]
        full = gathered(jnp.concatenate(pieces, axis=0))
        deep = MEMBERS * HEAD_SIZE // 2
        upper, lower = [part[:deep] for part in full], [part[deep:] for part in full]
        late = [(n_pieces - 1, 0), (n_pieces - 1, 1)]
        early = [(k, half) for half in range(2) for k in range(n_pieces - 1)]
        for segs in ((0, 1), (2, 3)):
            project(segs, early, late, (upper, lower), 0)
        pieces = [upper[-1]]
        finish = lambda at, *others: lower[-1][:, at]

    halves = [slice(k * HEAD_SIZE, (k + 2) * HEAD_SIZE) for k in (0, 2, 4)]
    lower_kv, lower_q0 = finish(halves[0]), finish(halves[1])
    found = call(
        functools.partial(kv_body, len(pieces) + 1),
        [shape((length, 2 * HEAD_SIZE), bf16), shape((HEAD_SIZE, 2 * HEAD_SIZE), f32)] * MEMBERS
        + [shape((HEAD_SIZE, 2 * HEAD_SIZE), bf16)],
        [VMEM] * (len(pieces) + 1 + 3 * MEMBERS),
        flops=2 * MEMBERS * length * len(late) * MEMBERS * HEAD_SIZE * HEAD_SIZE,
    )(*pieces, lower_kv, *sums, *lates, *messages)
    kvs, deltas, total = found[0:-1:2], found[1:-1:2], found[-1]

    base = None
    for a in range(1, n_groups):
        term = permute(total, lambda gg, mm, zz: (gg ^ a, mm, zz) if gg < gg ^ a else None)
        base = term if base is None else base.astype(f32) + term.astype(f32)

    lower_q1 = finish(halves[2], total)
    half = group // 2

    def local(segs, part, lower_q):
        found = call(
            functools.partial(local_body, len(segs), len(pieces) + 1, halves[1 + part].start, half),
            [shape((length, half * HEAD_SIZE), bf16), shape((length, half * HEAD_SIZE), f32)] * len(segs),
            [VMEM] * (len(pieces) + 1 + 4 * len(segs)),
            flops=4 * len(segs) * length * length * half * HEAD_SIZE,
        )(*pieces, lower_q, *[one[s] for one in (kvs, messages, sums, lates) for s in segs])
        return {(s, part): (found[2 * at], found[2 * at + 1]) for at, s in enumerate(segs)}

    def mix(segs, parts, base, ready):
        keys = [(s, part) for s in segs for part in parts]
        return call(
            functools.partial(mix_body, segs, parts, group),
            [shape((length, half * HEAD_SIZE), bf16)] * len(keys),
            [SMEM] * 2 + [VMEM] * (1 + MEMBERS + len(segs) + 2 * len(keys)),
            flops=2 * len(keys) * length * half * HEAD_SIZE * HEAD_SIZE * 6,
        )(
            here, gate_bias, base, *deltas, *[messages[s] for s in segs],
            *[ready[key][0] for key in keys], *[ready[key][1] for key in keys],
        )

    ready = local((2, 3, 1, 0), 0, lower_q0)
    base = after(base, *ready[2, 0])
    two0, three0 = mix((2, 3), (0,), base, ready)
    ready |= local((2, 3), 1, after(lower_q1, two0, three0))
    two1, three1 = mix((2, 3), (1,), base, ready)
    ready |= local((1, 0), 1, after(lower_q1, two1, three1))
    one0, one1, mine0, mine1 = mix((1, 0), (0, 1), after(base, two1, three1), ready)
    sent = [mine0, mine1]
    for k, parts in ((1, (one0, one1)), (2, (two0, two1)), (3, (three0, three1))):
        sent += [to_member(part, k) for part in parts]
    (output,) = call(
        functools.partial(assemble_body, (2,) * MEMBERS),
        [shape((length, w_query.shape[1]), bf16)],
        [SMEM] + [VMEM] * len(sent),
    )(here, *sent)
    return output[None]


def solution(mesh):
    in_specs = (
        P("fsdp", "seg", None),
        P(("seg", "fsdp"), None),
        P(("seg", "fsdp"), None),
        P(("seg", "fsdp"), None),
        P(),
        P("fsdp", "seg", None, None),
        P("fsdp", "seg"),
    )
    out_specs = P("fsdp", "seg", None)
    body = functools.partial(shards, (mesh.shape["seg"], mesh.shape["fsdp"]))
    return jax.shard_map(body, mesh=mesh, in_specs=in_specs, out_specs=out_specs, check_vma=False)
```

time: 133 us -> 120 us (0.902)
  Pallas kernels: 32.7 us -> 20.9 us
  local copies, waits for them, and re-layouts: 5.81 us -> 3.62 us
  starting transfers between devices: 50.6 us -> 52.2 us
    pallas_call x9, Pallas kernels: 30.4 us -> 18.7 us  [the longest x2 10 us: project(): call(functools.partial(project_body, early, late, line), [shape((length,...]
    unnamed x26 -> x12, local copies, waits for them, and re-layouts: 5.73 us -> 3.54 us
    ppermute x33, starting transfers between devices: 50.6 us -> 52.2 us  [permute(): return lax.ppermute(array, AXES, pairs)]
  transfers between devices with their start and end apart: 33 -> 33, of which waited for: 12 -> 18; matrix products, arithmetic and copies ran while one was open for 3% -> 4% of each run, Pallas kernels for 24% -> 16%
where the time goes in v8:
time: 120 us; the launch traced here: 119 us
  starting transfers between devices  52.2 us (44%)
  waiting for transfers between devices  36.5 us (30%)
  Pallas kernels  20.9 us (17%)
  other arithmetic  4.35 us (4%)
  local copies, waits for them, and re-layouts  3.62 us (3%)
    ppermute x33, starting transfers between devices, permute(): return lax.ppermute(array, AXES, pairs)  52.2 us
    ppermute x33, waiting for transfers between devices, permute(): return lax.ppermute(array, AXES, pairs)  36.5 us
    pallas_call x2, Pallas kernels, project(): call(functools.partial(project_body, early, late, line), [shape((length,...  10 us
    pallas_call x3, Pallas kernels, mix(): call(functools.partial(mix_body, segs, parts, group), [shape((length, hal...  3.95 us
    pallas_call x3, Pallas kernels, local(): call(functools.partial(local_body, len(segs), len(pieces) + 1, halves[1 +...  3.59 us
    unnamed x12, local copies, waits for them, and re-layouts  3.54 us
  transfers between devices with their start and end apart: 33, of which 18 were waited for; matrix products, arithmetic and copies ran while one was open for 4% of the time, Pallas kernels for 16%

profile of v8, /device:TPU:9, one launch (start us, length us, event | category | flops | bytes accessed | tf_op | source)
XLA Modules:
  0.0 118.5 jit_solution(4197141664077093634)
XLA Ops:
  0.0 0.7 collective-permute-start.3
  1.4 1.0 copy-done
  2.5 0.9 copy-done.1
  3.4 0.9 copy-done.2
  4.3 0.7 copy-done.4
  4.9 0.6 shard_map.73
  5.6 1.3 %collective-permute-start.1 = (bf16[144,768]{1,0:T(8,128)(2,1)S(1)}, bf16[144,768]{1,0:T(8,128)(2,1)S(1)}, u32[]{:S(2)}, u32[]{:S(2)}) collective-permute-start(bf16[144,768]{1,0:T(8,128)(2,1)S(1)} %get-tuple-element.83), channel_id=1, source_target_pairs={{0,8},{1,9},{2,10},{3,11},{4,12},{5,13},{6,14},{7,15},{8,0},{9,1},... | collective-permute-start | bytes 663560 | tf_op jit(solution)/shard_map/ppermute | solution.py:263
  6.9 0.4 collective-permute-start.2
  7.3 0.2 collective-permute-start
  7.5 5.2 %collective-permute-done.1.refs_14_.refs_8_.refs_4_.refs_6_ = bf16[144,768]{1,0:T(8,128)(2,1)S(1)} collective-permute-done((bf16[144,768]{1,0:T(8,128)(2,1)S(1)}, bf16[144,768]{1,0:T(8,128)(2,1)S(1)}, u32[]{:S(2)}, u32[]{:S(2)}) %collective-permute-start.1) | collective-permute-done | bytes 221216 | tf_op jit(solution)/shard_map/ppermute | solution.py:263
  12.7 4.8 %collective-permute-done.2.refs_15_.refs_9_.refs_5_.refs_7_ = bf16[144,768]{1,0:T(8,128)(2,1)S(1)} collective-permute-done((bf16[144,768]{1,0:T(8,128)(2,1)S(1)}, bf16[144,768]{1,0:T(8,128)(2,1)S(1)}, u32[]{:S(2)}, u32[]{:S(2)}) %collective-permute-start.2) | collective-permute-done | bytes 221216 | tf_op jit(solution)/shard_map/ppermute | solution.py:263
  17.8 1.4 %collective-permute-start.21 = (bf16[256,4096]{1,0:T(8,128)(2,1)}, bf16[256,4096]{1,0:T(8,128)(2,1)}, u32[]{:S(2)}, u32[]{:S(2)}) collective-permute-start(bf16[256,4096]{1,0:T(8,128)(2,1)} %bitcast.3.refs_0_), channel_id=1, source_target_pairs={{0,8},{1,9},{2,10},{3,11},{4,12},{5,13},{6,14},{7,15},{8,0},{9,1},... | collective-permute-start | bytes 6291464 | tf_op jit(solution)/shard_map/ppermute | solution.py:263
  19.1 4.3 %collective-permute-start.5 = (bf16[256,768]{1,0:T(8,128)(2,1)S(1)}, bf16[256,768]{1,0:T(8,128)(2,1)}, u32[]{:S(2)}, u32[]{:S(2)}) collective-permute-start(bf16[256,768]{1,0:T(8,128)(2,1)S(1)} %pad_maximum_fusion.refs_2_), channel_id=1, source_target_pairs={{1,2},{2,1},{5,6},{6,5},{9,10},{10,9},{13,14},{14,13},{17,18},{18,... | collective-permute-start | bytes 1179656 | tf_op jit(solution)/shard_map/ppermute | solution.py:263
  23.5 1.3 %collective-permute-start.6 = (bf16[256,768]{1,0:T(8,128)(2,1)S(1)}, bf16[256,768]{1,0:T(8,128)(2,1)S(1)}, u32[]{:S(2)}, u32[]{:S(2)}) collective-permute-start(bf16[256,768]{1,0:T(8,128)(2,1)S(1)} %pad_maximum_fusion.refs_2_), channel_id=1, source_target_pairs={{0,16},{1,17},{2,18},{3,19},{4,20},{5,21},{6,22},{7,23},{8,24},{9,... | collective-permute-start | bytes 1179656 | tf_op jit(solution)/shard_map/ppermute | solution.py:263
  24.8 3.5 %collective-permute-done.4.refs_3_ = bf16[256,768]{1,0:T(8,128)(2,1)S(1)} collective-permute-done((bf16[256,768]{1,0:T(8,128)(2,1)S(1)}, bf16[256,768]{1,0:T(8,128)(2,1)S(1)}, u32[]{:S(2)}, u32[]{:S(2)}) %collective-permute-start.4) | collective-permute-done | bytes 393248 | tf_op jit(solution)/shard_map/ppermute | solution.py:263
  28.3 3.2 %collective-permute-start.14 = (bf16[256,768]{1,0:T(8,128)(2,1)S(1)}, bf16[256,768]{1,0:T(8,128)(2,1)S(1)}, u32[]{:S(2)}, u32[]{:S(2)}) collective-permute-start(bf16[256,768]{1,0:T(8,128)(2,1)S(1)} %pad_maximum_fusion.1.refs_9_), channel_id=1, source_target_pairs={{1,2},{2,1},{5,6},{6,5},{9,10},{10,9},{13,14},{14,13},{17,18},{18,... | collective-permute-start | bytes 1179656 | tf_op jit(solution)/shard_map/ppermute | solution.py:263
  31.5 0.7 collective-permute-done.5
  32.2 1.2 %collective-permute-start.15 = (bf16[256,768]{1,0:T(8,128)(2,1)S(1)}, bf16[256,768]{1,0:T(8,128)(2,1)S(1)}, u32[]{:S(2)}, u32[]{:S(2)}) collective-permute-start(bf16[256,768]{1,0:T(8,128)(2,1)S(1)} %pad_maximum_fusion.1.refs_9_), channel_id=1, source_target_pairs={{0,16},{1,17},{2,18},{3,19},{4,20},{5,21},{6,22},{7,23},{8,24},{9,... | collective-permute-start | bytes 1179656 | tf_op jit(solution)/shard_map/ppermute | solution.py:263
  33.4 3.0 %collective-permute-start.7 = (bf16[256,768]{1,0:T(8,128)(2,1)S(1)}, bf16[256,768]{1,0:T(8,128)(2,1)}, u32[]{:S(2)}, u32[]{:S(2)}) collective-permute-start(bf16[256,768]{1,0:T(8,128)(2,1)S(1)} %collective-permute-done.4.refs_3_), channel_id=1, source_target_pairs={{1,2},{2,1},{5,6},{6,5},{9,10},{10,9},{13,14},{14,13},{17,18},{18,... | collective-permute-start | bytes 1179656 | tf_op jit(solution)/shard_map/ppermute | solution.py:263
  36.5 0.2 collective-permute-done.13.refs_10_
  36.7 2.6 %collective-permute-start.8 = (bf16[256,768]{1,0:T(8,128)(2,1)}, bf16[256,768]{1,0:T(8,128)(2,1)}, u32[]{:S(2)}, u32[]{:S(2)}) collective-permute-start(bf16[256,768]{1,0:T(8,128)(2,1)} %collective-permute-done.5), channel_id=1, source_target_pairs={{1,0},{2,3},{5,4},{6,7},{9,8},{10,11},{13,12},{14,15},{17,16},{18,... | collective-permute-start | bytes 1179656 | tf_op jit(solution)/shard_map/ppermute | solution.py:263
  39.3 0.4 collective-permute-done.14
  39.6 1.2 %collective-permute-start.9 = (bf16[256,768]{1,0:T(8,128)(2,1)S(1)}, bf16[256,768]{1,0:T(8,128)(2,1)}, u32[]{:S(2)}, u32[]{:S(2)}) collective-permute-start(bf16[256,768]{1,0:T(8,128)(2,1)S(1)} %collective-permute-done.4.refs_3_), channel_id=1, source_target_pairs={{0,16},{1,17},{2,18},{3,19},{4,20},{5,21},{6,22},{7,23},{8,24},{9,... | collective-permute-start | bytes 1179656 | tf_op jit(solution)/shard_map/ppermute | solution.py:263
  40.9 0.4 collective-permute-done.15.refs_12_
  41.2 3.8 %collective-permute-start.16 = (bf16[256,768]{1,0:T(8,128)(2,1)S(1)}, bf16[256,768]{1,0:T(8,128)(2,1)}, u32[]{:S(2)}, u32[]{:S(2)}) collective-permute-start(bf16[256,768]{1,0:T(8,128)(2,1)S(1)} %collective-permute-done.13.refs_10_), channel_id=1, source_target_pairs={{1,2},{2,1},{5,6},{6,5},{9,10},{10,9},{13,14},{14,13},{17,18},{18,... | collective-permute-start | bytes 1179656 | tf_op jit(solution)/shard_map/ppermute | solution.py:263
  45.1 3.0 %collective-permute-done.7 = bf16[256,768]{1,0:T(8,128)(2,1)} collective-permute-done((bf16[256,768]{1,0:T(8,128)(2,1)S(1)}, bf16[256,768]{1,0:T(8,128)(2,1)}, u32[]{:S(2)}, u32[]{:S(2)}) %collective-permute-start.7) | collective-permute-done | bytes 393248 | tf_op jit(solution)/shard_map/ppermute | solution.py:263
  48.1 2.0 %collective-permute-start.17 = (bf16[256,768]{1,0:T(8,128)(2,1)}, bf16[256,768]{1,0:T(8,128)(2,1)}, u32[]{:S(2)}, u32[]{:S(2)}) collective-permute-start(bf16[256,768]{1,0:T(8,128)(2,1)} %copy-done.5), channel_id=1, source_target_pairs={{1,0},{2,3},{5,4},{6,7},{9,8},{10,11},{13,12},{14,15},{17,16},{18,... | collective-permute-start | bytes 1179656 | tf_op jit(solution)/shard_map/ppermute | solution.py:263
  50.1 1.2 %collective-permute-start.18 = (bf16[256,768]{1,0:T(8,128)(2,1)S(1)}, bf16[256,768]{1,0:T(8,128)(2,1)}, u32[]{:S(2)}, u32[]{:S(2)}) collective-permute-start(bf16[256,768]{1,0:T(8,128)(2,1)S(1)} %collective-permute-done.13.refs_10_), channel_id=1, source_target_pairs={{0,16},{1,17},{2,18},{3,19},{4,20},{5,21},{6,22},{7,23},{8,24},{9,... | collective-permute-start | bytes 1179656 | tf_op jit(solution)/shard_map/ppermute | solution.py:263
  51.3 1.0 broadcast_select_fusion.3.refs_4_
  52.4 0.3 collective-permute-start.11
  52.7 3.8 %collective-permute-done.16 = bf16[256,768]{1,0:T(8,128)(2,1)} collective-permute-done((bf16[256,768]{1,0:T(8,128)(2,1)S(1)}, bf16[256,768]{1,0:T(8,128)(2,1)}, u32[]{:S(2)}, u32[]{:S(2)}) %collective-permute-start.16) | collective-permute-done | bytes 393248 | tf_op jit(solution)/shard_map/ppermute | solution.py:263
  56.5 1.3 %collective-permute-start.10 = (bf16[256,768]{1,0:T(8,128)(2,1)}, bf16[256,768]{1,0:T(8,128)(2,1)S(1)}, u32[]{:S(2)}, u32[]{:S(2)}) collective-permute-start(bf16[256,768]{1,0:T(8,128)(2,1)} %collective-permute-done.7), channel_id=1, source_target_pairs={{1,0},{2,3},{5,4},{6,7},{9,8},{10,11},{13,12},{14,15},{17,16},{18,... | collective-permute-start | bytes 1179656 | tf_op jit(solution)/shard_map/ppermute | solution.py:263
  57.8 1.1 broadcast_select_fusion.1.refs_11_
  58.9 1.3 %collective-permute-start.20 = (bf16[256,768]{1,0:T(8,128)(2,1)S(1)}, bf16[256,768]{1,0:T(8,128)(2,1)S(1)}, u32[]{:S(2)}, u32[]{:S(2)}) collective-permute-start(bf16[256,768]{1,0:T(8,128)(2,1)S(1)} %broadcast_select_fusion.1.refs_11_), channel_id=1, source_target_pairs={{0,16},{1,17},{2,18},{3,19},{4,20},{5,21},{6,22},{7,23},{8,24},{9,... | collective-permute-start | bytes 1179656 | tf_op jit(solution)/shard_map/ppermute | solution.py:263
  60.2 1.5 %collective-permute-start.19 = (bf16[256,768]{1,0:T(8,128)(2,1)}, bf16[256,768]{1,0:T(8,128)(2,1)S(1)}, u32[]{:S(2)}, u32[]{:S(2)}) collective-permute-start(bf16[256,768]{1,0:T(8,128)(2,1)} %collective-permute-done.16), channel_id=1, source_target_pairs={{1,0},{2,3},{5,4},{6,7},{9,8},{10,11},{13,12},{14,15},{17,16},{18,... | collective-permute-start | bytes 1179656 | tf_op jit(solution)/shard_map/ppermute | solution.py:263
  61.7 3.2 %collective-permute-done.11.refs_8_ = bf16[256,768]{1,0:T(8,128)(2,1)S(1)} collective-permute-done((bf16[256,768]{1,0:T(8,128)(2,1)S(1)}, bf16[256,768]{1,0:T(8,128)(2,1)S(1)}, u32[]{:S(2)}, u32[]{:S(2)}) %collective-permute-start.11) | collective-permute-done | bytes 393248 | tf_op jit(solution)/shard_map/ppermute | solution.py:263
  64.9 0.2 collective-permute-done.10
  65.1 1.1 broadcast_select_fusion.2.refs_5_
  66.1 5.3 %shard_map.74 = (f32[256,768]{1,0:T(8,128)S(1)}, f32[256,768]{1,0:T(8,128)S(1)}, bf16[256,1024]{1,0:T(8,128)(2,1)S(1)}, bf16[256,1024]{1,0:T(8,128)(2,1)S(1)}) custom-call(s32[3]{0:T(128)S(1)} %pad_add_fusion.here_ref, bf16[256,4096]{1,0:T(8,128)(2,1)} %bitcast.3.refs_0_, bf16[256,4096]{1,0:T(8,128)(2,1)} %collective-permute-done.3.refs_1_, ...), custom_call_target="tpu_custom_call" | custom-call | flops 2415919104 | bytes 4194304 | tf_op jit(solution)/shard_map/pallas_call | solution.py:300
  71.4 1.8 %collective-permute-done.20.refs_2_ = bf16[256,768]{1,0:T(8,128)(2,1)S(1)} collective-permute-done((bf16[256,768]{1,0:T(8,128)(2,1)S(1)}, bf16[256,768]{1,0:T(8,128)(2,1)S(1)}, u32[]{:S(2)}, u32[]{:S(2)}) %collective-permute-start.20) | collective-permute-done | bytes 393248 | tf_op jit(solution)/shard_map/ppermute | solution.py:263
  73.2 7.5 %collective-permute-start.23 = (bf16[256,4096]{1,0:T(8,128)(2,1)}, bf16[256,4096]{1,0:T(8,128)(2,1)S(1)}, u32[]{:S(2)}, u32[]{:S(2)}) collective-permute-start(bf16[256,4096]{1,0:T(8,128)(2,1)} %collective-permute-done.21.refs_0_), channel_id=1, source_target_pairs={{0,4},{1,5},{2,6},{3,7},{4,0},{5,1},{6,2},{7,3},{8,12},{9,13},{10,... | collective-permute-start | bytes 6291464 | tf_op jit(solution)/shard_map/ppermute | solution.py:263
  80.7 1.3 %collective-permute-start.12 = (bf16[256,768]{1,0:T(8,128)(2,1)S(1)}, bf16[256,768]{1,0:T(8,128)(2,1)S(1)}, u32[]{:S(2)}, u32[]{:S(2)}) collective-permute-start(bf16[256,768]{1,0:T(8,128)(2,1)S(1)} %broadcast_select_fusion.2.refs_5_), channel_id=1, source_target_pairs={{0,16},{1,17},{2,18},{3,19},{4,20},{5,21},{6,22},{7,23},{8,24},{9,... | collective-permute-start | bytes 1179656 | tf_op jit(solution)/shard_map/ppermute | solution.py:263
  82.0 1.1 broadcast_select_fusion.refs_1_
  83.1 0.3 collective-permute-start.22
  83.4 1.2 %collective-permute-start.25 = (bf16[256,256]{1,0:T(8,128)(2,1)S(1)}, bf16[256,256]{1,0:T(8,128)(2,1)S(1)}, u32[]{:S(2)}, u32[]{:S(2)}) collective-permute-start(bf16[256,256]{1,0:T(8,128)(2,1)S(1)} %get-tuple-element.158), channel_id=1, source_target_pairs={{0,16},{1,17},{2,18},{3,19},{4,20},{5,21},{6,22},{7,23},{8,24},{9,... | collective-permute-start | bytes 393224 | tf_op jit(solution)/shard_map/ppermute | solution.py:263
  84.7 4.7 %shard_map.75 = (f32[256,768]{1,0:T(8,128)S(1)}, f32[256,768]{1,0:T(8,128)S(1)}, bf16[256,1024]{1,0:T(8,128)(2,1)S(1)}, bf16[256,1024]{1,0:T(8,128)(2,1)S(1)}) custom-call(s32[3]{0:T(128)S(1)} %pad_add_fusion.here_ref, bf16[256,4096]{1,0:T(8,128)(2,1)} %collective-permute-done.21.refs_0_, bf16[256,4096]{1,0:T(8,128)(2,1)S(1)} %collective-permute-done.23.refs_1_, ...), custom_call_target="tpu_custom_call" | custom-call | flops 2415919104 | bytes 4194304 | tf_op jit(solution)/shard_map/pallas_call | solution.py:300
  89.5 2.0 %collective-permute-done.12.refs_0_ = bf16[256,768]{1,0:T(8,128)(2,1)S(1)} collective-permute-done((bf16[256,768]{1,0:T(8,128)(2,1)S(1)}, bf16[256,768]{1,0:T(8,128)(2,1)S(1)}, u32[]{:S(2)}, u32[]{:S(2)}) %collective-permute-start.12) | collective-permute-done | bytes 393248 | tf_op jit(solution)/shard_map/ppermute | solution.py:263
  91.4 2.8 %collective-permute-done.22.refs_3_ = bf16[256,256]{1,0:T(8,128)(2,1)S(1)} collective-permute-done((bf16[256,256]{1,0:T(8,128)(2,1)S(1)}, bf16[256,256]{1,0:T(8,128)(2,1)S(1)}, u32[]{:S(2)}, u32[]{:S(2)}) %collective-permute-start.22) | collective-permute-done | bytes 131104 | tf_op jit(solution)/shard_map/ppermute | solution.py:263
  94.2 1.1 shard_map.76
  95.4 3.3 %collective-permute-start.24 = (bf16[128,256]{1,0:T(8,128)(2,1)S(1)}, bf16[128,256]{1,0:T(8,128)(2,1)S(1)}, u32[]{:S(2)}, u32[]{:S(2)}) collective-permute-start(bf16[128,256]{1,0:T(8,128)(2,1)S(1)} %get-tuple-element.119), channel_id=1, source_target_pairs={{0,16},{1,17},{2,18},{3,19},{4,20},{5,21},{6,22},{7,23},{8,24},{9,... | collective-permute-start | bytes 196616 | tf_op jit(solution)/shard_map/ppermute | solution.py:263
  98.8 1.6 %shard_map.77 = (bf16[256,256]{1,0:T(8,128)(2,1)S(1)}, f32[256,256]{1,0:T(8,128)S(1)}, bf16[256,256]{1,0:T(8,128)(2,1)S(1)}, f32[256,256]{1,0:T(8,128)S(1)}, bf1...) custom-call(bf16[256,768]{1,0:T(8,128)(2,1)S(1)} %collective-permute-, ...), custom_call_target="tpu_custom_call" | custom-call | flops 268435456 | bytes 4194304 | tf_op jit(solution)/shard_map/pallas_call | solution.py:385
  100.4 1.2 shard_map.78
  101.5 0.8 collective-permute-start.29
  102.3 2.8 %collective-permute-start.31 = (bf16[256,256]{1,0:T(8,128)(2,1)S(1)}, bf16[256,256]{1,0:T(8,128)(2,1)S(1)}, u32[]{:S(2)}, u32[]{:S(2)}) collective-permute-start(bf16[256,256]{1,0:T(8,128)(2,1)S(1)} %get-tuple-element.135), channel_id=1, source_target_pairs={{0,12},{1,13},{2,14},{3,15},{4,8},{5,9},{6,10},{7,11},{8,4},{9,5},... | collective-permute-start | bytes 393224 | tf_op jit(solution)/shard_map/ppermute | solution.py:263
  105.1 1.0 shard_map.79
  106.1 1.2 shard_map.80
  107.3 0.8 collective-permute-start.30
  108.0 1.0 shard_map.81
  109.1 1.6 %shard_map.82 = (bf16[256,256]{1,0:T(8,128)(2,1)S(1)}, bf16[256,256]{1,0:T(8,128)(2,1)S(1)}, bf16[256,256]{1,0:T(8,128)(2,1)S(1)}, bf16[256,256]{1,0:T(8,128)(2,1)S(1)}) custom-call(s32[3]{0:T(128)S(1)} %pad_add_fusion.here_ref, f32[16]{0:T(128)S(1)} %copy-done.3, bf16[128,256]{1,0:T(8,128)(2,1)S(1)} %collective-permute-done.24.base_ref, ...), custom_call_target="tpu_custom_call" | custom-call | flops 402653184 | bytes 4194304 | tf_op jit(solution)/shard_map/pallas_call | solution.py:395
  110.7 0.6 collective-permute-start.27
  111.3 1.1 collective-permute-start.32
  112.6 0.3 collective-permute-done.30.refs_5_
  112.9 4.0 %collective-permute-done.32.refs_7_ = bf16[256,256]{1,0:T(8,128)(2,1)S(1)} collective-permute-done((bf16[256,256]{1,0:T(8,128)(2,1)S(1)}, bf16[256,256]{1,0:T(8,128)(2,1)S(1)}, u32[]{:S(2)}, u32[]{:S(2)}) %collective-permute-start.32) | collective-permute-done | bytes 131104 | tf_op jit(solution)/shard_map/ppermute | solution.py:263
  116.9 1.6 %shard_map.83 = bf16[256,2048]{1,0:T(8,128)(2,1)} custom-call(s32[3]{0:T(128)S(1)} %pad_add_fusion.here_ref, bf16[256,256]{1,0:T(8,128)(2,1)S(1)} %get-tuple-element.153.refs_0_, bf16[256,256]{1,0:T(8,128)(2,1)S(1)} %get-tuple-element.154.refs_1_, bf16[256,256]{1,0:T(8,128)(2,1)S(1)} %collective-permute-done.27.refs_2_, ...), custom_call_target="tpu_custom_call" | custom-call | bytes 4194304 | tf_op jit(solution)/shard_map/pallas_call | solution.py:415
  (37 shorter events, 0.8 us)
Async XLA Ops:
  0.0 17.7 %collective-permute-start.3 = (bf16[256,4096]{1,0:T(8,128)(2,1)}, bf16[256,4096]{1,0:T(8,128)(2,1)}, u32[]{:S(2)}, u32[]{:S(2)}) collective-permute-start(bf16[256,4096]{1,0:T(8,128)(2,1)} %bitcast.3.refs_0_), channel_id=1, source_target_pairs={{0,4},{1,5},{2,6},{3,7},{4,0},{5,1},{6,2},{7,3},{8,12},{9,13},{10,... | collective-permute-start | bytes 6291464 | tf_op jit(solution)/shard_map/ppermute | solution.py:263
  1.4 1.0 copy-start
  2.5 0.9 copy-start.1
  3.4 0.9 copy-start.2
  4.3 0.7 copy-start.4
  5.6 7.1 %collective-permute-start.1 = (bf16[144,768]{1,0:T(8,128)(2,1)S(1)}, bf16[144,768]{1,0:T(8,128)(2,1)S(1)}, u32[]{:S(2)}, u32[]{:S(2)}) collective-permute-start(bf16[144,768]{1,0:T(8,128)(2,1)S(1)} %get-tuple-element.83), channel_id=1, source_target_pairs={{0,8},{1,9},{2,10},{3,11},{4,12},{5,13},{6,14},{7,15},{8,0},{9,1},... | collective-permute-start | bytes 663560 | tf_op jit(solution)/shard_map/ppermute | solution.py:263
  6.9 10.7 %collective-permute-start.2 = (bf16[144,768]{1,0:T(8,128)(2,1)S(1)}, bf16[144,768]{1,0:T(8,128)(2,1)S(1)}, u32[]{:S(2)}, u32[]{:S(2)}) collective-permute-start(bf16[144,768]{1,0:T(8,128)(2,1)S(1)} %get-tuple-element.84), channel_id=1, source_target_pairs={{0,12},{1,13},{2,14},{3,15},{4,8},{5,9},{6,10},{7,11},{8,4},{9,5},... | collective-permute-start | bytes 663560 | tf_op jit(solution)/shard_map/ppermute | solution.py:263
  7.3 10.3 %collective-permute-start = (bf16[144,768]{1,0:T(8,128)(2,1)S(1)}, bf16[144,768]{1,0:T(8,128)(2,1)S(1)}, u32[]{:S(2)}, u32[]{:S(2)}) collective-permute-start(bf16[144,768]{1,0:T(8,128)(2,1)S(1)} %get-tuple-element.82), channel_id=1, source_target_pairs={{0,4},{1,5},{2,6},{3,7},{4,0},{5,1},{6,2},{7,3},{8,12},{9,13},{10,... | collective-permute-start | bytes 663560 | tf_op jit(solution)/shard_map/ppermute | solution.py:263
  17.7 10.6 %collective-permute-start.4 = (bf16[256,768]{1,0:T(8,128)(2,1)S(1)}, bf16[256,768]{1,0:T(8,128)(2,1)S(1)}, u32[]{:S(2)}, u32[]{:S(2)}) collective-permute-start(bf16[256,768]{1,0:T(8,128)(2,1)S(1)} %pad_maximum_fusion.refs_2_), channel_id=1, source_target_pairs={{0,1},{1,0},{2,3},{3,2},{4,5},{5,4},{6,7},{7,6},{8,9},{9,8},{10,11... | collective-permute-start | bytes 1179656 | tf_op jit(solution)/shard_map/ppermute | solution.py:263
  17.8 53.7 %collective-permute-start.21 = (bf16[256,4096]{1,0:T(8,128)(2,1)}, bf16[256,4096]{1,0:T(8,128)(2,1)}, u32[]{:S(2)}, u32[]{:S(2)}) collective-permute-start(bf16[256,4096]{1,0:T(8,128)(2,1)} %bitcast.3.refs_0_), channel_id=1, source_target_pairs={{0,8},{1,9},{2,10},{3,11},{4,12},{5,13},{6,14},{7,15},{8,0},{9,1},... | collective-permute-start | bytes 6291464 | tf_op jit(solution)/shard_map/ppermute | solution.py:263
  19.1 13.0 %collective-permute-start.5 = (bf16[256,768]{1,0:T(8,128)(2,1)S(1)}, bf16[256,768]{1,0:T(8,128)(2,1)}, u32[]{:S(2)}, u32[]{:S(2)}) collective-permute-start(bf16[256,768]{1,0:T(8,128)(2,1)S(1)} %pad_maximum_fusion.refs_2_), channel_id=1, source_target_pairs={{1,2},{2,1},{5,6},{6,5},{9,10},{10,9},{13,14},{14,13},{17,18},{18,... | collective-permute-start | bytes 1179656 | tf_op jit(solution)/shard_map/ppermute | solution.py:263
  23.5 10.0 %collective-permute-start.6 = (bf16[256,768]{1,0:T(8,128)(2,1)S(1)}, bf16[256,768]{1,0:T(8,128)(2,1)S(1)}, u32[]{:S(2)}, u32[]{:S(2)}) collective-permute-start(bf16[256,768]{1,0:T(8,128)(2,1)S(1)} %pad_maximum_fusion.refs_2_), channel_id=1, source_target_pairs={{0,16},{1,17},{2,18},{3,19},{4,20},{5,21},{6,22},{7,23},{8,24},{9,... | collective-permute-start | bytes 1179656 | tf_op jit(solution)/shard_map/ppermute | solution.py:263
  24.8 11.9 %collective-permute-start.13 = (bf16[256,768]{1,0:T(8,128)(2,1)S(1)}, bf16[256,768]{1,0:T(8,128)(2,1)S(1)}, u32[]{:S(2)}, u32[]{:S(2)}) collective-permute-start(bf16[256,768]{1,0:T(8,128)(2,1)S(1)} %pad_maximum_fusion.1.refs_9_), channel_id=1, source_target_pairs={{0,1},{1,0},{2,3},{3,2},{4,5},{5,4},{6,7},{7,6},{8,9},{9,8},{10,11... | collective-permute-start | bytes 1179656 | tf_op jit(solution)/shard_map/ppermute | solution.py:263
  28.3 11.4 %collective-permute-start.14 = (bf16[256,768]{1,0:T(8,128)(2,1)S(1)}, bf16[256,768]{1,0:T(8,128)(2,1)S(1)}, u32[]{:S(2)}, u32[]{:S(2)}) collective-permute-start(bf16[256,768]{1,0:T(8,128)(2,1)S(1)} %pad_maximum_fusion.1.refs_9_), channel_id=1, source_target_pairs={{1,2},{2,1},{5,6},{6,5},{9,10},{10,9},{13,14},{14,13},{17,18},{18,... | collective-permute-start | bytes 1179656 | tf_op jit(solution)/shard_map/ppermute | solution.py:263
  32.2 9.1 %collective-permute-start.15 = (bf16[256,768]{1,0:T(8,128)(2,1)S(1)}, bf16[256,768]{1,0:T(8,128)(2,1)S(1)}, u32[]{:S(2)}, u32[]{:S(2)}) collective-permute-start(bf16[256,768]{1,0:T(8,128)(2,1)S(1)} %pad_maximum_fusion.1.refs_9_), channel_id=1, source_target_pairs={{0,16},{1,17},{2,18},{3,19},{4,20},{5,21},{6,22},{7,23},{8,24},{9,... | collective-permute-start | bytes 1179656 | tf_op jit(solution)/shard_map/ppermute | solution.py:263
  33.4 14.7 %collective-permute-start.7 = (bf16[256,768]{1,0:T(8,128)(2,1)S(1)}, bf16[256,768]{1,0:T(8,128)(2,1)}, u32[]{:S(2)}, u32[]{:S(2)}) collective-permute-start(bf16[256,768]{1,0:T(8,128)(2,1)S(1)} %collective-permute-done.4.refs_3_), channel_id=1, source_target_pairs={{1,2},{2,1},{5,6},{6,5},{9,10},{10,9},{13,14},{14,13},{17,18},{18,... | collective-permute-start | bytes 1179656 | tf_op jit(solution)/shard_map/ppermute | solution.py:263
  36.7 13.4 %collective-permute-start.8 = (bf16[256,768]{1,0:T(8,128)(2,1)}, bf16[256,768]{1,0:T(8,128)(2,1)}, u32[]{:S(2)}, u32[]{:S(2)}) collective-permute-start(bf16[256,768]{1,0:T(8,128)(2,1)} %collective-permute-done.5), channel_id=1, source_target_pairs={{1,0},{2,3},{5,4},{6,7},{9,8},{10,11},{13,12},{14,15},{17,16},{18,... | collective-permute-start | bytes 1179656 | tf_op jit(solution)/shard_map/ppermute | solution.py:263
  39.6 1.6 %copy-start.5 = (bf16[256,768]{1,0:T(8,128)(2,1)}, bf16[256,768]{1,0:T(8,128)(2,1)S(1)}, u32[]{:S(2)}) copy-start(bf16[256,768]{1,0:T(8,128)(2,1)S(1)} %collective-permute-done.14) | copy-start | bytes 1179652
  39.6 11.7 %collective-permute-start.9 = (bf16[256,768]{1,0:T(8,128)(2,1)S(1)}, bf16[256,768]{1,0:T(8,128)(2,1)}, u32[]{:S(2)}, u32[]{:S(2)}) collective-permute-start(bf16[256,768]{1,0:T(8,128)(2,1)S(1)} %collective-permute-done.4.refs_3_), channel_id=1, source_target_pairs={{0,16},{1,17},{2,18},{3,19},{4,20},{5,21},{6,22},{7,23},{8,24},{9,... | collective-permute-start | bytes 1179656 | tf_op jit(solution)/shard_map/ppermute | solution.py:263
  41.2 15.2 %collective-permute-start.16 = (bf16[256,768]{1,0:T(8,128)(2,1)S(1)}, bf16[256,768]{1,0:T(8,128)(2,1)}, u32[]{:S(2)}, u32[]{:S(2)}) collective-permute-start(bf16[256,768]{1,0:T(8,128)(2,1)S(1)} %collective-permute-done.13.refs_10_), channel_id=1, source_target_pairs={{1,2},{2,1},{5,6},{6,5},{9,10},{10,9},{13,14},{14,13},{17,18},{18,... | collective-permute-start | bytes 1179656 | tf_op jit(solution)/shard_map/ppermute | solution.py:263
  48.1 9.7 %collective-permute-start.17 = (bf16[256,768]{1,0:T(8,128)(2,1)}, bf16[256,768]{1,0:T(8,128)(2,1)}, u32[]{:S(2)}, u32[]{:S(2)}) collective-permute-start(bf16[256,768]{1,0:T(8,128)(2,1)} %copy-done.5), channel_id=1, source_target_pairs={{1,0},{2,3},{5,4},{6,7},{9,8},{10,11},{13,12},{14,15},{17,16},{18,... | collective-permute-start | bytes 1179656 | tf_op jit(solution)/shard_map/ppermute | solution.py:263
  50.1 7.7 %collective-permute-start.18 = (bf16[256,768]{1,0:T(8,128)(2,1)S(1)}, bf16[256,768]{1,0:T(8,128)(2,1)}, u32[]{:S(2)}, u32[]{:S(2)}) collective-permute-start(bf16[256,768]{1,0:T(8,128)(2,1)S(1)} %collective-permute-done.13.refs_10_), channel_id=1, source_target_pairs={{0,16},{1,17},{2,18},{3,19},{4,20},{5,21},{6,22},{7,23},{8,24},{9,... | collective-permute-start | bytes 1179656 | tf_op jit(solution)/shard_map/ppermute | solution.py:263
  52.4 12.5 %collective-permute-start.11 = (bf16[256,768]{1,0:T(8,128)(2,1)S(1)}, bf16[256,768]{1,0:T(8,128)(2,1)S(1)}, u32[]{:S(2)}, u32[]{:S(2)}) collective-permute-start(bf16[256,768]{1,0:T(8,128)(2,1)S(1)} %broadcast_select_fusion.3.refs_4_), channel_id=1, source_target_pairs={{0,16},{1,17},{2,18},{3,19},{4,20},{5,21},{6,22},{7,23},{8,24},{9,... | collective-permute-start | bytes 1179656 | tf_op jit(solution)/shard_map/ppermute | solution.py:263
  56.5 8.6 %collective-permute-start.10 = (bf16[256,768]{1,0:T(8,128)(2,1)}, bf16[256,768]{1,0:T(8,128)(2,1)S(1)}, u32[]{:S(2)}, u32[]{:S(2)}) collective-permute-start(bf16[256,768]{1,0:T(8,128)(2,1)} %collective-permute-done.7), channel_id=1, source_target_pairs={{1,0},{2,3},{5,4},{6,7},{9,8},{10,11},{13,12},{14,15},{17,16},{18,... | collective-permute-start | bytes 1179656 | tf_op jit(solution)/shard_map/ppermute | solution.py:263
  58.9 14.3 %collective-permute-start.20 = (bf16[256,768]{1,0:T(8,128)(2,1)S(1)}, bf16[256,768]{1,0:T(8,128)(2,1)S(1)}, u32[]{:S(2)}, u32[]{:S(2)}) collective-permute-start(bf16[256,768]{1,0:T(8,128)(2,1)S(1)} %broadcast_select_fusion.1.refs_11_), channel_id=1, source_target_pairs={{0,16},{1,17},{2,18},{3,19},{4,20},{5,21},{6,22},{7,23},{8,24},{9,... | collective-permute-start | bytes 1179656 | tf_op jit(solution)/shard_map/ppermute | solution.py:263
  60.2 13.0 %collective-permute-start.19 = (bf16[256,768]{1,0:T(8,128)(2,1)}, bf16[256,768]{1,0:T(8,128)(2,1)S(1)}, u32[]{:S(2)}, u32[]{:S(2)}) collective-permute-start(bf16[256,768]{1,0:T(8,128)(2,1)} %collective-permute-done.16), channel_id=1, source_target_pairs={{1,0},{2,3},{5,4},{6,7},{9,8},{10,11},{13,12},{14,15},{17,16},{18,... | collective-permute-start | bytes 1179656 | tf_op jit(solution)/shard_map/ppermute | solution.py:263
  73.2 11.5 %collective-permute-start.23 = (bf16[256,4096]{1,0:T(8,128)(2,1)}, bf16[256,4096]{1,0:T(8,128)(2,1)S(1)}, u32[]{:S(2)}, u32[]{:S(2)}) collective-permute-start(bf16[256,4096]{1,0:T(8,128)(2,1)} %collective-permute-done.21.refs_0_), channel_id=1, source_target_pairs={{0,4},{1,5},{2,6},{3,7},{4,0},{5,1},{6,2},{7,3},{8,12},{9,13},{10,... | collective-permute-start | bytes 6291464 | tf_op jit(solution)/shard_map/ppermute | solution.py:263
  80.7 10.7 %collective-permute-start.12 = (bf16[256,768]{1,0:T(8,128)(2,1)S(1)}, bf16[256,768]{1,0:T(8,128)(2,1)S(1)}, u32[]{:S(2)}, u32[]{:S(2)}) collective-permute-start(bf16[256,768]{1,0:T(8,128)(2,1)S(1)} %broadcast_select_fusion.2.refs_5_), channel_id=1, source_target_pairs={{0,16},{1,17},{2,18},{3,19},{4,20},{5,21},{6,22},{7,23},{8,24},{9,... | collective-permute-start | bytes 1179656 | tf_op jit(solution)/shard_map/ppermute | solution.py:263
  83.1 11.2 %collective-permute-start.22 = (bf16[256,256]{1,0:T(8,128)(2,1)S(1)}, bf16[256,256]{1,0:T(8,128)(2,1)S(1)}, u32[]{:S(2)}, u32[]{:S(2)}) collective-permute-start(bf16[256,256]{1,0:T(8,128)(2,1)S(1)} %get-tuple-element.159), channel_id=1, source_target_pairs={{0,16},{1,17},{2,18},{3,19},{4,20},{5,21},{6,22},{7,23},{8,24},{9,... | collective-permute-start | bytes 393224 | tf_op jit(solution)/shard_map/ppermute | solution.py:263
  83.4 15.4 %collective-permute-start.25 = (bf16[256,256]{1,0:T(8,128)(2,1)S(1)}, bf16[256,256]{1,0:T(8,128)(2,1)S(1)}, u32[]{:S(2)}, u32[]{:S(2)}) collective-permute-start(bf16[256,256]{1,0:T(8,128)(2,1)S(1)} %get-tuple-element.158), channel_id=1, source_target_pairs={{0,16},{1,17},{2,18},{3,19},{4,20},{5,21},{6,22},{7,23},{8,24},{9,... | collective-permute-start | bytes 393224 | tf_op jit(solution)/shard_map/ppermute | solution.py:263
  95.4 5.0 %collective-permute-start.24 = (bf16[128,256]{1,0:T(8,128)(2,1)S(1)}, bf16[128,256]{1,0:T(8,128)(2,1)S(1)}, u32[]{:S(2)}, u32[]{:S(2)}) collective-permute-start(bf16[128,256]{1,0:T(8,128)(2,1)S(1)} %get-tuple-element.119), channel_id=1, source_target_pairs={{0,16},{1,17},{2,18},{3,19},{4,20},{5,21},{6,22},{7,23},{8,24},{9,... | collective-permute-start | bytes 196616 | tf_op jit(solution)/shard_map/ppermute | solution.py:263
  98.7 6.4 %collective-permute-start.26 = (bf16[256,256]{1,0:T(8,128)(2,1)S(1)}, bf16[256,256]{1,0:T(8,128)(2,1)S(1)}, u32[]{:S(2)}, u32[]{:S(2)}) collective-permute-start(bf16[256,256]{1,0:T(8,128)(2,1)S(1)} %get-tuple-element.131), channel_id=1, source_target_pairs={{0,16},{1,17},{2,18},{3,19},{4,20},{5,21},{6,22},{7,23},{8,24},{9,... | collective-permute-start | bytes 393224 | tf_op jit(solution)/shard_map/ppermute | solution.py:263
  98.8 1.6 %copy-start.3 = (f32[16]{0:T(128)S(1)}, f32[16]{0:T(128)}, u32[]{:S(2)}) copy-start(f32[16]{0:T(128)} %gate_ref.5) | copy-start | bytes 196
  101.5 9.8 %collective-permute-start.29 = (bf16[256,256]{1,0:T(8,128)(2,1)S(1)}, bf16[256,256]{1,0:T(8,128)(2,1)S(1)}, u32[]{:S(2)}, u32[]{:S(2)}) collective-permute-start(bf16[256,256]{1,0:T(8,128)(2,1)S(1)} %get-tuple-element.134), channel_id=1, source_target_pairs={{0,8},{1,9},{2,10},{3,11},{4,12},{5,13},{6,14},{7,15},{8,0},{9,1},... | collective-permute-start | bytes 393224 | tf_op jit(solution)/shard_map/ppermute | solution.py:263
  102.3 10.1 %collective-permute-start.31 = (bf16[256,256]{1,0:T(8,128)(2,1)S(1)}, bf16[256,256]{1,0:T(8,128)(2,1)S(1)}, u32[]{:S(2)}, u32[]{:S(2)}) collective-permute-start(bf16[256,256]{1,0:T(8,128)(2,1)S(1)} %get-tuple-element.135), channel_id=1, source_target_pairs={{0,12},{1,13},{2,14},{3,15},{4,8},{5,9},{6,10},{7,11},{8,4},{9,5},... | collective-permute-start | bytes 393224 | tf_op jit(solution)/shard_map/ppermute | solution.py:263
  107.3 5.6 %collective-permute-start.30 = (bf16[256,256]{1,0:T(8,128)(2,1)S(1)}, bf16[256,256]{1,0:T(8,128)(2,1)S(1)}, u32[]{:S(2)}, u32[]{:S(2)}) collective-permute-start(bf16[256,256]{1,0:T(8,128)(2,1)S(1)} %get-tuple-element.141), channel_id=1, source_target_pairs={{0,8},{1,9},{2,10},{3,11},{4,12},{5,13},{6,14},{7,15},{8,0},{9,1},... | collective-permute-start | bytes 393224 | tf_op jit(solution)/shard_map/ppermute | solution.py:263
  110.7 1.7 %collective-permute-start.27 = (bf16[256,256]{1,0:T(8,128)(2,1)S(1)}, bf16[256,256]{1,0:T(8,128)(2,1)S(1)}, u32[]{:S(2)}, u32[]{:S(2)}) collective-permute-start(bf16[256,256]{1,0:T(8,128)(2,1)S(1)} %get-tuple-element.155), channel_id=1, source_target_pairs={{0,4},{1,5},{2,6},{3,7},{4,0},{5,1},{6,2},{7,3},{8,12},{9,13},{10,... | collective-permute-start | bytes 393224 | tf_op jit(solution)/shard_map/ppermute | solution.py:263
  111.2 1.3 %collective-permute-start.28 = (bf16[256,256]{1,0:T(8,128)(2,1)S(1)}, bf16[256,256]{1,0:T(8,128)(2,1)S(1)}, u32[]{:S(2)}, u32[]{:S(2)}) collective-permute-start(bf16[256,256]{1,0:T(8,128)(2,1)S(1)} %get-tuple-element.156), channel_id=1, source_target_pairs={{0,4},{1,5},{2,6},{3,7},{4,0},{5,1},{6,2},{7,3},{8,12},{9,13},{10,... | collective-permute-start | bytes 393224 | tf_op jit(solution)/shard_map/ppermute | solution.py:263
  111.3 5.6 %collective-permute-start.32 = (bf16[256,256]{1,0:T(8,128)(2,1)S(1)}, bf16[256,256]{1,0:T(8,128)(2,1)S(1)}, u32[]{:S(2)}, u32[]{:S(2)}) collective-permute-start(bf16[256,256]{1,0:T(8,128)(2,1)S(1)} %get-tuple-element.142), channel_id=1, source_target_pairs={{0,12},{1,13},{2,14},{3,15},{4,8},{5,9},{6,10},{7,11},{8,4},{9,5},... | collective-permute-start | bytes 393224 | tf_op jit(solution)/shard_map/ppermute | solution.py:263

commit v9 on v8

--- a/solution.py
+++ b/solution.py
@@ -103,17 +103,29 @@
     return high, (values - high.astype(jnp.float32)).astype(jnp.bfloat16)
 
 
-def late_rows(pieces, start):
-    width = pieces[-1].shape[1]
-    rows = [piece[:, start : start + width] for piece in pieces[:-1]]
-    return jnp.concatenate(rows + [pieces[-1][...]], axis=0)
-
-
-def kv_body(n_late, *refs):
-    pieces, refs = refs[:n_late], refs[n_late:]
+def late_rows(here_ref, last_ref, start, width, *pieces):
+    *whole, upper, inner, outer = pieces
+    rows = [piece[:, start : start + width] for piece in whole]
+    lost = whole[0].shape[1] - upper.shape[1] if start else 0
+    rows.append(upper[:, start - lost : start - lost + width])
+    inside = (here_ref[2] == 1) | (here_ref[2] == 2)
+
+    @pl.when(inside)
+    def _():
+        last_ref[...] = inner[:, start : start + width]
+
+    @pl.when(jnp.logical_not(inside))
+    def _():
+        last_ref[...] = outer[...]
+
+    return jnp.concatenate(rows + [last_ref[...]], axis=0)
+
+
+def kv_body(n_late, here_ref, *refs):
+    pieces, refs, last_ref = refs[:n_late], refs[n_late:-1], refs[-1]
     sums, lates, messages = refs[:MEMBERS], refs[MEMBERS : 2 * MEMBERS], refs[2 * MEMBERS : 3 * MEMBERS]
     outs = refs[3 * MEMBERS :]
-    rows = late_rows(pieces, 0)
+    rows = late_rows(here_ref, last_ref, 0, 2 * HEAD_SIZE, *pieces)
     kvs = []
     for seg in range(MEMBERS):
         total = sums[seg][:, : 2 * HEAD_SIZE]
@@ -139,10 +151,10 @@
     outs[-1][...] = whole.astype(jnp.bfloat16)
 
 
-def local_body(n, n_late, start, heads, *refs):
-    pieces, refs = refs[:n_late], refs[n_late:]
+def local_body(n, n_late, start, heads, here_ref, *refs):
+    pieces, refs, last_ref = refs[:n_late], refs[n_late:-1], refs[-1]
     kvs, messages, sums, lates, outs = [refs[k * n : (k + 1) * n] for k in range(4)] + [refs[4 * n :]]
-    rows = late_rows(pieces, start)
+    rows = late_rows(here_ref, last_ref, start, heads * HEAD_SIZE, *pieces)
     columns = slice(start, start + heads * HEAD_SIZE)
     queries = []
     for at in range(n):
@@ -306,6 +318,7 @@
         for at, s in enumerate(segs):
             sums[s], lates[s] = found[at], found[2 + at]
 
+    cut = 2 * HEAD_SIZE
     if n_groups == 2 and n_z == 4:
         assert rows == HEAD_SIZE
         inside = (z == 1) | (z == 2)
@@ -331,24 +344,25 @@
         a_two = jnp.where(inside, a_inner, a_outer)
         a_last, a_far2 = stage3(a_middle, a_two)
         b_two = jnp.where(inside, b_inner, b_outer)
-        b_last, b_far2 = stage3(b_middle, b_two)
+        b_last, b_far2, b_inner = *stage3(b_middle, b_two), inward(b_far1)
         a_last, a_far2, a_middle = locked(a_last, a_far2, a_middle)
         a_three = jnp.where(inside, a_middle, a_last)
-        a_far3 = over(a_three)
         books = [own, sibling]
-        upper = [a, a_one, a_two, a_three, a_far0, a_far1, a_far2]
+        upper = [a, a_one, a_two, None, a_far0, a_far1]
         lower = [b, b_one, b_two, None, b_far0, b_far1]
-        late = [(7, 0), (3, 1), (6, 1), (7, 1)]
-        early = [(k, half) for half in range(2) for k in range(8) if (k, half) not in late]
+        early = [(k, half) for half in range(2) for k in (0, 1, 2, 4, 5)]
+        late = [(3, 0), (6, 0), (3, 1), (6, 1), (7, 0), (7, 1)]
         project((0, 1), early, late, (upper, lower), n_z)
-        b_last, b_far2, b_middle, sums[0], sums[1], across = locked(
-            b_last, b_far2, b_middle, sums[0], sums[1], after(across, a_last, a_far2)
+        b_last, b_far2, b_middle, b_inner, sums[0], sums[1], across = locked(
+            b_last, b_far2, b_middle, b_inner, sums[0], sums[1], after(across, a_last, a_far2)
         )
         books += [across, to_member(across, 1)]
         project((2, 3), early, late, (upper, lower), n_z)
         b_three = jnp.where(inside, b_middle, b_last)
-        pieces = [a_far3, b_three, b_far2]
-        finish = lambda at, *others: over(after(b_three[:, at], *others))
+        pieces = [a_three, a_far2, b_three, b_far2]
+        upper_kv, upper_q = [over(a_three[:, at]) for at in (slice(0, cut), slice(cut, None))]
+        inner = b_inner
+        finish = lambda at, *others: outward(after(b_inner[:, at], *others))
     else:
         across, sibling = to_member(tokens[0], 2), to_member(tokens[0], 1)
         books = [tokens[0], sibling, across, to_member(across, 1)]
@@ -357,20 +371,25 @@
         upper, lower = [part[:deep] for part in full], [part[deep:] for part in full]
         late = [(n_pieces - 1, 0), (n_pieces - 1, 1)]
         early = [(k, half) for half in range(2) for k in range(n_pieces - 1)]
+        late = [(n_pieces - 2, 1)] + late
+        early.remove(late[0])
         for segs in ((0, 1), (2, 3)):
             project(segs, early, late, (upper, lower), 0)
-        pieces = [upper[-1]]
-        finish = lambda at, *others: lower[-1][:, at]
+        pieces = [lower[-2]]
+        upper_kv, upper_q = upper[-1][:, :cut], upper[-1][:, cut:]
+        inner = lower[-1]
+        finish = lambda at, *others: inner[:, at]
 
     halves = [slice(k * HEAD_SIZE, (k + 2) * HEAD_SIZE) for k in (0, 2, 4)]
     lower_kv, lower_q0 = finish(halves[0]), finish(halves[1])
     found = call(
-        functools.partial(kv_body, len(pieces) + 1),
+        functools.partial(kv_body, len(late) + 1),
         [shape((length, 2 * HEAD_SIZE), bf16), shape((HEAD_SIZE, 2 * HEAD_SIZE), f32)] * MEMBERS
         + [shape((HEAD_SIZE, 2 * HEAD_SIZE), bf16)],
-        [VMEM] * (len(pieces) + 1 + 3 * MEMBERS),
+        [SMEM] + [VMEM] * (len(late) + 1 + 3 * MEMBERS),
         flops=2 * MEMBERS * length * len(late) * MEMBERS * HEAD_SIZE * HEAD_SIZE,
-    )(*pieces, lower_kv, *sums, *lates, *messages)
+        scratch=[pltpu.VMEM((MEMBERS * HEAD_SIZE // 2, cut), bf16)],
+    )(here, *pieces, upper_kv, inner, lower_kv, *sums, *lates, *messages)
     kvs, deltas, total = found[0:-1:2], found[1:-1:2], found[-1]
 
     base = None
@@ -383,11 +402,12 @@
 
     def local(segs, part, lower_q):
         found = call(
-            functools.partial(local_body, len(segs), len(pieces) + 1, halves[1 + part].start, half),
+            functools.partial(local_body, len(segs), len(late) + 1, halves[1 + part].start, half),
             [shape((length, half * HEAD_SIZE), bf16), shape((length, half * HEAD_SIZE), f32)] * len(segs),
-            [VMEM] * (len(pieces) + 1 + 4 * len(segs)),
+            [SMEM] + [VMEM] * (len(late) + 1 + 4 * len(segs)),
             flops=4 * len(segs) * length * length * half * HEAD_SIZE,
-        )(*pieces, lower_q, *[one[s] for one in (kvs, messages, sums, lates) for s in segs])
+            scratch=[pltpu.VMEM((MEMBERS * HEAD_SIZE // 2, half * HEAD_SIZE), bf16)],
+        )(here, *pieces, upper_q, inner, lower_q, *[one[s] for one in (kvs, messages, sums, lates) for s in segs])
         return {(s, part): (found[2 * at], found[2 * at + 1]) for at, s in enumerate(segs)}
 
     def mix(segs, parts, base, ready):

time: 120 us -> 120 us (level)
  waiting for transfers between devices: 36.5 us -> 26.3 us
  starting transfers between devices: 52.2 us -> 60.5 us
  Pallas kernels: 20.9 us -> 23.7 us
    ppermute x33 -> x35, waiting for transfers between devices: 36.5 us -> 26.3 us  [permute(): return lax.ppermute(array, AXES, pairs)]
    ppermute x33 -> x35, starting transfers between devices: 52.2 us -> 60.5 us  [permute(): return lax.ppermute(array, AXES, pairs)]
    pallas_call x4, Pallas kernels: 4.71 us -> 8.09 us  [the longest x3 6.13 us: local(): call(functools.partial(local_body, len(segs), len(late) + 1, halves[1 + p...]
    unnamed x12 -> x18, local copies, waits for them, and re-layouts: 3.54 us -> 4.3 us
  transfers between devices with their start and end apart: 33 -> 35, of which waited for: 18 -> 9; matrix products, arithmetic and copies ran while one was open for 4% -> 3% of each run, Pallas kernels for 16% -> 18%
where the time goes in v9:
time: 120 us; the launch traced here: 119 us
  starting transfers between devices  60.5 us (50%)
  waiting for transfers between devices  26.3 us (22%)
  Pallas kernels  23.7 us (20%)
  local copies, waits for them, and re-layouts  4.41 us (4%)
  other arithmetic  3.35 us (3%)
    ppermute x35, starting transfers between devices, permute(): return lax.ppermute(array, AXES, pairs)  60.5 us
    ppermute x35, waiting for transfers between devices, permute(): return lax.ppermute(array, AXES, pairs)  26.3 us
    pallas_call x2, Pallas kernels, project(): call(functools.partial(project_body, early, late, line), [shape((length,...  9.38 us
    pallas_call x3, Pallas kernels, local(): call(functools.partial(local_body, len(segs), len(late) + 1, halves[1 + p...  6.13 us
    unnamed x18, local copies, waits for them, and re-layouts  4.3 us
    pallas_call x3, Pallas kernels, mix(): call(functools.partial(mix_body, segs, parts, group), [shape((length, hal...  3.95 us
  transfers between devices with their start and end apart: 35, of which 9 were waited for; matrix products, arithmetic and copies ran while one was open for 3% of the time, Pallas kernels for 18%

profile of v9, /device:TPU:9, one launch (start us, length us, event | category | flops | bytes accessed | tf_op | source)
XLA Modules:
  0.0 119.3 jit_solution(10250028071128993566)
XLA Ops:
  0.0 0.7 collective-permute-start.3
  1.3 0.1 pad_add_fusion.here_ref
  1.4 1.0 copy-done
  2.5 0.9 copy-done.1
  3.4 0.9 copy-done.2
  4.3 0.7 copy-done.4
  4.9 0.6 shard_map.73
  5.6 0.1 collective-permute-start
  5.7 1.6 %collective-permute-start.2 = (bf16[144,768]{1,0:T(8,128)(2,1)S(1)}, bf16[144,768]{1,0:T(8,128)(2,1)S(1)}, u32[]{:S(2)}, u32[]{:S(2)}) collective-permute-start(bf16[144,768]{1,0:T(8,128)(2,1)S(1)} %get-tuple-element.85), channel_id=1, source_target_pairs={{0,12},{1,13},{2,14},{3,15},{4,8},{5,9},{6,10},{7,11},{8,4},{9,5},... | collective-permute-start | bytes 663560 | tf_op jit(solution)/shard_map/ppermute | solution.py:275
  7.3 0.3 collective-permute-start.1
  7.6 5.9 %collective-permute-done.2.refs_18_.refs_12_.refs_5_.refs_10_ = bf16[144,768]{1,0:T(8,128)(2,1)S(1)} collective-permute-done((bf16[144,768]{1,0:T(8,128)(2,1)S(1)}, bf16[144,768]{1,0:T(8,128)(2,1)S(1)}, u32[]{:S(2)}, u32[]{:S(2)}) %collective-permute-start.2) | collective-permute-done | bytes 221216 | tf_op jit(solution)/shard_map/ppermute | solution.py:275
  13.5 4.5 %collective-permute-done.1.refs_17_.refs_11_.refs_4_.refs_9_ = bf16[144,768]{1,0:T(8,128)(2,1)S(1)} collective-permute-done((bf16[144,768]{1,0:T(8,128)(2,1)S(1)}, bf16[144,768]{1,0:T(8,128)(2,1)S(1)}, u32[]{:S(2)}, u32[]{:S(2)}) %collective-permute-start.1) | collective-permute-done | bytes 221216 | tf_op jit(solution)/shard_map/ppermute | solution.py:275
  18.1 1.3 %collective-permute-start.21 = (bf16[256,4096]{1,0:T(8,128)(2,1)}, bf16[256,4096]{1,0:T(8,128)(2,1)}, u32[]{:S(2)}, u32[]{:S(2)}) collective-permute-start(bf16[256,4096]{1,0:T(8,128)(2,1)} %bitcast.3.refs_0_), channel_id=1, source_target_pairs={{0,8},{1,9},{2,10},{3,11},{4,12},{5,13},{6,14},{7,15},{8,0},{9,1},... | collective-permute-start | bytes 6291464 | tf_op jit(solution)/shard_map/ppermute | solution.py:275
  19.3 0.2 collective-permute-start.4
  19.5 4.3 %collective-permute-start.5 = (bf16[256,768]{1,0:T(8,128)(2,1)S(1)}, bf16[256,768]{1,0:T(8,128)(2,1)S(1)}, u32[]{:S(2)}, u32[]{:S(2)}) collective-permute-start(bf16[256,768]{1,0:T(8,128)(2,1)S(1)} %pad_maximum_fusion.refs_2_), channel_id=1, source_target_pairs={{1,2},{2,1},{5,6},{6,5},{9,10},{10,9},{13,14},{14,13},{17,18},{18,... | collective-permute-start | bytes 1179656 | tf_op jit(solution)/shard_map/ppermute | solution.py:275
  23.8 1.3 %collective-permute-start.6 = (bf16[256,768]{1,0:T(8,128)(2,1)S(1)}, bf16[256,768]{1,0:T(8,128)(2,1)S(1)}, u32[]{:S(2)}, u32[]{:S(2)}) collective-permute-start(bf16[256,768]{1,0:T(8,128)(2,1)S(1)} %pad_maximum_fusion.refs_2_), channel_id=1, source_target_pairs={{0,16},{1,17},{2,18},{3,19},{4,20},{5,21},{6,22},{7,23},{8,24},{9,... | collective-permute-start | bytes 1179656 | tf_op jit(solution)/shard_map/ppermute | solution.py:275
  25.2 4.0 %collective-permute-done.4.refs_3_ = bf16[256,768]{1,0:T(8,128)(2,1)S(1)} collective-permute-done((bf16[256,768]{1,0:T(8,128)(2,1)S(1)}, bf16[256,768]{1,0:T(8,128)(2,1)S(1)}, u32[]{:S(2)}, u32[]{:S(2)}) %collective-permute-start.4) | collective-permute-done | bytes 393248 | tf_op jit(solution)/shard_map/ppermute | solution.py:275
  29.1 3.2 %collective-permute-start.13 = (bf16[256,768]{1,0:T(8,128)(2,1)S(1)}, bf16[256,768]{1,0:T(8,128)(2,1)}, u32[]{:S(2)}, u32[]{:S(2)}) collective-permute-start(bf16[256,768]{1,0:T(8,128)(2,1)S(1)} %pad_maximum_fusion.1.refs_7_), channel_id=1, source_target_pairs={{1,2},{2,1},{5,6},{6,5},{9,10},{10,9},{13,14},{14,13},{17,18},{18,... | collective-permute-start | bytes 1179656 | tf_op jit(solution)/shard_map/ppermute | solution.py:275
  32.4 1.3 %collective-permute-start.14 = (bf16[256,768]{1,0:T(8,128)(2,1)S(1)}, bf16[256,768]{1,0:T(8,128)(2,1)S(1)}, u32[]{:S(2)}, u32[]{:S(2)}) collective-permute-start(bf16[256,768]{1,0:T(8,128)(2,1)S(1)} %pad_maximum_fusion.1.refs_7_), channel_id=1, source_target_pairs={{0,16},{1,17},{2,18},{3,19},{4,20},{5,21},{6,22},{7,23},{8,24},{9,... | collective-permute-start | bytes 1179656 | tf_op jit(solution)/shard_map/ppermute | solution.py:275
  33.7 2.8 %collective-permute-start.7 = (bf16[256,768]{1,0:T(8,128)(2,1)S(1)}, bf16[256,768]{1,0:T(8,128)(2,1)S(1)}, u32[]{:S(2)}, u32[]{:S(2)}) collective-permute-start(bf16[256,768]{1,0:T(8,128)(2,1)S(1)} %collective-permute-done.4.refs_3_), channel_id=1, source_target_pairs={{1,2},{2,1},{5,6},{6,5},{9,10},{10,9},{13,14},{14,13},{17,18},{18,... | collective-permute-start | bytes 1179656 | tf_op jit(solution)/shard_map/ppermute | solution.py:275
  36.5 1.1 collective-permute-done.12.refs_8_
  37.6 2.1 %collective-permute-start.8 = (bf16[256,768]{1,0:T(8,128)(2,1)S(1)}, bf16[256,768]{1,0:T(8,128)(2,1)S(1)}, u32[]{:S(2)}, u32[]{:S(2)}) collective-permute-start(bf16[256,768]{1,0:T(8,128)(2,1)S(1)} %collective-permute-done.5), channel_id=1, source_target_pairs={{1,0},{2,3},{5,4},{6,7},{9,8},{10,11},{13,12},{14,15},{17,16},{18,... | collective-permute-start | bytes 1179656 | tf_op jit(solution)/shard_map/ppermute | solution.py:275
  39.7 1.3 %collective-permute-start.9 = (bf16[256,768]{1,0:T(8,128)(2,1)S(1)}, bf16[256,768]{1,0:T(8,128)(2,1)}, u32[]{:S(2)}, u32[]{:S(2)}) collective-permute-start(bf16[256,768]{1,0:T(8,128)(2,1)S(1)} %collective-permute-done.4.refs_3_), channel_id=1, source_target_pairs={{0,16},{1,17},{2,18},{3,19},{4,20},{5,21},{6,22},{7,23},{8,24},{9,... | collective-permute-start | bytes 1179656 | tf_op jit(solution)/shard_map/ppermute | solution.py:275
  41.0 4.3 %collective-permute-start.15 = (bf16[256,768]{1,0:T(8,128)(2,1)S(1)}, bf16[256,768]{1,0:T(8,128)(2,1)}, u32[]{:S(2)}, u32[]{:S(2)}) collective-permute-start(bf16[256,768]{1,0:T(8,128)(2,1)S(1)} %collective-permute-done.12.refs_8_), channel_id=1, source_target_pairs={{1,2},{2,1},{5,6},{6,5},{9,10},{10,9},{13,14},{14,13},{17,18},{18,... | collective-permute-start | bytes 1179656 | tf_op jit(solution)/shard_map/ppermute | solution.py:275
  45.3 1.7 %collective-permute-done.7 = bf16[256,768]{1,0:T(8,128)(2,1)S(1)} collective-permute-done((bf16[256,768]{1,0:T(8,128)(2,1)S(1)}, bf16[256,768]{1,0:T(8,128)(2,1)S(1)}, u32[]{:S(2)}, u32[]{:S(2)}) %collective-permute-start.7) | collective-permute-done | bytes 393248 | tf_op jit(solution)/shard_map/ppermute | solution.py:275
  47.0 2.0 %collective-permute-start.16 = (bf16[256,768]{1,0:T(8,128)(2,1)}, bf16[256,768]{1,0:T(8,128)(2,1)}, u32[]{:S(2)}, u32[]{:S(2)}) collective-permute-start(bf16[256,768]{1,0:T(8,128)(2,1)} %collective-permute-done.13), channel_id=1, source_target_pairs={{1,0},{2,3},{5,4},{6,7},{9,8},{10,11},{13,12},{14,15},{17,16},{18,... | collective-permute-start | bytes 1179656 | tf_op jit(solution)/shard_map/ppermute | solution.py:275
  49.0 0.7 copy-done.8
  49.8 1.2 %collective-permute-start.17 = (bf16[256,768]{1,0:T(8,128)(2,1)S(1)}, bf16[256,768]{1,0:T(8,128)(2,1)}, u32[]{:S(2)}, u32[]{:S(2)}) collective-permute-start(bf16[256,768]{1,0:T(8,128)(2,1)S(1)} %collective-permute-done.12.refs_8_), channel_id=1, source_target_pairs={{0,16},{1,17},{2,18},{3,19},{4,20},{5,21},{6,22},{7,23},{8,24},{9,... | collective-permute-start | bytes 1179656 | tf_op jit(solution)/shard_map/ppermute | solution.py:275
  51.0 1.5 %collective-permute-start.10 = (bf16[256,768]{1,0:T(8,128)(2,1)}, bf16[256,768]{1,0:T(8,128)(2,1)S(1)}, u32[]{:S(2)}, u32[]{:S(2)}) collective-permute-start(bf16[256,768]{1,0:T(8,128)(2,1)} %copy-done.5), channel_id=1, source_target_pairs={{1,0},{2,3},{5,4},{6,7},{9,8},{10,11},{13,12},{14,15},{17,16},{18,... | collective-permute-start | bytes 1179656 | tf_op jit(solution)/shard_map/ppermute | solution.py:275
  52.5 1.1 broadcast_select_fusion.3.refs_4_
  53.6 1.8 %collective-permute-done.15 = bf16[256,768]{1,0:T(8,128)(2,1)} collective-permute-done((bf16[256,768]{1,0:T(8,128)(2,1)S(1)}, bf16[256,768]{1,0:T(8,128)(2,1)}, u32[]{:S(2)}, u32[]{:S(2)}) %collective-permute-start.15) | collective-permute-done | bytes 393248 | tf_op jit(solution)/shard_map/ppermute | solution.py:275
  55.4 1.2 %collective-permute-start.11 = (bf16[256,768]{1,0:T(8,128)(2,1)S(1)}, bf16[256,768]{1,0:T(8,128)(2,1)S(1)}, u32[]{:S(2)}, u32[]{:S(2)}) collective-permute-start(bf16[256,768]{1,0:T(8,128)(2,1)S(1)} %broadcast_select_fusion.3.refs_4_), channel_id=1, source_target_pairs={{0,16},{1,17},{2,18},{3,19},{4,20},{5,21},{6,22},{7,23},{8,24},{9,... | collective-permute-start | bytes 1179656 | tf_op jit(solution)/shard_map/ppermute | solution.py:275
  56.6 1.4 %collective-permute-done.17.refs_11_ = bf16[256,768]{1,0:T(8,128)(2,1)} collective-permute-done((bf16[256,768]{1,0:T(8,128)(2,1)S(1)}, bf16[256,768]{1,0:T(8,128)(2,1)}, u32[]{:S(2)}, u32[]{:S(2)}) %collective-permute-start.17) | collective-permute-done | bytes 393248 | tf_op jit(solution)/shard_map/ppermute | solution.py:275
  58.1 1.3 %collective-permute-start.18 = (bf16[256,768]{1,0:T(8,128)(2,1)}, bf16[256,768]{1,0:T(8,128)(2,1)S(1)}, u32[]{:S(2)}, u32[]{:S(2)}) collective-permute-start(bf16[256,768]{1,0:T(8,128)(2,1)} %collective-permute-done.15), channel_id=1, source_target_pairs={{1,0},{2,3},{5,4},{6,7},{9,8},{10,11},{13,12},{14,15},{17,16},{18,... | collective-permute-start | bytes 1179656 | tf_op jit(solution)/shard_map/ppermute | solution.py:275
  59.4 1.1 broadcast_select_fusion.1.refs_9_
  60.5 0.0 copy-start.6
  60.5 1.3 %collective-permute-start.19 = (bf16[256,768]{1,0:T(8,128)(2,1)S(1)}, bf16[256,768]{1,0:T(8,128)(2,1)S(1)}, u32[]{:S(2)}, u32[]{:S(2)}) collective-permute-start(bf16[256,768]{1,0:T(8,128)(2,1)S(1)} %broadcast_select_fusion.1.refs_9_), channel_id=1, source_target_pairs={{0,16},{1,17},{2,18},{3,19},{4,20},{5,21},{6,22},{7,23},{8,24},{9,... | collective-permute-start | bytes 1179656 | tf_op jit(solution)/shard_map/ppermute | solution.py:275
  61.8 3.7 %collective-permute-start.20 = (bf16[256,768]{1,0:T(8,128)(2,1)}, bf16[256,768]{1,0:T(8,128)(2,1)S(1)}, u32[]{:S(2)}, u32[]{:S(2)}) collective-permute-start(bf16[256,768]{1,0:T(8,128)(2,1)} %collective-permute-done.17.refs_11_), channel_id=1, source_target_pairs={{1,2},{2,1},{5,6},{6,5},{9,10},{10,9},{13,14},{14,13},{17,18},{18,... | collective-permute-start | bytes 1179656 | tf_op jit(solution)/shard_map/ppermute | solution.py:275
  65.5 5.0 %shard_map.74 = (f32[256,768]{1,0:T(8,128)S(1)}, f32[256,768]{1,0:T(8,128)S(1)}, bf16[256,1536]{1,0:T(8,128)(2,1)S(1)}, bf16[256,1536]{1,0:T(8,128)(2,1)S(1)}) custom-call(s32[3]{0:T(128)S(1)} %pad_add_fusion.here_ref, bf16[256,4096]{1,0:T(8,128)(2,1)} %bitcast.3.refs_0_, bf16[256,4096]{1,0:T(8,128)(2,1)} %collective-permute-done.3.refs_1_, ...), custom_call_target="tpu_custom_call" | custom-call | flops 2013265920 | bytes 4194304 | tf_op jit(solution)/shard_map/pallas_call | solution.py:312
  70.5 1.8 %collective-permute-done.19.refs_3_ = bf16[256,768]{1,0:T(8,128)(2,1)S(1)} collective-permute-done((bf16[256,768]{1,0:T(8,128)(2,1)S(1)}, bf16[256,768]{1,0:T(8,128)(2,1)S(1)}, u32[]{:S(2)}, u32[]{:S(2)}) %collective-permute-start.19) | collective-permute-done | bytes 393248 | tf_op jit(solution)/shard_map/ppermute | solution.py:275
  72.3 11.2 %collective-permute-start.24 = (bf16[256,4096]{1,0:T(8,128)(2,1)}, bf16[256,4096]{1,0:T(8,128)(2,1)S(1)}, u32[]{:S(2)}, u32[]{:S(2)}) collective-permute-start(bf16[256,4096]{1,0:T(8,128)(2,1)} %collective-permute-done.21.refs_0_), channel_id=1, source_target_pairs={{0,4},{1,5},{2,6},{3,7},{4,0},{5,1},{6,2},{7,3},{8,12},{9,13},{10,... | collective-permute-start | bytes 6291464 | tf_op jit(solution)/shard_map/ppermute | solution.py:275
  83.6 0.3 collective-permute-start.22
  83.9 1.2 %collective-permute-start.26 = (bf16[256,512]{1,0:T(8,128)(2,1)S(1)}, bf16[256,512]{1,0:T(8,128)(2,1)S(1)}, u32[]{:S(2)}, u32[]{:S(2)}) collective-permute-start(bf16[256,512]{1,0:T(8,128)(2,1)S(1)} %slice.40), channel_id=1, source_target_pairs={{0,16},{1,17},{2,18},{3,19},{4,20},{5,21},{6,22},{7,23},{8,24},{9,... | collective-permute-start | bytes 786440 | tf_op jit(solution)/shard_map/ppermute | solution.py:275
  85.1 1.3 %collective-permute-start.23 = (bf16[256,256]{1,0:T(8,128)(2,1)S(1)}, bf16[256,256]{1,0:T(8,128)(2,1)S(1)}, u32[]{:S(2)}, u32[]{:S(2)}) collective-permute-start(bf16[256,256]{1,0:T(8,128)(2,1)S(1)} %get-tuple-element.161), channel_id=1, source_target_pairs={{1,0},{2,3},{5,4},{6,7},{9,8},{10,11},{13,12},{14,15},{17,16},{18,... | collective-permute-start | bytes 393224 | tf_op jit(solution)/shard_map/ppermute | solution.py:275
  86.5 1.3 %collective-permute-start.27 = (bf16[256,256]{1,0:T(8,128)(2,1)S(1)}, bf16[256,256]{1,0:T(8,128)(2,1)S(1)}, u32[]{:S(2)}, u32[]{:S(2)}) collective-permute-start(bf16[256,256]{1,0:T(8,128)(2,1)S(1)} %get-tuple-element.160), channel_id=1, source_target_pairs={{1,0},{2,3},{5,4},{6,7},{9,8},{10,11},{13,12},{14,15},{17,16},{18,... | collective-permute-start | bytes 393224 | tf_op jit(solution)/shard_map/ppermute | solution.py:275
  87.8 1.1 broadcast_select_fusion.refs_2_
  88.8 4.4 %shard_map.75 = (f32[256,768]{1,0:T(8,128)S(1)}, f32[256,768]{1,0:T(8,128)S(1)}, bf16[256,1536]{1,0:T(8,128)(2,1)S(1)}, bf16[256,1536]{1,0:T(8,128)(2,1)S(1)}) custom-call(s32[3]{0:T(128)S(1)} %pad_add_fusion.here_ref, bf16[256,4096]{1,0:T(8,128)(2,1)} %collective-permute-done.21.refs_0_, bf16[256,4096]{1,0:T(8,128)(2,1)S(1)} %collective-permute-done.24.refs_1_, ...), custom_call_target="tpu_custom_call" | custom-call | flops 2013265920 | bytes 4194304 | tf_op jit(solution)/shard_map/pallas_call | solution.py:312
  93.2 2.0 %shard_map.76 = (bf16[256,256]{1,0:T(8,128)(2,1)S(1)}, f32[128,256]{1,0:T(8,128)S(1)}, bf16[256,256]{1,0:T(8,128)(2,1)S(1)}, f32[128,256]{1,0:T(8,128)S(1)}, bf1...) custom-call(s32[3]{0:T(128)S(1)} %pad_add_fusion.here_ref, ...), custom_call_target="tpu_custom_call" | custom-call | flops 805306368 | bytes 4194304 | tf_op jit(solution)/shard_map/pallas_call | solution.py:385
  95.2 2.1 %collective-permute-start.25 = (bf16[128,256]{1,0:T(8,128)(2,1)S(1)}, bf16[128,256]{1,0:T(8,128)(2,1)S(1)}, u32[]{:S(2)}, u32[]{:S(2)}) collective-permute-start(bf16[128,256]{1,0:T(8,128)(2,1)S(1)} %get-tuple-element.121), channel_id=1, source_target_pairs={{0,16},{1,17},{2,18},{3,19},{4,20},{5,21},{6,22},{7,23},{8,24},{9,... | collective-permute-start | bytes 196616 | tf_op jit(solution)/shard_map/ppermute | solution.py:275
  97.4 1.3 %collective-permute-start.28 = (bf16[256,256]{1,0:T(8,128)(2,1)S(1)}, bf16[256,256]{1,0:T(8,128)(2,1)S(1)}, u32[]{:S(2)}, u32[]{:S(2)}) collective-permute-start(bf16[256,256]{1,0:T(8,128)(2,1)S(1)} %get-tuple-element.133), channel_id=1, source_target_pairs={{1,0},{2,3},{5,4},{6,7},{9,8},{10,11},{13,12},{14,15},{17,16},{18,... | collective-permute-start | bytes 393224 | tf_op jit(solution)/shard_map/ppermute | solution.py:275
  98.7 2.5 %shard_map.77 = (bf16[256,256]{1,0:T(8,128)(2,1)S(1)}, f32[256,256]{1,0:T(8,128)S(1)}, bf16[256,256]{1,0:T(8,128)(2,1)S(1)}, f32[256,256]{1,0:T(8,128)S(1)}, bf1...) custom-call(s32[3]{0:T(128)S(1)} %pad_add_fusion.here_ref, ...), custom_call_target="tpu_custom_call" | custom-call | flops 268435456 | bytes 4194304 | tf_op jit(solution)/shard_map/pallas_call | solution.py:404
  101.2 1.2 shard_map.78
  102.4 0.2 collective-permute-start.31
  102.5 2.5 %collective-permute-start.33 = (bf16[256,256]{1,0:T(8,128)(2,1)S(1)}, bf16[256,256]{1,0:T(8,128)(2,1)S(1)}, u32[]{:S(2)}, u32[]{:S(2)}) collective-permute-start(bf16[256,256]{1,0:T(8,128)(2,1)S(1)} %get-tuple-element.137), channel_id=1, source_target_pairs={{0,12},{1,13},{2,14},{3,15},{4,8},{5,9},{6,10},{7,11},{8,4},{9,5},... | collective-permute-start | bytes 393224 | tf_op jit(solution)/shard_map/ppermute | solution.py:275
  105.0 1.9 %shard_map.79 = (bf16[256,256]{1,0:T(8,128)(2,1)S(1)}, f32[256,256]{1,0:T(8,128)S(1)}, bf16[256,256]{1,0:T(8,128)(2,1)S(1)}, f32[256,256]{1,0:T(8,128)S(1)}) custom-call(s32[3]{0:T(128)S(1)} %pad_add_fusion.here_ref, bf16[256,768]{1,0:T(8,128)(2,1)S(1)} %broadcast_select_fusion.2.refs_0_, bf16[256,768]{1,0:T(8,128)(2,1)S(1)} %collective-permute-done.11.refs_1_, ...), custom_call_target="tpu_custom_call" | custom-call | flops 134217728 | bytes 4194304 | tf_op jit(solution)/shard_map/pallas_call | solution.py:404
  106.9 1.2 shard_map.80
  108.1 0.1 collective-permute-start.32
  108.2 1.7 %shard_map.81 = (bf16[256,256]{1,0:T(8,128)(2,1)S(1)}, f32[256,256]{1,0:T(8,128)S(1)}, bf16[256,256]{1,0:T(8,128)(2,1)S(1)}, f32[256,256]{1,0:T(8,128)S(1)}) custom-call(s32[3]{0:T(128)S(1)} %pad_add_fusion.here_ref, bf16[256,768]{1,0:T(8,128)(2,1)S(1)} %broadcast_select_fusion.2.refs_0_, bf16[256,768]{1,0:T(8,128)(2,1)S(1)} %collective-permute-done.11.refs_1_, ...), custom_call_target="tpu_custom_call" | custom-call | flops 134217728 | bytes 4194304 | tf_op jit(solution)/shard_map/pallas_call | solution.py:404
  110.0 1.6 %shard_map.82 = (bf16[256,256]{1,0:T(8,128)(2,1)S(1)}, bf16[256,256]{1,0:T(8,128)(2,1)S(1)}, bf16[256,256]{1,0:T(8,128)(2,1)S(1)}, bf16[256,256]{1,0:T(8,128)(2,1)S(1)}) custom-call(s32[3]{0:T(128)S(1)} %pad_add_fusion.here_ref, f32[16]{0:T(128)S(1)} %copy-done.3, bf16[128,256]{1,0:T(8,128)(2,1)S(1)} %collective-permute-done.25.base_ref, ...), custom_call_target="tpu_custom_call" | custom-call | flops 402653184 | bytes 4194304 | tf_op jit(solution)/shard_map/pallas_call | solution.py:415
  111.6 0.4 collective-permute-start.29
  112.0 0.2 collective-permute-start.30
  112.2 1.4 %collective-permute-start.34 = (bf16[256,256]{1,0:T(8,128)(2,1)S(1)}, bf16[256,256]{1,0:T(8,128)(2,1)S(1)}, u32[]{:S(2)}, u32[]{:S(2)}) collective-permute-start(bf16[256,256]{1,0:T(8,128)(2,1)S(1)} %get-tuple-element.144), channel_id=1, source_target_pairs={{0,12},{1,13},{2,14},{3,15},{4,8},{5,9},{6,10},{7,11},{8,4},{9,5},... | collective-permute-start | bytes 393224 | tf_op jit(solution)/shard_map/ppermute | solution.py:275
  113.6 4.0 %collective-permute-done.34.refs_7_ = bf16[256,256]{1,0:T(8,128)(2,1)S(1)} collective-permute-done((bf16[256,256]{1,0:T(8,128)(2,1)S(1)}, bf16[256,256]{1,0:T(8,128)(2,1)S(1)}, u32[]{:S(2)}, u32[]{:S(2)}) %collective-permute-start.34) | collective-permute-done | bytes 131104 | tf_op jit(solution)/shard_map/ppermute | solution.py:275
  117.6 1.6 %shard_map.83 = bf16[256,2048]{1,0:T(8,128)(2,1)} custom-call(s32[3]{0:T(128)S(1)} %pad_add_fusion.here_ref, bf16[256,256]{1,0:T(8,128)(2,1)S(1)} %get-tuple-element.155.refs_0_, bf16[256,256]{1,0:T(8,128)(2,1)S(1)} %get-tuple-element.156.refs_1_, bf16[256,256]{1,0:T(8,128)(2,1)S(1)} %collective-permute-done.29.refs_2_, ...), custom_call_target="tpu_custom_call" | custom-call | bytes 4194304 | tf_op jit(solution)/shard_map/pallas_call | solution.py:435
  (49 shorter events, 0.3 us)
Async XLA Ops:
  0.0 18.1 %collective-permute-start.3 = (bf16[256,4096]{1,0:T(8,128)(2,1)}, bf16[256,4096]{1,0:T(8,128)(2,1)}, u32[]{:S(2)}, u32[]{:S(2)}) collective-permute-start(bf16[256,4096]{1,0:T(8,128)(2,1)} %bitcast.3.refs_0_), channel_id=1, source_target_pairs={{0,4},{1,5},{2,6},{3,7},{4,0},{5,1},{6,2},{7,3},{8,12},{9,13},{10,... | collective-permute-start | bytes 6291464 | tf_op jit(solution)/shard_map/ppermute | solution.py:275
  1.4 1.0 copy-start
  2.5 0.9 copy-start.1
  3.4 0.9 copy-start.2
  4.3 0.7 copy-start.4
  5.6 2.0 %collective-permute-start = (bf16[144,768]{1,0:T(8,128)(2,1)S(1)}, bf16[144,768]{1,0:T(8,128)(2,1)S(1)}, u32[]{:S(2)}, u32[]{:S(2)}) collective-permute-start(bf16[144,768]{1,0:T(8,128)(2,1)S(1)} %get-tuple-element.83), channel_id=1, source_target_pairs={{0,4},{1,5},{2,6},{3,7},{4,0},{5,1},{6,2},{7,3},{8,12},{9,13},{10,... | collective-permute-start | bytes 663560 | tf_op jit(solution)/shard_map/ppermute | solution.py:275
  5.7 7.8 %collective-permute-start.2 = (bf16[144,768]{1,0:T(8,128)(2,1)S(1)}, bf16[144,768]{1,0:T(8,128)(2,1)S(1)}, u32[]{:S(2)}, u32[]{:S(2)}) collective-permute-start(bf16[144,768]{1,0:T(8,128)(2,1)S(1)} %get-tuple-element.85), channel_id=1, source_target_pairs={{0,12},{1,13},{2,14},{3,15},{4,8},{5,9},{6,10},{7,11},{8,4},{9,5},... | collective-permute-start | bytes 663560 | tf_op jit(solution)/shard_map/ppermute | solution.py:275
  7.3 10.7 %collective-permute-start.1 = (bf16[144,768]{1,0:T(8,128)(2,1)S(1)}, bf16[144,768]{1,0:T(8,128)(2,1)S(1)}, u32[]{:S(2)}, u32[]{:S(2)}) collective-permute-start(bf16[144,768]{1,0:T(8,128)(2,1)S(1)} %get-tuple-element.84), channel_id=1, source_target_pairs={{0,8},{1,9},{2,10},{3,11},{4,12},{5,13},{6,14},{7,15},{8,0},{9,1},... | collective-permute-start | bytes 663560 | tf_op jit(solution)/shard_map/ppermute | solution.py:275
  18.1 52.4 %collective-permute-start.21 = (bf16[256,4096]{1,0:T(8,128)(2,1)}, bf16[256,4096]{1,0:T(8,128)(2,1)}, u32[]{:S(2)}, u32[]{:S(2)}) collective-permute-start(bf16[256,4096]{1,0:T(8,128)(2,1)} %bitcast.3.refs_0_), channel_id=1, source_target_pairs={{0,8},{1,9},{2,10},{3,11},{4,12},{5,13},{6,14},{7,15},{8,0},{9,1},... | collective-permute-start | bytes 6291464 | tf_op jit(solution)/shard_map/ppermute | solution.py:275
  19.3 9.8 %collective-permute-start.4 = (bf16[256,768]{1,0:T(8,128)(2,1)S(1)}, bf16[256,768]{1,0:T(8,128)(2,1)S(1)}, u32[]{:S(2)}, u32[]{:S(2)}) collective-permute-start(bf16[256,768]{1,0:T(8,128)(2,1)S(1)} %pad_maximum_fusion.refs_2_), channel_id=1, source_target_pairs={{0,1},{1,0},{2,3},{3,2},{4,5},{5,4},{6,7},{7,6},{8,9},{9,8},{10,11... | collective-permute-start | bytes 1179656 | tf_op jit(solution)/shard_map/ppermute | solution.py:275
  19.5 12.8 %collective-permute-start.5 = (bf16[256,768]{1,0:T(8,128)(2,1)S(1)}, bf16[256,768]{1,0:T(8,128)(2,1)S(1)}, u32[]{:S(2)}, u32[]{:S(2)}) collective-permute-start(bf16[256,768]{1,0:T(8,128)(2,1)S(1)} %pad_maximum_fusion.refs_2_), channel_id=1, source_target_pairs={{1,2},{2,1},{5,6},{6,5},{9,10},{10,9},{13,14},{14,13},{17,18},{18,... | collective-permute-start | bytes 1179656 | tf_op jit(solution)/shard_map/ppermute | solution.py:275
  23.8 9.8 %collective-permute-start.6 = (bf16[256,768]{1,0:T(8,128)(2,1)S(1)}, bf16[256,768]{1,0:T(8,128)(2,1)S(1)}, u32[]{:S(2)}, u32[]{:S(2)}) collective-permute-start(bf16[256,768]{1,0:T(8,128)(2,1)S(1)} %pad_maximum_fusion.refs_2_), channel_id=1, source_target_pairs={{0,16},{1,17},{2,18},{3,19},{4,20},{5,21},{6,22},{7,23},{8,24},{9,... | collective-permute-start | bytes 1179656 | tf_op jit(solution)/shard_map/ppermute | solution.py:275
  25.1 12.4 %collective-permute-start.12 = (bf16[256,768]{1,0:T(8,128)(2,1)S(1)}, bf16[256,768]{1,0:T(8,128)(2,1)S(1)}, u32[]{:S(2)}, u32[]{:S(2)}) collective-permute-start(bf16[256,768]{1,0:T(8,128)(2,1)S(1)} %pad_maximum_fusion.1.refs_7_), channel_id=1, source_target_pairs={{0,1},{1,0},{2,3},{3,2},{4,5},{5,4},{6,7},{7,6},{8,9},{9,8},{10,11... | collective-permute-start | bytes 1179656 | tf_op jit(solution)/shard_map/ppermute | solution.py:275
  29.1 10.5 %collective-permute-start.13 = (bf16[256,768]{1,0:T(8,128)(2,1)S(1)}, bf16[256,768]{1,0:T(8,128)(2,1)}, u32[]{:S(2)}, u32[]{:S(2)}) collective-permute-start(bf16[256,768]{1,0:T(8,128)(2,1)S(1)} %pad_maximum_fusion.1.refs_7_), channel_id=1, source_target_pairs={{1,2},{2,1},{5,6},{6,5},{9,10},{10,9},{13,14},{14,13},{17,18},{18,... | collective-permute-start | bytes 1179656 | tf_op jit(solution)/shard_map/ppermute | solution.py:275
  32.3 16.7 %copy-start.7 = (bf16[256,768]{1,0:T(8,128)(2,1)}, bf16[256,768]{1,0:T(8,128)(2,1)S(1)}, u32[]{:S(2)}) copy-start(bf16[256,768]{1,0:T(8,128)(2,1)S(1)} %collective-permute-done.5) | copy-start | bytes 1179652
  32.4 8.6 %collective-permute-start.14 = (bf16[256,768]{1,0:T(8,128)(2,1)S(1)}, bf16[256,768]{1,0:T(8,128)(2,1)S(1)}, u32[]{:S(2)}, u32[]{:S(2)}) collective-permute-start(bf16[256,768]{1,0:T(8,128)(2,1)S(1)} %pad_maximum_fusion.1.refs_7_), channel_id=1, source_target_pairs={{0,16},{1,17},{2,18},{3,19},{4,20},{5,21},{6,22},{7,23},{8,24},{9,... | collective-permute-start | bytes 1179656 | tf_op jit(solution)/shard_map/ppermute | solution.py:275
  33.7 13.3 %collective-permute-start.7 = (bf16[256,768]{1,0:T(8,128)(2,1)S(1)}, bf16[256,768]{1,0:T(8,128)(2,1)S(1)}, u32[]{:S(2)}, u32[]{:S(2)}) collective-permute-start(bf16[256,768]{1,0:T(8,128)(2,1)S(1)} %collective-permute-done.4.refs_3_), channel_id=1, source_target_pairs={{1,2},{2,1},{5,6},{6,5},{9,10},{10,9},{13,14},{14,13},{17,18},{18,... | collective-permute-start | bytes 1179656 | tf_op jit(solution)/shard_map/ppermute | solution.py:275
  37.6 11.5 %collective-permute-start.8 = (bf16[256,768]{1,0:T(8,128)(2,1)S(1)}, bf16[256,768]{1,0:T(8,128)(2,1)S(1)}, u32[]{:S(2)}, u32[]{:S(2)}) collective-permute-start(bf16[256,768]{1,0:T(8,128)(2,1)S(1)} %collective-permute-done.5), channel_id=1, source_target_pairs={{1,0},{2,3},{5,4},{6,7},{9,8},{10,11},{13,12},{14,15},{17,16},{18,... | collective-permute-start | bytes 1179656 | tf_op jit(solution)/shard_map/ppermute | solution.py:275
  39.7 11.4 %collective-permute-start.9 = (bf16[256,768]{1,0:T(8,128)(2,1)S(1)}, bf16[256,768]{1,0:T(8,128)(2,1)}, u32[]{:S(2)}, u32[]{:S(2)}) collective-permute-start(bf16[256,768]{1,0:T(8,128)(2,1)S(1)} %collective-permute-done.4.refs_3_), channel_id=1, source_target_pairs={{0,16},{1,17},{2,18},{3,19},{4,20},{5,21},{6,22},{7,23},{8,24},{9,... | collective-permute-start | bytes 1179656 | tf_op jit(solution)/shard_map/ppermute | solution.py:275
  41.0 14.4 %collective-permute-start.15 = (bf16[256,768]{1,0:T(8,128)(2,1)S(1)}, bf16[256,768]{1,0:T(8,128)(2,1)}, u32[]{:S(2)}, u32[]{:S(2)}) collective-permute-start(bf16[256,768]{1,0:T(8,128)(2,1)S(1)} %collective-permute-done.12.refs_8_), channel_id=1, source_target_pairs={{1,2},{2,1},{5,6},{6,5},{9,10},{10,9},{13,14},{14,13},{17,18},{18,... | collective-permute-start | bytes 1179656 | tf_op jit(solution)/shard_map/ppermute | solution.py:275
  47.0 2.0 %copy-start.5 = (bf16[256,768]{1,0:T(8,128)(2,1)}, bf16[256,768]{1,0:T(8,128)(2,1)S(1)}, u32[]{:S(2)}) copy-start(bf16[256,768]{1,0:T(8,128)(2,1)S(1)} %collective-permute-done.7) | copy-start | bytes 1179652
  47.0 9.7 %collective-permute-start.16 = (bf16[256,768]{1,0:T(8,128)(2,1)}, bf16[256,768]{1,0:T(8,128)(2,1)}, u32[]{:S(2)}, u32[]{:S(2)}) collective-permute-start(bf16[256,768]{1,0:T(8,128)(2,1)} %collective-permute-done.13), channel_id=1, source_target_pairs={{1,0},{2,3},{5,4},{6,7},{9,8},{10,11},{13,12},{14,15},{17,16},{18,... | collective-permute-start | bytes 1179656 | tf_op jit(solution)/shard_map/ppermute | solution.py:275
  49.0 0.8 copy-start.8
  49.8 8.3 %collective-permute-start.17 = (bf16[256,768]{1,0:T(8,128)(2,1)S(1)}, bf16[256,768]{1,0:T(8,128)(2,1)}, u32[]{:S(2)}, u32[]{:S(2)}) collective-permute-start(bf16[256,768]{1,0:T(8,128)(2,1)S(1)} %collective-permute-done.12.refs_8_), channel_id=1, source_target_pairs={{0,16},{1,17},{2,18},{3,19},{4,20},{5,21},{6,22},{7,23},{8,24},{9,... | collective-permute-start | bytes 1179656 | tf_op jit(solution)/shard_map/ppermute | solution.py:275
  51.0 10.8 %collective-permute-start.10 = (bf16[256,768]{1,0:T(8,128)(2,1)}, bf16[256,768]{1,0:T(8,128)(2,1)S(1)}, u32[]{:S(2)}, u32[]{:S(2)}) collective-permute-start(bf16[256,768]{1,0:T(8,128)(2,1)} %copy-done.5), channel_id=1, source_target_pairs={{1,0},{2,3},{5,4},{6,7},{9,8},{10,11},{13,12},{14,15},{17,16},{18,... | collective-permute-start | bytes 1179656 | tf_op jit(solution)/shard_map/ppermute | solution.py:275
  55.4 15.1 %collective-permute-start.11 = (bf16[256,768]{1,0:T(8,128)(2,1)S(1)}, bf16[256,768]{1,0:T(8,128)(2,1)S(1)}, u32[]{:S(2)}, u32[]{:S(2)}) collective-permute-start(bf16[256,768]{1,0:T(8,128)(2,1)S(1)} %broadcast_select_fusion.3.refs_4_), channel_id=1, source_target_pairs={{0,16},{1,17},{2,18},{3,19},{4,20},{5,21},{6,22},{7,23},{8,24},{9,... | collective-permute-start | bytes 1179656 | tf_op jit(solution)/shard_map/ppermute | solution.py:275
  58.1 12.4 %collective-permute-start.18 = (bf16[256,768]{1,0:T(8,128)(2,1)}, bf16[256,768]{1,0:T(8,128)(2,1)S(1)}, u32[]{:S(2)}, u32[]{:S(2)}) collective-permute-start(bf16[256,768]{1,0:T(8,128)(2,1)} %collective-permute-done.15), channel_id=1, source_target_pairs={{1,0},{2,3},{5,4},{6,7},{9,8},{10,11},{13,12},{14,15},{17,16},{18,... | collective-permute-start | bytes 1179656 | tf_op jit(solution)/shard_map/ppermute | solution.py:275
  60.5 23.0 %copy-start.6 = (bf16[256,768]{1,0:T(8,128)(2,1)S(1)}, bf16[256,768]{1,0:T(8,128)(2,1)}, u32[]{:S(2)}) copy-start(bf16[256,768]{1,0:T(8,128)(2,1)} %copy-done.5) | copy-start | bytes 1179652
  60.5 11.8 %collective-permute-start.19 = (bf16[256,768]{1,0:T(8,128)(2,1)S(1)}, bf16[256,768]{1,0:T(8,128)(2,1)S(1)}, u32[]{:S(2)}, u32[]{:S(2)}) collective-permute-start(bf16[256,768]{1,0:T(8,128)(2,1)S(1)} %broadcast_select_fusion.1.refs_9_), channel_id=1, source_target_pairs={{0,16},{1,17},{2,18},{3,19},{4,20},{5,21},{6,22},{7,23},{8,24},{9,... | collective-permute-start | bytes 1179656 | tf_op jit(solution)/shard_map/ppermute | solution.py:275
  61.8 10.5 %collective-permute-start.20 = (bf16[256,768]{1,0:T(8,128)(2,1)}, bf16[256,768]{1,0:T(8,128)(2,1)S(1)}, u32[]{:S(2)}, u32[]{:S(2)}) collective-permute-start(bf16[256,768]{1,0:T(8,128)(2,1)} %collective-permute-done.17.refs_11_), channel_id=1, source_target_pairs={{1,2},{2,1},{5,6},{6,5},{9,10},{10,9},{13,14},{14,13},{17,18},{18,... | collective-permute-start | bytes 1179656 | tf_op jit(solution)/shard_map/ppermute | solution.py:275
  72.3 16.5 %collective-permute-start.24 = (bf16[256,4096]{1,0:T(8,128)(2,1)}, bf16[256,4096]{1,0:T(8,128)(2,1)S(1)}, u32[]{:S(2)}, u32[]{:S(2)}) collective-permute-start(bf16[256,4096]{1,0:T(8,128)(2,1)} %collective-permute-done.21.refs_0_), channel_id=1, source_target_pairs={{0,4},{1,5},{2,6},{3,7},{4,0},{5,1},{6,2},{7,3},{8,12},{9,13},{10,... | collective-permute-start | bytes 6291464 | tf_op jit(solution)/shard_map/ppermute | solution.py:275
  83.6 9.6 %collective-permute-start.22 = (bf16[256,256]{1,0:T(8,128)(2,1)S(1)}, bf16[256,256]{1,0:T(8,128)(2,1)S(1)}, u32[]{:S(2)}, u32[]{:S(2)}) collective-permute-start(bf16[256,256]{1,0:T(8,128)(2,1)S(1)} %slice.39), channel_id=1, source_target_pairs={{0,16},{1,17},{2,18},{3,19},{4,20},{5,21},{6,22},{7,23},{8,24},{9,... | collective-permute-start | bytes 393224 | tf_op jit(solution)/shard_map/ppermute | solution.py:275
  83.9 14.8 %collective-permute-start.26 = (bf16[256,512]{1,0:T(8,128)(2,1)S(1)}, bf16[256,512]{1,0:T(8,128)(2,1)S(1)}, u32[]{:S(2)}, u32[]{:S(2)}) collective-permute-start(bf16[256,512]{1,0:T(8,128)(2,1)S(1)} %slice.40), channel_id=1, source_target_pairs={{0,16},{1,17},{2,18},{3,19},{4,20},{5,21},{6,22},{7,23},{8,24},{9,... | collective-permute-start | bytes 786440 | tf_op jit(solution)/shard_map/ppermute | solution.py:275
  85.1 8.1 %collective-permute-start.23 = (bf16[256,256]{1,0:T(8,128)(2,1)S(1)}, bf16[256,256]{1,0:T(8,128)(2,1)S(1)}, u32[]{:S(2)}, u32[]{:S(2)}) collective-permute-start(bf16[256,256]{1,0:T(8,128)(2,1)S(1)} %get-tuple-element.161), channel_id=1, source_target_pairs={{1,0},{2,3},{5,4},{6,7},{9,8},{10,11},{13,12},{14,15},{17,16},{18,... | collective-permute-start | bytes 393224 | tf_op jit(solution)/shard_map/ppermute | solution.py:275
  86.5 12.2 %collective-permute-start.27 = (bf16[256,256]{1,0:T(8,128)(2,1)S(1)}, bf16[256,256]{1,0:T(8,128)(2,1)S(1)}, u32[]{:S(2)}, u32[]{:S(2)}) collective-permute-start(bf16[256,256]{1,0:T(8,128)(2,1)S(1)} %get-tuple-element.160), channel_id=1, source_target_pairs={{1,0},{2,3},{5,4},{6,7},{9,8},{10,11},{13,12},{14,15},{17,16},{18,... | collective-permute-start | bytes 393224 | tf_op jit(solution)/shard_map/ppermute | solution.py:275
  95.2 6.0 %collective-permute-start.25 = (bf16[128,256]{1,0:T(8,128)(2,1)S(1)}, bf16[128,256]{1,0:T(8,128)(2,1)S(1)}, u32[]{:S(2)}, u32[]{:S(2)}) collective-permute-start(bf16[128,256]{1,0:T(8,128)(2,1)S(1)} %get-tuple-element.121), channel_id=1, source_target_pairs={{0,16},{1,17},{2,18},{3,19},{4,20},{5,21},{6,22},{7,23},{8,24},{9,... | collective-permute-start | bytes 196616 | tf_op jit(solution)/shard_map/ppermute | solution.py:275
  97.4 7.6 %collective-permute-start.28 = (bf16[256,256]{1,0:T(8,128)(2,1)S(1)}, bf16[256,256]{1,0:T(8,128)(2,1)S(1)}, u32[]{:S(2)}, u32[]{:S(2)}) collective-permute-start(bf16[256,256]{1,0:T(8,128)(2,1)S(1)} %get-tuple-element.133), channel_id=1, source_target_pairs={{1,0},{2,3},{5,4},{6,7},{9,8},{10,11},{13,12},{14,15},{17,16},{18,... | collective-permute-start | bytes 393224 | tf_op jit(solution)/shard_map/ppermute | solution.py:275
  98.7 2.5 %copy-start.3 = (f32[16]{0:T(128)S(1)}, f32[16]{0:T(128)}, u32[]{:S(2)}) copy-start(f32[16]{0:T(128)} %gate_ref.5) | copy-start | bytes 196
  102.4 9.8 %collective-permute-start.31 = (bf16[256,256]{1,0:T(8,128)(2,1)S(1)}, bf16[256,256]{1,0:T(8,128)(2,1)S(1)}, u32[]{:S(2)}, u32[]{:S(2)}) collective-permute-start(bf16[256,256]{1,0:T(8,128)(2,1)S(1)} %get-tuple-element.136), channel_id=1, source_target_pairs={{0,8},{1,9},{2,10},{3,11},{4,12},{5,13},{6,14},{7,15},{8,0},{9,1},... | collective-permute-start | bytes 393224 | tf_op jit(solution)/shard_map/ppermute | solution.py:275
  102.5 11.0 %collective-permute-start.33 = (bf16[256,256]{1,0:T(8,128)(2,1)S(1)}, bf16[256,256]{1,0:T(8,128)(2,1)S(1)}, u32[]{:S(2)}, u32[]{:S(2)}) collective-permute-start(bf16[256,256]{1,0:T(8,128)(2,1)S(1)} %get-tuple-element.137), channel_id=1, source_target_pairs={{0,12},{1,13},{2,14},{3,15},{4,8},{5,9},{6,10},{7,11},{8,4},{9,5},... | collective-permute-start | bytes 393224 | tf_op jit(solution)/shard_map/ppermute | solution.py:275
  108.1 5.5 %collective-permute-start.32 = (bf16[256,256]{1,0:T(8,128)(2,1)S(1)}, bf16[256,256]{1,0:T(8,128)(2,1)S(1)}, u32[]{:S(2)}, u32[]{:S(2)}) collective-permute-start(bf16[256,256]{1,0:T(8,128)(2,1)S(1)} %get-tuple-element.143), channel_id=1, source_target_pairs={{0,8},{1,9},{2,10},{3,11},{4,12},{5,13},{6,14},{7,15},{8,0},{9,1},... | collective-permute-start | bytes 393224 | tf_op jit(solution)/shard_map/ppermute | solution.py:275
  111.6 2.0 %collective-permute-start.29 = (bf16[256,256]{1,0:T(8,128)(2,1)S(1)}, bf16[256,256]{1,0:T(8,128)(2,1)S(1)}, u32[]{:S(2)}, u32[]{:S(2)}) collective-permute-start(bf16[256,256]{1,0:T(8,128)(2,1)S(1)} %get-tuple-element.157), channel_id=1, source_target_pairs={{0,4},{1,5},{2,6},{3,7},{4,0},{5,1},{6,2},{7,3},{8,12},{9,13},{10,... | collective-permute-start | bytes 393224 | tf_op jit(solution)/shard_map/ppermute | solution.py:275
  112.0 1.6 %collective-permute-start.30 = (bf16[256,256]{1,0:T(8,128)(2,1)S(1)}, bf16[256,256]{1,0:T(8,128)(2,1)S(1)}, u32[]{:S(2)}, u32[]{:S(2)}) collective-permute-start(bf16[256,256]{1,0:T(8,128)(2,1)S(1)} %get-tuple-element.158), channel_id=1, source_target_pairs={{0,4},{1,5},{2,6},{3,7},{4,0},{5,1},{6,2},{7,3},{8,12},{9,13},{10,... | collective-permute-start | bytes 393224 | tf_op jit(solution)/shard_map/ppermute | solution.py:275
  112.2 5.5 %collective-permute-start.34 = (bf16[256,256]{1,0:T(8,128)(2,1)S(1)}, bf16[256,256]{1,0:T(8,128)(2,1)S(1)}, u32[]{:S(2)}, u32[]{:S(2)}) collective-permute-start(bf16[256,256]{1,0:T(8,128)(2,1)S(1)} %get-tuple-element.144), channel_id=1, source_target_pairs={{0,12},{1,13},{2,14},{3,15},{4,8},{5,9},{6,10},{7,11},{8,4},{9,5},... | collective-permute-start | bytes 393224 | tf_op jit(solution)/shard_map/ppermute | solution.py:275

commit v10 on v9

--- a/solution.py
+++ b/solution.py
@@ -103,29 +103,28 @@
     return high, (values - high.astype(jnp.float32)).astype(jnp.bfloat16)
 
 
-def late_rows(here_ref, last_ref, start, width, *pieces):
-    *whole, upper, inner, outer = pieces
-    rows = [piece[:, start : start + width] for piece in whole]
-    lost = whole[0].shape[1] - upper.shape[1] if start else 0
-    rows.append(upper[:, start - lost : start - lost + width])
+def late_rows(here_ref, chosen_ref, start, width, *pieces):
+    *whole, inner, outer, part = pieces
+    lost = inner.shape[1] - outer.shape[1] if start else 0
     inside = (here_ref[2] == 1) | (here_ref[2] == 2)
 
     @pl.when(inside)
     def _():
-        last_ref[...] = inner[:, start : start + width]
+        chosen_ref[...] = inner[:, start : start + width]
 
     @pl.when(jnp.logical_not(inside))
     def _():
-        last_ref[...] = outer[...]
-
-    return jnp.concatenate(rows + [last_ref[...]], axis=0)
+        chosen_ref[...] = outer[:, start - lost : start - lost + width]
+
+    rows = [piece[:, start : start + width] for piece in whole]
+    return jnp.concatenate(rows + [chosen_ref[...], part[...]], axis=0)
 
 
 def kv_body(n_late, here_ref, *refs):
-    pieces, refs, last_ref = refs[:n_late], refs[n_late:-1], refs[-1]
+    pieces, refs, chosen_ref = refs[:n_late], refs[n_late:-1], refs[-1]
     sums, lates, messages = refs[:MEMBERS], refs[MEMBERS : 2 * MEMBERS], refs[2 * MEMBERS : 3 * MEMBERS]
     outs = refs[3 * MEMBERS :]
-    rows = late_rows(here_ref, last_ref, 0, 2 * HEAD_SIZE, *pieces)
+    rows = late_rows(here_ref, chosen_ref, 0, 2 * HEAD_SIZE, *pieces)
     kvs = []
     for seg in range(MEMBERS):
         total = sums[seg][:, : 2 * HEAD_SIZE]
@@ -152,9 +151,9 @@
 
 
 def local_body(n, n_late, start, heads, here_ref, *refs):
-    pieces, refs, last_ref = refs[:n_late], refs[n_late:-1], refs[-1]
+    pieces, refs, chosen_ref = refs[:n_late], refs[n_late:-1], refs[-1]
     kvs, messages, sums, lates, outs = [refs[k * n : (k + 1) * n] for k in range(4)] + [refs[4 * n :]]
-    rows = late_rows(here_ref, last_ref, start, heads * HEAD_SIZE, *pieces)
+    rows = late_rows(here_ref, chosen_ref, start, heads * HEAD_SIZE, *pieces)
     columns = slice(start, start + heads * HEAD_SIZE)
     queries = []
     for at in range(n):
@@ -342,10 +341,10 @@
         a_middle, a_outer, a_far1 = locked(*stage2(a_one, a_inner))
         b_middle, b_outer, b_far1 = locked(*stage2(b_one, b_inner))
         a_two = jnp.where(inside, a_inner, a_outer)
-        a_last, a_far2 = stage3(a_middle, a_two)
+        a_inner, (a_last, a_far2) = inward(a_far1), stage3(a_middle, a_two)
         b_two = jnp.where(inside, b_inner, b_outer)
-        b_last, b_far2, b_inner = *stage3(b_middle, b_two), inward(b_far1)
-        a_last, a_far2, a_middle = locked(a_last, a_far2, a_middle)
+        b_last, b_far2 = stage3(b_middle, b_two)
+        a_last, a_far2, a_middle, a_inner = locked(a_last, a_far2, a_middle, a_inner)
         a_three = jnp.where(inside, a_middle, a_last)
         books = [own, sibling]
         upper = [a, a_one, a_two, None, a_far0, a_far1]
@@ -353,16 +352,16 @@
         early = [(k, half) for half in range(2) for k in (0, 1, 2, 4, 5)]
         late = [(3, 0), (6, 0), (3, 1), (6, 1), (7, 0), (7, 1)]
         project((0, 1), early, late, (upper, lower), n_z)
-        b_last, b_far2, b_middle, b_inner, sums[0], sums[1], across = locked(
-            b_last, b_far2, b_middle, b_inner, sums[0], sums[1], after(across, a_last, a_far2)
+        b_last, b_far2, b_middle, sums[0], sums[1], across = locked(
+            b_last, b_far2, b_middle, sums[0], sums[1], after(across, a_last, a_far2)
         )
         books += [across, to_member(across, 1)]
         project((2, 3), early, late, (upper, lower), n_z)
         b_three = jnp.where(inside, b_middle, b_last)
         pieces = [a_three, a_far2, b_three, b_far2]
-        upper_kv, upper_q = [over(a_three[:, at]) for at in (slice(0, cut), slice(cut, None))]
-        inner = b_inner
-        finish = lambda at, *others: outward(after(b_inner[:, at], *others))
+        outer_kv, outer_q = [outward(a_inner[:, at]) for at in (slice(0, cut), slice(cut, None))]
+        inner = a_inner
+        finish = lambda at, *others: over(after(b_three[:, at], *others))
     else:
         across, sibling = to_member(tokens[0], 2), to_member(tokens[0], 1)
         books = [tokens[0], sibling, across, to_member(across, 1)]
@@ -376,9 +375,9 @@
         for segs in ((0, 1), (2, 3)):
             project(segs, early, late, (upper, lower), 0)
         pieces = [lower[-2]]
-        upper_kv, upper_q = upper[-1][:, :cut], upper[-1][:, cut:]
-        inner = lower[-1]
-        finish = lambda at, *others: inner[:, at]
+        outer_kv, outer_q = upper[-1][:, :cut], upper[-1][:, cut:]
+        inner = upper[-1]
+        finish = lambda at, *others: lower[-1][:, at]
 
     halves = [slice(k * HEAD_SIZE, (k + 2) * HEAD_SIZE) for k in (0, 2, 4)]
     lower_kv, lower_q0 = finish(halves[0]), finish(halves[1])
@@ -389,7 +388,7 @@
         [SMEM] + [VMEM] * (len(late) + 1 + 3 * MEMBERS),
         flops=2 * MEMBERS * length * len(late) * MEMBERS * HEAD_SIZE * HEAD_SIZE,
         scratch=[pltpu.VMEM((MEMBERS * HEAD_SIZE // 2, cut), bf16)],
-    )(here, *pieces, upper_kv, inner, lower_kv, *sums, *lates, *messages)
+    )(here, *pieces, inner, outer_kv, lower_kv, *sums, *lates, *messages)
     kvs, deltas, total = found[0:-1:2], found[1:-1:2], found[-1]
 
     base = None
@@ -407,7 +406,7 @@
             [SMEM] + [VMEM] * (len(late) + 1 + 4 * len(segs)),
             flops=4 * len(segs) * length * length * half * HEAD_SIZE,
             scratch=[pltpu.VMEM((MEMBERS * HEAD_SIZE // 2, half * HEAD_SIZE), bf16)],
-        )(here, *pieces, upper_q, inner, lower_q, *[one[s] for one in (kvs, messages, sums, lates) for s in segs])
+        )(here, *pieces, inner, outer_q, lower_q, *[one[s] for one in (kvs, messages, sums, lates) for s in segs])
         return {(s, part): (found[2 * at], found[2 * at + 1]) for at, s in enumerate(segs)}
 
     def mix(segs, parts, base, ready):

time: 120 us -> 119 us (level); the launches traced: 119 us -> 117 us
  starting transfers between devices: 60.5 us -> 55.2 us
  waiting for transfers between devices: 26.3 us -> 29 us
    ppermute x35, starting transfers between devices: 60.5 us -> 55.2 us  [permute(): return lax.ppermute(array, AXES, pairs)]
    ppermute x35, waiting for transfers between devices: 26.3 us -> 29 us  [permute(): return lax.ppermute(array, AXES, pairs)]
  transfers between devices with their start and end apart: 35 -> 35, of which waited for: 9 -> 10; matrix products, arithmetic and copies ran while one was open for 3% -> 3% of each run, Pallas kernels for 18% -> 19%
where the time goes in v10:
time: 119 us; the launch traced here: 117 us
  starting transfers between devices  55.2 us (46%)
  waiting for transfers between devices  29 us (24%)
  Pallas kernels  23.5 us (20%)
  local copies, waits for them, and re-layouts  4.41 us (4%)
  other arithmetic  3.35 us (3%)
    ppermute x35, starting transfers between devices, permute(): return lax.ppermute(array, AXES, pairs)  55.2 us
    ppermute x35, waiting for transfers between devices, permute(): return lax.ppermute(array, AXES, pairs)  29 us
    pallas_call x2, Pallas kernels, project(): call(functools.partial(project_body, early, late, line), [shape((length,...  9.37 us
    pallas_call x3, Pallas kernels, local(): call(functools.partial(local_body, len(segs), len(late) + 1, halves[1 + p...  6.02 us
    unnamed x18, local copies, waits for them, and re-layouts  4.3 us
    pallas_call x3, Pallas kernels, mix(): call(functools.partial(mix_body, segs, parts, group), [shape((length, hal...  3.96 us
  transfers between devices with their start and end apart: 35, of which 10 were waited for; matrix products, arithmetic and copies ran while one was open for 3% of the time, Pallas kernels for 19%

profile of v10, /device:TPU:9, one launch (start us, length us, event | category | flops | bytes accessed | tf_op | source)
XLA Modules:
  0.0 116.6 jit_solution(18174741909606327897)
XLA Ops:
  0.0 0.7 collective-permute-start.3
  1.3 0.1 pad_add_fusion.here_ref
  1.4 1.0 copy-done
  2.5 0.9 copy-done.1
  3.4 0.9 copy-done.2
  4.3 0.7 copy-done.4
  4.9 0.6 shard_map.73
  5.6 0.1 collective-permute-start
  5.7 1.6 %collective-permute-start.2 = (bf16[144,768]{1,0:T(8,128)(2,1)S(1)}, bf16[144,768]{1,0:T(8,128)(2,1)S(1)}, u32[]{:S(2)}, u32[]{:S(2)}) collective-permute-start(bf16[144,768]{1,0:T(8,128)(2,1)S(1)} %get-tuple-element.85), channel_id=1, source_target_pairs={{0,12},{1,13},{2,14},{3,15},{4,8},{5,9},{6,10},{7,11},{8,4},{9,5},... | collective-permute-start | bytes 663560 | tf_op jit(solution)/shard_map/ppermute | solution.py:274
  7.3 0.3 collective-permute-start.1
  7.6 5.9 %collective-permute-done.2.refs_18_.refs_12_.refs_5_.refs_10_ = bf16[144,768]{1,0:T(8,128)(2,1)S(1)} collective-permute-done((bf16[144,768]{1,0:T(8,128)(2,1)S(1)}, bf16[144,768]{1,0:T(8,128)(2,1)S(1)}, u32[]{:S(2)}, u32[]{:S(2)}) %collective-permute-start.2) | collective-permute-done | bytes 221216 | tf_op jit(solution)/shard_map/ppermute | solution.py:274
  13.5 4.5 %collective-permute-done.1.refs_17_.refs_11_.refs_4_.refs_9_ = bf16[144,768]{1,0:T(8,128)(2,1)S(1)} collective-permute-done((bf16[144,768]{1,0:T(8,128)(2,1)S(1)}, bf16[144,768]{1,0:T(8,128)(2,1)S(1)}, u32[]{:S(2)}, u32[]{:S(2)}) %collective-permute-start.1) | collective-permute-done | bytes 221216 | tf_op jit(solution)/shard_map/ppermute | solution.py:274
  18.1 1.3 %collective-permute-start.21 = (bf16[256,4096]{1,0:T(8,128)(2,1)}, bf16[256,4096]{1,0:T(8,128)(2,1)}, u32[]{:S(2)}, u32[]{:S(2)}) collective-permute-start(bf16[256,4096]{1,0:T(8,128)(2,1)} %bitcast.3.refs_0_), channel_id=1, source_target_pairs={{0,8},{1,9},{2,10},{3,11},{4,12},{5,13},{6,14},{7,15},{8,0},{9,1},... | collective-permute-start | bytes 6291464 | tf_op jit(solution)/shard_map/ppermute | solution.py:274
  19.3 0.2 collective-permute-start.4
  19.5 4.3 %collective-permute-start.5 = (bf16[256,768]{1,0:T(8,128)(2,1)S(1)}, bf16[256,768]{1,0:T(8,128)(2,1)S(1)}, u32[]{:S(2)}, u32[]{:S(2)}) collective-permute-start(bf16[256,768]{1,0:T(8,128)(2,1)S(1)} %pad_maximum_fusion.refs_2_), channel_id=1, source_target_pairs={{1,2},{2,1},{5,6},{6,5},{9,10},{10,9},{13,14},{14,13},{17,18},{18,... | collective-permute-start | bytes 1179656 | tf_op jit(solution)/shard_map/ppermute | solution.py:274
  23.8 1.3 %collective-permute-start.6 = (bf16[256,768]{1,0:T(8,128)(2,1)S(1)}, bf16[256,768]{1,0:T(8,128)(2,1)S(1)}, u32[]{:S(2)}, u32[]{:S(2)}) collective-permute-start(bf16[256,768]{1,0:T(8,128)(2,1)S(1)} %pad_maximum_fusion.refs_2_), channel_id=1, source_target_pairs={{0,16},{1,17},{2,18},{3,19},{4,20},{5,21},{6,22},{7,23},{8,24},{9,... | collective-permute-start | bytes 1179656 | tf_op jit(solution)/shard_map/ppermute | solution.py:274
  25.2 4.0 %collective-permute-done.4.refs_3_ = bf16[256,768]{1,0:T(8,128)(2,1)S(1)} collective-permute-done((bf16[256,768]{1,0:T(8,128)(2,1)S(1)}, bf16[256,768]{1,0:T(8,128)(2,1)S(1)}, u32[]{:S(2)}, u32[]{:S(2)}) %collective-permute-start.4) | collective-permute-done | bytes 393248 | tf_op jit(solution)/shard_map/ppermute | solution.py:274
  29.1 3.2 %collective-permute-start.14 = (bf16[256,768]{1,0:T(8,128)(2,1)S(1)}, bf16[256,768]{1,0:T(8,128)(2,1)}, u32[]{:S(2)}, u32[]{:S(2)}) collective-permute-start(bf16[256,768]{1,0:T(8,128)(2,1)S(1)} %pad_maximum_fusion.1.refs_7_), channel_id=1, source_target_pairs={{1,2},{2,1},{5,6},{6,5},{9,10},{10,9},{13,14},{14,13},{17,18},{18,... | collective-permute-start | bytes 1179656 | tf_op jit(solution)/shard_map/ppermute | solution.py:274
  32.4 1.3 %collective-permute-start.15 = (bf16[256,768]{1,0:T(8,128)(2,1)S(1)}, bf16[256,768]{1,0:T(8,128)(2,1)S(1)}, u32[]{:S(2)}, u32[]{:S(2)}) collective-permute-start(bf16[256,768]{1,0:T(8,128)(2,1)S(1)} %pad_maximum_fusion.1.refs_7_), channel_id=1, source_target_pairs={{0,16},{1,17},{2,18},{3,19},{4,20},{5,21},{6,22},{7,23},{8,24},{9,... | collective-permute-start | bytes 1179656 | tf_op jit(solution)/shard_map/ppermute | solution.py:274
  33.7 2.8 %collective-permute-start.7 = (bf16[256,768]{1,0:T(8,128)(2,1)S(1)}, bf16[256,768]{1,0:T(8,128)(2,1)S(1)}, u32[]{:S(2)}, u32[]{:S(2)}) collective-permute-start(bf16[256,768]{1,0:T(8,128)(2,1)S(1)} %collective-permute-done.4.refs_3_), channel_id=1, source_target_pairs={{1,2},{2,1},{5,6},{6,5},{9,10},{10,9},{13,14},{14,13},{17,18},{18,... | collective-permute-start | bytes 1179656 | tf_op jit(solution)/shard_map/ppermute | solution.py:274
  36.5 1.1 collective-permute-done.13.refs_8_
  37.6 2.1 %collective-permute-start.8 = (bf16[256,768]{1,0:T(8,128)(2,1)S(1)}, bf16[256,768]{1,0:T(8,128)(2,1)S(1)}, u32[]{:S(2)}, u32[]{:S(2)}) collective-permute-start(bf16[256,768]{1,0:T(8,128)(2,1)S(1)} %collective-permute-done.5), channel_id=1, source_target_pairs={{1,0},{2,3},{5,4},{6,7},{9,8},{10,11},{13,12},{14,15},{17,16},{18,... | collective-permute-start | bytes 1179656 | tf_op jit(solution)/shard_map/ppermute | solution.py:274
  39.7 1.3 %collective-permute-start.9 = (bf16[256,768]{1,0:T(8,128)(2,1)S(1)}, bf16[256,768]{1,0:T(8,128)(2,1)}, u32[]{:S(2)}, u32[]{:S(2)}) collective-permute-start(bf16[256,768]{1,0:T(8,128)(2,1)S(1)} %collective-permute-done.4.refs_3_), channel_id=1, source_target_pairs={{0,16},{1,17},{2,18},{3,19},{4,20},{5,21},{6,22},{7,23},{8,24},{9,... | collective-permute-start | bytes 1179656 | tf_op jit(solution)/shard_map/ppermute | solution.py:274
  41.0 4.3 %collective-permute-start.16 = (bf16[256,768]{1,0:T(8,128)(2,1)S(1)}, bf16[256,768]{1,0:T(8,128)(2,1)}, u32[]{:S(2)}, u32[]{:S(2)}) collective-permute-start(bf16[256,768]{1,0:T(8,128)(2,1)S(1)} %collective-permute-done.13.refs_8_), channel_id=1, source_target_pairs={{1,2},{2,1},{5,6},{6,5},{9,10},{10,9},{13,14},{14,13},{17,18},{18,... | collective-permute-start | bytes 1179656 | tf_op jit(solution)/shard_map/ppermute | solution.py:274
  45.3 1.7 %collective-permute-done.7 = bf16[256,768]{1,0:T(8,128)(2,1)S(1)} collective-permute-done((bf16[256,768]{1,0:T(8,128)(2,1)S(1)}, bf16[256,768]{1,0:T(8,128)(2,1)S(1)}, u32[]{:S(2)}, u32[]{:S(2)}) %collective-permute-start.7) | collective-permute-done | bytes 393248 | tf_op jit(solution)/shard_map/ppermute | solution.py:274
  47.0 2.0 %collective-permute-start.17 = (bf16[256,768]{1,0:T(8,128)(2,1)}, bf16[256,768]{1,0:T(8,128)(2,1)}, u32[]{:S(2)}, u32[]{:S(2)}) collective-permute-start(bf16[256,768]{1,0:T(8,128)(2,1)} %collective-permute-done.14), channel_id=1, source_target_pairs={{1,0},{2,3},{5,4},{6,7},{9,8},{10,11},{13,12},{14,15},{17,16},{18,... | collective-permute-start | bytes 1179656 | tf_op jit(solution)/shard_map/ppermute | solution.py:274
  49.0 0.7 copy-done.8
  49.8 1.2 %collective-permute-start.18 = (bf16[256,768]{1,0:T(8,128)(2,1)S(1)}, bf16[256,768]{1,0:T(8,128)(2,1)}, u32[]{:S(2)}, u32[]{:S(2)}) collective-permute-start(bf16[256,768]{1,0:T(8,128)(2,1)S(1)} %collective-permute-done.13.refs_8_), channel_id=1, source_target_pairs={{0,16},{1,17},{2,18},{3,19},{4,20},{5,21},{6,22},{7,23},{8,24},{9,... | collective-permute-start | bytes 1179656 | tf_op jit(solution)/shard_map/ppermute | solution.py:274
  51.0 1.5 %collective-permute-start.10 = (bf16[256,768]{1,0:T(8,128)(2,1)}, bf16[256,768]{1,0:T(8,128)(2,1)S(1)}, u32[]{:S(2)}, u32[]{:S(2)}) collective-permute-start(bf16[256,768]{1,0:T(8,128)(2,1)} %copy-done.5), channel_id=1, source_target_pairs={{1,0},{2,3},{5,4},{6,7},{9,8},{10,11},{13,12},{14,15},{17,16},{18,... | collective-permute-start | bytes 1179656 | tf_op jit(solution)/shard_map/ppermute | solution.py:274
  52.5 1.1 broadcast_select_fusion.3.refs_4_
  53.6 1.8 %collective-permute-done.16 = bf16[256,768]{1,0:T(8,128)(2,1)} collective-permute-done((bf16[256,768]{1,0:T(8,128)(2,1)S(1)}, bf16[256,768]{1,0:T(8,128)(2,1)}, u32[]{:S(2)}, u32[]{:S(2)}) %collective-permute-start.16) | collective-permute-done | bytes 393248 | tf_op jit(solution)/shard_map/ppermute | solution.py:274
  55.4 1.2 %collective-permute-start.11 = (bf16[256,768]{1,0:T(8,128)(2,1)S(1)}, bf16[256,768]{1,0:T(8,128)(2,1)S(1)}, u32[]{:S(2)}, u32[]{:S(2)}) collective-permute-start(bf16[256,768]{1,0:T(8,128)(2,1)S(1)} %broadcast_select_fusion.3.refs_4_), channel_id=1, source_target_pairs={{0,16},{1,17},{2,18},{3,19},{4,20},{5,21},{6,22},{7,23},{8,24},{9,... | collective-permute-start | bytes 1179656 | tf_op jit(solution)/shard_map/ppermute | solution.py:274
  56.6 3.2 %collective-permute-start.12 = (bf16[256,768]{1,0:T(8,128)(2,1)}, bf16[256,768]{1,0:T(8,128)(2,1)S(1)}, u32[]{:S(2)}, u32[]{:S(2)}) collective-permute-start(bf16[256,768]{1,0:T(8,128)(2,1)} %collective-permute-done.9.refs_6_), channel_id=1, source_target_pairs={{1,2},{2,1},{5,6},{6,5},{9,10},{10,9},{13,14},{14,13},{17,18},{18,... | collective-permute-start | bytes 1179656 | tf_op jit(solution)/shard_map/ppermute | solution.py:274
  59.8 1.3 %collective-permute-start.19 = (bf16[256,768]{1,0:T(8,128)(2,1)}, bf16[256,768]{1,0:T(8,128)(2,1)S(1)}, u32[]{:S(2)}, u32[]{:S(2)}) collective-permute-start(bf16[256,768]{1,0:T(8,128)(2,1)} %collective-permute-done.16), channel_id=1, source_target_pairs={{1,0},{2,3},{5,4},{6,7},{9,8},{10,11},{13,12},{14,15},{17,16},{18,... | collective-permute-start | bytes 1179656 | tf_op jit(solution)/shard_map/ppermute | solution.py:274
  61.2 1.1 broadcast_select_fusion.1.refs_9_
  62.2 0.3 collective-permute-start.20
  62.5 5.0 %shard_map.74 = (f32[256,768]{1,0:T(8,128)S(1)}, f32[256,768]{1,0:T(8,128)S(1)}, bf16[256,1536]{1,0:T(8,128)(2,1)S(1)}, bf16[256,1536]{1,0:T(8,128)(2,1)S(1)}) custom-call(s32[3]{0:T(128)S(1)} %pad_add_fusion.here_ref, bf16[256,4096]{1,0:T(8,128)(2,1)} %bitcast.3.refs_0_, bf16[256,4096]{1,0:T(8,128)(2,1)} %collective-permute-done.3.refs_1_, ...), custom_call_target="tpu_custom_call" | custom-call | flops 2013265920 | bytes 4194304 | tf_op jit(solution)/shard_map/pallas_call | solution.py:311
  67.6 2.6 %collective-permute-done.19 = bf16[256,768]{1,0:T(8,128)(2,1)S(1)} collective-permute-done((bf16[256,768]{1,0:T(8,128)(2,1)}, bf16[256,768]{1,0:T(8,128)(2,1)S(1)}, u32[]{:S(2)}, u32[]{:S(2)}) %collective-permute-start.19) | collective-permute-done | bytes 393248 | tf_op jit(solution)/shard_map/ppermute | solution.py:274
  70.1 3.4 %collective-permute-done.20.refs_3_ = bf16[256,768]{1,0:T(8,128)(2,1)S(1)} collective-permute-done((bf16[256,768]{1,0:T(8,128)(2,1)S(1)}, bf16[256,768]{1,0:T(8,128)(2,1)S(1)}, u32[]{:S(2)}, u32[]{:S(2)}) %collective-permute-start.20) | collective-permute-done | bytes 393248 | tf_op jit(solution)/shard_map/ppermute | solution.py:274
  73.5 6.1 %collective-permute-start.24 = (bf16[256,4096]{1,0:T(8,128)(2,1)}, bf16[256,4096]{1,0:T(8,128)(2,1)S(1)}, u32[]{:S(2)}, u32[]{:S(2)}) collective-permute-start(bf16[256,4096]{1,0:T(8,128)(2,1)} %collective-permute-done.21.refs_0_), channel_id=1, source_target_pairs={{0,4},{1,5},{2,6},{3,7},{4,0},{5,1},{6,2},{7,3},{8,12},{9,13},{10,... | collective-permute-start | bytes 6291464 | tf_op jit(solution)/shard_map/ppermute | solution.py:274
  79.6 2.4 %collective-permute-start.22 = (bf16[256,256]{1,0:T(8,128)(2,1)S(1)}, bf16[256,256]{1,0:T(8,128)(2,1)S(1)}, u32[]{:S(2)}, u32[]{:S(2)}) collective-permute-start(bf16[256,256]{1,0:T(8,128)(2,1)S(1)} %slice.31), channel_id=1, source_target_pairs={{1,0},{2,3},{5,4},{6,7},{9,8},{10,11},{13,12},{14,15},{17,16},{18,... | collective-permute-start | bytes 393224 | tf_op jit(solution)/shard_map/ppermute | solution.py:274
  82.1 1.3 %collective-permute-start.26 = (bf16[256,512]{1,0:T(8,128)(2,1)S(1)}, bf16[256,512]{1,0:T(8,128)(2,1)S(1)}, u32[]{:S(2)}, u32[]{:S(2)}) collective-permute-start(bf16[256,512]{1,0:T(8,128)(2,1)S(1)} %slice.33), channel_id=1, source_target_pairs={{1,0},{2,3},{5,4},{6,7},{9,8},{10,11},{13,12},{14,15},{17,16},{18,... | collective-permute-start | bytes 786440 | tf_op jit(solution)/shard_map/ppermute | solution.py:274
  83.4 1.1 broadcast_select_fusion.refs_2_
  84.5 1.6 %collective-permute-start.23 = (bf16[256,256]{1,0:T(8,128)(2,1)S(1)}, bf16[256,256]{1,0:T(8,128)(2,1)S(1)}, u32[]{:S(2)}, u32[]{:S(2)}) collective-permute-start(bf16[256,256]{1,0:T(8,128)(2,1)S(1)} %get-tuple-element.161), channel_id=1, source_target_pairs={{0,16},{1,17},{2,18},{3,19},{4,20},{5,21},{6,22},{7,23},{8,24},{9,... | collective-permute-start | bytes 393224 | tf_op jit(solution)/shard_map/ppermute | solution.py:274
  86.1 0.1 collective-permute-start.27
  86.2 4.4 %shard_map.75 = (f32[256,768]{1,0:T(8,128)S(1)}, f32[256,768]{1,0:T(8,128)S(1)}, bf16[256,1536]{1,0:T(8,128)(2,1)S(1)}, bf16[256,1536]{1,0:T(8,128)(2,1)S(1)}) custom-call(s32[3]{0:T(128)S(1)} %pad_add_fusion.here_ref, bf16[256,4096]{1,0:T(8,128)(2,1)} %collective-permute-done.21.refs_0_, bf16[256,4096]{1,0:T(8,128)(2,1)S(1)} %collective-permute-done.24.refs_1_, ...), custom_call_target="tpu_custom_call" | custom-call | flops 2013265920 | bytes 4194304 | tf_op jit(solution)/shard_map/pallas_call | solution.py:311
  90.6 1.9 %shard_map.76 = (bf16[256,256]{1,0:T(8,128)(2,1)S(1)}, f32[128,256]{1,0:T(8,128)S(1)}, bf16[256,256]{1,0:T(8,128)(2,1)S(1)}, f32[128,256]{1,0:T(8,128)S(1)}, bf1...) custom-call(s32[3]{0:T(128)S(1)} %pad_add_fusion.here_ref, ...), custom_call_target="tpu_custom_call" | custom-call | flops 805306368 | bytes 4194304 | tf_op jit(solution)/shard_map/pallas_call | solution.py:384
  92.5 3.3 %collective-permute-start.25 = (bf16[128,256]{1,0:T(8,128)(2,1)S(1)}, bf16[128,256]{1,0:T(8,128)(2,1)S(1)}, u32[]{:S(2)}, u32[]{:S(2)}) collective-permute-start(bf16[128,256]{1,0:T(8,128)(2,1)S(1)} %get-tuple-element.121), channel_id=1, source_target_pairs={{0,16},{1,17},{2,18},{3,19},{4,20},{5,21},{6,22},{7,23},{8,24},{9,... | collective-permute-start | bytes 196616 | tf_op jit(solution)/shard_map/ppermute | solution.py:274
  95.8 0.1 collective-permute-start.28
  95.9 2.4 %shard_map.77 = (bf16[256,256]{1,0:T(8,128)(2,1)S(1)}, f32[256,256]{1,0:T(8,128)S(1)}, bf16[256,256]{1,0:T(8,128)(2,1)S(1)}, f32[256,256]{1,0:T(8,128)S(1)}, bf1...) custom-call(s32[3]{0:T(128)S(1)} %pad_add_fusion.here_ref, ...), custom_call_target="tpu_custom_call" | custom-call | flops 268435456 | bytes 4194304 | tf_op jit(solution)/shard_map/pallas_call | solution.py:403
  98.4 1.2 %shard_map.78 = (bf16[256,256]{1,0:T(8,128)(2,1)S(1)}, bf16[256,256]{1,0:T(8,128)(2,1)S(1)}) custom-call(s32[3]{0:T(128)S(1)} %pad_add_fusion.here_ref, f32[16]{0:T(128)S(1)} %copy-done.3, bf16[128,256]{1,0:T(8,128)(2,1)S(1)} %collective-permute-done.25.base_ref, f32[128,256]{1,0:T(8,128)S(1)} %get-tuple-element.129.refs_0_, ...), custom_call_target="tpu_custom_call" | custom-call | flops 201326592 | bytes 4194304 | tf_op jit(solution)/shard_map/pallas_call | solution.py:414
  99.6 0.3 collective-permute-start.31
  99.9 2.5 %collective-permute-start.33 = (bf16[256,256]{1,0:T(8,128)(2,1)S(1)}, bf16[256,256]{1,0:T(8,128)(2,1)S(1)}, u32[]{:S(2)}, u32[]{:S(2)}) collective-permute-start(bf16[256,256]{1,0:T(8,128)(2,1)S(1)} %get-tuple-element.137), channel_id=1, source_target_pairs={{0,12},{1,13},{2,14},{3,15},{4,8},{5,9},{6,10},{7,11},{8,4},{9,5},... | collective-permute-start | bytes 393224 | tf_op jit(solution)/shard_map/ppermute | solution.py:274
  102.4 1.9 %shard_map.79 = (bf16[256,256]{1,0:T(8,128)(2,1)S(1)}, f32[256,256]{1,0:T(8,128)S(1)}, bf16[256,256]{1,0:T(8,128)(2,1)S(1)}, f32[256,256]{1,0:T(8,128)S(1)}) custom-call(s32[3]{0:T(128)S(1)} %pad_add_fusion.here_ref, bf16[256,768]{1,0:T(8,128)(2,1)S(1)} %broadcast_select_fusion.2.refs_0_, bf16[256,768]{1,0:T(8,128)(2,1)S(1)} %collective-permute-done.11.refs_1_, ...), custom_call_target="tpu_custom_call" | custom-call | flops 134217728 | bytes 4194304 | tf_op jit(solution)/shard_map/pallas_call | solution.py:403
  104.3 1.2 %shard_map.80 = (bf16[256,256]{1,0:T(8,128)(2,1)S(1)}, bf16[256,256]{1,0:T(8,128)(2,1)S(1)}) custom-call(s32[3]{0:T(128)S(1)} %pad_add_fusion.here_ref, f32[16]{0:T(128)S(1)} %copy-done.3, bf16[128,256]{1,0:T(8,128)(2,1)S(1)} %collective-permute-done.25.base_ref, f32[128,256]{1,0:T(8,128)S(1)} %get-tuple-element.129.refs_0_, ...), custom_call_target="tpu_custom_call" | custom-call | flops 201326592 | bytes 4194304 | tf_op jit(solution)/shard_map/pallas_call | solution.py:414
  105.5 0.3 collective-permute-start.32
  105.8 1.7 %shard_map.81 = (bf16[256,256]{1,0:T(8,128)(2,1)S(1)}, f32[256,256]{1,0:T(8,128)S(1)}, bf16[256,256]{1,0:T(8,128)(2,1)S(1)}, f32[256,256]{1,0:T(8,128)S(1)}) custom-call(s32[3]{0:T(128)S(1)} %pad_add_fusion.here_ref, bf16[256,768]{1,0:T(8,128)(2,1)S(1)} %broadcast_select_fusion.2.refs_0_, bf16[256,768]{1,0:T(8,128)(2,1)S(1)} %collective-permute-done.11.refs_1_, ...), custom_call_target="tpu_custom_call" | custom-call | flops 134217728 | bytes 4194304 | tf_op jit(solution)/shard_map/pallas_call | solution.py:403
  107.5 1.6 %shard_map.82 = (bf16[256,256]{1,0:T(8,128)(2,1)S(1)}, bf16[256,256]{1,0:T(8,128)(2,1)S(1)}, bf16[256,256]{1,0:T(8,128)(2,1)S(1)}, bf16[256,256]{1,0:T(8,128)(2,1)S(1)}) custom-call(s32[3]{0:T(128)S(1)} %pad_add_fusion.here_ref, f32[16]{0:T(128)S(1)} %copy-done.3, bf16[128,256]{1,0:T(8,128)(2,1)S(1)} %collective-permute-done.25.base_ref, ...), custom_call_target="tpu_custom_call" | custom-call | flops 402653184 | bytes 4194304 | tf_op jit(solution)/shard_map/pallas_call | solution.py:414
  109.1 0.2 collective-permute-start.29
  109.3 0.4 collective-permute-start.30
  109.7 1.2 collective-permute-start.34
  110.9 0.1 collective-permute-done.32.refs_5_
  111.0 4.0 %collective-permute-done.34.refs_7_ = bf16[256,256]{1,0:T(8,128)(2,1)S(1)} collective-permute-done((bf16[256,256]{1,0:T(8,128)(2,1)S(1)}, bf16[256,256]{1,0:T(8,128)(2,1)S(1)}, u32[]{:S(2)}, u32[]{:S(2)}) %collective-permute-start.34) | collective-permute-done | bytes 131104 | tf_op jit(solution)/shard_map/ppermute | solution.py:274
  114.9 1.6 %shard_map.83 = bf16[256,2048]{1,0:T(8,128)(2,1)} custom-call(s32[3]{0:T(128)S(1)} %pad_add_fusion.here_ref, bf16[256,256]{1,0:T(8,128)(2,1)S(1)} %get-tuple-element.155.refs_0_, bf16[256,256]{1,0:T(8,128)(2,1)S(1)} %get-tuple-element.156.refs_1_, bf16[256,256]{1,0:T(8,128)(2,1)S(1)} %collective-permute-done.29.refs_2_, ...), custom_call_target="tpu_custom_call" | custom-call | bytes 4194304 | tf_op jit(solution)/shard_map/pallas_call | solution.py:434
  (49 shorter events, 0.3 us)
Async XLA Ops:
  0.0 18.1 %collective-permute-start.3 = (bf16[256,4096]{1,0:T(8,128)(2,1)}, bf16[256,4096]{1,0:T(8,128)(2,1)}, u32[]{:S(2)}, u32[]{:S(2)}) collective-permute-start(bf16[256,4096]{1,0:T(8,128)(2,1)} %bitcast.3.refs_0_), channel_id=1, source_target_pairs={{0,4},{1,5},{2,6},{3,7},{4,0},{5,1},{6,2},{7,3},{8,12},{9,13},{10,... | collective-permute-start | bytes 6291464 | tf_op jit(solution)/shard_map/ppermute | solution.py:274
  1.4 1.0 copy-start
  2.5 0.9 copy-start.1
  3.4 0.9 copy-start.2
  4.3 0.7 copy-start.4
  5.6 2.0 %collective-permute-start = (bf16[144,768]{1,0:T(8,128)(2,1)S(1)}, bf16[144,768]{1,0:T(8,128)(2,1)S(1)}, u32[]{:S(2)}, u32[]{:S(2)}) collective-permute-start(bf16[144,768]{1,0:T(8,128)(2,1)S(1)} %get-tuple-element.83), channel_id=1, source_target_pairs={{0,4},{1,5},{2,6},{3,7},{4,0},{5,1},{6,2},{7,3},{8,12},{9,13},{10,... | collective-permute-start | bytes 663560 | tf_op jit(solution)/shard_map/ppermute | solution.py:274
  5.7 7.8 %collective-permute-start.2 = (bf16[144,768]{1,0:T(8,128)(2,1)S(1)}, bf16[144,768]{1,0:T(8,128)(2,1)S(1)}, u32[]{:S(2)}, u32[]{:S(2)}) collective-permute-start(bf16[144,768]{1,0:T(8,128)(2,1)S(1)} %get-tuple-element.85), channel_id=1, source_target_pairs={{0,12},{1,13},{2,14},{3,15},{4,8},{5,9},{6,10},{7,11},{8,4},{9,5},... | collective-permute-start | bytes 663560 | tf_op jit(solution)/shard_map/ppermute | solution.py:274
  7.3 10.7 %collective-permute-start.1 = (bf16[144,768]{1,0:T(8,128)(2,1)S(1)}, bf16[144,768]{1,0:T(8,128)(2,1)S(1)}, u32[]{:S(2)}, u32[]{:S(2)}) collective-permute-start(bf16[144,768]{1,0:T(8,128)(2,1)S(1)} %get-tuple-element.84), channel_id=1, source_target_pairs={{0,8},{1,9},{2,10},{3,11},{4,12},{5,13},{6,14},{7,15},{8,0},{9,1},... | collective-permute-start | bytes 663560 | tf_op jit(solution)/shard_map/ppermute | solution.py:274
  18.1 49.5 %collective-permute-start.21 = (bf16[256,4096]{1,0:T(8,128)(2,1)}, bf16[256,4096]{1,0:T(8,128)(2,1)}, u32[]{:S(2)}, u32[]{:S(2)}) collective-permute-start(bf16[256,4096]{1,0:T(8,128)(2,1)} %bitcast.3.refs_0_), channel_id=1, source_target_pairs={{0,8},{1,9},{2,10},{3,11},{4,12},{5,13},{6,14},{7,15},{8,0},{9,1},... | collective-permute-start | bytes 6291464 | tf_op jit(solution)/shard_map/ppermute | solution.py:274
  19.3 9.8 %collective-permute-start.4 = (bf16[256,768]{1,0:T(8,128)(2,1)S(1)}, bf16[256,768]{1,0:T(8,128)(2,1)S(1)}, u32[]{:S(2)}, u32[]{:S(2)}) collective-permute-start(bf16[256,768]{1,0:T(8,128)(2,1)S(1)} %pad_maximum_fusion.refs_2_), channel_id=1, source_target_pairs={{0,1},{1,0},{2,3},{3,2},{4,5},{5,4},{6,7},{7,6},{8,9},{9,8},{10,11... | collective-permute-start | bytes 1179656 | tf_op jit(solution)/shard_map/ppermute | solution.py:274
  19.5 12.8 %collective-permute-start.5 = (bf16[256,768]{1,0:T(8,128)(2,1)S(1)}, bf16[256,768]{1,0:T(8,128)(2,1)S(1)}, u32[]{:S(2)}, u32[]{:S(2)}) collective-permute-start(bf16[256,768]{1,0:T(8,128)(2,1)S(1)} %pad_maximum_fusion.refs_2_), channel_id=1, source_target_pairs={{1,2},{2,1},{5,6},{6,5},{9,10},{10,9},{13,14},{14,13},{17,18},{18,... | collective-permute-start | bytes 1179656 | tf_op jit(solution)/shard_map/ppermute | solution.py:274
  23.8 9.8 %collective-permute-start.6 = (bf16[256,768]{1,0:T(8,128)(2,1)S(1)}, bf16[256,768]{1,0:T(8,128)(2,1)S(1)}, u32[]{:S(2)}, u32[]{:S(2)}) collective-permute-start(bf16[256,768]{1,0:T(8,128)(2,1)S(1)} %pad_maximum_fusion.refs_2_), channel_id=1, source_target_pairs={{0,16},{1,17},{2,18},{3,19},{4,20},{5,21},{6,22},{7,23},{8,24},{9,... | collective-permute-start | bytes 1179656 | tf_op jit(solution)/shard_map/ppermute | solution.py:274
  25.1 12.4 %collective-permute-start.13 = (bf16[256,768]{1,0:T(8,128)(2,1)S(1)}, bf16[256,768]{1,0:T(8,128)(2,1)S(1)}, u32[]{:S(2)}, u32[]{:S(2)}) collective-permute-start(bf16[256,768]{1,0:T(8,128)(2,1)S(1)} %pad_maximum_fusion.1.refs_7_), channel_id=1, source_target_pairs={{0,1},{1,0},{2,3},{3,2},{4,5},{5,4},{6,7},{7,6},{8,9},{9,8},{10,11... | collective-permute-start | bytes 1179656 | tf_op jit(solution)/shard_map/ppermute | solution.py:274
  29.1 10.5 %collective-permute-start.14 = (bf16[256,768]{1,0:T(8,128)(2,1)S(1)}, bf16[256,768]{1,0:T(8,128)(2,1)}, u32[]{:S(2)}, u32[]{:S(2)}) collective-permute-start(bf16[256,768]{1,0:T(8,128)(2,1)S(1)} %pad_maximum_fusion.1.refs_7_), channel_id=1, source_target_pairs={{1,2},{2,1},{5,6},{6,5},{9,10},{10,9},{13,14},{14,13},{17,18},{18,... | collective-permute-start | bytes 1179656 | tf_op jit(solution)/shard_map/ppermute | solution.py:274
  32.3 16.7 %copy-start.7 = (bf16[256,768]{1,0:T(8,128)(2,1)}, bf16[256,768]{1,0:T(8,128)(2,1)S(1)}, u32[]{:S(2)}) copy-start(bf16[256,768]{1,0:T(8,128)(2,1)S(1)} %collective-permute-done.5) | copy-start | bytes 1179652
  32.4 8.6 %collective-permute-start.15 = (bf16[256,768]{1,0:T(8,128)(2,1)S(1)}, bf16[256,768]{1,0:T(8,128)(2,1)S(1)}, u32[]{:S(2)}, u32[]{:S(2)}) collective-permute-start(bf16[256,768]{1,0:T(8,128)(2,1)S(1)} %pad_maximum_fusion.1.refs_7_), channel_id=1, source_target_pairs={{0,16},{1,17},{2,18},{3,19},{4,20},{5,21},{6,22},{7,23},{8,24},{9,... | collective-permute-start | bytes 1179656 | tf_op jit(solution)/shard_map/ppermute | solution.py:274
  33.7 13.3 %collective-permute-start.7 = (bf16[256,768]{1,0:T(8,128)(2,1)S(1)}, bf16[256,768]{1,0:T(8,128)(2,1)S(1)}, u32[]{:S(2)}, u32[]{:S(2)}) collective-permute-start(bf16[256,768]{1,0:T(8,128)(2,1)S(1)} %collective-permute-done.4.refs_3_), channel_id=1, source_target_pairs={{1,2},{2,1},{5,6},{6,5},{9,10},{10,9},{13,14},{14,13},{17,18},{18,... | collective-permute-start | bytes 1179656 | tf_op jit(solution)/shard_map/ppermute | solution.py:274
  37.6 11.5 %collective-permute-start.8 = (bf16[256,768]{1,0:T(8,128)(2,1)S(1)}, bf16[256,768]{1,0:T(8,128)(2,1)S(1)}, u32[]{:S(2)}, u32[]{:S(2)}) collective-permute-start(bf16[256,768]{1,0:T(8,128)(2,1)S(1)} %collective-permute-done.5), channel_id=1, source_target_pairs={{1,0},{2,3},{5,4},{6,7},{9,8},{10,11},{13,12},{14,15},{17,16},{18,... | collective-permute-start | bytes 1179656 | tf_op jit(solution)/shard_map/ppermute | solution.py:274
  39.7 11.4 %collective-permute-start.9 = (bf16[256,768]{1,0:T(8,128)(2,1)S(1)}, bf16[256,768]{1,0:T(8,128)(2,1)}, u32[]{:S(2)}, u32[]{:S(2)}) collective-permute-start(bf16[256,768]{1,0:T(8,128)(2,1)S(1)} %collective-permute-done.4.refs_3_), channel_id=1, source_target_pairs={{0,16},{1,17},{2,18},{3,19},{4,20},{5,21},{6,22},{7,23},{8,24},{9,... | collective-permute-start | bytes 1179656 | tf_op jit(solution)/shard_map/ppermute | solution.py:274
  41.0 14.4 %collective-permute-start.16 = (bf16[256,768]{1,0:T(8,128)(2,1)S(1)}, bf16[256,768]{1,0:T(8,128)(2,1)}, u32[]{:S(2)}, u32[]{:S(2)}) collective-permute-start(bf16[256,768]{1,0:T(8,128)(2,1)S(1)} %collective-permute-done.13.refs_8_), channel_id=1, source_target_pairs={{1,2},{2,1},{5,6},{6,5},{9,10},{10,9},{13,14},{14,13},{17,18},{18,... | collective-permute-start | bytes 1179656 | tf_op jit(solution)/shard_map/ppermute | solution.py:274
  47.0 2.0 %copy-start.5 = (bf16[256,768]{1,0:T(8,128)(2,1)}, bf16[256,768]{1,0:T(8,128)(2,1)S(1)}, u32[]{:S(2)}) copy-start(bf16[256,768]{1,0:T(8,128)(2,1)S(1)} %collective-permute-done.7) | copy-start | bytes 1179652
  47.0 9.7 %collective-permute-start.17 = (bf16[256,768]{1,0:T(8,128)(2,1)}, bf16[256,768]{1,0:T(8,128)(2,1)}, u32[]{:S(2)}, u32[]{:S(2)}) collective-permute-start(bf16[256,768]{1,0:T(8,128)(2,1)} %collective-permute-done.14), channel_id=1, source_target_pairs={{1,0},{2,3},{5,4},{6,7},{9,8},{10,11},{13,12},{14,15},{17,16},{18,... | collective-permute-start | bytes 1179656 | tf_op jit(solution)/shard_map/ppermute | solution.py:274
  49.0 0.8 copy-start.8
  49.8 10.1 %collective-permute-start.18 = (bf16[256,768]{1,0:T(8,128)(2,1)S(1)}, bf16[256,768]{1,0:T(8,128)(2,1)}, u32[]{:S(2)}, u32[]{:S(2)}) collective-permute-start(bf16[256,768]{1,0:T(8,128)(2,1)S(1)} %collective-permute-done.13.refs_8_), channel_id=1, source_target_pairs={{0,16},{1,17},{2,18},{3,19},{4,20},{5,21},{6,22},{7,23},{8,24},{9,... | collective-permute-start | bytes 1179656 | tf_op jit(solution)/shard_map/ppermute | solution.py:274
  51.0 11.2 %collective-permute-start.10 = (bf16[256,768]{1,0:T(8,128)(2,1)}, bf16[256,768]{1,0:T(8,128)(2,1)S(1)}, u32[]{:S(2)}, u32[]{:S(2)}) collective-permute-start(bf16[256,768]{1,0:T(8,128)(2,1)} %copy-done.5), channel_id=1, source_target_pairs={{1,0},{2,3},{5,4},{6,7},{9,8},{10,11},{13,12},{14,15},{17,16},{18,... | collective-permute-start | bytes 1179656 | tf_op jit(solution)/shard_map/ppermute | solution.py:274
  55.4 12.2 %collective-permute-start.11 = (bf16[256,768]{1,0:T(8,128)(2,1)S(1)}, bf16[256,768]{1,0:T(8,128)(2,1)S(1)}, u32[]{:S(2)}, u32[]{:S(2)}) collective-permute-start(bf16[256,768]{1,0:T(8,128)(2,1)S(1)} %broadcast_select_fusion.3.refs_4_), channel_id=1, source_target_pairs={{0,16},{1,17},{2,18},{3,19},{4,20},{5,21},{6,22},{7,23},{8,24},{9,... | collective-permute-start | bytes 1179656 | tf_op jit(solution)/shard_map/ppermute | solution.py:274
  56.6 10.9 %collective-permute-start.12 = (bf16[256,768]{1,0:T(8,128)(2,1)}, bf16[256,768]{1,0:T(8,128)(2,1)S(1)}, u32[]{:S(2)}, u32[]{:S(2)}) collective-permute-start(bf16[256,768]{1,0:T(8,128)(2,1)} %collective-permute-done.9.refs_6_), channel_id=1, source_target_pairs={{1,2},{2,1},{5,6},{6,5},{9,10},{10,9},{13,14},{14,13},{17,18},{18,... | collective-permute-start | bytes 1179656 | tf_op jit(solution)/shard_map/ppermute | solution.py:274
  59.8 10.3 %collective-permute-start.19 = (bf16[256,768]{1,0:T(8,128)(2,1)}, bf16[256,768]{1,0:T(8,128)(2,1)S(1)}, u32[]{:S(2)}, u32[]{:S(2)}) collective-permute-start(bf16[256,768]{1,0:T(8,128)(2,1)} %collective-permute-done.16), channel_id=1, source_target_pairs={{1,0},{2,3},{5,4},{6,7},{9,8},{10,11},{13,12},{14,15},{17,16},{18,... | collective-permute-start | bytes 1179656 | tf_op jit(solution)/shard_map/ppermute | solution.py:274
  62.2 21.2 %copy-start.6 = (bf16[256,768]{1,0:T(8,128)(2,1)S(1)}, bf16[256,768]{1,0:T(8,128)(2,1)}, u32[]{:S(2)}) copy-start(bf16[256,768]{1,0:T(8,128)(2,1)} %copy-done.5) | copy-start | bytes 1179652
  62.2 11.3 %collective-permute-start.20 = (bf16[256,768]{1,0:T(8,128)(2,1)S(1)}, bf16[256,768]{1,0:T(8,128)(2,1)S(1)}, u32[]{:S(2)}, u32[]{:S(2)}) collective-permute-start(bf16[256,768]{1,0:T(8,128)(2,1)S(1)} %broadcast_select_fusion.1.refs_9_), channel_id=1, source_target_pairs={{0,16},{1,17},{2,18},{3,19},{4,20},{5,21},{6,22},{7,23},{8,24},{9,... | collective-permute-start | bytes 1179656 | tf_op jit(solution)/shard_map/ppermute | solution.py:274
  73.5 12.7 %collective-permute-start.24 = (bf16[256,4096]{1,0:T(8,128)(2,1)}, bf16[256,4096]{1,0:T(8,128)(2,1)S(1)}, u32[]{:S(2)}, u32[]{:S(2)}) collective-permute-start(bf16[256,4096]{1,0:T(8,128)(2,1)} %collective-permute-done.21.refs_0_), channel_id=1, source_target_pairs={{0,4},{1,5},{2,6},{3,7},{4,0},{5,1},{6,2},{7,3},{8,12},{9,13},{10,... | collective-permute-start | bytes 6291464 | tf_op jit(solution)/shard_map/ppermute | solution.py:274
  79.6 11.0 %collective-permute-start.22 = (bf16[256,256]{1,0:T(8,128)(2,1)S(1)}, bf16[256,256]{1,0:T(8,128)(2,1)S(1)}, u32[]{:S(2)}, u32[]{:S(2)}) collective-permute-start(bf16[256,256]{1,0:T(8,128)(2,1)S(1)} %slice.31), channel_id=1, source_target_pairs={{1,0},{2,3},{5,4},{6,7},{9,8},{10,11},{13,12},{14,15},{17,16},{18,... | collective-permute-start | bytes 393224 | tf_op jit(solution)/shard_map/ppermute | solution.py:274
  82.1 13.9 %collective-permute-start.26 = (bf16[256,512]{1,0:T(8,128)(2,1)S(1)}, bf16[256,512]{1,0:T(8,128)(2,1)S(1)}, u32[]{:S(2)}, u32[]{:S(2)}) collective-permute-start(bf16[256,512]{1,0:T(8,128)(2,1)S(1)} %slice.33), channel_id=1, source_target_pairs={{1,0},{2,3},{5,4},{6,7},{9,8},{10,11},{13,12},{14,15},{17,16},{18,... | collective-permute-start | bytes 786440 | tf_op jit(solution)/shard_map/ppermute | solution.py:274
  84.5 6.1 %collective-permute-start.23 = (bf16[256,256]{1,0:T(8,128)(2,1)S(1)}, bf16[256,256]{1,0:T(8,128)(2,1)S(1)}, u32[]{:S(2)}, u32[]{:S(2)}) collective-permute-start(bf16[256,256]{1,0:T(8,128)(2,1)S(1)} %get-tuple-element.161), channel_id=1, source_target_pairs={{0,16},{1,17},{2,18},{3,19},{4,20},{5,21},{6,22},{7,23},{8,24},{9,... | collective-permute-start | bytes 393224 | tf_op jit(solution)/shard_map/ppermute | solution.py:274
  86.1 9.8 %collective-permute-start.27 = (bf16[256,256]{1,0:T(8,128)(2,1)S(1)}, bf16[256,256]{1,0:T(8,128)(2,1)S(1)}, u32[]{:S(2)}, u32[]{:S(2)}) collective-permute-start(bf16[256,256]{1,0:T(8,128)(2,1)S(1)} %get-tuple-element.160), channel_id=1, source_target_pairs={{0,16},{1,17},{2,18},{3,19},{4,20},{5,21},{6,22},{7,23},{8,24},{9,... | collective-permute-start | bytes 393224 | tf_op jit(solution)/shard_map/ppermute | solution.py:274
  92.5 5.8 %collective-permute-start.25 = (bf16[128,256]{1,0:T(8,128)(2,1)S(1)}, bf16[128,256]{1,0:T(8,128)(2,1)S(1)}, u32[]{:S(2)}, u32[]{:S(2)}) collective-permute-start(bf16[128,256]{1,0:T(8,128)(2,1)S(1)} %get-tuple-element.121), channel_id=1, source_target_pairs={{0,16},{1,17},{2,18},{3,19},{4,20},{5,21},{6,22},{7,23},{8,24},{9,... | collective-permute-start | bytes 196616 | tf_op jit(solution)/shard_map/ppermute | solution.py:274
  95.8 6.5 %collective-permute-start.28 = (bf16[256,256]{1,0:T(8,128)(2,1)S(1)}, bf16[256,256]{1,0:T(8,128)(2,1)S(1)}, u32[]{:S(2)}, u32[]{:S(2)}) collective-permute-start(bf16[256,256]{1,0:T(8,128)(2,1)S(1)} %get-tuple-element.133), channel_id=1, source_target_pairs={{0,16},{1,17},{2,18},{3,19},{4,20},{5,21},{6,22},{7,23},{8,24},{9,... | collective-permute-start | bytes 393224 | tf_op jit(solution)/shard_map/ppermute | solution.py:274
  95.9 2.4 %copy-start.3 = (f32[16]{0:T(128)S(1)}, f32[16]{0:T(128)}, u32[]{:S(2)}) copy-start(f32[16]{0:T(128)} %gate_ref.5) | copy-start | bytes 196
  99.6 10.1 %collective-permute-start.31 = (bf16[256,256]{1,0:T(8,128)(2,1)S(1)}, bf16[256,256]{1,0:T(8,128)(2,1)S(1)}, u32[]{:S(2)}, u32[]{:S(2)}) collective-permute-start(bf16[256,256]{1,0:T(8,128)(2,1)S(1)} %get-tuple-element.136), channel_id=1, source_target_pairs={{0,8},{1,9},{2,10},{3,11},{4,12},{5,13},{6,14},{7,15},{8,0},{9,1},... | collective-permute-start | bytes 393224 | tf_op jit(solution)/shard_map/ppermute | solution.py:274
  99.9 11.0 %collective-permute-start.33 = (bf16[256,256]{1,0:T(8,128)(2,1)S(1)}, bf16[256,256]{1,0:T(8,128)(2,1)S(1)}, u32[]{:S(2)}, u32[]{:S(2)}) collective-permute-start(bf16[256,256]{1,0:T(8,128)(2,1)S(1)} %get-tuple-element.137), channel_id=1, source_target_pairs={{0,12},{1,13},{2,14},{3,15},{4,8},{5,9},{6,10},{7,11},{8,4},{9,5},... | collective-permute-start | bytes 393224 | tf_op jit(solution)/shard_map/ppermute | solution.py:274
  105.5 5.5 %collective-permute-start.32 = (bf16[256,256]{1,0:T(8,128)(2,1)S(1)}, bf16[256,256]{1,0:T(8,128)(2,1)S(1)}, u32[]{:S(2)}, u32[]{:S(2)}) collective-permute-start(bf16[256,256]{1,0:T(8,128)(2,1)S(1)} %get-tuple-element.143), channel_id=1, source_target_pairs={{0,8},{1,9},{2,10},{3,11},{4,12},{5,13},{6,14},{7,15},{8,0},{9,1},... | collective-permute-start | bytes 393224 | tf_op jit(solution)/shard_map/ppermute | solution.py:274
  109.1 1.7 %collective-permute-start.29 = (bf16[256,256]{1,0:T(8,128)(2,1)S(1)}, bf16[256,256]{1,0:T(8,128)(2,1)S(1)}, u32[]{:S(2)}, u32[]{:S(2)}) collective-permute-start(bf16[256,256]{1,0:T(8,128)(2,1)S(1)} %get-tuple-element.157), channel_id=1, source_target_pairs={{0,4},{1,5},{2,6},{3,7},{4,0},{5,1},{6,2},{7,3},{8,12},{9,13},{10,... | collective-permute-start | bytes 393224 | tf_op jit(solution)/shard_map/ppermute | solution.py:274
  109.3 1.6 %collective-permute-start.30 = (bf16[256,256]{1,0:T(8,128)(2,1)S(1)}, bf16[256,256]{1,0:T(8,128)(2,1)S(1)}, u32[]{:S(2)}, u32[]{:S(2)}) collective-permute-start(bf16[256,256]{1,0:T(8,128)(2,1)S(1)} %get-tuple-element.158), channel_id=1, source_target_pairs={{0,4},{1,5},{2,6},{3,7},{4,0},{5,1},{6,2},{7,3},{8,12},{9,13},{10,... | collective-permute-start | bytes 393224 | tf_op jit(solution)/shard_map/ppermute | solution.py:274
  109.7 5.3 %collective-permute-start.34 = (bf16[256,256]{1,0:T(8,128)(2,1)S(1)}, bf16[256,256]{1,0:T(8,128)(2,1)S(1)}, u32[]{:S(2)}, u32[]{:S(2)}) collective-permute-start(bf16[256,256]{1,0:T(8,128)(2,1)S(1)} %get-tuple-element.144), channel_id=1, source_target_pairs={{0,12},{1,13},{2,14},{3,15},{4,8},{5,9},{6,10},{7,11},{8,4},{9,5},... | collective-permute-start | bytes 393224 | tf_op jit(solution)/shard_map/ppermute | solution.py:274

commit v11 on v10

--- a/solution.py
+++ b/solution.py
@@ -209,7 +209,7 @@
     work = [(at, p, h) for at in range(len(segs)) for p in range(len(parts)) for h in range(heads)]
     memories = []
     for seg in segs:
-        memory = base_ref[...].astype(jnp.float32)
+        memory = jnp.where(here_ref[3] > 0, 1.0, 0.0) * base_ref[...].astype(jnp.float32)
         for other in range(MEMBERS):
             if other != seg:
                 earlier = jnp.where((me ^ other) < (me ^ seg), 1.0, 0.0)
@@ -234,13 +234,26 @@
         outs[at * len(parts) + p][:, columns(h)] = jnp.where(live, mixed, 0.0).astype(jnp.bfloat16)
 
 
-def assemble_body(counts, here_ref, *refs):
-    parts, out = list(refs[:-1]), refs[-1]
-    width = out.shape[1] // MEMBERS
-    for k, count in enumerate(counts):
-        for c in range(count):
-            at = (here_ref[1] ^ k) * width + c * (width // count)
-            out[:, pl.ds(aligned(at), width // count)] = parts.pop(0)[...]
+def assemble_body(places, here_ref, *refs):
+    out = refs[-1]
+    for (k, c), part in zip(places, refs):
+        width = part.shape[1]
+        at = (here_ref[1] ^ k) * 2 * width + c * width
+        out[:, pl.ds(aligned(at), width)] = part[...]
+
+
+def finish_body(places, here_ref, *refs):
+    out, sems = refs[-2:]
+    copies = []
+    for n, ((k, c), part) in enumerate(zip(places, refs)):
+        width = part.shape[1]
+        at = (here_ref[1] ^ k) * 2 * width + c * width
+        copies.append(
+            pltpu.make_async_copy(part, out.at[:, pl.ds(aligned(at), width)], sems.at[n])
+        )
+        copies[-1].start()
+    for one in copies:
+        one.wait()
 
 
 def after(array, *others):
@@ -258,7 +271,7 @@
     seg = lax.axis_index("seg")
     z = lax.axis_index("fsdp")
     g, m = seg // MEMBERS, seg % MEMBERS
-    here = jnp.stack([g, m, z]).astype(jnp.int32)
+    here = jnp.stack([g, m, z, g if n_groups == 2 else 1]).astype(jnp.int32)
     bf16, f32 = jnp.bfloat16, jnp.float32
     shape = jax.ShapeDtypeStruct
 
@@ -277,11 +290,12 @@
         return permute(array, lambda gg, mm, zz: (gg, mm ^ k, zz))
 
     wide = (2 + group) * HEAD_SIZE
+    sibling = to_member(tokens[0], 1)
     packed = call(
         functools.partial(pack_body, group),
         [shape((rows + META_ROWS, wide), bf16)] * MEMBERS,
         [SMEM] * 3 + [VMEM] * 3,
-    )(here, valid_len, block_mask, w_query, w_key, value_weight)
+    )(after(here, sibling), valid_len, block_mask, w_query, w_key, value_weight)
     messages = [packed[0], *[to_member(packed[k], k) for k in (1, 2, 3)]]
 
     def gathered(piece):
@@ -334,9 +348,11 @@
         stage2 = lambda one, inner: (inward(one), outward(inner), over(one))
         stage3 = lambda middle, two: (outward(middle), over(two))
 
-        a, b, own, sibling = locked(*pieces, tokens[0], to_member(tokens[0], 1))
+        a = pieces[0]
+        a_one, a_inner, a_far0 = locked(*stage1(a))
+        own = after(tokens[0], messages[2], messages[3])
         across = to_member(own, 2)
-        a_one, a_inner, a_far0 = locked(*stage1(a))
+        b = after(pieces[1], a_one)
         b_one, b_inner, b_far0 = locked(*stage1(b))
         a_middle, a_outer, a_far1 = locked(*stage2(a_one, a_inner))
         b_middle, b_outer, b_far1 = locked(*stage2(b_one, b_inner))
@@ -363,7 +379,7 @@
         inner = a_inner
         finish = lambda at, *others: over(after(b_three[:, at], *others))
     else:
-        across, sibling = to_member(tokens[0], 2), to_member(tokens[0], 1)
+        across = to_member(tokens[0], 2)
         books = [tokens[0], sibling, across, to_member(across, 1)]
         full = gathered(jnp.concatenate(pieces, axis=0))
         deep = MEMBERS * HEAD_SIZE // 2
@@ -393,8 +409,10 @@
 
     base = None
     for a in range(1, n_groups):
-        term = permute(total, lambda gg, mm, zz: (gg ^ a, mm, zz) if gg < gg ^ a else None)
-        base = term if base is None else base.astype(f32) + term.astype(f32)
+        term = permute(total, lambda gg, mm, zz: (gg ^ a, mm, zz))
+        if n_groups > 2:
+            term = jnp.where((g ^ a) < g, term, 0).astype(f32)
+        base = term if base is None else base + term
 
     lower_q1 = finish(halves[2], total)
     half = group // 2
@@ -421,21 +439,33 @@
             *[ready[key][0] for key in keys], *[ready[key][1] for key in keys],
         )
 
-    ready = local((2, 3, 1, 0), 0, lower_q0)
+    ready = local((2, 3), 0, lower_q0)
     base = after(base, *ready[2, 0])
     two0, three0 = mix((2, 3), (0,), base, ready)
     ready |= local((2, 3), 1, after(lower_q1, two0, three0))
     two1, three1 = mix((2, 3), (1,), base, ready)
+    ready |= local((1, 0), 0, after(lower_q0, two1, three1))
     ready |= local((1, 0), 1, after(lower_q1, two1, three1))
     one0, one1, mine0, mine1 = mix((1, 0), (0, 1), after(base, two1, three1), ready)
-    sent = [mine0, mine1]
-    for k, parts in ((1, (one0, one1)), (2, (two0, two1)), (3, (three0, three1))):
-        sent += [to_member(part, k) for part in parts]
+    parts = {(0, 0): mine0, (0, 1): mine1}
+    for k, mixed in ((1, (one0, one1)), (2, (two0, two1)), (3, (three0, three1))):
+        for c in range(2):
+            parts[k, c] = to_member(mixed[c], k)
+    last = [(1, 0), (1, 1)]
+    first = [key for key in parts if key not in last]
+    out_shape = shape((length, w_query.shape[1]), bf16)
     (output,) = call(
-        functools.partial(assemble_body, (2,) * MEMBERS),
-        [shape((length, w_query.shape[1]), bf16)],
-        [SMEM] + [VMEM] * len(sent),
-    )(here, *sent)
+        functools.partial(assemble_body, first), [out_shape], [SMEM] + [VMEM] * len(first)
+    )(here, *[parts[key] for key in first])
+    output = pl.pallas_call(
+        functools.partial(finish_body, last),
+        out_shape=out_shape,
+        in_specs=[SMEM] + [VMEM] * len(last) + [ANY],
+        out_specs=ANY,
+        scratch_shapes=[pltpu.SemaphoreType.DMA((len(last),))],
+        input_output_aliases={1 + len(last): 0},
+        cost_estimate=pl.CostEstimate(flops=0, bytes_accessed=1 << 20, transcendentals=0),
+    )(here, *[parts[key] for key in last], output)
     return output[None]
 
 

time: 119 us -> 118 us (level); the launches traced: 117 us -> 118 us
  starting transfers between devices: 55.2 us -> 50 us
  local copies, waits for them, and re-layouts: 4.41 us -> 7.65 us
  Pallas kernels: 23.5 us -> 25.6 us
    ppermute x35, starting transfers between devices: 55.2 us -> 50 us  [permute(): return lax.ppermute(array, AXES, pairs)]
    unnamed x18 -> x28, local copies, waits for them, and re-layouts: 4.3 us -> 7.54 us
    pallas_call x1 -> x2, Pallas kernels: 1.64 us -> 3.31 us  [the longest x1 1.7 us: shards(): pl.pallas_call(functools.partial(finish_body, last), out_shape=out_shape,...]
    pallas_call x3 -> x4, Pallas kernels: 6.02 us -> 7.04 us  [local(): call(functools.partial(local_body, len(segs), len(late) + 1, halves[1 + p...]
  transfers between devices with their start and end apart: 35 -> 35, of which waited for: 10 -> 13; matrix products, arithmetic and copies ran while one was open for 3% -> 3% of each run, Pallas kernels for 19% -> 20%
where the time goes in v11:
time: 118 us
  starting transfers between devices  50 us (42%)
  waiting for transfers between devices  30 us (25%)
  Pallas kernels  25.6 us (22%)
  local copies, waits for them, and re-layouts  7.65 us (6%)
  other arithmetic  3.35 us (3%)
    ppermute x35, starting transfers between devices, permute(): return lax.ppermute(array, AXES, pairs)  50 us
    ppermute x35, waiting for transfers between devices, permute(): return lax.ppermute(array, AXES, pairs)  30 us
    pallas_call x2, Pallas kernels, project(): call(functools.partial(project_body, early, late, line), [shape((length,...  8.72 us
    unnamed x28, local copies, waits for them, and re-layouts  7.54 us
    pallas_call x4, Pallas kernels, local(): call(functools.partial(local_body, len(segs), len(late) + 1, halves[1 + p...  7.04 us
    pallas_call x3, Pallas kernels, mix(): call(functools.partial(mix_body, segs, parts, group), [shape((length, hal...  3.96 us
  transfers between devices with their start and end apart: 35, of which 13 were waited for; matrix products, arithmetic and copies ran while one was open for 3% of the time, Pallas kernels for 20%

profile of v11, /device:TPU:9, one launch (start us, length us, event | category | flops | bytes accessed | tf_op | source)
XLA Modules:
  0.0 117.7 jit_solution(12238871425377629207)
XLA Ops:
  0.0 0.7 collective-permute-start
  1.4 3.3 %collective-permute-done.refs_1_ = bf16[256,4096]{1,0:T(8,128)(2,1)S(1)} collective-permute-done((bf16[256,4096]{1,0:T(8,128)(2,1)}, bf16[256,4096]{1,0:T(8,128)(2,1)S(1)}, u32[]{:S(2)}, u32[]{:S(2)}) %collective-permute-start) | collective-permute-done | bytes 2097184 | tf_op jit(solution)/shard_map/ppermute | solution.py:287
  4.7 1.4 %copy-done = bf16[256,4096]{1,0:T(8,128)(2,1)} copy-done((bf16[256,4096]{1,0:T(8,128)(2,1)}, bf16[256,4096]{1,0:T(8,128)(2,1)S(1)}, u32[]{:S(2)}) %copy-start) | copy-done | bytes 2097176
  6.0 1.0 copy-done.2
  7.1 0.9 copy-done.3
  8.0 0.9 copy-done.4
  8.9 0.7 copy-done.7
  9.6 0.6 shard_map.73
  10.2 0.4 collective-permute-start.1
  10.7 1.3 %collective-permute-start.12 = (bf16[144,768]{1,0:T(8,128)(2,1)S(1)}, bf16[144,768]{1,0:T(8,128)(2,1)S(1)}, u32[]{:S(2)}, u32[]{:S(2)}) collective-permute-start(bf16[144,768]{1,0:T(8,128)(2,1)S(1)} %get-tuple-element.94), channel_id=1, source_target_pairs={{0,12},{1,13},{2,14},{3,15},{4,8},{5,9},{6,10},{7,11},{8,4},{9,5},... | collective-permute-start | bytes 663560 | tf_op jit(solution)/shard_map/ppermute | solution.py:287
  12.4 4.5 %collective-permute-start.3 = (bf16[256,768]{1,0:T(8,128)(2,1)S(1)}, bf16[256,768]{1,0:T(8,128)(2,1)S(1)}, u32[]{:S(2)}, u32[]{:S(2)}) collective-permute-start(bf16[256,768]{1,0:T(8,128)(2,1)S(1)} %pad_maximum_fusion.refs_2_), channel_id=1, source_target_pairs={{1,2},{2,1},{5,6},{6,5},{9,10},{10,9},{13,14},{14,13},{17,18},{18,... | collective-permute-start | bytes 1179656 | tf_op jit(solution)/shard_map/ppermute | solution.py:287
  16.9 1.3 %collective-permute-start.4 = (bf16[256,768]{1,0:T(8,128)(2,1)S(1)}, bf16[256,768]{1,0:T(8,128)(2,1)S(1)}, u32[]{:S(2)}, u32[]{:S(2)}) collective-permute-start(bf16[256,768]{1,0:T(8,128)(2,1)S(1)} %pad_maximum_fusion.refs_2_), channel_id=1, source_target_pairs={{0,16},{1,17},{2,18},{3,19},{4,20},{5,21},{6,22},{7,23},{8,24},{9,... | collective-permute-start | bytes 1179656 | tf_op jit(solution)/shard_map/ppermute | solution.py:287
  18.2 0.5 collective-permute-done.12.refs_18_.refs_10_.refs_5_
  18.7 3.8 %collective-permute-done.11.refs_17_.refs_9_.refs_4_ = bf16[144,768]{1,0:T(8,128)(2,1)S(1)} collective-permute-done((bf16[144,768]{1,0:T(8,128)(2,1)S(1)}, bf16[144,768]{1,0:T(8,128)(2,1)S(1)}, u32[]{:S(2)}, u32[]{:S(2)}) %collective-permute-start.11) | collective-permute-done | bytes 221216 | tf_op jit(solution)/shard_map/ppermute | solution.py:287
  22.5 1.2 %collective-permute-start.21 = (bf16[256,4096]{1,0:T(8,128)(2,1)}, bf16[256,4096]{1,0:T(8,128)(2,1)}, u32[]{:S(2)}, u32[]{:S(2)}) collective-permute-start(bf16[256,4096]{1,0:T(8,128)(2,1)} %bitcast.3.refs_0_), channel_id=1, source_target_pairs={{0,8},{1,9},{2,10},{3,11},{4,12},{5,13},{6,14},{7,15},{8,0},{9,1},... | collective-permute-start | bytes 6291464 | tf_op jit(solution)/shard_map/ppermute | solution.py:287
  23.8 1.6 %collective-permute-done.3 = bf16[256,768]{1,0:T(8,128)(2,1)S(1)} collective-permute-done((bf16[256,768]{1,0:T(8,128)(2,1)S(1)}, bf16[256,768]{1,0:T(8,128)(2,1)S(1)}, u32[]{:S(2)}, u32[]{:S(2)}) %collective-permute-start.3) | collective-permute-done | bytes 393248 | tf_op jit(solution)/shard_map/ppermute | solution.py:287
  25.4 0.9 collective-permute-done.4.refs_5_
  26.3 2.2 %collective-permute-start.14 = (bf16[256,768]{1,0:T(8,128)(2,1)S(1)}, bf16[256,768]{1,0:T(8,128)(2,1)}, u32[]{:S(2)}, u32[]{:S(2)}) collective-permute-start(bf16[256,768]{1,0:T(8,128)(2,1)S(1)} %pad_maximum_fusion.1.refs_7_), channel_id=1, source_target_pairs={{1,2},{2,1},{5,6},{6,5},{9,10},{10,9},{13,14},{14,13},{17,18},{18,... | collective-permute-start | bytes 1179656 | tf_op jit(solution)/shard_map/ppermute | solution.py:287
  28.6 1.3 %collective-permute-start.15 = (bf16[256,768]{1,0:T(8,128)(2,1)S(1)}, bf16[256,768]{1,0:T(8,128)(2,1)S(1)}, u32[]{:S(2)}, u32[]{:S(2)}) collective-permute-start(bf16[256,768]{1,0:T(8,128)(2,1)S(1)} %pad_maximum_fusion.1.refs_7_), channel_id=1, source_target_pairs={{0,16},{1,17},{2,18},{3,19},{4,20},{5,21},{6,22},{7,23},{8,24},{9,... | collective-permute-start | bytes 1179656 | tf_op jit(solution)/shard_map/ppermute | solution.py:287
  29.9 3.1 %collective-permute-start.5 = (bf16[256,768]{1,0:T(8,128)(2,1)S(1)}, bf16[256,768]{1,0:T(8,128)(2,1)S(1)}, u32[]{:S(2)}, u32[]{:S(2)}) collective-permute-start(bf16[256,768]{1,0:T(8,128)(2,1)S(1)} %collective-permute-done.2.refs_3_), channel_id=1, source_target_pairs={{1,2},{2,1},{5,6},{6,5},{9,10},{10,9},{13,14},{14,13},{17,18},{18,... | collective-permute-start | bytes 1179656 | tf_op jit(solution)/shard_map/ppermute | solution.py:287
  32.9 2.0 %collective-permute-done.13.refs_8_ = bf16[256,768]{1,0:T(8,128)(2,1)S(1)} collective-permute-done((bf16[256,768]{1,0:T(8,128)(2,1)S(1)}, bf16[256,768]{1,0:T(8,128)(2,1)S(1)}, u32[]{:S(2)}, u32[]{:S(2)}) %collective-permute-start.13) | collective-permute-done | bytes 393248 | tf_op jit(solution)/shard_map/ppermute | solution.py:287
  34.9 2.2 %collective-permute-start.6 = (bf16[256,768]{1,0:T(8,128)(2,1)S(1)}, bf16[256,768]{1,0:T(8,128)(2,1)S(1)}, u32[]{:S(2)}, u32[]{:S(2)}) collective-permute-start(bf16[256,768]{1,0:T(8,128)(2,1)S(1)} %collective-permute-done.3), channel_id=1, source_target_pairs={{1,0},{2,3},{5,4},{6,7},{9,8},{10,11},{13,12},{14,15},{17,16},{18,... | collective-permute-start | bytes 1179656 | tf_op jit(solution)/shard_map/ppermute | solution.py:287
  37.1 1.3 %collective-permute-start.7 = (bf16[256,768]{1,0:T(8,128)(2,1)S(1)}, bf16[256,768]{1,0:T(8,128)(2,1)}, u32[]{:S(2)}, u32[]{:S(2)}) collective-permute-start(bf16[256,768]{1,0:T(8,128)(2,1)S(1)} %collective-permute-done.2.refs_3_), channel_id=1, source_target_pairs={{0,16},{1,17},{2,18},{3,19},{4,20},{5,21},{6,22},{7,23},{8,24},{9,... | collective-permute-start | bytes 1179656 | tf_op jit(solution)/shard_map/ppermute | solution.py:287
  38.5 2.5 %collective-permute-start.16 = (bf16[256,768]{1,0:T(8,128)(2,1)S(1)}, bf16[256,768]{1,0:T(8,128)(2,1)}, u32[]{:S(2)}, u32[]{:S(2)}) collective-permute-start(bf16[256,768]{1,0:T(8,128)(2,1)S(1)} %collective-permute-done.13.refs_8_), channel_id=1, source_target_pairs={{1,2},{2,1},{5,6},{6,5},{9,10},{10,9},{13,14},{14,13},{17,18},{18,... | collective-permute-start | bytes 1179656 | tf_op jit(solution)/shard_map/ppermute | solution.py:287
  41.0 4.3 %collective-permute-done.5 = bf16[256,768]{1,0:T(8,128)(2,1)S(1)} collective-permute-done((bf16[256,768]{1,0:T(8,128)(2,1)S(1)}, bf16[256,768]{1,0:T(8,128)(2,1)S(1)}, u32[]{:S(2)}, u32[]{:S(2)}) %collective-permute-start.5) | collective-permute-done | bytes 393248 | tf_op jit(solution)/shard_map/ppermute | solution.py:287
  45.2 2.0 %collective-permute-start.17 = (bf16[256,768]{1,0:T(8,128)(2,1)}, bf16[256,768]{1,0:T(8,128)(2,1)}, u32[]{:S(2)}, u32[]{:S(2)}) collective-permute-start(bf16[256,768]{1,0:T(8,128)(2,1)} %collective-permute-done.14), channel_id=1, source_target_pairs={{1,0},{2,3},{5,4},{6,7},{9,8},{10,11},{13,12},{14,15},{17,16},{18,... | collective-permute-start | bytes 1179656 | tf_op jit(solution)/shard_map/ppermute | solution.py:287
  47.3 0.7 copy-done.11
  48.0 1.2 %collective-permute-start.18 = (bf16[256,768]{1,0:T(8,128)(2,1)S(1)}, bf16[256,768]{1,0:T(8,128)(2,1)}, u32[]{:S(2)}, u32[]{:S(2)}) collective-permute-start(bf16[256,768]{1,0:T(8,128)(2,1)S(1)} %collective-permute-done.13.refs_8_), channel_id=1, source_target_pairs={{0,16},{1,17},{2,18},{3,19},{4,20},{5,21},{6,22},{7,23},{8,24},{9,... | collective-permute-start | bytes 1179656 | tf_op jit(solution)/shard_map/ppermute | solution.py:287
  49.3 1.4 %collective-permute-start.8 = (bf16[256,768]{1,0:T(8,128)(2,1)}, bf16[256,768]{1,0:T(8,128)(2,1)S(1)}, u32[]{:S(2)}, u32[]{:S(2)}) collective-permute-start(bf16[256,768]{1,0:T(8,128)(2,1)} %copy-done.8), channel_id=1, source_target_pairs={{1,0},{2,3},{5,4},{6,7},{9,8},{10,11},{13,12},{14,15},{17,16},{18,... | collective-permute-start | bytes 1179656 | tf_op jit(solution)/shard_map/ppermute | solution.py:287
  50.7 1.1 broadcast_select_fusion.3.refs_4_
  51.8 1.9 %collective-permute-done.16 = bf16[256,768]{1,0:T(8,128)(2,1)} collective-permute-done((bf16[256,768]{1,0:T(8,128)(2,1)S(1)}, bf16[256,768]{1,0:T(8,128)(2,1)}, u32[]{:S(2)}, u32[]{:S(2)}) %collective-permute-start.16) | collective-permute-done | bytes 393248 | tf_op jit(solution)/shard_map/ppermute | solution.py:287
  53.7 1.2 %collective-permute-start.9 = (bf16[256,768]{1,0:T(8,128)(2,1)S(1)}, bf16[256,768]{1,0:T(8,128)(2,1)S(1)}, u32[]{:S(2)}, u32[]{:S(2)}) collective-permute-start(bf16[256,768]{1,0:T(8,128)(2,1)S(1)} %broadcast_select_fusion.3.refs_4_), channel_id=1, source_target_pairs={{0,16},{1,17},{2,18},{3,19},{4,20},{5,21},{6,22},{7,23},{8,24},{9,... | collective-permute-start | bytes 1179656 | tf_op jit(solution)/shard_map/ppermute | solution.py:287
  54.9 2.5 %collective-permute-start.10 = (bf16[256,768]{1,0:T(8,128)(2,1)}, bf16[256,768]{1,0:T(8,128)(2,1)S(1)}, u32[]{:S(2)}, u32[]{:S(2)}) collective-permute-start(bf16[256,768]{1,0:T(8,128)(2,1)} %collective-permute-done.7.refs_6_), channel_id=1, source_target_pairs={{1,2},{2,1},{5,6},{6,5},{9,10},{10,9},{13,14},{14,13},{17,18},{18,... | collective-permute-start | bytes 1179656 | tf_op jit(solution)/shard_map/ppermute | solution.py:287
  57.4 1.3 %collective-permute-start.19 = (bf16[256,768]{1,0:T(8,128)(2,1)}, bf16[256,768]{1,0:T(8,128)(2,1)S(1)}, u32[]{:S(2)}, u32[]{:S(2)}) collective-permute-start(bf16[256,768]{1,0:T(8,128)(2,1)} %collective-permute-done.16), channel_id=1, source_target_pairs={{1,0},{2,3},{5,4},{6,7},{9,8},{10,11},{13,12},{14,15},{17,16},{18,... | collective-permute-start | bytes 1179656 | tf_op jit(solution)/shard_map/ppermute | solution.py:287
  58.8 1.1 broadcast_select_fusion.1.refs_9_
  60.1 4.5 %collective-permute-done.9.refs_1_ = bf16[256,768]{1,0:T(8,128)(2,1)S(1)} collective-permute-done((bf16[256,768]{1,0:T(8,128)(2,1)S(1)}, bf16[256,768]{1,0:T(8,128)(2,1)S(1)}, u32[]{:S(2)}, u32[]{:S(2)}) %collective-permute-start.9) | collective-permute-done | bytes 393248 | tf_op jit(solution)/shard_map/ppermute | solution.py:287
  64.6 4.4 %shard_map.74 = (f32[256,768]{1,0:T(8,128)S(1)}, f32[256,768]{1,0:T(8,128)S(1)}, bf16[256,1536]{1,0:T(8,128)(2,1)S(1)}, bf16[256,1536]{1,0:T(8,128)(2,1)S(1)}) custom-call(s32[4]{0:T(128)S(1)} %pad_add_fusion.here_ref, bf16[256,4096]{1,0:T(8,128)(2,1)} %bitcast.3.refs_0_, bf16[256,4096]{1,0:T(8,128)(2,1)S(1)} %copy-done.1, ...), custom_call_target="tpu_custom_call" | custom-call | flops 2013265920 | bytes 4194304 | tf_op jit(solution)/shard_map/pallas_call | solution.py:325
  69.1 3.8 %collective-permute-done.20.refs_3_ = bf16[256,768]{1,0:T(8,128)(2,1)S(1)} collective-permute-done((bf16[256,768]{1,0:T(8,128)(2,1)S(1)}, bf16[256,768]{1,0:T(8,128)(2,1)S(1)}, u32[]{:S(2)}, u32[]{:S(2)}) %collective-permute-start.20) | collective-permute-done | bytes 393248 | tf_op jit(solution)/shard_map/ppermute | solution.py:287
  72.9 5.2 %collective-permute-start.24 = (bf16[256,4096]{1,0:T(8,128)(2,1)}, bf16[256,4096]{1,0:T(8,128)(2,1)S(1)}, u32[]{:S(2)}, u32[]{:S(2)}) collective-permute-start(bf16[256,4096]{1,0:T(8,128)(2,1)} %collective-permute-done.21.refs_0_), channel_id=1, source_target_pairs={{0,4},{1,5},{2,6},{3,7},{4,0},{5,1},{6,2},{7,3},{8,12},{9,13},{10,... | collective-permute-start | bytes 6291464 | tf_op jit(solution)/shard_map/ppermute | solution.py:287
  78.1 2.5 %collective-permute-start.22 = (bf16[256,256]{1,0:T(8,128)(2,1)S(1)}, bf16[256,256]{1,0:T(8,128)(2,1)S(1)}, u32[]{:S(2)}, u32[]{:S(2)}) collective-permute-start(bf16[256,256]{1,0:T(8,128)(2,1)S(1)} %slice.31), channel_id=1, source_target_pairs={{1,0},{2,3},{5,4},{6,7},{9,8},{10,11},{13,12},{14,15},{17,16},{18,... | collective-permute-start | bytes 393224 | tf_op jit(solution)/shard_map/ppermute | solution.py:287
  80.6 1.3 %collective-permute-start.26 = (bf16[256,512]{1,0:T(8,128)(2,1)S(1)}, bf16[256,512]{1,0:T(8,128)(2,1)S(1)}, u32[]{:S(2)}, u32[]{:S(2)}) collective-permute-start(bf16[256,512]{1,0:T(8,128)(2,1)S(1)} %slice.33), channel_id=1, source_target_pairs={{1,0},{2,3},{5,4},{6,7},{9,8},{10,11},{13,12},{14,15},{17,16},{18,... | collective-permute-start | bytes 786440 | tf_op jit(solution)/shard_map/ppermute | solution.py:287
  82.0 1.1 broadcast_select_fusion.refs_2_
  83.1 1.3 %collective-permute-start.23 = (bf16[256,256]{1,0:T(8,128)(2,1)S(1)}, bf16[256,256]{1,0:T(8,128)(2,1)S(1)}, u32[]{:S(2)}, u32[]{:S(2)}) collective-permute-start(bf16[256,256]{1,0:T(8,128)(2,1)S(1)} %get-tuple-element.161), channel_id=1, source_target_pairs={{0,16},{1,17},{2,18},{3,19},{4,20},{5,21},{6,22},{7,23},{8,24},{9,... | collective-permute-start | bytes 393224 | tf_op jit(solution)/shard_map/ppermute | solution.py:287
  84.6 4.4 %shard_map.75 = (f32[256,768]{1,0:T(8,128)S(1)}, f32[256,768]{1,0:T(8,128)S(1)}, bf16[256,1536]{1,0:T(8,128)(2,1)S(1)}, bf16[256,1536]{1,0:T(8,128)(2,1)S(1)}) custom-call(s32[4]{0:T(128)S(1)} %pad_add_fusion.here_ref, bf16[256,4096]{1,0:T(8,128)(2,1)} %collective-permute-done.21.refs_0_, bf16[256,4096]{1,0:T(8,128)(2,1)S(1)} %collective-permute-done.24.refs_1_, ...), custom_call_target="tpu_custom_call" | custom-call | flops 2013265920 | bytes 4194304 | tf_op jit(solution)/shard_map/pallas_call | solution.py:325
  89.0 1.9 %shard_map.76 = (bf16[256,256]{1,0:T(8,128)(2,1)S(1)}, f32[128,256]{1,0:T(8,128)S(1)}, bf16[256,256]{1,0:T(8,128)(2,1)S(1)}, f32[128,256]{1,0:T(8,128)S(1)}, bf1...) custom-call(s32[4]{0:T(128)S(1)} %pad_add_fusion.here_ref, ...), custom_call_target="tpu_custom_call" | custom-call | flops 805306368 | bytes 4194304 | tf_op jit(solution)/shard_map/pallas_call | solution.py:400
  90.9 1.3 %collective-permute-start.28 = (bf16[256,256]{1,0:T(8,128)(2,1)S(1)}, bf16[256,256]{1,0:T(8,128)(2,1)S(1)}, u32[]{:S(2)}, u32[]{:S(2)}) collective-permute-start(bf16[256,256]{1,0:T(8,128)(2,1)S(1)} %get-tuple-element.130), channel_id=1, source_target_pairs={{0,16},{1,17},{2,18},{3,19},{4,20},{5,21},{6,22},{7,23},{8,24},{9,... | collective-permute-start | bytes 393224 | tf_op jit(solution)/shard_map/ppermute | solution.py:287
  92.5 1.7 %shard_map.77 = (bf16[256,256]{1,0:T(8,128)(2,1)S(1)}, f32[256,256]{1,0:T(8,128)S(1)}, bf16[256,256]{1,0:T(8,128)(2,1)S(1)}, f32[256,256]{1,0:T(8,128)S(1)}) custom-call(s32[4]{0:T(128)S(1)} %pad_add_fusion.here_ref, bf16[256,768]{1,0:T(8,128)(2,1)S(1)} %broadcast_select_fusion.2.refs_0_, bf16[256,768]{1,0:T(8,128)(2,1)S(1)} %collective-permute-done.9.refs_1_, ...), custom_call_target="tpu_custom_call" | custom-call | flops 134217728 | bytes 4194304 | tf_op jit(solution)/shard_map/pallas_call | solution.py:421
  94.2 2.4 %collective-permute-done.25.base_ref = bf16[128,256]{1,0:T(8,128)(2,1)S(1)} collective-permute-done((bf16[128,256]{1,0:T(8,128)(2,1)S(1)}, bf16[128,256]{1,0:T(8,128)(2,1)S(1)}, u32[]{:S(2)}, u32[]{:S(2)}) %collective-permute-start.25) | collective-permute-done | bytes 65568 | tf_op jit(solution)/shard_map/ppermute | solution.py:287
  96.6 1.2 shard_map.78
  97.7 1.3 %collective-permute-start.31 = (bf16[256,256]{1,0:T(8,128)(2,1)S(1)}, bf16[256,256]{1,0:T(8,128)(2,1)S(1)}, u32[]{:S(2)}, u32[]{:S(2)}) collective-permute-start(bf16[256,256]{1,0:T(8,128)(2,1)S(1)} %get-tuple-element.133), channel_id=1, source_target_pairs={{0,8},{1,9},{2,10},{3,11},{4,12},{5,13},{6,14},{7,15},{8,0},{9,1},... | collective-permute-start | bytes 393224 | tf_op jit(solution)/shard_map/ppermute | solution.py:287
  99.0 2.2 %collective-permute-start.33 = (bf16[256,256]{1,0:T(8,128)(2,1)S(1)}, bf16[256,256]{1,0:T(8,128)(2,1)S(1)}, u32[]{:S(2)}, u32[]{:S(2)}) collective-permute-start(bf16[256,256]{1,0:T(8,128)(2,1)S(1)} %get-tuple-element.134), channel_id=1, source_target_pairs={{0,12},{1,13},{2,14},{3,15},{4,8},{5,9},{6,10},{7,11},{8,4},{9,5},... | collective-permute-start | bytes 393224 | tf_op jit(solution)/shard_map/ppermute | solution.py:287
  101.2 1.7 %shard_map.79 = (bf16[256,256]{1,0:T(8,128)(2,1)S(1)}, f32[256,256]{1,0:T(8,128)S(1)}, bf16[256,256]{1,0:T(8,128)(2,1)S(1)}, f32[256,256]{1,0:T(8,128)S(1)}) custom-call(s32[4]{0:T(128)S(1)} %pad_add_fusion.here_ref, bf16[256,768]{1,0:T(8,128)(2,1)S(1)} %broadcast_select_fusion.2.refs_0_, bf16[256,768]{1,0:T(8,128)(2,1)S(1)} %collective-permute-done.9.refs_1_, ...), custom_call_target="tpu_custom_call" | custom-call | flops 134217728 | bytes 4194304 | tf_op jit(solution)/shard_map/pallas_call | solution.py:421
  102.9 1.2 %shard_map.80 = (bf16[256,256]{1,0:T(8,128)(2,1)S(1)}, bf16[256,256]{1,0:T(8,128)(2,1)S(1)}) custom-call(s32[4]{0:T(128)S(1)} %pad_add_fusion.here_ref, f32[16]{0:T(128)S(1)} %copy-done.6, bf16[128,256]{1,0:T(8,128)(2,1)S(1)} %collective-permute-done.25.base_ref, f32[128,256]{1,0:T(8,128)S(1)} %get-tuple-element.126.refs_0_, ...), custom_call_target="tpu_custom_call" | custom-call | flops 201326592 | bytes 4194304 | tf_op jit(solution)/shard_map/pallas_call | solution.py:432
  104.1 1.3 %collective-permute-start.32 = (bf16[256,256]{1,0:T(8,128)(2,1)S(1)}, bf16[256,256]{1,0:T(8,128)(2,1)S(1)}, u32[]{:S(2)}, u32[]{:S(2)}) collective-permute-start(bf16[256,256]{1,0:T(8,128)(2,1)S(1)} %get-tuple-element.140), channel_id=1, source_target_pairs={{0,8},{1,9},{2,10},{3,11},{4,12},{5,13},{6,14},{7,15},{8,0},{9,1},... | collective-permute-start | bytes 393224 | tf_op jit(solution)/shard_map/ppermute | solution.py:287
  105.7 1.9 %shard_map.81 = (bf16[256,256]{1,0:T(8,128)(2,1)S(1)}, f32[256,256]{1,0:T(8,128)S(1)}, bf16[256,256]{1,0:T(8,128)(2,1)S(1)}, f32[256,256]{1,0:T(8,128)S(1)}) custom-call(s32[4]{0:T(128)S(1)} %pad_add_fusion.here_ref, bf16[256,768]{1,0:T(8,128)(2,1)S(1)} %broadcast_select_fusion.2.refs_0_, bf16[256,768]{1,0:T(8,128)(2,1)S(1)} %collective-permute-done.9.refs_1_, ...), custom_call_target="tpu_custom_call" | custom-call | flops 134217728 | bytes 4194304 | tf_op jit(solution)/shard_map/pallas_call | solution.py:421
  107.6 1.7 %shard_map.82 = (bf16[256,256]{1,0:T(8,128)(2,1)S(1)}, f32[256,256]{1,0:T(8,128)S(1)}, bf16[256,256]{1,0:T(8,128)(2,1)S(1)}, f32[256,256]{1,0:T(8,128)S(1)}) custom-call(s32[4]{0:T(128)S(1)} %pad_add_fusion.here_ref, bf16[256,768]{1,0:T(8,128)(2,1)S(1)} %broadcast_select_fusion.2.refs_0_, bf16[256,768]{1,0:T(8,128)(2,1)S(1)} %collective-permute-done.9.refs_1_, ...), custom_call_target="tpu_custom_call" | custom-call | flops 134217728 | bytes 4194304 | tf_op jit(solution)/shard_map/pallas_call | solution.py:421
  109.3 1.6 %shard_map.83 = (bf16[256,256]{1,0:T(8,128)(2,1)S(1)}, bf16[256,256]{1,0:T(8,128)(2,1)S(1)}, bf16[256,256]{1,0:T(8,128)(2,1)S(1)}, bf16[256,256]{1,0:T(8,128)(2,1)S(1)}) custom-call(s32[4]{0:T(128)S(1)} %pad_add_fusion.here_ref, f32[16]{0:T(128)S(1)} %copy-done.6, bf16[128,256]{1,0:T(8,128)(2,1)S(1)} %collective-permute-done.25.base_ref, ...), custom_call_target="tpu_custom_call" | custom-call | flops 402653184 | bytes 4194304 | tf_op jit(solution)/shard_map/pallas_call | solution.py:432
  110.9 0.4 collective-permute-start.29
  111.5 0.8 collective-permute-done.34.refs_5_
  112.3 1.6 %shard_map.84.refs_2_ = bf16[256,2048]{1,0:T(8,128)(2,1)} custom-call(s32[4]{0:T(128)S(1)} %pad_add_fusion.here_ref, bf16[256,256]{1,0:T(8,128)(2,1)S(1)} %get-tuple-element.157.refs_0_, bf16[256,256]{1,0:T(8,128)(2,1)S(1)} %get-tuple-element.158.refs_1_, bf16[256,256]{1,0:T(8,128)(2,1)S(1)} %collective-permute-done.31.refs_2_, ...), custom_call_target="tpu_custom_call" | custom-call | bytes 4194304 | tf_op jit(solution)/shard_map/pallas_call | solution.py:457
  113.9 0.6 copy-done.5
  114.5 0.7 copy-done.12
  115.2 0.6 copy-done.13
  115.8 1.7 %shard_map.85 = bf16[256,2048]{1,0:T(8,128)(2,1)} custom-call(s32[4]{0:T(128)} %copy-done.5, bf16[256,256]{1,0:T(8,128)(2,1)} %copy-done.12, bf16[256,256]{1,0:T(8,128)(2,1)} %copy-done.13, bf16[256,2048]{1,0:T(8,128)(2,1)} %shard_map.84.refs_2_), custom_call_target="tpu_custom_call", output_to_operand_aliasing={{}: (3, {})} | custom-call | bytes 1048576 | tf_op jit(solution)/shard_map/pallas_call | solution.py:460
  (61 shorter events, 2.0 us)
Async XLA Ops:
  0.0 4.7 %collective-permute-start = (bf16[256,4096]{1,0:T(8,128)(2,1)}, bf16[256,4096]{1,0:T(8,128)(2,1)S(1)}, u32[]{:S(2)}, u32[]{:S(2)}) collective-permute-start(bf16[256,4096]{1,0:T(8,128)(2,1)} %bitcast.3.refs_0_), channel_id=1, source_target_pairs={{0,4},{1,5},{2,6},{3,7},{4,0},{5,1},{6,2},{7,3},{8,12},{9,13},{10,... | collective-permute-start | bytes 6291464 | tf_op jit(solution)/shard_map/ppermute | solution.py:287
  4.7 1.4 %copy-start = (bf16[256,4096]{1,0:T(8,128)(2,1)}, bf16[256,4096]{1,0:T(8,128)(2,1)S(1)}, u32[]{:S(2)}) copy-start(bf16[256,4096]{1,0:T(8,128)(2,1)S(1)} %collective-permute-done.refs_1_) | copy-start | bytes 6291460
  6.0 1.0 copy-start.2
  7.1 0.9 copy-start.3
  8.0 0.9 copy-start.4
  8.9 0.7 copy-start.7
  10.2 2.0 %collective-permute-start.1 = (bf16[144,768]{1,0:T(8,128)(2,1)S(1)}, bf16[144,768]{1,0:T(8,128)(2,1)S(1)}, u32[]{:S(2)}, u32[]{:S(2)}) collective-permute-start(bf16[144,768]{1,0:T(8,128)(2,1)S(1)} %get-tuple-element.84), channel_id=1, source_target_pairs={{0,4},{1,5},{2,6},{3,7},{4,0},{5,1},{6,2},{7,3},{8,12},{9,13},{10,... | collective-permute-start | bytes 663560 | tf_op jit(solution)/shard_map/ppermute | solution.py:287
  10.7 8.0 %collective-permute-start.12 = (bf16[144,768]{1,0:T(8,128)(2,1)S(1)}, bf16[144,768]{1,0:T(8,128)(2,1)S(1)}, u32[]{:S(2)}, u32[]{:S(2)}) collective-permute-start(bf16[144,768]{1,0:T(8,128)(2,1)S(1)} %get-tuple-element.94), channel_id=1, source_target_pairs={{0,12},{1,13},{2,14},{3,15},{4,8},{5,9},{6,10},{7,11},{8,4},{9,5},... | collective-permute-start | bytes 663560 | tf_op jit(solution)/shard_map/ppermute | solution.py:287
  12.0 10.5 %collective-permute-start.11 = (bf16[144,768]{1,0:T(8,128)(2,1)S(1)}, bf16[144,768]{1,0:T(8,128)(2,1)S(1)}, u32[]{:S(2)}, u32[]{:S(2)}) collective-permute-start(bf16[144,768]{1,0:T(8,128)(2,1)S(1)} %get-tuple-element.93), channel_id=1, source_target_pairs={{0,8},{1,9},{2,10},{3,11},{4,12},{5,13},{6,14},{7,15},{8,0},{9,1},... | collective-permute-start | bytes 663560 | tf_op jit(solution)/shard_map/ppermute | solution.py:287
  12.3 11.5 %collective-permute-start.2 = (bf16[256,768]{1,0:T(8,128)(2,1)S(1)}, bf16[256,768]{1,0:T(8,128)(2,1)S(1)}, u32[]{:S(2)}, u32[]{:S(2)}) collective-permute-start(bf16[256,768]{1,0:T(8,128)(2,1)S(1)} %pad_maximum_fusion.refs_2_), channel_id=1, source_target_pairs={{0,1},{1,0},{2,3},{3,2},{4,5},{5,4},{6,7},{7,6},{8,9},{9,8},{10,11... | collective-permute-start | bytes 1179656 | tf_op jit(solution)/shard_map/ppermute | solution.py:287
  12.4 13.0 %collective-permute-start.3 = (bf16[256,768]{1,0:T(8,128)(2,1)S(1)}, bf16[256,768]{1,0:T(8,128)(2,1)S(1)}, u32[]{:S(2)}, u32[]{:S(2)}) collective-permute-start(bf16[256,768]{1,0:T(8,128)(2,1)S(1)} %pad_maximum_fusion.refs_2_), channel_id=1, source_target_pairs={{1,2},{2,1},{5,6},{6,5},{9,10},{10,9},{13,14},{14,13},{17,18},{18,... | collective-permute-start | bytes 1179656 | tf_op jit(solution)/shard_map/ppermute | solution.py:287
  16.9 9.5 %collective-permute-start.4 = (bf16[256,768]{1,0:T(8,128)(2,1)S(1)}, bf16[256,768]{1,0:T(8,128)(2,1)S(1)}, u32[]{:S(2)}, u32[]{:S(2)}) collective-permute-start(bf16[256,768]{1,0:T(8,128)(2,1)S(1)} %pad_maximum_fusion.refs_2_), channel_id=1, source_target_pairs={{0,16},{1,17},{2,18},{3,19},{4,20},{5,21},{6,22},{7,23},{8,24},{9,... | collective-permute-start | bytes 1179656 | tf_op jit(solution)/shard_map/ppermute | solution.py:287
  22.5 46.6 %collective-permute-start.21 = (bf16[256,4096]{1,0:T(8,128)(2,1)}, bf16[256,4096]{1,0:T(8,128)(2,1)}, u32[]{:S(2)}, u32[]{:S(2)}) collective-permute-start(bf16[256,4096]{1,0:T(8,128)(2,1)} %bitcast.3.refs_0_), channel_id=1, source_target_pairs={{0,8},{1,9},{2,10},{3,11},{4,12},{5,13},{6,14},{7,15},{8,0},{9,1},... | collective-permute-start | bytes 6291464 | tf_op jit(solution)/shard_map/ppermute | solution.py:287
  25.4 21.9 %copy-start.10 = (bf16[256,768]{1,0:T(8,128)(2,1)}, bf16[256,768]{1,0:T(8,128)(2,1)S(1)}, u32[]{:S(2)}) copy-start(bf16[256,768]{1,0:T(8,128)(2,1)S(1)} %collective-permute-done.3) | copy-start | bytes 1179652
  26.3 8.6 %collective-permute-start.13 = (bf16[256,768]{1,0:T(8,128)(2,1)S(1)}, bf16[256,768]{1,0:T(8,128)(2,1)S(1)}, u32[]{:S(2)}, u32[]{:S(2)}) collective-permute-start(bf16[256,768]{1,0:T(8,128)(2,1)S(1)} %pad_maximum_fusion.1.refs_7_), channel_id=1, source_target_pairs={{0,1},{1,0},{2,3},{3,2},{4,5},{5,4},{6,7},{7,6},{8,9},{9,8},{10,11... | collective-permute-start | bytes 1179656 | tf_op jit(solution)/shard_map/ppermute | solution.py:287
  26.3 10.8 %collective-permute-start.14 = (bf16[256,768]{1,0:T(8,128)(2,1)S(1)}, bf16[256,768]{1,0:T(8,128)(2,1)}, u32[]{:S(2)}, u32[]{:S(2)}) collective-permute-start(bf16[256,768]{1,0:T(8,128)(2,1)S(1)} %pad_maximum_fusion.1.refs_7_), channel_id=1, source_target_pairs={{1,2},{2,1},{5,6},{6,5},{9,10},{10,9},{13,14},{14,13},{17,18},{18,... | collective-permute-start | bytes 1179656 | tf_op jit(solution)/shard_map/ppermute | solution.py:287
  28.6 9.9 %collective-permute-start.15 = (bf16[256,768]{1,0:T(8,128)(2,1)S(1)}, bf16[256,768]{1,0:T(8,128)(2,1)S(1)}, u32[]{:S(2)}, u32[]{:S(2)}) collective-permute-start(bf16[256,768]{1,0:T(8,128)(2,1)S(1)} %pad_maximum_fusion.1.refs_7_), channel_id=1, source_target_pairs={{0,16},{1,17},{2,18},{3,19},{4,20},{5,21},{6,22},{7,23},{8,24},{9,... | collective-permute-start | bytes 1179656 | tf_op jit(solution)/shard_map/ppermute | solution.py:287
  29.9 15.4 %collective-permute-start.5 = (bf16[256,768]{1,0:T(8,128)(2,1)S(1)}, bf16[256,768]{1,0:T(8,128)(2,1)S(1)}, u32[]{:S(2)}, u32[]{:S(2)}) collective-permute-start(bf16[256,768]{1,0:T(8,128)(2,1)S(1)} %collective-permute-done.2.refs_3_), channel_id=1, source_target_pairs={{1,2},{2,1},{5,6},{6,5},{9,10},{10,9},{13,14},{14,13},{17,18},{18,... | collective-permute-start | bytes 1179656 | tf_op jit(solution)/shard_map/ppermute | solution.py:287
  34.9 12.4 %collective-permute-start.6 = (bf16[256,768]{1,0:T(8,128)(2,1)S(1)}, bf16[256,768]{1,0:T(8,128)(2,1)S(1)}, u32[]{:S(2)}, u32[]{:S(2)}) collective-permute-start(bf16[256,768]{1,0:T(8,128)(2,1)S(1)} %collective-permute-done.3), channel_id=1, source_target_pairs={{1,0},{2,3},{5,4},{6,7},{9,8},{10,11},{13,12},{14,15},{17,16},{18,... | collective-permute-start | bytes 1179656 | tf_op jit(solution)/shard_map/ppermute | solution.py:287
  37.1 12.1 %collective-permute-start.7 = (bf16[256,768]{1,0:T(8,128)(2,1)S(1)}, bf16[256,768]{1,0:T(8,128)(2,1)}, u32[]{:S(2)}, u32[]{:S(2)}) collective-permute-start(bf16[256,768]{1,0:T(8,128)(2,1)S(1)} %collective-permute-done.2.refs_3_), channel_id=1, source_target_pairs={{0,16},{1,17},{2,18},{3,19},{4,20},{5,21},{6,22},{7,23},{8,24},{9,... | collective-permute-start | bytes 1179656 | tf_op jit(solution)/shard_map/ppermute | solution.py:287
  38.5 15.2 %collective-permute-start.16 = (bf16[256,768]{1,0:T(8,128)(2,1)S(1)}, bf16[256,768]{1,0:T(8,128)(2,1)}, u32[]{:S(2)}, u32[]{:S(2)}) collective-permute-start(bf16[256,768]{1,0:T(8,128)(2,1)S(1)} %collective-permute-done.13.refs_8_), channel_id=1, source_target_pairs={{1,2},{2,1},{5,6},{6,5},{9,10},{10,9},{13,14},{14,13},{17,18},{18,... | collective-permute-start | bytes 1179656 | tf_op jit(solution)/shard_map/ppermute | solution.py:287
  45.2 2.0 %copy-start.8 = (bf16[256,768]{1,0:T(8,128)(2,1)}, bf16[256,768]{1,0:T(8,128)(2,1)S(1)}, u32[]{:S(2)}) copy-start(bf16[256,768]{1,0:T(8,128)(2,1)S(1)} %collective-permute-done.5) | copy-start | bytes 1179652
  45.2 9.7 %collective-permute-start.17 = (bf16[256,768]{1,0:T(8,128)(2,1)}, bf16[256,768]{1,0:T(8,128)(2,1)}, u32[]{:S(2)}, u32[]{:S(2)}) collective-permute-start(bf16[256,768]{1,0:T(8,128)(2,1)} %collective-permute-done.14), channel_id=1, source_target_pairs={{1,0},{2,3},{5,4},{6,7},{9,8},{10,11},{13,12},{14,15},{17,16},{18,... | collective-permute-start | bytes 1179656 | tf_op jit(solution)/shard_map/ppermute | solution.py:287
  47.3 0.7 copy-start.11
  48.0 9.4 %collective-permute-start.18 = (bf16[256,768]{1,0:T(8,128)(2,1)S(1)}, bf16[256,768]{1,0:T(8,128)(2,1)}, u32[]{:S(2)}, u32[]{:S(2)}) collective-permute-start(bf16[256,768]{1,0:T(8,128)(2,1)S(1)} %collective-permute-done.13.refs_8_), channel_id=1, source_target_pairs={{0,16},{1,17},{2,18},{3,19},{4,20},{5,21},{6,22},{7,23},{8,24},{9,... | collective-permute-start | bytes 1179656 | tf_op jit(solution)/shard_map/ppermute | solution.py:287
  49.3 15.3 %copy-start.1 = (bf16[256,4096]{1,0:T(8,128)(2,1)S(1)}, bf16[256,4096]{1,0:T(8,128)(2,1)}, u32[]{:S(2)}) copy-start(bf16[256,4096]{1,0:T(8,128)(2,1)} %copy-done) | copy-start | bytes 6291460
  49.3 10.6 %collective-permute-start.8 = (bf16[256,768]{1,0:T(8,128)(2,1)}, bf16[256,768]{1,0:T(8,128)(2,1)S(1)}, u32[]{:S(2)}, u32[]{:S(2)}) collective-permute-start(bf16[256,768]{1,0:T(8,128)(2,1)} %copy-done.8), channel_id=1, source_target_pairs={{1,0},{2,3},{5,4},{6,7},{9,8},{10,11},{13,12},{14,15},{17,16},{18,... | collective-permute-start | bytes 1179656 | tf_op jit(solution)/shard_map/ppermute | solution.py:287
  53.7 10.9 %collective-permute-start.9 = (bf16[256,768]{1,0:T(8,128)(2,1)S(1)}, bf16[256,768]{1,0:T(8,128)(2,1)S(1)}, u32[]{:S(2)}, u32[]{:S(2)}) collective-permute-start(bf16[256,768]{1,0:T(8,128)(2,1)S(1)} %broadcast_select_fusion.3.refs_4_), channel_id=1, source_target_pairs={{0,16},{1,17},{2,18},{3,19},{4,20},{5,21},{6,22},{7,23},{8,24},{9,... | collective-permute-start | bytes 1179656 | tf_op jit(solution)/shard_map/ppermute | solution.py:287
  54.9 9.7 %collective-permute-start.10 = (bf16[256,768]{1,0:T(8,128)(2,1)}, bf16[256,768]{1,0:T(8,128)(2,1)S(1)}, u32[]{:S(2)}, u32[]{:S(2)}) collective-permute-start(bf16[256,768]{1,0:T(8,128)(2,1)} %collective-permute-done.7.refs_6_), channel_id=1, source_target_pairs={{1,2},{2,1},{5,6},{6,5},{9,10},{10,9},{13,14},{14,13},{17,18},{18,... | collective-permute-start | bytes 1179656 | tf_op jit(solution)/shard_map/ppermute | solution.py:287
  57.4 11.7 %collective-permute-start.19 = (bf16[256,768]{1,0:T(8,128)(2,1)}, bf16[256,768]{1,0:T(8,128)(2,1)S(1)}, u32[]{:S(2)}, u32[]{:S(2)}) collective-permute-start(bf16[256,768]{1,0:T(8,128)(2,1)} %collective-permute-done.16), channel_id=1, source_target_pairs={{1,0},{2,3},{5,4},{6,7},{9,8},{10,11},{13,12},{14,15},{17,16},{18,... | collective-permute-start | bytes 1179656 | tf_op jit(solution)/shard_map/ppermute | solution.py:287
  59.8 22.1 %copy-start.9 = (bf16[256,768]{1,0:T(8,128)(2,1)S(1)}, bf16[256,768]{1,0:T(8,128)(2,1)}, u32[]{:S(2)}) copy-start(bf16[256,768]{1,0:T(8,128)(2,1)} %copy-done.8) | copy-start | bytes 1179652
  59.8 13.1 %collective-permute-start.20 = (bf16[256,768]{1,0:T(8,128)(2,1)S(1)}, bf16[256,768]{1,0:T(8,128)(2,1)S(1)}, u32[]{:S(2)}, u32[]{:S(2)}) collective-permute-start(bf16[256,768]{1,0:T(8,128)(2,1)S(1)} %broadcast_select_fusion.1.refs_9_), channel_id=1, source_target_pairs={{0,16},{1,17},{2,18},{3,19},{4,20},{5,21},{6,22},{7,23},{8,24},{9,... | collective-permute-start | bytes 1179656 | tf_op jit(solution)/shard_map/ppermute | solution.py:287
  72.9 11.7 %collective-permute-start.24 = (bf16[256,4096]{1,0:T(8,128)(2,1)}, bf16[256,4096]{1,0:T(8,128)(2,1)S(1)}, u32[]{:S(2)}, u32[]{:S(2)}) collective-permute-start(bf16[256,4096]{1,0:T(8,128)(2,1)} %collective-permute-done.21.refs_0_), channel_id=1, source_target_pairs={{0,4},{1,5},{2,6},{3,7},{4,0},{5,1},{6,2},{7,3},{8,12},{9,13},{10,... | collective-permute-start | bytes 6291464 | tf_op jit(solution)/shard_map/ppermute | solution.py:287
  78.1 10.9 %collective-permute-start.22 = (bf16[256,256]{1,0:T(8,128)(2,1)S(1)}, bf16[256,256]{1,0:T(8,128)(2,1)S(1)}, u32[]{:S(2)}, u32[]{:S(2)}) collective-permute-start(bf16[256,256]{1,0:T(8,128)(2,1)S(1)} %slice.31), channel_id=1, source_target_pairs={{1,0},{2,3},{5,4},{6,7},{9,8},{10,11},{13,12},{14,15},{17,16},{18,... | collective-permute-start | bytes 393224 | tf_op jit(solution)/shard_map/ppermute | solution.py:287
  80.6 11.8 %collective-permute-start.26 = (bf16[256,512]{1,0:T(8,128)(2,1)S(1)}, bf16[256,512]{1,0:T(8,128)(2,1)S(1)}, u32[]{:S(2)}, u32[]{:S(2)}) collective-permute-start(bf16[256,512]{1,0:T(8,128)(2,1)S(1)} %slice.33), channel_id=1, source_target_pairs={{1,0},{2,3},{5,4},{6,7},{9,8},{10,11},{13,12},{14,15},{17,16},{18,... | collective-permute-start | bytes 786440 | tf_op jit(solution)/shard_map/ppermute | solution.py:287
  83.1 5.9 %collective-permute-start.23 = (bf16[256,256]{1,0:T(8,128)(2,1)S(1)}, bf16[256,256]{1,0:T(8,128)(2,1)S(1)}, u32[]{:S(2)}, u32[]{:S(2)}) collective-permute-start(bf16[256,256]{1,0:T(8,128)(2,1)S(1)} %get-tuple-element.161), channel_id=1, source_target_pairs={{0,16},{1,17},{2,18},{3,19},{4,20},{5,21},{6,22},{7,23},{8,24},{9,... | collective-permute-start | bytes 393224 | tf_op jit(solution)/shard_map/ppermute | solution.py:287
  84.4 8.1 %collective-permute-start.27 = (bf16[256,256]{1,0:T(8,128)(2,1)S(1)}, bf16[256,256]{1,0:T(8,128)(2,1)S(1)}, u32[]{:S(2)}, u32[]{:S(2)}) collective-permute-start(bf16[256,256]{1,0:T(8,128)(2,1)S(1)} %get-tuple-element.160), channel_id=1, source_target_pairs={{0,16},{1,17},{2,18},{3,19},{4,20},{5,21},{6,22},{7,23},{8,24},{9,... | collective-permute-start | bytes 393224 | tf_op jit(solution)/shard_map/ppermute | solution.py:287
  90.9 10.3 %collective-permute-start.28 = (bf16[256,256]{1,0:T(8,128)(2,1)S(1)}, bf16[256,256]{1,0:T(8,128)(2,1)S(1)}, u32[]{:S(2)}, u32[]{:S(2)}) collective-permute-start(bf16[256,256]{1,0:T(8,128)(2,1)S(1)} %get-tuple-element.130), channel_id=1, source_target_pairs={{0,16},{1,17},{2,18},{3,19},{4,20},{5,21},{6,22},{7,23},{8,24},{9,... | collective-permute-start | bytes 393224 | tf_op jit(solution)/shard_map/ppermute | solution.py:287
  92.2 4.3 %collective-permute-start.25 = (bf16[128,256]{1,0:T(8,128)(2,1)S(1)}, bf16[128,256]{1,0:T(8,128)(2,1)S(1)}, u32[]{:S(2)}, u32[]{:S(2)}) collective-permute-start(bf16[128,256]{1,0:T(8,128)(2,1)S(1)} %get-tuple-element.120), channel_id=1, source_target_pairs={{0,16},{1,17},{2,18},{3,19},{4,20},{5,21},{6,22},{7,23},{8,24},{9,... | collective-permute-start | bytes 196616 | tf_op jit(solution)/shard_map/ppermute | solution.py:287
  92.5 4.1 %copy-start.6 = (f32[16]{0:T(128)S(1)}, f32[16]{0:T(128)}, u32[]{:S(2)}) copy-start(f32[16]{0:T(128)} %gate_ref.5) | copy-start | bytes 196
  97.7 13.6 %collective-permute-start.31 = (bf16[256,256]{1,0:T(8,128)(2,1)S(1)}, bf16[256,256]{1,0:T(8,128)(2,1)S(1)}, u32[]{:S(2)}, u32[]{:S(2)}) collective-permute-start(bf16[256,256]{1,0:T(8,128)(2,1)S(1)} %get-tuple-element.133), channel_id=1, source_target_pairs={{0,8},{1,9},{2,10},{3,11},{4,12},{5,13},{6,14},{7,15},{8,0},{9,1},... | collective-permute-start | bytes 393224 | tf_op jit(solution)/shard_map/ppermute | solution.py:287
  99.0 12.5 %collective-permute-start.33 = (bf16[256,256]{1,0:T(8,128)(2,1)S(1)}, bf16[256,256]{1,0:T(8,128)(2,1)S(1)}, u32[]{:S(2)}, u32[]{:S(2)}) collective-permute-start(bf16[256,256]{1,0:T(8,128)(2,1)S(1)} %get-tuple-element.134), channel_id=1, source_target_pairs={{0,12},{1,13},{2,14},{3,15},{4,8},{5,9},{6,10},{7,11},{8,4},{9,5},... | collective-permute-start | bytes 393224 | tf_op jit(solution)/shard_map/ppermute | solution.py:287
  104.1 7.4 %collective-permute-start.32 = (bf16[256,256]{1,0:T(8,128)(2,1)S(1)}, bf16[256,256]{1,0:T(8,128)(2,1)S(1)}, u32[]{:S(2)}, u32[]{:S(2)}) collective-permute-start(bf16[256,256]{1,0:T(8,128)(2,1)S(1)} %get-tuple-element.140), channel_id=1, source_target_pairs={{0,8},{1,9},{2,10},{3,11},{4,12},{5,13},{6,14},{7,15},{8,0},{9,1},... | collective-permute-start | bytes 393224 | tf_op jit(solution)/shard_map/ppermute | solution.py:287
  105.4 6.9 %collective-permute-start.34 = (bf16[256,256]{1,0:T(8,128)(2,1)S(1)}, bf16[256,256]{1,0:T(8,128)(2,1)S(1)}, u32[]{:S(2)}, u32[]{:S(2)}) collective-permute-start(bf16[256,256]{1,0:T(8,128)(2,1)S(1)} %get-tuple-element.141), channel_id=1, source_target_pairs={{0,12},{1,13},{2,14},{3,15},{4,8},{5,9},{6,10},{7,11},{8,4},{9,5},... | collective-permute-start | bytes 393224 | tf_op jit(solution)/shard_map/ppermute | solution.py:287
  110.9 3.6 %collective-permute-start.29 = (bf16[256,256]{1,0:T(8,128)(2,1)S(1)}, bf16[256,256]{1,0:T(8,128)(2,1)S(1)}, u32[]{:S(2)}, u32[]{:S(2)}) collective-permute-start(bf16[256,256]{1,0:T(8,128)(2,1)S(1)} %get-tuple-element.155), channel_id=1, source_target_pairs={{0,4},{1,5},{2,6},{3,7},{4,0},{5,1},{6,2},{7,3},{8,12},{9,13},{10,... | collective-permute-start | bytes 393224 | tf_op jit(solution)/shard_map/ppermute | solution.py:287
  111.3 3.2 %collective-permute-start.30 = (bf16[256,256]{1,0:T(8,128)(2,1)S(1)}, bf16[256,256]{1,0:T(8,128)(2,1)S(1)}, u32[]{:S(2)}, u32[]{:S(2)}) collective-permute-start(bf16[256,256]{1,0:T(8,128)(2,1)S(1)} %get-tuple-element.156), channel_id=1, source_target_pairs={{0,4},{1,5},{2,6},{3,7},{4,0},{5,1},{6,2},{7,3},{8,12},{9,13},{10,... | collective-permute-start | bytes 393224 | tf_op jit(solution)/shard_map/ppermute | solution.py:287
  113.9 0.6 copy-start.5
  114.5 0.7 copy-start.12
  115.2 0.6 copy-start.13

commit v12 on v10

--- a/solution.py
+++ b/solution.py
@@ -20,7 +20,7 @@
 HBM = pl.BlockSpec(memory_space=pltpu.HBM)
 
 
-def call(body, outs, in_specs, flops=0, scratch=(), out_spec=VMEM, limit=16 << 20):
+def call(body, outs, in_specs, flops=0, scratch=(), out_spec=VMEM, limit=16 << 20, moved=4 << 20):
     return pl.pallas_call(
         body,
         out_shape=outs,
@@ -28,7 +28,7 @@
         out_specs=[out_spec] * len(outs),
         scratch_shapes=list(scratch),
         compiler_params=pltpu.CompilerParams(vmem_limit_bytes=limit),
-        cost_estimate=pl.CostEstimate(flops=flops, bytes_accessed=4 << 20, transcendentals=0),
+        cost_estimate=pl.CostEstimate(flops=flops, bytes_accessed=moved, transcendentals=0),
     )
 
 
@@ -41,13 +41,14 @@
     row = lax.broadcasted_iota(jnp.int32, (META_ROWS, outs[0].shape[1]), 0)
     facts = jnp.where(row < HALF, valid_ref[0, 0], mask_ref[0, 0, 1, 0])
     facts = facts.astype(jnp.float32).astype(jnp.bfloat16)
-    for k in range(MEMBERS):
-        head, out = here_ref[1] ^ k, outs[k]
-        at = aligned(head * HEAD_SIZE)
-        out[:rows, :HEAD_SIZE] = wk_ref[:, pl.ds(at, HEAD_SIZE)]
-        out[:rows, HEAD_SIZE : 2 * HEAD_SIZE] = wv_ref[:, pl.ds(at, HEAD_SIZE)]
-        out[:rows, 2 * HEAD_SIZE :] = wq_ref[:, pl.ds(aligned(head * wide), wide)]
-        out[rows:, :] = facts
+    for k, out, first in ((2, outs[2], 0), (3, outs[2], rows), (0, outs[0], 0), (1, outs[1], 0)):
+        head = here_ref[1] ^ k
+        at, to = aligned(head * HEAD_SIZE), slice(first, first + rows)
+        out[to, :HEAD_SIZE] = wk_ref[:, pl.ds(at, HEAD_SIZE)]
+        out[to, HEAD_SIZE : 2 * HEAD_SIZE] = wv_ref[:, pl.ds(at, HEAD_SIZE)]
+        out[to, 2 * HEAD_SIZE :] = wq_ref[:, pl.ds(aligned(head * wide), wide)]
+    for out in outs:
+        out[out.shape[0] - META_ROWS :, :] = facts
 
 
 def columns_of(tokens_ref, here_ref, piece, half, line):
@@ -209,7 +210,7 @@
     work = [(at, p, h) for at in range(len(segs)) for p in range(len(parts)) for h in range(heads)]
     memories = []
     for seg in segs:
-        memory = base_ref[...].astype(jnp.float32)
+        memory = jnp.where(here_ref[3] > 0, 1.0, 0.0) * base_ref[...].astype(jnp.float32)
         for other in range(MEMBERS):
             if other != seg:
                 earlier = jnp.where((me ^ other) < (me ^ seg), 1.0, 0.0)
@@ -243,6 +244,18 @@
             out[:, pl.ds(aligned(at), width // count)] = parts.pop(0)[...]
 
 
+def stack_body(first, upper_ref, lower_ref, out_ref):
+    rows = out_ref.shape[0] // 2
+    out_ref[:rows] = upper_ref[:rows]
+    out_ref[rows:] = lower_ref[first : first + rows]
+
+
+def gate_body(here_ref, *refs):
+    out = refs[-1]
+    for n in range(out.shape[0]):
+        out[n] = here_ref[n]
+
+
 def after(array, *others):
     return lax.optimization_barrier((array,) + others)[0]
 
@@ -258,7 +271,7 @@
     seg = lax.axis_index("seg")
     z = lax.axis_index("fsdp")
     g, m = seg // MEMBERS, seg % MEMBERS
-    here = jnp.stack([g, m, z]).astype(jnp.int32)
+    here = jnp.stack([g, m, z, g if n_groups == 2 else 1]).astype(jnp.int32)
     bf16, f32 = jnp.bfloat16, jnp.float32
     shape = jax.ShapeDtypeStruct
 
@@ -279,10 +292,10 @@
     wide = (2 + group) * HEAD_SIZE
     packed = call(
         functools.partial(pack_body, group),
-        [shape((rows + META_ROWS, wide), bf16)] * MEMBERS,
+        [shape((n * rows + META_ROWS, wide), bf16) for n in (1, 1, 2)],
         [SMEM] * 3 + [VMEM] * 3,
     )(here, valid_len, block_mask, w_query, w_key, value_weight)
-    messages = [packed[0], *[to_member(packed[k], k) for k in (1, 2, 3)]]
+    messages = [packed[0], to_member(packed[1], 1), to_member(packed[2], 2)]
 
     def gathered(piece):
         index = lambda gg, mm, zz: (gg * MEMBERS + mm) * n_z + zz
@@ -300,9 +313,9 @@
         natural = jnp.take(natural, members, axis=2).transpose(0, 2, 1, 3, 4)
         return list(natural.reshape(-1, MEMBERS * HEAD_SIZE, columns))
 
-    pieces = [
-        jnp.concatenate([messages[k][:rows] for k in members], axis=0) for members in ((0, 1), (2, 3))
-    ]
+    stack = lambda first, *pair: call(
+        functools.partial(stack_body, first), [shape((2 * rows, wide), bf16)], [VMEM] * 2, moved=1 << 20
+    )(*pair)[0]
     n_pieces = width // (MEMBERS * HEAD_SIZE)
     sums, lates = [None] * MEMBERS, [None] * MEMBERS
 
@@ -334,9 +347,12 @@
         stage2 = lambda one, inner: (inward(one), outward(inner), over(one))
         stage3 = lambda middle, two: (outward(middle), over(two))
 
-        a, b, own, sibling = locked(*pieces, tokens[0], to_member(tokens[0], 1))
+        a = stack(0, *messages[:2])
+        a_one, a_inner, a_far0 = locked(*stage1(a))
+        messages.append(to_member(after(messages[2], a_one), 1))
+        own = after(tokens[0], messages[2], a_one)
         across = to_member(own, 2)
-        a_one, a_inner, a_far0 = locked(*stage1(a))
+        b, sibling = locked(stack(rows, *messages[2:]), to_member(own, 1))
         b_one, b_inner, b_far0 = locked(*stage1(b))
         a_middle, a_outer, a_far1 = locked(*stage2(a_one, a_inner))
         b_middle, b_outer, b_far1 = locked(*stage2(b_one, b_inner))
@@ -361,11 +377,12 @@
         pieces = [a_three, a_far2, b_three, b_far2]
         outer_kv, outer_q = [outward(a_inner[:, at]) for at in (slice(0, cut), slice(cut, None))]
         inner = a_inner
-        finish = lambda at, *others: over(after(b_three[:, at], *others))
+        finish = lambda at: over(b_three[:, at])
     else:
         across, sibling = to_member(tokens[0], 2), to_member(tokens[0], 1)
         books = [tokens[0], sibling, across, to_member(across, 1)]
-        full = gathered(jnp.concatenate(pieces, axis=0))
+        messages.append(to_member(messages[2], 1))
+        full = gathered(jnp.concatenate([stack(0, *messages[:2]), stack(rows, *messages[2:])], axis=0))
         deep = MEMBERS * HEAD_SIZE // 2
         upper, lower = [part[:deep] for part in full], [part[deep:] for part in full]
         late = [(n_pieces - 1, 0), (n_pieces - 1, 1)]
@@ -377,10 +394,10 @@
         pieces = [lower[-2]]
         outer_kv, outer_q = upper[-1][:, :cut], upper[-1][:, cut:]
         inner = upper[-1]
-        finish = lambda at, *others: lower[-1][:, at]
+        finish = lambda at: lower[-1][:, at]
 
     halves = [slice(k * HEAD_SIZE, (k + 2) * HEAD_SIZE) for k in (0, 2, 4)]
-    lower_kv, lower_q0 = finish(halves[0]), finish(halves[1])
+    lower_kv, lower_q0, lower_q1 = [finish(at) for at in halves]
     found = call(
         functools.partial(kv_body, len(late) + 1),
         [shape((length, 2 * HEAD_SIZE), bf16), shape((HEAD_SIZE, 2 * HEAD_SIZE), f32)] * MEMBERS
@@ -393,10 +410,11 @@
 
     base = None
     for a in range(1, n_groups):
-        term = permute(total, lambda gg, mm, zz: (gg ^ a, mm, zz) if gg < gg ^ a else None)
-        base = term if base is None else base.astype(f32) + term.astype(f32)
-
-    lower_q1 = finish(halves[2], total)
+        term = permute(total, lambda gg, mm, zz: (gg ^ a, mm, zz))
+        if n_groups > 2:
+            term = jnp.where((g ^ a) < g, term, 0).astype(f32)
+        base = term if base is None else base + term
+
     half = group // 2
 
     def local(segs, part, lower_q):
@@ -431,11 +449,15 @@
     sent = [mine0, mine1]
     for k, parts in ((1, (one0, one1)), (2, (two0, two1)), (3, (three0, three1))):
         sent += [to_member(part, k) for part in parts]
+    far = sent[4:]
+    (there,) = call(
+        gate_body, [shape((4,), jnp.int32)], [SMEM] + [ANY] * len(far), out_spec=SMEM, moved=16 << 20
+    )(here, *far)
     (output,) = call(
         functools.partial(assemble_body, (2,) * MEMBERS),
         [shape((length, w_query.shape[1]), bf16)],
         [SMEM] + [VMEM] * len(sent),
-    )(here, *sent)
+    )(there, *sent)
     return output[None]
 
 

time: 119 us -> 117 us (0.983); the launches traced: 117 us -> 116 us
  starting transfers between devices: 55.2 us -> 49.8 us
  local copies, waits for them, and re-layouts: 4.41 us -> 9.1 us
    ppermute x35, starting transfers between devices: 55.2 us -> 49.8 us  [permute(): return lax.ppermute(array, AXES, pairs)]
    unnamed x18 -> x30, local copies, waits for them, and re-layouts: 4.3 us -> 9.04 us
    pallas_call x2, Pallas kernels: 9.37 us -> 8.16 us  [project(): call(functools.partial(project_body, early, late, line), [shape((length,...]
    pallas_call x1 -> x4, Pallas kernels: 0.63 us -> 1.82 us  [the longest x1 1.14 us: shards(): call(gate_body, [shape((4,), jnp.int32)], [SMEM] + [ANY] * len(far), out_...]
  transfers between devices with their start and end apart: 35 -> 35, of which waited for: 10 -> 12; matrix products, arithmetic and copies ran while one was open for 3% -> 3% of each run, Pallas kernels for 19% -> 18%
where the time goes in v12:
time: 117 us; the launch traced here: 116 us
  starting transfers between devices  49.8 us (43%)
  waiting for transfers between devices  29.7 us (25%)
  Pallas kernels  23.5 us (20%)
  local copies, waits for them, and re-layouts  9.1 us (8%)
  other arithmetic  3.29 us (3%)
    ppermute x35, starting transfers between devices, permute(): return lax.ppermute(array, AXES, pairs)  49.8 us
    ppermute x35, waiting for transfers between devices, permute(): return lax.ppermute(array, AXES, pairs)  29.7 us
    unnamed x30, local copies, waits for them, and re-layouts  9.04 us
    pallas_call x2, Pallas kernels, project(): call(functools.partial(project_body, early, late, line), [shape((length,...  8.16 us
    pallas_call x3, Pallas kernels, local(): call(functools.partial(local_body, len(segs), len(late) + 1, halves[1 + p...  6.01 us
    pallas_call x3, Pallas kernels, mix(): call(functools.partial(mix_body, segs, parts, group), [shape((length, hal...  3.96 us
  transfers between devices with their start and end apart: 35, of which 12 were waited for; matrix products, arithmetic and copies ran while one was open for 3% of the time, Pallas kernels for 18%

profile of v12, /device:TPU:9, one launch (start us, length us, event | category | flops | bytes accessed | tf_op | source)
XLA Modules:
  0.0 116.5 jit_solution(5953575668280092756)
XLA Ops:
  0.7 1.0 copy-done.6
  1.8 0.9 copy-done.7
  2.7 0.9 copy-done.8
  3.6 0.7 copy-done.10
  4.3 0.6 shard_map.73
  4.9 0.7 collective-permute-start
  5.7 1.2 %collective-permute-start.10 = (bf16[272,768]{1,0:T(8,128)(2,1)S(1)}, bf16[272,768]{1,0:T(8,128)(2,1)S(1)}, u32[]{:S(2)}, u32[]{:S(2)}) collective-permute-start(bf16[272,768]{1,0:T(8,128)(2,1)S(1)} %get-tuple-element.90), channel_id=1, source_target_pairs={{0,8},{1,9},{2,10},{3,11},{4,12},{5,13},{6,14},{7,15},{8,0},{9,1},... | collective-permute-start | bytes 1253384 | tf_op jit(solution)/shard_map/ppermute | solution.py:287
  7.1 4.3 %collective-permute-start.2 = (bf16[256,768]{1,0:T(8,128)(2,1)S(1)}, bf16[256,768]{1,0:T(8,128)(2,1)S(1)}, u32[]{:S(2)}, u32[]{:S(2)}) collective-permute-start(bf16[256,768]{1,0:T(8,128)(2,1)S(1)} %shard_map.74.refs_2_), channel_id=1, source_target_pairs={{1,2},{2,1},{5,6},{6,5},{9,10},{10,9},{13,14},{14,13},{17,18},{18,... | collective-permute-start | bytes 1179656 | tf_op jit(solution)/shard_map/ppermute | solution.py:287
  11.5 1.3 %collective-permute-start.3 = (bf16[256,768]{1,0:T(8,128)(2,1)S(1)}, bf16[256,768]{1,0:T(8,128)(2,1)S(1)}, u32[]{:S(2)}, u32[]{:S(2)}) collective-permute-start(bf16[256,768]{1,0:T(8,128)(2,1)S(1)} %shard_map.74.refs_2_), channel_id=1, source_target_pairs={{0,16},{1,17},{2,18},{3,19},{4,20},{5,21},{6,22},{7,23},{8,24},{9,... | collective-permute-start | bytes 1179656 | tf_op jit(solution)/shard_map/ppermute | solution.py:287
  12.8 4.6 %collective-permute-done.1.refs_3_ = bf16[256,768]{1,0:T(8,128)(2,1)S(1)} collective-permute-done((bf16[256,768]{1,0:T(8,128)(2,1)S(1)}, bf16[256,768]{1,0:T(8,128)(2,1)S(1)}, u32[]{:S(2)}, u32[]{:S(2)}) %collective-permute-start.1) | collective-permute-done | bytes 393248 | tf_op jit(solution)/shard_map/ppermute | solution.py:287
  17.3 3.0 %collective-permute-done.2 = bf16[256,768]{1,0:T(8,128)(2,1)S(1)} collective-permute-done((bf16[256,768]{1,0:T(8,128)(2,1)S(1)}, bf16[256,768]{1,0:T(8,128)(2,1)S(1)}, u32[]{:S(2)}, u32[]{:S(2)}) %collective-permute-start.2) | collective-permute-done | bytes 393248 | tf_op jit(solution)/shard_map/ppermute | solution.py:287
  20.4 0.9 collective-permute-done.3.refs_5_
  21.3 1.8 %collective-permute-start.12 = (bf16[256,4096]{1,0:T(8,128)(2,1)}, bf16[256,4096]{1,0:T(8,128)(2,1)S(1)}, u32[]{:S(2)}, u32[]{:S(2)}) collective-permute-start(bf16[256,4096]{1,0:T(8,128)(2,1)} %bitcast.5), channel_id=1, source_target_pairs={{0,4},{1,5},{2,6},{3,7},{4,0},{5,1},{6,2},{7,3},{8,12},{9,13},{10,... | collective-permute-start | bytes 6291464 | tf_op jit(solution)/shard_map/ppermute | solution.py:287
  23.1 1.1 collective-permute-start.21
  24.4 3.0 %collective-permute-done.11.lower_ref.refs_18_.refs_12_.refs_5_.refs_10_ = bf16[272,768]{1,0:T(8,128)(2,1)S(1)} collective-permute-done((bf16[272,768]{1,0:T(8,128)(2,1)S(1)}, bf16[272,768]{1,0:T(8,128)(2,1)S(1)}, u32[]{:S(2)}, u32[]{:S(2)}) %collective-permute-start.11) | collective-permute-done | bytes 417824 | tf_op jit(solution)/shard_map/ppermute | solution.py:287
  27.5 1.4 %copy-done.1 = bf16[256,4096]{1,0:T(8,128)(2,1)} copy-done((bf16[256,4096]{1,0:T(8,128)(2,1)}, bf16[256,4096]{1,0:T(8,128)(2,1)S(1)}, u32[]{:S(2)}) %copy-start.1) | copy-done | bytes 2097176
  28.9 1.9 %collective-permute-start.14 = (bf16[256,768]{1,0:T(8,128)(2,1)S(1)}, bf16[256,768]{1,0:T(8,128)(2,1)}, u32[]{:S(2)}, u32[]{:S(2)}) collective-permute-start(bf16[256,768]{1,0:T(8,128)(2,1)S(1)} %shard_map.75.refs_7_), channel_id=1, source_target_pairs={{1,2},{2,1},{5,6},{6,5},{9,10},{10,9},{13,14},{14,13},{17,18},{18,... | collective-permute-start | bytes 1179656 | tf_op jit(solution)/shard_map/ppermute | solution.py:287
  30.8 1.3 %collective-permute-start.15 = (bf16[256,768]{1,0:T(8,128)(2,1)S(1)}, bf16[256,768]{1,0:T(8,128)(2,1)S(1)}, u32[]{:S(2)}, u32[]{:S(2)}) collective-permute-start(bf16[256,768]{1,0:T(8,128)(2,1)S(1)} %shard_map.75.refs_7_), channel_id=1, source_target_pairs={{0,16},{1,17},{2,18},{3,19},{4,20},{5,21},{6,22},{7,23},{8,24},{9,... | collective-permute-start | bytes 1179656 | tf_op jit(solution)/shard_map/ppermute | solution.py:287
  32.1 3.4 %collective-permute-start.4 = (bf16[256,768]{1,0:T(8,128)(2,1)S(1)}, bf16[256,768]{1,0:T(8,128)(2,1)S(1)}, u32[]{:S(2)}, u32[]{:S(2)}) collective-permute-start(bf16[256,768]{1,0:T(8,128)(2,1)S(1)} %collective-permute-done.1.refs_3_), channel_id=1, source_target_pairs={{1,2},{2,1},{5,6},{6,5},{9,10},{10,9},{13,14},{14,13},{17,18},{18,... | collective-permute-start | bytes 1179656 | tf_op jit(solution)/shard_map/ppermute | solution.py:287
  35.5 3.9 %collective-permute-done.13.refs_8_ = bf16[256,768]{1,0:T(8,128)(2,1)S(1)} collective-permute-done((bf16[256,768]{1,0:T(8,128)(2,1)S(1)}, bf16[256,768]{1,0:T(8,128)(2,1)S(1)}, u32[]{:S(2)}, u32[]{:S(2)}) %collective-permute-start.13) | collective-permute-done | bytes 393248 | tf_op jit(solution)/shard_map/ppermute | solution.py:287
  39.3 2.2 %collective-permute-start.5 = (bf16[256,768]{1,0:T(8,128)(2,1)S(1)}, bf16[256,768]{1,0:T(8,128)(2,1)S(1)}, u32[]{:S(2)}, u32[]{:S(2)}) collective-permute-start(bf16[256,768]{1,0:T(8,128)(2,1)S(1)} %collective-permute-done.2), channel_id=1, source_target_pairs={{1,0},{2,3},{5,4},{6,7},{9,8},{10,11},{13,12},{14,15},{17,16},{18,... | collective-permute-start | bytes 1179656 | tf_op jit(solution)/shard_map/ppermute | solution.py:287
  41.6 1.3 %collective-permute-start.6 = (bf16[256,768]{1,0:T(8,128)(2,1)S(1)}, bf16[256,768]{1,0:T(8,128)(2,1)}, u32[]{:S(2)}, u32[]{:S(2)}) collective-permute-start(bf16[256,768]{1,0:T(8,128)(2,1)S(1)} %collective-permute-done.1.refs_3_), channel_id=1, source_target_pairs={{0,16},{1,17},{2,18},{3,19},{4,20},{5,21},{6,22},{7,23},{8,24},{9,... | collective-permute-start | bytes 1179656 | tf_op jit(solution)/shard_map/ppermute | solution.py:287
  42.9 0.8 copy-done.3
  43.7 1.9 %collective-permute-start.16 = (bf16[256,768]{1,0:T(8,128)(2,1)S(1)}, bf16[256,768]{1,0:T(8,128)(2,1)}, u32[]{:S(2)}, u32[]{:S(2)}) collective-permute-start(bf16[256,768]{1,0:T(8,128)(2,1)S(1)} %collective-permute-done.13.refs_8_), channel_id=1, source_target_pairs={{1,2},{2,1},{5,6},{6,5},{9,10},{10,9},{13,14},{14,13},{17,18},{18,... | collective-permute-start | bytes 1179656 | tf_op jit(solution)/shard_map/ppermute | solution.py:287
  45.6 4.1 %collective-permute-done.4 = bf16[256,768]{1,0:T(8,128)(2,1)S(1)} collective-permute-done((bf16[256,768]{1,0:T(8,128)(2,1)S(1)}, bf16[256,768]{1,0:T(8,128)(2,1)S(1)}, u32[]{:S(2)}, u32[]{:S(2)}) %collective-permute-start.4) | collective-permute-done | bytes 393248 | tf_op jit(solution)/shard_map/ppermute | solution.py:287
  49.6 2.0 %collective-permute-start.17 = (bf16[256,768]{1,0:T(8,128)(2,1)}, bf16[256,768]{1,0:T(8,128)(2,1)}, u32[]{:S(2)}, u32[]{:S(2)}) collective-permute-start(bf16[256,768]{1,0:T(8,128)(2,1)} %collective-permute-done.14), channel_id=1, source_target_pairs={{1,0},{2,3},{5,4},{6,7},{9,8},{10,11},{13,12},{14,15},{17,16},{18,... | collective-permute-start | bytes 1179656 | tf_op jit(solution)/shard_map/ppermute | solution.py:287
  51.7 0.8 copy-done.14
  52.4 1.2 %collective-permute-start.18 = (bf16[256,768]{1,0:T(8,128)(2,1)S(1)}, bf16[256,768]{1,0:T(8,128)(2,1)}, u32[]{:S(2)}, u32[]{:S(2)}) collective-permute-start(bf16[256,768]{1,0:T(8,128)(2,1)S(1)} %collective-permute-done.13.refs_8_), channel_id=1, source_target_pairs={{0,16},{1,17},{2,18},{3,19},{4,20},{5,21},{6,22},{7,23},{8,24},{9,... | collective-permute-start | bytes 1179656 | tf_op jit(solution)/shard_map/ppermute | solution.py:287
  53.7 1.9 %collective-permute-start.7 = (bf16[256,768]{1,0:T(8,128)(2,1)}, bf16[256,768]{1,0:T(8,128)(2,1)S(1)}, u32[]{:S(2)}, u32[]{:S(2)}) collective-permute-start(bf16[256,768]{1,0:T(8,128)(2,1)} %copy-done.11), channel_id=1, source_target_pairs={{1,0},{2,3},{5,4},{6,7},{9,8},{10,11},{13,12},{14,15},{17,16},{18,... | collective-permute-start | bytes 1179656 | tf_op jit(solution)/shard_map/ppermute | solution.py:287
  55.5 1.1 broadcast_select_fusion.3.refs_4_
  56.6 1.4 %collective-permute-done.16 = bf16[256,768]{1,0:T(8,128)(2,1)} collective-permute-done((bf16[256,768]{1,0:T(8,128)(2,1)S(1)}, bf16[256,768]{1,0:T(8,128)(2,1)}, u32[]{:S(2)}, u32[]{:S(2)}) %collective-permute-start.16) | collective-permute-done | bytes 393248 | tf_op jit(solution)/shard_map/ppermute | solution.py:287
  58.0 1.2 %collective-permute-start.8 = (bf16[256,768]{1,0:T(8,128)(2,1)S(1)}, bf16[256,768]{1,0:T(8,128)(2,1)S(1)}, u32[]{:S(2)}, u32[]{:S(2)}) collective-permute-start(bf16[256,768]{1,0:T(8,128)(2,1)S(1)} %broadcast_select_fusion.3.refs_4_), channel_id=1, source_target_pairs={{0,16},{1,17},{2,18},{3,19},{4,20},{5,21},{6,22},{7,23},{8,24},{9,... | collective-permute-start | bytes 1179656 | tf_op jit(solution)/shard_map/ppermute | solution.py:287
  59.3 1.9 %collective-permute-start.9 = (bf16[256,768]{1,0:T(8,128)(2,1)}, bf16[256,768]{1,0:T(8,128)(2,1)S(1)}, u32[]{:S(2)}, u32[]{:S(2)}) collective-permute-start(bf16[256,768]{1,0:T(8,128)(2,1)} %collective-permute-done.6.refs_6_), channel_id=1, source_target_pairs={{1,2},{2,1},{5,6},{6,5},{9,10},{10,9},{13,14},{14,13},{17,18},{18,... | collective-permute-start | bytes 1179656 | tf_op jit(solution)/shard_map/ppermute | solution.py:287
  61.2 2.1 %collective-permute-start.19 = (bf16[256,768]{1,0:T(8,128)(2,1)}, bf16[256,768]{1,0:T(8,128)(2,1)S(1)}, u32[]{:S(2)}, u32[]{:S(2)}) collective-permute-start(bf16[256,768]{1,0:T(8,128)(2,1)} %collective-permute-done.16), channel_id=1, source_target_pairs={{1,0},{2,3},{5,4},{6,7},{9,8},{10,11},{13,12},{14,15},{17,16},{18,... | collective-permute-start | bytes 1179656 | tf_op jit(solution)/shard_map/ppermute | solution.py:287
  63.3 1.1 broadcast_select_fusion.1.refs_9_
  64.4 2.1 %collective-permute-done.7 = bf16[256,768]{1,0:T(8,128)(2,1)S(1)} collective-permute-done((bf16[256,768]{1,0:T(8,128)(2,1)}, bf16[256,768]{1,0:T(8,128)(2,1)S(1)}, u32[]{:S(2)}, u32[]{:S(2)}) %collective-permute-start.7) | collective-permute-done | bytes 393248 | tf_op jit(solution)/shard_map/ppermute | solution.py:287
  66.4 1.2 %collective-permute-start.20 = (bf16[256,768]{1,0:T(8,128)(2,1)S(1)}, bf16[256,768]{1,0:T(8,128)(2,1)S(1)}, u32[]{:S(2)}, u32[]{:S(2)}) collective-permute-start(bf16[256,768]{1,0:T(8,128)(2,1)S(1)} %broadcast_select_fusion.1.refs_9_), channel_id=1, source_target_pairs={{0,16},{1,17},{2,18},{3,19},{4,20},{5,21},{6,22},{7,23},{8,24},{9,... | collective-permute-start | bytes 1179656 | tf_op jit(solution)/shard_map/ppermute | solution.py:287
  67.7 2.0 %collective-permute-done.8.refs_1_ = bf16[256,768]{1,0:T(8,128)(2,1)S(1)} collective-permute-done((bf16[256,768]{1,0:T(8,128)(2,1)S(1)}, bf16[256,768]{1,0:T(8,128)(2,1)S(1)}, u32[]{:S(2)}, u32[]{:S(2)}) %collective-permute-start.8) | collective-permute-done | bytes 393248 | tf_op jit(solution)/shard_map/ppermute | solution.py:287
  69.7 1.0 collective-permute-done.21.refs_0_
  70.7 1.6 %copy-done.2 = bf16[256,4096]{1,0:T(8,128)(2,1)S(1)} copy-done((bf16[256,4096]{1,0:T(8,128)(2,1)S(1)}, bf16[256,4096]{1,0:T(8,128)(2,1)}, u32[]{:S(2)}) %copy-start.2) | copy-done | bytes 2097176
  72.2 1.0 copy-done.4
  73.2 3.8 %shard_map.76 = (f32[256,768]{1,0:T(8,128)S(1)}, f32[256,768]{1,0:T(8,128)S(1)}, bf16[256,1536]{1,0:T(8,128)(2,1)S(1)}, bf16[256,1536]{1,0:T(8,128)(2,1)S(1)}) custom-call(s32[4]{0:T(128)S(1)} %pad_add_fusion.here_ref, bf16[256,4096]{1,0:T(8,128)(2,1)S(1)} %bitcast.7, bf16[256,4096]{1,0:T(8,128)(2,1)S(1)} %copy-done.2, ...), custom_call_target="tpu_custom_call" | custom-call | flops 2013265920 | bytes 4194304 | tf_op jit(solution)/shard_map/pallas_call | solution.py:324
  77.1 0.9 collective-permute-done.20.refs_3_
  78.0 3.3 %collective-permute-start.24 = (bf16[256,4096]{1,0:T(8,128)(2,1)}, bf16[256,4096]{1,0:T(8,128)(2,1)S(1)}, u32[]{:S(2)}, u32[]{:S(2)}) collective-permute-start(bf16[256,4096]{1,0:T(8,128)(2,1)} %collective-permute-done.21.refs_0_), channel_id=1, source_target_pairs={{0,4},{1,5},{2,6},{3,7},{4,0},{5,1},{6,2},{7,3},{8,12},{9,13},{10,... | collective-permute-start | bytes 6291464 | tf_op jit(solution)/shard_map/ppermute | solution.py:287
  81.3 1.8 %collective-permute-start.22 = (bf16[256,256]{1,0:T(8,128)(2,1)S(1)}, bf16[256,256]{1,0:T(8,128)(2,1)S(1)}, u32[]{:S(2)}, u32[]{:S(2)}) collective-permute-start(bf16[256,256]{1,0:T(8,128)(2,1)S(1)} %slice.15), channel_id=1, source_target_pairs={{1,0},{2,3},{5,4},{6,7},{9,8},{10,11},{13,12},{14,15},{17,16},{18,... | collective-permute-start | bytes 393224 | tf_op jit(solution)/shard_map/ppermute | solution.py:287
  83.2 1.3 %collective-permute-start.26 = (bf16[256,512]{1,0:T(8,128)(2,1)S(1)}, bf16[256,512]{1,0:T(8,128)(2,1)S(1)}, u32[]{:S(2)}, u32[]{:S(2)}) collective-permute-start(bf16[256,512]{1,0:T(8,128)(2,1)S(1)} %slice.17), channel_id=1, source_target_pairs={{1,0},{2,3},{5,4},{6,7},{9,8},{10,11},{13,12},{14,15},{17,16},{18,... | collective-permute-start | bytes 786440 | tf_op jit(solution)/shard_map/ppermute | solution.py:287
  84.6 1.1 broadcast_select_fusion.refs_2_
  85.7 1.1 collective-permute-start.23
  87.2 4.4 %shard_map.77 = (f32[256,768]{1,0:T(8,128)S(1)}, f32[256,768]{1,0:T(8,128)S(1)}, bf16[256,1536]{1,0:T(8,128)(2,1)S(1)}, bf16[256,1536]{1,0:T(8,128)(2,1)S(1)}) custom-call(s32[4]{0:T(128)S(1)} %pad_add_fusion.here_ref, bf16[256,4096]{1,0:T(8,128)(2,1)} %collective-permute-done.21.refs_0_, bf16[256,4096]{1,0:T(8,128)(2,1)S(1)} %collective-permute-done.24.refs_1_, ...), custom_call_target="tpu_custom_call" | custom-call | flops 2013265920 | bytes 4194304 | tf_op jit(solution)/shard_map/pallas_call | solution.py:324
  91.6 1.9 %shard_map.78 = (bf16[256,256]{1,0:T(8,128)(2,1)S(1)}, f32[128,256]{1,0:T(8,128)S(1)}, bf16[256,256]{1,0:T(8,128)(2,1)S(1)}, f32[128,256]{1,0:T(8,128)S(1)}, bf1...) custom-call(s32[4]{0:T(128)S(1)} %pad_add_fusion.here_ref, ...), custom_call_target="tpu_custom_call" | custom-call | flops 805306368 | bytes 4194304 | tf_op jit(solution)/shard_map/pallas_call | solution.py:401
  93.5 1.1 collective-permute-start.25
  95.1 2.4 %shard_map.79 = (bf16[256,256]{1,0:T(8,128)(2,1)S(1)}, f32[256,256]{1,0:T(8,128)S(1)}, bf16[256,256]{1,0:T(8,128)(2,1)S(1)}, f32[256,256]{1,0:T(8,128)S(1)}, bf1...) custom-call(s32[4]{0:T(128)S(1)} %pad_add_fusion.here_ref, ...), custom_call_target="tpu_custom_call" | custom-call | flops 268435456 | bytes 4194304 | tf_op jit(solution)/shard_map/pallas_call | solution.py:421
  97.5 1.2 %shard_map.80 = (bf16[256,256]{1,0:T(8,128)(2,1)S(1)}, bf16[256,256]{1,0:T(8,128)(2,1)S(1)}) custom-call(s32[4]{0:T(128)S(1)} %pad_add_fusion.here_ref, f32[16]{0:T(128)S(1)} %copy-done.9, bf16[128,256]{1,0:T(8,128)(2,1)S(1)} %collective-permute-done.25.base_ref, f32[128,256]{1,0:T(8,128)S(1)} %get-tuple-element.126.refs_0_, ...), custom_call_target="tpu_custom_call" | custom-call | flops 201326592 | bytes 4194304 | tf_op jit(solution)/shard_map/pallas_call | solution.py:432
  98.7 1.2 %collective-permute-start.28 = (bf16[256,256]{1,0:T(8,128)(2,1)S(1)}, bf16[256,256]{1,0:T(8,128)(2,1)S(1)}, u32[]{:S(2)}, u32[]{:S(2)}) collective-permute-start(bf16[256,256]{1,0:T(8,128)(2,1)S(1)} %get-tuple-element.132), channel_id=1, source_target_pairs={{0,8},{1,9},{2,10},{3,11},{4,12},{5,13},{6,14},{7,15},{8,0},{9,1},... | collective-permute-start | bytes 393224 | tf_op jit(solution)/shard_map/ppermute | solution.py:287
  99.8 2.4 %collective-permute-start.31 = (bf16[256,256]{1,0:T(8,128)(2,1)S(1)}, bf16[256,256]{1,0:T(8,128)(2,1)S(1)}, u32[]{:S(2)}, u32[]{:S(2)}) collective-permute-start(bf16[256,256]{1,0:T(8,128)(2,1)S(1)} %get-tuple-element.133), channel_id=1, source_target_pairs={{0,12},{1,13},{2,14},{3,15},{4,8},{5,9},{6,10},{7,11},{8,4},{9,5},... | collective-permute-start | bytes 393224 | tf_op jit(solution)/shard_map/ppermute | solution.py:287
  102.3 1.9 %shard_map.81 = (bf16[256,256]{1,0:T(8,128)(2,1)S(1)}, f32[256,256]{1,0:T(8,128)S(1)}, bf16[256,256]{1,0:T(8,128)(2,1)S(1)}, f32[256,256]{1,0:T(8,128)S(1)}) custom-call(s32[4]{0:T(128)S(1)} %pad_add_fusion.here_ref, bf16[256,768]{1,0:T(8,128)(2,1)S(1)} %broadcast_select_fusion.2.refs_0_, bf16[256,768]{1,0:T(8,128)(2,1)S(1)} %collective-permute-done.8.refs_1_, ...), custom_call_target="tpu_custom_call" | custom-call | flops 134217728 | bytes 4194304 | tf_op jit(solution)/shard_map/pallas_call | solution.py:421
  104.2 1.2 %shard_map.82 = (bf16[256,256]{1,0:T(8,128)(2,1)S(1)}, bf16[256,256]{1,0:T(8,128)(2,1)S(1)}) custom-call(s32[4]{0:T(128)S(1)} %pad_add_fusion.here_ref, f32[16]{0:T(128)S(1)} %copy-done.9, bf16[128,256]{1,0:T(8,128)(2,1)S(1)} %collective-permute-done.25.base_ref, f32[128,256]{1,0:T(8,128)S(1)} %get-tuple-element.126.refs_0_, ...), custom_call_target="tpu_custom_call" | custom-call | flops 201326592 | bytes 4194304 | tf_op jit(solution)/shard_map/pallas_call | solution.py:432
  105.4 1.1 collective-permute-start.30
  106.7 1.7 %shard_map.84 = (bf16[256,256]{1,0:T(8,128)(2,1)S(1)}, f32[256,256]{1,0:T(8,128)S(1)}, bf16[256,256]{1,0:T(8,128)(2,1)S(1)}, f32[256,256]{1,0:T(8,128)S(1)}) custom-call(s32[4]{0:T(128)S(1)} %pad_add_fusion.here_ref, bf16[256,768]{1,0:T(8,128)(2,1)S(1)} %broadcast_select_fusion.2.refs_0_, bf16[256,768]{1,0:T(8,128)(2,1)S(1)} %collective-permute-done.8.refs_1_, ...), custom_call_target="tpu_custom_call" | custom-call | flops 134217728 | bytes 4194304 | tf_op jit(solution)/shard_map/pallas_call | solution.py:421
  108.4 1.6 %shard_map.85 = (bf16[256,256]{1,0:T(8,128)(2,1)S(1)}, bf16[256,256]{1,0:T(8,128)(2,1)S(1)}, bf16[256,256]{1,0:T(8,128)(2,1)S(1)}, bf16[256,256]{1,0:T(8,128)(2,1)S(1)}) custom-call(s32[4]{0:T(128)S(1)} %pad_add_fusion.here_ref, f32[16]{0:T(128)S(1)} %copy-done.9, bf16[128,256]{1,0:T(8,128)(2,1)S(1)} %collective-permute-done.25.base_ref, ...), custom_call_target="tpu_custom_call" | custom-call | flops 402653184 | bytes 4194304 | tf_op jit(solution)/shard_map/pallas_call | solution.py:432
  110.1 0.6 collective-permute-start.33
  110.8 2.8 %collective-permute-done.32.refs_3_.refs_7_ = bf16[256,256]{1,0:T(8,128)(2,1)S(1)} collective-permute-done((bf16[256,256]{1,0:T(8,128)(2,1)S(1)}, bf16[256,256]{1,0:T(8,128)(2,1)S(1)}, u32[]{:S(2)}, u32[]{:S(2)}) %collective-permute-start.32) | collective-permute-done | bytes 131104 | tf_op jit(solution)/shard_map/ppermute | solution.py:287
  113.6 1.1 shard_map.83.here_ref
  114.8 1.6 %shard_map.86 = bf16[256,2048]{1,0:T(8,128)(2,1)} custom-call(s32[4]{0:T(128)S(1)} %shard_map.83.here_ref, bf16[256,256]{1,0:T(8,128)(2,1)S(1)} %get-tuple-element.151.refs_0_, bf16[256,256]{1,0:T(8,128)(2,1)S(1)} %get-tuple-element.152.refs_1_, bf16[256,256]{1,0:T(8,128)(2,1)S(1)} %collective-permute-done.33.refs_2_, ...), custom_call_target="tpu_custom_call" | custom-call | bytes 4194304 | tf_op jit(solution)/shard_map/pallas_call | solution.py:456
  (58 shorter events, 2.2 us)
Async XLA Ops:
  0.7 1.0 copy-start.6
  1.8 0.9 copy-start.7
  2.7 0.9 copy-start.8
  3.6 0.7 copy-start.10
  4.9 2.0 %collective-permute-start = (bf16[144,768]{1,0:T(8,128)(2,1)S(1)}, bf16[144,768]{1,0:T(8,128)(2,1)S(1)}, u32[]{:S(2)}, u32[]{:S(2)}) collective-permute-start(bf16[144,768]{1,0:T(8,128)(2,1)S(1)} %get-tuple-element.81), channel_id=1, source_target_pairs={{0,4},{1,5},{2,6},{3,7},{4,0},{5,1},{6,2},{7,3},{8,12},{9,13},{10,... | collective-permute-start | bytes 663560 | tf_op jit(solution)/shard_map/ppermute | solution.py:287
  5.7 15.6 %collective-permute-start.10 = (bf16[272,768]{1,0:T(8,128)(2,1)S(1)}, bf16[272,768]{1,0:T(8,128)(2,1)S(1)}, u32[]{:S(2)}, u32[]{:S(2)}) collective-permute-start(bf16[272,768]{1,0:T(8,128)(2,1)S(1)} %get-tuple-element.90), channel_id=1, source_target_pairs={{0,8},{1,9},{2,10},{3,11},{4,12},{5,13},{6,14},{7,15},{8,0},{9,1},... | collective-permute-start | bytes 1253384 | tf_op jit(solution)/shard_map/ppermute | solution.py:287
  6.9 10.4 %collective-permute-start.1 = (bf16[256,768]{1,0:T(8,128)(2,1)S(1)}, bf16[256,768]{1,0:T(8,128)(2,1)S(1)}, u32[]{:S(2)}, u32[]{:S(2)}) collective-permute-start(bf16[256,768]{1,0:T(8,128)(2,1)S(1)} %shard_map.74.refs_2_), channel_id=1, source_target_pairs={{0,1},{1,0},{2,3},{3,2},{4,5},{5,4},{6,7},{7,6},{8,9},{9,8},{10,11... | collective-permute-start | bytes 1179656 | tf_op jit(solution)/shard_map/ppermute | solution.py:287
  7.1 13.2 %collective-permute-start.2 = (bf16[256,768]{1,0:T(8,128)(2,1)S(1)}, bf16[256,768]{1,0:T(8,128)(2,1)S(1)}, u32[]{:S(2)}, u32[]{:S(2)}) collective-permute-start(bf16[256,768]{1,0:T(8,128)(2,1)S(1)} %shard_map.74.refs_2_), channel_id=1, source_target_pairs={{1,2},{2,1},{5,6},{6,5},{9,10},{10,9},{13,14},{14,13},{17,18},{18,... | collective-permute-start | bytes 1179656 | tf_op jit(solution)/shard_map/ppermute | solution.py:287
  11.5 9.8 %collective-permute-start.3 = (bf16[256,768]{1,0:T(8,128)(2,1)S(1)}, bf16[256,768]{1,0:T(8,128)(2,1)S(1)}, u32[]{:S(2)}, u32[]{:S(2)}) collective-permute-start(bf16[256,768]{1,0:T(8,128)(2,1)S(1)} %shard_map.74.refs_2_), channel_id=1, source_target_pairs={{0,16},{1,17},{2,18},{3,19},{4,20},{5,21},{6,22},{7,23},{8,24},{9,... | collective-permute-start | bytes 1179656 | tf_op jit(solution)/shard_map/ppermute | solution.py:287
  20.4 31.3 %copy-start.13 = (bf16[256,768]{1,0:T(8,128)(2,1)}, bf16[256,768]{1,0:T(8,128)(2,1)S(1)}, u32[]{:S(2)}) copy-start(bf16[256,768]{1,0:T(8,128)(2,1)S(1)} %collective-permute-done.2) | copy-start | bytes 1179652
  21.3 6.2 %collective-permute-start.12 = (bf16[256,4096]{1,0:T(8,128)(2,1)}, bf16[256,4096]{1,0:T(8,128)(2,1)S(1)}, u32[]{:S(2)}, u32[]{:S(2)}) collective-permute-start(bf16[256,4096]{1,0:T(8,128)(2,1)} %bitcast.5), channel_id=1, source_target_pairs={{0,4},{1,5},{2,6},{3,7},{4,0},{5,1},{6,2},{7,3},{8,12},{9,13},{10,... | collective-permute-start | bytes 6291464 | tf_op jit(solution)/shard_map/ppermute | solution.py:287
  23.1 47.6 %collective-permute-start.21 = (bf16[256,4096]{1,0:T(8,128)(2,1)}, bf16[256,4096]{1,0:T(8,128)(2,1)}, u32[]{:S(2)}, u32[]{:S(2)}) collective-permute-start(bf16[256,4096]{1,0:T(8,128)(2,1)} %bitcast.6), channel_id=1, source_target_pairs={{0,8},{1,9},{2,10},{3,11},{4,12},{5,13},{6,14},{7,15},{8,0},{9,1},... | collective-permute-start | bytes 6291464 | tf_op jit(solution)/shard_map/ppermute | solution.py:287
  24.2 3.3 %collective-permute-start.11 = (bf16[272,768]{1,0:T(8,128)(2,1)S(1)}, bf16[272,768]{1,0:T(8,128)(2,1)S(1)}, u32[]{:S(2)}, u32[]{:S(2)}) collective-permute-start(bf16[272,768]{1,0:T(8,128)(2,1)S(1)} %collective-permute-done.10.upper_ref.refs_17_.refs_11_.refs_4_.refs_9_), channel_id=1, source_target_pairs={{0,4},{1,5},{2,6},{3,7},{4,0},{5,1},{6,2},{7,3},{8,12},{9,13},{10,... | collective-permute-start | bytes 1253384 | tf_op jit(solution)/shard_map/ppermute | solution.py:287
  27.5 1.4 %copy-start.1 = (bf16[256,4096]{1,0:T(8,128)(2,1)}, bf16[256,4096]{1,0:T(8,128)(2,1)S(1)}, u32[]{:S(2)}) copy-start(bf16[256,4096]{1,0:T(8,128)(2,1)S(1)} %collective-permute-done.12.refs_1_) | copy-start | bytes 6291460
  28.9 10.4 %collective-permute-start.13 = (bf16[256,768]{1,0:T(8,128)(2,1)S(1)}, bf16[256,768]{1,0:T(8,128)(2,1)S(1)}, u32[]{:S(2)}, u32[]{:S(2)}) collective-permute-start(bf16[256,768]{1,0:T(8,128)(2,1)S(1)} %shard_map.75.refs_7_), channel_id=1, source_target_pairs={{0,1},{1,0},{2,3},{3,2},{4,5},{5,4},{6,7},{7,6},{8,9},{9,8},{10,11... | collective-permute-start | bytes 1179656 | tf_op jit(solution)/shard_map/ppermute | solution.py:287
  28.9 12.7 %collective-permute-start.14 = (bf16[256,768]{1,0:T(8,128)(2,1)S(1)}, bf16[256,768]{1,0:T(8,128)(2,1)}, u32[]{:S(2)}, u32[]{:S(2)}) collective-permute-start(bf16[256,768]{1,0:T(8,128)(2,1)S(1)} %shard_map.75.refs_7_), channel_id=1, source_target_pairs={{1,2},{2,1},{5,6},{6,5},{9,10},{10,9},{13,14},{14,13},{17,18},{18,... | collective-permute-start | bytes 1179656 | tf_op jit(solution)/shard_map/ppermute | solution.py:287
  30.8 12.1 %collective-permute-start.15 = (bf16[256,768]{1,0:T(8,128)(2,1)S(1)}, bf16[256,768]{1,0:T(8,128)(2,1)S(1)}, u32[]{:S(2)}, u32[]{:S(2)}) collective-permute-start(bf16[256,768]{1,0:T(8,128)(2,1)S(1)} %shard_map.75.refs_7_), channel_id=1, source_target_pairs={{0,16},{1,17},{2,18},{3,19},{4,20},{5,21},{6,22},{7,23},{8,24},{9,... | collective-permute-start | bytes 1179656 | tf_op jit(solution)/shard_map/ppermute | solution.py:287
  32.1 17.5 %collective-permute-start.4 = (bf16[256,768]{1,0:T(8,128)(2,1)S(1)}, bf16[256,768]{1,0:T(8,128)(2,1)S(1)}, u32[]{:S(2)}, u32[]{:S(2)}) collective-permute-start(bf16[256,768]{1,0:T(8,128)(2,1)S(1)} %collective-permute-done.1.refs_3_), channel_id=1, source_target_pairs={{1,2},{2,1},{5,6},{6,5},{9,10},{10,9},{13,14},{14,13},{17,18},{18,... | collective-permute-start | bytes 1179656 | tf_op jit(solution)/shard_map/ppermute | solution.py:287
  39.3 12.3 %collective-permute-start.5 = (bf16[256,768]{1,0:T(8,128)(2,1)S(1)}, bf16[256,768]{1,0:T(8,128)(2,1)S(1)}, u32[]{:S(2)}, u32[]{:S(2)}) collective-permute-start(bf16[256,768]{1,0:T(8,128)(2,1)S(1)} %collective-permute-done.2), channel_id=1, source_target_pairs={{1,0},{2,3},{5,4},{6,7},{9,8},{10,11},{13,12},{14,15},{17,16},{18,... | collective-permute-start | bytes 1179656 | tf_op jit(solution)/shard_map/ppermute | solution.py:287
  41.6 12.1 %collective-permute-start.6 = (bf16[256,768]{1,0:T(8,128)(2,1)S(1)}, bf16[256,768]{1,0:T(8,128)(2,1)}, u32[]{:S(2)}, u32[]{:S(2)}) collective-permute-start(bf16[256,768]{1,0:T(8,128)(2,1)S(1)} %collective-permute-done.1.refs_3_), channel_id=1, source_target_pairs={{0,16},{1,17},{2,18},{3,19},{4,20},{5,21},{6,22},{7,23},{8,24},{9,... | collective-permute-start | bytes 1179656 | tf_op jit(solution)/shard_map/ppermute | solution.py:287
  42.9 0.8 copy-start.3
  43.7 14.4 %collective-permute-start.16 = (bf16[256,768]{1,0:T(8,128)(2,1)S(1)}, bf16[256,768]{1,0:T(8,128)(2,1)}, u32[]{:S(2)}, u32[]{:S(2)}) collective-permute-start(bf16[256,768]{1,0:T(8,128)(2,1)S(1)} %collective-permute-done.13.refs_8_), channel_id=1, source_target_pairs={{1,2},{2,1},{5,6},{6,5},{9,10},{10,9},{13,14},{14,13},{17,18},{18,... | collective-permute-start | bytes 1179656 | tf_op jit(solution)/shard_map/ppermute | solution.py:287
  49.6 2.0 %copy-start.11 = (bf16[256,768]{1,0:T(8,128)(2,1)}, bf16[256,768]{1,0:T(8,128)(2,1)S(1)}, u32[]{:S(2)}) copy-start(bf16[256,768]{1,0:T(8,128)(2,1)S(1)} %collective-permute-done.4) | copy-start | bytes 1179652
  49.6 9.7 %collective-permute-start.17 = (bf16[256,768]{1,0:T(8,128)(2,1)}, bf16[256,768]{1,0:T(8,128)(2,1)}, u32[]{:S(2)}, u32[]{:S(2)}) collective-permute-start(bf16[256,768]{1,0:T(8,128)(2,1)} %collective-permute-done.14), channel_id=1, source_target_pairs={{1,0},{2,3},{5,4},{6,7},{9,8},{10,11},{13,12},{14,15},{17,16},{18,... | collective-permute-start | bytes 1179656 | tf_op jit(solution)/shard_map/ppermute | solution.py:287
  51.7 0.8 copy-start.14
  52.4 8.8 %collective-permute-start.18 = (bf16[256,768]{1,0:T(8,128)(2,1)S(1)}, bf16[256,768]{1,0:T(8,128)(2,1)}, u32[]{:S(2)}, u32[]{:S(2)}) collective-permute-start(bf16[256,768]{1,0:T(8,128)(2,1)S(1)} %collective-permute-done.13.refs_8_), channel_id=1, source_target_pairs={{0,16},{1,17},{2,18},{3,19},{4,20},{5,21},{6,22},{7,23},{8,24},{9,... | collective-permute-start | bytes 1179656 | tf_op jit(solution)/shard_map/ppermute | solution.py:287
  53.7 17.0 %copy-start = (bf16[1,256,4096]{2,1,0:T(8,128)(2,1)S(1)}, bf16[1,256,4096]{2,1,0:T(8,128)(2,1)}, u32[]{:S(2)}) copy-start(bf16[1,256,4096]{2,1,0:T(8,128)(2,1)} %param.7) | copy-start | bytes 6291460
  53.7 12.8 %collective-permute-start.7 = (bf16[256,768]{1,0:T(8,128)(2,1)}, bf16[256,768]{1,0:T(8,128)(2,1)S(1)}, u32[]{:S(2)}, u32[]{:S(2)}) collective-permute-start(bf16[256,768]{1,0:T(8,128)(2,1)} %copy-done.11), channel_id=1, source_target_pairs={{1,0},{2,3},{5,4},{6,7},{9,8},{10,11},{13,12},{14,15},{17,16},{18,... | collective-permute-start | bytes 1179656 | tf_op jit(solution)/shard_map/ppermute | solution.py:287
  58.0 11.6 %collective-permute-start.8 = (bf16[256,768]{1,0:T(8,128)(2,1)S(1)}, bf16[256,768]{1,0:T(8,128)(2,1)S(1)}, u32[]{:S(2)}, u32[]{:S(2)}) collective-permute-start(bf16[256,768]{1,0:T(8,128)(2,1)S(1)} %broadcast_select_fusion.3.refs_4_), channel_id=1, source_target_pairs={{0,16},{1,17},{2,18},{3,19},{4,20},{5,21},{6,22},{7,23},{8,24},{9,... | collective-permute-start | bytes 1179656 | tf_op jit(solution)/shard_map/ppermute | solution.py:287
  59.3 10.4 %collective-permute-start.9 = (bf16[256,768]{1,0:T(8,128)(2,1)}, bf16[256,768]{1,0:T(8,128)(2,1)S(1)}, u32[]{:S(2)}, u32[]{:S(2)}) collective-permute-start(bf16[256,768]{1,0:T(8,128)(2,1)} %collective-permute-done.6.refs_6_), channel_id=1, source_target_pairs={{1,2},{2,1},{5,6},{6,5},{9,10},{10,9},{13,14},{14,13},{17,18},{18,... | collective-permute-start | bytes 1179656 | tf_op jit(solution)/shard_map/ppermute | solution.py:287
  61.2 15.8 %collective-permute-start.19 = (bf16[256,768]{1,0:T(8,128)(2,1)}, bf16[256,768]{1,0:T(8,128)(2,1)S(1)}, u32[]{:S(2)}, u32[]{:S(2)}) collective-permute-start(bf16[256,768]{1,0:T(8,128)(2,1)} %collective-permute-done.16), channel_id=1, source_target_pairs={{1,0},{2,3},{5,4},{6,7},{9,8},{10,11},{13,12},{14,15},{17,16},{18,... | collective-permute-start | bytes 1179656 | tf_op jit(solution)/shard_map/ppermute | solution.py:287
  66.4 11.6 %collective-permute-start.20 = (bf16[256,768]{1,0:T(8,128)(2,1)S(1)}, bf16[256,768]{1,0:T(8,128)(2,1)S(1)}, u32[]{:S(2)}, u32[]{:S(2)}) collective-permute-start(bf16[256,768]{1,0:T(8,128)(2,1)S(1)} %broadcast_select_fusion.1.refs_9_), channel_id=1, source_target_pairs={{0,16},{1,17},{2,18},{3,19},{4,20},{5,21},{6,22},{7,23},{8,24},{9,... | collective-permute-start | bytes 1179656 | tf_op jit(solution)/shard_map/ppermute | solution.py:287
  70.7 1.6 %copy-start.2 = (bf16[256,4096]{1,0:T(8,128)(2,1)S(1)}, bf16[256,4096]{1,0:T(8,128)(2,1)}, u32[]{:S(2)}) copy-start(bf16[256,4096]{1,0:T(8,128)(2,1)} %copy-done.1) | copy-start | bytes 6291460
  72.2 1.0 copy-start.4
  73.2 11.3 %copy-start.12 = (bf16[256,768]{1,0:T(8,128)(2,1)S(1)}, bf16[256,768]{1,0:T(8,128)(2,1)}, u32[]{:S(2)}) copy-start(bf16[256,768]{1,0:T(8,128)(2,1)} %copy-done.11) | copy-start | bytes 1179652
  77.0 10.2 %copy-start.5 = (bf16[256,768]{1,0:T(8,128)(2,1)S(1)}, bf16[256,768]{1,0:T(8,128)(2,1)}, u32[]{:S(2)}) copy-start(bf16[256,768]{1,0:T(8,128)(2,1)} %copy-done.3) | copy-start | bytes 1179652
  78.0 9.2 %collective-permute-start.24 = (bf16[256,4096]{1,0:T(8,128)(2,1)}, bf16[256,4096]{1,0:T(8,128)(2,1)S(1)}, u32[]{:S(2)}, u32[]{:S(2)}) collective-permute-start(bf16[256,4096]{1,0:T(8,128)(2,1)} %collective-permute-done.21.refs_0_), channel_id=1, source_target_pairs={{0,4},{1,5},{2,6},{3,7},{4,0},{5,1},{6,2},{7,3},{8,12},{9,13},{10,... | collective-permute-start | bytes 6291464 | tf_op jit(solution)/shard_map/ppermute | solution.py:287
  81.3 10.2 %collective-permute-start.22 = (bf16[256,256]{1,0:T(8,128)(2,1)S(1)}, bf16[256,256]{1,0:T(8,128)(2,1)S(1)}, u32[]{:S(2)}, u32[]{:S(2)}) collective-permute-start(bf16[256,256]{1,0:T(8,128)(2,1)S(1)} %slice.15), channel_id=1, source_target_pairs={{1,0},{2,3},{5,4},{6,7},{9,8},{10,11},{13,12},{14,15},{17,16},{18,... | collective-permute-start | bytes 393224 | tf_op jit(solution)/shard_map/ppermute | solution.py:287
  83.2 11.9 %collective-permute-start.26 = (bf16[256,512]{1,0:T(8,128)(2,1)S(1)}, bf16[256,512]{1,0:T(8,128)(2,1)S(1)}, u32[]{:S(2)}, u32[]{:S(2)}) collective-permute-start(bf16[256,512]{1,0:T(8,128)(2,1)S(1)} %slice.17), channel_id=1, source_target_pairs={{1,0},{2,3},{5,4},{6,7},{9,8},{10,11},{13,12},{14,15},{17,16},{18,... | collective-permute-start | bytes 786440 | tf_op jit(solution)/shard_map/ppermute | solution.py:287
  85.7 5.9 %collective-permute-start.23 = (bf16[256,256]{1,0:T(8,128)(2,1)S(1)}, bf16[256,256]{1,0:T(8,128)(2,1)S(1)}, u32[]{:S(2)}, u32[]{:S(2)}) collective-permute-start(bf16[256,256]{1,0:T(8,128)(2,1)S(1)} %get-tuple-element.157), channel_id=1, source_target_pairs={{0,16},{1,17},{2,18},{3,19},{4,20},{5,21},{6,22},{7,23},{8,24},{9,... | collective-permute-start | bytes 393224 | tf_op jit(solution)/shard_map/ppermute | solution.py:287
  86.7 8.3 %collective-permute-start.27 = (bf16[256,256]{1,0:T(8,128)(2,1)S(1)}, bf16[256,256]{1,0:T(8,128)(2,1)S(1)}, u32[]{:S(2)}, u32[]{:S(2)}) collective-permute-start(bf16[256,256]{1,0:T(8,128)(2,1)S(1)} %get-tuple-element.156), channel_id=1, source_target_pairs={{0,16},{1,17},{2,18},{3,19},{4,20},{5,21},{6,22},{7,23},{8,24},{9,... | collective-permute-start | bytes 393224 | tf_op jit(solution)/shard_map/ppermute | solution.py:287
  93.5 4.0 %collective-permute-start.25 = (bf16[128,256]{1,0:T(8,128)(2,1)S(1)}, bf16[128,256]{1,0:T(8,128)(2,1)S(1)}, u32[]{:S(2)}, u32[]{:S(2)}) collective-permute-start(bf16[128,256]{1,0:T(8,128)(2,1)S(1)} %get-tuple-element.118), channel_id=1, source_target_pairs={{0,16},{1,17},{2,18},{3,19},{4,20},{5,21},{6,22},{7,23},{8,24},{9,... | collective-permute-start | bytes 196616 | tf_op jit(solution)/shard_map/ppermute | solution.py:287
  94.6 7.7 %collective-permute-start.29 = (bf16[256,256]{1,0:T(8,128)(2,1)S(1)}, bf16[256,256]{1,0:T(8,128)(2,1)S(1)}, u32[]{:S(2)}, u32[]{:S(2)}) collective-permute-start(bf16[256,256]{1,0:T(8,128)(2,1)S(1)} %get-tuple-element.155), channel_id=1, source_target_pairs={{0,16},{1,17},{2,18},{3,19},{4,20},{5,21},{6,22},{7,23},{8,24},{9,... | collective-permute-start | bytes 393224 | tf_op jit(solution)/shard_map/ppermute | solution.py:287
  95.1 2.4 %copy-start.9 = (f32[16]{0:T(128)S(1)}, f32[16]{0:T(128)}, u32[]{:S(2)}) copy-start(f32[16]{0:T(128)} %gate_ref.5) | copy-start | bytes 196
  98.7 12.0 %collective-permute-start.28 = (bf16[256,256]{1,0:T(8,128)(2,1)S(1)}, bf16[256,256]{1,0:T(8,128)(2,1)S(1)}, u32[]{:S(2)}, u32[]{:S(2)}) collective-permute-start(bf16[256,256]{1,0:T(8,128)(2,1)S(1)} %get-tuple-element.132), channel_id=1, source_target_pairs={{0,8},{1,9},{2,10},{3,11},{4,12},{5,13},{6,14},{7,15},{8,0},{9,1},... | collective-permute-start | bytes 393224 | tf_op jit(solution)/shard_map/ppermute | solution.py:287
  99.8 11.0 %collective-permute-start.31 = (bf16[256,256]{1,0:T(8,128)(2,1)S(1)}, bf16[256,256]{1,0:T(8,128)(2,1)S(1)}, u32[]{:S(2)}, u32[]{:S(2)}) collective-permute-start(bf16[256,256]{1,0:T(8,128)(2,1)S(1)} %get-tuple-element.133), channel_id=1, source_target_pairs={{0,12},{1,13},{2,14},{3,15},{4,8},{5,9},{6,10},{7,11},{8,4},{9,5},... | collective-permute-start | bytes 393224 | tf_op jit(solution)/shard_map/ppermute | solution.py:287
  105.4 5.5 %collective-permute-start.30 = (bf16[256,256]{1,0:T(8,128)(2,1)S(1)}, bf16[256,256]{1,0:T(8,128)(2,1)S(1)}, u32[]{:S(2)}, u32[]{:S(2)}) collective-permute-start(bf16[256,256]{1,0:T(8,128)(2,1)S(1)} %get-tuple-element.139), channel_id=1, source_target_pairs={{0,8},{1,9},{2,10},{3,11},{4,12},{5,13},{6,14},{7,15},{8,0},{9,1},... | collective-permute-start | bytes 393224 | tf_op jit(solution)/shard_map/ppermute | solution.py:287
  106.5 7.2 %collective-permute-start.32 = (bf16[256,256]{1,0:T(8,128)(2,1)S(1)}, bf16[256,256]{1,0:T(8,128)(2,1)S(1)}, u32[]{:S(2)}, u32[]{:S(2)}) collective-permute-start(bf16[256,256]{1,0:T(8,128)(2,1)S(1)} %get-tuple-element.140), channel_id=1, source_target_pairs={{0,12},{1,13},{2,14},{3,15},{4,8},{5,9},{6,10},{7,11},{8,4},{9,5},... | collective-permute-start | bytes 393224 | tf_op jit(solution)/shard_map/ppermute | solution.py:287
  110.1 4.7 %collective-permute-start.33 = (bf16[256,256]{1,0:T(8,128)(2,1)S(1)}, bf16[256,256]{1,0:T(8,128)(2,1)S(1)}, u32[]{:S(2)}, u32[]{:S(2)}) collective-permute-start(bf16[256,256]{1,0:T(8,128)(2,1)S(1)} %get-tuple-element.153), channel_id=1, source_target_pairs={{0,4},{1,5},{2,6},{3,7},{4,0},{5,1},{6,2},{7,3},{8,12},{9,13},{10,... | collective-permute-start | bytes 393224 | tf_op jit(solution)/shard_map/ppermute | solution.py:287
  110.7 4.1 %collective-permute-start.34 = (bf16[256,256]{1,0:T(8,128)(2,1)S(1)}, bf16[256,256]{1,0:T(8,128)(2,1)S(1)}, u32[]{:S(2)}, u32[]{:S(2)}) collective-permute-start(bf16[256,256]{1,0:T(8,128)(2,1)S(1)} %get-tuple-element.154), channel_id=1, source_target_pairs={{0,4},{1,5},{2,6},{3,7},{4,0},{5,1},{6,2},{7,3},{8,12},{9,13},{10,... | collective-permute-start | bytes 393224 | tf_op jit(solution)/shard_map/ppermute | solution.py:287

commit v13 on v12

--- a/solution.py
+++ b/solution.py
@@ -79,7 +79,18 @@
     return lax.broadcasted_iota(jnp.int32, shape, dimension).astype(jnp.float32)
 
 
-def project_body(early, late, line, here_ref, *refs):
+def project_body(early, late, line, far, here_ref, *refs):
+    if far:
+        *refs, books_ref, sems = refs
+        copies = [
+            pltpu.make_async_copy(refs[0].at[here_ref[1] ^ k], books_ref.at[n], sems.at[n])
+            for n, k in enumerate(far)
+        ]
+        for one in copies:
+            one.start()
+        for one in copies:
+            one.wait()
+        refs = [books_ref.at[0], books_ref.at[1], *refs[1:]]
     tokens, pieces, outs = refs[:2], refs[2 : 2 + len(early)], refs[2 + len(early) :]
     length = tokens[0].shape[0]
     total = None
@@ -236,7 +247,7 @@
 
 
 def assemble_body(counts, here_ref, *refs):
-    parts, out = list(refs[:-1]), refs[-1]
+    parts, out = list(refs[1:-1]), refs[-1]
     width = out.shape[1] // MEMBERS
     for k, count in enumerate(counts):
         for c in range(count):
@@ -250,10 +261,8 @@
     out_ref[rows:] = lower_ref[first : first + rows]
 
 
-def gate_body(here_ref, *refs):
-    out = refs[-1]
-    for n in range(out.shape[0]):
-        out[n] = here_ref[n]
+def gate_body(*refs):
+    refs[-1][...] = jnp.zeros_like(refs[-1])
 
 
 def after(array, *others):
@@ -313,6 +322,11 @@
         natural = jnp.take(natural, members, axis=2).transpose(0, 2, 1, 3, 4)
         return list(natural.reshape(-1, MEMBERS * HEAD_SIZE, columns))
 
+    gather_tokens = lambda part: lax.all_gather(
+        part,
+        "seg",
+        axis_index_groups=[[gg * MEMBERS + mm for mm in range(MEMBERS)] for gg in range(n_groups)],
+    )
     stack = lambda first, *pair: call(
         functools.partial(stack_body, first), [shape((2 * rows, wide), bf16)], [VMEM] * 2, moved=1 << 20
     )(*pair)[0]
@@ -320,13 +334,15 @@
     sums, lates = [None] * MEMBERS, [None] * MEMBERS
 
     def project(segs, early, late, halves, line):
+        far = segs if segs == (2, 3) else ()
         deep = MEMBERS * HEAD_SIZE // 2
         found = call(
-            functools.partial(project_body, early, late, line),
+            functools.partial(project_body, early, late, line, far),
             [shape((length, wide), f32)] * 2 + [shape((length, len(late) * deep), bf16)] * 2,
-            [SMEM] + [VMEM] * (2 + len(early)),
+            [SMEM] + ([ANY] if far else [VMEM] * 2) + [VMEM] * len(early),
             flops=2 * 2 * length * len(early) * deep * wide,
-        )(here, *[books[s] for s in segs], *[halves[half][piece] for piece, half in early])
+            scratch=[pltpu.VMEM((2, length, width), bf16), pltpu.SemaphoreType.DMA((2,))] if far else (),
+        )(here, *([group_tokens] if far else books), *[halves[half][piece] for piece, half in early])
         for at, s in enumerate(segs):
             sums[s], lates[s] = found[at], found[2 + at]
 
@@ -348,11 +364,12 @@
         stage3 = lambda middle, two: (outward(middle), over(two))
 
         a = stack(0, *messages[:2])
+        messages.append(to_member(messages[2], 1))
+        a, b, sibling, own = locked(
+            a, stack(rows, *messages[2:]), to_member(tokens[0], 1), tokens[0]
+        )
+        group_tokens = gather_tokens(own)
         a_one, a_inner, a_far0 = locked(*stage1(a))
-        messages.append(to_member(after(messages[2], a_one), 1))
-        own = after(tokens[0], messages[2], a_one)
-        across = to_member(own, 2)
-        b, sibling = locked(stack(rows, *messages[2:]), to_member(own, 1))
         b_one, b_inner, b_far0 = locked(*stage1(b))
         a_middle, a_outer, a_far1 = locked(*stage2(a_one, a_inner))
         b_middle, b_outer, b_far1 = locked(*stage2(b_one, b_inner))
@@ -362,16 +379,13 @@
         b_last, b_far2 = stage3(b_middle, b_two)
         a_last, a_far2, a_middle, a_inner = locked(a_last, a_far2, a_middle, a_inner)
         a_three = jnp.where(inside, a_middle, a_last)
-        books = [own, sibling]
+        books = [tokens[0], sibling]
         upper = [a, a_one, a_two, None, a_far0, a_far1]
         lower = [b, b_one, b_two, None, b_far0, b_far1]
         early = [(k, half) for half in range(2) for k in (0, 1, 2, 4, 5)]
         late = [(3, 0), (6, 0), (3, 1), (6, 1), (7, 0), (7, 1)]
         project((0, 1), early, late, (upper, lower), n_z)
-        b_last, b_far2, b_middle, sums[0], sums[1], across = locked(
-            b_last, b_far2, b_middle, sums[0], sums[1], after(across, a_last, a_far2)
-        )
-        books += [across, to_member(across, 1)]
+        b_last, b_far2, b_middle, sums[0], sums[1] = locked(b_last, b_far2, b_middle, sums[0], sums[1])
         project((2, 3), early, late, (upper, lower), n_z)
         b_three = jnp.where(inside, b_middle, b_last)
         pieces = [a_three, a_far2, b_three, b_far2]
@@ -379,8 +393,8 @@
         inner = a_inner
         finish = lambda at: over(b_three[:, at])
     else:
-        across, sibling = to_member(tokens[0], 2), to_member(tokens[0], 1)
-        books = [tokens[0], sibling, across, to_member(across, 1)]
+        books = [tokens[0], to_member(tokens[0], 1)]
+        group_tokens = gather_tokens(tokens[0])
         messages.append(to_member(messages[2], 1))
         full = gathered(jnp.concatenate([stack(0, *messages[:2]), stack(rows, *messages[2:])], axis=0))
         deep = MEMBERS * HEAD_SIZE // 2
@@ -450,14 +464,12 @@
     for k, parts in ((1, (one0, one1)), (2, (two0, two1)), (3, (three0, three1))):
         sent += [to_member(part, k) for part in parts]
     far = sent[4:]
-    (there,) = call(
-        gate_body, [shape((4,), jnp.int32)], [SMEM] + [ANY] * len(far), out_spec=SMEM, moved=16 << 20
-    )(here, *far)
+    (gate,) = call(gate_body, [shape((8, HEAD_SIZE), f32)], [ANY] * len(far), moved=16 << 20)(*far)
     (output,) = call(
         functools.partial(assemble_body, (2,) * MEMBERS),
         [shape((length, w_query.shape[1]), bf16)],
-        [SMEM] + [VMEM] * len(sent),
-    )(there, *sent)
+        [SMEM] + [VMEM] * (1 + len(sent)),
+    )(here, gate, *sent)
     return output[None]
 
 

time: 117 us -> 154 us (1.32)
  local copies, waits for them, and re-layouts: 9.1 us -> 28.5 us
  between operations: 0.99 us -> 14.5 us
  waiting for transfers between devices: 29.7 us -> 33.7 us
    unnamed x30 -> x86, local copies, waits for them, and re-layouts: 9.04 us -> 26.2 us
    ppermute x35 -> x33, waiting for transfers between devices: 29.7 us -> 33.6 us  [permute(): return lax.ppermute(array, AXES, pairs)]
    ppermute x35 -> x33, starting transfers between devices: 49.8 us -> 48.8 us  [permute(): return lax.ppermute(array, AXES, pairs)]
  transfers between devices with their start and end apart: 35 -> 34, of which waited for: 12 -> 14; matrix products, arithmetic and copies ran while one was open for 3% -> 4% of each run, Pallas kernels for 18% -> 13%
where the time goes in v13:
time: 154 us; the launch traced here: 153 us
  starting transfers between devices  48.8 us (32%)
  waiting for transfers between devices  33.7 us (22%)
  local copies, waits for them, and re-layouts  28.5 us (19%)
  Pallas kernels  24.4 us (16%)
  between operations  14.5 us (9%)
  other arithmetic  3.27 us (2%)
    ppermute x33, starting transfers between devices, permute(): return lax.ppermute(array, AXES, pairs)  48.8 us
    ppermute x33, waiting for transfers between devices, permute(): return lax.ppermute(array, AXES, pairs)  33.6 us
    unnamed x86, local copies, waits for them, and re-layouts  26.2 us
    pallas_call x2, Pallas kernels, project(): call(functools.partial(project_body, early, late, line, far), [shape((len...  8.46 us
    pallas_call x3, Pallas kernels, local(): call(functools.partial(local_body, len(segs), len(late) + 1, halves[1 + p...  7.33 us
    pallas_call x3, Pallas kernels, mix(): call(functools.partial(mix_body, segs, parts, group), [shape((length, hal...  3.94 us
  transfers between devices with their start and end apart: 34, of which 14 were waited for; matrix products, arithmetic and copies ran while one was open for 4% of the time, Pallas kernels for 13%

profile of v13, /device:TPU:9, one launch (start us, length us, event | category | flops | bytes accessed | tf_op | source)
XLA Modules:
  0.0 153.1 jit_solution(15372582461576196318)
XLA Ops:
  8.0 1.0 copy-done.36
  9.0 0.9 copy-done.37
  9.9 0.9 copy-done.38
  12.1 1.3 collective-permute-start.1
  13.4 10.1 %collective-permute-done.1.upper_ref.refs_17_.refs_11_.refs_4_.refs_9_ = bf16[272,768]{1,0:T(8,128)(2,1)S(1)} collective-permute-done((bf16[272,768]{1,0:T(8,128)(2,1)S(1)}, bf16[272,768]{1,0:T(8,128)(2,1)S(1)}, u32[]{:S(2)}, u32[]{:S(2)}) %collective-permute-start.1) | collective-permute-done | bytes 417824 | tf_op jit(solution)/shard_map/ppermute | solution.py:296
  24.3 1.7 %collective-permute-done.lower_ref.refs_16_.refs_13_.refs_9_.refs_4_ = bf16[144,768]{1,0:T(8,128)(2,1)S(1)} collective-permute-done((bf16[144,768]{1,0:T(8,128)(2,1)S(1)}, bf16[144,768]{1,0:T(8,128)(2,1)S(1)}, u32[]{:S(2)}, u32[]{:S(2)}) %collective-permute-start) | collective-permute-done | bytes 221216 | tf_op jit(solution)/shard_map/ppermute | solution.py:296
  26.8 4.5 %collective-permute-start.14 = (bf16[256,768]{1,0:T(8,128)(2,1)S(1)}, bf16[256,768]{1,0:T(8,128)(2,1)}, u32[]{:S(2)}, u32[]{:S(2)}) collective-permute-start(bf16[256,768]{1,0:T(8,128)(2,1)S(1)} %shard_map.75.refs_7_.refs_6_), channel_id=1, source_target_pairs={{1,2},{2,1},{5,6},{6,5},{9,10},{10,9},{13,14},{14,13},{17,18},{18,... | collective-permute-start | bytes 1179656 | tf_op jit(solution)/shard_map/ppermute | solution.py:296
  31.3 1.3 collective-permute-start.15
  32.6 1.9 %collective-permute-start.5 = (bf16[256,768]{1,0:T(8,128)(2,1)S(1)}, bf16[256,768]{1,0:T(8,128)(2,1)}, u32[]{:S(2)}, u32[]{:S(2)}) collective-permute-start(bf16[256,768]{1,0:T(8,128)(2,1)S(1)} %shard_map.74.refs_2_.refs_1_), channel_id=1, source_target_pairs={{1,2},{2,1},{5,6},{6,5},{9,10},{10,9},{13,14},{14,13},{17,18},{18,... | collective-permute-start | bytes 1179656 | tf_op jit(solution)/shard_map/ppermute | solution.py:296
  34.5 2.7 %collective-permute-done.13.refs_8_.refs_7_ = bf16[256,768]{1,0:T(8,128)(2,1)S(1)} collective-permute-done((bf16[256,768]{1,0:T(8,128)(2,1)S(1)}, bf16[256,768]{1,0:T(8,128)(2,1)S(1)}, u32[]{:S(2)}, u32[]{:S(2)}) %collective-permute-start.13) | collective-permute-done | bytes 393248 | tf_op jit(solution)/shard_map/ppermute | solution.py:296
  37.2 1.2 collective-permute-start.6
  38.5 1.8 %collective-permute-done.14 = bf16[256,768]{1,0:T(8,128)(2,1)} collective-permute-done((bf16[256,768]{1,0:T(8,128)(2,1)S(1)}, bf16[256,768]{1,0:T(8,128)(2,1)}, u32[]{:S(2)}, u32[]{:S(2)}) %collective-permute-start.14) | collective-permute-done | bytes 393248 | tf_op jit(solution)/shard_map/ppermute | solution.py:296
  41.1 2.2 %collective-permute-start.16 = (bf16[256,768]{1,0:T(8,128)(2,1)S(1)}, bf16[256,768]{1,0:T(8,128)(2,1)S(1)}, u32[]{:S(2)}, u32[]{:S(2)}) collective-permute-start(bf16[256,768]{1,0:T(8,128)(2,1)S(1)} %collective-permute-done.13.refs_8_.refs_7_), channel_id=1, source_target_pairs={{1,2},{2,1},{5,6},{6,5},{9,10},{10,9},{13,14},{14,13},{17,18},{18,... | collective-permute-start | bytes 1179656 | tf_op jit(solution)/shard_map/ppermute | solution.py:296
  43.4 1.3 collective-permute-start.18
  44.7 1.0 collective-permute-done.4.refs_3_.refs_2_
  45.6 2.7 %collective-permute-start.17 = (bf16[256,768]{1,0:T(8,128)(2,1)}, bf16[256,768]{1,0:T(8,128)(2,1)}, u32[]{:S(2)}, u32[]{:S(2)}) collective-permute-start(bf16[256,768]{1,0:T(8,128)(2,1)} %collective-permute-done.14), channel_id=1, source_target_pairs={{1,0},{2,3},{5,4},{6,7},{9,8},{10,11},{13,12},{14,15},{17,16},{18,... | collective-permute-start | bytes 1179656 | tf_op jit(solution)/shard_map/ppermute | solution.py:296
  50.3 3.2 %collective-permute-start.7 = (bf16[256,768]{1,0:T(8,128)(2,1)S(1)}, bf16[256,768]{1,0:T(8,128)(2,1)}, u32[]{:S(2)}, u32[]{:S(2)}) collective-permute-start(bf16[256,768]{1,0:T(8,128)(2,1)S(1)} %collective-permute-done.4.refs_3_.refs_2_), channel_id=1, source_target_pairs={{1,2},{2,1},{5,6},{6,5},{9,10},{10,9},{13,14},{14,13},{17,18},{18,... | collective-permute-start | bytes 1179656 | tf_op jit(solution)/shard_map/ppermute | solution.py:296
  53.5 2.1 %collective-permute-start.8 = (bf16[256,768]{1,0:T(8,128)(2,1)}, bf16[256,768]{1,0:T(8,128)(2,1)}, u32[]{:S(2)}, u32[]{:S(2)}) collective-permute-start(bf16[256,768]{1,0:T(8,128)(2,1)} %collective-permute-done.5), channel_id=1, source_target_pairs={{1,0},{2,3},{5,4},{6,7},{9,8},{10,11},{13,12},{14,15},{17,16},{18,... | collective-permute-start | bytes 1179656 | tf_op jit(solution)/shard_map/ppermute | solution.py:296
  55.6 1.5 collective-permute-done.16
  57.8 1.2 collective-permute-start.9
  59.1 6.4 %collective-permute-done.7 = bf16[256,768]{1,0:T(8,128)(2,1)} collective-permute-done((bf16[256,768]{1,0:T(8,128)(2,1)S(1)}, bf16[256,768]{1,0:T(8,128)(2,1)}, u32[]{:S(2)}, u32[]{:S(2)}) %collective-permute-start.7) | collective-permute-done | bytes 393248 | tf_op jit(solution)/shard_map/ppermute | solution.py:296
  65.5 1.1 collective-permute-done.9.refs_6_.refs_5_
  67.4 1.0 broadcast_select_fusion.3.refs_4_.refs_3_
  68.5 1.3 collective-permute-start.11
  69.8 1.6 %collective-permute-start.10 = (bf16[256,768]{1,0:T(8,128)(2,1)}, bf16[256,768]{1,0:T(8,128)(2,1)S(1)}, u32[]{:S(2)}, u32[]{:S(2)}) collective-permute-start(bf16[256,768]{1,0:T(8,128)(2,1)} %collective-permute-done.7), channel_id=1, source_target_pairs={{1,0},{2,3},{5,4},{6,7},{9,8},{10,11},{13,12},{14,15},{17,16},{18,... | collective-permute-start | bytes 1179656 | tf_op jit(solution)/shard_map/ppermute | solution.py:296
  71.4 3.9 %collective-permute-start.12 = (bf16[256,768]{1,0:T(8,128)(2,1)}, bf16[256,768]{1,0:T(8,128)(2,1)S(1)}, u32[]{:S(2)}, u32[]{:S(2)}) collective-permute-start(bf16[256,768]{1,0:T(8,128)(2,1)} %copy-done.33), channel_id=1, source_target_pairs={{1,2},{2,1},{5,6},{6,5},{9,10},{10,9},{13,14},{14,13},{17,18},{18,... | collective-permute-start | bytes 1179656 | tf_op jit(solution)/shard_map/ppermute | solution.py:296
  75.4 1.1 broadcast_select_fusion.1.refs_9_.refs_8_
  76.7 1.3 collective-permute-start.19
  78.1 1.6 %copy-done.1 = bf16[1,256,4096]{2,1,0:T(8,128)(2,1)S(1)} copy-done((bf16[1,256,4096]{2,1,0:T(8,128)(2,1)S(1)}, bf16[1,256,4096]{2,1,0:T(8,128)(2,1)}, u32[]{:S(2)}) %copy-start.1) | copy-done | bytes 2097176
  79.7 1.0 copy-done.15
  80.6 1.0 copy-done.22
  81.6 1.0 copy-done.25
  82.6 1.0 copy-done.28
  83.6 1.0 copy-done.34
  84.6 4.3 %shard_map.76 = (f32[256,768]{1,0:T(8,128)S(1)}, f32[256,768]{1,0:T(8,128)S(1)}, bf16[256,1536]{1,0:T(8,128)(2,1)S(1)}, bf16[256,1536]{1,0:T(8,128)(2,1)S(1)}) custom-call(s32[4]{0:T(128)S(1)} %pad_add_fusion.here_ref, bf16[256,4096]{1,0:T(8,128)(2,1)S(1)} %bitcast.9, bf16[256,4096]{1,0:T(8,128)(2,1)} %collective-permute-done.3.refs_1_, ...), custom_call_target="tpu_custom_call" | custom-call | flops 2013265920 | bytes 4194304 | tf_op jit(solution)/shard_map/pallas_call | solution.py:339
  92.2 1.2 collective-permute-start.22
  93.4 1.9 %collective-permute-start.21 = (bf16[256,256]{1,0:T(8,128)(2,1)}, bf16[256,256]{1,0:T(8,128)(2,1)}, u32[]{:S(2)}, u32[]{:S(2)}) collective-permute-start(bf16[256,256]{1,0:T(8,128)(2,1)} %slice.15), channel_id=1, source_target_pairs={{1,0},{2,3},{5,4},{6,7},{9,8},{10,11},{13,12},{14,15},{17,16},{18,... | collective-permute-start | bytes 393224 | tf_op jit(solution)/shard_map/ppermute | solution.py:296
  95.6 2.0 %collective-permute-start.24 = (bf16[256,512]{1,0:T(8,128)(2,1)}, bf16[256,512]{1,0:T(8,128)(2,1)}, u32[]{:S(2)}, u32[]{:S(2)}) collective-permute-start(bf16[256,512]{1,0:T(8,128)(2,1)} %slice.17), channel_id=1, source_target_pairs={{1,0},{2,3},{5,4},{6,7},{9,8},{10,11},{13,12},{14,15},{17,16},{18,... | collective-permute-start | bytes 786440 | tf_op jit(solution)/shard_map/ppermute | solution.py:296
  97.6 1.2 collective-permute-start.27
  98.8 1.1 broadcast_select_fusion.2.refs_0_
  99.9 3.4 %copy-done = bf16[1024,4096]{1,0:T(8,128)(2,1)S(1)} copy-done((bf16[1024,4096]{1,0:T(8,128)(2,1)S(1)}, bf16[1024,4096]{1,0:T(8,128)(2,1)}, u32[]{:S(2)}) %copy-start) | copy-done | bytes 8388632
  103.3 1.0 copy-done.13
  104.3 1.0 copy-done.16
  105.3 1.0 copy-done.18
  106.3 1.0 copy-done.20
  107.3 1.0 copy-done.23
  108.3 1.0 copy-done.26
  109.3 1.0 copy-done.29
  110.3 1.0 copy-done.32
  111.3 1.0 copy-done.35
  112.3 4.1 %shard_map.77 = (f32[256,768]{1,0:T(8,128)S(1)}, f32[256,768]{1,0:T(8,128)S(1)}, bf16[256,1536]{1,0:T(8,128)(2,1)S(1)}, bf16[256,1536]{1,0:T(8,128)(2,1)S(1)}) custom-call(s32[4]{0:T(128)S(1)} %pad_add_fusion.here_ref, bf16[4,256,4096]{2,1,0:T(8,128)(2,1)S(1)} %bitcast.6, bf16[256,768]{1,0:T(8,128)(2,1)S(1)} %copy-done.13, bf16[256,768]{1,0:T(8,128)(2,1)S(1)} %copy-done.29, ...), custom_call_target="tpu_custom_call" | custom-call | flops 2013265920 | bytes 4194304 | tf_op jit(solution)/shard_map/pallas_call | solution.py:339
  116.5 2.3 %shard_map.78 = (bf16[256,256]{1,0:T(8,128)(2,1)S(1)}, f32[128,256]{1,0:T(8,128)S(1)}, bf16[256,256]{1,0:T(8,128)(2,1)S(1)}, f32[128,256]{1,0:T(8,128)S(1)}, bf1...) custom-call(s32[4]{0:T(128)S(1)} %pad_add_fusion.here_ref, ...), custom_call_target="tpu_custom_call" | custom-call | flops 805306368 | bytes 4194304 | tf_op jit(solution)/shard_map/pallas_call | solution.py:415
  119.1 2.9 %shard_map.79 = (bf16[256,256]{1,0:T(8,128)(2,1)S(1)}, f32[256,256]{1,0:T(8,128)S(1)}, bf16[256,256]{1,0:T(8,128)(2,1)S(1)}, f32[256,256]{1,0:T(8,128)S(1)}, bf1...) custom-call(s32[4]{0:T(128)S(1)} %pad_add_fusion.here_ref, ...), custom_call_target="tpu_custom_call" | custom-call | flops 268435456 | bytes 4194304 | tf_op jit(solution)/shard_map/pallas_call | solution.py:435
  122.0 1.2 shard_map.80
  123.2 2.3 %shard_map.81 = (bf16[256,256]{1,0:T(8,128)(2,1)S(1)}, f32[256,256]{1,0:T(8,128)S(1)}, bf16[256,256]{1,0:T(8,128)(2,1)S(1)}, f32[256,256]{1,0:T(8,128)S(1)}) custom-call(s32[4]{0:T(128)S(1)} %pad_add_fusion.here_ref, bf16[256,768]{1,0:T(8,128)(2,1)S(1)} %broadcast_select_fusion.2.refs_0_, bf16[256,768]{1,0:T(8,128)(2,1)S(1)} %collective-permute-done.11.refs_1_, ...), custom_call_target="tpu_custom_call" | custom-call | flops 134217728 | bytes 4194304 | tf_op jit(solution)/shard_map/pallas_call | solution.py:435
  125.5 1.2 shard_map.82
  126.7 1.3 collective-permute-start.28
  128.1 5.5 %collective-permute-start.30 = (bf16[256,256]{1,0:T(8,128)(2,1)S(1)}, bf16[256,256]{1,0:T(8,128)(2,1)S(1)}, u32[]{:S(2)}, u32[]{:S(2)}) collective-permute-start(bf16[256,256]{1,0:T(8,128)(2,1)S(1)} %get-tuple-element.136), channel_id=1, source_target_pairs={{0,12},{1,13},{2,14},{3,15},{4,8},{5,9},{6,10},{7,11},{8,4},{9,5},... | collective-permute-start | bytes 393224 | tf_op jit(solution)/shard_map/ppermute | solution.py:296
  133.5 1.2 collective-permute-start.26
  135.0 2.1 %shard_map.84 = (bf16[256,256]{1,0:T(8,128)(2,1)S(1)}, f32[256,256]{1,0:T(8,128)S(1)}, bf16[256,256]{1,0:T(8,128)(2,1)S(1)}, f32[256,256]{1,0:T(8,128)S(1)}) custom-call(s32[4]{0:T(128)S(1)} %pad_add_fusion.here_ref, bf16[256,768]{1,0:T(8,128)(2,1)S(1)} %broadcast_select_fusion.2.refs_0_, bf16[256,768]{1,0:T(8,128)(2,1)S(1)} %collective-permute-done.11.refs_1_, ...), custom_call_target="tpu_custom_call" | custom-call | flops 134217728 | bytes 4194304 | tf_op jit(solution)/shard_map/pallas_call | solution.py:435
  137.2 1.6 %shard_map.85 = (bf16[256,256]{1,0:T(8,128)(2,1)S(1)}, bf16[256,256]{1,0:T(8,128)(2,1)S(1)}, bf16[256,256]{1,0:T(8,128)(2,1)S(1)}, bf16[256,256]{1,0:T(8,128)(2,1)S(1)}) custom-call(s32[4]{0:T(128)S(1)} %pad_add_fusion.here_ref, f32[16]{0:T(128)S(1)} %copy-done.39, bf16[128,256]{1,0:T(8,128)(2,1)S(1)} %collective-permute-done.23.base_ref, ...), custom_call_target="tpu_custom_call" | custom-call | flops 402653184 | bytes 4194304 | tf_op jit(solution)/shard_map/pallas_call | solution.py:446
  139.5 2.0 %collective-permute-done.26.refs_0_.refs_5_ = bf16[256,256]{1,0:T(8,128)(2,1)S(1)} collective-permute-done((bf16[256,256]{1,0:T(8,128)(2,1)S(1)}, bf16[256,256]{1,0:T(8,128)(2,1)S(1)}, u32[]{:S(2)}, u32[]{:S(2)}) %collective-permute-start.26) | collective-permute-done | bytes 131104 | tf_op jit(solution)/shard_map/ppermute | solution.py:296
  141.5 3.1 %collective-permute-done.29.refs_2_.refs_7_ = bf16[256,256]{1,0:T(8,128)(2,1)S(1)} collective-permute-done((bf16[256,256]{1,0:T(8,128)(2,1)S(1)}, bf16[256,256]{1,0:T(8,128)(2,1)S(1)}, u32[]{:S(2)}, u32[]{:S(2)}) %collective-permute-start.29) | collective-permute-done | bytes 131104 | tf_op jit(solution)/shard_map/ppermute | solution.py:296
  144.6 1.6 %shard_map.86 = bf16[256,2048]{1,0:T(8,128)(2,1)} custom-call(s32[4]{0:T(128)S(1)} %pad_add_fusion.here_ref, f32[8,128]{1,0:T(8,128)S(1)} %shard_map.83.refs_0_, bf16[256,256]{1,0:T(8,128)(2,1)S(1)} %get-tuple-element.147.refs_1_, bf16[256,256]{1,0:T(8,128)(2,1)S(1)} %get-tuple-element.148.refs_2_, bf16[256,256]{1,0:T(8,128)(2,1)S(1)} %collective-permute-done.31.refs_3_, ...), custom_call_target="tpu_custom_call" | custom-call | bytes 4194304 | tf_op jit(solution)/shard_map/pallas_call | solution.py:468
  (113 shorter events, 13.2 us)
Async XLA Ops:
  6.5 93.4 %all-gather.3.cloned.1.call-start = ((), (), s32[]{:S(2)}) async-start(), calls=%async_computation | async-start | bytes 10485760 | tf_op jit(solution)/shard_map/all_gather | solution.py:325
  6.5 20.1 %collective-permute-start.3 = (bf16[256,4096]{1,0:T(8,128)(2,1)}, bf16[256,4096]{1,0:T(8,128)(2,1)}, u32[]{:S(2)}, u32[]{:S(2)}) collective-permute-start(bf16[256,4096]{1,0:T(8,128)(2,1)} %bitcast.7), channel_id=1, source_target_pairs={{0,4},{1,5},{2,6},{3,7},{4,0},{5,1},{6,2},{7,3},{8,12},{9,13},{10,... | collective-permute-start | bytes 6291464 | tf_op jit(solution)/shard_map/ppermute | solution.py:296
  7.9 1.0 copy-start.36
  12.1 11.3 %collective-permute-start.1 = (bf16[272,768]{1,0:T(8,128)(2,1)S(1)}, bf16[272,768]{1,0:T(8,128)(2,1)S(1)}, u32[]{:S(2)}, u32[]{:S(2)}) collective-permute-start(bf16[272,768]{1,0:T(8,128)(2,1)S(1)} %get-tuple-element.80), channel_id=1, source_target_pairs={{0,8},{1,9},{2,10},{3,11},{4,12},{5,13},{6,14},{7,15},{8,0},{9,1},... | collective-permute-start | bytes 1253384 | tf_op jit(solution)/shard_map/ppermute | solution.py:296
  23.5 2.5 %collective-permute-start.2 = (bf16[272,768]{1,0:T(8,128)(2,1)S(1)}, bf16[272,768]{1,0:T(8,128)(2,1)S(1)}, u32[]{:S(2)}, u32[]{:S(2)}) collective-permute-start(bf16[272,768]{1,0:T(8,128)(2,1)S(1)} %collective-permute-done.1.upper_ref.refs_17_.refs_11_.refs_4_.refs_9_), channel_id=1, source_target_pairs={{0,4},{1,5},{2,6},{3,7},{4,0},{5,1},{6,2},{7,3},{8,12},{9,13},{10,... | collective-permute-start | bytes 1253384 | tf_op jit(solution)/shard_map/ppermute | solution.py:296
  24.2 1.7 %collective-permute-start = (bf16[144,768]{1,0:T(8,128)(2,1)S(1)}, bf16[144,768]{1,0:T(8,128)(2,1)S(1)}, u32[]{:S(2)}, u32[]{:S(2)}) collective-permute-start(bf16[144,768]{1,0:T(8,128)(2,1)S(1)} %get-tuple-element.79), channel_id=1, source_target_pairs={{0,4},{1,5},{2,6},{3,7},{4,0},{5,1},{6,2},{7,3},{8,12},{9,13},{10,... | collective-permute-start | bytes 663560 | tf_op jit(solution)/shard_map/ppermute | solution.py:296
  26.0 52.1 %copy-start.12 = (bf16[256,768]{1,0:T(8,128)(2,1)}, bf16[256,768]{1,0:T(8,128)(2,1)S(1)}, u32[]{:S(2)}) copy-start(bf16[256,768]{1,0:T(8,128)(2,1)S(1)} %shard_map.74.refs_2_.refs_1_) | copy-start | bytes 1179652
  26.7 48.7 %copy-start.14 = (bf16[256,768]{1,0:T(8,128)(2,1)}, bf16[256,768]{1,0:T(8,128)(2,1)S(1)}, u32[]{:S(2)}) copy-start(bf16[256,768]{1,0:T(8,128)(2,1)S(1)} %shard_map.75.refs_7_.refs_6_) | copy-start | bytes 1179652
  26.7 10.5 %collective-permute-start.13 = (bf16[256,768]{1,0:T(8,128)(2,1)S(1)}, bf16[256,768]{1,0:T(8,128)(2,1)S(1)}, u32[]{:S(2)}, u32[]{:S(2)}) collective-permute-start(bf16[256,768]{1,0:T(8,128)(2,1)S(1)} %shard_map.75.refs_7_.refs_6_), channel_id=1, source_target_pairs={{0,1},{1,0},{2,3},{3,2},{4,5},{5,4},{6,7},{7,6},{8,9},{9,8},{10,11... | collective-permute-start | bytes 1179656 | tf_op jit(solution)/shard_map/ppermute | solution.py:296
  26.8 13.4 %collective-permute-start.14 = (bf16[256,768]{1,0:T(8,128)(2,1)S(1)}, bf16[256,768]{1,0:T(8,128)(2,1)}, u32[]{:S(2)}, u32[]{:S(2)}) collective-permute-start(bf16[256,768]{1,0:T(8,128)(2,1)S(1)} %shard_map.75.refs_7_.refs_6_), channel_id=1, source_target_pairs={{1,2},{2,1},{5,6},{6,5},{9,10},{10,9},{13,14},{14,13},{17,18},{18,... | collective-permute-start | bytes 1179656 | tf_op jit(solution)/shard_map/ppermute | solution.py:296
  31.3 9.9 %collective-permute-start.15 = (bf16[256,768]{1,0:T(8,128)(2,1)S(1)}, bf16[256,768]{1,0:T(8,128)(2,1)S(1)}, u32[]{:S(2)}, u32[]{:S(2)}) collective-permute-start(bf16[256,768]{1,0:T(8,128)(2,1)S(1)} %shard_map.75.refs_7_.refs_6_), channel_id=1, source_target_pairs={{0,16},{1,17},{2,18},{3,19},{4,20},{5,21},{6,22},{7,23},{8,24},{9,... | collective-permute-start | bytes 1179656 | tf_op jit(solution)/shard_map/ppermute | solution.py:296
  32.6 13.1 %collective-permute-start.4 = (bf16[256,768]{1,0:T(8,128)(2,1)S(1)}, bf16[256,768]{1,0:T(8,128)(2,1)S(1)}, u32[]{:S(2)}, u32[]{:S(2)}) collective-permute-start(bf16[256,768]{1,0:T(8,128)(2,1)S(1)} %shard_map.74.refs_2_.refs_1_), channel_id=1, source_target_pairs={{0,1},{1,0},{2,3},{3,2},{4,5},{5,4},{6,7},{7,6},{8,9},{9,8},{10,11... | collective-permute-start | bytes 1179656 | tf_op jit(solution)/shard_map/ppermute | solution.py:296
  32.6 16.1 %collective-permute-start.5 = (bf16[256,768]{1,0:T(8,128)(2,1)S(1)}, bf16[256,768]{1,0:T(8,128)(2,1)}, u32[]{:S(2)}, u32[]{:S(2)}) collective-permute-start(bf16[256,768]{1,0:T(8,128)(2,1)S(1)} %shard_map.74.refs_2_.refs_1_), channel_id=1, source_target_pairs={{1,2},{2,1},{5,6},{6,5},{9,10},{10,9},{13,14},{14,13},{17,18},{18,... | collective-permute-start | bytes 1179656 | tf_op jit(solution)/shard_map/ppermute | solution.py:296
  37.2 32.6 %copy-start.21 = (bf16[256,768]{1,0:T(8,128)(2,1)}, bf16[256,768]{1,0:T(8,128)(2,1)S(1)}, u32[]{:S(2)}) copy-start(bf16[256,768]{1,0:T(8,128)(2,1)S(1)} %collective-permute-done.13.refs_8_.refs_7_) | copy-start | bytes 1179652
  37.2 12.3 %collective-permute-start.6 = (bf16[256,768]{1,0:T(8,128)(2,1)S(1)}, bf16[256,768]{1,0:T(8,128)(2,1)S(1)}, u32[]{:S(2)}, u32[]{:S(2)}) collective-permute-start(bf16[256,768]{1,0:T(8,128)(2,1)S(1)} %shard_map.74.refs_2_.refs_1_), channel_id=1, source_target_pairs={{0,16},{1,17},{2,18},{3,19},{4,20},{5,21},{6,22},{7,23},{8,24},{9,... | collective-permute-start | bytes 1179656 | tf_op jit(solution)/shard_map/ppermute | solution.py:296
  41.1 35.6 %copy-start.24 = (bf16[256,768]{1,0:T(8,128)(2,1)}, bf16[256,768]{1,0:T(8,128)(2,1)S(1)}, u32[]{:S(2)}) copy-start(bf16[256,768]{1,0:T(8,128)(2,1)S(1)} %collective-permute-done.15.refs_10_.refs_9_) | copy-start | bytes 1179652
  41.1 16.0 %collective-permute-start.16 = (bf16[256,768]{1,0:T(8,128)(2,1)S(1)}, bf16[256,768]{1,0:T(8,128)(2,1)S(1)}, u32[]{:S(2)}, u32[]{:S(2)}) collective-permute-start(bf16[256,768]{1,0:T(8,128)(2,1)S(1)} %collective-permute-done.13.refs_8_.refs_7_), channel_id=1, source_target_pairs={{1,2},{2,1},{5,6},{6,5},{9,10},{10,9},{13,14},{14,13},{17,18},{18,... | collective-permute-start | bytes 1179656 | tf_op jit(solution)/shard_map/ppermute | solution.py:296
  43.4 15.7 %collective-permute-start.18 = (bf16[256,768]{1,0:T(8,128)(2,1)S(1)}, bf16[256,768]{1,0:T(8,128)(2,1)}, u32[]{:S(2)}, u32[]{:S(2)}) collective-permute-start(bf16[256,768]{1,0:T(8,128)(2,1)S(1)} %collective-permute-done.13.refs_8_.refs_7_), channel_id=1, source_target_pairs={{0,16},{1,17},{2,18},{3,19},{4,20},{5,21},{6,22},{7,23},{8,24},{9,... | collective-permute-start | bytes 1179656 | tf_op jit(solution)/shard_map/ppermute | solution.py:296
  45.6 31.1 %copy-start.27 = (bf16[256,768]{1,0:T(8,128)(2,1)}, bf16[256,768]{1,0:T(8,128)(2,1)S(1)}, u32[]{:S(2)}) copy-start(bf16[256,768]{1,0:T(8,128)(2,1)S(1)} %collective-permute-done.4.refs_3_.refs_2_) | copy-start | bytes 1179652
  45.6 13.4 %collective-permute-start.17 = (bf16[256,768]{1,0:T(8,128)(2,1)}, bf16[256,768]{1,0:T(8,128)(2,1)}, u32[]{:S(2)}, u32[]{:S(2)}) collective-permute-start(bf16[256,768]{1,0:T(8,128)(2,1)} %collective-permute-done.14), channel_id=1, source_target_pairs={{1,0},{2,3},{5,4},{6,7},{9,8},{10,11},{13,12},{14,15},{17,16},{18,... | collective-permute-start | bytes 1179656 | tf_op jit(solution)/shard_map/ppermute | solution.py:296
  50.3 15.2 %collective-permute-start.7 = (bf16[256,768]{1,0:T(8,128)(2,1)S(1)}, bf16[256,768]{1,0:T(8,128)(2,1)}, u32[]{:S(2)}, u32[]{:S(2)}) collective-permute-start(bf16[256,768]{1,0:T(8,128)(2,1)S(1)} %collective-permute-done.4.refs_3_.refs_2_), channel_id=1, source_target_pairs={{1,2},{2,1},{5,6},{6,5},{9,10},{10,9},{13,14},{14,13},{17,18},{18,... | collective-permute-start | bytes 1179656 | tf_op jit(solution)/shard_map/ppermute | solution.py:296
  53.5 12.0 %collective-permute-start.8 = (bf16[256,768]{1,0:T(8,128)(2,1)}, bf16[256,768]{1,0:T(8,128)(2,1)}, u32[]{:S(2)}, u32[]{:S(2)}) collective-permute-start(bf16[256,768]{1,0:T(8,128)(2,1)} %collective-permute-done.5), channel_id=1, source_target_pairs={{1,0},{2,3},{5,4},{6,7},{9,8},{10,11},{13,12},{14,15},{17,16},{18,... | collective-permute-start | bytes 1179656 | tf_op jit(solution)/shard_map/ppermute | solution.py:296
  57.8 8.8 %collective-permute-start.9 = (bf16[256,768]{1,0:T(8,128)(2,1)S(1)}, bf16[256,768]{1,0:T(8,128)(2,1)S(1)}, u32[]{:S(2)}, u32[]{:S(2)}) collective-permute-start(bf16[256,768]{1,0:T(8,128)(2,1)S(1)} %collective-permute-done.4.refs_3_.refs_2_), channel_id=1, source_target_pairs={{0,16},{1,17},{2,18},{3,19},{4,20},{5,21},{6,22},{7,23},{8,24},{9,... | collective-permute-start | bytes 1179656 | tf_op jit(solution)/shard_map/ppermute | solution.py:296
  59.1 17.6 %copy-start.42 = (bf16[256,768]{1,0:T(8,128)(2,1)S(1)}, bf16[256,768]{1,0:T(8,128)(2,1)}, u32[]{:S(2)}) copy-start(bf16[256,768]{1,0:T(8,128)(2,1)} %copy-done.41) | copy-start | bytes 1179652
  59.1 19.0 %copy-start.31 = (bf16[256,768]{1,0:T(8,128)(2,1)S(1)}, bf16[256,768]{1,0:T(8,128)(2,1)}, u32[]{:S(2)}) copy-start(bf16[256,768]{1,0:T(8,128)(2,1)} %copy-done.30) | copy-start | bytes 1179652
  68.5 20.5 %copy-start.17 = (bf16[256,768]{1,0:T(8,128)(2,1)}, bf16[256,768]{1,0:T(8,128)(2,1)S(1)}, u32[]{:S(2)}) copy-start(bf16[256,768]{1,0:T(8,128)(2,1)S(1)} %broadcast_select_fusion.3.refs_4_.refs_3_) | copy-start | bytes 1179652
  68.5 20.6 %collective-permute-start.11 = (bf16[256,768]{1,0:T(8,128)(2,1)S(1)}, bf16[256,768]{1,0:T(8,128)(2,1)S(1)}, u32[]{:S(2)}, u32[]{:S(2)}) collective-permute-start(bf16[256,768]{1,0:T(8,128)(2,1)S(1)} %broadcast_select_fusion.3.refs_4_.refs_3_), channel_id=1, source_target_pairs={{0,16},{1,17},{2,18},{3,19},{4,20},{5,21},{6,22},{7,23},{8,24},{9,... | collective-permute-start | bytes 1179656 | tf_op jit(solution)/shard_map/ppermute | solution.py:296
  69.8 19.3 %collective-permute-start.10 = (bf16[256,768]{1,0:T(8,128)(2,1)}, bf16[256,768]{1,0:T(8,128)(2,1)S(1)}, u32[]{:S(2)}, u32[]{:S(2)}) collective-permute-start(bf16[256,768]{1,0:T(8,128)(2,1)} %collective-permute-done.7), channel_id=1, source_target_pairs={{1,0},{2,3},{5,4},{6,7},{9,8},{10,11},{13,12},{14,15},{17,16},{18,... | collective-permute-start | bytes 1179656 | tf_op jit(solution)/shard_map/ppermute | solution.py:296
  71.4 17.7 %collective-permute-start.12 = (bf16[256,768]{1,0:T(8,128)(2,1)}, bf16[256,768]{1,0:T(8,128)(2,1)S(1)}, u32[]{:S(2)}, u32[]{:S(2)}) collective-permute-start(bf16[256,768]{1,0:T(8,128)(2,1)} %copy-done.33), channel_id=1, source_target_pairs={{1,2},{2,1},{5,6},{6,5},{9,10},{10,9},{13,14},{14,13},{17,18},{18,... | collective-permute-start | bytes 1179656 | tf_op jit(solution)/shard_map/ppermute | solution.py:296
  76.4 12.6 %copy-start.19 = (bf16[256,768]{1,0:T(8,128)(2,1)}, bf16[256,768]{1,0:T(8,128)(2,1)S(1)}, u32[]{:S(2)}) copy-start(bf16[256,768]{1,0:T(8,128)(2,1)S(1)} %broadcast_select_fusion.1.refs_9_.refs_8_) | copy-start | bytes 1179652
  76.4 14.2 %collective-permute-start.20 = (bf16[256,768]{1,0:T(8,128)(2,1)S(1)}, bf16[256,768]{1,0:T(8,128)(2,1)S(1)}, u32[]{:S(2)}, u32[]{:S(2)}) collective-permute-start(bf16[256,768]{1,0:T(8,128)(2,1)S(1)} %broadcast_select_fusion.1.refs_9_.refs_8_), channel_id=1, source_target_pairs={{0,16},{1,17},{2,18},{3,19},{4,20},{5,21},{6,22},{7,23},{8,24},{9,... | collective-permute-start | bytes 1179656 | tf_op jit(solution)/shard_map/ppermute | solution.py:296
  76.7 14.6 %collective-permute-start.19 = (bf16[256,768]{1,0:T(8,128)(2,1)S(1)}, bf16[256,768]{1,0:T(8,128)(2,1)S(1)}, u32[]{:S(2)}, u32[]{:S(2)}) collective-permute-start(bf16[256,768]{1,0:T(8,128)(2,1)S(1)} %copy-done.42), channel_id=1, source_target_pairs={{1,0},{2,3},{5,4},{6,7},{9,8},{10,11},{13,12},{14,15},{17,16},{18,... | collective-permute-start | bytes 1179656 | tf_op jit(solution)/shard_map/ppermute | solution.py:296
  78.1 1.6 %copy-start.1 = (bf16[1,256,4096]{2,1,0:T(8,128)(2,1)S(1)}, bf16[1,256,4096]{2,1,0:T(8,128)(2,1)}, u32[]{:S(2)}) copy-start(bf16[1,256,4096]{2,1,0:T(8,128)(2,1)} %param.7) | copy-start | bytes 6291460
  79.7 1.0 copy-start.15
  80.6 1.0 copy-start.22
  81.6 1.0 copy-start.25
  83.6 1.0 copy-start.34
  89.0 8.6 %copy-start.2 = (f32[256,768]{1,0:T(8,128)}, f32[256,768]{1,0:T(8,128)S(1)}, u32[]{:S(2)}) copy-start(f32[256,768]{1,0:T(8,128)S(1)} %get-tuple-element.106.refs_8_.refs_17_.refs_11_) | copy-start | bytes 2359300
  89.0 9.8 %copy-start.4 = (bf16[256,1536]{1,0:T(8,128)(2,1)}, bf16[256,1536]{1,0:T(8,128)(2,1)S(1)}, u32[]{:S(2)}) copy-start(bf16[256,1536]{1,0:T(8,128)(2,1)S(1)} %get-tuple-element.110.refs_11_.refs_22_.refs_14_) | copy-start | bytes 2359300
  89.0 9.8 %copy-start.6 = (bf16[256,1536]{1,0:T(8,128)(2,1)}, bf16[256,1536]{1,0:T(8,128)(2,1)S(1)}, u32[]{:S(2)}) copy-start(bf16[256,1536]{1,0:T(8,128)(2,1)S(1)} %get-tuple-element.111.refs_12_.refs_21_.refs_13_) | copy-start | bytes 2359300
  92.2 24.2 %collective-permute-start.22 = (bf16[256,256]{1,0:T(8,128)(2,1)}, bf16[256,256]{1,0:T(8,128)(2,1)}, u32[]{:S(2)}, u32[]{:S(2)}) collective-permute-start(bf16[256,256]{1,0:T(8,128)(2,1)} %get-tuple-element.153), channel_id=1, source_target_pairs={{0,16},{1,17},{2,18},{3,19},{4,20},{5,21},{6,22},{7,23},{8,24},{9,... | collective-permute-start | bytes 393224 | tf_op jit(solution)/shard_map/ppermute | solution.py:296
  93.4 23.0 %collective-permute-start.21 = (bf16[256,256]{1,0:T(8,128)(2,1)}, bf16[256,256]{1,0:T(8,128)(2,1)}, u32[]{:S(2)}, u32[]{:S(2)}) collective-permute-start(bf16[256,256]{1,0:T(8,128)(2,1)} %slice.15), channel_id=1, source_target_pairs={{1,0},{2,3},{5,4},{6,7},{9,8},{10,11},{13,12},{14,15},{17,16},{18,... | collective-permute-start | bytes 393224 | tf_op jit(solution)/shard_map/ppermute | solution.py:296
  95.3 23.8 %collective-permute-start.25 = (bf16[256,256]{1,0:T(8,128)(2,1)}, bf16[256,256]{1,0:T(8,128)(2,1)}, u32[]{:S(2)}, u32[]{:S(2)}) collective-permute-start(bf16[256,256]{1,0:T(8,128)(2,1)} %get-tuple-element.152), channel_id=1, source_target_pairs={{0,16},{1,17},{2,18},{3,19},{4,20},{5,21},{6,22},{7,23},{8,24},{9,... | collective-permute-start | bytes 393224 | tf_op jit(solution)/shard_map/ppermute | solution.py:296
  95.6 23.6 %collective-permute-start.24 = (bf16[256,512]{1,0:T(8,128)(2,1)}, bf16[256,512]{1,0:T(8,128)(2,1)}, u32[]{:S(2)}, u32[]{:S(2)}) collective-permute-start(bf16[256,512]{1,0:T(8,128)(2,1)} %slice.17), channel_id=1, source_target_pairs={{1,0},{2,3},{5,4},{6,7},{9,8},{10,11},{13,12},{14,15},{17,16},{18,... | collective-permute-start | bytes 786440 | tf_op jit(solution)/shard_map/ppermute | solution.py:296
  97.6 25.6 %collective-permute-start.27 = (bf16[256,256]{1,0:T(8,128)(2,1)}, bf16[256,256]{1,0:T(8,128)(2,1)S(1)}, u32[]{:S(2)}, u32[]{:S(2)}) collective-permute-start(bf16[256,256]{1,0:T(8,128)(2,1)} %get-tuple-element.151), channel_id=1, source_target_pairs={{0,16},{1,17},{2,18},{3,19},{4,20},{5,21},{6,22},{7,23},{8,24},{9,... | collective-permute-start | bytes 393224 | tf_op jit(solution)/shard_map/ppermute | solution.py:296
  99.9 3.4 %copy-start = (bf16[1024,4096]{1,0:T(8,128)(2,1)S(1)}, bf16[1024,4096]{1,0:T(8,128)(2,1)}, u32[]{:S(2)}) copy-start(bf16[1024,4096]{1,0:T(8,128)(2,1)} %all-gather.3.cloned.1.call-done) | copy-start | bytes 25165828
  105.3 1.0 copy-start.18
  106.3 1.0 copy-start.20
  107.3 1.0 copy-start.23
  110.3 1.0 copy-start.32
  111.3 1.0 copy-start.35
  112.3 4.2 %copy-start.3 = (f32[256,768]{1,0:T(8,128)S(1)}, f32[256,768]{1,0:T(8,128)}, u32[]{:S(2)}) copy-start(f32[256,768]{1,0:T(8,128)} %copy-done.2) | copy-start | bytes 2359300
  112.3 4.2 %copy-start.5 = (bf16[256,1536]{1,0:T(8,128)(2,1)S(1)}, bf16[256,1536]{1,0:T(8,128)(2,1)}, u32[]{:S(2)}) copy-start(bf16[256,1536]{1,0:T(8,128)(2,1)} %copy-done.4) | copy-start | bytes 2359300
  112.3 4.2 %copy-start.7 = (bf16[256,1536]{1,0:T(8,128)(2,1)S(1)}, bf16[256,1536]{1,0:T(8,128)(2,1)}, u32[]{:S(2)}) copy-start(bf16[256,1536]{1,0:T(8,128)(2,1)} %copy-done.6) | copy-start | bytes 2359300
  112.3 4.2 %copy-start.9 = (bf16[256,768]{1,0:T(8,128)(2,1)S(1)}, bf16[256,768]{1,0:T(8,128)(2,1)}, u32[]{:S(2)}) copy-start(bf16[256,768]{1,0:T(8,128)(2,1)} %copy-done.8) | copy-start | bytes 1179652
  112.3 4.2 %copy-start.11 = (bf16[144,768]{1,0:T(8,128)(2,1)S(1)}, bf16[144,768]{1,0:T(8,128)(2,1)}, u32[]{:S(2)}) copy-start(bf16[144,768]{1,0:T(8,128)(2,1)} %copy-done.10) | copy-start | bytes 663556
  118.8 3.2 %collective-permute-start.23 = (bf16[128,256]{1,0:T(8,128)(2,1)S(1)}, bf16[128,256]{1,0:T(8,128)(2,1)S(1)}, u32[]{:S(2)}, u32[]{:S(2)}) collective-permute-start(bf16[128,256]{1,0:T(8,128)(2,1)S(1)} %get-tuple-element.114), channel_id=1, source_target_pairs={{0,16},{1,17},{2,18},{3,19},{4,20},{5,21},{6,22},{7,23},{8,24},{9,... | collective-permute-start | bytes 196616 | tf_op jit(solution)/shard_map/ppermute | solution.py:296
  119.1 2.9 %copy-start.39 = (f32[16]{0:T(128)S(1)}, f32[16]{0:T(128)}, u32[]{:S(2)}) copy-start(f32[16]{0:T(128)} %gate_ref.5) | copy-start | bytes 196
  126.7 12.5 %collective-permute-start.28 = (bf16[256,256]{1,0:T(8,128)(2,1)S(1)}, bf16[256,256]{1,0:T(8,128)(2,1)S(1)}, u32[]{:S(2)}, u32[]{:S(2)}) collective-permute-start(bf16[256,256]{1,0:T(8,128)(2,1)S(1)} %get-tuple-element.135), channel_id=1, source_target_pairs={{0,8},{1,9},{2,10},{3,11},{4,12},{5,13},{6,14},{7,15},{8,0},{9,1},... | collective-permute-start | bytes 393224 | tf_op jit(solution)/shard_map/ppermute | solution.py:296
  128.1 11.5 %collective-permute-start.30 = (bf16[256,256]{1,0:T(8,128)(2,1)S(1)}, bf16[256,256]{1,0:T(8,128)(2,1)S(1)}, u32[]{:S(2)}, u32[]{:S(2)}) collective-permute-start(bf16[256,256]{1,0:T(8,128)(2,1)S(1)} %get-tuple-element.136), channel_id=1, source_target_pairs={{0,12},{1,13},{2,14},{3,15},{4,8},{5,9},{6,10},{7,11},{8,4},{9,5},... | collective-permute-start | bytes 393224 | tf_op jit(solution)/shard_map/ppermute | solution.py:296
  133.5 8.0 %collective-permute-start.26 = (bf16[256,256]{1,0:T(8,128)(2,1)S(1)}, bf16[256,256]{1,0:T(8,128)(2,1)S(1)}, u32[]{:S(2)}, u32[]{:S(2)}) collective-permute-start(bf16[256,256]{1,0:T(8,128)(2,1)S(1)} %get-tuple-element.128), channel_id=1, source_target_pairs={{0,8},{1,9},{2,10},{3,11},{4,12},{5,13},{6,14},{7,15},{8,0},{9,1},... | collective-permute-start | bytes 393224 | tf_op jit(solution)/shard_map/ppermute | solution.py:296
  134.7 9.9 %collective-permute-start.29 = (bf16[256,256]{1,0:T(8,128)(2,1)S(1)}, bf16[256,256]{1,0:T(8,128)(2,1)S(1)}, u32[]{:S(2)}, u32[]{:S(2)}) collective-permute-start(bf16[256,256]{1,0:T(8,128)(2,1)S(1)} %get-tuple-element.129), channel_id=1, source_target_pairs={{0,12},{1,13},{2,14},{3,15},{4,8},{5,9},{6,10},{7,11},{8,4},{9,5},... | collective-permute-start | bytes 393224 | tf_op jit(solution)/shard_map/ppermute | solution.py:296
  138.8 5.8 %collective-permute-start.31 = (bf16[256,256]{1,0:T(8,128)(2,1)S(1)}, bf16[256,256]{1,0:T(8,128)(2,1)S(1)}, u32[]{:S(2)}, u32[]{:S(2)}) collective-permute-start(bf16[256,256]{1,0:T(8,128)(2,1)S(1)} %get-tuple-element.149), channel_id=1, source_target_pairs={{0,4},{1,5},{2,6},{3,7},{4,0},{5,1},{6,2},{7,3},{8,12},{9,13},{10,... | collective-permute-start | bytes 393224 | tf_op jit(solution)/shard_map/ppermute | solution.py:296
  139.2 5.4 %collective-permute-start.32 = (bf16[256,256]{1,0:T(8,128)(2,1)S(1)}, bf16[256,256]{1,0:T(8,128)(2,1)S(1)}, u32[]{:S(2)}, u32[]{:S(2)}) collective-permute-start(bf16[256,256]{1,0:T(8,128)(2,1)S(1)} %get-tuple-element.150), channel_id=1, source_target_pairs={{0,4},{1,5},{2,6},{3,7},{4,0},{5,1},{6,2},{7,3},{8,12},{9,13},{10,... | collective-permute-start | bytes 393224 | tf_op jit(solution)/shard_map/ppermute | solution.py:296
  (13 other events, 11.2 us)
Sparse Core Ops, SparseCore 0:
  26.8 59.5 all-gather.2

commit v14 on v10

--- a/solution.py
+++ b/solution.py
@@ -20,7 +20,7 @@
 HBM = pl.BlockSpec(memory_space=pltpu.HBM)
 
 
-def call(body, outs, in_specs, flops=0, scratch=(), out_spec=VMEM, limit=16 << 20):
+def call(body, outs, in_specs, flops=0, scratch=(), out_spec=VMEM, limit=16 << 20, moved=4 << 20):
     return pl.pallas_call(
         body,
         out_shape=outs,
@@ -28,7 +28,7 @@
         out_specs=[out_spec] * len(outs),
         scratch_shapes=list(scratch),
         compiler_params=pltpu.CompilerParams(vmem_limit_bytes=limit),
-        cost_estimate=pl.CostEstimate(flops=flops, bytes_accessed=4 << 20, transcendentals=0),
+        cost_estimate=pl.CostEstimate(flops=flops, bytes_accessed=moved, transcendentals=0),
     )
 
 
@@ -106,6 +106,7 @@
 def late_rows(here_ref, chosen_ref, start, width, *pieces):
     *whole, inner, outer, part = pieces
     lost = inner.shape[1] - outer.shape[1] if start else 0
+    at = slice(start - lost, start - lost + width)
     inside = (here_ref[2] == 1) | (here_ref[2] == 2)
 
     @pl.when(inside)
@@ -114,10 +115,10 @@
 
     @pl.when(jnp.logical_not(inside))
     def _():
-        chosen_ref[...] = outer[:, start - lost : start - lost + width]
+        chosen_ref[...] = outer[:, at]
 
     rows = [piece[:, start : start + width] for piece in whole]
-    return jnp.concatenate(rows + [chosen_ref[...], part[...]], axis=0)
+    return jnp.concatenate(rows + [chosen_ref[...], part[:, at]], axis=0)
 
 
 def kv_body(n_late, here_ref, *refs):
@@ -209,7 +210,7 @@
     work = [(at, p, h) for at in range(len(segs)) for p in range(len(parts)) for h in range(heads)]
     memories = []
     for seg in segs:
-        memory = base_ref[...].astype(jnp.float32)
+        memory = jnp.where(here_ref[3] > 0, 1.0, 0.0) * base_ref[...].astype(jnp.float32)
         for other in range(MEMBERS):
             if other != seg:
                 earlier = jnp.where((me ^ other) < (me ^ seg), 1.0, 0.0)
@@ -235,12 +236,16 @@
 
 
 def assemble_body(counts, here_ref, *refs):
-    parts, out = list(refs[:-1]), refs[-1]
+    parts, out = list(refs[1:-1]), refs[-1]
     width = out.shape[1] // MEMBERS
     for k, count in enumerate(counts):
         for c in range(count):
             at = (here_ref[1] ^ k) * width + c * (width // count)
             out[:, pl.ds(aligned(at), width // count)] = parts.pop(0)[...]
+
+
+def gate_body(*refs):
+    refs[-1][...] = jnp.zeros_like(refs[-1])
 
 
 def after(array, *others):
@@ -258,7 +263,7 @@
     seg = lax.axis_index("seg")
     z = lax.axis_index("fsdp")
     g, m = seg // MEMBERS, seg % MEMBERS
-    here = jnp.stack([g, m, z]).astype(jnp.int32)
+    here = jnp.stack([g, m, z, g if n_groups == 2 else 1]).astype(jnp.int32)
     bf16, f32 = jnp.bfloat16, jnp.float32
     shape = jax.ShapeDtypeStruct
 
@@ -281,6 +286,7 @@
         functools.partial(pack_body, group),
         [shape((rows + META_ROWS, wide), bf16)] * MEMBERS,
         [SMEM] * 3 + [VMEM] * 3,
+        limit=56 << 20,
     )(here, valid_len, block_mask, w_query, w_key, value_weight)
     messages = [packed[0], *[to_member(packed[k], k) for k in (1, 2, 3)]]
 
@@ -347,10 +353,10 @@
         a_last, a_far2, a_middle, a_inner = locked(a_last, a_far2, a_middle, a_inner)
         a_three = jnp.where(inside, a_middle, a_last)
         books = [own, sibling]
-        upper = [a, a_one, a_two, None, a_far0, a_far1]
+        upper = [a, a_one, a_two, a_three, a_far0, a_far1, a_far2]
         lower = [b, b_one, b_two, None, b_far0, b_far1]
-        early = [(k, half) for half in range(2) for k in (0, 1, 2, 4, 5)]
-        late = [(3, 0), (6, 0), (3, 1), (6, 1), (7, 0), (7, 1)]
+        late = [(3, 1), (6, 1), (7, 0), (7, 1)]
+        early = [(k, half) for half in range(2) for k in range(8) if (k, half) not in late]
         project((0, 1), early, late, (upper, lower), n_z)
         b_last, b_far2, b_middle, sums[0], sums[1], across = locked(
             b_last, b_far2, b_middle, sums[0], sums[1], after(across, a_last, a_far2)
@@ -358,10 +364,10 @@
         books += [across, to_member(across, 1)]
         project((2, 3), early, late, (upper, lower), n_z)
         b_three = jnp.where(inside, b_middle, b_last)
-        pieces = [a_three, a_far2, b_three, b_far2]
+        pieces = [b_three, b_far2]
         outer_kv, outer_q = [outward(a_inner[:, at]) for at in (slice(0, cut), slice(cut, None))]
         inner = a_inner
-        finish = lambda at, *others: over(after(b_three[:, at], *others))
+        finish = lambda at: over(b_three[:, at])
     else:
         across, sibling = to_member(tokens[0], 2), to_member(tokens[0], 1)
         books = [tokens[0], sibling, across, to_member(across, 1)]
@@ -377,10 +383,10 @@
         pieces = [lower[-2]]
         outer_kv, outer_q = upper[-1][:, :cut], upper[-1][:, cut:]
         inner = upper[-1]
-        finish = lambda at, *others: lower[-1][:, at]
+        finish = lambda at: lower[-1][:, at]
 
     halves = [slice(k * HEAD_SIZE, (k + 2) * HEAD_SIZE) for k in (0, 2, 4)]
-    lower_kv, lower_q0 = finish(halves[0]), finish(halves[1])
+    lower_kv, lower_q = finish(slice(0, cut)), finish(slice(cut, None))
     found = call(
         functools.partial(kv_body, len(late) + 1),
         [shape((length, 2 * HEAD_SIZE), bf16), shape((HEAD_SIZE, 2 * HEAD_SIZE), f32)] * MEMBERS
@@ -393,20 +399,21 @@
 
     base = None
     for a in range(1, n_groups):
-        term = permute(total, lambda gg, mm, zz: (gg ^ a, mm, zz) if gg < gg ^ a else None)
-        base = term if base is None else base.astype(f32) + term.astype(f32)
-
-    lower_q1 = finish(halves[2], total)
+        term = permute(total, lambda gg, mm, zz: (gg ^ a, mm, zz))
+        if n_groups > 2:
+            term = jnp.where((g ^ a) < g, term, 0).astype(f32)
+        base = term if base is None else base + term
+
     half = group // 2
 
-    def local(segs, part, lower_q):
+    def local(segs, part, *others):
         found = call(
             functools.partial(local_body, len(segs), len(late) + 1, halves[1 + part].start, half),
             [shape((length, half * HEAD_SIZE), bf16), shape((length, half * HEAD_SIZE), f32)] * len(segs),
             [SMEM] + [VMEM] * (len(late) + 1 + 4 * len(segs)),
             flops=4 * len(segs) * length * length * half * HEAD_SIZE,
             scratch=[pltpu.VMEM((MEMBERS * HEAD_SIZE // 2, half * HEAD_SIZE), bf16)],
-        )(here, *pieces, inner, outer_q, lower_q, *[one[s] for one in (kvs, messages, sums, lates) for s in segs])
+        )(here, *pieces, inner, outer_q, after(lower_q, *others), *[one[s] for one in (kvs, messages, sums, lates) for s in segs])
         return {(s, part): (found[2 * at], found[2 * at + 1]) for at, s in enumerate(segs)}
 
     def mix(segs, parts, base, ready):
@@ -421,21 +428,23 @@
             *[ready[key][0] for key in keys], *[ready[key][1] for key in keys],
         )
 
-    ready = local((2, 3, 1, 0), 0, lower_q0)
+    ready = local((2, 3, 1, 0), 0)
     base = after(base, *ready[2, 0])
     two0, three0 = mix((2, 3), (0,), base, ready)
-    ready |= local((2, 3), 1, after(lower_q1, two0, three0))
+    ready |= local((2, 3), 1, two0, three0)
     two1, three1 = mix((2, 3), (1,), base, ready)
-    ready |= local((1, 0), 1, after(lower_q1, two1, three1))
+    ready |= local((1, 0), 1, two1, three1)
     one0, one1, mine0, mine1 = mix((1, 0), (0, 1), after(base, two1, three1), ready)
     sent = [mine0, mine1]
     for k, parts in ((1, (one0, one1)), (2, (two0, two1)), (3, (three0, three1))):
         sent += [to_member(part, k) for part in parts]
+    far = sent[4:]
+    (gate,) = call(gate_body, [shape((8, HEAD_SIZE), f32)], [ANY] * len(far), moved=16 << 20)(*far)
     (output,) = call(
         functools.partial(assemble_body, (2,) * MEMBERS),
         [shape((length, w_query.shape[1]), bf16)],
-        [SMEM] + [VMEM] * len(sent),
-    )(here, *sent)
+        [SMEM] + [VMEM] * (1 + len(sent)),
+    )(here, gate, *sent)
     return output[None]
 
 

time: 119 us -> 115 us (0.966); the launches traced: 117 us -> 114 us
  starting transfers between devices: 55.2 us -> 52.4 us
  local copies, waits for them, and re-layouts: 4.41 us -> 2.56 us
  other arithmetic: 3.35 us -> 4.94 us
    ppermute x35 -> x34, starting transfers between devices: 55.2 us -> 52.4 us  [permute(): return lax.ppermute(array, AXES, pairs)]
    unnamed x18 -> x16, local copies, waits for them, and re-layouts: 4.3 us -> 1.52 us
    pallas_call x1, Pallas kernels: 0.63 us -> 2.14 us  [shards(): call(functools.partial(pack_body, group), [shape((rows + META_ROWS, wide)...]
    ppermute x35 -> x34, waiting for transfers between devices: 29 us -> 28.7 us  [permute(): return lax.ppermute(array, AXES, pairs)]
  transfers between devices with their start and end apart: 35 -> 34, of which waited for: 10 -> 11; matrix products, arithmetic and copies ran while one was open for 3% -> 5% of each run, Pallas kernels for 19% -> 19%
where the time goes in v14:
time: 115 us; the launch traced here: 114 us
  starting transfers between devices  52.4 us (46%)
  waiting for transfers between devices  28.7 us (25%)
  Pallas kernels  24.6 us (21%)
  other arithmetic  4.94 us (4%)
  local copies, waits for them, and re-layouts  2.56 us (2%)
    ppermute x34, starting transfers between devices, permute(): return lax.ppermute(array, AXES, pairs)  52.4 us
    ppermute x34, waiting for transfers between devices, permute(): return lax.ppermute(array, AXES, pairs)  28.7 us
    pallas_call x2, Pallas kernels, project(): call(functools.partial(project_body, early, late, line), [shape((length,...  9.76 us
    pallas_call x3, Pallas kernels, local(): call(functools.partial(local_body, len(segs), len(late) + 1, halves[1 + p...  5.44 us
    pallas_call x3, Pallas kernels, mix(): call(functools.partial(mix_body, segs, parts, group), [shape((length, hal...  3.96 us
  transfers between devices with their start and end apart: 34, of which 11 were waited for; matrix products, arithmetic and copies ran while one was open for 5% of the time, Pallas kernels for 19%

profile of v14, /device:TPU:9, one launch (start us, length us, event | category | flops | bytes accessed | tf_op | source)
XLA Modules:
  0.0 114.3 jit_solution(5400141792639837423)
XLA Ops:
  0.0 0.7 collective-permute-start.3
  1.3 0.7 pad_add_fusion.here_ref
  2.0 2.1 %shard_map.73 = (bf16[144,768]{1,0:T(8,128)(2,1)}, bf16[144,768]{1,0:T(8,128)(2,1)}, bf16[144,768]{1,0:T(8,128)(2,1)}, bf16[144,768]{1,0:T(8,128)(2,1)}) custom-call(s32[4]{0:T(128)} %pad_add_fusion.here_ref, s32[1,1]{1,0:T(1,128)S(6)} %copy.8.valid_ref, s32[1,1,2,2]{3,2,1,0:T(2,128)} %mask_ref.1, bf16[128,2048]{1,0:T(8,128)(2,1)} %wq_ref.1, ...), custom_call_target="tpu_custom_call" | custom-call | bytes 4194304 | tf_op jit(solution)/shard_map/pallas_call | solution.py:285
  4.1 0.2 collective-permute-start
  4.3 1.5 %collective-permute-start.2 = (bf16[144,768]{1,0:T(8,128)(2,1)}, bf16[144,768]{1,0:T(8,128)(2,1)S(1)}, u32[]{:S(2)}, u32[]{:S(2)}) collective-permute-start(bf16[144,768]{1,0:T(8,128)(2,1)} %get-tuple-element.84), channel_id=1, source_target_pairs={{0,12},{1,13},{2,14},{3,15},{4,8},{5,9},{6,10},{7,11},{8,4},{9,5},... | collective-permute-start | bytes 663560 | tf_op jit(solution)/shard_map/ppermute | solution.py:279
  5.8 0.3 collective-permute-start.1
  6.0 0.9 slice.24
  7.0 0.0 collective-permute-done.refs_14_.refs_11_.refs_7_.refs_4_
  7.0 5.3 %collective-permute-done.2.refs_16_.refs_10_.refs_5_.refs_8_ = bf16[144,768]{1,0:T(8,128)(2,1)S(1)} collective-permute-done((bf16[144,768]{1,0:T(8,128)(2,1)}, bf16[144,768]{1,0:T(8,128)(2,1)S(1)}, u32[]{:S(2)}, u32[]{:S(2)}) %collective-permute-start.2) | collective-permute-done | bytes 221216 | tf_op jit(solution)/shard_map/ppermute | solution.py:279
  12.3 4.4 %collective-permute-done.1.refs_15_.refs_9_.refs_4_.refs_7_ = bf16[144,768]{1,0:T(8,128)(2,1)S(1)} collective-permute-done((bf16[144,768]{1,0:T(8,128)(2,1)}, bf16[144,768]{1,0:T(8,128)(2,1)S(1)}, u32[]{:S(2)}, u32[]{:S(2)}) %collective-permute-start.1) | collective-permute-done | bytes 221216 | tf_op jit(solution)/shard_map/ppermute | solution.py:279
  16.7 0.1 collective-permute-start.12
  16.8 1.4 %collective-permute-start.21 = (bf16[256,4096]{1,0:T(8,128)(2,1)S(1)}, bf16[256,4096]{1,0:T(8,128)(2,1)}, u32[]{:S(2)}, u32[]{:S(2)}) collective-permute-start(bf16[256,4096]{1,0:T(8,128)(2,1)S(1)} %bitcast.6), channel_id=1, source_target_pairs={{0,8},{1,9},{2,10},{3,11},{4,12},{5,13},{6,14},{7,15},{8,0},{9,1},... | collective-permute-start | bytes 6291464 | tf_op jit(solution)/shard_map/ppermute | solution.py:279
  18.2 4.3 %collective-permute-start.13 = (bf16[256,768]{1,0:T(8,128)(2,1)S(1)}, bf16[256,768]{1,0:T(8,128)(2,1)}, u32[]{:S(2)}, u32[]{:S(2)}) collective-permute-start(bf16[256,768]{1,0:T(8,128)(2,1)S(1)} %pad_maximum_fusion.refs_2_), channel_id=1, source_target_pairs={{1,2},{2,1},{5,6},{6,5},{9,10},{10,9},{13,14},{14,13},{17,18},{18,... | collective-permute-start | bytes 1179656 | tf_op jit(solution)/shard_map/ppermute | solution.py:279
  22.5 1.3 %collective-permute-start.14 = (bf16[256,768]{1,0:T(8,128)(2,1)S(1)}, bf16[256,768]{1,0:T(8,128)(2,1)S(1)}, u32[]{:S(2)}, u32[]{:S(2)}) collective-permute-start(bf16[256,768]{1,0:T(8,128)(2,1)S(1)} %pad_maximum_fusion.refs_2_), channel_id=1, source_target_pairs={{0,16},{1,17},{2,18},{3,19},{4,20},{5,21},{6,22},{7,23},{8,24},{9,... | collective-permute-start | bytes 1179656 | tf_op jit(solution)/shard_map/ppermute | solution.py:279
  23.8 3.0 %collective-permute-done.12.refs_3_ = bf16[256,768]{1,0:T(8,128)(2,1)} collective-permute-done((bf16[256,768]{1,0:T(8,128)(2,1)S(1)}, bf16[256,768]{1,0:T(8,128)(2,1)}, u32[]{:S(2)}, u32[]{:S(2)}) %collective-permute-start.12) | collective-permute-done | bytes 393248 | tf_op jit(solution)/shard_map/ppermute | solution.py:279
  26.8 3.2 %collective-permute-start.5 = (bf16[256,768]{1,0:T(8,128)(2,1)S(1)}, bf16[256,768]{1,0:T(8,128)(2,1)}, u32[]{:S(2)}, u32[]{:S(2)}) collective-permute-start(bf16[256,768]{1,0:T(8,128)(2,1)S(1)} %pad_maximum_fusion.1.refs_9_), channel_id=1, source_target_pairs={{1,2},{2,1},{5,6},{6,5},{9,10},{10,9},{13,14},{14,13},{17,18},{18,... | collective-permute-start | bytes 1179656 | tf_op jit(solution)/shard_map/ppermute | solution.py:279
  30.0 0.7 collective-permute-done.13
  30.7 1.2 %collective-permute-start.6 = (bf16[256,768]{1,0:T(8,128)(2,1)S(1)}, bf16[256,768]{1,0:T(8,128)(2,1)S(1)}, u32[]{:S(2)}, u32[]{:S(2)}) collective-permute-start(bf16[256,768]{1,0:T(8,128)(2,1)S(1)} %pad_maximum_fusion.1.refs_9_), channel_id=1, source_target_pairs={{0,16},{1,17},{2,18},{3,19},{4,20},{5,21},{6,22},{7,23},{8,24},{9,... | collective-permute-start | bytes 1179656 | tf_op jit(solution)/shard_map/ppermute | solution.py:279
  32.0 0.7 copy-done.4
  32.7 3.1 %collective-permute-start.15 = (bf16[256,768]{1,0:T(8,128)(2,1)}, bf16[256,768]{1,0:T(8,128)(2,1)}, u32[]{:S(2)}, u32[]{:S(2)}) collective-permute-start(bf16[256,768]{1,0:T(8,128)(2,1)} %collective-permute-done.12.refs_3_), channel_id=1, source_target_pairs={{1,2},{2,1},{5,6},{6,5},{9,10},{10,9},{13,14},{14,13},{17,18},{18,... | collective-permute-start | bytes 1179656 | tf_op jit(solution)/shard_map/ppermute | solution.py:279
  35.8 2.5 %collective-permute-start.16 = (bf16[256,768]{1,0:T(8,128)(2,1)}, bf16[256,768]{1,0:T(8,128)(2,1)}, u32[]{:S(2)}, u32[]{:S(2)}) collective-permute-start(bf16[256,768]{1,0:T(8,128)(2,1)} %collective-permute-done.13), channel_id=1, source_target_pairs={{1,0},{2,3},{5,4},{6,7},{9,8},{10,11},{13,12},{14,15},{17,16},{18,... | collective-permute-start | bytes 1179656 | tf_op jit(solution)/shard_map/ppermute | solution.py:279
  38.3 1.1 collective-permute-start.17
  39.4 0.7 copy-done.6
  40.1 4.3 %collective-permute-start.7 = (bf16[256,768]{1,0:T(8,128)(2,1)}, bf16[256,768]{1,0:T(8,128)(2,1)}, u32[]{:S(2)}, u32[]{:S(2)}) collective-permute-start(bf16[256,768]{1,0:T(8,128)(2,1)} %collective-permute-done.4.refs_10_), channel_id=1, source_target_pairs={{1,2},{2,1},{5,6},{6,5},{9,10},{10,9},{13,14},{14,13},{17,18},{18,... | collective-permute-start | bytes 1179656 | tf_op jit(solution)/shard_map/ppermute | solution.py:279
  44.4 2.1 %collective-permute-done.15 = bf16[256,768]{1,0:T(8,128)(2,1)} collective-permute-done((bf16[256,768]{1,0:T(8,128)(2,1)}, bf16[256,768]{1,0:T(8,128)(2,1)}, u32[]{:S(2)}, u32[]{:S(2)}) %collective-permute-start.15) | collective-permute-done | bytes 393248 | tf_op jit(solution)/shard_map/ppermute | solution.py:279
  46.5 2.0 %collective-permute-start.8 = (bf16[256,768]{1,0:T(8,128)(2,1)}, bf16[256,768]{1,0:T(8,128)(2,1)}, u32[]{:S(2)}, u32[]{:S(2)}) collective-permute-start(bf16[256,768]{1,0:T(8,128)(2,1)} %collective-permute-done.5), channel_id=1, source_target_pairs={{1,0},{2,3},{5,4},{6,7},{9,8},{10,11},{13,12},{14,15},{17,16},{18,... | collective-permute-start | bytes 1179656 | tf_op jit(solution)/shard_map/ppermute | solution.py:279
  48.6 1.2 %collective-permute-start.9 = (bf16[256,768]{1,0:T(8,128)(2,1)}, bf16[256,768]{1,0:T(8,128)(2,1)S(1)}, u32[]{:S(2)}, u32[]{:S(2)}) collective-permute-start(bf16[256,768]{1,0:T(8,128)(2,1)} %collective-permute-done.4.refs_10_), channel_id=1, source_target_pairs={{0,16},{1,17},{2,18},{3,19},{4,20},{5,21},{6,22},{7,23},{8,24},{9,... | collective-permute-start | bytes 1179656 | tf_op jit(solution)/shard_map/ppermute | solution.py:279
  49.8 1.3 %collective-permute-start.18 = (bf16[256,768]{1,0:T(8,128)(2,1)}, bf16[256,768]{1,0:T(8,128)(2,1)S(1)}, u32[]{:S(2)}, u32[]{:S(2)}) collective-permute-start(bf16[256,768]{1,0:T(8,128)(2,1)} %collective-permute-done.15), channel_id=1, source_target_pairs={{1,0},{2,3},{5,4},{6,7},{9,8},{10,11},{13,12},{14,15},{17,16},{18,... | collective-permute-start | bytes 1179656 | tf_op jit(solution)/shard_map/ppermute | solution.py:279
  51.1 1.1 broadcast_select_fusion.2.refs_4_
  52.2 2.8 %collective-permute-done.7 = bf16[256,768]{1,0:T(8,128)(2,1)} collective-permute-done((bf16[256,768]{1,0:T(8,128)(2,1)}, bf16[256,768]{1,0:T(8,128)(2,1)}, u32[]{:S(2)}, u32[]{:S(2)}) %collective-permute-start.7) | collective-permute-done | bytes 393248 | tf_op jit(solution)/shard_map/ppermute | solution.py:279
  54.9 1.2 %collective-permute-start.19 = (bf16[256,768]{1,0:T(8,128)(2,1)S(1)}, bf16[256,768]{1,0:T(8,128)(2,1)S(1)}, u32[]{:S(2)}, u32[]{:S(2)}) collective-permute-start(bf16[256,768]{1,0:T(8,128)(2,1)S(1)} %broadcast_select_fusion.2.refs_4_), channel_id=1, source_target_pairs={{0,16},{1,17},{2,18},{3,19},{4,20},{5,21},{6,22},{7,23},{8,24},{9,... | collective-permute-start | bytes 1179656 | tf_op jit(solution)/shard_map/ppermute | solution.py:279
  56.2 3.5 %collective-permute-start.20 = (bf16[256,768]{1,0:T(8,128)(2,1)}, bf16[256,768]{1,0:T(8,128)(2,1)S(1)}, u32[]{:S(2)}, u32[]{:S(2)}) collective-permute-start(bf16[256,768]{1,0:T(8,128)(2,1)} %collective-permute-done.17.refs_7_), channel_id=1, source_target_pairs={{1,2},{2,1},{5,6},{6,5},{9,10},{10,9},{13,14},{14,13},{17,18},{18,... | collective-permute-start | bytes 1179656 | tf_op jit(solution)/shard_map/ppermute | solution.py:279
  59.7 1.3 %collective-permute-start.10 = (bf16[256,768]{1,0:T(8,128)(2,1)}, bf16[256,768]{1,0:T(8,128)(2,1)S(1)}, u32[]{:S(2)}, u32[]{:S(2)}) collective-permute-start(bf16[256,768]{1,0:T(8,128)(2,1)} %collective-permute-done.7), channel_id=1, source_target_pairs={{1,0},{2,3},{5,4},{6,7},{9,8},{10,11},{13,12},{14,15},{17,16},{18,... | collective-permute-start | bytes 1179656 | tf_op jit(solution)/shard_map/ppermute | solution.py:279
  61.0 1.1 broadcast_select_fusion.3.refs_11_
  62.1 0.3 collective-permute-start.11
  62.4 3.7 %collective-permute-done.19.refs_8_ = bf16[256,768]{1,0:T(8,128)(2,1)S(1)} collective-permute-done((bf16[256,768]{1,0:T(8,128)(2,1)S(1)}, bf16[256,768]{1,0:T(8,128)(2,1)S(1)}, u32[]{:S(2)}, u32[]{:S(2)}) %collective-permute-start.19) | collective-permute-done | bytes 393248 | tf_op jit(solution)/shard_map/ppermute | solution.py:279
  66.1 1.1 broadcast_select_fusion.1.refs_5_
  67.2 4.9 %shard_map.74 = (f32[256,768]{1,0:T(8,128)S(1)}, f32[256,768]{1,0:T(8,128)S(1)}, bf16[256,1024]{1,0:T(8,128)(2,1)S(1)}, bf16[256,1024]{1,0:T(8,128)(2,1)S(1)}) custom-call(s32[4]{0:T(128)S(1)} %copy-done.1, bf16[256,4096]{1,0:T(8,128)(2,1)S(1)} %bitcast.7, bf16[256,4096]{1,0:T(8,128)(2,1)} %collective-permute-done.3.refs_1_, ...), custom_call_target="tpu_custom_call" | custom-call | flops 2415919104 | bytes 4194304 | tf_op jit(solution)/shard_map/pallas_call | solution.py:317
  72.1 2.4 %collective-permute-done.11.refs_1_ = bf16[256,768]{1,0:T(8,128)(2,1)S(1)} collective-permute-done((bf16[256,768]{1,0:T(8,128)(2,1)S(1)}, bf16[256,768]{1,0:T(8,128)(2,1)S(1)}, u32[]{:S(2)}, u32[]{:S(2)}) %collective-permute-start.11) | collective-permute-done | bytes 393248 | tf_op jit(solution)/shard_map/ppermute | solution.py:279
  74.5 6.2 %collective-permute-start.24 = (bf16[256,4096]{1,0:T(8,128)(2,1)}, bf16[256,4096]{1,0:T(8,128)(2,1)S(1)}, u32[]{:S(2)}, u32[]{:S(2)}) collective-permute-start(bf16[256,4096]{1,0:T(8,128)(2,1)} %collective-permute-done.21.refs_0_), channel_id=1, source_target_pairs={{0,4},{1,5},{2,6},{3,7},{4,0},{5,1},{6,2},{7,3},{8,12},{9,13},{10,... | collective-permute-start | bytes 6291464 | tf_op jit(solution)/shard_map/ppermute | solution.py:279
  80.8 1.3 %collective-permute-start.22 = (bf16[256,256]{1,0:T(8,128)(2,1)S(1)}, bf16[256,256]{1,0:T(8,128)(2,1)S(1)}, u32[]{:S(2)}, u32[]{:S(2)}) collective-permute-start(bf16[256,256]{1,0:T(8,128)(2,1)S(1)} %slice.28), channel_id=1, source_target_pairs={{1,0},{2,3},{5,4},{6,7},{9,8},{10,11},{13,12},{14,15},{17,16},{18,... | collective-permute-start | bytes 393224 | tf_op jit(solution)/shard_map/ppermute | solution.py:279
  82.1 1.3 %collective-permute-start.26 = (bf16[256,512]{1,0:T(8,128)(2,1)S(1)}, bf16[256,512]{1,0:T(8,128)(2,1)S(1)}, u32[]{:S(2)}, u32[]{:S(2)}) collective-permute-start(bf16[256,512]{1,0:T(8,128)(2,1)S(1)} %slice.30), channel_id=1, source_target_pairs={{1,0},{2,3},{5,4},{6,7},{9,8},{10,11},{13,12},{14,15},{17,16},{18,... | collective-permute-start | bytes 786440 | tf_op jit(solution)/shard_map/ppermute | solution.py:279
  83.4 1.1 broadcast_select_fusion.refs_0_
  84.5 1.3 %collective-permute-start.23 = (bf16[256,256]{1,0:T(8,128)(2,1)S(1)}, bf16[256,256]{1,0:T(8,128)(2,1)S(1)}, u32[]{:S(2)}, u32[]{:S(2)}) collective-permute-start(bf16[256,256]{1,0:T(8,128)(2,1)S(1)} %slice.35), channel_id=1, source_target_pairs={{0,16},{1,17},{2,18},{3,19},{4,20},{5,21},{6,22},{7,23},{8,24},{9,... | collective-permute-start | bytes 393224 | tf_op jit(solution)/shard_map/ppermute | solution.py:279
  85.9 0.2 collective-permute-start.27
  86.0 4.9 %shard_map.75 = (f32[256,768]{1,0:T(8,128)S(1)}, f32[256,768]{1,0:T(8,128)S(1)}, bf16[256,1024]{1,0:T(8,128)(2,1)S(1)}, bf16[256,1024]{1,0:T(8,128)(2,1)S(1)}) custom-call(s32[4]{0:T(128)S(1)} %copy-done.1, bf16[256,4096]{1,0:T(8,128)(2,1)} %collective-permute-done.21.refs_0_, bf16[256,4096]{1,0:T(8,128)(2,1)S(1)} %collective-permute-done.24.refs_1_, ...), custom_call_target="tpu_custom_call" | custom-call | flops 2415919104 | bytes 4194304 | tf_op jit(solution)/shard_map/pallas_call | solution.py:317
  91.0 1.7 %shard_map.76 = (bf16[256,256]{1,0:T(8,128)(2,1)S(1)}, f32[128,256]{1,0:T(8,128)S(1)}, bf16[256,256]{1,0:T(8,128)(2,1)S(1)}, f32[128,256]{1,0:T(8,128)S(1)}, bf1...) custom-call(s32[4]{0:T(128)S(1)} %copy-done.1, ...), custom_call_target="tpu_custom_call" | custom-call | flops 536870912 | bytes 4194304 | tf_op jit(solution)/shard_map/pallas_call | solution.py:390
  92.7 1.3 %collective-permute-start.25 = (bf16[128,256]{1,0:T(8,128)(2,1)S(1)}, bf16[128,256]{1,0:T(8,128)(2,1)S(1)}, u32[]{:S(2)}, u32[]{:S(2)}) collective-permute-start(bf16[128,256]{1,0:T(8,128)(2,1)S(1)} %get-tuple-element.120), channel_id=1, source_target_pairs={{0,16},{1,17},{2,18},{3,19},{4,20},{5,21},{6,22},{7,23},{8,24},{9,... | collective-permute-start | bytes 196616 | tf_op jit(solution)/shard_map/ppermute | solution.py:279
  94.0 1.3 %collective-permute-done.27.refs_4_ = bf16[256,512]{1,0:T(8,128)(2,1)S(1)} collective-permute-done((bf16[256,512]{1,0:T(8,128)(2,1)S(1)}, bf16[256,512]{1,0:T(8,128)(2,1)S(1)}, u32[]{:S(2)}, u32[]{:S(2)}) %collective-permute-start.27) | collective-permute-done | bytes 262176 | tf_op jit(solution)/shard_map/ppermute | solution.py:279
  95.3 2.1 %shard_map.77 = (bf16[256,256]{1,0:T(8,128)(2,1)S(1)}, f32[256,256]{1,0:T(8,128)S(1)}, bf16[256,256]{1,0:T(8,128)(2,1)S(1)}, f32[256,256]{1,0:T(8,128)S(1)}, bf1...) custom-call(s32[4]{0:T(128)S(1)} %copy-done.1, ...), custom_call_target="tpu_custom_call" | custom-call | flops 268435456 | bytes 4194304 | tf_op jit(solution)/shard_map/pallas_call | solution.py:410
  97.4 1.2 %shard_map.78 = (bf16[256,256]{1,0:T(8,128)(2,1)S(1)}, bf16[256,256]{1,0:T(8,128)(2,1)S(1)}) custom-call(s32[4]{0:T(128)S(1)} %copy-done.1, f32[16]{0:T(128)S(1)} %copy-done.2, bf16[128,256]{1,0:T(8,128)(2,1)S(1)} %collective-permute-done.25.base_ref, f32[128,256]{1,0:T(8,128)S(1)} %get-tuple-element.128.refs_0_, f32[128,256]{1,0:T(8,128)S(1)} %get-tuple-element.129.refs_1_, ...), custom_call_target="tpu_custom_call" | custom-call | flops 201326592 | bytes 4194304 | tf_op jit(solution)/shard_map/pallas_call | solution.py:421
  98.6 0.4 collective-permute-start.28
  99.0 2.3 %collective-permute-start.30 = (bf16[256,256]{1,0:T(8,128)(2,1)S(1)}, bf16[256,256]{1,0:T(8,128)(2,1)S(1)}, u32[]{:S(2)}, u32[]{:S(2)}) collective-permute-start(bf16[256,256]{1,0:T(8,128)(2,1)S(1)} %get-tuple-element.135), channel_id=1, source_target_pairs={{0,12},{1,13},{2,14},{3,15},{4,8},{5,9},{6,10},{7,11},{8,4},{9,5},... | collective-permute-start | bytes 393224 | tf_op jit(solution)/shard_map/ppermute | solution.py:279
  101.3 1.8 %shard_map.79 = (bf16[256,256]{1,0:T(8,128)(2,1)S(1)}, f32[256,256]{1,0:T(8,128)S(1)}, bf16[256,256]{1,0:T(8,128)(2,1)S(1)}, f32[256,256]{1,0:T(8,128)S(1)}) custom-call(s32[4]{0:T(128)S(1)} %copy-done.1, bf16[256,768]{1,0:T(8,128)(2,1)S(1)} %broadcast_select_fusion.refs_0_, bf16[256,768]{1,0:T(8,128)(2,1)S(1)} %collective-permute-done.11.refs_1_, ...), custom_call_target="tpu_custom_call" | custom-call | flops 134217728 | bytes 4194304 | tf_op jit(solution)/shard_map/pallas_call | solution.py:410
  103.1 1.2 %shard_map.80 = (bf16[256,256]{1,0:T(8,128)(2,1)S(1)}, bf16[256,256]{1,0:T(8,128)(2,1)S(1)}) custom-call(s32[4]{0:T(128)S(1)} %copy-done.1, f32[16]{0:T(128)S(1)} %copy-done.2, bf16[128,256]{1,0:T(8,128)(2,1)S(1)} %collective-permute-done.25.base_ref, f32[128,256]{1,0:T(8,128)S(1)} %get-tuple-element.128.refs_0_, f32[128,256]{1,0:T(8,128)S(1)} %get-tuple-element.129.refs_1_, ...), custom_call_target="tpu_custom_call" | custom-call | flops 201326592 | bytes 4194304 | tf_op jit(solution)/shard_map/pallas_call | solution.py:421
  104.3 0.4 collective-permute-start.29
  104.6 0.5 collective-permute-start.31
  105.2 1.6 %shard_map.82 = (bf16[256,256]{1,0:T(8,128)(2,1)S(1)}, f32[256,256]{1,0:T(8,128)S(1)}, bf16[256,256]{1,0:T(8,128)(2,1)S(1)}, f32[256,256]{1,0:T(8,128)S(1)}) custom-call(s32[4]{0:T(128)S(1)} %copy-done.1, bf16[256,768]{1,0:T(8,128)(2,1)S(1)} %broadcast_select_fusion.refs_0_, bf16[256,768]{1,0:T(8,128)(2,1)S(1)} %collective-permute-done.11.refs_1_, ...), custom_call_target="tpu_custom_call" | custom-call | flops 134217728 | bytes 4194304 | tf_op jit(solution)/shard_map/pallas_call | solution.py:410
  106.8 1.6 %shard_map.83 = (bf16[256,256]{1,0:T(8,128)(2,1)S(1)}, bf16[256,256]{1,0:T(8,128)(2,1)S(1)}, bf16[256,256]{1,0:T(8,128)(2,1)S(1)}, bf16[256,256]{1,0:T(8,128)(2,1)S(1)}) custom-call(s32[4]{0:T(128)S(1)} %copy-done.1, f32[16]{0:T(128)S(1)} %copy-done.2, bf16[128,256]{1,0:T(8,128)(2,1)S(1)} %collective-permute-done.25.base_ref, ...), custom_call_target="tpu_custom_call" | custom-call | flops 402653184 | bytes 4194304 | tf_op jit(solution)/shard_map/pallas_call | solution.py:421
  108.4 1.1 collective-permute-start.32
  109.5 0.1 collective-permute-start.33
  109.6 0.3 collective-permute-done.29.refs_1_.refs_6_
  109.9 2.8 %collective-permute-done.31.refs_3_.refs_8_ = bf16[256,256]{1,0:T(8,128)(2,1)S(1)} collective-permute-done((bf16[256,256]{1,0:T(8,128)(2,1)S(1)}, bf16[256,256]{1,0:T(8,128)(2,1)S(1)}, u32[]{:S(2)}, u32[]{:S(2)}) %collective-permute-start.31) | collective-permute-done | bytes 131104 | tf_op jit(solution)/shard_map/ppermute | solution.py:279
  112.7 1.6 %shard_map.84 = bf16[256,2048]{1,0:T(8,128)(2,1)} custom-call(s32[4]{0:T(128)S(1)} %copy-done.1, f32[8,128]{1,0:T(8,128)S(1)} %shard_map.81.refs_0_, bf16[256,256]{1,0:T(8,128)(2,1)S(1)} %get-tuple-element.153.refs_1_, bf16[256,256]{1,0:T(8,128)(2,1)S(1)} %get-tuple-element.154.refs_2_, bf16[256,256]{1,0:T(8,128)(2,1)S(1)} %collective-permute-done.32.refs_3_, ...), custom_call_target="tpu_custom_call" | custom-call | bytes 4194304 | tf_op jit(solution)/shard_map/pallas_call | solution.py:443
  (47 shorter events, 0.2 us)
Async XLA Ops:
  0.0 16.8 %copy-start.3 = (bf16[1,256,4096]{2,1,0:T(8,128)(2,1)S(1)}, bf16[1,256,4096]{2,1,0:T(8,128)(2,1)}, u32[]{:S(2)}) copy-start(bf16[1,256,4096]{2,1,0:T(8,128)(2,1)} %param.7) | copy-start | bytes 6291460
  0.0 16.7 %collective-permute-start.3 = (bf16[256,4096]{1,0:T(8,128)(2,1)}, bf16[256,4096]{1,0:T(8,128)(2,1)}, u32[]{:S(2)}, u32[]{:S(2)}) collective-permute-start(bf16[256,4096]{1,0:T(8,128)(2,1)} %bitcast.5), channel_id=1, source_target_pairs={{0,4},{1,5},{2,6},{3,7},{4,0},{5,1},{6,2},{7,3},{8,12},{9,13},{10,... | collective-permute-start | bytes 6291464 | tf_op jit(solution)/shard_map/ppermute | solution.py:279
  4.1 2.8 %collective-permute-start = (bf16[144,768]{1,0:T(8,128)(2,1)}, bf16[144,768]{1,0:T(8,128)(2,1)S(1)}, u32[]{:S(2)}, u32[]{:S(2)}) collective-permute-start(bf16[144,768]{1,0:T(8,128)(2,1)} %get-tuple-element.82), channel_id=1, source_target_pairs={{0,4},{1,5},{2,6},{3,7},{4,0},{5,1},{6,2},{7,3},{8,12},{9,13},{10,... | collective-permute-start | bytes 663560 | tf_op jit(solution)/shard_map/ppermute | solution.py:279
  4.3 7.9 %collective-permute-start.2 = (bf16[144,768]{1,0:T(8,128)(2,1)}, bf16[144,768]{1,0:T(8,128)(2,1)S(1)}, u32[]{:S(2)}, u32[]{:S(2)}) collective-permute-start(bf16[144,768]{1,0:T(8,128)(2,1)} %get-tuple-element.84), channel_id=1, source_target_pairs={{0,12},{1,13},{2,14},{3,15},{4,8},{5,9},{6,10},{7,11},{8,4},{9,5},... | collective-permute-start | bytes 663560 | tf_op jit(solution)/shard_map/ppermute | solution.py:279
  5.8 10.9 %collective-permute-start.1 = (bf16[144,768]{1,0:T(8,128)(2,1)}, bf16[144,768]{1,0:T(8,128)(2,1)S(1)}, u32[]{:S(2)}, u32[]{:S(2)}) collective-permute-start(bf16[144,768]{1,0:T(8,128)(2,1)} %get-tuple-element.83), channel_id=1, source_target_pairs={{0,8},{1,9},{2,10},{3,11},{4,12},{5,13},{6,14},{7,15},{8,0},{9,1},... | collective-permute-start | bytes 663560 | tf_op jit(solution)/shard_map/ppermute | solution.py:279
  16.7 50.5 %copy-start.1 = (s32[4]{0:T(128)S(1)}, s32[4]{0:T(128)}, u32[]{:S(2)}) copy-start(s32[4]{0:T(128)} %pad_add_fusion.here_ref) | copy-start | bytes 52
  16.7 10.1 %collective-permute-start.12 = (bf16[256,768]{1,0:T(8,128)(2,1)S(1)}, bf16[256,768]{1,0:T(8,128)(2,1)}, u32[]{:S(2)}, u32[]{:S(2)}) collective-permute-start(bf16[256,768]{1,0:T(8,128)(2,1)S(1)} %pad_maximum_fusion.refs_2_), channel_id=1, source_target_pairs={{0,1},{1,0},{2,3},{3,2},{4,5},{5,4},{6,7},{7,6},{8,9},{9,8},{10,11... | collective-permute-start | bytes 1179656 | tf_op jit(solution)/shard_map/ppermute | solution.py:279
  16.8 55.3 %collective-permute-start.21 = (bf16[256,4096]{1,0:T(8,128)(2,1)S(1)}, bf16[256,4096]{1,0:T(8,128)(2,1)}, u32[]{:S(2)}, u32[]{:S(2)}) collective-permute-start(bf16[256,4096]{1,0:T(8,128)(2,1)S(1)} %bitcast.6), channel_id=1, source_target_pairs={{0,8},{1,9},{2,10},{3,11},{4,12},{5,13},{6,14},{7,15},{8,0},{9,1},... | collective-permute-start | bytes 6291464 | tf_op jit(solution)/shard_map/ppermute | solution.py:279
  18.2 12.6 %collective-permute-start.13 = (bf16[256,768]{1,0:T(8,128)(2,1)S(1)}, bf16[256,768]{1,0:T(8,128)(2,1)}, u32[]{:S(2)}, u32[]{:S(2)}) collective-permute-start(bf16[256,768]{1,0:T(8,128)(2,1)S(1)} %pad_maximum_fusion.refs_2_), channel_id=1, source_target_pairs={{1,2},{2,1},{5,6},{6,5},{9,10},{10,9},{13,14},{14,13},{17,18},{18,... | collective-permute-start | bytes 1179656 | tf_op jit(solution)/shard_map/ppermute | solution.py:279
  22.5 9.5 %collective-permute-start.14 = (bf16[256,768]{1,0:T(8,128)(2,1)S(1)}, bf16[256,768]{1,0:T(8,128)(2,1)S(1)}, u32[]{:S(2)}, u32[]{:S(2)}) collective-permute-start(bf16[256,768]{1,0:T(8,128)(2,1)S(1)} %pad_maximum_fusion.refs_2_), channel_id=1, source_target_pairs={{0,16},{1,17},{2,18},{3,19},{4,20},{5,21},{6,22},{7,23},{8,24},{9,... | collective-permute-start | bytes 1179656 | tf_op jit(solution)/shard_map/ppermute | solution.py:279
  23.8 12.0 %collective-permute-start.4 = (bf16[256,768]{1,0:T(8,128)(2,1)S(1)}, bf16[256,768]{1,0:T(8,128)(2,1)}, u32[]{:S(2)}, u32[]{:S(2)}) collective-permute-start(bf16[256,768]{1,0:T(8,128)(2,1)S(1)} %pad_maximum_fusion.1.refs_9_), channel_id=1, source_target_pairs={{0,1},{1,0},{2,3},{3,2},{4,5},{5,4},{6,7},{7,6},{8,9},{9,8},{10,11... | collective-permute-start | bytes 1179656 | tf_op jit(solution)/shard_map/ppermute | solution.py:279
  26.8 11.5 %collective-permute-start.5 = (bf16[256,768]{1,0:T(8,128)(2,1)S(1)}, bf16[256,768]{1,0:T(8,128)(2,1)}, u32[]{:S(2)}, u32[]{:S(2)}) collective-permute-start(bf16[256,768]{1,0:T(8,128)(2,1)S(1)} %pad_maximum_fusion.1.refs_9_), channel_id=1, source_target_pairs={{1,2},{2,1},{5,6},{6,5},{9,10},{10,9},{13,14},{14,13},{17,18},{18,... | collective-permute-start | bytes 1179656 | tf_op jit(solution)/shard_map/ppermute | solution.py:279
  30.7 8.6 %collective-permute-start.6 = (bf16[256,768]{1,0:T(8,128)(2,1)S(1)}, bf16[256,768]{1,0:T(8,128)(2,1)S(1)}, u32[]{:S(2)}, u32[]{:S(2)}) collective-permute-start(bf16[256,768]{1,0:T(8,128)(2,1)S(1)} %pad_maximum_fusion.1.refs_9_), channel_id=1, source_target_pairs={{0,16},{1,17},{2,18},{3,19},{4,20},{5,21},{6,22},{7,23},{8,24},{9,... | collective-permute-start | bytes 1179656 | tf_op jit(solution)/shard_map/ppermute | solution.py:279
  32.0 0.7 copy-start.4
  32.7 13.8 %collective-permute-start.15 = (bf16[256,768]{1,0:T(8,128)(2,1)}, bf16[256,768]{1,0:T(8,128)(2,1)}, u32[]{:S(2)}, u32[]{:S(2)}) collective-permute-start(bf16[256,768]{1,0:T(8,128)(2,1)} %collective-permute-done.12.refs_3_), channel_id=1, source_target_pairs={{1,2},{2,1},{5,6},{6,5},{9,10},{10,9},{13,14},{14,13},{17,18},{18,... | collective-permute-start | bytes 1179656 | tf_op jit(solution)/shard_map/ppermute | solution.py:279
  35.8 12.8 %collective-permute-start.16 = (bf16[256,768]{1,0:T(8,128)(2,1)}, bf16[256,768]{1,0:T(8,128)(2,1)}, u32[]{:S(2)}, u32[]{:S(2)}) collective-permute-start(bf16[256,768]{1,0:T(8,128)(2,1)} %collective-permute-done.13), channel_id=1, source_target_pairs={{1,0},{2,3},{5,4},{6,7},{9,8},{10,11},{13,12},{14,15},{17,16},{18,... | collective-permute-start | bytes 1179656 | tf_op jit(solution)/shard_map/ppermute | solution.py:279
  38.3 11.6 %collective-permute-start.17 = (bf16[256,768]{1,0:T(8,128)(2,1)}, bf16[256,768]{1,0:T(8,128)(2,1)}, u32[]{:S(2)}, u32[]{:S(2)}) collective-permute-start(bf16[256,768]{1,0:T(8,128)(2,1)} %collective-permute-done.12.refs_3_), channel_id=1, source_target_pairs={{0,16},{1,17},{2,18},{3,19},{4,20},{5,21},{6,22},{7,23},{8,24},{9,... | collective-permute-start | bytes 1179656 | tf_op jit(solution)/shard_map/ppermute | solution.py:279
  39.4 0.7 copy-start.6
  40.1 14.8 %collective-permute-start.7 = (bf16[256,768]{1,0:T(8,128)(2,1)}, bf16[256,768]{1,0:T(8,128)(2,1)}, u32[]{:S(2)}, u32[]{:S(2)}) collective-permute-start(bf16[256,768]{1,0:T(8,128)(2,1)} %collective-permute-done.4.refs_10_), channel_id=1, source_target_pairs={{1,2},{2,1},{5,6},{6,5},{9,10},{10,9},{13,14},{14,13},{17,18},{18,... | collective-permute-start | bytes 1179656 | tf_op jit(solution)/shard_map/ppermute | solution.py:279
  46.5 9.7 %collective-permute-start.8 = (bf16[256,768]{1,0:T(8,128)(2,1)}, bf16[256,768]{1,0:T(8,128)(2,1)}, u32[]{:S(2)}, u32[]{:S(2)}) collective-permute-start(bf16[256,768]{1,0:T(8,128)(2,1)} %collective-permute-done.5), channel_id=1, source_target_pairs={{1,0},{2,3},{5,4},{6,7},{9,8},{10,11},{13,12},{14,15},{17,16},{18,... | collective-permute-start | bytes 1179656 | tf_op jit(solution)/shard_map/ppermute | solution.py:279
  48.6 18.6 %copy-start.5 = (bf16[256,768]{1,0:T(8,128)(2,1)S(1)}, bf16[256,768]{1,0:T(8,128)(2,1)}, u32[]{:S(2)}) copy-start(bf16[256,768]{1,0:T(8,128)(2,1)} %copy-done.4) | copy-start | bytes 1179652
  48.6 18.6 %copy-start.7 = (bf16[256,768]{1,0:T(8,128)(2,1)S(1)}, bf16[256,768]{1,0:T(8,128)(2,1)}, u32[]{:S(2)}) copy-start(bf16[256,768]{1,0:T(8,128)(2,1)} %copy-done.6) | copy-start | bytes 1179652
  48.6 11.1 %collective-permute-start.9 = (bf16[256,768]{1,0:T(8,128)(2,1)}, bf16[256,768]{1,0:T(8,128)(2,1)S(1)}, u32[]{:S(2)}, u32[]{:S(2)}) collective-permute-start(bf16[256,768]{1,0:T(8,128)(2,1)} %collective-permute-done.4.refs_10_), channel_id=1, source_target_pairs={{0,16},{1,17},{2,18},{3,19},{4,20},{5,21},{6,22},{7,23},{8,24},{9,... | collective-permute-start | bytes 1179656 | tf_op jit(solution)/shard_map/ppermute | solution.py:279
  49.8 12.3 %collective-permute-start.18 = (bf16[256,768]{1,0:T(8,128)(2,1)}, bf16[256,768]{1,0:T(8,128)(2,1)S(1)}, u32[]{:S(2)}, u32[]{:S(2)}) collective-permute-start(bf16[256,768]{1,0:T(8,128)(2,1)} %collective-permute-done.15), channel_id=1, source_target_pairs={{1,0},{2,3},{5,4},{6,7},{9,8},{10,11},{13,12},{14,15},{17,16},{18,... | collective-permute-start | bytes 1179656 | tf_op jit(solution)/shard_map/ppermute | solution.py:279
  54.9 11.1 %collective-permute-start.19 = (bf16[256,768]{1,0:T(8,128)(2,1)S(1)}, bf16[256,768]{1,0:T(8,128)(2,1)S(1)}, u32[]{:S(2)}, u32[]{:S(2)}) collective-permute-start(bf16[256,768]{1,0:T(8,128)(2,1)S(1)} %broadcast_select_fusion.2.refs_4_), channel_id=1, source_target_pairs={{0,16},{1,17},{2,18},{3,19},{4,20},{5,21},{6,22},{7,23},{8,24},{9,... | collective-permute-start | bytes 1179656 | tf_op jit(solution)/shard_map/ppermute | solution.py:279
  56.2 9.9 %collective-permute-start.20 = (bf16[256,768]{1,0:T(8,128)(2,1)}, bf16[256,768]{1,0:T(8,128)(2,1)S(1)}, u32[]{:S(2)}, u32[]{:S(2)}) collective-permute-start(bf16[256,768]{1,0:T(8,128)(2,1)} %collective-permute-done.17.refs_7_), channel_id=1, source_target_pairs={{1,2},{2,1},{5,6},{6,5},{9,10},{10,9},{13,14},{14,13},{17,18},{18,... | collective-permute-start | bytes 1179656 | tf_op jit(solution)/shard_map/ppermute | solution.py:279
  59.7 12.4 %collective-permute-start.10 = (bf16[256,768]{1,0:T(8,128)(2,1)}, bf16[256,768]{1,0:T(8,128)(2,1)S(1)}, u32[]{:S(2)}, u32[]{:S(2)}) collective-permute-start(bf16[256,768]{1,0:T(8,128)(2,1)} %collective-permute-done.7), channel_id=1, source_target_pairs={{1,0},{2,3},{5,4},{6,7},{9,8},{10,11},{13,12},{14,15},{17,16},{18,... | collective-permute-start | bytes 1179656 | tf_op jit(solution)/shard_map/ppermute | solution.py:279
  62.1 12.4 %collective-permute-start.11 = (bf16[256,768]{1,0:T(8,128)(2,1)S(1)}, bf16[256,768]{1,0:T(8,128)(2,1)S(1)}, u32[]{:S(2)}, u32[]{:S(2)}) collective-permute-start(bf16[256,768]{1,0:T(8,128)(2,1)S(1)} %broadcast_select_fusion.3.refs_11_), channel_id=1, source_target_pairs={{0,16},{1,17},{2,18},{3,19},{4,20},{5,21},{6,22},{7,23},{8,24},{9,... | collective-permute-start | bytes 1179656 | tf_op jit(solution)/shard_map/ppermute | solution.py:279
  74.5 11.5 %collective-permute-start.24 = (bf16[256,4096]{1,0:T(8,128)(2,1)}, bf16[256,4096]{1,0:T(8,128)(2,1)S(1)}, u32[]{:S(2)}, u32[]{:S(2)}) collective-permute-start(bf16[256,4096]{1,0:T(8,128)(2,1)} %collective-permute-done.21.refs_0_), channel_id=1, source_target_pairs={{0,4},{1,5},{2,6},{3,7},{4,0},{5,1},{6,2},{7,3},{8,12},{9,13},{10,... | collective-permute-start | bytes 6291464 | tf_op jit(solution)/shard_map/ppermute | solution.py:279
  80.8 10.2 %collective-permute-start.22 = (bf16[256,256]{1,0:T(8,128)(2,1)S(1)}, bf16[256,256]{1,0:T(8,128)(2,1)S(1)}, u32[]{:S(2)}, u32[]{:S(2)}) collective-permute-start(bf16[256,256]{1,0:T(8,128)(2,1)S(1)} %slice.28), channel_id=1, source_target_pairs={{1,0},{2,3},{5,4},{6,7},{9,8},{10,11},{13,12},{14,15},{17,16},{18,... | collective-permute-start | bytes 393224 | tf_op jit(solution)/shard_map/ppermute | solution.py:279
  82.1 13.2 %collective-permute-start.26 = (bf16[256,512]{1,0:T(8,128)(2,1)S(1)}, bf16[256,512]{1,0:T(8,128)(2,1)S(1)}, u32[]{:S(2)}, u32[]{:S(2)}) collective-permute-start(bf16[256,512]{1,0:T(8,128)(2,1)S(1)} %slice.30), channel_id=1, source_target_pairs={{1,0},{2,3},{5,4},{6,7},{9,8},{10,11},{13,12},{14,15},{17,16},{18,... | collective-permute-start | bytes 786440 | tf_op jit(solution)/shard_map/ppermute | solution.py:279
  84.5 6.4 %copy-start = (bf16[144,768]{1,0:T(8,128)(2,1)S(1)}, bf16[144,768]{1,0:T(8,128)(2,1)}, u32[]{:S(2)}) copy-start(bf16[144,768]{1,0:T(8,128)(2,1)} %get-tuple-element.81.refs_13_.refs_12_.refs_8_.refs_5_) | copy-start | bytes 663556
  84.5 6.4 %collective-permute-start.23 = (bf16[256,256]{1,0:T(8,128)(2,1)S(1)}, bf16[256,256]{1,0:T(8,128)(2,1)S(1)}, u32[]{:S(2)}, u32[]{:S(2)}) collective-permute-start(bf16[256,256]{1,0:T(8,128)(2,1)S(1)} %slice.35), channel_id=1, source_target_pairs={{0,16},{1,17},{2,18},{3,19},{4,20},{5,21},{6,22},{7,23},{8,24},{9,... | collective-permute-start | bytes 393224 | tf_op jit(solution)/shard_map/ppermute | solution.py:279
  85.9 9.5 %collective-permute-start.27 = (bf16[256,512]{1,0:T(8,128)(2,1)S(1)}, bf16[256,512]{1,0:T(8,128)(2,1)S(1)}, u32[]{:S(2)}, u32[]{:S(2)}) collective-permute-start(bf16[256,512]{1,0:T(8,128)(2,1)S(1)} %slice.36), channel_id=1, source_target_pairs={{0,16},{1,17},{2,18},{3,19},{4,20},{5,21},{6,22},{7,23},{8,24},{9,... | collective-permute-start | bytes 786440 | tf_op jit(solution)/shard_map/ppermute | solution.py:279
  92.7 4.8 %collective-permute-start.25 = (bf16[128,256]{1,0:T(8,128)(2,1)S(1)}, bf16[128,256]{1,0:T(8,128)(2,1)S(1)}, u32[]{:S(2)}, u32[]{:S(2)}) collective-permute-start(bf16[128,256]{1,0:T(8,128)(2,1)S(1)} %get-tuple-element.120), channel_id=1, source_target_pairs={{0,16},{1,17},{2,18},{3,19},{4,20},{5,21},{6,22},{7,23},{8,24},{9,... | collective-permute-start | bytes 196616 | tf_op jit(solution)/shard_map/ppermute | solution.py:279
  95.3 2.1 %copy-start.2 = (f32[16]{0:T(128)S(1)}, f32[16]{0:T(128)}, u32[]{:S(2)}) copy-start(f32[16]{0:T(128)} %gate_ref.5) | copy-start | bytes 196
  98.6 10.8 %collective-permute-start.28 = (bf16[256,256]{1,0:T(8,128)(2,1)S(1)}, bf16[256,256]{1,0:T(8,128)(2,1)S(1)}, u32[]{:S(2)}, u32[]{:S(2)}) collective-permute-start(bf16[256,256]{1,0:T(8,128)(2,1)S(1)} %get-tuple-element.134), channel_id=1, source_target_pairs={{0,8},{1,9},{2,10},{3,11},{4,12},{5,13},{6,14},{7,15},{8,0},{9,1},... | collective-permute-start | bytes 393224 | tf_op jit(solution)/shard_map/ppermute | solution.py:279
  99.0 10.9 %collective-permute-start.30 = (bf16[256,256]{1,0:T(8,128)(2,1)S(1)}, bf16[256,256]{1,0:T(8,128)(2,1)S(1)}, u32[]{:S(2)}, u32[]{:S(2)}) collective-permute-start(bf16[256,256]{1,0:T(8,128)(2,1)S(1)} %get-tuple-element.135), channel_id=1, source_target_pairs={{0,12},{1,13},{2,14},{3,15},{4,8},{5,9},{6,10},{7,11},{8,4},{9,5},... | collective-permute-start | bytes 393224 | tf_op jit(solution)/shard_map/ppermute | solution.py:279
  104.3 5.6 %collective-permute-start.29 = (bf16[256,256]{1,0:T(8,128)(2,1)S(1)}, bf16[256,256]{1,0:T(8,128)(2,1)S(1)}, u32[]{:S(2)}, u32[]{:S(2)}) collective-permute-start(bf16[256,256]{1,0:T(8,128)(2,1)S(1)} %get-tuple-element.141), channel_id=1, source_target_pairs={{0,8},{1,9},{2,10},{3,11},{4,12},{5,13},{6,14},{7,15},{8,0},{9,1},... | collective-permute-start | bytes 393224 | tf_op jit(solution)/shard_map/ppermute | solution.py:279
  104.6 8.0 %collective-permute-start.31 = (bf16[256,256]{1,0:T(8,128)(2,1)S(1)}, bf16[256,256]{1,0:T(8,128)(2,1)S(1)}, u32[]{:S(2)}, u32[]{:S(2)}) collective-permute-start(bf16[256,256]{1,0:T(8,128)(2,1)S(1)} %get-tuple-element.142), channel_id=1, source_target_pairs={{0,12},{1,13},{2,14},{3,15},{4,8},{5,9},{6,10},{7,11},{8,4},{9,5},... | collective-permute-start | bytes 393224 | tf_op jit(solution)/shard_map/ppermute | solution.py:279
  108.4 4.3 %collective-permute-start.32 = (bf16[256,256]{1,0:T(8,128)(2,1)S(1)}, bf16[256,256]{1,0:T(8,128)(2,1)S(1)}, u32[]{:S(2)}, u32[]{:S(2)}) collective-permute-start(bf16[256,256]{1,0:T(8,128)(2,1)S(1)} %get-tuple-element.155), channel_id=1, source_target_pairs={{0,4},{1,5},{2,6},{3,7},{4,0},{5,1},{6,2},{7,3},{8,12},{9,13},{10,... | collective-permute-start | bytes 393224 | tf_op jit(solution)/shard_map/ppermute | solution.py:279
  109.5 3.2 %collective-permute-start.33 = (bf16[256,256]{1,0:T(8,128)(2,1)S(1)}, bf16[256,256]{1,0:T(8,128)(2,1)S(1)}, u32[]{:S(2)}, u32[]{:S(2)}) collective-permute-start(bf16[256,256]{1,0:T(8,128)(2,1)S(1)} %get-tuple-element.156), channel_id=1, source_target_pairs={{0,4},{1,5},{2,6},{3,7},{4,0},{5,1},{6,2},{7,3},{8,12},{9,13},{10,... | collective-permute-start | bytes 393224 | tf_op jit(solution)/shard_map/ppermute | solution.py:279

commit v15 on v14

--- a/solution.py
+++ b/solution.py
@@ -118,7 +118,7 @@
         chosen_ref[...] = outer[:, at]
 
     rows = [piece[:, start : start + width] for piece in whole]
-    return jnp.concatenate(rows + [chosen_ref[...], part[:, at]], axis=0)
+    return jnp.concatenate(rows + [chosen_ref[...], part[...]], axis=0)
 
 
 def kv_body(n_late, here_ref, *refs):
@@ -367,7 +367,7 @@
         pieces = [b_three, b_far2]
         outer_kv, outer_q = [outward(a_inner[:, at]) for at in (slice(0, cut), slice(cut, None))]
         inner = a_inner
-        finish = lambda at: over(b_three[:, at])
+        finish = lambda at, *others: over(after(b_three[:, at], *others))
     else:
         across, sibling = to_member(tokens[0], 2), to_member(tokens[0], 1)
         books = [tokens[0], sibling, across, to_member(across, 1)]
@@ -383,10 +383,10 @@
         pieces = [lower[-2]]
         outer_kv, outer_q = upper[-1][:, :cut], upper[-1][:, cut:]
         inner = upper[-1]
-        finish = lambda at: lower[-1][:, at]
+        finish = lambda at, *others: lower[-1][:, at]
 
     halves = [slice(k * HEAD_SIZE, (k + 2) * HEAD_SIZE) for k in (0, 2, 4)]
-    lower_kv, lower_q = finish(slice(0, cut)), finish(slice(cut, None))
+    lower_kv, lower_q0 = finish(halves[0]), finish(halves[1])
     found = call(
         functools.partial(kv_body, len(late) + 1),
         [shape((length, 2 * HEAD_SIZE), bf16), shape((HEAD_SIZE, 2 * HEAD_SIZE), f32)] * MEMBERS
@@ -406,14 +406,14 @@
 
     half = group // 2
 
-    def local(segs, part, *others):
+    def local(segs, part, lower_q):
         found = call(
             functools.partial(local_body, len(segs), len(late) + 1, halves[1 + part].start, half),
             [shape((length, half * HEAD_SIZE), bf16), shape((length, half * HEAD_SIZE), f32)] * len(segs),
             [SMEM] + [VMEM] * (len(late) + 1 + 4 * len(segs)),
             flops=4 * len(segs) * length * length * half * HEAD_SIZE,
             scratch=[pltpu.VMEM((MEMBERS * HEAD_SIZE // 2, half * HEAD_SIZE), bf16)],
-        )(here, *pieces, inner, outer_q, after(lower_q, *others), *[one[s] for one in (kvs, messages, sums, lates) for s in segs])
+        )(here, *pieces, inner, outer_q, lower_q, *[one[s] for one in (kvs, messages, sums, lates) for s in segs])
         return {(s, part): (found[2 * at], found[2 * at + 1]) for at, s in enumerate(segs)}
 
     def mix(segs, parts, base, ready):
@@ -428,12 +428,13 @@
             *[ready[key][0] for key in keys], *[ready[key][1] for key in keys],
         )
 
-    ready = local((2, 3, 1, 0), 0)
+    ready = local((2, 3, 1, 0), 0, lower_q0)
     base = after(base, *ready[2, 0])
+    lower_q1 = finish(halves[2], base)
     two0, three0 = mix((2, 3), (0,), base, ready)
-    ready |= local((2, 3), 1, two0, three0)
+    ready |= local((2, 3), 1, after(lower_q1, two0, three0))
     two1, three1 = mix((2, 3), (1,), base, ready)
-    ready |= local((1, 0), 1, two1, three1)
+    ready |= local((1, 0), 1, after(lower_q1, two1, three1))
     one0, one1, mine0, mine1 = mix((1, 0), (0, 1), after(base, two1, three1), ready)
     sent = [mine0, mine1]
     for k, parts in ((1, (one0, one1)), (2, (two0, two1)), (3, (three0, three1))):

time: 115 us -> 118 us (1.026)
  starting transfers between devices: 52.4 us -> 59 us
  waiting for transfers between devices: 28.7 us -> 24.9 us
    ppermute x34 -> x35, starting transfers between devices: 52.4 us -> 59 us  [permute(): return lax.ppermute(array, AXES, pairs)]
    ppermute x34 -> x35, waiting for transfers between devices: 28.7 us -> 24.9 us  [permute(): return lax.ppermute(array, AXES, pairs)]
  transfers between devices with their start and end apart: 34 -> 35, of which waited for: 11 -> 11; matrix products, arithmetic and copies ran while one was open for 5% -> 5% of each run, Pallas kernels for 19% -> 20%
where the time goes in v15:
time: 118 us; the launch traced here: 117 us
  starting transfers between devices  59 us (50%)
  waiting for transfers between devices  24.9 us (21%)
  Pallas kernels  24.7 us (21%)
  other arithmetic  4.85 us (4%)
  local copies, waits for them, and re-layouts  2.56 us (2%)
    ppermute x35, starting transfers between devices, permute(): return lax.ppermute(array, AXES, pairs)  59 us
    ppermute x35, waiting for transfers between devices, permute(): return lax.ppermute(array, AXES, pairs)  24.9 us
    pallas_call x2, Pallas kernels, project(): call(functools.partial(project_body, early, late, line), [shape((length,...  9.76 us
    pallas_call x3, Pallas kernels, local(): call(functools.partial(local_body, len(segs), len(late) + 1, halves[1 + p...  5.49 us
    pallas_call x3, Pallas kernels, mix(): call(functools.partial(mix_body, segs, parts, group), [shape((length, hal...  3.97 us
  transfers between devices with their start and end apart: 35, of which 11 were waited for; matrix products, arithmetic and copies ran while one was open for 5% of the time, Pallas kernels for 20%

profile of v15, /device:TPU:9, one launch (start us, length us, event | category | flops | bytes accessed | tf_op | source)
XLA Modules:
  0.0 117.1 jit_solution(3546794396608814857)
XLA Ops:
  0.0 0.7 collective-permute-start.3
  1.3 0.6 pad_add_fusion.here_ref
  1.9 2.1 %shard_map.73 = (bf16[144,768]{1,0:T(8,128)(2,1)}, bf16[144,768]{1,0:T(8,128)(2,1)}, bf16[144,768]{1,0:T(8,128)(2,1)}, bf16[144,768]{1,0:T(8,128)(2,1)}) custom-call(s32[4]{0:T(128)} %pad_add_fusion.here_ref, s32[1,1]{1,0:T(1,128)S(6)} %copy.8.valid_ref, s32[1,1,2,2]{3,2,1,0:T(2,128)} %mask_ref.1, bf16[128,2048]{1,0:T(8,128)(2,1)} %wq_ref.1, ...), custom_call_target="tpu_custom_call" | custom-call | bytes 4194304 | tf_op jit(solution)/shard_map/pallas_call | solution.py:285
  4.0 1.2 %collective-permute-start.1 = (bf16[144,768]{1,0:T(8,128)(2,1)}, bf16[144,768]{1,0:T(8,128)(2,1)S(1)}, u32[]{:S(2)}, u32[]{:S(2)}) collective-permute-start(bf16[144,768]{1,0:T(8,128)(2,1)} %get-tuple-element.84), channel_id=1, source_target_pairs={{0,8},{1,9},{2,10},{3,11},{4,12},{5,13},{6,14},{7,15},{8,0},{9,1},... | collective-permute-start | bytes 663560 | tf_op jit(solution)/shard_map/ppermute | solution.py:279
  5.2 0.6 collective-permute-start.2
  5.8 0.1 collective-permute-start
  5.9 0.9 slice.27
  6.8 4.3 %collective-permute-done.1.refs_15_.refs_9_.refs_4_.refs_7_ = bf16[144,768]{1,0:T(8,128)(2,1)S(1)} collective-permute-done((bf16[144,768]{1,0:T(8,128)(2,1)}, bf16[144,768]{1,0:T(8,128)(2,1)S(1)}, u32[]{:S(2)}, u32[]{:S(2)}) %collective-permute-start.1) | collective-permute-done | bytes 221216 | tf_op jit(solution)/shard_map/ppermute | solution.py:279
  11.1 5.0 %collective-permute-done.2.refs_16_.refs_10_.refs_5_.refs_8_ = bf16[144,768]{1,0:T(8,128)(2,1)S(1)} collective-permute-done((bf16[144,768]{1,0:T(8,128)(2,1)}, bf16[144,768]{1,0:T(8,128)(2,1)S(1)}, u32[]{:S(2)}, u32[]{:S(2)}) %collective-permute-start.2) | collective-permute-done | bytes 221216 | tf_op jit(solution)/shard_map/ppermute | solution.py:279
  16.3 0.1 collective-permute-start.12
  16.4 1.4 %collective-permute-start.21 = (bf16[256,4096]{1,0:T(8,128)(2,1)S(1)}, bf16[256,4096]{1,0:T(8,128)(2,1)}, u32[]{:S(2)}, u32[]{:S(2)}) collective-permute-start(bf16[256,4096]{1,0:T(8,128)(2,1)S(1)} %bitcast.6), channel_id=1, source_target_pairs={{0,8},{1,9},{2,10},{3,11},{4,12},{5,13},{6,14},{7,15},{8,0},{9,1},... | collective-permute-start | bytes 6291464 | tf_op jit(solution)/shard_map/ppermute | solution.py:279
  17.8 4.3 %collective-permute-start.13 = (bf16[256,768]{1,0:T(8,128)(2,1)S(1)}, bf16[256,768]{1,0:T(8,128)(2,1)}, u32[]{:S(2)}, u32[]{:S(2)}) collective-permute-start(bf16[256,768]{1,0:T(8,128)(2,1)S(1)} %pad_maximum_fusion.refs_2_), channel_id=1, source_target_pairs={{1,2},{2,1},{5,6},{6,5},{9,10},{10,9},{13,14},{14,13},{17,18},{18,... | collective-permute-start | bytes 1179656 | tf_op jit(solution)/shard_map/ppermute | solution.py:279
  22.1 1.3 %collective-permute-start.14 = (bf16[256,768]{1,0:T(8,128)(2,1)S(1)}, bf16[256,768]{1,0:T(8,128)(2,1)S(1)}, u32[]{:S(2)}, u32[]{:S(2)}) collective-permute-start(bf16[256,768]{1,0:T(8,128)(2,1)S(1)} %pad_maximum_fusion.refs_2_), channel_id=1, source_target_pairs={{0,16},{1,17},{2,18},{3,19},{4,20},{5,21},{6,22},{7,23},{8,24},{9,... | collective-permute-start | bytes 1179656 | tf_op jit(solution)/shard_map/ppermute | solution.py:279
  23.4 3.7 %collective-permute-done.12.refs_3_ = bf16[256,768]{1,0:T(8,128)(2,1)} collective-permute-done((bf16[256,768]{1,0:T(8,128)(2,1)S(1)}, bf16[256,768]{1,0:T(8,128)(2,1)}, u32[]{:S(2)}, u32[]{:S(2)}) %collective-permute-start.12) | collective-permute-done | bytes 393248 | tf_op jit(solution)/shard_map/ppermute | solution.py:279
  27.1 3.2 %collective-permute-start.5 = (bf16[256,768]{1,0:T(8,128)(2,1)S(1)}, bf16[256,768]{1,0:T(8,128)(2,1)}, u32[]{:S(2)}, u32[]{:S(2)}) collective-permute-start(bf16[256,768]{1,0:T(8,128)(2,1)S(1)} %pad_maximum_fusion.1.refs_9_), channel_id=1, source_target_pairs={{1,2},{2,1},{5,6},{6,5},{9,10},{10,9},{13,14},{14,13},{17,18},{18,... | collective-permute-start | bytes 1179656 | tf_op jit(solution)/shard_map/ppermute | solution.py:279
  30.3 0.7 collective-permute-done.13
  31.1 1.2 %collective-permute-start.6 = (bf16[256,768]{1,0:T(8,128)(2,1)S(1)}, bf16[256,768]{1,0:T(8,128)(2,1)S(1)}, u32[]{:S(2)}, u32[]{:S(2)}) collective-permute-start(bf16[256,768]{1,0:T(8,128)(2,1)S(1)} %pad_maximum_fusion.1.refs_9_), channel_id=1, source_target_pairs={{0,16},{1,17},{2,18},{3,19},{4,20},{5,21},{6,22},{7,23},{8,24},{9,... | collective-permute-start | bytes 1179656 | tf_op jit(solution)/shard_map/ppermute | solution.py:279
  32.3 0.7 copy-done.4
  33.1 3.0 %collective-permute-start.15 = (bf16[256,768]{1,0:T(8,128)(2,1)}, bf16[256,768]{1,0:T(8,128)(2,1)}, u32[]{:S(2)}, u32[]{:S(2)}) collective-permute-start(bf16[256,768]{1,0:T(8,128)(2,1)} %collective-permute-done.12.refs_3_), channel_id=1, source_target_pairs={{1,2},{2,1},{5,6},{6,5},{9,10},{10,9},{13,14},{14,13},{17,18},{18,... | collective-permute-start | bytes 1179656 | tf_op jit(solution)/shard_map/ppermute | solution.py:279
  36.1 2.1 %collective-permute-start.16 = (bf16[256,768]{1,0:T(8,128)(2,1)}, bf16[256,768]{1,0:T(8,128)(2,1)}, u32[]{:S(2)}, u32[]{:S(2)}) collective-permute-start(bf16[256,768]{1,0:T(8,128)(2,1)} %collective-permute-done.13), channel_id=1, source_target_pairs={{1,0},{2,3},{5,4},{6,7},{9,8},{10,11},{13,12},{14,15},{17,16},{18,... | collective-permute-start | bytes 1179656 | tf_op jit(solution)/shard_map/ppermute | solution.py:279
  38.2 0.2 collective-permute-done.5
  38.4 1.2 %collective-permute-start.17 = (bf16[256,768]{1,0:T(8,128)(2,1)}, bf16[256,768]{1,0:T(8,128)(2,1)}, u32[]{:S(2)}, u32[]{:S(2)}) collective-permute-start(bf16[256,768]{1,0:T(8,128)(2,1)} %collective-permute-done.12.refs_3_), channel_id=1, source_target_pairs={{0,16},{1,17},{2,18},{3,19},{4,20},{5,21},{6,22},{7,23},{8,24},{9,... | collective-permute-start | bytes 1179656 | tf_op jit(solution)/shard_map/ppermute | solution.py:279
  39.7 0.9 collective-permute-done.6.refs_12_
  40.6 0.7 copy-done.6
  41.3 3.4 %collective-permute-start.7 = (bf16[256,768]{1,0:T(8,128)(2,1)}, bf16[256,768]{1,0:T(8,128)(2,1)}, u32[]{:S(2)}, u32[]{:S(2)}) collective-permute-start(bf16[256,768]{1,0:T(8,128)(2,1)} %collective-permute-done.4.refs_10_), channel_id=1, source_target_pairs={{1,2},{2,1},{5,6},{6,5},{9,10},{10,9},{13,14},{14,13},{17,18},{18,... | collective-permute-start | bytes 1179656 | tf_op jit(solution)/shard_map/ppermute | solution.py:279
  44.8 2.1 %collective-permute-done.15 = bf16[256,768]{1,0:T(8,128)(2,1)} collective-permute-done((bf16[256,768]{1,0:T(8,128)(2,1)}, bf16[256,768]{1,0:T(8,128)(2,1)}, u32[]{:S(2)}, u32[]{:S(2)}) %collective-permute-start.15) | collective-permute-done | bytes 393248 | tf_op jit(solution)/shard_map/ppermute | solution.py:279
  46.9 2.1 %collective-permute-start.8 = (bf16[256,768]{1,0:T(8,128)(2,1)}, bf16[256,768]{1,0:T(8,128)(2,1)}, u32[]{:S(2)}, u32[]{:S(2)}) collective-permute-start(bf16[256,768]{1,0:T(8,128)(2,1)} %collective-permute-done.5), channel_id=1, source_target_pairs={{1,0},{2,3},{5,4},{6,7},{9,8},{10,11},{13,12},{14,15},{17,16},{18,... | collective-permute-start | bytes 1179656 | tf_op jit(solution)/shard_map/ppermute | solution.py:279
  48.9 1.2 %collective-permute-start.9 = (bf16[256,768]{1,0:T(8,128)(2,1)}, bf16[256,768]{1,0:T(8,128)(2,1)S(1)}, u32[]{:S(2)}, u32[]{:S(2)}) collective-permute-start(bf16[256,768]{1,0:T(8,128)(2,1)} %collective-permute-done.4.refs_10_), channel_id=1, source_target_pairs={{0,16},{1,17},{2,18},{3,19},{4,20},{5,21},{6,22},{7,23},{8,24},{9,... | collective-permute-start | bytes 1179656 | tf_op jit(solution)/shard_map/ppermute | solution.py:279
  50.2 1.0 broadcast_select_fusion.2.refs_4_
  51.2 0.3 collective-permute-start.19
  51.5 3.8 %collective-permute-done.7 = bf16[256,768]{1,0:T(8,128)(2,1)} collective-permute-done((bf16[256,768]{1,0:T(8,128)(2,1)}, bf16[256,768]{1,0:T(8,128)(2,1)}, u32[]{:S(2)}, u32[]{:S(2)}) %collective-permute-start.7) | collective-permute-done | bytes 393248 | tf_op jit(solution)/shard_map/ppermute | solution.py:279
  55.3 1.3 %collective-permute-start.18 = (bf16[256,768]{1,0:T(8,128)(2,1)}, bf16[256,768]{1,0:T(8,128)(2,1)S(1)}, u32[]{:S(2)}, u32[]{:S(2)}) collective-permute-start(bf16[256,768]{1,0:T(8,128)(2,1)} %collective-permute-done.15), channel_id=1, source_target_pairs={{1,0},{2,3},{5,4},{6,7},{9,8},{10,11},{13,12},{14,15},{17,16},{18,... | collective-permute-start | bytes 1179656 | tf_op jit(solution)/shard_map/ppermute | solution.py:279
  56.6 3.5 %collective-permute-start.20 = (bf16[256,768]{1,0:T(8,128)(2,1)}, bf16[256,768]{1,0:T(8,128)(2,1)S(1)}, u32[]{:S(2)}, u32[]{:S(2)}) collective-permute-start(bf16[256,768]{1,0:T(8,128)(2,1)} %collective-permute-done.17.refs_7_), channel_id=1, source_target_pairs={{1,2},{2,1},{5,6},{6,5},{9,10},{10,9},{13,14},{14,13},{17,18},{18,... | collective-permute-start | bytes 1179656 | tf_op jit(solution)/shard_map/ppermute | solution.py:279
  60.1 1.1 broadcast_select_fusion.3.refs_11_
  61.2 1.3 %collective-permute-start.11 = (bf16[256,768]{1,0:T(8,128)(2,1)S(1)}, bf16[256,768]{1,0:T(8,128)(2,1)S(1)}, u32[]{:S(2)}, u32[]{:S(2)}) collective-permute-start(bf16[256,768]{1,0:T(8,128)(2,1)S(1)} %broadcast_select_fusion.3.refs_11_), channel_id=1, source_target_pairs={{0,16},{1,17},{2,18},{3,19},{4,20},{5,21},{6,22},{7,23},{8,24},{9,... | collective-permute-start | bytes 1179656 | tf_op jit(solution)/shard_map/ppermute | solution.py:279
  62.5 1.7 %collective-permute-done.19.refs_8_ = bf16[256,768]{1,0:T(8,128)(2,1)S(1)} collective-permute-done((bf16[256,768]{1,0:T(8,128)(2,1)S(1)}, bf16[256,768]{1,0:T(8,128)(2,1)S(1)}, u32[]{:S(2)}, u32[]{:S(2)}) %collective-permute-start.19) | collective-permute-done | bytes 393248 | tf_op jit(solution)/shard_map/ppermute | solution.py:279
  64.2 2.8 %collective-permute-start.10 = (bf16[256,768]{1,0:T(8,128)(2,1)}, bf16[256,768]{1,0:T(8,128)(2,1)S(1)}, u32[]{:S(2)}, u32[]{:S(2)}) collective-permute-start(bf16[256,768]{1,0:T(8,128)(2,1)} %collective-permute-done.7), channel_id=1, source_target_pairs={{1,0},{2,3},{5,4},{6,7},{9,8},{10,11},{13,12},{14,15},{17,16},{18,... | collective-permute-start | bytes 1179656 | tf_op jit(solution)/shard_map/ppermute | solution.py:279
  67.0 0.4 collective-permute-done.20.refs_2_
  67.4 1.1 broadcast_select_fusion.1.refs_5_
  68.5 4.9 %shard_map.74 = (f32[256,768]{1,0:T(8,128)S(1)}, f32[256,768]{1,0:T(8,128)S(1)}, bf16[256,1024]{1,0:T(8,128)(2,1)S(1)}, bf16[256,1024]{1,0:T(8,128)(2,1)S(1)}) custom-call(s32[4]{0:T(128)S(1)} %copy-done.1, bf16[256,4096]{1,0:T(8,128)(2,1)S(1)} %bitcast.7, bf16[256,4096]{1,0:T(8,128)(2,1)} %collective-permute-done.3.refs_1_, ...), custom_call_target="tpu_custom_call" | custom-call | flops 2415919104 | bytes 4194304 | tf_op jit(solution)/shard_map/pallas_call | solution.py:317
  73.4 7.3 %collective-permute-start.24 = (bf16[256,4096]{1,0:T(8,128)(2,1)}, bf16[256,4096]{1,0:T(8,128)(2,1)S(1)}, u32[]{:S(2)}, u32[]{:S(2)}) collective-permute-start(bf16[256,4096]{1,0:T(8,128)(2,1)} %collective-permute-done.21.refs_0_), channel_id=1, source_target_pairs={{0,4},{1,5},{2,6},{3,7},{4,0},{5,1},{6,2},{7,3},{8,12},{9,13},{10,... | collective-permute-start | bytes 6291464 | tf_op jit(solution)/shard_map/ppermute | solution.py:279
  80.8 3.5 %collective-permute-start.22 = (bf16[256,256]{1,0:T(8,128)(2,1)S(1)}, bf16[256,256]{1,0:T(8,128)(2,1)S(1)}, u32[]{:S(2)}, u32[]{:S(2)}) collective-permute-start(bf16[256,256]{1,0:T(8,128)(2,1)S(1)} %slice.31), channel_id=1, source_target_pairs={{1,0},{2,3},{5,4},{6,7},{9,8},{10,11},{13,12},{14,15},{17,16},{18,... | collective-permute-start | bytes 393224 | tf_op jit(solution)/shard_map/ppermute | solution.py:279
  84.2 1.3 %collective-permute-start.26 = (bf16[256,512]{1,0:T(8,128)(2,1)S(1)}, bf16[256,512]{1,0:T(8,128)(2,1)S(1)}, u32[]{:S(2)}, u32[]{:S(2)}) collective-permute-start(bf16[256,512]{1,0:T(8,128)(2,1)S(1)} %slice.33), channel_id=1, source_target_pairs={{1,0},{2,3},{5,4},{6,7},{9,8},{10,11},{13,12},{14,15},{17,16},{18,... | collective-permute-start | bytes 786440 | tf_op jit(solution)/shard_map/ppermute | solution.py:279
  85.5 1.1 broadcast_select_fusion.refs_0_
  86.7 1.3 %collective-permute-start.23 = (bf16[256,256]{1,0:T(8,128)(2,1)S(1)}, bf16[256,256]{1,0:T(8,128)(2,1)S(1)}, u32[]{:S(2)}, u32[]{:S(2)}) collective-permute-start(bf16[256,256]{1,0:T(8,128)(2,1)S(1)} %get-tuple-element.161), channel_id=1, source_target_pairs={{0,16},{1,17},{2,18},{3,19},{4,20},{5,21},{6,22},{7,23},{8,24},{9,... | collective-permute-start | bytes 393224 | tf_op jit(solution)/shard_map/ppermute | solution.py:279
  88.0 0.2 collective-permute-start.27
  88.2 4.9 %shard_map.75 = (f32[256,768]{1,0:T(8,128)S(1)}, f32[256,768]{1,0:T(8,128)S(1)}, bf16[256,1024]{1,0:T(8,128)(2,1)S(1)}, bf16[256,1024]{1,0:T(8,128)(2,1)S(1)}) custom-call(s32[4]{0:T(128)S(1)} %copy-done.1, bf16[256,4096]{1,0:T(8,128)(2,1)} %collective-permute-done.21.refs_0_, bf16[256,4096]{1,0:T(8,128)(2,1)S(1)} %collective-permute-done.24.refs_1_, ...), custom_call_target="tpu_custom_call" | custom-call | flops 2415919104 | bytes 4194304 | tf_op jit(solution)/shard_map/pallas_call | solution.py:317
  93.1 1.7 %shard_map.76 = (bf16[256,256]{1,0:T(8,128)(2,1)S(1)}, f32[128,256]{1,0:T(8,128)S(1)}, bf16[256,256]{1,0:T(8,128)(2,1)S(1)}, f32[128,256]{1,0:T(8,128)S(1)}, bf1...) custom-call(s32[4]{0:T(128)S(1)} %copy-done.1, ...), custom_call_target="tpu_custom_call" | custom-call | flops 536870912 | bytes 4194304 | tf_op jit(solution)/shard_map/pallas_call | solution.py:390
  94.8 1.3 %collective-permute-start.25 = (bf16[128,256]{1,0:T(8,128)(2,1)S(1)}, bf16[128,256]{1,0:T(8,128)(2,1)S(1)}, u32[]{:S(2)}, u32[]{:S(2)}) collective-permute-start(bf16[128,256]{1,0:T(8,128)(2,1)S(1)} %get-tuple-element.121), channel_id=1, source_target_pairs={{0,16},{1,17},{2,18},{3,19},{4,20},{5,21},{6,22},{7,23},{8,24},{9,... | collective-permute-start | bytes 196616 | tf_op jit(solution)/shard_map/ppermute | solution.py:279
  96.1 2.1 %shard_map.77 = (bf16[256,256]{1,0:T(8,128)(2,1)S(1)}, f32[256,256]{1,0:T(8,128)S(1)}, bf16[256,256]{1,0:T(8,128)(2,1)S(1)}, f32[256,256]{1,0:T(8,128)S(1)}, bf1...) custom-call(s32[4]{0:T(128)S(1)} %copy-done.1, ...), custom_call_target="tpu_custom_call" | custom-call | flops 268435456 | bytes 4194304 | tf_op jit(solution)/shard_map/pallas_call | solution.py:410
  98.3 0.9 collective-permute-start.29
  99.2 1.2 %shard_map.78 = (bf16[256,256]{1,0:T(8,128)(2,1)S(1)}, bf16[256,256]{1,0:T(8,128)(2,1)S(1)}) custom-call(s32[4]{0:T(128)S(1)} %copy-done.1, f32[16]{0:T(128)S(1)} %copy-done.2, bf16[128,256]{1,0:T(8,128)(2,1)S(1)} %collective-permute-done.25.base_ref, f32[128,256]{1,0:T(8,128)S(1)} %get-tuple-element.129.refs_0_, f32[128,256]{1,0:T(8,128)S(1)} %get-tuple-element.130.refs_1_, ...), custom_call_target="tpu_custom_call" | custom-call | flops 201326592 | bytes 4194304 | tf_op jit(solution)/shard_map/pallas_call | solution.py:421
  100.4 1.2 %collective-permute-start.28 = (bf16[256,256]{1,0:T(8,128)(2,1)S(1)}, bf16[256,256]{1,0:T(8,128)(2,1)S(1)}, u32[]{:S(2)}, u32[]{:S(2)}) collective-permute-start(bf16[256,256]{1,0:T(8,128)(2,1)S(1)} %get-tuple-element.135), channel_id=1, source_target_pairs={{0,8},{1,9},{2,10},{3,11},{4,12},{5,13},{6,14},{7,15},{8,0},{9,1},... | collective-permute-start | bytes 393224 | tf_op jit(solution)/shard_map/ppermute | solution.py:279
  101.7 2.7 %collective-permute-start.31 = (bf16[256,256]{1,0:T(8,128)(2,1)S(1)}, bf16[256,256]{1,0:T(8,128)(2,1)S(1)}, u32[]{:S(2)}, u32[]{:S(2)}) collective-permute-start(bf16[256,256]{1,0:T(8,128)(2,1)S(1)} %get-tuple-element.137), channel_id=1, source_target_pairs={{0,12},{1,13},{2,14},{3,15},{4,8},{5,9},{6,10},{7,11},{8,4},{9,5},... | collective-permute-start | bytes 393224 | tf_op jit(solution)/shard_map/ppermute | solution.py:279
  104.4 1.8 %shard_map.79 = (bf16[256,256]{1,0:T(8,128)(2,1)S(1)}, f32[256,256]{1,0:T(8,128)S(1)}, bf16[256,256]{1,0:T(8,128)(2,1)S(1)}, f32[256,256]{1,0:T(8,128)S(1)}) custom-call(s32[4]{0:T(128)S(1)} %copy-done.1, bf16[256,768]{1,0:T(8,128)(2,1)S(1)} %broadcast_select_fusion.refs_0_, bf16[256,768]{1,0:T(8,128)(2,1)S(1)} %collective-permute-done.11.refs_1_, ...), custom_call_target="tpu_custom_call" | custom-call | flops 134217728 | bytes 4194304 | tf_op jit(solution)/shard_map/pallas_call | solution.py:410
  106.1 1.2 %shard_map.80 = (bf16[256,256]{1,0:T(8,128)(2,1)S(1)}, bf16[256,256]{1,0:T(8,128)(2,1)S(1)}) custom-call(s32[4]{0:T(128)S(1)} %copy-done.1, f32[16]{0:T(128)S(1)} %copy-done.2, bf16[128,256]{1,0:T(8,128)(2,1)S(1)} %collective-permute-done.25.base_ref, f32[128,256]{1,0:T(8,128)S(1)} %get-tuple-element.129.refs_0_, f32[128,256]{1,0:T(8,128)S(1)} %get-tuple-element.130.refs_1_, ...), custom_call_target="tpu_custom_call" | custom-call | flops 201326592 | bytes 4194304 | tf_op jit(solution)/shard_map/pallas_call | solution.py:421
  107.3 1.2 %collective-permute-start.30 = (bf16[256,256]{1,0:T(8,128)(2,1)S(1)}, bf16[256,256]{1,0:T(8,128)(2,1)S(1)}, u32[]{:S(2)}, u32[]{:S(2)}) collective-permute-start(bf16[256,256]{1,0:T(8,128)(2,1)S(1)} %get-tuple-element.143), channel_id=1, source_target_pairs={{0,8},{1,9},{2,10},{3,11},{4,12},{5,13},{6,14},{7,15},{8,0},{9,1},... | collective-permute-start | bytes 393224 | tf_op jit(solution)/shard_map/ppermute | solution.py:279
  108.6 1.0 collective-permute-start.32
  109.6 1.6 %shard_map.82 = (bf16[256,256]{1,0:T(8,128)(2,1)S(1)}, f32[256,256]{1,0:T(8,128)S(1)}, bf16[256,256]{1,0:T(8,128)(2,1)S(1)}, f32[256,256]{1,0:T(8,128)S(1)}) custom-call(s32[4]{0:T(128)S(1)} %copy-done.1, bf16[256,768]{1,0:T(8,128)(2,1)S(1)} %broadcast_select_fusion.refs_0_, bf16[256,768]{1,0:T(8,128)(2,1)S(1)} %collective-permute-done.11.refs_1_, ...), custom_call_target="tpu_custom_call" | custom-call | flops 134217728 | bytes 4194304 | tf_op jit(solution)/shard_map/pallas_call | solution.py:410
  111.2 1.6 %shard_map.83 = (bf16[256,256]{1,0:T(8,128)(2,1)S(1)}, bf16[256,256]{1,0:T(8,128)(2,1)S(1)}, bf16[256,256]{1,0:T(8,128)(2,1)S(1)}, bf16[256,256]{1,0:T(8,128)(2,1)S(1)}) custom-call(s32[4]{0:T(128)S(1)} %copy-done.1, f32[16]{0:T(128)S(1)} %copy-done.2, bf16[128,256]{1,0:T(8,128)(2,1)S(1)} %collective-permute-done.25.base_ref, ...), custom_call_target="tpu_custom_call" | custom-call | flops 402653184 | bytes 4194304 | tf_op jit(solution)/shard_map/pallas_call | solution.py:421
  112.8 0.1 collective-permute-start.33
  112.9 0.5 collective-permute-start.34
  113.4 2.1 %collective-permute-done.32.refs_3_.refs_8_ = bf16[256,256]{1,0:T(8,128)(2,1)S(1)} collective-permute-done((bf16[256,256]{1,0:T(8,128)(2,1)S(1)}, bf16[256,256]{1,0:T(8,128)(2,1)S(1)}, u32[]{:S(2)}, u32[]{:S(2)}) %collective-permute-start.32) | collective-permute-done | bytes 131104 | tf_op jit(solution)/shard_map/ppermute | solution.py:279
  115.5 1.6 %shard_map.84 = bf16[256,2048]{1,0:T(8,128)(2,1)} custom-call(s32[4]{0:T(128)S(1)} %copy-done.1, f32[8,128]{1,0:T(8,128)S(1)} %shard_map.81.refs_0_, bf16[256,256]{1,0:T(8,128)(2,1)S(1)} %get-tuple-element.155.refs_1_, bf16[256,256]{1,0:T(8,128)(2,1)S(1)} %get-tuple-element.156.refs_2_, bf16[256,256]{1,0:T(8,128)(2,1)S(1)} %collective-permute-done.33.refs_3_, ...), custom_call_target="tpu_custom_call" | custom-call | bytes 4194304 | tf_op jit(solution)/shard_map/pallas_call | solution.py:444
  (48 shorter events, 0.2 us)
Async XLA Ops:
  0.0 16.4 %copy-start.3 = (bf16[1,256,4096]{2,1,0:T(8,128)(2,1)S(1)}, bf16[1,256,4096]{2,1,0:T(8,128)(2,1)}, u32[]{:S(2)}) copy-start(bf16[1,256,4096]{2,1,0:T(8,128)(2,1)} %param.7) | copy-start | bytes 6291460
  0.0 16.3 %collective-permute-start.3 = (bf16[256,4096]{1,0:T(8,128)(2,1)}, bf16[256,4096]{1,0:T(8,128)(2,1)}, u32[]{:S(2)}, u32[]{:S(2)}) collective-permute-start(bf16[256,4096]{1,0:T(8,128)(2,1)} %bitcast.5), channel_id=1, source_target_pairs={{0,4},{1,5},{2,6},{3,7},{4,0},{5,1},{6,2},{7,3},{8,12},{9,13},{10,... | collective-permute-start | bytes 6291464 | tf_op jit(solution)/shard_map/ppermute | solution.py:279
  4.0 7.1 %collective-permute-start.1 = (bf16[144,768]{1,0:T(8,128)(2,1)}, bf16[144,768]{1,0:T(8,128)(2,1)S(1)}, u32[]{:S(2)}, u32[]{:S(2)}) collective-permute-start(bf16[144,768]{1,0:T(8,128)(2,1)} %get-tuple-element.84), channel_id=1, source_target_pairs={{0,8},{1,9},{2,10},{3,11},{4,12},{5,13},{6,14},{7,15},{8,0},{9,1},... | collective-permute-start | bytes 663560 | tf_op jit(solution)/shard_map/ppermute | solution.py:279
  5.2 10.9 %collective-permute-start.2 = (bf16[144,768]{1,0:T(8,128)(2,1)}, bf16[144,768]{1,0:T(8,128)(2,1)S(1)}, u32[]{:S(2)}, u32[]{:S(2)}) collective-permute-start(bf16[144,768]{1,0:T(8,128)(2,1)} %get-tuple-element.85), channel_id=1, source_target_pairs={{0,12},{1,13},{2,14},{3,15},{4,8},{5,9},{6,10},{7,11},{8,4},{9,5},... | collective-permute-start | bytes 663560 | tf_op jit(solution)/shard_map/ppermute | solution.py:279
  5.8 10.3 %collective-permute-start = (bf16[144,768]{1,0:T(8,128)(2,1)}, bf16[144,768]{1,0:T(8,128)(2,1)S(1)}, u32[]{:S(2)}, u32[]{:S(2)}) collective-permute-start(bf16[144,768]{1,0:T(8,128)(2,1)} %get-tuple-element.83), channel_id=1, source_target_pairs={{0,4},{1,5},{2,6},{3,7},{4,0},{5,1},{6,2},{7,3},{8,12},{9,13},{10,... | collective-permute-start | bytes 663560 | tf_op jit(solution)/shard_map/ppermute | solution.py:279
  16.2 52.2 %copy-start.1 = (s32[4]{0:T(128)S(1)}, s32[4]{0:T(128)}, u32[]{:S(2)}) copy-start(s32[4]{0:T(128)} %pad_add_fusion.here_ref) | copy-start | bytes 52
  16.3 10.9 %collective-permute-start.12 = (bf16[256,768]{1,0:T(8,128)(2,1)S(1)}, bf16[256,768]{1,0:T(8,128)(2,1)}, u32[]{:S(2)}, u32[]{:S(2)}) collective-permute-start(bf16[256,768]{1,0:T(8,128)(2,1)S(1)} %pad_maximum_fusion.refs_2_), channel_id=1, source_target_pairs={{0,1},{1,0},{2,3},{3,2},{4,5},{5,4},{6,7},{7,6},{8,9},{9,8},{10,11... | collective-permute-start | bytes 1179656 | tf_op jit(solution)/shard_map/ppermute | solution.py:279
  16.4 57.0 %collective-permute-start.21 = (bf16[256,4096]{1,0:T(8,128)(2,1)S(1)}, bf16[256,4096]{1,0:T(8,128)(2,1)}, u32[]{:S(2)}, u32[]{:S(2)}) collective-permute-start(bf16[256,4096]{1,0:T(8,128)(2,1)S(1)} %bitcast.6), channel_id=1, source_target_pairs={{0,8},{1,9},{2,10},{3,11},{4,12},{5,13},{6,14},{7,15},{8,0},{9,1},... | collective-permute-start | bytes 6291464 | tf_op jit(solution)/shard_map/ppermute | solution.py:279
  17.8 13.3 %collective-permute-start.13 = (bf16[256,768]{1,0:T(8,128)(2,1)S(1)}, bf16[256,768]{1,0:T(8,128)(2,1)}, u32[]{:S(2)}, u32[]{:S(2)}) collective-permute-start(bf16[256,768]{1,0:T(8,128)(2,1)S(1)} %pad_maximum_fusion.refs_2_), channel_id=1, source_target_pairs={{1,2},{2,1},{5,6},{6,5},{9,10},{10,9},{13,14},{14,13},{17,18},{18,... | collective-permute-start | bytes 1179656 | tf_op jit(solution)/shard_map/ppermute | solution.py:279
  22.1 10.2 %collective-permute-start.14 = (bf16[256,768]{1,0:T(8,128)(2,1)S(1)}, bf16[256,768]{1,0:T(8,128)(2,1)S(1)}, u32[]{:S(2)}, u32[]{:S(2)}) collective-permute-start(bf16[256,768]{1,0:T(8,128)(2,1)S(1)} %pad_maximum_fusion.refs_2_), channel_id=1, source_target_pairs={{0,16},{1,17},{2,18},{3,19},{4,20},{5,21},{6,22},{7,23},{8,24},{9,... | collective-permute-start | bytes 1179656 | tf_op jit(solution)/shard_map/ppermute | solution.py:279
  23.4 12.7 %collective-permute-start.4 = (bf16[256,768]{1,0:T(8,128)(2,1)S(1)}, bf16[256,768]{1,0:T(8,128)(2,1)}, u32[]{:S(2)}, u32[]{:S(2)}) collective-permute-start(bf16[256,768]{1,0:T(8,128)(2,1)S(1)} %pad_maximum_fusion.1.refs_9_), channel_id=1, source_target_pairs={{0,1},{1,0},{2,3},{3,2},{4,5},{5,4},{6,7},{7,6},{8,9},{9,8},{10,11... | collective-permute-start | bytes 1179656 | tf_op jit(solution)/shard_map/ppermute | solution.py:279
  27.1 11.3 %collective-permute-start.5 = (bf16[256,768]{1,0:T(8,128)(2,1)S(1)}, bf16[256,768]{1,0:T(8,128)(2,1)}, u32[]{:S(2)}, u32[]{:S(2)}) collective-permute-start(bf16[256,768]{1,0:T(8,128)(2,1)S(1)} %pad_maximum_fusion.1.refs_9_), channel_id=1, source_target_pairs={{1,2},{2,1},{5,6},{6,5},{9,10},{10,9},{13,14},{14,13},{17,18},{18,... | collective-permute-start | bytes 1179656 | tf_op jit(solution)/shard_map/ppermute | solution.py:279
  31.1 9.5 %collective-permute-start.6 = (bf16[256,768]{1,0:T(8,128)(2,1)S(1)}, bf16[256,768]{1,0:T(8,128)(2,1)S(1)}, u32[]{:S(2)}, u32[]{:S(2)}) collective-permute-start(bf16[256,768]{1,0:T(8,128)(2,1)S(1)} %pad_maximum_fusion.1.refs_9_), channel_id=1, source_target_pairs={{0,16},{1,17},{2,18},{3,19},{4,20},{5,21},{6,22},{7,23},{8,24},{9,... | collective-permute-start | bytes 1179656 | tf_op jit(solution)/shard_map/ppermute | solution.py:279
  32.3 0.7 copy-start.4
  33.1 13.8 %collective-permute-start.15 = (bf16[256,768]{1,0:T(8,128)(2,1)}, bf16[256,768]{1,0:T(8,128)(2,1)}, u32[]{:S(2)}, u32[]{:S(2)}) collective-permute-start(bf16[256,768]{1,0:T(8,128)(2,1)} %collective-permute-done.12.refs_3_), channel_id=1, source_target_pairs={{1,2},{2,1},{5,6},{6,5},{9,10},{10,9},{13,14},{14,13},{17,18},{18,... | collective-permute-start | bytes 1179656 | tf_op jit(solution)/shard_map/ppermute | solution.py:279
  36.1 12.8 %collective-permute-start.16 = (bf16[256,768]{1,0:T(8,128)(2,1)}, bf16[256,768]{1,0:T(8,128)(2,1)}, u32[]{:S(2)}, u32[]{:S(2)}) collective-permute-start(bf16[256,768]{1,0:T(8,128)(2,1)} %collective-permute-done.13), channel_id=1, source_target_pairs={{1,0},{2,3},{5,4},{6,7},{9,8},{10,11},{13,12},{14,15},{17,16},{18,... | collective-permute-start | bytes 1179656 | tf_op jit(solution)/shard_map/ppermute | solution.py:279
  38.4 11.7 %collective-permute-start.17 = (bf16[256,768]{1,0:T(8,128)(2,1)}, bf16[256,768]{1,0:T(8,128)(2,1)}, u32[]{:S(2)}, u32[]{:S(2)}) collective-permute-start(bf16[256,768]{1,0:T(8,128)(2,1)} %collective-permute-done.12.refs_3_), channel_id=1, source_target_pairs={{0,16},{1,17},{2,18},{3,19},{4,20},{5,21},{6,22},{7,23},{8,24},{9,... | collective-permute-start | bytes 1179656 | tf_op jit(solution)/shard_map/ppermute | solution.py:279
  40.6 0.8 copy-start.6
  41.3 13.9 %collective-permute-start.7 = (bf16[256,768]{1,0:T(8,128)(2,1)}, bf16[256,768]{1,0:T(8,128)(2,1)}, u32[]{:S(2)}, u32[]{:S(2)}) collective-permute-start(bf16[256,768]{1,0:T(8,128)(2,1)} %collective-permute-done.4.refs_10_), channel_id=1, source_target_pairs={{1,2},{2,1},{5,6},{6,5},{9,10},{10,9},{13,14},{14,13},{17,18},{18,... | collective-permute-start | bytes 1179656 | tf_op jit(solution)/shard_map/ppermute | solution.py:279
  46.9 9.7 %collective-permute-start.8 = (bf16[256,768]{1,0:T(8,128)(2,1)}, bf16[256,768]{1,0:T(8,128)(2,1)}, u32[]{:S(2)}, u32[]{:S(2)}) collective-permute-start(bf16[256,768]{1,0:T(8,128)(2,1)} %collective-permute-done.5), channel_id=1, source_target_pairs={{1,0},{2,3},{5,4},{6,7},{9,8},{10,11},{13,12},{14,15},{17,16},{18,... | collective-permute-start | bytes 1179656 | tf_op jit(solution)/shard_map/ppermute | solution.py:279
  48.9 19.5 %copy-start.5 = (bf16[256,768]{1,0:T(8,128)(2,1)S(1)}, bf16[256,768]{1,0:T(8,128)(2,1)}, u32[]{:S(2)}) copy-start(bf16[256,768]{1,0:T(8,128)(2,1)} %copy-done.4) | copy-start | bytes 1179652
  48.9 19.5 %copy-start.7 = (bf16[256,768]{1,0:T(8,128)(2,1)S(1)}, bf16[256,768]{1,0:T(8,128)(2,1)}, u32[]{:S(2)}) copy-start(bf16[256,768]{1,0:T(8,128)(2,1)} %copy-done.6) | copy-start | bytes 1179652
  48.9 11.2 %collective-permute-start.9 = (bf16[256,768]{1,0:T(8,128)(2,1)}, bf16[256,768]{1,0:T(8,128)(2,1)S(1)}, u32[]{:S(2)}, u32[]{:S(2)}) collective-permute-start(bf16[256,768]{1,0:T(8,128)(2,1)} %collective-permute-done.4.refs_10_), channel_id=1, source_target_pairs={{0,16},{1,17},{2,18},{3,19},{4,20},{5,21},{6,22},{7,23},{8,24},{9,... | collective-permute-start | bytes 1179656 | tf_op jit(solution)/shard_map/ppermute | solution.py:279
  51.2 13.0 %collective-permute-start.19 = (bf16[256,768]{1,0:T(8,128)(2,1)S(1)}, bf16[256,768]{1,0:T(8,128)(2,1)S(1)}, u32[]{:S(2)}, u32[]{:S(2)}) collective-permute-start(bf16[256,768]{1,0:T(8,128)(2,1)S(1)} %broadcast_select_fusion.2.refs_4_), channel_id=1, source_target_pairs={{0,16},{1,17},{2,18},{3,19},{4,20},{5,21},{6,22},{7,23},{8,24},{9,... | collective-permute-start | bytes 1179656 | tf_op jit(solution)/shard_map/ppermute | solution.py:279
  55.3 11.7 %collective-permute-start.18 = (bf16[256,768]{1,0:T(8,128)(2,1)}, bf16[256,768]{1,0:T(8,128)(2,1)S(1)}, u32[]{:S(2)}, u32[]{:S(2)}) collective-permute-start(bf16[256,768]{1,0:T(8,128)(2,1)} %collective-permute-done.15), channel_id=1, source_target_pairs={{1,0},{2,3},{5,4},{6,7},{9,8},{10,11},{13,12},{14,15},{17,16},{18,... | collective-permute-start | bytes 1179656 | tf_op jit(solution)/shard_map/ppermute | solution.py:279
  56.6 10.8 %collective-permute-start.20 = (bf16[256,768]{1,0:T(8,128)(2,1)}, bf16[256,768]{1,0:T(8,128)(2,1)S(1)}, u32[]{:S(2)}, u32[]{:S(2)}) collective-permute-start(bf16[256,768]{1,0:T(8,128)(2,1)} %collective-permute-done.17.refs_7_), channel_id=1, source_target_pairs={{1,2},{2,1},{5,6},{6,5},{9,10},{10,9},{13,14},{14,13},{17,18},{18,... | collective-permute-start | bytes 1179656 | tf_op jit(solution)/shard_map/ppermute | solution.py:279
  61.2 12.2 %collective-permute-start.11 = (bf16[256,768]{1,0:T(8,128)(2,1)S(1)}, bf16[256,768]{1,0:T(8,128)(2,1)S(1)}, u32[]{:S(2)}, u32[]{:S(2)}) collective-permute-start(bf16[256,768]{1,0:T(8,128)(2,1)S(1)} %broadcast_select_fusion.3.refs_11_), channel_id=1, source_target_pairs={{0,16},{1,17},{2,18},{3,19},{4,20},{5,21},{6,22},{7,23},{8,24},{9,... | collective-permute-start | bytes 1179656 | tf_op jit(solution)/shard_map/ppermute | solution.py:279
  64.2 9.2 %collective-permute-start.10 = (bf16[256,768]{1,0:T(8,128)(2,1)}, bf16[256,768]{1,0:T(8,128)(2,1)S(1)}, u32[]{:S(2)}, u32[]{:S(2)}) collective-permute-start(bf16[256,768]{1,0:T(8,128)(2,1)} %collective-permute-done.7), channel_id=1, source_target_pairs={{1,0},{2,3},{5,4},{6,7},{9,8},{10,11},{13,12},{14,15},{17,16},{18,... | collective-permute-start | bytes 1179656 | tf_op jit(solution)/shard_map/ppermute | solution.py:279
  73.4 14.8 %collective-permute-start.24 = (bf16[256,4096]{1,0:T(8,128)(2,1)}, bf16[256,4096]{1,0:T(8,128)(2,1)S(1)}, u32[]{:S(2)}, u32[]{:S(2)}) collective-permute-start(bf16[256,4096]{1,0:T(8,128)(2,1)} %collective-permute-done.21.refs_0_), channel_id=1, source_target_pairs={{0,4},{1,5},{2,6},{3,7},{4,0},{5,1},{6,2},{7,3},{8,12},{9,13},{10,... | collective-permute-start | bytes 6291464 | tf_op jit(solution)/shard_map/ppermute | solution.py:279
  80.8 12.3 %collective-permute-start.22 = (bf16[256,256]{1,0:T(8,128)(2,1)S(1)}, bf16[256,256]{1,0:T(8,128)(2,1)S(1)}, u32[]{:S(2)}, u32[]{:S(2)}) collective-permute-start(bf16[256,256]{1,0:T(8,128)(2,1)S(1)} %slice.31), channel_id=1, source_target_pairs={{1,0},{2,3},{5,4},{6,7},{9,8},{10,11},{13,12},{14,15},{17,16},{18,... | collective-permute-start | bytes 393224 | tf_op jit(solution)/shard_map/ppermute | solution.py:279
  84.2 11.9 %collective-permute-start.26 = (bf16[256,512]{1,0:T(8,128)(2,1)S(1)}, bf16[256,512]{1,0:T(8,128)(2,1)S(1)}, u32[]{:S(2)}, u32[]{:S(2)}) collective-permute-start(bf16[256,512]{1,0:T(8,128)(2,1)S(1)} %slice.33), channel_id=1, source_target_pairs={{1,0},{2,3},{5,4},{6,7},{9,8},{10,11},{13,12},{14,15},{17,16},{18,... | collective-permute-start | bytes 786440 | tf_op jit(solution)/shard_map/ppermute | solution.py:279
  86.7 6.4 %collective-permute-start.23 = (bf16[256,256]{1,0:T(8,128)(2,1)S(1)}, bf16[256,256]{1,0:T(8,128)(2,1)S(1)}, u32[]{:S(2)}, u32[]{:S(2)}) collective-permute-start(bf16[256,256]{1,0:T(8,128)(2,1)S(1)} %get-tuple-element.161), channel_id=1, source_target_pairs={{0,16},{1,17},{2,18},{3,19},{4,20},{5,21},{6,22},{7,23},{8,24},{9,... | collective-permute-start | bytes 393224 | tf_op jit(solution)/shard_map/ppermute | solution.py:279
  88.0 5.1 %copy-start = (bf16[144,768]{1,0:T(8,128)(2,1)S(1)}, bf16[144,768]{1,0:T(8,128)(2,1)}, u32[]{:S(2)}) copy-start(bf16[144,768]{1,0:T(8,128)(2,1)} %get-tuple-element.82.refs_13_.refs_12_.refs_8_.refs_5_) | copy-start | bytes 663556
  88.0 8.2 %collective-permute-start.27 = (bf16[256,256]{1,0:T(8,128)(2,1)S(1)}, bf16[256,256]{1,0:T(8,128)(2,1)S(1)}, u32[]{:S(2)}, u32[]{:S(2)}) collective-permute-start(bf16[256,256]{1,0:T(8,128)(2,1)S(1)} %get-tuple-element.160), channel_id=1, source_target_pairs={{0,16},{1,17},{2,18},{3,19},{4,20},{5,21},{6,22},{7,23},{8,24},{9,... | collective-permute-start | bytes 393224 | tf_op jit(solution)/shard_map/ppermute | solution.py:279
  94.8 3.5 %collective-permute-start.25 = (bf16[128,256]{1,0:T(8,128)(2,1)S(1)}, bf16[128,256]{1,0:T(8,128)(2,1)S(1)}, u32[]{:S(2)}, u32[]{:S(2)}) collective-permute-start(bf16[128,256]{1,0:T(8,128)(2,1)S(1)} %get-tuple-element.121), channel_id=1, source_target_pairs={{0,16},{1,17},{2,18},{3,19},{4,20},{5,21},{6,22},{7,23},{8,24},{9,... | collective-permute-start | bytes 196616 | tf_op jit(solution)/shard_map/ppermute | solution.py:279
  96.1 3.1 %copy-start.2 = (f32[16]{0:T(128)S(1)}, f32[16]{0:T(128)}, u32[]{:S(2)}) copy-start(f32[16]{0:T(128)} %gate_ref.5) | copy-start | bytes 196
  98.3 6.1 %collective-permute-start.29 = (bf16[256,256]{1,0:T(8,128)(2,1)S(1)}, bf16[256,256]{1,0:T(8,128)(2,1)S(1)}, u32[]{:S(2)}, u32[]{:S(2)}) collective-permute-start(bf16[256,256]{1,0:T(8,128)(2,1)S(1)} %get-tuple-element.136), channel_id=1, source_target_pairs={{0,16},{1,17},{2,18},{3,19},{4,20},{5,21},{6,22},{7,23},{8,24},{9,... | collective-permute-start | bytes 393224 | tf_op jit(solution)/shard_map/ppermute | solution.py:279
  100.4 12.5 %collective-permute-start.28 = (bf16[256,256]{1,0:T(8,128)(2,1)S(1)}, bf16[256,256]{1,0:T(8,128)(2,1)S(1)}, u32[]{:S(2)}, u32[]{:S(2)}) collective-permute-start(bf16[256,256]{1,0:T(8,128)(2,1)S(1)} %get-tuple-element.135), channel_id=1, source_target_pairs={{0,8},{1,9},{2,10},{3,11},{4,12},{5,13},{6,14},{7,15},{8,0},{9,1},... | collective-permute-start | bytes 393224 | tf_op jit(solution)/shard_map/ppermute | solution.py:279
  101.7 11.7 %collective-permute-start.31 = (bf16[256,256]{1,0:T(8,128)(2,1)S(1)}, bf16[256,256]{1,0:T(8,128)(2,1)S(1)}, u32[]{:S(2)}, u32[]{:S(2)}) collective-permute-start(bf16[256,256]{1,0:T(8,128)(2,1)S(1)} %get-tuple-element.137), channel_id=1, source_target_pairs={{0,12},{1,13},{2,14},{3,15},{4,8},{5,9},{6,10},{7,11},{8,4},{9,5},... | collective-permute-start | bytes 393224 | tf_op jit(solution)/shard_map/ppermute | solution.py:279
  107.3 6.1 %collective-permute-start.30 = (bf16[256,256]{1,0:T(8,128)(2,1)S(1)}, bf16[256,256]{1,0:T(8,128)(2,1)S(1)}, u32[]{:S(2)}, u32[]{:S(2)}) collective-permute-start(bf16[256,256]{1,0:T(8,128)(2,1)S(1)} %get-tuple-element.143), channel_id=1, source_target_pairs={{0,8},{1,9},{2,10},{3,11},{4,12},{5,13},{6,14},{7,15},{8,0},{9,1},... | collective-permute-start | bytes 393224 | tf_op jit(solution)/shard_map/ppermute | solution.py:279
  108.6 6.9 %collective-permute-start.32 = (bf16[256,256]{1,0:T(8,128)(2,1)S(1)}, bf16[256,256]{1,0:T(8,128)(2,1)S(1)}, u32[]{:S(2)}, u32[]{:S(2)}) collective-permute-start(bf16[256,256]{1,0:T(8,128)(2,1)S(1)} %get-tuple-element.144), channel_id=1, source_target_pairs={{0,12},{1,13},{2,14},{3,15},{4,8},{5,9},{6,10},{7,11},{8,4},{9,5},... | collective-permute-start | bytes 393224 | tf_op jit(solution)/shard_map/ppermute | solution.py:279
  112.8 2.7 %collective-permute-start.33 = (bf16[256,256]{1,0:T(8,128)(2,1)S(1)}, bf16[256,256]{1,0:T(8,128)(2,1)S(1)}, u32[]{:S(2)}, u32[]{:S(2)}) collective-permute-start(bf16[256,256]{1,0:T(8,128)(2,1)S(1)} %get-tuple-element.157), channel_id=1, source_target_pairs={{0,4},{1,5},{2,6},{3,7},{4,0},{5,1},{6,2},{7,3},{8,12},{9,13},{10,... | collective-permute-start | bytes 393224 | tf_op jit(solution)/shard_map/ppermute | solution.py:279
  112.9 2.6 %collective-permute-start.34 = (bf16[256,256]{1,0:T(8,128)(2,1)S(1)}, bf16[256,256]{1,0:T(8,128)(2,1)S(1)}, u32[]{:S(2)}, u32[]{:S(2)}) collective-permute-start(bf16[256,256]{1,0:T(8,128)(2,1)S(1)} %get-tuple-element.158), channel_id=1, source_target_pairs={{0,4},{1,5},{2,6},{3,7},{4,0},{5,1},{6,2},{7,3},{8,12},{9,13},{10,... | collective-permute-start | bytes 393224 | tf_op jit(solution)/shard_map/ppermute | solution.py:279

commit v16 on v14

--- a/solution.py
+++ b/solution.py
@@ -79,19 +79,38 @@
 
 
 def project_body(early, late, line, here_ref, *refs):
-    tokens, pieces, outs = refs[:2], refs[2 : 2 + len(early)], refs[2 + len(early) :]
-    length = tokens[0].shape[0]
+    books, pieces, outs = refs[:2], refs[2 : 2 + len(early)], refs[2 + len(early) : -2]
+    tokens_ref, sems = refs[-2:]
+    length, width = books[0].shape
+    deep = width // 2
+    mine = here_ref[0] if line else 0
+    copies = []
+    for side in range(2):
+        at = pl.ds(pl.multiple_of((mine ^ side) * deep, deep), deep)
+        for n in range(2):
+            copies.append(
+                pltpu.make_async_copy(books[n].at[:, at], tokens_ref.at[n, :, at], sems.at[2 * side + n])
+            )
+            copies[-1].start()
+    tokens = [tokens_ref.at[n] for n in range(2)]
     total = None
-    for place, piece in zip(early, pieces):
-        columns = jnp.concatenate([columns_of(one, here_ref, *place, line) for one in tokens], axis=0)
-        term = jnp.dot(columns, piece[...], preferred_element_type=jnp.float32)
-        total = term if total is None else total + term
+    near = [n for n, (piece, half) in enumerate(early) if piece < line]
+    far = [n for n in range(len(early)) if n not in near]
+    for side, members in enumerate((near, far)):
+        for one in copies[2 * side : 2 * side + 2]:
+            one.wait()
+        for at in members:
+            columns = jnp.concatenate(
+                [columns_of(one, here_ref, *early[at], line) for one in tokens], axis=0
+            )
+            term = jnp.dot(columns, pieces[at][...], preferred_element_type=jnp.float32)
+            total = term if total is None else total + term
     for n in range(2):
         outs[n][...] = total[n * length : (n + 1) * length]
         for k, place in enumerate(late):
             columns = columns_of(tokens[n], here_ref, *place, line)
-            deep = columns.shape[1]
-            outs[2 + n][:, k * deep : (k + 1) * deep] = columns
+            wide = columns.shape[1]
+            outs[2 + n][:, k * wide : (k + 1) * wide] = columns
 
 
 def sigma_plus(v):
@@ -317,8 +336,9 @@
         found = call(
             functools.partial(project_body, early, late, line),
             [shape((length, wide), f32)] * 2 + [shape((length, len(late) * deep), bf16)] * 2,
-            [SMEM] + [VMEM] * (2 + len(early)),
+            [SMEM] + [ANY] * 2 + [VMEM] * len(early),
             flops=2 * 2 * length * len(early) * deep * wide,
+            scratch=[pltpu.VMEM((2, length, width), bf16), pltpu.SemaphoreType.DMA((4,))],
         )(here, *[books[s] for s in segs], *[halves[half][piece] for piece, half in early])
         for at, s in enumerate(segs):
             sums[s], lates[s] = found[at], found[2 + at]
@@ -365,7 +385,7 @@
         project((2, 3), early, late, (upper, lower), n_z)
         b_three = jnp.where(inside, b_middle, b_last)
         pieces = [b_three, b_far2]
-        outer_kv, outer_q = [outward(a_inner[:, at]) for at in (slice(0, cut), slice(cut, None))]
+        outer_kv, outer_q = [outward(after(a_inner[:, at], b_three)) for at in (slice(0, cut), slice(cut, None))]
         inner = a_inner
         finish = lambda at: over(b_three[:, at])
     else:
@@ -428,11 +448,12 @@
             *[ready[key][0] for key in keys], *[ready[key][1] for key in keys],
         )
 
-    ready = local((2, 3, 1, 0), 0)
+    ready = local((2, 3), 0)
     base = after(base, *ready[2, 0])
     two0, three0 = mix((2, 3), (0,), base, ready)
     ready |= local((2, 3), 1, two0, three0)
     two1, three1 = mix((2, 3), (1,), base, ready)
+    ready |= local((1, 0), 0, two1, three1)
     ready |= local((1, 0), 1, two1, three1)
     one0, one1, mine0, mine1 = mix((1, 0), (0, 1), after(base, two1, three1), ready)
     sent = [mine0, mine1]

time: 115 us -> 117 us (1.017)
  waiting for transfers between devices: 28.7 us -> 24.7 us
  Pallas kernels: 24.6 us -> 28.3 us
  starting transfers between devices: 52.4 us -> 54.6 us
    ppermute x34, waiting for transfers between devices: 28.7 us -> 24.7 us  [permute(): return lax.ppermute(array, AXES, pairs)]
    pallas_call x2, Pallas kernels: 9.76 us -> 12.4 us  [project(): call(functools.partial(project_body, early, late, line), [shape((length,...]
    ppermute x34, starting transfers between devices: 52.4 us -> 54.6 us  [permute(): return lax.ppermute(array, AXES, pairs)]
    pallas_call x3 -> x4, Pallas kernels: 5.44 us -> 6.5 us  [local(): call(functools.partial(local_body, len(segs), len(late) + 1, halves[1 + p...]
  transfers between devices with their start and end apart: 34 -> 34, of which waited for: 11 -> 10; matrix products, arithmetic and copies ran while one was open for 5% -> 5% of each run, Pallas kernels for 19% -> 22%
where the time goes in v16:
time: 117 us; the launch traced here: 116 us
  starting transfers between devices  54.6 us (47%)
  Pallas kernels  28.3 us (24%)
  waiting for transfers between devices  24.7 us (21%)
  other arithmetic  4.87 us (4%)
  local copies, waits for them, and re-layouts  2.56 us (2%)
    ppermute x34, starting transfers between devices, permute(): return lax.ppermute(array, AXES, pairs)  54.6 us
    ppermute x34, waiting for transfers between devices, permute(): return lax.ppermute(array, AXES, pairs)  24.7 us
    pallas_call x2, Pallas kernels, project(): call(functools.partial(project_body, early, late, line), [shape((length,...  12.4 us
    pallas_call x4, Pallas kernels, local(): call(functools.partial(local_body, len(segs), len(late) + 1, halves[1 + p...  6.5 us
    pallas_call x3, Pallas kernels, mix(): call(functools.partial(mix_body, segs, parts, group), [shape((length, hal...  3.95 us
  transfers between devices with their start and end apart: 34, of which 10 were waited for; matrix products, arithmetic and copies ran while one was open for 5% of the time, Pallas kernels for 22%

profile of v16, /device:TPU:9, one launch (start us, length us, event | category | flops | bytes accessed | tf_op | source)
XLA Modules:
  0.0 116.1 jit_solution(9394334281799473596)
XLA Ops:
  0.0 0.7 collective-permute-start.3
  1.3 0.6 pad_add_fusion.here_ref
  1.9 2.1 %shard_map.73 = (bf16[144,768]{1,0:T(8,128)(2,1)}, bf16[144,768]{1,0:T(8,128)(2,1)}, bf16[144,768]{1,0:T(8,128)(2,1)}, bf16[144,768]{1,0:T(8,128)(2,1)}) custom-call(s32[4]{0:T(128)} %pad_add_fusion.here_ref, s32[1,1]{1,0:T(1,128)S(6)} %copy.8.valid_ref, s32[1,1,2,2]{3,2,1,0:T(2,128)} %mask_ref.1, bf16[128,2048]{1,0:T(8,128)(2,1)} %wq_ref.1, ...), custom_call_target="tpu_custom_call" | custom-call | bytes 4194304 | tf_op jit(solution)/shard_map/pallas_call | solution.py:304
  4.1 0.2 collective-permute-start
  4.2 1.5 %collective-permute-start.2 = (bf16[144,768]{1,0:T(8,128)(2,1)}, bf16[144,768]{1,0:T(8,128)(2,1)S(1)}, u32[]{:S(2)}, u32[]{:S(2)}) collective-permute-start(bf16[144,768]{1,0:T(8,128)(2,1)} %get-tuple-element.86), channel_id=1, source_target_pairs={{0,12},{1,13},{2,14},{3,15},{4,8},{5,9},{6,10},{7,11},{8,4},{9,5},... | collective-permute-start | bytes 663560 | tf_op jit(solution)/shard_map/ppermute | solution.py:298
  5.7 0.3 collective-permute-start.1
  5.9 0.9 slice.24
  6.9 5.3 %collective-permute-done.2.refs_16_.refs_8_.refs_5_ = bf16[144,768]{1,0:T(8,128)(2,1)S(1)} collective-permute-done((bf16[144,768]{1,0:T(8,128)(2,1)}, bf16[144,768]{1,0:T(8,128)(2,1)S(1)}, u32[]{:S(2)}, u32[]{:S(2)}) %collective-permute-start.2) | collective-permute-done | bytes 221216 | tf_op jit(solution)/shard_map/ppermute | solution.py:298
  12.2 4.4 %collective-permute-done.1.refs_15_.refs_7_.refs_4_ = bf16[144,768]{1,0:T(8,128)(2,1)S(1)} collective-permute-done((bf16[144,768]{1,0:T(8,128)(2,1)}, bf16[144,768]{1,0:T(8,128)(2,1)S(1)}, u32[]{:S(2)}, u32[]{:S(2)}) %collective-permute-start.1) | collective-permute-done | bytes 221216 | tf_op jit(solution)/shard_map/ppermute | solution.py:298
  16.6 0.0 collective-permute-done.3.refs_1_
  16.6 0.1 collective-permute-start.12
  16.7 1.4 %collective-permute-start.21 = (bf16[256,4096]{1,0:T(8,128)(2,1)S(1)}, bf16[256,4096]{1,0:T(8,128)(2,1)}, u32[]{:S(2)}, u32[]{:S(2)}) collective-permute-start(bf16[256,4096]{1,0:T(8,128)(2,1)S(1)} %bitcast.6), channel_id=1, source_target_pairs={{0,8},{1,9},{2,10},{3,11},{4,12},{5,13},{6,14},{7,15},{8,0},{9,1},... | collective-permute-start | bytes 6291464 | tf_op jit(solution)/shard_map/ppermute | solution.py:298
  18.1 4.3 %collective-permute-start.13 = (bf16[256,768]{1,0:T(8,128)(2,1)S(1)}, bf16[256,768]{1,0:T(8,128)(2,1)}, u32[]{:S(2)}, u32[]{:S(2)}) collective-permute-start(bf16[256,768]{1,0:T(8,128)(2,1)S(1)} %pad_maximum_fusion.refs_2_), channel_id=1, source_target_pairs={{1,2},{2,1},{5,6},{6,5},{9,10},{10,9},{13,14},{14,13},{17,18},{18,... | collective-permute-start | bytes 1179656 | tf_op jit(solution)/shard_map/ppermute | solution.py:298
  22.4 1.3 %collective-permute-start.14 = (bf16[256,768]{1,0:T(8,128)(2,1)S(1)}, bf16[256,768]{1,0:T(8,128)(2,1)S(1)}, u32[]{:S(2)}, u32[]{:S(2)}) collective-permute-start(bf16[256,768]{1,0:T(8,128)(2,1)S(1)} %pad_maximum_fusion.refs_2_), channel_id=1, source_target_pairs={{0,16},{1,17},{2,18},{3,19},{4,20},{5,21},{6,22},{7,23},{8,24},{9,... | collective-permute-start | bytes 1179656 | tf_op jit(solution)/shard_map/ppermute | solution.py:298
  23.7 3.0 %collective-permute-done.12.refs_3_ = bf16[256,768]{1,0:T(8,128)(2,1)} collective-permute-done((bf16[256,768]{1,0:T(8,128)(2,1)S(1)}, bf16[256,768]{1,0:T(8,128)(2,1)}, u32[]{:S(2)}, u32[]{:S(2)}) %collective-permute-start.12) | collective-permute-done | bytes 393248 | tf_op jit(solution)/shard_map/ppermute | solution.py:298
  26.7 3.2 %collective-permute-start.5 = (bf16[256,768]{1,0:T(8,128)(2,1)S(1)}, bf16[256,768]{1,0:T(8,128)(2,1)}, u32[]{:S(2)}, u32[]{:S(2)}) collective-permute-start(bf16[256,768]{1,0:T(8,128)(2,1)S(1)} %pad_maximum_fusion.1.refs_9_), channel_id=1, source_target_pairs={{1,2},{2,1},{5,6},{6,5},{9,10},{10,9},{13,14},{14,13},{17,18},{18,... | collective-permute-start | bytes 1179656 | tf_op jit(solution)/shard_map/ppermute | solution.py:298
  29.9 0.7 collective-permute-done.13
  30.6 1.2 %collective-permute-start.6 = (bf16[256,768]{1,0:T(8,128)(2,1)S(1)}, bf16[256,768]{1,0:T(8,128)(2,1)S(1)}, u32[]{:S(2)}, u32[]{:S(2)}) collective-permute-start(bf16[256,768]{1,0:T(8,128)(2,1)S(1)} %pad_maximum_fusion.1.refs_9_), channel_id=1, source_target_pairs={{0,16},{1,17},{2,18},{3,19},{4,20},{5,21},{6,22},{7,23},{8,24},{9,... | collective-permute-start | bytes 1179656 | tf_op jit(solution)/shard_map/ppermute | solution.py:298
  31.9 0.7 copy-done.4
  32.6 3.1 %collective-permute-start.15 = (bf16[256,768]{1,0:T(8,128)(2,1)}, bf16[256,768]{1,0:T(8,128)(2,1)}, u32[]{:S(2)}, u32[]{:S(2)}) collective-permute-start(bf16[256,768]{1,0:T(8,128)(2,1)} %collective-permute-done.12.refs_3_), channel_id=1, source_target_pairs={{1,2},{2,1},{5,6},{6,5},{9,10},{10,9},{13,14},{14,13},{17,18},{18,... | collective-permute-start | bytes 1179656 | tf_op jit(solution)/shard_map/ppermute | solution.py:298
  35.7 2.5 %collective-permute-start.16 = (bf16[256,768]{1,0:T(8,128)(2,1)}, bf16[256,768]{1,0:T(8,128)(2,1)}, u32[]{:S(2)}, u32[]{:S(2)}) collective-permute-start(bf16[256,768]{1,0:T(8,128)(2,1)} %collective-permute-done.13), channel_id=1, source_target_pairs={{1,0},{2,3},{5,4},{6,7},{9,8},{10,11},{13,12},{14,15},{17,16},{18,... | collective-permute-start | bytes 1179656 | tf_op jit(solution)/shard_map/ppermute | solution.py:298
  38.2 1.1 collective-permute-start.17
  39.3 0.8 copy-done.6
  40.0 4.3 %collective-permute-start.7 = (bf16[256,768]{1,0:T(8,128)(2,1)}, bf16[256,768]{1,0:T(8,128)(2,1)}, u32[]{:S(2)}, u32[]{:S(2)}) collective-permute-start(bf16[256,768]{1,0:T(8,128)(2,1)} %collective-permute-done.4.refs_10_), channel_id=1, source_target_pairs={{1,2},{2,1},{5,6},{6,5},{9,10},{10,9},{13,14},{14,13},{17,18},{18,... | collective-permute-start | bytes 1179656 | tf_op jit(solution)/shard_map/ppermute | solution.py:298
  44.4 2.1 %collective-permute-done.15 = bf16[256,768]{1,0:T(8,128)(2,1)} collective-permute-done((bf16[256,768]{1,0:T(8,128)(2,1)}, bf16[256,768]{1,0:T(8,128)(2,1)}, u32[]{:S(2)}, u32[]{:S(2)}) %collective-permute-start.15) | collective-permute-done | bytes 393248 | tf_op jit(solution)/shard_map/ppermute | solution.py:298
  46.4 2.1 %collective-permute-start.8 = (bf16[256,768]{1,0:T(8,128)(2,1)}, bf16[256,768]{1,0:T(8,128)(2,1)}, u32[]{:S(2)}, u32[]{:S(2)}) collective-permute-start(bf16[256,768]{1,0:T(8,128)(2,1)} %collective-permute-done.5), channel_id=1, source_target_pairs={{1,0},{2,3},{5,4},{6,7},{9,8},{10,11},{13,12},{14,15},{17,16},{18,... | collective-permute-start | bytes 1179656 | tf_op jit(solution)/shard_map/ppermute | solution.py:298
  48.5 1.2 %collective-permute-start.9 = (bf16[256,768]{1,0:T(8,128)(2,1)}, bf16[256,768]{1,0:T(8,128)(2,1)S(1)}, u32[]{:S(2)}, u32[]{:S(2)}) collective-permute-start(bf16[256,768]{1,0:T(8,128)(2,1)} %collective-permute-done.4.refs_10_), channel_id=1, source_target_pairs={{0,16},{1,17},{2,18},{3,19},{4,20},{5,21},{6,22},{7,23},{8,24},{9,... | collective-permute-start | bytes 1179656 | tf_op jit(solution)/shard_map/ppermute | solution.py:298
  49.8 1.3 %collective-permute-start.18 = (bf16[256,768]{1,0:T(8,128)(2,1)}, bf16[256,768]{1,0:T(8,128)(2,1)S(1)}, u32[]{:S(2)}, u32[]{:S(2)}) collective-permute-start(bf16[256,768]{1,0:T(8,128)(2,1)} %collective-permute-done.15), channel_id=1, source_target_pairs={{1,0},{2,3},{5,4},{6,7},{9,8},{10,11},{13,12},{14,15},{17,16},{18,... | collective-permute-start | bytes 1179656 | tf_op jit(solution)/shard_map/ppermute | solution.py:298
  51.1 1.1 broadcast_select_fusion.2.refs_4_
  52.1 2.8 %collective-permute-done.7 = bf16[256,768]{1,0:T(8,128)(2,1)} collective-permute-done((bf16[256,768]{1,0:T(8,128)(2,1)}, bf16[256,768]{1,0:T(8,128)(2,1)}, u32[]{:S(2)}, u32[]{:S(2)}) %collective-permute-start.7) | collective-permute-done | bytes 393248 | tf_op jit(solution)/shard_map/ppermute | solution.py:298
  54.9 1.2 %collective-permute-start.19 = (bf16[256,768]{1,0:T(8,128)(2,1)S(1)}, bf16[256,768]{1,0:T(8,128)(2,1)S(1)}, u32[]{:S(2)}, u32[]{:S(2)}) collective-permute-start(bf16[256,768]{1,0:T(8,128)(2,1)S(1)} %broadcast_select_fusion.2.refs_4_), channel_id=1, source_target_pairs={{0,16},{1,17},{2,18},{3,19},{4,20},{5,21},{6,22},{7,23},{8,24},{9,... | collective-permute-start | bytes 1179656 | tf_op jit(solution)/shard_map/ppermute | solution.py:298
  56.1 3.5 %collective-permute-start.20 = (bf16[256,768]{1,0:T(8,128)(2,1)}, bf16[256,768]{1,0:T(8,128)(2,1)S(1)}, u32[]{:S(2)}, u32[]{:S(2)}) collective-permute-start(bf16[256,768]{1,0:T(8,128)(2,1)} %collective-permute-done.17.refs_7_), channel_id=1, source_target_pairs={{1,2},{2,1},{5,6},{6,5},{9,10},{10,9},{13,14},{14,13},{17,18},{18,... | collective-permute-start | bytes 1179656 | tf_op jit(solution)/shard_map/ppermute | solution.py:298
  59.6 1.3 %collective-permute-start.10 = (bf16[256,768]{1,0:T(8,128)(2,1)}, bf16[256,768]{1,0:T(8,128)(2,1)S(1)}, u32[]{:S(2)}, u32[]{:S(2)}) collective-permute-start(bf16[256,768]{1,0:T(8,128)(2,1)} %collective-permute-done.7), channel_id=1, source_target_pairs={{1,0},{2,3},{5,4},{6,7},{9,8},{10,11},{13,12},{14,15},{17,16},{18,... | collective-permute-start | bytes 1179656 | tf_op jit(solution)/shard_map/ppermute | solution.py:298
  61.0 1.1 broadcast_select_fusion.3.refs_11_
  62.0 0.3 collective-permute-start.11
  62.3 3.7 %collective-permute-done.19.refs_8_ = bf16[256,768]{1,0:T(8,128)(2,1)S(1)} collective-permute-done((bf16[256,768]{1,0:T(8,128)(2,1)S(1)}, bf16[256,768]{1,0:T(8,128)(2,1)S(1)}, u32[]{:S(2)}, u32[]{:S(2)}) %collective-permute-start.19) | collective-permute-done | bytes 393248 | tf_op jit(solution)/shard_map/ppermute | solution.py:298
  66.0 1.1 broadcast_select_fusion.1.refs_5_
  67.1 6.2 %shard_map.74 = (f32[256,768]{1,0:T(8,128)S(1)}, f32[256,768]{1,0:T(8,128)S(1)}, bf16[256,1024]{1,0:T(8,128)(2,1)S(1)}, bf16[256,1024]{1,0:T(8,128)(2,1)S(1)}) custom-call(s32[4]{0:T(128)S(1)} %copy-done.1, bf16[256,4096]{1,0:T(8,128)(2,1)S(1)} %bitcast.7, bf16[256,4096]{1,0:T(8,128)(2,1)} %collective-permute-done.3.refs_1_, ...), custom_call_target="tpu_custom_call" | custom-call | flops 2415919104 | bytes 4194304 | tf_op jit(solution)/shard_map/pallas_call | solution.py:336
  73.4 1.1 collective-permute-done.11.refs_1_
  74.4 7.6 %collective-permute-start.24 = (bf16[256,4096]{1,0:T(8,128)(2,1)}, bf16[256,4096]{1,0:T(8,128)(2,1)S(1)}, u32[]{:S(2)}, u32[]{:S(2)}) collective-permute-start(bf16[256,4096]{1,0:T(8,128)(2,1)} %collective-permute-done.21.refs_0_), channel_id=1, source_target_pairs={{0,4},{1,5},{2,6},{3,7},{4,0},{5,1},{6,2},{7,3},{8,12},{9,13},{10,... | collective-permute-start | bytes 6291464 | tf_op jit(solution)/shard_map/ppermute | solution.py:298
  82.0 1.1 broadcast_select_fusion.refs_0_
  83.2 1.4 %collective-permute-start.22 = (bf16[256,256]{1,0:T(8,128)(2,1)S(1)}, bf16[256,256]{1,0:T(8,128)(2,1)S(1)}, u32[]{:S(2)}, u32[]{:S(2)}) collective-permute-start(bf16[256,256]{1,0:T(8,128)(2,1)S(1)} %slice.28), channel_id=1, source_target_pairs={{1,0},{2,3},{5,4},{6,7},{9,8},{10,11},{13,12},{14,15},{17,16},{18,... | collective-permute-start | bytes 393224 | tf_op jit(solution)/shard_map/ppermute | solution.py:298
  84.6 1.3 %collective-permute-start.23 = (bf16[256,256]{1,0:T(8,128)(2,1)S(1)}, bf16[256,256]{1,0:T(8,128)(2,1)S(1)}, u32[]{:S(2)}, u32[]{:S(2)}) collective-permute-start(bf16[256,256]{1,0:T(8,128)(2,1)S(1)} %slice.35), channel_id=1, source_target_pairs={{0,16},{1,17},{2,18},{3,19},{4,20},{5,21},{6,22},{7,23},{8,24},{9,... | collective-permute-start | bytes 393224 | tf_op jit(solution)/shard_map/ppermute | solution.py:298
  85.9 1.3 %collective-permute-start.26 = (bf16[256,512]{1,0:T(8,128)(2,1)S(1)}, bf16[256,512]{1,0:T(8,128)(2,1)S(1)}, u32[]{:S(2)}, u32[]{:S(2)}) collective-permute-start(bf16[256,512]{1,0:T(8,128)(2,1)S(1)} %slice.30), channel_id=1, source_target_pairs={{1,0},{2,3},{5,4},{6,7},{9,8},{10,11},{13,12},{14,15},{17,16},{18,... | collective-permute-start | bytes 786440 | tf_op jit(solution)/shard_map/ppermute | solution.py:298
  87.2 0.3 collective-permute-start.27
  87.5 6.1 %shard_map.75 = (f32[256,768]{1,0:T(8,128)S(1)}, f32[256,768]{1,0:T(8,128)S(1)}, bf16[256,1024]{1,0:T(8,128)(2,1)S(1)}, bf16[256,1024]{1,0:T(8,128)(2,1)S(1)}) custom-call(s32[4]{0:T(128)S(1)} %copy-done.1, bf16[256,4096]{1,0:T(8,128)(2,1)} %collective-permute-done.21.refs_0_, bf16[256,4096]{1,0:T(8,128)(2,1)S(1)} %collective-permute-done.24.refs_1_, ...), custom_call_target="tpu_custom_call" | custom-call | flops 2415919104 | bytes 4194304 | tf_op jit(solution)/shard_map/pallas_call | solution.py:336
  93.7 1.7 %shard_map.76 = (bf16[256,256]{1,0:T(8,128)(2,1)S(1)}, f32[128,256]{1,0:T(8,128)S(1)}, bf16[256,256]{1,0:T(8,128)(2,1)S(1)}, f32[128,256]{1,0:T(8,128)S(1)}, bf1...) custom-call(s32[4]{0:T(128)S(1)} %copy-done.1, ...), custom_call_target="tpu_custom_call" | custom-call | flops 536870912 | bytes 4194304 | tf_op jit(solution)/shard_map/pallas_call | solution.py:410
  95.4 1.3 %collective-permute-start.25 = (bf16[128,256]{1,0:T(8,128)(2,1)S(1)}, bf16[128,256]{1,0:T(8,128)(2,1)S(1)}, u32[]{:S(2)}, u32[]{:S(2)}) collective-permute-start(bf16[128,256]{1,0:T(8,128)(2,1)S(1)} %get-tuple-element.123), channel_id=1, source_target_pairs={{0,16},{1,17},{2,18},{3,19},{4,20},{5,21},{6,22},{7,23},{8,24},{9,... | collective-permute-start | bytes 196616 | tf_op jit(solution)/shard_map/ppermute | solution.py:298
  96.7 1.6 %shard_map.77 = (bf16[256,256]{1,0:T(8,128)(2,1)S(1)}, f32[256,256]{1,0:T(8,128)S(1)}, bf16[256,256]{1,0:T(8,128)(2,1)S(1)}, f32[256,256]{1,0:T(8,128)S(1)}) custom-call(s32[4]{0:T(128)S(1)} %copy-done.1, bf16[256,768]{1,0:T(8,128)(2,1)S(1)} %broadcast_select_fusion.refs_0_, bf16[256,768]{1,0:T(8,128)(2,1)S(1)} %collective-permute-done.11.refs_1_, ...), custom_call_target="tpu_custom_call" | custom-call | flops 134217728 | bytes 4194304 | tf_op jit(solution)/shard_map/pallas_call | solution.py:430
  98.3 0.3 collective-permute-done.25.base_ref
  98.6 1.2 %shard_map.78 = (bf16[256,256]{1,0:T(8,128)(2,1)S(1)}, bf16[256,256]{1,0:T(8,128)(2,1)S(1)}) custom-call(s32[4]{0:T(128)S(1)} %copy-done.1, f32[16]{0:T(128)S(1)} %copy-done.2, bf16[128,256]{1,0:T(8,128)(2,1)S(1)} %collective-permute-done.25.base_ref, f32[128,256]{1,0:T(8,128)S(1)} %get-tuple-element.130.refs_0_, f32[128,256]{1,0:T(8,128)S(1)} %get-tuple-element.131.refs_1_, ...), custom_call_target="tpu_custom_call" | custom-call | flops 201326592 | bytes 4194304 | tf_op jit(solution)/shard_map/pallas_call | solution.py:441
  99.7 0.3 collective-permute-start.28
  100.1 3.1 %collective-permute-start.30 = (bf16[256,256]{1,0:T(8,128)(2,1)S(1)}, bf16[256,256]{1,0:T(8,128)(2,1)S(1)}, u32[]{:S(2)}, u32[]{:S(2)}) collective-permute-start(bf16[256,256]{1,0:T(8,128)(2,1)S(1)} %get-tuple-element.137), channel_id=1, source_target_pairs={{0,12},{1,13},{2,14},{3,15},{4,8},{5,9},{6,10},{7,11},{8,4},{9,5},... | collective-permute-start | bytes 393224 | tf_op jit(solution)/shard_map/ppermute | solution.py:298
  103.2 1.8 %shard_map.79 = (bf16[256,256]{1,0:T(8,128)(2,1)S(1)}, f32[256,256]{1,0:T(8,128)S(1)}, bf16[256,256]{1,0:T(8,128)(2,1)S(1)}, f32[256,256]{1,0:T(8,128)S(1)}) custom-call(s32[4]{0:T(128)S(1)} %copy-done.1, bf16[256,768]{1,0:T(8,128)(2,1)S(1)} %broadcast_select_fusion.refs_0_, bf16[256,768]{1,0:T(8,128)(2,1)S(1)} %collective-permute-done.11.refs_1_, ...), custom_call_target="tpu_custom_call" | custom-call | flops 134217728 | bytes 4194304 | tf_op jit(solution)/shard_map/pallas_call | solution.py:430
  104.9 1.2 %shard_map.80 = (bf16[256,256]{1,0:T(8,128)(2,1)S(1)}, bf16[256,256]{1,0:T(8,128)(2,1)S(1)}) custom-call(s32[4]{0:T(128)S(1)} %copy-done.1, f32[16]{0:T(128)S(1)} %copy-done.2, bf16[128,256]{1,0:T(8,128)(2,1)S(1)} %collective-permute-done.25.base_ref, f32[128,256]{1,0:T(8,128)S(1)} %get-tuple-element.130.refs_0_, f32[128,256]{1,0:T(8,128)S(1)} %get-tuple-element.131.refs_1_, ...), custom_call_target="tpu_custom_call" | custom-call | flops 201326592 | bytes 4194304 | tf_op jit(solution)/shard_map/pallas_call | solution.py:441
  106.1 0.3 collective-permute-start.29
  106.4 0.3 collective-permute-start.31
  106.7 1.6 %shard_map.82 = (bf16[256,256]{1,0:T(8,128)(2,1)S(1)}, f32[256,256]{1,0:T(8,128)S(1)}, bf16[256,256]{1,0:T(8,128)(2,1)S(1)}, f32[256,256]{1,0:T(8,128)S(1)}) custom-call(s32[4]{0:T(128)S(1)} %copy-done.1, bf16[256,768]{1,0:T(8,128)(2,1)S(1)} %broadcast_select_fusion.refs_0_, bf16[256,768]{1,0:T(8,128)(2,1)S(1)} %collective-permute-done.11.refs_1_, ...), custom_call_target="tpu_custom_call" | custom-call | flops 134217728 | bytes 4194304 | tf_op jit(solution)/shard_map/pallas_call | solution.py:430
  108.3 1.6 %shard_map.83 = (bf16[256,256]{1,0:T(8,128)(2,1)S(1)}, f32[256,256]{1,0:T(8,128)S(1)}, bf16[256,256]{1,0:T(8,128)(2,1)S(1)}, f32[256,256]{1,0:T(8,128)S(1)}) custom-call(s32[4]{0:T(128)S(1)} %copy-done.1, bf16[256,768]{1,0:T(8,128)(2,1)S(1)} %broadcast_select_fusion.refs_0_, bf16[256,768]{1,0:T(8,128)(2,1)S(1)} %collective-permute-done.11.refs_1_, ...), custom_call_target="tpu_custom_call" | custom-call | flops 134217728 | bytes 4194304 | tf_op jit(solution)/shard_map/pallas_call | solution.py:430
  109.9 1.6 %shard_map.84 = (bf16[256,256]{1,0:T(8,128)(2,1)S(1)}, bf16[256,256]{1,0:T(8,128)(2,1)S(1)}, bf16[256,256]{1,0:T(8,128)(2,1)S(1)}, bf16[256,256]{1,0:T(8,128)(2,1)S(1)}) custom-call(s32[4]{0:T(128)S(1)} %copy-done.1, f32[16]{0:T(128)S(1)} %copy-done.2, bf16[128,256]{1,0:T(8,128)(2,1)S(1)} %collective-permute-done.25.base_ref, ...), custom_call_target="tpu_custom_call" | custom-call | flops 402653184 | bytes 4194304 | tf_op jit(solution)/shard_map/pallas_call | solution.py:441
  111.5 1.4 %collective-permute-start.32 = (bf16[256,256]{1,0:T(8,128)(2,1)S(1)}, bf16[256,256]{1,0:T(8,128)(2,1)S(1)}, u32[]{:S(2)}, u32[]{:S(2)}) collective-permute-start(bf16[256,256]{1,0:T(8,128)(2,1)S(1)} %get-tuple-element.159), channel_id=1, source_target_pairs={{0,4},{1,5},{2,6},{3,7},{4,0},{5,1},{6,2},{7,3},{8,12},{9,13},{10,... | collective-permute-start | bytes 393224 | tf_op jit(solution)/shard_map/ppermute | solution.py:298
  112.9 0.1 collective-permute-start.33
  113.0 1.5 %collective-permute-done.31.refs_3_.refs_8_ = bf16[256,256]{1,0:T(8,128)(2,1)S(1)} collective-permute-done((bf16[256,256]{1,0:T(8,128)(2,1)S(1)}, bf16[256,256]{1,0:T(8,128)(2,1)S(1)}, u32[]{:S(2)}, u32[]{:S(2)}) %collective-permute-start.31) | collective-permute-done | bytes 131104 | tf_op jit(solution)/shard_map/ppermute | solution.py:298
  114.5 1.6 %shard_map.85 = bf16[256,2048]{1,0:T(8,128)(2,1)} custom-call(s32[4]{0:T(128)S(1)} %copy-done.1, f32[8,128]{1,0:T(8,128)S(1)} %shard_map.81.refs_0_, bf16[256,256]{1,0:T(8,128)(2,1)S(1)} %get-tuple-element.157.refs_1_, bf16[256,256]{1,0:T(8,128)(2,1)S(1)} %get-tuple-element.158.refs_2_, bf16[256,256]{1,0:T(8,128)(2,1)S(1)} %collective-permute-done.32.refs_3_, ...), custom_call_target="tpu_custom_call" | custom-call | bytes 4194304 | tf_op jit(solution)/shard_map/pallas_call | solution.py:464
  (48 shorter events, 0.2 us)
Async XLA Ops:
  0.0 16.7 %copy-start.3 = (bf16[1,256,4096]{2,1,0:T(8,128)(2,1)S(1)}, bf16[1,256,4096]{2,1,0:T(8,128)(2,1)}, u32[]{:S(2)}) copy-start(bf16[1,256,4096]{2,1,0:T(8,128)(2,1)} %param.7) | copy-start | bytes 6291460
  0.0 16.6 %collective-permute-start.3 = (bf16[256,4096]{1,0:T(8,128)(2,1)}, bf16[256,4096]{1,0:T(8,128)(2,1)}, u32[]{:S(2)}, u32[]{:S(2)}) collective-permute-start(bf16[256,4096]{1,0:T(8,128)(2,1)} %bitcast.5), channel_id=1, source_target_pairs={{0,4},{1,5},{2,6},{3,7},{4,0},{5,1},{6,2},{7,3},{8,12},{9,13},{10,... | collective-permute-start | bytes 6291464 | tf_op jit(solution)/shard_map/ppermute | solution.py:298
  4.1 2.8 %collective-permute-start = (bf16[144,768]{1,0:T(8,128)(2,1)}, bf16[144,768]{1,0:T(8,128)(2,1)S(1)}, u32[]{:S(2)}, u32[]{:S(2)}) collective-permute-start(bf16[144,768]{1,0:T(8,128)(2,1)} %get-tuple-element.84), channel_id=1, source_target_pairs={{0,4},{1,5},{2,6},{3,7},{4,0},{5,1},{6,2},{7,3},{8,12},{9,13},{10,... | collective-permute-start | bytes 663560 | tf_op jit(solution)/shard_map/ppermute | solution.py:298
  4.2 7.9 %collective-permute-start.2 = (bf16[144,768]{1,0:T(8,128)(2,1)}, bf16[144,768]{1,0:T(8,128)(2,1)S(1)}, u32[]{:S(2)}, u32[]{:S(2)}) collective-permute-start(bf16[144,768]{1,0:T(8,128)(2,1)} %get-tuple-element.86), channel_id=1, source_target_pairs={{0,12},{1,13},{2,14},{3,15},{4,8},{5,9},{6,10},{7,11},{8,4},{9,5},... | collective-permute-start | bytes 663560 | tf_op jit(solution)/shard_map/ppermute | solution.py:298
  5.7 10.9 %collective-permute-start.1 = (bf16[144,768]{1,0:T(8,128)(2,1)}, bf16[144,768]{1,0:T(8,128)(2,1)S(1)}, u32[]{:S(2)}, u32[]{:S(2)}) collective-permute-start(bf16[144,768]{1,0:T(8,128)(2,1)} %get-tuple-element.85), channel_id=1, source_target_pairs={{0,8},{1,9},{2,10},{3,11},{4,12},{5,13},{6,14},{7,15},{8,0},{9,1},... | collective-permute-start | bytes 663560 | tf_op jit(solution)/shard_map/ppermute | solution.py:298
  16.6 50.5 %copy-start.1 = (s32[4]{0:T(128)S(1)}, s32[4]{0:T(128)}, u32[]{:S(2)}) copy-start(s32[4]{0:T(128)} %pad_add_fusion.here_ref) | copy-start | bytes 52
  16.6 10.1 %collective-permute-start.12 = (bf16[256,768]{1,0:T(8,128)(2,1)S(1)}, bf16[256,768]{1,0:T(8,128)(2,1)}, u32[]{:S(2)}, u32[]{:S(2)}) collective-permute-start(bf16[256,768]{1,0:T(8,128)(2,1)S(1)} %pad_maximum_fusion.refs_2_), channel_id=1, source_target_pairs={{0,1},{1,0},{2,3},{3,2},{4,5},{5,4},{6,7},{7,6},{8,9},{9,8},{10,11... | collective-permute-start | bytes 1179656 | tf_op jit(solution)/shard_map/ppermute | solution.py:298
  16.7 56.6 %collective-permute-start.21 = (bf16[256,4096]{1,0:T(8,128)(2,1)S(1)}, bf16[256,4096]{1,0:T(8,128)(2,1)}, u32[]{:S(2)}, u32[]{:S(2)}) collective-permute-start(bf16[256,4096]{1,0:T(8,128)(2,1)S(1)} %bitcast.6), channel_id=1, source_target_pairs={{0,8},{1,9},{2,10},{3,11},{4,12},{5,13},{6,14},{7,15},{8,0},{9,1},... | collective-permute-start | bytes 6291464 | tf_op jit(solution)/shard_map/ppermute | solution.py:298
  18.1 12.6 %collective-permute-start.13 = (bf16[256,768]{1,0:T(8,128)(2,1)S(1)}, bf16[256,768]{1,0:T(8,128)(2,1)}, u32[]{:S(2)}, u32[]{:S(2)}) collective-permute-start(bf16[256,768]{1,0:T(8,128)(2,1)S(1)} %pad_maximum_fusion.refs_2_), channel_id=1, source_target_pairs={{1,2},{2,1},{5,6},{6,5},{9,10},{10,9},{13,14},{14,13},{17,18},{18,... | collective-permute-start | bytes 1179656 | tf_op jit(solution)/shard_map/ppermute | solution.py:298
  22.4 9.5 %collective-permute-start.14 = (bf16[256,768]{1,0:T(8,128)(2,1)S(1)}, bf16[256,768]{1,0:T(8,128)(2,1)S(1)}, u32[]{:S(2)}, u32[]{:S(2)}) collective-permute-start(bf16[256,768]{1,0:T(8,128)(2,1)S(1)} %pad_maximum_fusion.refs_2_), channel_id=1, source_target_pairs={{0,16},{1,17},{2,18},{3,19},{4,20},{5,21},{6,22},{7,23},{8,24},{9,... | collective-permute-start | bytes 1179656 | tf_op jit(solution)/shard_map/ppermute | solution.py:298
  23.7 12.0 %collective-permute-start.4 = (bf16[256,768]{1,0:T(8,128)(2,1)S(1)}, bf16[256,768]{1,0:T(8,128)(2,1)}, u32[]{:S(2)}, u32[]{:S(2)}) collective-permute-start(bf16[256,768]{1,0:T(8,128)(2,1)S(1)} %pad_maximum_fusion.1.refs_9_), channel_id=1, source_target_pairs={{0,1},{1,0},{2,3},{3,2},{4,5},{5,4},{6,7},{7,6},{8,9},{9,8},{10,11... | collective-permute-start | bytes 1179656 | tf_op jit(solution)/shard_map/ppermute | solution.py:298
  26.7 11.5 %collective-permute-start.5 = (bf16[256,768]{1,0:T(8,128)(2,1)S(1)}, bf16[256,768]{1,0:T(8,128)(2,1)}, u32[]{:S(2)}, u32[]{:S(2)}) collective-permute-start(bf16[256,768]{1,0:T(8,128)(2,1)S(1)} %pad_maximum_fusion.1.refs_9_), channel_id=1, source_target_pairs={{1,2},{2,1},{5,6},{6,5},{9,10},{10,9},{13,14},{14,13},{17,18},{18,... | collective-permute-start | bytes 1179656 | tf_op jit(solution)/shard_map/ppermute | solution.py:298
  30.6 8.6 %collective-permute-start.6 = (bf16[256,768]{1,0:T(8,128)(2,1)S(1)}, bf16[256,768]{1,0:T(8,128)(2,1)S(1)}, u32[]{:S(2)}, u32[]{:S(2)}) collective-permute-start(bf16[256,768]{1,0:T(8,128)(2,1)S(1)} %pad_maximum_fusion.1.refs_9_), channel_id=1, source_target_pairs={{0,16},{1,17},{2,18},{3,19},{4,20},{5,21},{6,22},{7,23},{8,24},{9,... | collective-permute-start | bytes 1179656 | tf_op jit(solution)/shard_map/ppermute | solution.py:298
  31.9 0.7 copy-start.4
  32.6 13.8 %collective-permute-start.15 = (bf16[256,768]{1,0:T(8,128)(2,1)}, bf16[256,768]{1,0:T(8,128)(2,1)}, u32[]{:S(2)}, u32[]{:S(2)}) collective-permute-start(bf16[256,768]{1,0:T(8,128)(2,1)} %collective-permute-done.12.refs_3_), channel_id=1, source_target_pairs={{1,2},{2,1},{5,6},{6,5},{9,10},{10,9},{13,14},{14,13},{17,18},{18,... | collective-permute-start | bytes 1179656 | tf_op jit(solution)/shard_map/ppermute | solution.py:298
  35.7 12.8 %collective-permute-start.16 = (bf16[256,768]{1,0:T(8,128)(2,1)}, bf16[256,768]{1,0:T(8,128)(2,1)}, u32[]{:S(2)}, u32[]{:S(2)}) collective-permute-start(bf16[256,768]{1,0:T(8,128)(2,1)} %collective-permute-done.13), channel_id=1, source_target_pairs={{1,0},{2,3},{5,4},{6,7},{9,8},{10,11},{13,12},{14,15},{17,16},{18,... | collective-permute-start | bytes 1179656 | tf_op jit(solution)/shard_map/ppermute | solution.py:298
  38.2 11.6 %collective-permute-start.17 = (bf16[256,768]{1,0:T(8,128)(2,1)}, bf16[256,768]{1,0:T(8,128)(2,1)}, u32[]{:S(2)}, u32[]{:S(2)}) collective-permute-start(bf16[256,768]{1,0:T(8,128)(2,1)} %collective-permute-done.12.refs_3_), channel_id=1, source_target_pairs={{0,16},{1,17},{2,18},{3,19},{4,20},{5,21},{6,22},{7,23},{8,24},{9,... | collective-permute-start | bytes 1179656 | tf_op jit(solution)/shard_map/ppermute | solution.py:298
  39.3 0.8 copy-start.6
  40.0 14.8 %collective-permute-start.7 = (bf16[256,768]{1,0:T(8,128)(2,1)}, bf16[256,768]{1,0:T(8,128)(2,1)}, u32[]{:S(2)}, u32[]{:S(2)}) collective-permute-start(bf16[256,768]{1,0:T(8,128)(2,1)} %collective-permute-done.4.refs_10_), channel_id=1, source_target_pairs={{1,2},{2,1},{5,6},{6,5},{9,10},{10,9},{13,14},{14,13},{17,18},{18,... | collective-permute-start | bytes 1179656 | tf_op jit(solution)/shard_map/ppermute | solution.py:298
  46.4 9.7 %collective-permute-start.8 = (bf16[256,768]{1,0:T(8,128)(2,1)}, bf16[256,768]{1,0:T(8,128)(2,1)}, u32[]{:S(2)}, u32[]{:S(2)}) collective-permute-start(bf16[256,768]{1,0:T(8,128)(2,1)} %collective-permute-done.5), channel_id=1, source_target_pairs={{1,0},{2,3},{5,4},{6,7},{9,8},{10,11},{13,12},{14,15},{17,16},{18,... | collective-permute-start | bytes 1179656 | tf_op jit(solution)/shard_map/ppermute | solution.py:298
  48.5 18.6 %copy-start.5 = (bf16[256,768]{1,0:T(8,128)(2,1)S(1)}, bf16[256,768]{1,0:T(8,128)(2,1)}, u32[]{:S(2)}) copy-start(bf16[256,768]{1,0:T(8,128)(2,1)} %copy-done.4) | copy-start | bytes 1179652
  48.5 18.6 %copy-start.7 = (bf16[256,768]{1,0:T(8,128)(2,1)S(1)}, bf16[256,768]{1,0:T(8,128)(2,1)}, u32[]{:S(2)}) copy-start(bf16[256,768]{1,0:T(8,128)(2,1)} %copy-done.6) | copy-start | bytes 1179652
  48.5 11.1 %collective-permute-start.9 = (bf16[256,768]{1,0:T(8,128)(2,1)}, bf16[256,768]{1,0:T(8,128)(2,1)S(1)}, u32[]{:S(2)}, u32[]{:S(2)}) collective-permute-start(bf16[256,768]{1,0:T(8,128)(2,1)} %collective-permute-done.4.refs_10_), channel_id=1, source_target_pairs={{0,16},{1,17},{2,18},{3,19},{4,20},{5,21},{6,22},{7,23},{8,24},{9,... | collective-permute-start | bytes 1179656 | tf_op jit(solution)/shard_map/ppermute | solution.py:298
  49.8 12.3 %collective-permute-start.18 = (bf16[256,768]{1,0:T(8,128)(2,1)}, bf16[256,768]{1,0:T(8,128)(2,1)S(1)}, u32[]{:S(2)}, u32[]{:S(2)}) collective-permute-start(bf16[256,768]{1,0:T(8,128)(2,1)} %collective-permute-done.15), channel_id=1, source_target_pairs={{1,0},{2,3},{5,4},{6,7},{9,8},{10,11},{13,12},{14,15},{17,16},{18,... | collective-permute-start | bytes 1179656 | tf_op jit(solution)/shard_map/ppermute | solution.py:298
  54.9 11.1 %collective-permute-start.19 = (bf16[256,768]{1,0:T(8,128)(2,1)S(1)}, bf16[256,768]{1,0:T(8,128)(2,1)S(1)}, u32[]{:S(2)}, u32[]{:S(2)}) collective-permute-start(bf16[256,768]{1,0:T(8,128)(2,1)S(1)} %broadcast_select_fusion.2.refs_4_), channel_id=1, source_target_pairs={{0,16},{1,17},{2,18},{3,19},{4,20},{5,21},{6,22},{7,23},{8,24},{9,... | collective-permute-start | bytes 1179656 | tf_op jit(solution)/shard_map/ppermute | solution.py:298
  56.1 9.9 %collective-permute-start.20 = (bf16[256,768]{1,0:T(8,128)(2,1)}, bf16[256,768]{1,0:T(8,128)(2,1)S(1)}, u32[]{:S(2)}, u32[]{:S(2)}) collective-permute-start(bf16[256,768]{1,0:T(8,128)(2,1)} %collective-permute-done.17.refs_7_), channel_id=1, source_target_pairs={{1,2},{2,1},{5,6},{6,5},{9,10},{10,9},{13,14},{14,13},{17,18},{18,... | collective-permute-start | bytes 1179656 | tf_op jit(solution)/shard_map/ppermute | solution.py:298
  59.6 13.7 %collective-permute-start.10 = (bf16[256,768]{1,0:T(8,128)(2,1)}, bf16[256,768]{1,0:T(8,128)(2,1)S(1)}, u32[]{:S(2)}, u32[]{:S(2)}) collective-permute-start(bf16[256,768]{1,0:T(8,128)(2,1)} %collective-permute-done.7), channel_id=1, source_target_pairs={{1,0},{2,3},{5,4},{6,7},{9,8},{10,11},{13,12},{14,15},{17,16},{18,... | collective-permute-start | bytes 1179656 | tf_op jit(solution)/shard_map/ppermute | solution.py:298
  62.0 12.4 %collective-permute-start.11 = (bf16[256,768]{1,0:T(8,128)(2,1)S(1)}, bf16[256,768]{1,0:T(8,128)(2,1)S(1)}, u32[]{:S(2)}, u32[]{:S(2)}) collective-permute-start(bf16[256,768]{1,0:T(8,128)(2,1)S(1)} %broadcast_select_fusion.3.refs_11_), channel_id=1, source_target_pairs={{0,16},{1,17},{2,18},{3,19},{4,20},{5,21},{6,22},{7,23},{8,24},{9,... | collective-permute-start | bytes 1179656 | tf_op jit(solution)/shard_map/ppermute | solution.py:298
  74.4 13.1 %collective-permute-start.24 = (bf16[256,4096]{1,0:T(8,128)(2,1)}, bf16[256,4096]{1,0:T(8,128)(2,1)S(1)}, u32[]{:S(2)}, u32[]{:S(2)}) collective-permute-start(bf16[256,4096]{1,0:T(8,128)(2,1)} %collective-permute-done.21.refs_0_), channel_id=1, source_target_pairs={{0,4},{1,5},{2,6},{3,7},{4,0},{5,1},{6,2},{7,3},{8,12},{9,13},{10,... | collective-permute-start | bytes 6291464 | tf_op jit(solution)/shard_map/ppermute | solution.py:298
  83.2 10.5 %copy-start = (bf16[144,768]{1,0:T(8,128)(2,1)S(1)}, bf16[144,768]{1,0:T(8,128)(2,1)}, u32[]{:S(2)}) copy-start(bf16[144,768]{1,0:T(8,128)(2,1)} %get-tuple-element.83.refs_13_.refs_8_.refs_5_) | copy-start | bytes 663556
  83.2 10.5 %collective-permute-start.22 = (bf16[256,256]{1,0:T(8,128)(2,1)S(1)}, bf16[256,256]{1,0:T(8,128)(2,1)S(1)}, u32[]{:S(2)}, u32[]{:S(2)}) collective-permute-start(bf16[256,256]{1,0:T(8,128)(2,1)S(1)} %slice.28), channel_id=1, source_target_pairs={{1,0},{2,3},{5,4},{6,7},{9,8},{10,11},{13,12},{14,15},{17,16},{18,... | collective-permute-start | bytes 393224 | tf_op jit(solution)/shard_map/ppermute | solution.py:298
  84.6 9.0 %collective-permute-start.23 = (bf16[256,256]{1,0:T(8,128)(2,1)S(1)}, bf16[256,256]{1,0:T(8,128)(2,1)S(1)}, u32[]{:S(2)}, u32[]{:S(2)}) collective-permute-start(bf16[256,256]{1,0:T(8,128)(2,1)S(1)} %slice.35), channel_id=1, source_target_pairs={{0,16},{1,17},{2,18},{3,19},{4,20},{5,21},{6,22},{7,23},{8,24},{9,... | collective-permute-start | bytes 393224 | tf_op jit(solution)/shard_map/ppermute | solution.py:298
  85.9 10.8 %collective-permute-start.26 = (bf16[256,512]{1,0:T(8,128)(2,1)S(1)}, bf16[256,512]{1,0:T(8,128)(2,1)S(1)}, u32[]{:S(2)}, u32[]{:S(2)}) collective-permute-start(bf16[256,512]{1,0:T(8,128)(2,1)S(1)} %slice.30), channel_id=1, source_target_pairs={{1,0},{2,3},{5,4},{6,7},{9,8},{10,11},{13,12},{14,15},{17,16},{18,... | collective-permute-start | bytes 786440 | tf_op jit(solution)/shard_map/ppermute | solution.py:298
  87.2 9.5 %collective-permute-start.27 = (bf16[256,512]{1,0:T(8,128)(2,1)S(1)}, bf16[256,512]{1,0:T(8,128)(2,1)S(1)}, u32[]{:S(2)}, u32[]{:S(2)}) collective-permute-start(bf16[256,512]{1,0:T(8,128)(2,1)S(1)} %slice.36), channel_id=1, source_target_pairs={{0,16},{1,17},{2,18},{3,19},{4,20},{5,21},{6,22},{7,23},{8,24},{9,... | collective-permute-start | bytes 786440 | tf_op jit(solution)/shard_map/ppermute | solution.py:298
  95.4 3.2 %collective-permute-start.25 = (bf16[128,256]{1,0:T(8,128)(2,1)S(1)}, bf16[128,256]{1,0:T(8,128)(2,1)S(1)}, u32[]{:S(2)}, u32[]{:S(2)}) collective-permute-start(bf16[128,256]{1,0:T(8,128)(2,1)S(1)} %get-tuple-element.123), channel_id=1, source_target_pairs={{0,16},{1,17},{2,18},{3,19},{4,20},{5,21},{6,22},{7,23},{8,24},{9,... | collective-permute-start | bytes 196616 | tf_op jit(solution)/shard_map/ppermute | solution.py:298
  96.7 1.9 %copy-start.2 = (f32[16]{0:T(128)S(1)}, f32[16]{0:T(128)}, u32[]{:S(2)}) copy-start(f32[16]{0:T(128)} %gate_ref.5) | copy-start | bytes 196
  99.7 13.1 %collective-permute-start.28 = (bf16[256,256]{1,0:T(8,128)(2,1)S(1)}, bf16[256,256]{1,0:T(8,128)(2,1)S(1)}, u32[]{:S(2)}, u32[]{:S(2)}) collective-permute-start(bf16[256,256]{1,0:T(8,128)(2,1)S(1)} %get-tuple-element.136), channel_id=1, source_target_pairs={{0,8},{1,9},{2,10},{3,11},{4,12},{5,13},{6,14},{7,15},{8,0},{9,1},... | collective-permute-start | bytes 393224 | tf_op jit(solution)/shard_map/ppermute | solution.py:298
  100.1 12.9 %collective-permute-start.30 = (bf16[256,256]{1,0:T(8,128)(2,1)S(1)}, bf16[256,256]{1,0:T(8,128)(2,1)S(1)}, u32[]{:S(2)}, u32[]{:S(2)}) collective-permute-start(bf16[256,256]{1,0:T(8,128)(2,1)S(1)} %get-tuple-element.137), channel_id=1, source_target_pairs={{0,12},{1,13},{2,14},{3,15},{4,8},{5,9},{6,10},{7,11},{8,4},{9,5},... | collective-permute-start | bytes 393224 | tf_op jit(solution)/shard_map/ppermute | solution.py:298
  106.1 6.9 %collective-permute-start.29 = (bf16[256,256]{1,0:T(8,128)(2,1)S(1)}, bf16[256,256]{1,0:T(8,128)(2,1)S(1)}, u32[]{:S(2)}, u32[]{:S(2)}) collective-permute-start(bf16[256,256]{1,0:T(8,128)(2,1)S(1)} %get-tuple-element.143), channel_id=1, source_target_pairs={{0,8},{1,9},{2,10},{3,11},{4,12},{5,13},{6,14},{7,15},{8,0},{9,1},... | collective-permute-start | bytes 393224 | tf_op jit(solution)/shard_map/ppermute | solution.py:298
  106.4 8.0 %collective-permute-start.31 = (bf16[256,256]{1,0:T(8,128)(2,1)S(1)}, bf16[256,256]{1,0:T(8,128)(2,1)S(1)}, u32[]{:S(2)}, u32[]{:S(2)}) collective-permute-start(bf16[256,256]{1,0:T(8,128)(2,1)S(1)} %get-tuple-element.144), channel_id=1, source_target_pairs={{0,12},{1,13},{2,14},{3,15},{4,8},{5,9},{6,10},{7,11},{8,4},{9,5},... | collective-permute-start | bytes 393224 | tf_op jit(solution)/shard_map/ppermute | solution.py:298
  111.5 3.0 %collective-permute-start.32 = (bf16[256,256]{1,0:T(8,128)(2,1)S(1)}, bf16[256,256]{1,0:T(8,128)(2,1)S(1)}, u32[]{:S(2)}, u32[]{:S(2)}) collective-permute-start(bf16[256,256]{1,0:T(8,128)(2,1)S(1)} %get-tuple-element.159), channel_id=1, source_target_pairs={{0,4},{1,5},{2,6},{3,7},{4,0},{5,1},{6,2},{7,3},{8,12},{9,13},{10,... | collective-permute-start | bytes 393224 | tf_op jit(solution)/shard_map/ppermute | solution.py:298
  112.9 1.6 %collective-permute-start.33 = (bf16[256,256]{1,0:T(8,128)(2,1)S(1)}, bf16[256,256]{1,0:T(8,128)(2,1)S(1)}, u32[]{:S(2)}, u32[]{:S(2)}) collective-permute-start(bf16[256,256]{1,0:T(8,128)(2,1)S(1)} %get-tuple-element.160), channel_id=1, source_target_pairs={{0,4},{1,5},{2,6},{3,7},{4,0},{5,1},{6,2},{7,3},{8,12},{9,13},{10,... | collective-permute-start | bytes 393224 | tf_op jit(solution)/shard_map/ppermute | solution.py:298

commit v17 on v14

--- a/solution.py
+++ b/solution.py
@@ -428,11 +428,12 @@
             *[ready[key][0] for key in keys], *[ready[key][1] for key in keys],
         )
 
-    ready = local((2, 3, 1, 0), 0)
+    ready = local((2, 3), 0)
     base = after(base, *ready[2, 0])
     two0, three0 = mix((2, 3), (0,), base, ready)
     ready |= local((2, 3), 1, two0, three0)
     two1, three1 = mix((2, 3), (1,), base, ready)
+    ready |= local((1, 0), 0, two1, three1)
     ready |= local((1, 0), 1, two1, three1)
     one0, one1, mine0, mine1 = mix((1, 0), (0, 1), after(base, two1, three1), ready)
     sent = [mine0, mine1]

time: 115 us -> 114 us (level)
  waiting for transfers between devices: 28.7 us -> 27.1 us
    ppermute x34, waiting for transfers between devices: 28.7 us -> 27.1 us  [permute(): return lax.ppermute(array, AXES, pairs)]
    pallas_call x3 -> x4, Pallas kernels: 5.44 us -> 6.49 us  [local(): call(functools.partial(local_body, len(segs), len(late) + 1, halves[1 + p...]
  transfers between devices with their start and end apart: 34 -> 34, of which waited for: 11 -> 10; matrix products, arithmetic and copies ran while one was open for 5% -> 5% of each run, Pallas kernels for 19% -> 20%
where the time goes in v17:
time: 114 us
  starting transfers between devices  52.4 us (46%)
  waiting for transfers between devices  27.1 us (24%)
  Pallas kernels  25.7 us (23%)
  other arithmetic  4.87 us (4%)
  local copies, waits for them, and re-layouts  2.56 us (2%)
    ppermute x34, starting transfers between devices, permute(): return lax.ppermute(array, AXES, pairs)  52.4 us
    ppermute x34, waiting for transfers between devices, permute(): return lax.ppermute(array, AXES, pairs)  27.1 us
    pallas_call x2, Pallas kernels, project(): call(functools.partial(project_body, early, late, line), [shape((length,...  9.75 us
    pallas_call x4, Pallas kernels, local(): call(functools.partial(local_body, len(segs), len(late) + 1, halves[1 + p...  6.49 us
    pallas_call x3, Pallas kernels, mix(): call(functools.partial(mix_body, segs, parts, group), [shape((length, hal...  3.96 us
  transfers between devices with their start and end apart: 34, of which 10 were waited for; matrix products, arithmetic and copies ran while one was open for 5% of the time, Pallas kernels for 20%

profile of v17, /device:TPU:9, one launch (start us, length us, event | category | flops | bytes accessed | tf_op | source)
XLA Modules:
  0.0 113.7 jit_solution(2754254864128910151)
XLA Ops:
  0.0 0.7 collective-permute-start.3
  1.3 0.6 pad_add_fusion.here_ref
  1.9 2.1 %shard_map.73 = (bf16[144,768]{1,0:T(8,128)(2,1)}, bf16[144,768]{1,0:T(8,128)(2,1)}, bf16[144,768]{1,0:T(8,128)(2,1)}, bf16[144,768]{1,0:T(8,128)(2,1)}) custom-call(s32[4]{0:T(128)} %pad_add_fusion.here_ref, s32[1,1]{1,0:T(1,128)S(6)} %copy.8.valid_ref, s32[1,1,2,2]{3,2,1,0:T(2,128)} %mask_ref.1, bf16[128,2048]{1,0:T(8,128)(2,1)} %wq_ref.1, ...), custom_call_target="tpu_custom_call" | custom-call | bytes 4194304 | tf_op jit(solution)/shard_map/pallas_call | solution.py:285
  4.1 0.2 collective-permute-start
  4.2 1.5 %collective-permute-start.2 = (bf16[144,768]{1,0:T(8,128)(2,1)}, bf16[144,768]{1,0:T(8,128)(2,1)S(1)}, u32[]{:S(2)}, u32[]{:S(2)}) collective-permute-start(bf16[144,768]{1,0:T(8,128)(2,1)} %get-tuple-element.84), channel_id=1, source_target_pairs={{0,12},{1,13},{2,14},{3,15},{4,8},{5,9},{6,10},{7,11},{8,4},{9,5},... | collective-permute-start | bytes 663560 | tf_op jit(solution)/shard_map/ppermute | solution.py:279
  5.7 0.3 collective-permute-start.1
  5.9 0.9 slice.24
  6.9 5.3 %collective-permute-done.2.refs_16_.refs_8_.refs_5_ = bf16[144,768]{1,0:T(8,128)(2,1)S(1)} collective-permute-done((bf16[144,768]{1,0:T(8,128)(2,1)}, bf16[144,768]{1,0:T(8,128)(2,1)S(1)}, u32[]{:S(2)}, u32[]{:S(2)}) %collective-permute-start.2) | collective-permute-done | bytes 221216 | tf_op jit(solution)/shard_map/ppermute | solution.py:279
  12.2 4.4 %collective-permute-done.1.refs_15_.refs_7_.refs_4_ = bf16[144,768]{1,0:T(8,128)(2,1)S(1)} collective-permute-done((bf16[144,768]{1,0:T(8,128)(2,1)}, bf16[144,768]{1,0:T(8,128)(2,1)S(1)}, u32[]{:S(2)}, u32[]{:S(2)}) %collective-permute-start.1) | collective-permute-done | bytes 221216 | tf_op jit(solution)/shard_map/ppermute | solution.py:279
  16.6 0.0 collective-permute-done.3.refs_1_
  16.6 0.1 collective-permute-start.12
  16.7 1.4 %collective-permute-start.21 = (bf16[256,4096]{1,0:T(8,128)(2,1)S(1)}, bf16[256,4096]{1,0:T(8,128)(2,1)}, u32[]{:S(2)}, u32[]{:S(2)}) collective-permute-start(bf16[256,4096]{1,0:T(8,128)(2,1)S(1)} %bitcast.6), channel_id=1, source_target_pairs={{0,8},{1,9},{2,10},{3,11},{4,12},{5,13},{6,14},{7,15},{8,0},{9,1},... | collective-permute-start | bytes 6291464 | tf_op jit(solution)/shard_map/ppermute | solution.py:279
  18.1 4.3 %collective-permute-start.13 = (bf16[256,768]{1,0:T(8,128)(2,1)S(1)}, bf16[256,768]{1,0:T(8,128)(2,1)}, u32[]{:S(2)}, u32[]{:S(2)}) collective-permute-start(bf16[256,768]{1,0:T(8,128)(2,1)S(1)} %pad_maximum_fusion.refs_2_), channel_id=1, source_target_pairs={{1,2},{2,1},{5,6},{6,5},{9,10},{10,9},{13,14},{14,13},{17,18},{18,... | collective-permute-start | bytes 1179656 | tf_op jit(solution)/shard_map/ppermute | solution.py:279
  22.4 1.3 %collective-permute-start.14 = (bf16[256,768]{1,0:T(8,128)(2,1)S(1)}, bf16[256,768]{1,0:T(8,128)(2,1)S(1)}, u32[]{:S(2)}, u32[]{:S(2)}) collective-permute-start(bf16[256,768]{1,0:T(8,128)(2,1)S(1)} %pad_maximum_fusion.refs_2_), channel_id=1, source_target_pairs={{0,16},{1,17},{2,18},{3,19},{4,20},{5,21},{6,22},{7,23},{8,24},{9,... | collective-permute-start | bytes 1179656 | tf_op jit(solution)/shard_map/ppermute | solution.py:279
  23.7 3.0 %collective-permute-done.12.refs_3_ = bf16[256,768]{1,0:T(8,128)(2,1)} collective-permute-done((bf16[256,768]{1,0:T(8,128)(2,1)S(1)}, bf16[256,768]{1,0:T(8,128)(2,1)}, u32[]{:S(2)}, u32[]{:S(2)}) %collective-permute-start.12) | collective-permute-done | bytes 393248 | tf_op jit(solution)/shard_map/ppermute | solution.py:279
  26.7 3.2 %collective-permute-start.5 = (bf16[256,768]{1,0:T(8,128)(2,1)S(1)}, bf16[256,768]{1,0:T(8,128)(2,1)}, u32[]{:S(2)}, u32[]{:S(2)}) collective-permute-start(bf16[256,768]{1,0:T(8,128)(2,1)S(1)} %pad_maximum_fusion.1.refs_9_), channel_id=1, source_target_pairs={{1,2},{2,1},{5,6},{6,5},{9,10},{10,9},{13,14},{14,13},{17,18},{18,... | collective-permute-start | bytes 1179656 | tf_op jit(solution)/shard_map/ppermute | solution.py:279
  29.9 0.7 collective-permute-done.13
  30.6 1.2 %collective-permute-start.6 = (bf16[256,768]{1,0:T(8,128)(2,1)S(1)}, bf16[256,768]{1,0:T(8,128)(2,1)S(1)}, u32[]{:S(2)}, u32[]{:S(2)}) collective-permute-start(bf16[256,768]{1,0:T(8,128)(2,1)S(1)} %pad_maximum_fusion.1.refs_9_), channel_id=1, source_target_pairs={{0,16},{1,17},{2,18},{3,19},{4,20},{5,21},{6,22},{7,23},{8,24},{9,... | collective-permute-start | bytes 1179656 | tf_op jit(solution)/shard_map/ppermute | solution.py:279
  31.9 0.7 copy-done.4
  32.6 3.1 %collective-permute-start.15 = (bf16[256,768]{1,0:T(8,128)(2,1)}, bf16[256,768]{1,0:T(8,128)(2,1)}, u32[]{:S(2)}, u32[]{:S(2)}) collective-permute-start(bf16[256,768]{1,0:T(8,128)(2,1)} %collective-permute-done.12.refs_3_), channel_id=1, source_target_pairs={{1,2},{2,1},{5,6},{6,5},{9,10},{10,9},{13,14},{14,13},{17,18},{18,... | collective-permute-start | bytes 1179656 | tf_op jit(solution)/shard_map/ppermute | solution.py:279
  35.7 2.5 %collective-permute-start.16 = (bf16[256,768]{1,0:T(8,128)(2,1)}, bf16[256,768]{1,0:T(8,128)(2,1)}, u32[]{:S(2)}, u32[]{:S(2)}) collective-permute-start(bf16[256,768]{1,0:T(8,128)(2,1)} %collective-permute-done.13), channel_id=1, source_target_pairs={{1,0},{2,3},{5,4},{6,7},{9,8},{10,11},{13,12},{14,15},{17,16},{18,... | collective-permute-start | bytes 1179656 | tf_op jit(solution)/shard_map/ppermute | solution.py:279
  38.2 1.1 collective-permute-start.17
  39.3 0.8 copy-done.6
  40.0 4.3 %collective-permute-start.7 = (bf16[256,768]{1,0:T(8,128)(2,1)}, bf16[256,768]{1,0:T(8,128)(2,1)}, u32[]{:S(2)}, u32[]{:S(2)}) collective-permute-start(bf16[256,768]{1,0:T(8,128)(2,1)} %collective-permute-done.4.refs_10_), channel_id=1, source_target_pairs={{1,2},{2,1},{5,6},{6,5},{9,10},{10,9},{13,14},{14,13},{17,18},{18,... | collective-permute-start | bytes 1179656 | tf_op jit(solution)/shard_map/ppermute | solution.py:279
  44.4 2.1 %collective-permute-done.15 = bf16[256,768]{1,0:T(8,128)(2,1)} collective-permute-done((bf16[256,768]{1,0:T(8,128)(2,1)}, bf16[256,768]{1,0:T(8,128)(2,1)}, u32[]{:S(2)}, u32[]{:S(2)}) %collective-permute-start.15) | collective-permute-done | bytes 393248 | tf_op jit(solution)/shard_map/ppermute | solution.py:279
  46.4 2.1 %collective-permute-start.8 = (bf16[256,768]{1,0:T(8,128)(2,1)}, bf16[256,768]{1,0:T(8,128)(2,1)}, u32[]{:S(2)}, u32[]{:S(2)}) collective-permute-start(bf16[256,768]{1,0:T(8,128)(2,1)} %collective-permute-done.5), channel_id=1, source_target_pairs={{1,0},{2,3},{5,4},{6,7},{9,8},{10,11},{13,12},{14,15},{17,16},{18,... | collective-permute-start | bytes 1179656 | tf_op jit(solution)/shard_map/ppermute | solution.py:279
  48.5 1.2 %collective-permute-start.9 = (bf16[256,768]{1,0:T(8,128)(2,1)}, bf16[256,768]{1,0:T(8,128)(2,1)S(1)}, u32[]{:S(2)}, u32[]{:S(2)}) collective-permute-start(bf16[256,768]{1,0:T(8,128)(2,1)} %collective-permute-done.4.refs_10_), channel_id=1, source_target_pairs={{0,16},{1,17},{2,18},{3,19},{4,20},{5,21},{6,22},{7,23},{8,24},{9,... | collective-permute-start | bytes 1179656 | tf_op jit(solution)/shard_map/ppermute | solution.py:279
  49.8 1.3 %collective-permute-start.18 = (bf16[256,768]{1,0:T(8,128)(2,1)}, bf16[256,768]{1,0:T(8,128)(2,1)S(1)}, u32[]{:S(2)}, u32[]{:S(2)}) collective-permute-start(bf16[256,768]{1,0:T(8,128)(2,1)} %collective-permute-done.15), channel_id=1, source_target_pairs={{1,0},{2,3},{5,4},{6,7},{9,8},{10,11},{13,12},{14,15},{17,16},{18,... | collective-permute-start | bytes 1179656 | tf_op jit(solution)/shard_map/ppermute | solution.py:279
  51.1 1.1 broadcast_select_fusion.2.refs_4_
  52.1 2.8 %collective-permute-done.7 = bf16[256,768]{1,0:T(8,128)(2,1)} collective-permute-done((bf16[256,768]{1,0:T(8,128)(2,1)}, bf16[256,768]{1,0:T(8,128)(2,1)}, u32[]{:S(2)}, u32[]{:S(2)}) %collective-permute-start.7) | collective-permute-done | bytes 393248 | tf_op jit(solution)/shard_map/ppermute | solution.py:279
  54.9 1.2 %collective-permute-start.19 = (bf16[256,768]{1,0:T(8,128)(2,1)S(1)}, bf16[256,768]{1,0:T(8,128)(2,1)S(1)}, u32[]{:S(2)}, u32[]{:S(2)}) collective-permute-start(bf16[256,768]{1,0:T(8,128)(2,1)S(1)} %broadcast_select_fusion.2.refs_4_), channel_id=1, source_target_pairs={{0,16},{1,17},{2,18},{3,19},{4,20},{5,21},{6,22},{7,23},{8,24},{9,... | collective-permute-start | bytes 1179656 | tf_op jit(solution)/shard_map/ppermute | solution.py:279
  56.1 3.5 %collective-permute-start.20 = (bf16[256,768]{1,0:T(8,128)(2,1)}, bf16[256,768]{1,0:T(8,128)(2,1)S(1)}, u32[]{:S(2)}, u32[]{:S(2)}) collective-permute-start(bf16[256,768]{1,0:T(8,128)(2,1)} %collective-permute-done.17.refs_7_), channel_id=1, source_target_pairs={{1,2},{2,1},{5,6},{6,5},{9,10},{10,9},{13,14},{14,13},{17,18},{18,... | collective-permute-start | bytes 1179656 | tf_op jit(solution)/shard_map/ppermute | solution.py:279
  59.6 1.3 %collective-permute-start.10 = (bf16[256,768]{1,0:T(8,128)(2,1)}, bf16[256,768]{1,0:T(8,128)(2,1)S(1)}, u32[]{:S(2)}, u32[]{:S(2)}) collective-permute-start(bf16[256,768]{1,0:T(8,128)(2,1)} %collective-permute-done.7), channel_id=1, source_target_pairs={{1,0},{2,3},{5,4},{6,7},{9,8},{10,11},{13,12},{14,15},{17,16},{18,... | collective-permute-start | bytes 1179656 | tf_op jit(solution)/shard_map/ppermute | solution.py:279
  61.0 1.1 broadcast_select_fusion.3.refs_11_
  62.0 0.3 collective-permute-start.11
  62.3 3.7 %collective-permute-done.19.refs_8_ = bf16[256,768]{1,0:T(8,128)(2,1)S(1)} collective-permute-done((bf16[256,768]{1,0:T(8,128)(2,1)S(1)}, bf16[256,768]{1,0:T(8,128)(2,1)S(1)}, u32[]{:S(2)}, u32[]{:S(2)}) %collective-permute-start.19) | collective-permute-done | bytes 393248 | tf_op jit(solution)/shard_map/ppermute | solution.py:279
  66.0 1.1 broadcast_select_fusion.1.refs_5_
  67.1 4.9 %shard_map.74 = (f32[256,768]{1,0:T(8,128)S(1)}, f32[256,768]{1,0:T(8,128)S(1)}, bf16[256,1024]{1,0:T(8,128)(2,1)S(1)}, bf16[256,1024]{1,0:T(8,128)(2,1)S(1)}) custom-call(s32[4]{0:T(128)S(1)} %copy-done.1, bf16[256,4096]{1,0:T(8,128)(2,1)S(1)} %bitcast.7, bf16[256,4096]{1,0:T(8,128)(2,1)} %collective-permute-done.3.refs_1_, ...), custom_call_target="tpu_custom_call" | custom-call | flops 2415919104 | bytes 4194304 | tf_op jit(solution)/shard_map/pallas_call | solution.py:317
  72.0 2.4 %collective-permute-done.11.refs_1_ = bf16[256,768]{1,0:T(8,128)(2,1)S(1)} collective-permute-done((bf16[256,768]{1,0:T(8,128)(2,1)S(1)}, bf16[256,768]{1,0:T(8,128)(2,1)S(1)}, u32[]{:S(2)}, u32[]{:S(2)}) %collective-permute-start.11) | collective-permute-done | bytes 393248 | tf_op jit(solution)/shard_map/ppermute | solution.py:279
  74.4 6.2 %collective-permute-start.24 = (bf16[256,4096]{1,0:T(8,128)(2,1)}, bf16[256,4096]{1,0:T(8,128)(2,1)S(1)}, u32[]{:S(2)}, u32[]{:S(2)}) collective-permute-start(bf16[256,4096]{1,0:T(8,128)(2,1)} %collective-permute-done.21.refs_0_), channel_id=1, source_target_pairs={{0,4},{1,5},{2,6},{3,7},{4,0},{5,1},{6,2},{7,3},{8,12},{9,13},{10,... | collective-permute-start | bytes 6291464 | tf_op jit(solution)/shard_map/ppermute | solution.py:279
  80.7 1.3 %collective-permute-start.22 = (bf16[256,256]{1,0:T(8,128)(2,1)S(1)}, bf16[256,256]{1,0:T(8,128)(2,1)S(1)}, u32[]{:S(2)}, u32[]{:S(2)}) collective-permute-start(bf16[256,256]{1,0:T(8,128)(2,1)S(1)} %slice.28), channel_id=1, source_target_pairs={{1,0},{2,3},{5,4},{6,7},{9,8},{10,11},{13,12},{14,15},{17,16},{18,... | collective-permute-start | bytes 393224 | tf_op jit(solution)/shard_map/ppermute | solution.py:279
  82.0 1.3 %collective-permute-start.26 = (bf16[256,512]{1,0:T(8,128)(2,1)S(1)}, bf16[256,512]{1,0:T(8,128)(2,1)S(1)}, u32[]{:S(2)}, u32[]{:S(2)}) collective-permute-start(bf16[256,512]{1,0:T(8,128)(2,1)S(1)} %slice.30), channel_id=1, source_target_pairs={{1,0},{2,3},{5,4},{6,7},{9,8},{10,11},{13,12},{14,15},{17,16},{18,... | collective-permute-start | bytes 786440 | tf_op jit(solution)/shard_map/ppermute | solution.py:279
  83.3 1.1 broadcast_select_fusion.refs_0_
  84.4 1.3 %collective-permute-start.23 = (bf16[256,256]{1,0:T(8,128)(2,1)S(1)}, bf16[256,256]{1,0:T(8,128)(2,1)S(1)}, u32[]{:S(2)}, u32[]{:S(2)}) collective-permute-start(bf16[256,256]{1,0:T(8,128)(2,1)S(1)} %slice.35), channel_id=1, source_target_pairs={{0,16},{1,17},{2,18},{3,19},{4,20},{5,21},{6,22},{7,23},{8,24},{9,... | collective-permute-start | bytes 393224 | tf_op jit(solution)/shard_map/ppermute | solution.py:279
  85.8 0.2 collective-permute-start.27
  86.0 4.9 %shard_map.75 = (f32[256,768]{1,0:T(8,128)S(1)}, f32[256,768]{1,0:T(8,128)S(1)}, bf16[256,1024]{1,0:T(8,128)(2,1)S(1)}, bf16[256,1024]{1,0:T(8,128)(2,1)S(1)}) custom-call(s32[4]{0:T(128)S(1)} %copy-done.1, bf16[256,4096]{1,0:T(8,128)(2,1)} %collective-permute-done.21.refs_0_, bf16[256,4096]{1,0:T(8,128)(2,1)S(1)} %collective-permute-done.24.refs_1_, ...), custom_call_target="tpu_custom_call" | custom-call | flops 2415919104 | bytes 4194304 | tf_op jit(solution)/shard_map/pallas_call | solution.py:317
  90.9 1.7 %shard_map.76 = (bf16[256,256]{1,0:T(8,128)(2,1)S(1)}, f32[128,256]{1,0:T(8,128)S(1)}, bf16[256,256]{1,0:T(8,128)(2,1)S(1)}, f32[128,256]{1,0:T(8,128)S(1)}, bf1...) custom-call(s32[4]{0:T(128)S(1)} %copy-done.1, ...), custom_call_target="tpu_custom_call" | custom-call | flops 536870912 | bytes 4194304 | tf_op jit(solution)/shard_map/pallas_call | solution.py:390
  92.6 1.3 %collective-permute-start.25 = (bf16[128,256]{1,0:T(8,128)(2,1)S(1)}, bf16[128,256]{1,0:T(8,128)(2,1)S(1)}, u32[]{:S(2)}, u32[]{:S(2)}) collective-permute-start(bf16[128,256]{1,0:T(8,128)(2,1)S(1)} %get-tuple-element.120), channel_id=1, source_target_pairs={{0,16},{1,17},{2,18},{3,19},{4,20},{5,21},{6,22},{7,23},{8,24},{9,... | collective-permute-start | bytes 196616 | tf_op jit(solution)/shard_map/ppermute | solution.py:279
  93.9 1.3 %collective-permute-done.27.refs_4_ = bf16[256,512]{1,0:T(8,128)(2,1)S(1)} collective-permute-done((bf16[256,512]{1,0:T(8,128)(2,1)S(1)}, bf16[256,512]{1,0:T(8,128)(2,1)S(1)}, u32[]{:S(2)}, u32[]{:S(2)}) %collective-permute-start.27) | collective-permute-done | bytes 262176 | tf_op jit(solution)/shard_map/ppermute | solution.py:279
  95.2 1.6 %shard_map.77 = (bf16[256,256]{1,0:T(8,128)(2,1)S(1)}, f32[256,256]{1,0:T(8,128)S(1)}, bf16[256,256]{1,0:T(8,128)(2,1)S(1)}, f32[256,256]{1,0:T(8,128)S(1)}) custom-call(s32[4]{0:T(128)S(1)} %copy-done.1, bf16[256,768]{1,0:T(8,128)(2,1)S(1)} %broadcast_select_fusion.refs_0_, bf16[256,768]{1,0:T(8,128)(2,1)S(1)} %collective-permute-done.11.refs_1_, ...), custom_call_target="tpu_custom_call" | custom-call | flops 134217728 | bytes 4194304 | tf_op jit(solution)/shard_map/pallas_call | solution.py:410
  96.8 1.2 %shard_map.78 = (bf16[256,256]{1,0:T(8,128)(2,1)S(1)}, bf16[256,256]{1,0:T(8,128)(2,1)S(1)}) custom-call(s32[4]{0:T(128)S(1)} %copy-done.1, f32[16]{0:T(128)S(1)} %copy-done.2, bf16[128,256]{1,0:T(8,128)(2,1)S(1)} %collective-permute-done.25.base_ref, f32[128,256]{1,0:T(8,128)S(1)} %get-tuple-element.126.refs_0_, f32[128,256]{1,0:T(8,128)S(1)} %get-tuple-element.127.refs_1_, ...), custom_call_target="tpu_custom_call" | custom-call | flops 201326592 | bytes 4194304 | tf_op jit(solution)/shard_map/pallas_call | solution.py:421
  98.0 0.3 collective-permute-start.28
  98.4 2.4 %collective-permute-start.30 = (bf16[256,256]{1,0:T(8,128)(2,1)S(1)}, bf16[256,256]{1,0:T(8,128)(2,1)S(1)}, u32[]{:S(2)}, u32[]{:S(2)}) collective-permute-start(bf16[256,256]{1,0:T(8,128)(2,1)S(1)} %get-tuple-element.133), channel_id=1, source_target_pairs={{0,12},{1,13},{2,14},{3,15},{4,8},{5,9},{6,10},{7,11},{8,4},{9,5},... | collective-permute-start | bytes 393224 | tf_op jit(solution)/shard_map/ppermute | solution.py:279
  100.7 1.8 %shard_map.79 = (bf16[256,256]{1,0:T(8,128)(2,1)S(1)}, f32[256,256]{1,0:T(8,128)S(1)}, bf16[256,256]{1,0:T(8,128)(2,1)S(1)}, f32[256,256]{1,0:T(8,128)S(1)}) custom-call(s32[4]{0:T(128)S(1)} %copy-done.1, bf16[256,768]{1,0:T(8,128)(2,1)S(1)} %broadcast_select_fusion.refs_0_, bf16[256,768]{1,0:T(8,128)(2,1)S(1)} %collective-permute-done.11.refs_1_, ...), custom_call_target="tpu_custom_call" | custom-call | flops 134217728 | bytes 4194304 | tf_op jit(solution)/shard_map/pallas_call | solution.py:410
  102.5 1.2 %shard_map.80 = (bf16[256,256]{1,0:T(8,128)(2,1)S(1)}, bf16[256,256]{1,0:T(8,128)(2,1)S(1)}) custom-call(s32[4]{0:T(128)S(1)} %copy-done.1, f32[16]{0:T(128)S(1)} %copy-done.2, bf16[128,256]{1,0:T(8,128)(2,1)S(1)} %collective-permute-done.25.base_ref, f32[128,256]{1,0:T(8,128)S(1)} %get-tuple-element.126.refs_0_, f32[128,256]{1,0:T(8,128)S(1)} %get-tuple-element.127.refs_1_, ...), custom_call_target="tpu_custom_call" | custom-call | flops 201326592 | bytes 4194304 | tf_op jit(solution)/shard_map/pallas_call | solution.py:421
  103.7 0.3 collective-permute-start.29
  104.0 0.6 collective-permute-start.31
  104.6 1.6 %shard_map.82 = (bf16[256,256]{1,0:T(8,128)(2,1)S(1)}, f32[256,256]{1,0:T(8,128)S(1)}, bf16[256,256]{1,0:T(8,128)(2,1)S(1)}, f32[256,256]{1,0:T(8,128)S(1)}) custom-call(s32[4]{0:T(128)S(1)} %copy-done.1, bf16[256,768]{1,0:T(8,128)(2,1)S(1)} %broadcast_select_fusion.refs_0_, bf16[256,768]{1,0:T(8,128)(2,1)S(1)} %collective-permute-done.11.refs_1_, ...), custom_call_target="tpu_custom_call" | custom-call | flops 134217728 | bytes 4194304 | tf_op jit(solution)/shard_map/pallas_call | solution.py:410
  106.2 1.6 %shard_map.83 = (bf16[256,256]{1,0:T(8,128)(2,1)S(1)}, f32[256,256]{1,0:T(8,128)S(1)}, bf16[256,256]{1,0:T(8,128)(2,1)S(1)}, f32[256,256]{1,0:T(8,128)S(1)}) custom-call(s32[4]{0:T(128)S(1)} %copy-done.1, bf16[256,768]{1,0:T(8,128)(2,1)S(1)} %broadcast_select_fusion.refs_0_, bf16[256,768]{1,0:T(8,128)(2,1)S(1)} %collective-permute-done.11.refs_1_, ...), custom_call_target="tpu_custom_call" | custom-call | flops 134217728 | bytes 4194304 | tf_op jit(solution)/shard_map/pallas_call | solution.py:410
  107.8 1.6 %shard_map.84 = (bf16[256,256]{1,0:T(8,128)(2,1)S(1)}, bf16[256,256]{1,0:T(8,128)(2,1)S(1)}, bf16[256,256]{1,0:T(8,128)(2,1)S(1)}, bf16[256,256]{1,0:T(8,128)(2,1)S(1)}) custom-call(s32[4]{0:T(128)S(1)} %copy-done.1, f32[16]{0:T(128)S(1)} %copy-done.2, bf16[128,256]{1,0:T(8,128)(2,1)S(1)} %collective-permute-done.25.base_ref, ...), custom_call_target="tpu_custom_call" | custom-call | flops 402653184 | bytes 4194304 | tf_op jit(solution)/shard_map/pallas_call | solution.py:421
  109.4 1.1 collective-permute-start.32
  110.5 0.1 collective-permute-start.33
  110.5 1.5 %collective-permute-done.31.refs_3_.refs_8_ = bf16[256,256]{1,0:T(8,128)(2,1)S(1)} collective-permute-done((bf16[256,256]{1,0:T(8,128)(2,1)S(1)}, bf16[256,256]{1,0:T(8,128)(2,1)S(1)}, u32[]{:S(2)}, u32[]{:S(2)}) %collective-permute-start.31) | collective-permute-done | bytes 131104 | tf_op jit(solution)/shard_map/ppermute | solution.py:279
  112.0 1.6 %shard_map.85 = bf16[256,2048]{1,0:T(8,128)(2,1)} custom-call(s32[4]{0:T(128)S(1)} %copy-done.1, f32[8,128]{1,0:T(8,128)S(1)} %shard_map.81.refs_0_, bf16[256,256]{1,0:T(8,128)(2,1)S(1)} %get-tuple-element.153.refs_1_, bf16[256,256]{1,0:T(8,128)(2,1)S(1)} %get-tuple-element.154.refs_2_, bf16[256,256]{1,0:T(8,128)(2,1)S(1)} %collective-permute-done.32.refs_3_, ...), custom_call_target="tpu_custom_call" | custom-call | bytes 4194304 | tf_op jit(solution)/shard_map/pallas_call | solution.py:444
  (48 shorter events, 0.2 us)
Async XLA Ops:
  0.0 16.7 %copy-start.3 = (bf16[1,256,4096]{2,1,0:T(8,128)(2,1)S(1)}, bf16[1,256,4096]{2,1,0:T(8,128)(2,1)}, u32[]{:S(2)}) copy-start(bf16[1,256,4096]{2,1,0:T(8,128)(2,1)} %param.7) | copy-start | bytes 6291460
  0.0 16.6 %collective-permute-start.3 = (bf16[256,4096]{1,0:T(8,128)(2,1)}, bf16[256,4096]{1,0:T(8,128)(2,1)}, u32[]{:S(2)}, u32[]{:S(2)}) collective-permute-start(bf16[256,4096]{1,0:T(8,128)(2,1)} %bitcast.5), channel_id=1, source_target_pairs={{0,4},{1,5},{2,6},{3,7},{4,0},{5,1},{6,2},{7,3},{8,12},{9,13},{10,... | collective-permute-start | bytes 6291464 | tf_op jit(solution)/shard_map/ppermute | solution.py:279
  4.1 2.8 %collective-permute-start = (bf16[144,768]{1,0:T(8,128)(2,1)}, bf16[144,768]{1,0:T(8,128)(2,1)S(1)}, u32[]{:S(2)}, u32[]{:S(2)}) collective-permute-start(bf16[144,768]{1,0:T(8,128)(2,1)} %get-tuple-element.82), channel_id=1, source_target_pairs={{0,4},{1,5},{2,6},{3,7},{4,0},{5,1},{6,2},{7,3},{8,12},{9,13},{10,... | collective-permute-start | bytes 663560 | tf_op jit(solution)/shard_map/ppermute | solution.py:279
  4.2 7.9 %collective-permute-start.2 = (bf16[144,768]{1,0:T(8,128)(2,1)}, bf16[144,768]{1,0:T(8,128)(2,1)S(1)}, u32[]{:S(2)}, u32[]{:S(2)}) collective-permute-start(bf16[144,768]{1,0:T(8,128)(2,1)} %get-tuple-element.84), channel_id=1, source_target_pairs={{0,12},{1,13},{2,14},{3,15},{4,8},{5,9},{6,10},{7,11},{8,4},{9,5},... | collective-permute-start | bytes 663560 | tf_op jit(solution)/shard_map/ppermute | solution.py:279
  5.7 10.9 %collective-permute-start.1 = (bf16[144,768]{1,0:T(8,128)(2,1)}, bf16[144,768]{1,0:T(8,128)(2,1)S(1)}, u32[]{:S(2)}, u32[]{:S(2)}) collective-permute-start(bf16[144,768]{1,0:T(8,128)(2,1)} %get-tuple-element.83), channel_id=1, source_target_pairs={{0,8},{1,9},{2,10},{3,11},{4,12},{5,13},{6,14},{7,15},{8,0},{9,1},... | collective-permute-start | bytes 663560 | tf_op jit(solution)/shard_map/ppermute | solution.py:279
  16.6 50.5 %copy-start.1 = (s32[4]{0:T(128)S(1)}, s32[4]{0:T(128)}, u32[]{:S(2)}) copy-start(s32[4]{0:T(128)} %pad_add_fusion.here_ref) | copy-start | bytes 52
  16.6 10.1 %collective-permute-start.12 = (bf16[256,768]{1,0:T(8,128)(2,1)S(1)}, bf16[256,768]{1,0:T(8,128)(2,1)}, u32[]{:S(2)}, u32[]{:S(2)}) collective-permute-start(bf16[256,768]{1,0:T(8,128)(2,1)S(1)} %pad_maximum_fusion.refs_2_), channel_id=1, source_target_pairs={{0,1},{1,0},{2,3},{3,2},{4,5},{5,4},{6,7},{7,6},{8,9},{9,8},{10,11... | collective-permute-start | bytes 1179656 | tf_op jit(solution)/shard_map/ppermute | solution.py:279
  16.7 55.3 %collective-permute-start.21 = (bf16[256,4096]{1,0:T(8,128)(2,1)S(1)}, bf16[256,4096]{1,0:T(8,128)(2,1)}, u32[]{:S(2)}, u32[]{:S(2)}) collective-permute-start(bf16[256,4096]{1,0:T(8,128)(2,1)S(1)} %bitcast.6), channel_id=1, source_target_pairs={{0,8},{1,9},{2,10},{3,11},{4,12},{5,13},{6,14},{7,15},{8,0},{9,1},... | collective-permute-start | bytes 6291464 | tf_op jit(solution)/shard_map/ppermute | solution.py:279
  18.1 12.6 %collective-permute-start.13 = (bf16[256,768]{1,0:T(8,128)(2,1)S(1)}, bf16[256,768]{1,0:T(8,128)(2,1)}, u32[]{:S(2)}, u32[]{:S(2)}) collective-permute-start(bf16[256,768]{1,0:T(8,128)(2,1)S(1)} %pad_maximum_fusion.refs_2_), channel_id=1, source_target_pairs={{1,2},{2,1},{5,6},{6,5},{9,10},{10,9},{13,14},{14,13},{17,18},{18,... | collective-permute-start | bytes 1179656 | tf_op jit(solution)/shard_map/ppermute | solution.py:279
  22.4 9.5 %collective-permute-start.14 = (bf16[256,768]{1,0:T(8,128)(2,1)S(1)}, bf16[256,768]{1,0:T(8,128)(2,1)S(1)}, u32[]{:S(2)}, u32[]{:S(2)}) collective-permute-start(bf16[256,768]{1,0:T(8,128)(2,1)S(1)} %pad_maximum_fusion.refs_2_), channel_id=1, source_target_pairs={{0,16},{1,17},{2,18},{3,19},{4,20},{5,21},{6,22},{7,23},{8,24},{9,... | collective-permute-start | bytes 1179656 | tf_op jit(solution)/shard_map/ppermute | solution.py:279
  23.7 12.0 %collective-permute-start.4 = (bf16[256,768]{1,0:T(8,128)(2,1)S(1)}, bf16[256,768]{1,0:T(8,128)(2,1)}, u32[]{:S(2)}, u32[]{:S(2)}) collective-permute-start(bf16[256,768]{1,0:T(8,128)(2,1)S(1)} %pad_maximum_fusion.1.refs_9_), channel_id=1, source_target_pairs={{0,1},{1,0},{2,3},{3,2},{4,5},{5,4},{6,7},{7,6},{8,9},{9,8},{10,11... | collective-permute-start | bytes 1179656 | tf_op jit(solution)/shard_map/ppermute | solution.py:279
  26.7 11.5 %collective-permute-start.5 = (bf16[256,768]{1,0:T(8,128)(2,1)S(1)}, bf16[256,768]{1,0:T(8,128)(2,1)}, u32[]{:S(2)}, u32[]{:S(2)}) collective-permute-start(bf16[256,768]{1,0:T(8,128)(2,1)S(1)} %pad_maximum_fusion.1.refs_9_), channel_id=1, source_target_pairs={{1,2},{2,1},{5,6},{6,5},{9,10},{10,9},{13,14},{14,13},{17,18},{18,... | collective-permute-start | bytes 1179656 | tf_op jit(solution)/shard_map/ppermute | solution.py:279
  30.6 8.6 %collective-permute-start.6 = (bf16[256,768]{1,0:T(8,128)(2,1)S(1)}, bf16[256,768]{1,0:T(8,128)(2,1)S(1)}, u32[]{:S(2)}, u32[]{:S(2)}) collective-permute-start(bf16[256,768]{1,0:T(8,128)(2,1)S(1)} %pad_maximum_fusion.1.refs_9_), channel_id=1, source_target_pairs={{0,16},{1,17},{2,18},{3,19},{4,20},{5,21},{6,22},{7,23},{8,24},{9,... | collective-permute-start | bytes 1179656 | tf_op jit(solution)/shard_map/ppermute | solution.py:279
  31.9 0.7 copy-start.4
  32.6 13.8 %collective-permute-start.15 = (bf16[256,768]{1,0:T(8,128)(2,1)}, bf16[256,768]{1,0:T(8,128)(2,1)}, u32[]{:S(2)}, u32[]{:S(2)}) collective-permute-start(bf16[256,768]{1,0:T(8,128)(2,1)} %collective-permute-done.12.refs_3_), channel_id=1, source_target_pairs={{1,2},{2,1},{5,6},{6,5},{9,10},{10,9},{13,14},{14,13},{17,18},{18,... | collective-permute-start | bytes 1179656 | tf_op jit(solution)/shard_map/ppermute | solution.py:279
  35.7 12.8 %collective-permute-start.16 = (bf16[256,768]{1,0:T(8,128)(2,1)}, bf16[256,768]{1,0:T(8,128)(2,1)}, u32[]{:S(2)}, u32[]{:S(2)}) collective-permute-start(bf16[256,768]{1,0:T(8,128)(2,1)} %collective-permute-done.13), channel_id=1, source_target_pairs={{1,0},{2,3},{5,4},{6,7},{9,8},{10,11},{13,12},{14,15},{17,16},{18,... | collective-permute-start | bytes 1179656 | tf_op jit(solution)/shard_map/ppermute | solution.py:279
  38.2 11.6 %collective-permute-start.17 = (bf16[256,768]{1,0:T(8,128)(2,1)}, bf16[256,768]{1,0:T(8,128)(2,1)}, u32[]{:S(2)}, u32[]{:S(2)}) collective-permute-start(bf16[256,768]{1,0:T(8,128)(2,1)} %collective-permute-done.12.refs_3_), channel_id=1, source_target_pairs={{0,16},{1,17},{2,18},{3,19},{4,20},{5,21},{6,22},{7,23},{8,24},{9,... | collective-permute-start | bytes 1179656 | tf_op jit(solution)/shard_map/ppermute | solution.py:279
  39.3 0.8 copy-start.6
  40.0 14.8 %collective-permute-start.7 = (bf16[256,768]{1,0:T(8,128)(2,1)}, bf16[256,768]{1,0:T(8,128)(2,1)}, u32[]{:S(2)}, u32[]{:S(2)}) collective-permute-start(bf16[256,768]{1,0:T(8,128)(2,1)} %collective-permute-done.4.refs_10_), channel_id=1, source_target_pairs={{1,2},{2,1},{5,6},{6,5},{9,10},{10,9},{13,14},{14,13},{17,18},{18,... | collective-permute-start | bytes 1179656 | tf_op jit(solution)/shard_map/ppermute | solution.py:279
  46.4 9.7 %collective-permute-start.8 = (bf16[256,768]{1,0:T(8,128)(2,1)}, bf16[256,768]{1,0:T(8,128)(2,1)}, u32[]{:S(2)}, u32[]{:S(2)}) collective-permute-start(bf16[256,768]{1,0:T(8,128)(2,1)} %collective-permute-done.5), channel_id=1, source_target_pairs={{1,0},{2,3},{5,4},{6,7},{9,8},{10,11},{13,12},{14,15},{17,16},{18,... | collective-permute-start | bytes 1179656 | tf_op jit(solution)/shard_map/ppermute | solution.py:279
  48.5 18.6 %copy-start.5 = (bf16[256,768]{1,0:T(8,128)(2,1)S(1)}, bf16[256,768]{1,0:T(8,128)(2,1)}, u32[]{:S(2)}) copy-start(bf16[256,768]{1,0:T(8,128)(2,1)} %copy-done.4) | copy-start | bytes 1179652
  48.5 18.6 %copy-start.7 = (bf16[256,768]{1,0:T(8,128)(2,1)S(1)}, bf16[256,768]{1,0:T(8,128)(2,1)}, u32[]{:S(2)}) copy-start(bf16[256,768]{1,0:T(8,128)(2,1)} %copy-done.6) | copy-start | bytes 1179652
  48.5 11.1 %collective-permute-start.9 = (bf16[256,768]{1,0:T(8,128)(2,1)}, bf16[256,768]{1,0:T(8,128)(2,1)S(1)}, u32[]{:S(2)}, u32[]{:S(2)}) collective-permute-start(bf16[256,768]{1,0:T(8,128)(2,1)} %collective-permute-done.4.refs_10_), channel_id=1, source_target_pairs={{0,16},{1,17},{2,18},{3,19},{4,20},{5,21},{6,22},{7,23},{8,24},{9,... | collective-permute-start | bytes 1179656 | tf_op jit(solution)/shard_map/ppermute | solution.py:279
  49.8 12.3 %collective-permute-start.18 = (bf16[256,768]{1,0:T(8,128)(2,1)}, bf16[256,768]{1,0:T(8,128)(2,1)S(1)}, u32[]{:S(2)}, u32[]{:S(2)}) collective-permute-start(bf16[256,768]{1,0:T(8,128)(2,1)} %collective-permute-done.15), channel_id=1, source_target_pairs={{1,0},{2,3},{5,4},{6,7},{9,8},{10,11},{13,12},{14,15},{17,16},{18,... | collective-permute-start | bytes 1179656 | tf_op jit(solution)/shard_map/ppermute | solution.py:279
  54.9 11.1 %collective-permute-start.19 = (bf16[256,768]{1,0:T(8,128)(2,1)S(1)}, bf16[256,768]{1,0:T(8,128)(2,1)S(1)}, u32[]{:S(2)}, u32[]{:S(2)}) collective-permute-start(bf16[256,768]{1,0:T(8,128)(2,1)S(1)} %broadcast_select_fusion.2.refs_4_), channel_id=1, source_target_pairs={{0,16},{1,17},{2,18},{3,19},{4,20},{5,21},{6,22},{7,23},{8,24},{9,... | collective-permute-start | bytes 1179656 | tf_op jit(solution)/shard_map/ppermute | solution.py:279
  56.1 9.9 %collective-permute-start.20 = (bf16[256,768]{1,0:T(8,128)(2,1)}, bf16[256,768]{1,0:T(8,128)(2,1)S(1)}, u32[]{:S(2)}, u32[]{:S(2)}) collective-permute-start(bf16[256,768]{1,0:T(8,128)(2,1)} %collective-permute-done.17.refs_7_), channel_id=1, source_target_pairs={{1,2},{2,1},{5,6},{6,5},{9,10},{10,9},{13,14},{14,13},{17,18},{18,... | collective-permute-start | bytes 1179656 | tf_op jit(solution)/shard_map/ppermute | solution.py:279
  59.6 12.4 %collective-permute-start.10 = (bf16[256,768]{1,0:T(8,128)(2,1)}, bf16[256,768]{1,0:T(8,128)(2,1)S(1)}, u32[]{:S(2)}, u32[]{:S(2)}) collective-permute-start(bf16[256,768]{1,0:T(8,128)(2,1)} %collective-permute-done.7), channel_id=1, source_target_pairs={{1,0},{2,3},{5,4},{6,7},{9,8},{10,11},{13,12},{14,15},{17,16},{18,... | collective-permute-start | bytes 1179656 | tf_op jit(solution)/shard_map/ppermute | solution.py:279
  62.0 12.4 %collective-permute-start.11 = (bf16[256,768]{1,0:T(8,128)(2,1)S(1)}, bf16[256,768]{1,0:T(8,128)(2,1)S(1)}, u32[]{:S(2)}, u32[]{:S(2)}) collective-permute-start(bf16[256,768]{1,0:T(8,128)(2,1)S(1)} %broadcast_select_fusion.3.refs_11_), channel_id=1, source_target_pairs={{0,16},{1,17},{2,18},{3,19},{4,20},{5,21},{6,22},{7,23},{8,24},{9,... | collective-permute-start | bytes 1179656 | tf_op jit(solution)/shard_map/ppermute | solution.py:279
  74.4 11.5 %collective-permute-start.24 = (bf16[256,4096]{1,0:T(8,128)(2,1)}, bf16[256,4096]{1,0:T(8,128)(2,1)S(1)}, u32[]{:S(2)}, u32[]{:S(2)}) collective-permute-start(bf16[256,4096]{1,0:T(8,128)(2,1)} %collective-permute-done.21.refs_0_), channel_id=1, source_target_pairs={{0,4},{1,5},{2,6},{3,7},{4,0},{5,1},{6,2},{7,3},{8,12},{9,13},{10,... | collective-permute-start | bytes 6291464 | tf_op jit(solution)/shard_map/ppermute | solution.py:279
  80.7 10.1 %collective-permute-start.22 = (bf16[256,256]{1,0:T(8,128)(2,1)S(1)}, bf16[256,256]{1,0:T(8,128)(2,1)S(1)}, u32[]{:S(2)}, u32[]{:S(2)}) collective-permute-start(bf16[256,256]{1,0:T(8,128)(2,1)S(1)} %slice.28), channel_id=1, source_target_pairs={{1,0},{2,3},{5,4},{6,7},{9,8},{10,11},{13,12},{14,15},{17,16},{18,... | collective-permute-start | bytes 393224 | tf_op jit(solution)/shard_map/ppermute | solution.py:279
  82.0 13.2 %collective-permute-start.26 = (bf16[256,512]{1,0:T(8,128)(2,1)S(1)}, bf16[256,512]{1,0:T(8,128)(2,1)S(1)}, u32[]{:S(2)}, u32[]{:S(2)}) collective-permute-start(bf16[256,512]{1,0:T(8,128)(2,1)S(1)} %slice.30), channel_id=1, source_target_pairs={{1,0},{2,3},{5,4},{6,7},{9,8},{10,11},{13,12},{14,15},{17,16},{18,... | collective-permute-start | bytes 786440 | tf_op jit(solution)/shard_map/ppermute | solution.py:279
  84.4 6.4 %copy-start = (bf16[144,768]{1,0:T(8,128)(2,1)S(1)}, bf16[144,768]{1,0:T(8,128)(2,1)}, u32[]{:S(2)}) copy-start(bf16[144,768]{1,0:T(8,128)(2,1)} %get-tuple-element.81.refs_13_.refs_8_.refs_5_) | copy-start | bytes 663556
  84.4 6.4 %collective-permute-start.23 = (bf16[256,256]{1,0:T(8,128)(2,1)S(1)}, bf16[256,256]{1,0:T(8,128)(2,1)S(1)}, u32[]{:S(2)}, u32[]{:S(2)}) collective-permute-start(bf16[256,256]{1,0:T(8,128)(2,1)S(1)} %slice.35), channel_id=1, source_target_pairs={{0,16},{1,17},{2,18},{3,19},{4,20},{5,21},{6,22},{7,23},{8,24},{9,... | collective-permute-start | bytes 393224 | tf_op jit(solution)/shard_map/ppermute | solution.py:279
  85.8 9.5 %collective-permute-start.27 = (bf16[256,512]{1,0:T(8,128)(2,1)S(1)}, bf16[256,512]{1,0:T(8,128)(2,1)S(1)}, u32[]{:S(2)}, u32[]{:S(2)}) collective-permute-start(bf16[256,512]{1,0:T(8,128)(2,1)S(1)} %slice.36), channel_id=1, source_target_pairs={{0,16},{1,17},{2,18},{3,19},{4,20},{5,21},{6,22},{7,23},{8,24},{9,... | collective-permute-start | bytes 786440 | tf_op jit(solution)/shard_map/ppermute | solution.py:279
  92.6 4.2 %collective-permute-start.25 = (bf16[128,256]{1,0:T(8,128)(2,1)S(1)}, bf16[128,256]{1,0:T(8,128)(2,1)S(1)}, u32[]{:S(2)}, u32[]{:S(2)}) collective-permute-start(bf16[128,256]{1,0:T(8,128)(2,1)S(1)} %get-tuple-element.120), channel_id=1, source_target_pairs={{0,16},{1,17},{2,18},{3,19},{4,20},{5,21},{6,22},{7,23},{8,24},{9,... | collective-permute-start | bytes 196616 | tf_op jit(solution)/shard_map/ppermute | solution.py:279
  95.2 1.6 %copy-start.2 = (f32[16]{0:T(128)S(1)}, f32[16]{0:T(128)}, u32[]{:S(2)}) copy-start(f32[16]{0:T(128)} %gate_ref.5) | copy-start | bytes 196
  98.0 12.4 %collective-permute-start.28 = (bf16[256,256]{1,0:T(8,128)(2,1)S(1)}, bf16[256,256]{1,0:T(8,128)(2,1)S(1)}, u32[]{:S(2)}, u32[]{:S(2)}) collective-permute-start(bf16[256,256]{1,0:T(8,128)(2,1)S(1)} %get-tuple-element.132), channel_id=1, source_target_pairs={{0,8},{1,9},{2,10},{3,11},{4,12},{5,13},{6,14},{7,15},{8,0},{9,1},... | collective-permute-start | bytes 393224 | tf_op jit(solution)/shard_map/ppermute | solution.py:279
  98.4 12.2 %collective-permute-start.30 = (bf16[256,256]{1,0:T(8,128)(2,1)S(1)}, bf16[256,256]{1,0:T(8,128)(2,1)S(1)}, u32[]{:S(2)}, u32[]{:S(2)}) collective-permute-start(bf16[256,256]{1,0:T(8,128)(2,1)S(1)} %get-tuple-element.133), channel_id=1, source_target_pairs={{0,12},{1,13},{2,14},{3,15},{4,8},{5,9},{6,10},{7,11},{8,4},{9,5},... | collective-permute-start | bytes 393224 | tf_op jit(solution)/shard_map/ppermute | solution.py:279
  103.7 6.9 %collective-permute-start.29 = (bf16[256,256]{1,0:T(8,128)(2,1)S(1)}, bf16[256,256]{1,0:T(8,128)(2,1)S(1)}, u32[]{:S(2)}, u32[]{:S(2)}) collective-permute-start(bf16[256,256]{1,0:T(8,128)(2,1)S(1)} %get-tuple-element.139), channel_id=1, source_target_pairs={{0,8},{1,9},{2,10},{3,11},{4,12},{5,13},{6,14},{7,15},{8,0},{9,1},... | collective-permute-start | bytes 393224 | tf_op jit(solution)/shard_map/ppermute | solution.py:279
  104.0 8.0 %collective-permute-start.31 = (bf16[256,256]{1,0:T(8,128)(2,1)S(1)}, bf16[256,256]{1,0:T(8,128)(2,1)S(1)}, u32[]{:S(2)}, u32[]{:S(2)}) collective-permute-start(bf16[256,256]{1,0:T(8,128)(2,1)S(1)} %get-tuple-element.140), channel_id=1, source_target_pairs={{0,12},{1,13},{2,14},{3,15},{4,8},{5,9},{6,10},{7,11},{8,4},{9,5},... | collective-permute-start | bytes 393224 | tf_op jit(solution)/shard_map/ppermute | solution.py:279
  109.4 2.7 %collective-permute-start.32 = (bf16[256,256]{1,0:T(8,128)(2,1)S(1)}, bf16[256,256]{1,0:T(8,128)(2,1)S(1)}, u32[]{:S(2)}, u32[]{:S(2)}) collective-permute-start(bf16[256,256]{1,0:T(8,128)(2,1)S(1)} %get-tuple-element.155), channel_id=1, source_target_pairs={{0,4},{1,5},{2,6},{3,7},{4,0},{5,1},{6,2},{7,3},{8,12},{9,13},{10,... | collective-permute-start | bytes 393224 | tf_op jit(solution)/shard_map/ppermute | solution.py:279
  110.5 1.6 %collective-permute-start.33 = (bf16[256,256]{1,0:T(8,128)(2,1)S(1)}, bf16[256,256]{1,0:T(8,128)(2,1)S(1)}, u32[]{:S(2)}, u32[]{:S(2)}) collective-permute-start(bf16[256,256]{1,0:T(8,128)(2,1)S(1)} %get-tuple-element.156), channel_id=1, source_target_pairs={{0,4},{1,5},{2,6},{3,7},{4,0},{5,1},{6,2},{7,3},{8,12},{9,13},{10,... | collective-permute-start | bytes 393224 | tf_op jit(solution)/shard_map/ppermute | solution.py:279

commit v18 on v17

--- a/solution.py
+++ b/solution.py
@@ -78,11 +78,22 @@
     return lax.broadcasted_iota(jnp.int32, shape, dimension).astype(jnp.float32)
 
 
-def project_body(early, late, line, here_ref, *refs):
-    tokens, pieces, outs = refs[:2], refs[2 : 2 + len(early)], refs[2 + len(early) :]
+def project_body(early, late, line, held, here_ref, *refs):
+    if held:
+        *refs, held_ref, sems = refs
+    tokens, pieces, outs = refs[:2], list(refs[2 : 2 + len(early)]), refs[2 + len(early) :]
     length = tokens[0].shape[0]
+    copies = [
+        pltpu.make_async_copy(pieces[len(early) - held + n], held_ref.at[n], sems.at[n])
+        for n in range(held)
+    ]
+    for n, one in enumerate(copies):
+        one.start()
+        pieces[len(early) - held + n] = held_ref.at[n]
     total = None
-    for place, piece in zip(early, pieces):
+    for at, (place, piece) in enumerate(zip(early, pieces)):
+        if at >= len(early) - held:
+            copies[at - len(early) + held].wait()
         columns = jnp.concatenate([columns_of(one, here_ref, *place, line) for one in tokens], axis=0)
         term = jnp.dot(columns, piece[...], preferred_element_type=jnp.float32)
         total = term if total is None else total + term
@@ -312,13 +323,14 @@
     n_pieces = width // (MEMBERS * HEAD_SIZE)
     sums, lates = [None] * MEMBERS, [None] * MEMBERS
 
-    def project(segs, early, late, halves, line):
+    def project(segs, early, late, halves, line, held=0):
         deep = MEMBERS * HEAD_SIZE // 2
         found = call(
-            functools.partial(project_body, early, late, line),
+            functools.partial(project_body, early, late, line, held),
             [shape((length, wide), f32)] * 2 + [shape((length, len(late) * deep), bf16)] * 2,
-            [SMEM] + [VMEM] * (2 + len(early)),
+            [SMEM] + [VMEM] * (2 + len(early) - held) + [ANY] * held,
             flops=2 * 2 * length * len(early) * deep * wide,
+            scratch=[pltpu.VMEM((held, deep, wide), bf16), pltpu.SemaphoreType.DMA((held,))] if held else (),
         )(here, *[books[s] for s in segs], *[halves[half][piece] for piece, half in early])
         for at, s in enumerate(segs):
             sums[s], lates[s] = found[at], found[2 + at]
@@ -356,13 +368,14 @@
         upper = [a, a_one, a_two, a_three, a_far0, a_far1, a_far2]
         lower = [b, b_one, b_two, None, b_far0, b_far1]
         late = [(3, 1), (6, 1), (7, 0), (7, 1)]
-        early = [(k, half) for half in range(2) for k in range(8) if (k, half) not in late]
-        project((0, 1), early, late, (upper, lower), n_z)
+        early = [(k, half) for half in range(2) for k in range(8) if k != 4 and (k, half) not in late]
+        early += [(4, 0), (4, 1)]
+        project((0, 1), early, late, (upper, lower), n_z, 2)
         b_last, b_far2, b_middle, sums[0], sums[1], across = locked(
             b_last, b_far2, b_middle, sums[0], sums[1], after(across, a_last, a_far2)
         )
         books += [across, to_member(across, 1)]
-        project((2, 3), early, late, (upper, lower), n_z)
+        project((2, 3), early, late, (upper, lower), n_z, 2)
         b_three = jnp.where(inside, b_middle, b_last)
         pieces = [b_three, b_far2]
         outer_kv, outer_q = [outward(a_inner[:, at]) for at in (slice(0, cut), slice(cut, None))]

time: 114 us -> 115 us (level)
  Pallas kernels: 25.7 us -> 27.1 us
  waiting for transfers between devices: 27.1 us -> 25.7 us
    pallas_call x2, Pallas kernels: 9.75 us -> 11.2 us  [project(): call(functools.partial(project_body, early, late, line, held), [shape((le...]
    ppermute x34, waiting for transfers between devices: 27.1 us -> 25.7 us  [permute(): return lax.ppermute(array, AXES, pairs)]
  transfers between devices with their start and end apart: 34 -> 34, of which waited for: 10 -> 10; matrix products, arithmetic and copies ran while one was open for 5% -> 5% of each run, Pallas kernels for 20% -> 21%
where the time goes in v18:
time: 115 us
  starting transfers between devices  53.5 us (47%)
  Pallas kernels  27.1 us (24%)
  waiting for transfers between devices  25.7 us (22%)
  other arithmetic  4.87 us (4%)
  local copies, waits for them, and re-layouts  2.56 us (2%)
    ppermute x34, starting transfers between devices, permute(): return lax.ppermute(array, AXES, pairs)  53.5 us
    ppermute x34, waiting for transfers between devices, permute(): return lax.ppermute(array, AXES, pairs)  25.7 us
    pallas_call x2, Pallas kernels, project(): call(functools.partial(project_body, early, late, line, held), [shape((le...  11.2 us
    pallas_call x4, Pallas kernels, local(): call(functools.partial(local_body, len(segs), len(late) + 1, halves[1 + p...  6.5 us
    pallas_call x3, Pallas kernels, mix(): call(functools.partial(mix_body, segs, parts, group), [shape((length, hal...  3.95 us
  transfers between devices with their start and end apart: 34, of which 10 were waited for; matrix products, arithmetic and copies ran while one was open for 5% of the time, Pallas kernels for 21%

profile of v18, /device:TPU:9, one launch (start us, length us, event | category | flops | bytes accessed | tf_op | source)
XLA Modules:
  0.0 114.8 jit_solution(8244174042879429015)
XLA Ops:
  0.0 0.7 collective-permute-start.3
  1.3 0.6 pad_add_fusion.here_ref
  1.9 2.1 %shard_map.73 = (bf16[144,768]{1,0:T(8,128)(2,1)}, bf16[144,768]{1,0:T(8,128)(2,1)}, bf16[144,768]{1,0:T(8,128)(2,1)}, bf16[144,768]{1,0:T(8,128)(2,1)}) custom-call(s32[4]{0:T(128)} %pad_add_fusion.here_ref, s32[1,1]{1,0:T(1,128)S(6)} %copy.8.valid_ref, s32[1,1,2,2]{3,2,1,0:T(2,128)} %mask_ref.1, bf16[128,2048]{1,0:T(8,128)(2,1)} %wq_ref.1, ...), custom_call_target="tpu_custom_call" | custom-call | bytes 4194304 | tf_op jit(solution)/shard_map/pallas_call | solution.py:296
  4.1 0.2 collective-permute-start
  4.2 1.5 %collective-permute-start.2 = (bf16[144,768]{1,0:T(8,128)(2,1)}, bf16[144,768]{1,0:T(8,128)(2,1)S(1)}, u32[]{:S(2)}, u32[]{:S(2)}) collective-permute-start(bf16[144,768]{1,0:T(8,128)(2,1)} %get-tuple-element.84), channel_id=1, source_target_pairs={{0,12},{1,13},{2,14},{3,15},{4,8},{5,9},{6,10},{7,11},{8,4},{9,5},... | collective-permute-start | bytes 663560 | tf_op jit(solution)/shard_map/ppermute | solution.py:290
  5.7 0.3 collective-permute-start.1
  5.9 0.9 slice.24
  6.9 0.0 collective-permute-done.refs_14_.refs_7_.refs_4_
  6.9 5.3 %collective-permute-done.2.refs_16_.refs_8_.refs_5_ = bf16[144,768]{1,0:T(8,128)(2,1)S(1)} collective-permute-done((bf16[144,768]{1,0:T(8,128)(2,1)}, bf16[144,768]{1,0:T(8,128)(2,1)S(1)}, u32[]{:S(2)}, u32[]{:S(2)}) %collective-permute-start.2) | collective-permute-done | bytes 221216 | tf_op jit(solution)/shard_map/ppermute | solution.py:290
  12.2 4.4 %collective-permute-done.1.refs_15_.refs_7_.refs_4_ = bf16[144,768]{1,0:T(8,128)(2,1)S(1)} collective-permute-done((bf16[144,768]{1,0:T(8,128)(2,1)}, bf16[144,768]{1,0:T(8,128)(2,1)S(1)}, u32[]{:S(2)}, u32[]{:S(2)}) %collective-permute-start.1) | collective-permute-done | bytes 221216 | tf_op jit(solution)/shard_map/ppermute | solution.py:290
  16.6 0.1 collective-permute-start.12
  16.7 1.4 %collective-permute-start.21 = (bf16[256,4096]{1,0:T(8,128)(2,1)S(1)}, bf16[256,4096]{1,0:T(8,128)(2,1)}, u32[]{:S(2)}, u32[]{:S(2)}) collective-permute-start(bf16[256,4096]{1,0:T(8,128)(2,1)S(1)} %bitcast.6), channel_id=1, source_target_pairs={{0,8},{1,9},{2,10},{3,11},{4,12},{5,13},{6,14},{7,15},{8,0},{9,1},... | collective-permute-start | bytes 6291464 | tf_op jit(solution)/shard_map/ppermute | solution.py:290
  18.1 4.3 %collective-permute-start.13 = (bf16[256,768]{1,0:T(8,128)(2,1)S(1)}, bf16[256,768]{1,0:T(8,128)(2,1)}, u32[]{:S(2)}, u32[]{:S(2)}) collective-permute-start(bf16[256,768]{1,0:T(8,128)(2,1)S(1)} %pad_maximum_fusion.refs_2_), channel_id=1, source_target_pairs={{1,2},{2,1},{5,6},{6,5},{9,10},{10,9},{13,14},{14,13},{17,18},{18,... | collective-permute-start | bytes 1179656 | tf_op jit(solution)/shard_map/ppermute | solution.py:290
  22.4 1.3 %collective-permute-start.14 = (bf16[256,768]{1,0:T(8,128)(2,1)S(1)}, bf16[256,768]{1,0:T(8,128)(2,1)S(1)}, u32[]{:S(2)}, u32[]{:S(2)}) collective-permute-start(bf16[256,768]{1,0:T(8,128)(2,1)S(1)} %pad_maximum_fusion.refs_2_), channel_id=1, source_target_pairs={{0,16},{1,17},{2,18},{3,19},{4,20},{5,21},{6,22},{7,23},{8,24},{9,... | collective-permute-start | bytes 1179656 | tf_op jit(solution)/shard_map/ppermute | solution.py:290
  23.7 3.0 %collective-permute-done.12.refs_3_ = bf16[256,768]{1,0:T(8,128)(2,1)} collective-permute-done((bf16[256,768]{1,0:T(8,128)(2,1)S(1)}, bf16[256,768]{1,0:T(8,128)(2,1)}, u32[]{:S(2)}, u32[]{:S(2)}) %collective-permute-start.12) | collective-permute-done | bytes 393248 | tf_op jit(solution)/shard_map/ppermute | solution.py:290
  26.7 3.2 %collective-permute-start.5 = (bf16[256,768]{1,0:T(8,128)(2,1)S(1)}, bf16[256,768]{1,0:T(8,128)(2,1)}, u32[]{:S(2)}, u32[]{:S(2)}) collective-permute-start(bf16[256,768]{1,0:T(8,128)(2,1)S(1)} %pad_maximum_fusion.1.refs_8_), channel_id=1, source_target_pairs={{1,2},{2,1},{5,6},{6,5},{9,10},{10,9},{13,14},{14,13},{17,18},{18,... | collective-permute-start | bytes 1179656 | tf_op jit(solution)/shard_map/ppermute | solution.py:290
  29.9 0.7 collective-permute-done.13
  30.6 1.2 %collective-permute-start.6 = (bf16[256,768]{1,0:T(8,128)(2,1)S(1)}, bf16[256,768]{1,0:T(8,128)(2,1)S(1)}, u32[]{:S(2)}, u32[]{:S(2)}) collective-permute-start(bf16[256,768]{1,0:T(8,128)(2,1)S(1)} %pad_maximum_fusion.1.refs_8_), channel_id=1, source_target_pairs={{0,16},{1,17},{2,18},{3,19},{4,20},{5,21},{6,22},{7,23},{8,24},{9,... | collective-permute-start | bytes 1179656 | tf_op jit(solution)/shard_map/ppermute | solution.py:290
  31.9 0.7 copy-done.4
  32.6 3.1 %collective-permute-start.15 = (bf16[256,768]{1,0:T(8,128)(2,1)}, bf16[256,768]{1,0:T(8,128)(2,1)}, u32[]{:S(2)}, u32[]{:S(2)}) collective-permute-start(bf16[256,768]{1,0:T(8,128)(2,1)} %collective-permute-done.12.refs_3_), channel_id=1, source_target_pairs={{1,2},{2,1},{5,6},{6,5},{9,10},{10,9},{13,14},{14,13},{17,18},{18,... | collective-permute-start | bytes 1179656 | tf_op jit(solution)/shard_map/ppermute | solution.py:290
  35.7 2.5 %collective-permute-start.16 = (bf16[256,768]{1,0:T(8,128)(2,1)}, bf16[256,768]{1,0:T(8,128)(2,1)}, u32[]{:S(2)}, u32[]{:S(2)}) collective-permute-start(bf16[256,768]{1,0:T(8,128)(2,1)} %collective-permute-done.13), channel_id=1, source_target_pairs={{1,0},{2,3},{5,4},{6,7},{9,8},{10,11},{13,12},{14,15},{17,16},{18,... | collective-permute-start | bytes 1179656 | tf_op jit(solution)/shard_map/ppermute | solution.py:290
  38.2 1.1 collective-permute-start.17
  39.3 0.8 copy-done.6
  40.0 4.3 %collective-permute-start.7 = (bf16[256,768]{1,0:T(8,128)(2,1)}, bf16[256,768]{1,0:T(8,128)(2,1)}, u32[]{:S(2)}, u32[]{:S(2)}) collective-permute-start(bf16[256,768]{1,0:T(8,128)(2,1)} %collective-permute-done.4.refs_9_), channel_id=1, source_target_pairs={{1,2},{2,1},{5,6},{6,5},{9,10},{10,9},{13,14},{14,13},{17,18},{18,... | collective-permute-start | bytes 1179656 | tf_op jit(solution)/shard_map/ppermute | solution.py:290
  44.4 2.1 %collective-permute-done.15 = bf16[256,768]{1,0:T(8,128)(2,1)} collective-permute-done((bf16[256,768]{1,0:T(8,128)(2,1)}, bf16[256,768]{1,0:T(8,128)(2,1)}, u32[]{:S(2)}, u32[]{:S(2)}) %collective-permute-start.15) | collective-permute-done | bytes 393248 | tf_op jit(solution)/shard_map/ppermute | solution.py:290
  46.4 2.1 %collective-permute-start.8 = (bf16[256,768]{1,0:T(8,128)(2,1)}, bf16[256,768]{1,0:T(8,128)(2,1)}, u32[]{:S(2)}, u32[]{:S(2)}) collective-permute-start(bf16[256,768]{1,0:T(8,128)(2,1)} %collective-permute-done.5), channel_id=1, source_target_pairs={{1,0},{2,3},{5,4},{6,7},{9,8},{10,11},{13,12},{14,15},{17,16},{18,... | collective-permute-start | bytes 1179656 | tf_op jit(solution)/shard_map/ppermute | solution.py:290
  48.5 1.2 %collective-permute-start.9 = (bf16[256,768]{1,0:T(8,128)(2,1)}, bf16[256,768]{1,0:T(8,128)(2,1)S(1)}, u32[]{:S(2)}, u32[]{:S(2)}) collective-permute-start(bf16[256,768]{1,0:T(8,128)(2,1)} %collective-permute-done.4.refs_9_), channel_id=1, source_target_pairs={{0,16},{1,17},{2,18},{3,19},{4,20},{5,21},{6,22},{7,23},{8,24},{9,... | collective-permute-start | bytes 1179656 | tf_op jit(solution)/shard_map/ppermute | solution.py:290
  49.8 1.3 %collective-permute-start.18 = (bf16[256,768]{1,0:T(8,128)(2,1)}, bf16[256,768]{1,0:T(8,128)(2,1)S(1)}, u32[]{:S(2)}, u32[]{:S(2)}) collective-permute-start(bf16[256,768]{1,0:T(8,128)(2,1)} %collective-permute-done.15), channel_id=1, source_target_pairs={{1,0},{2,3},{5,4},{6,7},{9,8},{10,11},{13,12},{14,15},{17,16},{18,... | collective-permute-start | bytes 1179656 | tf_op jit(solution)/shard_map/ppermute | solution.py:290
  51.1 1.1 broadcast_select_fusion.2.refs_4_
  52.1 2.8 %collective-permute-done.7 = bf16[256,768]{1,0:T(8,128)(2,1)} collective-permute-done((bf16[256,768]{1,0:T(8,128)(2,1)}, bf16[256,768]{1,0:T(8,128)(2,1)}, u32[]{:S(2)}, u32[]{:S(2)}) %collective-permute-start.7) | collective-permute-done | bytes 393248 | tf_op jit(solution)/shard_map/ppermute | solution.py:290
  54.9 1.2 %collective-permute-start.19 = (bf16[256,768]{1,0:T(8,128)(2,1)S(1)}, bf16[256,768]{1,0:T(8,128)(2,1)S(1)}, u32[]{:S(2)}, u32[]{:S(2)}) collective-permute-start(bf16[256,768]{1,0:T(8,128)(2,1)S(1)} %broadcast_select_fusion.2.refs_4_), channel_id=1, source_target_pairs={{0,16},{1,17},{2,18},{3,19},{4,20},{5,21},{6,22},{7,23},{8,24},{9,... | collective-permute-start | bytes 1179656 | tf_op jit(solution)/shard_map/ppermute | solution.py:290
  56.1 3.5 %collective-permute-start.20 = (bf16[256,768]{1,0:T(8,128)(2,1)}, bf16[256,768]{1,0:T(8,128)(2,1)S(1)}, u32[]{:S(2)}, u32[]{:S(2)}) collective-permute-start(bf16[256,768]{1,0:T(8,128)(2,1)} %collective-permute-done.17.refs_6_), channel_id=1, source_target_pairs={{1,2},{2,1},{5,6},{6,5},{9,10},{10,9},{13,14},{14,13},{17,18},{18,... | collective-permute-start | bytes 1179656 | tf_op jit(solution)/shard_map/ppermute | solution.py:290
  59.6 1.3 %collective-permute-start.10 = (bf16[256,768]{1,0:T(8,128)(2,1)}, bf16[256,768]{1,0:T(8,128)(2,1)S(1)}, u32[]{:S(2)}, u32[]{:S(2)}) collective-permute-start(bf16[256,768]{1,0:T(8,128)(2,1)} %collective-permute-done.7), channel_id=1, source_target_pairs={{1,0},{2,3},{5,4},{6,7},{9,8},{10,11},{13,12},{14,15},{17,16},{18,... | collective-permute-start | bytes 1179656 | tf_op jit(solution)/shard_map/ppermute | solution.py:290
  61.0 1.1 broadcast_select_fusion.3.refs_10_
  62.0 0.3 collective-permute-start.11
  62.3 3.7 %collective-permute-done.19.refs_7_ = bf16[256,768]{1,0:T(8,128)(2,1)S(1)} collective-permute-done((bf16[256,768]{1,0:T(8,128)(2,1)S(1)}, bf16[256,768]{1,0:T(8,128)(2,1)S(1)}, u32[]{:S(2)}, u32[]{:S(2)}) %collective-permute-start.19) | collective-permute-done | bytes 393248 | tf_op jit(solution)/shard_map/ppermute | solution.py:290
  66.0 1.1 broadcast_select_fusion.1.refs_5_
  67.1 5.6 %shard_map.74 = (f32[256,768]{1,0:T(8,128)S(1)}, f32[256,768]{1,0:T(8,128)S(1)}, bf16[256,1024]{1,0:T(8,128)(2,1)S(1)}, bf16[256,1024]{1,0:T(8,128)(2,1)S(1)}) custom-call(s32[4]{0:T(128)S(1)} %copy-done.1, bf16[256,4096]{1,0:T(8,128)(2,1)S(1)} %bitcast.7, bf16[256,4096]{1,0:T(8,128)(2,1)} %collective-permute-done.3.refs_1_, ...), custom_call_target="tpu_custom_call" | custom-call | flops 2415919104 | bytes 4194304 | tf_op jit(solution)/shard_map/pallas_call | solution.py:328
  72.7 1.7 %collective-permute-done.11.refs_1_ = bf16[256,768]{1,0:T(8,128)(2,1)S(1)} collective-permute-done((bf16[256,768]{1,0:T(8,128)(2,1)S(1)}, bf16[256,768]{1,0:T(8,128)(2,1)S(1)}, u32[]{:S(2)}, u32[]{:S(2)}) %collective-permute-start.11) | collective-permute-done | bytes 393248 | tf_op jit(solution)/shard_map/ppermute | solution.py:290
  74.4 6.9 %collective-permute-start.24 = (bf16[256,4096]{1,0:T(8,128)(2,1)}, bf16[256,4096]{1,0:T(8,128)(2,1)S(1)}, u32[]{:S(2)}, u32[]{:S(2)}) collective-permute-start(bf16[256,4096]{1,0:T(8,128)(2,1)} %collective-permute-done.21.refs_0_), channel_id=1, source_target_pairs={{0,4},{1,5},{2,6},{3,7},{4,0},{5,1},{6,2},{7,3},{8,12},{9,13},{10,... | collective-permute-start | bytes 6291464 | tf_op jit(solution)/shard_map/ppermute | solution.py:290
  81.4 1.3 %collective-permute-start.22 = (bf16[256,256]{1,0:T(8,128)(2,1)S(1)}, bf16[256,256]{1,0:T(8,128)(2,1)S(1)}, u32[]{:S(2)}, u32[]{:S(2)}) collective-permute-start(bf16[256,256]{1,0:T(8,128)(2,1)S(1)} %slice.28), channel_id=1, source_target_pairs={{1,0},{2,3},{5,4},{6,7},{9,8},{10,11},{13,12},{14,15},{17,16},{18,... | collective-permute-start | bytes 393224 | tf_op jit(solution)/shard_map/ppermute | solution.py:290
  82.7 1.3 %collective-permute-start.26 = (bf16[256,512]{1,0:T(8,128)(2,1)S(1)}, bf16[256,512]{1,0:T(8,128)(2,1)S(1)}, u32[]{:S(2)}, u32[]{:S(2)}) collective-permute-start(bf16[256,512]{1,0:T(8,128)(2,1)S(1)} %slice.30), channel_id=1, source_target_pairs={{1,0},{2,3},{5,4},{6,7},{9,8},{10,11},{13,12},{14,15},{17,16},{18,... | collective-permute-start | bytes 786440 | tf_op jit(solution)/shard_map/ppermute | solution.py:290
  84.0 1.1 broadcast_select_fusion.refs_0_
  85.2 1.3 %collective-permute-start.23 = (bf16[256,256]{1,0:T(8,128)(2,1)S(1)}, bf16[256,256]{1,0:T(8,128)(2,1)S(1)}, u32[]{:S(2)}, u32[]{:S(2)}) collective-permute-start(bf16[256,256]{1,0:T(8,128)(2,1)S(1)} %slice.35), channel_id=1, source_target_pairs={{0,16},{1,17},{2,18},{3,19},{4,20},{5,21},{6,22},{7,23},{8,24},{9,... | collective-permute-start | bytes 393224 | tf_op jit(solution)/shard_map/ppermute | solution.py:290
  86.5 0.2 collective-permute-start.27
  86.7 5.6 %shard_map.75 = (f32[256,768]{1,0:T(8,128)S(1)}, f32[256,768]{1,0:T(8,128)S(1)}, bf16[256,1024]{1,0:T(8,128)(2,1)S(1)}, bf16[256,1024]{1,0:T(8,128)(2,1)S(1)}) custom-call(s32[4]{0:T(128)S(1)} %copy-done.1, bf16[256,4096]{1,0:T(8,128)(2,1)} %collective-permute-done.21.refs_0_, bf16[256,4096]{1,0:T(8,128)(2,1)S(1)} %collective-permute-done.24.refs_1_, ...), custom_call_target="tpu_custom_call" | custom-call | flops 2415919104 | bytes 4194304 | tf_op jit(solution)/shard_map/pallas_call | solution.py:328
  92.3 1.7 %shard_map.76 = (bf16[256,256]{1,0:T(8,128)(2,1)S(1)}, f32[128,256]{1,0:T(8,128)S(1)}, bf16[256,256]{1,0:T(8,128)(2,1)S(1)}, f32[128,256]{1,0:T(8,128)S(1)}, bf1...) custom-call(s32[4]{0:T(128)S(1)} %copy-done.1, ...), custom_call_target="tpu_custom_call" | custom-call | flops 536870912 | bytes 4194304 | tf_op jit(solution)/shard_map/pallas_call | solution.py:403
  94.0 1.3 %collective-permute-start.25 = (bf16[128,256]{1,0:T(8,128)(2,1)S(1)}, bf16[128,256]{1,0:T(8,128)(2,1)S(1)}, u32[]{:S(2)}, u32[]{:S(2)}) collective-permute-start(bf16[128,256]{1,0:T(8,128)(2,1)S(1)} %get-tuple-element.120), channel_id=1, source_target_pairs={{0,16},{1,17},{2,18},{3,19},{4,20},{5,21},{6,22},{7,23},{8,24},{9,... | collective-permute-start | bytes 196616 | tf_op jit(solution)/shard_map/ppermute | solution.py:290
  95.4 0.6 collective-permute-done.27.refs_4_
  96.0 1.6 %shard_map.77 = (bf16[256,256]{1,0:T(8,128)(2,1)S(1)}, f32[256,256]{1,0:T(8,128)S(1)}, bf16[256,256]{1,0:T(8,128)(2,1)S(1)}, f32[256,256]{1,0:T(8,128)S(1)}) custom-call(s32[4]{0:T(128)S(1)} %copy-done.1, bf16[256,768]{1,0:T(8,128)(2,1)S(1)} %broadcast_select_fusion.refs_0_, bf16[256,768]{1,0:T(8,128)(2,1)S(1)} %collective-permute-done.11.refs_1_, ...), custom_call_target="tpu_custom_call" | custom-call | flops 134217728 | bytes 4194304 | tf_op jit(solution)/shard_map/pallas_call | solution.py:423
  97.6 1.2 %shard_map.78 = (bf16[256,256]{1,0:T(8,128)(2,1)S(1)}, bf16[256,256]{1,0:T(8,128)(2,1)S(1)}) custom-call(s32[4]{0:T(128)S(1)} %copy-done.1, f32[16]{0:T(128)S(1)} %copy-done.2, bf16[128,256]{1,0:T(8,128)(2,1)S(1)} %collective-permute-done.25.base_ref, f32[128,256]{1,0:T(8,128)S(1)} %get-tuple-element.126.refs_0_, f32[128,256]{1,0:T(8,128)S(1)} %get-tuple-element.127.refs_1_, ...), custom_call_target="tpu_custom_call" | custom-call | flops 201326592 | bytes 4194304 | tf_op jit(solution)/shard_map/pallas_call | solution.py:434
  98.7 0.3 collective-permute-start.28
  99.1 2.7 %collective-permute-start.30 = (bf16[256,256]{1,0:T(8,128)(2,1)S(1)}, bf16[256,256]{1,0:T(8,128)(2,1)S(1)}, u32[]{:S(2)}, u32[]{:S(2)}) collective-permute-start(bf16[256,256]{1,0:T(8,128)(2,1)S(1)} %get-tuple-element.133), channel_id=1, source_target_pairs={{0,12},{1,13},{2,14},{3,15},{4,8},{5,9},{6,10},{7,11},{8,4},{9,5},... | collective-permute-start | bytes 393224 | tf_op jit(solution)/shard_map/ppermute | solution.py:290
  101.8 1.8 %shard_map.79 = (bf16[256,256]{1,0:T(8,128)(2,1)S(1)}, f32[256,256]{1,0:T(8,128)S(1)}, bf16[256,256]{1,0:T(8,128)(2,1)S(1)}, f32[256,256]{1,0:T(8,128)S(1)}) custom-call(s32[4]{0:T(128)S(1)} %copy-done.1, bf16[256,768]{1,0:T(8,128)(2,1)S(1)} %broadcast_select_fusion.refs_0_, bf16[256,768]{1,0:T(8,128)(2,1)S(1)} %collective-permute-done.11.refs_1_, ...), custom_call_target="tpu_custom_call" | custom-call | flops 134217728 | bytes 4194304 | tf_op jit(solution)/shard_map/pallas_call | solution.py:423
  103.6 1.2 %shard_map.80 = (bf16[256,256]{1,0:T(8,128)(2,1)S(1)}, bf16[256,256]{1,0:T(8,128)(2,1)S(1)}) custom-call(s32[4]{0:T(128)S(1)} %copy-done.1, f32[16]{0:T(128)S(1)} %copy-done.2, bf16[128,256]{1,0:T(8,128)(2,1)S(1)} %collective-permute-done.25.base_ref, f32[128,256]{1,0:T(8,128)S(1)} %get-tuple-element.126.refs_0_, f32[128,256]{1,0:T(8,128)S(1)} %get-tuple-element.127.refs_1_, ...), custom_call_target="tpu_custom_call" | custom-call | flops 201326592 | bytes 4194304 | tf_op jit(solution)/shard_map/pallas_call | solution.py:434
  104.8 0.3 collective-permute-start.29
  105.1 0.3 collective-permute-start.31
  105.4 1.6 %shard_map.82 = (bf16[256,256]{1,0:T(8,128)(2,1)S(1)}, f32[256,256]{1,0:T(8,128)S(1)}, bf16[256,256]{1,0:T(8,128)(2,1)S(1)}, f32[256,256]{1,0:T(8,128)S(1)}) custom-call(s32[4]{0:T(128)S(1)} %copy-done.1, bf16[256,768]{1,0:T(8,128)(2,1)S(1)} %broadcast_select_fusion.refs_0_, bf16[256,768]{1,0:T(8,128)(2,1)S(1)} %collective-permute-done.11.refs_1_, ...), custom_call_target="tpu_custom_call" | custom-call | flops 134217728 | bytes 4194304 | tf_op jit(solution)/shard_map/pallas_call | solution.py:423
  107.0 1.6 %shard_map.83 = (bf16[256,256]{1,0:T(8,128)(2,1)S(1)}, f32[256,256]{1,0:T(8,128)S(1)}, bf16[256,256]{1,0:T(8,128)(2,1)S(1)}, f32[256,256]{1,0:T(8,128)S(1)}) custom-call(s32[4]{0:T(128)S(1)} %copy-done.1, bf16[256,768]{1,0:T(8,128)(2,1)S(1)} %broadcast_select_fusion.refs_0_, bf16[256,768]{1,0:T(8,128)(2,1)S(1)} %collective-permute-done.11.refs_1_, ...), custom_call_target="tpu_custom_call" | custom-call | flops 134217728 | bytes 4194304 | tf_op jit(solution)/shard_map/pallas_call | solution.py:423
  108.6 1.6 %shard_map.84 = (bf16[256,256]{1,0:T(8,128)(2,1)S(1)}, bf16[256,256]{1,0:T(8,128)(2,1)S(1)}, bf16[256,256]{1,0:T(8,128)(2,1)S(1)}, bf16[256,256]{1,0:T(8,128)(2,1)S(1)}) custom-call(s32[4]{0:T(128)S(1)} %copy-done.1, f32[16]{0:T(128)S(1)} %copy-done.2, bf16[128,256]{1,0:T(8,128)(2,1)S(1)} %collective-permute-done.25.base_ref, ...), custom_call_target="tpu_custom_call" | custom-call | flops 402653184 | bytes 4194304 | tf_op jit(solution)/shard_map/pallas_call | solution.py:434
  110.2 1.3 %collective-permute-start.32 = (bf16[256,256]{1,0:T(8,128)(2,1)S(1)}, bf16[256,256]{1,0:T(8,128)(2,1)S(1)}, u32[]{:S(2)}, u32[]{:S(2)}) collective-permute-start(bf16[256,256]{1,0:T(8,128)(2,1)S(1)} %get-tuple-element.155), channel_id=1, source_target_pairs={{0,4},{1,5},{2,6},{3,7},{4,0},{5,1},{6,2},{7,3},{8,12},{9,13},{10,... | collective-permute-start | bytes 393224 | tf_op jit(solution)/shard_map/ppermute | solution.py:290
  111.5 0.1 collective-permute-start.33
  111.6 1.5 %collective-permute-done.31.refs_3_.refs_8_ = bf16[256,256]{1,0:T(8,128)(2,1)S(1)} collective-permute-done((bf16[256,256]{1,0:T(8,128)(2,1)S(1)}, bf16[256,256]{1,0:T(8,128)(2,1)S(1)}, u32[]{:S(2)}, u32[]{:S(2)}) %collective-permute-start.31) | collective-permute-done | bytes 131104 | tf_op jit(solution)/shard_map/ppermute | solution.py:290
  113.1 1.6 %shard_map.85 = bf16[256,2048]{1,0:T(8,128)(2,1)} custom-call(s32[4]{0:T(128)S(1)} %copy-done.1, f32[8,128]{1,0:T(8,128)S(1)} %shard_map.81.refs_0_, bf16[256,256]{1,0:T(8,128)(2,1)S(1)} %get-tuple-element.153.refs_1_, bf16[256,256]{1,0:T(8,128)(2,1)S(1)} %get-tuple-element.154.refs_2_, bf16[256,256]{1,0:T(8,128)(2,1)S(1)} %collective-permute-done.32.refs_3_, ...), custom_call_target="tpu_custom_call" | custom-call | bytes 4194304 | tf_op jit(solution)/shard_map/pallas_call | solution.py:457
  (48 shorter events, 0.2 us)
Async XLA Ops:
  0.0 16.7 %copy-start.3 = (bf16[1,256,4096]{2,1,0:T(8,128)(2,1)S(1)}, bf16[1,256,4096]{2,1,0:T(8,128)(2,1)}, u32[]{:S(2)}) copy-start(bf16[1,256,4096]{2,1,0:T(8,128)(2,1)} %param.7) | copy-start | bytes 6291460
  0.0 16.6 %collective-permute-start.3 = (bf16[256,4096]{1,0:T(8,128)(2,1)}, bf16[256,4096]{1,0:T(8,128)(2,1)}, u32[]{:S(2)}, u32[]{:S(2)}) collective-permute-start(bf16[256,4096]{1,0:T(8,128)(2,1)} %bitcast.5), channel_id=1, source_target_pairs={{0,4},{1,5},{2,6},{3,7},{4,0},{5,1},{6,2},{7,3},{8,12},{9,13},{10,... | collective-permute-start | bytes 6291464 | tf_op jit(solution)/shard_map/ppermute | solution.py:290
  4.1 2.8 %collective-permute-start = (bf16[144,768]{1,0:T(8,128)(2,1)}, bf16[144,768]{1,0:T(8,128)(2,1)S(1)}, u32[]{:S(2)}, u32[]{:S(2)}) collective-permute-start(bf16[144,768]{1,0:T(8,128)(2,1)} %get-tuple-element.82), channel_id=1, source_target_pairs={{0,4},{1,5},{2,6},{3,7},{4,0},{5,1},{6,2},{7,3},{8,12},{9,13},{10,... | collective-permute-start | bytes 663560 | tf_op jit(solution)/shard_map/ppermute | solution.py:290
  4.2 7.9 %collective-permute-start.2 = (bf16[144,768]{1,0:T(8,128)(2,1)}, bf16[144,768]{1,0:T(8,128)(2,1)S(1)}, u32[]{:S(2)}, u32[]{:S(2)}) collective-permute-start(bf16[144,768]{1,0:T(8,128)(2,1)} %get-tuple-element.84), channel_id=1, source_target_pairs={{0,12},{1,13},{2,14},{3,15},{4,8},{5,9},{6,10},{7,11},{8,4},{9,5},... | collective-permute-start | bytes 663560 | tf_op jit(solution)/shard_map/ppermute | solution.py:290
  5.7 10.9 %collective-permute-start.1 = (bf16[144,768]{1,0:T(8,128)(2,1)}, bf16[144,768]{1,0:T(8,128)(2,1)S(1)}, u32[]{:S(2)}, u32[]{:S(2)}) collective-permute-start(bf16[144,768]{1,0:T(8,128)(2,1)} %get-tuple-element.83), channel_id=1, source_target_pairs={{0,8},{1,9},{2,10},{3,11},{4,12},{5,13},{6,14},{7,15},{8,0},{9,1},... | collective-permute-start | bytes 663560 | tf_op jit(solution)/shard_map/ppermute | solution.py:290
  16.6 50.5 %copy-start.1 = (s32[4]{0:T(128)S(1)}, s32[4]{0:T(128)}, u32[]{:S(2)}) copy-start(s32[4]{0:T(128)} %pad_add_fusion.here_ref) | copy-start | bytes 52
  16.6 10.1 %collective-permute-start.12 = (bf16[256,768]{1,0:T(8,128)(2,1)S(1)}, bf16[256,768]{1,0:T(8,128)(2,1)}, u32[]{:S(2)}, u32[]{:S(2)}) collective-permute-start(bf16[256,768]{1,0:T(8,128)(2,1)S(1)} %pad_maximum_fusion.refs_2_), channel_id=1, source_target_pairs={{0,1},{1,0},{2,3},{3,2},{4,5},{5,4},{6,7},{7,6},{8,9},{9,8},{10,11... | collective-permute-start | bytes 1179656 | tf_op jit(solution)/shard_map/ppermute | solution.py:290
  16.7 56.0 %collective-permute-start.21 = (bf16[256,4096]{1,0:T(8,128)(2,1)S(1)}, bf16[256,4096]{1,0:T(8,128)(2,1)}, u32[]{:S(2)}, u32[]{:S(2)}) collective-permute-start(bf16[256,4096]{1,0:T(8,128)(2,1)S(1)} %bitcast.6), channel_id=1, source_target_pairs={{0,8},{1,9},{2,10},{3,11},{4,12},{5,13},{6,14},{7,15},{8,0},{9,1},... | collective-permute-start | bytes 6291464 | tf_op jit(solution)/shard_map/ppermute | solution.py:290
  18.1 12.6 %collective-permute-start.13 = (bf16[256,768]{1,0:T(8,128)(2,1)S(1)}, bf16[256,768]{1,0:T(8,128)(2,1)}, u32[]{:S(2)}, u32[]{:S(2)}) collective-permute-start(bf16[256,768]{1,0:T(8,128)(2,1)S(1)} %pad_maximum_fusion.refs_2_), channel_id=1, source_target_pairs={{1,2},{2,1},{5,6},{6,5},{9,10},{10,9},{13,14},{14,13},{17,18},{18,... | collective-permute-start | bytes 1179656 | tf_op jit(solution)/shard_map/ppermute | solution.py:290
  22.4 9.5 %collective-permute-start.14 = (bf16[256,768]{1,0:T(8,128)(2,1)S(1)}, bf16[256,768]{1,0:T(8,128)(2,1)S(1)}, u32[]{:S(2)}, u32[]{:S(2)}) collective-permute-start(bf16[256,768]{1,0:T(8,128)(2,1)S(1)} %pad_maximum_fusion.refs_2_), channel_id=1, source_target_pairs={{0,16},{1,17},{2,18},{3,19},{4,20},{5,21},{6,22},{7,23},{8,24},{9,... | collective-permute-start | bytes 1179656 | tf_op jit(solution)/shard_map/ppermute | solution.py:290
  23.7 12.0 %collective-permute-start.4 = (bf16[256,768]{1,0:T(8,128)(2,1)S(1)}, bf16[256,768]{1,0:T(8,128)(2,1)}, u32[]{:S(2)}, u32[]{:S(2)}) collective-permute-start(bf16[256,768]{1,0:T(8,128)(2,1)S(1)} %pad_maximum_fusion.1.refs_8_), channel_id=1, source_target_pairs={{0,1},{1,0},{2,3},{3,2},{4,5},{5,4},{6,7},{7,6},{8,9},{9,8},{10,11... | collective-permute-start | bytes 1179656 | tf_op jit(solution)/shard_map/ppermute | solution.py:290
  26.7 11.5 %collective-permute-start.5 = (bf16[256,768]{1,0:T(8,128)(2,1)S(1)}, bf16[256,768]{1,0:T(8,128)(2,1)}, u32[]{:S(2)}, u32[]{:S(2)}) collective-permute-start(bf16[256,768]{1,0:T(8,128)(2,1)S(1)} %pad_maximum_fusion.1.refs_8_), channel_id=1, source_target_pairs={{1,2},{2,1},{5,6},{6,5},{9,10},{10,9},{13,14},{14,13},{17,18},{18,... | collective-permute-start | bytes 1179656 | tf_op jit(solution)/shard_map/ppermute | solution.py:290
  30.6 8.6 %collective-permute-start.6 = (bf16[256,768]{1,0:T(8,128)(2,1)S(1)}, bf16[256,768]{1,0:T(8,128)(2,1)S(1)}, u32[]{:S(2)}, u32[]{:S(2)}) collective-permute-start(bf16[256,768]{1,0:T(8,128)(2,1)S(1)} %pad_maximum_fusion.1.refs_8_), channel_id=1, source_target_pairs={{0,16},{1,17},{2,18},{3,19},{4,20},{5,21},{6,22},{7,23},{8,24},{9,... | collective-permute-start | bytes 1179656 | tf_op jit(solution)/shard_map/ppermute | solution.py:290
  31.9 0.7 copy-start.4
  32.6 13.8 %collective-permute-start.15 = (bf16[256,768]{1,0:T(8,128)(2,1)}, bf16[256,768]{1,0:T(8,128)(2,1)}, u32[]{:S(2)}, u32[]{:S(2)}) collective-permute-start(bf16[256,768]{1,0:T(8,128)(2,1)} %collective-permute-done.12.refs_3_), channel_id=1, source_target_pairs={{1,2},{2,1},{5,6},{6,5},{9,10},{10,9},{13,14},{14,13},{17,18},{18,... | collective-permute-start | bytes 1179656 | tf_op jit(solution)/shard_map/ppermute | solution.py:290
  35.7 12.8 %collective-permute-start.16 = (bf16[256,768]{1,0:T(8,128)(2,1)}, bf16[256,768]{1,0:T(8,128)(2,1)}, u32[]{:S(2)}, u32[]{:S(2)}) collective-permute-start(bf16[256,768]{1,0:T(8,128)(2,1)} %collective-permute-done.13), channel_id=1, source_target_pairs={{1,0},{2,3},{5,4},{6,7},{9,8},{10,11},{13,12},{14,15},{17,16},{18,... | collective-permute-start | bytes 1179656 | tf_op jit(solution)/shard_map/ppermute | solution.py:290
  38.2 11.6 %collective-permute-start.17 = (bf16[256,768]{1,0:T(8,128)(2,1)}, bf16[256,768]{1,0:T(8,128)(2,1)}, u32[]{:S(2)}, u32[]{:S(2)}) collective-permute-start(bf16[256,768]{1,0:T(8,128)(2,1)} %collective-permute-done.12.refs_3_), channel_id=1, source_target_pairs={{0,16},{1,17},{2,18},{3,19},{4,20},{5,21},{6,22},{7,23},{8,24},{9,... | collective-permute-start | bytes 1179656 | tf_op jit(solution)/shard_map/ppermute | solution.py:290
  39.3 0.8 copy-start.6
  40.0 14.8 %collective-permute-start.7 = (bf16[256,768]{1,0:T(8,128)(2,1)}, bf16[256,768]{1,0:T(8,128)(2,1)}, u32[]{:S(2)}, u32[]{:S(2)}) collective-permute-start(bf16[256,768]{1,0:T(8,128)(2,1)} %collective-permute-done.4.refs_9_), channel_id=1, source_target_pairs={{1,2},{2,1},{5,6},{6,5},{9,10},{10,9},{13,14},{14,13},{17,18},{18,... | collective-permute-start | bytes 1179656 | tf_op jit(solution)/shard_map/ppermute | solution.py:290
  46.4 9.7 %collective-permute-start.8 = (bf16[256,768]{1,0:T(8,128)(2,1)}, bf16[256,768]{1,0:T(8,128)(2,1)}, u32[]{:S(2)}, u32[]{:S(2)}) collective-permute-start(bf16[256,768]{1,0:T(8,128)(2,1)} %collective-permute-done.5), channel_id=1, source_target_pairs={{1,0},{2,3},{5,4},{6,7},{9,8},{10,11},{13,12},{14,15},{17,16},{18,... | collective-permute-start | bytes 1179656 | tf_op jit(solution)/shard_map/ppermute | solution.py:290
  48.5 18.6 %copy-start.5 = (bf16[256,768]{1,0:T(8,128)(2,1)S(1)}, bf16[256,768]{1,0:T(8,128)(2,1)}, u32[]{:S(2)}) copy-start(bf16[256,768]{1,0:T(8,128)(2,1)} %copy-done.4) | copy-start | bytes 1179652
  48.5 18.6 %copy-start.7 = (bf16[256,768]{1,0:T(8,128)(2,1)S(1)}, bf16[256,768]{1,0:T(8,128)(2,1)}, u32[]{:S(2)}) copy-start(bf16[256,768]{1,0:T(8,128)(2,1)} %copy-done.6) | copy-start | bytes 1179652
  48.5 11.1 %collective-permute-start.9 = (bf16[256,768]{1,0:T(8,128)(2,1)}, bf16[256,768]{1,0:T(8,128)(2,1)S(1)}, u32[]{:S(2)}, u32[]{:S(2)}) collective-permute-start(bf16[256,768]{1,0:T(8,128)(2,1)} %collective-permute-done.4.refs_9_), channel_id=1, source_target_pairs={{0,16},{1,17},{2,18},{3,19},{4,20},{5,21},{6,22},{7,23},{8,24},{9,... | collective-permute-start | bytes 1179656 | tf_op jit(solution)/shard_map/ppermute | solution.py:290
  49.8 12.3 %collective-permute-start.18 = (bf16[256,768]{1,0:T(8,128)(2,1)}, bf16[256,768]{1,0:T(8,128)(2,1)S(1)}, u32[]{:S(2)}, u32[]{:S(2)}) collective-permute-start(bf16[256,768]{1,0:T(8,128)(2,1)} %collective-permute-done.15), channel_id=1, source_target_pairs={{1,0},{2,3},{5,4},{6,7},{9,8},{10,11},{13,12},{14,15},{17,16},{18,... | collective-permute-start | bytes 1179656 | tf_op jit(solution)/shard_map/ppermute | solution.py:290
  54.9 11.1 %collective-permute-start.19 = (bf16[256,768]{1,0:T(8,128)(2,1)S(1)}, bf16[256,768]{1,0:T(8,128)(2,1)S(1)}, u32[]{:S(2)}, u32[]{:S(2)}) collective-permute-start(bf16[256,768]{1,0:T(8,128)(2,1)S(1)} %broadcast_select_fusion.2.refs_4_), channel_id=1, source_target_pairs={{0,16},{1,17},{2,18},{3,19},{4,20},{5,21},{6,22},{7,23},{8,24},{9,... | collective-permute-start | bytes 1179656 | tf_op jit(solution)/shard_map/ppermute | solution.py:290
  56.1 9.9 %collective-permute-start.20 = (bf16[256,768]{1,0:T(8,128)(2,1)}, bf16[256,768]{1,0:T(8,128)(2,1)S(1)}, u32[]{:S(2)}, u32[]{:S(2)}) collective-permute-start(bf16[256,768]{1,0:T(8,128)(2,1)} %collective-permute-done.17.refs_6_), channel_id=1, source_target_pairs={{1,2},{2,1},{5,6},{6,5},{9,10},{10,9},{13,14},{14,13},{17,18},{18,... | collective-permute-start | bytes 1179656 | tf_op jit(solution)/shard_map/ppermute | solution.py:290
  59.6 13.1 %collective-permute-start.10 = (bf16[256,768]{1,0:T(8,128)(2,1)}, bf16[256,768]{1,0:T(8,128)(2,1)S(1)}, u32[]{:S(2)}, u32[]{:S(2)}) collective-permute-start(bf16[256,768]{1,0:T(8,128)(2,1)} %collective-permute-done.7), channel_id=1, source_target_pairs={{1,0},{2,3},{5,4},{6,7},{9,8},{10,11},{13,12},{14,15},{17,16},{18,... | collective-permute-start | bytes 1179656 | tf_op jit(solution)/shard_map/ppermute | solution.py:290
  62.0 12.4 %collective-permute-start.11 = (bf16[256,768]{1,0:T(8,128)(2,1)S(1)}, bf16[256,768]{1,0:T(8,128)(2,1)S(1)}, u32[]{:S(2)}, u32[]{:S(2)}) collective-permute-start(bf16[256,768]{1,0:T(8,128)(2,1)S(1)} %broadcast_select_fusion.3.refs_10_), channel_id=1, source_target_pairs={{0,16},{1,17},{2,18},{3,19},{4,20},{5,21},{6,22},{7,23},{8,24},{9,... | collective-permute-start | bytes 1179656 | tf_op jit(solution)/shard_map/ppermute | solution.py:290
  74.4 12.3 %collective-permute-start.24 = (bf16[256,4096]{1,0:T(8,128)(2,1)}, bf16[256,4096]{1,0:T(8,128)(2,1)S(1)}, u32[]{:S(2)}, u32[]{:S(2)}) collective-permute-start(bf16[256,4096]{1,0:T(8,128)(2,1)} %collective-permute-done.21.refs_0_), channel_id=1, source_target_pairs={{0,4},{1,5},{2,6},{3,7},{4,0},{5,1},{6,2},{7,3},{8,12},{9,13},{10,... | collective-permute-start | bytes 6291464 | tf_op jit(solution)/shard_map/ppermute | solution.py:290
  81.4 10.9 %collective-permute-start.22 = (bf16[256,256]{1,0:T(8,128)(2,1)S(1)}, bf16[256,256]{1,0:T(8,128)(2,1)S(1)}, u32[]{:S(2)}, u32[]{:S(2)}) collective-permute-start(bf16[256,256]{1,0:T(8,128)(2,1)S(1)} %slice.28), channel_id=1, source_target_pairs={{1,0},{2,3},{5,4},{6,7},{9,8},{10,11},{13,12},{14,15},{17,16},{18,... | collective-permute-start | bytes 393224 | tf_op jit(solution)/shard_map/ppermute | solution.py:290
  82.7 13.2 %collective-permute-start.26 = (bf16[256,512]{1,0:T(8,128)(2,1)S(1)}, bf16[256,512]{1,0:T(8,128)(2,1)S(1)}, u32[]{:S(2)}, u32[]{:S(2)}) collective-permute-start(bf16[256,512]{1,0:T(8,128)(2,1)S(1)} %slice.30), channel_id=1, source_target_pairs={{1,0},{2,3},{5,4},{6,7},{9,8},{10,11},{13,12},{14,15},{17,16},{18,... | collective-permute-start | bytes 786440 | tf_op jit(solution)/shard_map/ppermute | solution.py:290
  85.1 7.2 %copy-start = (bf16[144,768]{1,0:T(8,128)(2,1)S(1)}, bf16[144,768]{1,0:T(8,128)(2,1)}, u32[]{:S(2)}) copy-start(bf16[144,768]{1,0:T(8,128)(2,1)} %get-tuple-element.81.refs_13_.refs_8_.refs_5_) | copy-start | bytes 663556
  85.2 7.2 %collective-permute-start.23 = (bf16[256,256]{1,0:T(8,128)(2,1)S(1)}, bf16[256,256]{1,0:T(8,128)(2,1)S(1)}, u32[]{:S(2)}, u32[]{:S(2)}) collective-permute-start(bf16[256,256]{1,0:T(8,128)(2,1)S(1)} %slice.35), channel_id=1, source_target_pairs={{0,16},{1,17},{2,18},{3,19},{4,20},{5,21},{6,22},{7,23},{8,24},{9,... | collective-permute-start | bytes 393224 | tf_op jit(solution)/shard_map/ppermute | solution.py:290
  86.5 9.5 %collective-permute-start.27 = (bf16[256,512]{1,0:T(8,128)(2,1)S(1)}, bf16[256,512]{1,0:T(8,128)(2,1)S(1)}, u32[]{:S(2)}, u32[]{:S(2)}) collective-permute-start(bf16[256,512]{1,0:T(8,128)(2,1)S(1)} %slice.36), channel_id=1, source_target_pairs={{0,16},{1,17},{2,18},{3,19},{4,20},{5,21},{6,22},{7,23},{8,24},{9,... | collective-permute-start | bytes 786440 | tf_op jit(solution)/shard_map/ppermute | solution.py:290
  94.0 3.5 %collective-permute-start.25 = (bf16[128,256]{1,0:T(8,128)(2,1)S(1)}, bf16[128,256]{1,0:T(8,128)(2,1)S(1)}, u32[]{:S(2)}, u32[]{:S(2)}) collective-permute-start(bf16[128,256]{1,0:T(8,128)(2,1)S(1)} %get-tuple-element.120), channel_id=1, source_target_pairs={{0,16},{1,17},{2,18},{3,19},{4,20},{5,21},{6,22},{7,23},{8,24},{9,... | collective-permute-start | bytes 196616 | tf_op jit(solution)/shard_map/ppermute | solution.py:290
  96.0 1.6 %copy-start.2 = (f32[16]{0:T(128)S(1)}, f32[16]{0:T(128)}, u32[]{:S(2)}) copy-start(f32[16]{0:T(128)} %gate_ref.5) | copy-start | bytes 196
  98.7 12.8 %collective-permute-start.28 = (bf16[256,256]{1,0:T(8,128)(2,1)S(1)}, bf16[256,256]{1,0:T(8,128)(2,1)S(1)}, u32[]{:S(2)}, u32[]{:S(2)}) collective-permute-start(bf16[256,256]{1,0:T(8,128)(2,1)S(1)} %get-tuple-element.132), channel_id=1, source_target_pairs={{0,8},{1,9},{2,10},{3,11},{4,12},{5,13},{6,14},{7,15},{8,0},{9,1},... | collective-permute-start | bytes 393224 | tf_op jit(solution)/shard_map/ppermute | solution.py:290
  99.1 12.5 %collective-permute-start.30 = (bf16[256,256]{1,0:T(8,128)(2,1)S(1)}, bf16[256,256]{1,0:T(8,128)(2,1)S(1)}, u32[]{:S(2)}, u32[]{:S(2)}) collective-permute-start(bf16[256,256]{1,0:T(8,128)(2,1)S(1)} %get-tuple-element.133), channel_id=1, source_target_pairs={{0,12},{1,13},{2,14},{3,15},{4,8},{5,9},{6,10},{7,11},{8,4},{9,5},... | collective-permute-start | bytes 393224 | tf_op jit(solution)/shard_map/ppermute | solution.py:290
  104.8 6.9 %collective-permute-start.29 = (bf16[256,256]{1,0:T(8,128)(2,1)S(1)}, bf16[256,256]{1,0:T(8,128)(2,1)S(1)}, u32[]{:S(2)}, u32[]{:S(2)}) collective-permute-start(bf16[256,256]{1,0:T(8,128)(2,1)S(1)} %get-tuple-element.139), channel_id=1, source_target_pairs={{0,8},{1,9},{2,10},{3,11},{4,12},{5,13},{6,14},{7,15},{8,0},{9,1},... | collective-permute-start | bytes 393224 | tf_op jit(solution)/shard_map/ppermute | solution.py:290
  105.1 8.0 %collective-permute-start.31 = (bf16[256,256]{1,0:T(8,128)(2,1)S(1)}, bf16[256,256]{1,0:T(8,128)(2,1)S(1)}, u32[]{:S(2)}, u32[]{:S(2)}) collective-permute-start(bf16[256,256]{1,0:T(8,128)(2,1)S(1)} %get-tuple-element.140), channel_id=1, source_target_pairs={{0,12},{1,13},{2,14},{3,15},{4,8},{5,9},{6,10},{7,11},{8,4},{9,5},... | collective-permute-start | bytes 393224 | tf_op jit(solution)/shard_map/ppermute | solution.py:290
  110.2 3.0 %collective-permute-start.32 = (bf16[256,256]{1,0:T(8,128)(2,1)S(1)}, bf16[256,256]{1,0:T(8,128)(2,1)S(1)}, u32[]{:S(2)}, u32[]{:S(2)}) collective-permute-start(bf16[256,256]{1,0:T(8,128)(2,1)S(1)} %get-tuple-element.155), channel_id=1, source_target_pairs={{0,4},{1,5},{2,6},{3,7},{4,0},{5,1},{6,2},{7,3},{8,12},{9,13},{10,... | collective-permute-start | bytes 393224 | tf_op jit(solution)/shard_map/ppermute | solution.py:290
  111.5 1.6 %collective-permute-start.33 = (bf16[256,256]{1,0:T(8,128)(2,1)S(1)}, bf16[256,256]{1,0:T(8,128)(2,1)S(1)}, u32[]{:S(2)}, u32[]{:S(2)}) collective-permute-start(bf16[256,256]{1,0:T(8,128)(2,1)S(1)} %get-tuple-element.156), channel_id=1, source_target_pairs={{0,4},{1,5},{2,6},{3,7},{4,0},{5,1},{6,2},{7,3},{8,12},{9,13},{10,... | collective-permute-start | bytes 393224 | tf_op jit(solution)/shard_map/ppermute | solution.py:290

commit v19 on v17

--- a/solution.py
+++ b/solution.py
@@ -430,7 +430,8 @@
 
     ready = local((2, 3), 0)
     base = after(base, *ready[2, 0])
-    two0, three0 = mix((2, 3), (0,), base, ready)
+    (two0,) = mix((2,), (0,), base, ready)
+    (three0,) = mix((3,), (0,), after(base, two0), ready)
     ready |= local((2, 3), 1, two0, three0)
     two1, three1 = mix((2, 3), (1,), base, ready)
     ready |= local((1, 0), 0, two1, three1)

time: 114 us -> 115 us (level)
    pallas_call x3 -> x4, Pallas kernels: 3.96 us -> 4.7 us  [mix(): call(functools.partial(mix_body, segs, parts, group), [shape((length, hal...]
  transfers between devices with their start and end apart: 34 -> 34, of which waited for: 10 -> 11; matrix products, arithmetic and copies ran while one was open for 5% -> 5% of each run, Pallas kernels for 20% -> 21%
where the time goes in v19:
time: 115 us; the launch traced here: 114 us
  starting transfers between devices  52.4 us (46%)
  waiting for transfers between devices  26.9 us (23%)
  Pallas kernels  26.4 us (23%)
  other arithmetic  4.94 us (4%)
  local copies, waits for them, and re-layouts  2.56 us (2%)
    ppermute x34, starting transfers between devices, permute(): return lax.ppermute(array, AXES, pairs)  52.4 us
    ppermute x34, waiting for transfers between devices, permute(): return lax.ppermute(array, AXES, pairs)  26.9 us
    pallas_call x2, Pallas kernels, project(): call(functools.partial(project_body, early, late, line), [shape((length,...  9.75 us
    pallas_call x4, Pallas kernels, local(): call(functools.partial(local_body, len(segs), len(late) + 1, halves[1 + p...  6.5 us
    pallas_call x4, Pallas kernels, mix(): call(functools.partial(mix_body, segs, parts, group), [shape((length, hal...  4.7 us
  transfers between devices with their start and end apart: 34, of which 11 were waited for; matrix products, arithmetic and copies ran while one was open for 5% of the time, Pallas kernels for 21%

profile of v19, /device:TPU:9, one launch (start us, length us, event | category | flops | bytes accessed | tf_op | source)
XLA Modules:
  0.0 114.3 jit_solution(17713621266367421425)
XLA Ops:
  0.0 0.7 collective-permute-start.3
  1.3 0.7 pad_add_fusion.here_ref
  2.0 2.1 %shard_map.73 = (bf16[144,768]{1,0:T(8,128)(2,1)}, bf16[144,768]{1,0:T(8,128)(2,1)}, bf16[144,768]{1,0:T(8,128)(2,1)}, bf16[144,768]{1,0:T(8,128)(2,1)}) custom-call(s32[4]{0:T(128)} %pad_add_fusion.here_ref, s32[1,1]{1,0:T(1,128)S(6)} %copy.8.valid_ref, s32[1,1,2,2]{3,2,1,0:T(2,128)} %mask_ref.1, bf16[128,2048]{1,0:T(8,128)(2,1)} %wq_ref.1, ...), custom_call_target="tpu_custom_call" | custom-call | bytes 4194304 | tf_op jit(solution)/shard_map/pallas_call | solution.py:285
  4.1 0.2 collective-permute-start
  4.3 1.5 %collective-permute-start.2 = (bf16[144,768]{1,0:T(8,128)(2,1)}, bf16[144,768]{1,0:T(8,128)(2,1)S(1)}, u32[]{:S(2)}, u32[]{:S(2)}) collective-permute-start(bf16[144,768]{1,0:T(8,128)(2,1)} %get-tuple-element.83), channel_id=1, source_target_pairs={{0,12},{1,13},{2,14},{3,15},{4,8},{5,9},{6,10},{7,11},{8,4},{9,5},... | collective-permute-start | bytes 663560 | tf_op jit(solution)/shard_map/ppermute | solution.py:279
  5.8 0.3 collective-permute-start.1
  6.0 0.9 slice.24
  7.0 5.3 %collective-permute-done.2.refs_16_.refs_8_.refs_4_.refs_5_ = bf16[144,768]{1,0:T(8,128)(2,1)S(1)} collective-permute-done((bf16[144,768]{1,0:T(8,128)(2,1)}, bf16[144,768]{1,0:T(8,128)(2,1)S(1)}, u32[]{:S(2)}, u32[]{:S(2)}) %collective-permute-start.2) | collective-permute-done | bytes 221216 | tf_op jit(solution)/shard_map/ppermute | solution.py:279
  12.3 4.4 %collective-permute-done.1.refs_15_.refs_7_.refs_4_ = bf16[144,768]{1,0:T(8,128)(2,1)S(1)} collective-permute-done((bf16[144,768]{1,0:T(8,128)(2,1)}, bf16[144,768]{1,0:T(8,128)(2,1)S(1)}, u32[]{:S(2)}, u32[]{:S(2)}) %collective-permute-start.1) | collective-permute-done | bytes 221216 | tf_op jit(solution)/shard_map/ppermute | solution.py:279
  16.8 1.4 %collective-permute-start.21 = (bf16[256,4096]{1,0:T(8,128)(2,1)S(1)}, bf16[256,4096]{1,0:T(8,128)(2,1)}, u32[]{:S(2)}, u32[]{:S(2)}) collective-permute-start(bf16[256,4096]{1,0:T(8,128)(2,1)S(1)} %bitcast.6), channel_id=1, source_target_pairs={{0,8},{1,9},{2,10},{3,11},{4,12},{5,13},{6,14},{7,15},{8,0},{9,1},... | collective-permute-start | bytes 6291464 | tf_op jit(solution)/shard_map/ppermute | solution.py:279
  18.2 4.3 %collective-permute-start.13 = (bf16[256,768]{1,0:T(8,128)(2,1)S(1)}, bf16[256,768]{1,0:T(8,128)(2,1)}, u32[]{:S(2)}, u32[]{:S(2)}) collective-permute-start(bf16[256,768]{1,0:T(8,128)(2,1)S(1)} %pad_maximum_fusion.refs_2_), channel_id=1, source_target_pairs={{1,2},{2,1},{5,6},{6,5},{9,10},{10,9},{13,14},{14,13},{17,18},{18,... | collective-permute-start | bytes 1179656 | tf_op jit(solution)/shard_map/ppermute | solution.py:279
  22.5 1.3 %collective-permute-start.14 = (bf16[256,768]{1,0:T(8,128)(2,1)S(1)}, bf16[256,768]{1,0:T(8,128)(2,1)S(1)}, u32[]{:S(2)}, u32[]{:S(2)}) collective-permute-start(bf16[256,768]{1,0:T(8,128)(2,1)S(1)} %pad_maximum_fusion.refs_2_), channel_id=1, source_target_pairs={{0,16},{1,17},{2,18},{3,19},{4,20},{5,21},{6,22},{7,23},{8,24},{9,... | collective-permute-start | bytes 1179656 | tf_op jit(solution)/shard_map/ppermute | solution.py:279
  23.8 3.0 %collective-permute-done.12.refs_3_ = bf16[256,768]{1,0:T(8,128)(2,1)} collective-permute-done((bf16[256,768]{1,0:T(8,128)(2,1)S(1)}, bf16[256,768]{1,0:T(8,128)(2,1)}, u32[]{:S(2)}, u32[]{:S(2)}) %collective-permute-start.12) | collective-permute-done | bytes 393248 | tf_op jit(solution)/shard_map/ppermute | solution.py:279
  26.8 3.2 %collective-permute-start.5 = (bf16[256,768]{1,0:T(8,128)(2,1)S(1)}, bf16[256,768]{1,0:T(8,128)(2,1)}, u32[]{:S(2)}, u32[]{:S(2)}) collective-permute-start(bf16[256,768]{1,0:T(8,128)(2,1)S(1)} %pad_maximum_fusion.1.refs_9_), channel_id=1, source_target_pairs={{1,2},{2,1},{5,6},{6,5},{9,10},{10,9},{13,14},{14,13},{17,18},{18,... | collective-permute-start | bytes 1179656 | tf_op jit(solution)/shard_map/ppermute | solution.py:279
  30.0 0.7 collective-permute-done.13
  30.7 1.2 %collective-permute-start.6 = (bf16[256,768]{1,0:T(8,128)(2,1)S(1)}, bf16[256,768]{1,0:T(8,128)(2,1)S(1)}, u32[]{:S(2)}, u32[]{:S(2)}) collective-permute-start(bf16[256,768]{1,0:T(8,128)(2,1)S(1)} %pad_maximum_fusion.1.refs_9_), channel_id=1, source_target_pairs={{0,16},{1,17},{2,18},{3,19},{4,20},{5,21},{6,22},{7,23},{8,24},{9,... | collective-permute-start | bytes 1179656 | tf_op jit(solution)/shard_map/ppermute | solution.py:279
  32.0 0.7 copy-done.4
  32.7 3.1 %collective-permute-start.15 = (bf16[256,768]{1,0:T(8,128)(2,1)}, bf16[256,768]{1,0:T(8,128)(2,1)}, u32[]{:S(2)}, u32[]{:S(2)}) collective-permute-start(bf16[256,768]{1,0:T(8,128)(2,1)} %collective-permute-done.12.refs_3_), channel_id=1, source_target_pairs={{1,2},{2,1},{5,6},{6,5},{9,10},{10,9},{13,14},{14,13},{17,18},{18,... | collective-permute-start | bytes 1179656 | tf_op jit(solution)/shard_map/ppermute | solution.py:279
  35.8 2.5 %collective-permute-start.16 = (bf16[256,768]{1,0:T(8,128)(2,1)}, bf16[256,768]{1,0:T(8,128)(2,1)}, u32[]{:S(2)}, u32[]{:S(2)}) collective-permute-start(bf16[256,768]{1,0:T(8,128)(2,1)} %collective-permute-done.13), channel_id=1, source_target_pairs={{1,0},{2,3},{5,4},{6,7},{9,8},{10,11},{13,12},{14,15},{17,16},{18,... | collective-permute-start | bytes 1179656 | tf_op jit(solution)/shard_map/ppermute | solution.py:279
  38.3 1.1 collective-permute-start.17
  39.4 0.7 copy-done.6
  40.1 4.3 %collective-permute-start.7 = (bf16[256,768]{1,0:T(8,128)(2,1)}, bf16[256,768]{1,0:T(8,128)(2,1)}, u32[]{:S(2)}, u32[]{:S(2)}) collective-permute-start(bf16[256,768]{1,0:T(8,128)(2,1)} %collective-permute-done.4.refs_10_), channel_id=1, source_target_pairs={{1,2},{2,1},{5,6},{6,5},{9,10},{10,9},{13,14},{14,13},{17,18},{18,... | collective-permute-start | bytes 1179656 | tf_op jit(solution)/shard_map/ppermute | solution.py:279
  44.4 2.1 %collective-permute-done.15 = bf16[256,768]{1,0:T(8,128)(2,1)} collective-permute-done((bf16[256,768]{1,0:T(8,128)(2,1)}, bf16[256,768]{1,0:T(8,128)(2,1)}, u32[]{:S(2)}, u32[]{:S(2)}) %collective-permute-start.15) | collective-permute-done | bytes 393248 | tf_op jit(solution)/shard_map/ppermute | solution.py:279
  46.5 2.0 %collective-permute-start.8 = (bf16[256,768]{1,0:T(8,128)(2,1)}, bf16[256,768]{1,0:T(8,128)(2,1)}, u32[]{:S(2)}, u32[]{:S(2)}) collective-permute-start(bf16[256,768]{1,0:T(8,128)(2,1)} %collective-permute-done.5), channel_id=1, source_target_pairs={{1,0},{2,3},{5,4},{6,7},{9,8},{10,11},{13,12},{14,15},{17,16},{18,... | collective-permute-start | bytes 1179656 | tf_op jit(solution)/shard_map/ppermute | solution.py:279
  48.6 1.2 %collective-permute-start.9 = (bf16[256,768]{1,0:T(8,128)(2,1)}, bf16[256,768]{1,0:T(8,128)(2,1)S(1)}, u32[]{:S(2)}, u32[]{:S(2)}) collective-permute-start(bf16[256,768]{1,0:T(8,128)(2,1)} %collective-permute-done.4.refs_10_), channel_id=1, source_target_pairs={{0,16},{1,17},{2,18},{3,19},{4,20},{5,21},{6,22},{7,23},{8,24},{9,... | collective-permute-start | bytes 1179656 | tf_op jit(solution)/shard_map/ppermute | solution.py:279
  49.8 1.3 %collective-permute-start.18 = (bf16[256,768]{1,0:T(8,128)(2,1)}, bf16[256,768]{1,0:T(8,128)(2,1)S(1)}, u32[]{:S(2)}, u32[]{:S(2)}) collective-permute-start(bf16[256,768]{1,0:T(8,128)(2,1)} %collective-permute-done.15), channel_id=1, source_target_pairs={{1,0},{2,3},{5,4},{6,7},{9,8},{10,11},{13,12},{14,15},{17,16},{18,... | collective-permute-start | bytes 1179656 | tf_op jit(solution)/shard_map/ppermute | solution.py:279
  51.1 1.1 broadcast_select_fusion.2.refs_4_
  52.2 2.8 %collective-permute-done.7 = bf16[256,768]{1,0:T(8,128)(2,1)} collective-permute-done((bf16[256,768]{1,0:T(8,128)(2,1)}, bf16[256,768]{1,0:T(8,128)(2,1)}, u32[]{:S(2)}, u32[]{:S(2)}) %collective-permute-start.7) | collective-permute-done | bytes 393248 | tf_op jit(solution)/shard_map/ppermute | solution.py:279
  54.9 1.2 %collective-permute-start.19 = (bf16[256,768]{1,0:T(8,128)(2,1)S(1)}, bf16[256,768]{1,0:T(8,128)(2,1)S(1)}, u32[]{:S(2)}, u32[]{:S(2)}) collective-permute-start(bf16[256,768]{1,0:T(8,128)(2,1)S(1)} %broadcast_select_fusion.2.refs_4_), channel_id=1, source_target_pairs={{0,16},{1,17},{2,18},{3,19},{4,20},{5,21},{6,22},{7,23},{8,24},{9,... | collective-permute-start | bytes 1179656 | tf_op jit(solution)/shard_map/ppermute | solution.py:279
  56.2 3.5 %collective-permute-start.20 = (bf16[256,768]{1,0:T(8,128)(2,1)}, bf16[256,768]{1,0:T(8,128)(2,1)S(1)}, u32[]{:S(2)}, u32[]{:S(2)}) collective-permute-start(bf16[256,768]{1,0:T(8,128)(2,1)} %collective-permute-done.17.refs_7_), channel_id=1, source_target_pairs={{1,2},{2,1},{5,6},{6,5},{9,10},{10,9},{13,14},{14,13},{17,18},{18,... | collective-permute-start | bytes 1179656 | tf_op jit(solution)/shard_map/ppermute | solution.py:279
  59.7 1.3 %collective-permute-start.10 = (bf16[256,768]{1,0:T(8,128)(2,1)}, bf16[256,768]{1,0:T(8,128)(2,1)S(1)}, u32[]{:S(2)}, u32[]{:S(2)}) collective-permute-start(bf16[256,768]{1,0:T(8,128)(2,1)} %collective-permute-done.7), channel_id=1, source_target_pairs={{1,0},{2,3},{5,4},{6,7},{9,8},{10,11},{13,12},{14,15},{17,16},{18,... | collective-permute-start | bytes 1179656 | tf_op jit(solution)/shard_map/ppermute | solution.py:279
  61.0 1.1 broadcast_select_fusion.3.refs_11_
  62.1 0.3 collective-permute-start.11
  62.4 3.7 %collective-permute-done.19.refs_8_ = bf16[256,768]{1,0:T(8,128)(2,1)S(1)} collective-permute-done((bf16[256,768]{1,0:T(8,128)(2,1)S(1)}, bf16[256,768]{1,0:T(8,128)(2,1)S(1)}, u32[]{:S(2)}, u32[]{:S(2)}) %collective-permute-start.19) | collective-permute-done | bytes 393248 | tf_op jit(solution)/shard_map/ppermute | solution.py:279
  66.1 1.1 broadcast_select_fusion.1.refs_5_
  67.2 4.9 %shard_map.74 = (f32[256,768]{1,0:T(8,128)S(1)}, f32[256,768]{1,0:T(8,128)S(1)}, bf16[256,1024]{1,0:T(8,128)(2,1)S(1)}, bf16[256,1024]{1,0:T(8,128)(2,1)S(1)}) custom-call(s32[4]{0:T(128)S(1)} %copy-done.1, bf16[256,4096]{1,0:T(8,128)(2,1)S(1)} %bitcast.7, bf16[256,4096]{1,0:T(8,128)(2,1)} %collective-permute-done.3.refs_1_, ...), custom_call_target="tpu_custom_call" | custom-call | flops 2415919104 | bytes 4194304 | tf_op jit(solution)/shard_map/pallas_call | solution.py:317
  72.1 2.4 %collective-permute-done.11.refs_1_ = bf16[256,768]{1,0:T(8,128)(2,1)S(1)} collective-permute-done((bf16[256,768]{1,0:T(8,128)(2,1)S(1)}, bf16[256,768]{1,0:T(8,128)(2,1)S(1)}, u32[]{:S(2)}, u32[]{:S(2)}) %collective-permute-start.11) | collective-permute-done | bytes 393248 | tf_op jit(solution)/shard_map/ppermute | solution.py:279
  74.5 6.2 %collective-permute-start.24 = (bf16[256,4096]{1,0:T(8,128)(2,1)}, bf16[256,4096]{1,0:T(8,128)(2,1)S(1)}, u32[]{:S(2)}, u32[]{:S(2)}) collective-permute-start(bf16[256,4096]{1,0:T(8,128)(2,1)} %collective-permute-done.21.refs_0_), channel_id=1, source_target_pairs={{0,4},{1,5},{2,6},{3,7},{4,0},{5,1},{6,2},{7,3},{8,12},{9,13},{10,... | collective-permute-start | bytes 6291464 | tf_op jit(solution)/shard_map/ppermute | solution.py:279
  80.8 1.3 %collective-permute-start.22 = (bf16[256,256]{1,0:T(8,128)(2,1)S(1)}, bf16[256,256]{1,0:T(8,128)(2,1)S(1)}, u32[]{:S(2)}, u32[]{:S(2)}) collective-permute-start(bf16[256,256]{1,0:T(8,128)(2,1)S(1)} %slice.28), channel_id=1, source_target_pairs={{1,0},{2,3},{5,4},{6,7},{9,8},{10,11},{13,12},{14,15},{17,16},{18,... | collective-permute-start | bytes 393224 | tf_op jit(solution)/shard_map/ppermute | solution.py:279
  82.1 1.3 %collective-permute-start.26 = (bf16[256,512]{1,0:T(8,128)(2,1)S(1)}, bf16[256,512]{1,0:T(8,128)(2,1)S(1)}, u32[]{:S(2)}, u32[]{:S(2)}) collective-permute-start(bf16[256,512]{1,0:T(8,128)(2,1)S(1)} %slice.30), channel_id=1, source_target_pairs={{1,0},{2,3},{5,4},{6,7},{9,8},{10,11},{13,12},{14,15},{17,16},{18,... | collective-permute-start | bytes 786440 | tf_op jit(solution)/shard_map/ppermute | solution.py:279
  83.4 1.1 broadcast_select_fusion.refs_0_
  84.5 1.3 %collective-permute-start.23 = (bf16[256,256]{1,0:T(8,128)(2,1)S(1)}, bf16[256,256]{1,0:T(8,128)(2,1)S(1)}, u32[]{:S(2)}, u32[]{:S(2)}) collective-permute-start(bf16[256,256]{1,0:T(8,128)(2,1)S(1)} %slice.35), channel_id=1, source_target_pairs={{0,16},{1,17},{2,18},{3,19},{4,20},{5,21},{6,22},{7,23},{8,24},{9,... | collective-permute-start | bytes 393224 | tf_op jit(solution)/shard_map/ppermute | solution.py:279
  85.9 0.2 collective-permute-start.27
  86.0 4.9 %shard_map.75 = (f32[256,768]{1,0:T(8,128)S(1)}, f32[256,768]{1,0:T(8,128)S(1)}, bf16[256,1024]{1,0:T(8,128)(2,1)S(1)}, bf16[256,1024]{1,0:T(8,128)(2,1)S(1)}) custom-call(s32[4]{0:T(128)S(1)} %copy-done.1, bf16[256,4096]{1,0:T(8,128)(2,1)} %collective-permute-done.21.refs_0_, bf16[256,4096]{1,0:T(8,128)(2,1)S(1)} %collective-permute-done.24.refs_1_, ...), custom_call_target="tpu_custom_call" | custom-call | flops 2415919104 | bytes 4194304 | tf_op jit(solution)/shard_map/pallas_call | solution.py:317
  90.9 1.7 %shard_map.76 = (bf16[256,256]{1,0:T(8,128)(2,1)S(1)}, f32[128,256]{1,0:T(8,128)S(1)}, bf16[256,256]{1,0:T(8,128)(2,1)S(1)}, f32[128,256]{1,0:T(8,128)S(1)}, bf1...) custom-call(s32[4]{0:T(128)S(1)} %copy-done.1, ...), custom_call_target="tpu_custom_call" | custom-call | flops 536870912 | bytes 4194304 | tf_op jit(solution)/shard_map/pallas_call | solution.py:390
  92.7 1.3 %collective-permute-start.25 = (bf16[128,256]{1,0:T(8,128)(2,1)S(1)}, bf16[128,256]{1,0:T(8,128)(2,1)S(1)}, u32[]{:S(2)}, u32[]{:S(2)}) collective-permute-start(bf16[128,256]{1,0:T(8,128)(2,1)S(1)} %get-tuple-element.119), channel_id=1, source_target_pairs={{0,16},{1,17},{2,18},{3,19},{4,20},{5,21},{6,22},{7,23},{8,24},{9,... | collective-permute-start | bytes 196616 | tf_op jit(solution)/shard_map/ppermute | solution.py:279
  94.0 1.3 %collective-permute-done.27.refs_4_ = bf16[256,512]{1,0:T(8,128)(2,1)S(1)} collective-permute-done((bf16[256,512]{1,0:T(8,128)(2,1)S(1)}, bf16[256,512]{1,0:T(8,128)(2,1)S(1)}, u32[]{:S(2)}, u32[]{:S(2)}) %collective-permute-start.27) | collective-permute-done | bytes 262176 | tf_op jit(solution)/shard_map/ppermute | solution.py:279
  95.3 1.6 %shard_map.77 = (bf16[256,256]{1,0:T(8,128)(2,1)S(1)}, f32[256,256]{1,0:T(8,128)S(1)}, bf16[256,256]{1,0:T(8,128)(2,1)S(1)}, f32[256,256]{1,0:T(8,128)S(1)}) custom-call(s32[4]{0:T(128)S(1)} %copy-done.1, bf16[256,768]{1,0:T(8,128)(2,1)S(1)} %broadcast_select_fusion.refs_0_, bf16[256,768]{1,0:T(8,128)(2,1)S(1)} %collective-permute-done.11.refs_1_, ...), custom_call_target="tpu_custom_call" | custom-call | flops 134217728 | bytes 4194304 | tf_op jit(solution)/shard_map/pallas_call | solution.py:410
  96.9 1.0 shard_map.78
  97.9 0.4 collective-permute-start.28
  98.2 1.0 shard_map.79
  99.2 2.4 %collective-permute-start.30 = (bf16[256,256]{1,0:T(8,128)(2,1)S(1)}, bf16[256,256]{1,0:T(8,128)(2,1)S(1)}, u32[]{:S(2)}, u32[]{:S(2)}) collective-permute-start(bf16[256,256]{1,0:T(8,128)(2,1)S(1)} %shard_map.79), channel_id=1, source_target_pairs={{0,12},{1,13},{2,14},{3,15},{4,8},{5,9},{6,10},{7,11},{8,4},{9,5},... | collective-permute-start | bytes 393224 | tf_op jit(solution)/shard_map/ppermute | solution.py:279
  101.6 1.8 %shard_map.80 = (bf16[256,256]{1,0:T(8,128)(2,1)S(1)}, f32[256,256]{1,0:T(8,128)S(1)}, bf16[256,256]{1,0:T(8,128)(2,1)S(1)}, f32[256,256]{1,0:T(8,128)S(1)}) custom-call(s32[4]{0:T(128)S(1)} %copy-done.1, bf16[256,768]{1,0:T(8,128)(2,1)S(1)} %broadcast_select_fusion.refs_0_, bf16[256,768]{1,0:T(8,128)(2,1)S(1)} %collective-permute-done.11.refs_1_, ...), custom_call_target="tpu_custom_call" | custom-call | flops 134217728 | bytes 4194304 | tf_op jit(solution)/shard_map/pallas_call | solution.py:410
  103.4 1.2 %shard_map.81 = (bf16[256,256]{1,0:T(8,128)(2,1)S(1)}, bf16[256,256]{1,0:T(8,128)(2,1)S(1)}) custom-call(s32[4]{0:T(128)S(1)} %copy-done.1, f32[16]{0:T(128)S(1)} %copy-done.2, bf16[128,256]{1,0:T(8,128)(2,1)S(1)} %collective-permute-done.25.base_ref, f32[128,256]{1,0:T(8,128)S(1)} %get-tuple-element.125.refs_0_, f32[128,256]{1,0:T(8,128)S(1)} %get-tuple-element.126.refs_1_, ...), custom_call_target="tpu_custom_call" | custom-call | flops 201326592 | bytes 4194304 | tf_op jit(solution)/shard_map/pallas_call | solution.py:421
  104.6 0.4 collective-permute-start.29
  104.9 0.5 collective-permute-start.31
  105.5 1.6 %shard_map.83 = (bf16[256,256]{1,0:T(8,128)(2,1)S(1)}, f32[256,256]{1,0:T(8,128)S(1)}, bf16[256,256]{1,0:T(8,128)(2,1)S(1)}, f32[256,256]{1,0:T(8,128)S(1)}) custom-call(s32[4]{0:T(128)S(1)} %copy-done.1, bf16[256,768]{1,0:T(8,128)(2,1)S(1)} %broadcast_select_fusion.refs_0_, bf16[256,768]{1,0:T(8,128)(2,1)S(1)} %collective-permute-done.11.refs_1_, ...), custom_call_target="tpu_custom_call" | custom-call | flops 134217728 | bytes 4194304 | tf_op jit(solution)/shard_map/pallas_call | solution.py:410
  107.0 1.6 %shard_map.84 = (bf16[256,256]{1,0:T(8,128)(2,1)S(1)}, f32[256,256]{1,0:T(8,128)S(1)}, bf16[256,256]{1,0:T(8,128)(2,1)S(1)}, f32[256,256]{1,0:T(8,128)S(1)}) custom-call(s32[4]{0:T(128)S(1)} %copy-done.1, bf16[256,768]{1,0:T(8,128)(2,1)S(1)} %broadcast_select_fusion.refs_0_, bf16[256,768]{1,0:T(8,128)(2,1)S(1)} %collective-permute-done.11.refs_1_, ...), custom_call_target="tpu_custom_call" | custom-call | flops 134217728 | bytes 4194304 | tf_op jit(solution)/shard_map/pallas_call | solution.py:410
  108.6 1.6 %shard_map.85 = (bf16[256,256]{1,0:T(8,128)(2,1)S(1)}, bf16[256,256]{1,0:T(8,128)(2,1)S(1)}, bf16[256,256]{1,0:T(8,128)(2,1)S(1)}, bf16[256,256]{1,0:T(8,128)(2,1)S(1)}) custom-call(s32[4]{0:T(128)S(1)} %copy-done.1, f32[16]{0:T(128)S(1)} %copy-done.2, bf16[128,256]{1,0:T(8,128)(2,1)S(1)} %collective-permute-done.25.base_ref, ...), custom_call_target="tpu_custom_call" | custom-call | flops 402653184 | bytes 4194304 | tf_op jit(solution)/shard_map/pallas_call | solution.py:421
  110.2 1.1 collective-permute-start.32
  111.3 0.1 collective-permute-start.33
  111.4 0.9 collective-permute-done.31.refs_3_.refs_8_
  112.3 0.4 collective-permute-done.33.refs_4_
  112.7 1.6 %shard_map.86 = bf16[256,2048]{1,0:T(8,128)(2,1)} custom-call(s32[4]{0:T(128)S(1)} %copy-done.1, f32[8,128]{1,0:T(8,128)S(1)} %shard_map.82.refs_0_, bf16[256,256]{1,0:T(8,128)(2,1)S(1)} %get-tuple-element.151.refs_1_, bf16[256,256]{1,0:T(8,128)(2,1)S(1)} %get-tuple-element.152.refs_2_, bf16[256,256]{1,0:T(8,128)(2,1)S(1)} %collective-permute-done.32.refs_3_, ...), custom_call_target="tpu_custom_call" | custom-call | bytes 4194304 | tf_op jit(solution)/shard_map/pallas_call | solution.py:445
  (49 shorter events, 0.3 us)
Async XLA Ops:
  0.0 16.8 %copy-start.3 = (bf16[1,256,4096]{2,1,0:T(8,128)(2,1)S(1)}, bf16[1,256,4096]{2,1,0:T(8,128)(2,1)}, u32[]{:S(2)}) copy-start(bf16[1,256,4096]{2,1,0:T(8,128)(2,1)} %param.7) | copy-start | bytes 6291460
  0.0 16.7 %collective-permute-start.3 = (bf16[256,4096]{1,0:T(8,128)(2,1)}, bf16[256,4096]{1,0:T(8,128)(2,1)}, u32[]{:S(2)}, u32[]{:S(2)}) collective-permute-start(bf16[256,4096]{1,0:T(8,128)(2,1)} %bitcast.5), channel_id=1, source_target_pairs={{0,4},{1,5},{2,6},{3,7},{4,0},{5,1},{6,2},{7,3},{8,12},{9,13},{10,... | collective-permute-start | bytes 6291464 | tf_op jit(solution)/shard_map/ppermute | solution.py:279
  4.1 2.8 %collective-permute-start = (bf16[144,768]{1,0:T(8,128)(2,1)}, bf16[144,768]{1,0:T(8,128)(2,1)S(1)}, u32[]{:S(2)}, u32[]{:S(2)}) collective-permute-start(bf16[144,768]{1,0:T(8,128)(2,1)} %get-tuple-element.81), channel_id=1, source_target_pairs={{0,4},{1,5},{2,6},{3,7},{4,0},{5,1},{6,2},{7,3},{8,12},{9,13},{10,... | collective-permute-start | bytes 663560 | tf_op jit(solution)/shard_map/ppermute | solution.py:279
  4.3 7.9 %collective-permute-start.2 = (bf16[144,768]{1,0:T(8,128)(2,1)}, bf16[144,768]{1,0:T(8,128)(2,1)S(1)}, u32[]{:S(2)}, u32[]{:S(2)}) collective-permute-start(bf16[144,768]{1,0:T(8,128)(2,1)} %get-tuple-element.83), channel_id=1, source_target_pairs={{0,12},{1,13},{2,14},{3,15},{4,8},{5,9},{6,10},{7,11},{8,4},{9,5},... | collective-permute-start | bytes 663560 | tf_op jit(solution)/shard_map/ppermute | solution.py:279
  5.8 10.9 %collective-permute-start.1 = (bf16[144,768]{1,0:T(8,128)(2,1)}, bf16[144,768]{1,0:T(8,128)(2,1)S(1)}, u32[]{:S(2)}, u32[]{:S(2)}) collective-permute-start(bf16[144,768]{1,0:T(8,128)(2,1)} %get-tuple-element.82), channel_id=1, source_target_pairs={{0,8},{1,9},{2,10},{3,11},{4,12},{5,13},{6,14},{7,15},{8,0},{9,1},... | collective-permute-start | bytes 663560 | tf_op jit(solution)/shard_map/ppermute | solution.py:279
  16.7 50.5 %copy-start.1 = (s32[4]{0:T(128)S(1)}, s32[4]{0:T(128)}, u32[]{:S(2)}) copy-start(s32[4]{0:T(128)} %pad_add_fusion.here_ref) | copy-start | bytes 52
  16.7 10.1 %collective-permute-start.12 = (bf16[256,768]{1,0:T(8,128)(2,1)S(1)}, bf16[256,768]{1,0:T(8,128)(2,1)}, u32[]{:S(2)}, u32[]{:S(2)}) collective-permute-start(bf16[256,768]{1,0:T(8,128)(2,1)S(1)} %pad_maximum_fusion.refs_2_), channel_id=1, source_target_pairs={{0,1},{1,0},{2,3},{3,2},{4,5},{5,4},{6,7},{7,6},{8,9},{9,8},{10,11... | collective-permute-start | bytes 1179656 | tf_op jit(solution)/shard_map/ppermute | solution.py:279
  16.8 55.3 %collective-permute-start.21 = (bf16[256,4096]{1,0:T(8,128)(2,1)S(1)}, bf16[256,4096]{1,0:T(8,128)(2,1)}, u32[]{:S(2)}, u32[]{:S(2)}) collective-permute-start(bf16[256,4096]{1,0:T(8,128)(2,1)S(1)} %bitcast.6), channel_id=1, source_target_pairs={{0,8},{1,9},{2,10},{3,11},{4,12},{5,13},{6,14},{7,15},{8,0},{9,1},... | collective-permute-start | bytes 6291464 | tf_op jit(solution)/shard_map/ppermute | solution.py:279
  18.2 12.6 %collective-permute-start.13 = (bf16[256,768]{1,0:T(8,128)(2,1)S(1)}, bf16[256,768]{1,0:T(8,128)(2,1)}, u32[]{:S(2)}, u32[]{:S(2)}) collective-permute-start(bf16[256,768]{1,0:T(8,128)(2,1)S(1)} %pad_maximum_fusion.refs_2_), channel_id=1, source_target_pairs={{1,2},{2,1},{5,6},{6,5},{9,10},{10,9},{13,14},{14,13},{17,18},{18,... | collective-permute-start | bytes 1179656 | tf_op jit(solution)/shard_map/ppermute | solution.py:279
  22.5 9.5 %collective-permute-start.14 = (bf16[256,768]{1,0:T(8,128)(2,1)S(1)}, bf16[256,768]{1,0:T(8,128)(2,1)S(1)}, u32[]{:S(2)}, u32[]{:S(2)}) collective-permute-start(bf16[256,768]{1,0:T(8,128)(2,1)S(1)} %pad_maximum_fusion.refs_2_), channel_id=1, source_target_pairs={{0,16},{1,17},{2,18},{3,19},{4,20},{5,21},{6,22},{7,23},{8,24},{9,... | collective-permute-start | bytes 1179656 | tf_op jit(solution)/shard_map/ppermute | solution.py:279
  23.8 12.0 %collective-permute-start.4 = (bf16[256,768]{1,0:T(8,128)(2,1)S(1)}, bf16[256,768]{1,0:T(8,128)(2,1)}, u32[]{:S(2)}, u32[]{:S(2)}) collective-permute-start(bf16[256,768]{1,0:T(8,128)(2,1)S(1)} %pad_maximum_fusion.1.refs_9_), channel_id=1, source_target_pairs={{0,1},{1,0},{2,3},{3,2},{4,5},{5,4},{6,7},{7,6},{8,9},{9,8},{10,11... | collective-permute-start | bytes 1179656 | tf_op jit(solution)/shard_map/ppermute | solution.py:279
  26.8 11.5 %collective-permute-start.5 = (bf16[256,768]{1,0:T(8,128)(2,1)S(1)}, bf16[256,768]{1,0:T(8,128)(2,1)}, u32[]{:S(2)}, u32[]{:S(2)}) collective-permute-start(bf16[256,768]{1,0:T(8,128)(2,1)S(1)} %pad_maximum_fusion.1.refs_9_), channel_id=1, source_target_pairs={{1,2},{2,1},{5,6},{6,5},{9,10},{10,9},{13,14},{14,13},{17,18},{18,... | collective-permute-start | bytes 1179656 | tf_op jit(solution)/shard_map/ppermute | solution.py:279
  30.7 8.6 %collective-permute-start.6 = (bf16[256,768]{1,0:T(8,128)(2,1)S(1)}, bf16[256,768]{1,0:T(8,128)(2,1)S(1)}, u32[]{:S(2)}, u32[]{:S(2)}) collective-permute-start(bf16[256,768]{1,0:T(8,128)(2,1)S(1)} %pad_maximum_fusion.1.refs_9_), channel_id=1, source_target_pairs={{0,16},{1,17},{2,18},{3,19},{4,20},{5,21},{6,22},{7,23},{8,24},{9,... | collective-permute-start | bytes 1179656 | tf_op jit(solution)/shard_map/ppermute | solution.py:279
  32.0 0.7 copy-start.4
  32.7 13.8 %collective-permute-start.15 = (bf16[256,768]{1,0:T(8,128)(2,1)}, bf16[256,768]{1,0:T(8,128)(2,1)}, u32[]{:S(2)}, u32[]{:S(2)}) collective-permute-start(bf16[256,768]{1,0:T(8,128)(2,1)} %collective-permute-done.12.refs_3_), channel_id=1, source_target_pairs={{1,2},{2,1},{5,6},{6,5},{9,10},{10,9},{13,14},{14,13},{17,18},{18,... | collective-permute-start | bytes 1179656 | tf_op jit(solution)/shard_map/ppermute | solution.py:279
  35.8 12.8 %collective-permute-start.16 = (bf16[256,768]{1,0:T(8,128)(2,1)}, bf16[256,768]{1,0:T(8,128)(2,1)}, u32[]{:S(2)}, u32[]{:S(2)}) collective-permute-start(bf16[256,768]{1,0:T(8,128)(2,1)} %collective-permute-done.13), channel_id=1, source_target_pairs={{1,0},{2,3},{5,4},{6,7},{9,8},{10,11},{13,12},{14,15},{17,16},{18,... | collective-permute-start | bytes 1179656 | tf_op jit(solution)/shard_map/ppermute | solution.py:279
  38.3 11.6 %collective-permute-start.17 = (bf16[256,768]{1,0:T(8,128)(2,1)}, bf16[256,768]{1,0:T(8,128)(2,1)}, u32[]{:S(2)}, u32[]{:S(2)}) collective-permute-start(bf16[256,768]{1,0:T(8,128)(2,1)} %collective-permute-done.12.refs_3_), channel_id=1, source_target_pairs={{0,16},{1,17},{2,18},{3,19},{4,20},{5,21},{6,22},{7,23},{8,24},{9,... | collective-permute-start | bytes 1179656 | tf_op jit(solution)/shard_map/ppermute | solution.py:279
  39.4 0.7 copy-start.6
  40.1 14.8 %collective-permute-start.7 = (bf16[256,768]{1,0:T(8,128)(2,1)}, bf16[256,768]{1,0:T(8,128)(2,1)}, u32[]{:S(2)}, u32[]{:S(2)}) collective-permute-start(bf16[256,768]{1,0:T(8,128)(2,1)} %collective-permute-done.4.refs_10_), channel_id=1, source_target_pairs={{1,2},{2,1},{5,6},{6,5},{9,10},{10,9},{13,14},{14,13},{17,18},{18,... | collective-permute-start | bytes 1179656 | tf_op jit(solution)/shard_map/ppermute | solution.py:279
  46.5 9.7 %collective-permute-start.8 = (bf16[256,768]{1,0:T(8,128)(2,1)}, bf16[256,768]{1,0:T(8,128)(2,1)}, u32[]{:S(2)}, u32[]{:S(2)}) collective-permute-start(bf16[256,768]{1,0:T(8,128)(2,1)} %collective-permute-done.5), channel_id=1, source_target_pairs={{1,0},{2,3},{5,4},{6,7},{9,8},{10,11},{13,12},{14,15},{17,16},{18,... | collective-permute-start | bytes 1179656 | tf_op jit(solution)/shard_map/ppermute | solution.py:279
  48.6 18.6 %copy-start.5 = (bf16[256,768]{1,0:T(8,128)(2,1)S(1)}, bf16[256,768]{1,0:T(8,128)(2,1)}, u32[]{:S(2)}) copy-start(bf16[256,768]{1,0:T(8,128)(2,1)} %copy-done.4) | copy-start | bytes 1179652
  48.6 18.6 %copy-start.7 = (bf16[256,768]{1,0:T(8,128)(2,1)S(1)}, bf16[256,768]{1,0:T(8,128)(2,1)}, u32[]{:S(2)}) copy-start(bf16[256,768]{1,0:T(8,128)(2,1)} %copy-done.6) | copy-start | bytes 1179652
  48.6 11.1 %collective-permute-start.9 = (bf16[256,768]{1,0:T(8,128)(2,1)}, bf16[256,768]{1,0:T(8,128)(2,1)S(1)}, u32[]{:S(2)}, u32[]{:S(2)}) collective-permute-start(bf16[256,768]{1,0:T(8,128)(2,1)} %collective-permute-done.4.refs_10_), channel_id=1, source_target_pairs={{0,16},{1,17},{2,18},{3,19},{4,20},{5,21},{6,22},{7,23},{8,24},{9,... | collective-permute-start | bytes 1179656 | tf_op jit(solution)/shard_map/ppermute | solution.py:279
  49.8 12.3 %collective-permute-start.18 = (bf16[256,768]{1,0:T(8,128)(2,1)}, bf16[256,768]{1,0:T(8,128)(2,1)S(1)}, u32[]{:S(2)}, u32[]{:S(2)}) collective-permute-start(bf16[256,768]{1,0:T(8,128)(2,1)} %collective-permute-done.15), channel_id=1, source_target_pairs={{1,0},{2,3},{5,4},{6,7},{9,8},{10,11},{13,12},{14,15},{17,16},{18,... | collective-permute-start | bytes 1179656 | tf_op jit(solution)/shard_map/ppermute | solution.py:279
  54.9 11.1 %collective-permute-start.19 = (bf16[256,768]{1,0:T(8,128)(2,1)S(1)}, bf16[256,768]{1,0:T(8,128)(2,1)S(1)}, u32[]{:S(2)}, u32[]{:S(2)}) collective-permute-start(bf16[256,768]{1,0:T(8,128)(2,1)S(1)} %broadcast_select_fusion.2.refs_4_), channel_id=1, source_target_pairs={{0,16},{1,17},{2,18},{3,19},{4,20},{5,21},{6,22},{7,23},{8,24},{9,... | collective-permute-start | bytes 1179656 | tf_op jit(solution)/shard_map/ppermute | solution.py:279
  56.2 9.9 %collective-permute-start.20 = (bf16[256,768]{1,0:T(8,128)(2,1)}, bf16[256,768]{1,0:T(8,128)(2,1)S(1)}, u32[]{:S(2)}, u32[]{:S(2)}) collective-permute-start(bf16[256,768]{1,0:T(8,128)(2,1)} %collective-permute-done.17.refs_7_), channel_id=1, source_target_pairs={{1,2},{2,1},{5,6},{6,5},{9,10},{10,9},{13,14},{14,13},{17,18},{18,... | collective-permute-start | bytes 1179656 | tf_op jit(solution)/shard_map/ppermute | solution.py:279
  59.7 12.4 %collective-permute-start.10 = (bf16[256,768]{1,0:T(8,128)(2,1)}, bf16[256,768]{1,0:T(8,128)(2,1)S(1)}, u32[]{:S(2)}, u32[]{:S(2)}) collective-permute-start(bf16[256,768]{1,0:T(8,128)(2,1)} %collective-permute-done.7), channel_id=1, source_target_pairs={{1,0},{2,3},{5,4},{6,7},{9,8},{10,11},{13,12},{14,15},{17,16},{18,... | collective-permute-start | bytes 1179656 | tf_op jit(solution)/shard_map/ppermute | solution.py:279
  62.1 12.4 %collective-permute-start.11 = (bf16[256,768]{1,0:T(8,128)(2,1)S(1)}, bf16[256,768]{1,0:T(8,128)(2,1)S(1)}, u32[]{:S(2)}, u32[]{:S(2)}) collective-permute-start(bf16[256,768]{1,0:T(8,128)(2,1)S(1)} %broadcast_select_fusion.3.refs_11_), channel_id=1, source_target_pairs={{0,16},{1,17},{2,18},{3,19},{4,20},{5,21},{6,22},{7,23},{8,24},{9,... | collective-permute-start | bytes 1179656 | tf_op jit(solution)/shard_map/ppermute | solution.py:279
  74.5 11.5 %collective-permute-start.24 = (bf16[256,4096]{1,0:T(8,128)(2,1)}, bf16[256,4096]{1,0:T(8,128)(2,1)S(1)}, u32[]{:S(2)}, u32[]{:S(2)}) collective-permute-start(bf16[256,4096]{1,0:T(8,128)(2,1)} %collective-permute-done.21.refs_0_), channel_id=1, source_target_pairs={{0,4},{1,5},{2,6},{3,7},{4,0},{5,1},{6,2},{7,3},{8,12},{9,13},{10,... | collective-permute-start | bytes 6291464 | tf_op jit(solution)/shard_map/ppermute | solution.py:279
  80.8 10.1 %collective-permute-start.22 = (bf16[256,256]{1,0:T(8,128)(2,1)S(1)}, bf16[256,256]{1,0:T(8,128)(2,1)S(1)}, u32[]{:S(2)}, u32[]{:S(2)}) collective-permute-start(bf16[256,256]{1,0:T(8,128)(2,1)S(1)} %slice.28), channel_id=1, source_target_pairs={{1,0},{2,3},{5,4},{6,7},{9,8},{10,11},{13,12},{14,15},{17,16},{18,... | collective-permute-start | bytes 393224 | tf_op jit(solution)/shard_map/ppermute | solution.py:279
  82.1 13.2 %collective-permute-start.26 = (bf16[256,512]{1,0:T(8,128)(2,1)S(1)}, bf16[256,512]{1,0:T(8,128)(2,1)S(1)}, u32[]{:S(2)}, u32[]{:S(2)}) collective-permute-start(bf16[256,512]{1,0:T(8,128)(2,1)S(1)} %slice.30), channel_id=1, source_target_pairs={{1,0},{2,3},{5,4},{6,7},{9,8},{10,11},{13,12},{14,15},{17,16},{18,... | collective-permute-start | bytes 786440 | tf_op jit(solution)/shard_map/ppermute | solution.py:279
  84.5 6.4 %copy-start = (bf16[144,768]{1,0:T(8,128)(2,1)S(1)}, bf16[144,768]{1,0:T(8,128)(2,1)}, u32[]{:S(2)}) copy-start(bf16[144,768]{1,0:T(8,128)(2,1)} %get-tuple-element.80.refs_13_.refs_8_.refs_5_) | copy-start | bytes 663556
  84.5 6.4 %collective-permute-start.23 = (bf16[256,256]{1,0:T(8,128)(2,1)S(1)}, bf16[256,256]{1,0:T(8,128)(2,1)S(1)}, u32[]{:S(2)}, u32[]{:S(2)}) collective-permute-start(bf16[256,256]{1,0:T(8,128)(2,1)S(1)} %slice.35), channel_id=1, source_target_pairs={{0,16},{1,17},{2,18},{3,19},{4,20},{5,21},{6,22},{7,23},{8,24},{9,... | collective-permute-start | bytes 393224 | tf_op jit(solution)/shard_map/ppermute | solution.py:279
  85.9 9.5 %collective-permute-start.27 = (bf16[256,512]{1,0:T(8,128)(2,1)S(1)}, bf16[256,512]{1,0:T(8,128)(2,1)S(1)}, u32[]{:S(2)}, u32[]{:S(2)}) collective-permute-start(bf16[256,512]{1,0:T(8,128)(2,1)S(1)} %slice.36), channel_id=1, source_target_pairs={{0,16},{1,17},{2,18},{3,19},{4,20},{5,21},{6,22},{7,23},{8,24},{9,... | collective-permute-start | bytes 786440 | tf_op jit(solution)/shard_map/ppermute | solution.py:279
  92.7 4.2 %collective-permute-start.25 = (bf16[128,256]{1,0:T(8,128)(2,1)S(1)}, bf16[128,256]{1,0:T(8,128)(2,1)S(1)}, u32[]{:S(2)}, u32[]{:S(2)}) collective-permute-start(bf16[128,256]{1,0:T(8,128)(2,1)S(1)} %get-tuple-element.119), channel_id=1, source_target_pairs={{0,16},{1,17},{2,18},{3,19},{4,20},{5,21},{6,22},{7,23},{8,24},{9,... | collective-permute-start | bytes 196616 | tf_op jit(solution)/shard_map/ppermute | solution.py:279
  95.3 1.6 %copy-start.2 = (f32[16]{0:T(128)S(1)}, f32[16]{0:T(128)}, u32[]{:S(2)}) copy-start(f32[16]{0:T(128)} %gate_ref.7) | copy-start | bytes 196
  97.9 13.4 %collective-permute-start.28 = (bf16[256,256]{1,0:T(8,128)(2,1)S(1)}, bf16[256,256]{1,0:T(8,128)(2,1)S(1)}, u32[]{:S(2)}, u32[]{:S(2)}) collective-permute-start(bf16[256,256]{1,0:T(8,128)(2,1)S(1)} %shard_map.78), channel_id=1, source_target_pairs={{0,8},{1,9},{2,10},{3,11},{4,12},{5,13},{6,14},{7,15},{8,0},{9,1},... | collective-permute-start | bytes 393224 | tf_op jit(solution)/shard_map/ppermute | solution.py:279
  99.2 12.2 %collective-permute-start.30 = (bf16[256,256]{1,0:T(8,128)(2,1)S(1)}, bf16[256,256]{1,0:T(8,128)(2,1)S(1)}, u32[]{:S(2)}, u32[]{:S(2)}) collective-permute-start(bf16[256,256]{1,0:T(8,128)(2,1)S(1)} %shard_map.79), channel_id=1, source_target_pairs={{0,12},{1,13},{2,14},{3,15},{4,8},{5,9},{6,10},{7,11},{8,4},{9,5},... | collective-permute-start | bytes 393224 | tf_op jit(solution)/shard_map/ppermute | solution.py:279
  104.6 6.9 %collective-permute-start.29 = (bf16[256,256]{1,0:T(8,128)(2,1)S(1)}, bf16[256,256]{1,0:T(8,128)(2,1)S(1)}, u32[]{:S(2)}, u32[]{:S(2)}) collective-permute-start(bf16[256,256]{1,0:T(8,128)(2,1)S(1)} %get-tuple-element.137), channel_id=1, source_target_pairs={{0,8},{1,9},{2,10},{3,11},{4,12},{5,13},{6,14},{7,15},{8,0},{9,1},... | collective-permute-start | bytes 393224 | tf_op jit(solution)/shard_map/ppermute | solution.py:279
  104.9 7.4 %collective-permute-start.31 = (bf16[256,256]{1,0:T(8,128)(2,1)S(1)}, bf16[256,256]{1,0:T(8,128)(2,1)S(1)}, u32[]{:S(2)}, u32[]{:S(2)}) collective-permute-start(bf16[256,256]{1,0:T(8,128)(2,1)S(1)} %get-tuple-element.138), channel_id=1, source_target_pairs={{0,12},{1,13},{2,14},{3,15},{4,8},{5,9},{6,10},{7,11},{8,4},{9,5},... | collective-permute-start | bytes 393224 | tf_op jit(solution)/shard_map/ppermute | solution.py:279
  110.2 2.1 %collective-permute-start.32 = (bf16[256,256]{1,0:T(8,128)(2,1)S(1)}, bf16[256,256]{1,0:T(8,128)(2,1)S(1)}, u32[]{:S(2)}, u32[]{:S(2)}) collective-permute-start(bf16[256,256]{1,0:T(8,128)(2,1)S(1)} %get-tuple-element.153), channel_id=1, source_target_pairs={{0,4},{1,5},{2,6},{3,7},{4,0},{5,1},{6,2},{7,3},{8,12},{9,13},{10,... | collective-permute-start | bytes 393224 | tf_op jit(solution)/shard_map/ppermute | solution.py:279
  111.3 1.3 %collective-permute-start.33 = (bf16[256,256]{1,0:T(8,128)(2,1)S(1)}, bf16[256,256]{1,0:T(8,128)(2,1)S(1)}, u32[]{:S(2)}, u32[]{:S(2)}) collective-permute-start(bf16[256,256]{1,0:T(8,128)(2,1)S(1)} %get-tuple-element.154), channel_id=1, source_target_pairs={{0,4},{1,5},{2,6},{3,7},{4,0},{5,1},{6,2},{7,3},{8,12},{9,13},{10,... | collective-permute-start | bytes 393224 | tf_op jit(solution)/shard_map/ppermute | solution.py:279

commit v20 on v17

--- a/solution.py
+++ b/solution.py
@@ -20,7 +20,7 @@
 HBM = pl.BlockSpec(memory_space=pltpu.HBM)
 
 
-def call(body, outs, in_specs, flops=0, scratch=(), out_spec=VMEM, limit=16 << 20, moved=4 << 20):
+def call(body, outs, in_specs, flops=0, scratch=(), out_spec=VMEM, limit=12 << 20, moved=4 << 20):
     return pl.pallas_call(
         body,
         out_shape=outs,

time: 114 us -> 114 us (level)
  no operation moved by 1% of the time
where the time goes in v20:
time: 114 us
  starting transfers between devices  52.4 us (46%)
  waiting for transfers between devices  27.1 us (24%)
  Pallas kernels  25.7 us (23%)
  other arithmetic  4.87 us (4%)
  local copies, waits for them, and re-layouts  2.56 us (2%)
    ppermute x34, starting transfers between devices, permute(): return lax.ppermute(array, AXES, pairs)  52.4 us
    ppermute x34, waiting for transfers between devices, permute(): return lax.ppermute(array, AXES, pairs)  27.1 us
    pallas_call x2, Pallas kernels, project(): call(functools.partial(project_body, early, late, line), [shape((length,...  9.75 us
    pallas_call x4, Pallas kernels, local(): call(functools.partial(local_body, len(segs), len(late) + 1, halves[1 + p...  6.49 us
    pallas_call x3, Pallas kernels, mix(): call(functools.partial(mix_body, segs, parts, group), [shape((length, hal...  3.96 us
  transfers between devices with their start and end apart: 34, of which 10 were waited for; matrix products, arithmetic and copies ran while one was open for 5% of the time, Pallas kernels for 20%

profile of v20, /device:TPU:9, one launch (start us, length us, event | category | flops | bytes accessed | tf_op | source)
XLA Modules:
  0.0 113.7 jit_solution(9061346522510404692)
XLA Ops:
  0.0 0.7 collective-permute-start.3
  1.3 0.6 pad_add_fusion.here_ref
  1.9 2.1 %shard_map.73 = (bf16[144,768]{1,0:T(8,128)(2,1)}, bf16[144,768]{1,0:T(8,128)(2,1)}, bf16[144,768]{1,0:T(8,128)(2,1)}, bf16[144,768]{1,0:T(8,128)(2,1)}) custom-call(s32[4]{0:T(128)} %pad_add_fusion.here_ref, s32[1,1]{1,0:T(1,128)S(6)} %copy.8.valid_ref, s32[1,1,2,2]{3,2,1,0:T(2,128)} %mask_ref.1, bf16[128,2048]{1,0:T(8,128)(2,1)} %wq_ref.1, ...), custom_call_target="tpu_custom_call" | custom-call | bytes 4194304 | tf_op jit(solution)/shard_map/pallas_call | solution.py:285
  4.1 0.2 collective-permute-start
  4.2 1.5 %collective-permute-start.2 = (bf16[144,768]{1,0:T(8,128)(2,1)}, bf16[144,768]{1,0:T(8,128)(2,1)S(1)}, u32[]{:S(2)}, u32[]{:S(2)}) collective-permute-start(bf16[144,768]{1,0:T(8,128)(2,1)} %get-tuple-element.84), channel_id=1, source_target_pairs={{0,12},{1,13},{2,14},{3,15},{4,8},{5,9},{6,10},{7,11},{8,4},{9,5},... | collective-permute-start | bytes 663560 | tf_op jit(solution)/shard_map/ppermute | solution.py:279
  5.7 0.3 collective-permute-start.1
  5.9 0.9 slice.24
  6.9 5.3 %collective-permute-done.2.refs_16_.refs_8_.refs_5_ = bf16[144,768]{1,0:T(8,128)(2,1)S(1)} collective-permute-done((bf16[144,768]{1,0:T(8,128)(2,1)}, bf16[144,768]{1,0:T(8,128)(2,1)S(1)}, u32[]{:S(2)}, u32[]{:S(2)}) %collective-permute-start.2) | collective-permute-done | bytes 221216 | tf_op jit(solution)/shard_map/ppermute | solution.py:279
  12.2 4.4 %collective-permute-done.1.refs_15_.refs_7_.refs_4_ = bf16[144,768]{1,0:T(8,128)(2,1)S(1)} collective-permute-done((bf16[144,768]{1,0:T(8,128)(2,1)}, bf16[144,768]{1,0:T(8,128)(2,1)S(1)}, u32[]{:S(2)}, u32[]{:S(2)}) %collective-permute-start.1) | collective-permute-done | bytes 221216 | tf_op jit(solution)/shard_map/ppermute | solution.py:279
  16.6 0.0 collective-permute-done.3.refs_1_
  16.6 0.1 collective-permute-start.12
  16.7 1.4 %collective-permute-start.21 = (bf16[256,4096]{1,0:T(8,128)(2,1)S(1)}, bf16[256,4096]{1,0:T(8,128)(2,1)}, u32[]{:S(2)}, u32[]{:S(2)}) collective-permute-start(bf16[256,4096]{1,0:T(8,128)(2,1)S(1)} %bitcast.6), channel_id=1, source_target_pairs={{0,8},{1,9},{2,10},{3,11},{4,12},{5,13},{6,14},{7,15},{8,0},{9,1},... | collective-permute-start | bytes 6291464 | tf_op jit(solution)/shard_map/ppermute | solution.py:279
  18.1 4.3 %collective-permute-start.13 = (bf16[256,768]{1,0:T(8,128)(2,1)S(1)}, bf16[256,768]{1,0:T(8,128)(2,1)}, u32[]{:S(2)}, u32[]{:S(2)}) collective-permute-start(bf16[256,768]{1,0:T(8,128)(2,1)S(1)} %pad_maximum_fusion.refs_2_), channel_id=1, source_target_pairs={{1,2},{2,1},{5,6},{6,5},{9,10},{10,9},{13,14},{14,13},{17,18},{18,... | collective-permute-start | bytes 1179656 | tf_op jit(solution)/shard_map/ppermute | solution.py:279
  22.4 1.3 %collective-permute-start.14 = (bf16[256,768]{1,0:T(8,128)(2,1)S(1)}, bf16[256,768]{1,0:T(8,128)(2,1)S(1)}, u32[]{:S(2)}, u32[]{:S(2)}) collective-permute-start(bf16[256,768]{1,0:T(8,128)(2,1)S(1)} %pad_maximum_fusion.refs_2_), channel_id=1, source_target_pairs={{0,16},{1,17},{2,18},{3,19},{4,20},{5,21},{6,22},{7,23},{8,24},{9,... | collective-permute-start | bytes 1179656 | tf_op jit(solution)/shard_map/ppermute | solution.py:279
  23.7 3.0 %collective-permute-done.12.refs_3_ = bf16[256,768]{1,0:T(8,128)(2,1)} collective-permute-done((bf16[256,768]{1,0:T(8,128)(2,1)S(1)}, bf16[256,768]{1,0:T(8,128)(2,1)}, u32[]{:S(2)}, u32[]{:S(2)}) %collective-permute-start.12) | collective-permute-done | bytes 393248 | tf_op jit(solution)/shard_map/ppermute | solution.py:279
  26.7 3.2 %collective-permute-start.5 = (bf16[256,768]{1,0:T(8,128)(2,1)S(1)}, bf16[256,768]{1,0:T(8,128)(2,1)}, u32[]{:S(2)}, u32[]{:S(2)}) collective-permute-start(bf16[256,768]{1,0:T(8,128)(2,1)S(1)} %pad_maximum_fusion.1.refs_9_), channel_id=1, source_target_pairs={{1,2},{2,1},{5,6},{6,5},{9,10},{10,9},{13,14},{14,13},{17,18},{18,... | collective-permute-start | bytes 1179656 | tf_op jit(solution)/shard_map/ppermute | solution.py:279
  29.9 0.7 collective-permute-done.13
  30.6 1.2 %collective-permute-start.6 = (bf16[256,768]{1,0:T(8,128)(2,1)S(1)}, bf16[256,768]{1,0:T(8,128)(2,1)S(1)}, u32[]{:S(2)}, u32[]{:S(2)}) collective-permute-start(bf16[256,768]{1,0:T(8,128)(2,1)S(1)} %pad_maximum_fusion.1.refs_9_), channel_id=1, source_target_pairs={{0,16},{1,17},{2,18},{3,19},{4,20},{5,21},{6,22},{7,23},{8,24},{9,... | collective-permute-start | bytes 1179656 | tf_op jit(solution)/shard_map/ppermute | solution.py:279
  31.9 0.7 copy-done.4
  32.6 3.1 %collective-permute-start.15 = (bf16[256,768]{1,0:T(8,128)(2,1)}, bf16[256,768]{1,0:T(8,128)(2,1)}, u32[]{:S(2)}, u32[]{:S(2)}) collective-permute-start(bf16[256,768]{1,0:T(8,128)(2,1)} %collective-permute-done.12.refs_3_), channel_id=1, source_target_pairs={{1,2},{2,1},{5,6},{6,5},{9,10},{10,9},{13,14},{14,13},{17,18},{18,... | collective-permute-start | bytes 1179656 | tf_op jit(solution)/shard_map/ppermute | solution.py:279
  35.7 2.5 %collective-permute-start.16 = (bf16[256,768]{1,0:T(8,128)(2,1)}, bf16[256,768]{1,0:T(8,128)(2,1)}, u32[]{:S(2)}, u32[]{:S(2)}) collective-permute-start(bf16[256,768]{1,0:T(8,128)(2,1)} %collective-permute-done.13), channel_id=1, source_target_pairs={{1,0},{2,3},{5,4},{6,7},{9,8},{10,11},{13,12},{14,15},{17,16},{18,... | collective-permute-start | bytes 1179656 | tf_op jit(solution)/shard_map/ppermute | solution.py:279
  38.2 1.1 collective-permute-start.17
  39.3 0.8 copy-done.6
  40.0 4.3 %collective-permute-start.7 = (bf16[256,768]{1,0:T(8,128)(2,1)}, bf16[256,768]{1,0:T(8,128)(2,1)}, u32[]{:S(2)}, u32[]{:S(2)}) collective-permute-start(bf16[256,768]{1,0:T(8,128)(2,1)} %collective-permute-done.4.refs_10_), channel_id=1, source_target_pairs={{1,2},{2,1},{5,6},{6,5},{9,10},{10,9},{13,14},{14,13},{17,18},{18,... | collective-permute-start | bytes 1179656 | tf_op jit(solution)/shard_map/ppermute | solution.py:279
  44.4 2.1 %collective-permute-done.15 = bf16[256,768]{1,0:T(8,128)(2,1)} collective-permute-done((bf16[256,768]{1,0:T(8,128)(2,1)}, bf16[256,768]{1,0:T(8,128)(2,1)}, u32[]{:S(2)}, u32[]{:S(2)}) %collective-permute-start.15) | collective-permute-done | bytes 393248 | tf_op jit(solution)/shard_map/ppermute | solution.py:279
  46.4 2.1 %collective-permute-start.8 = (bf16[256,768]{1,0:T(8,128)(2,1)}, bf16[256,768]{1,0:T(8,128)(2,1)}, u32[]{:S(2)}, u32[]{:S(2)}) collective-permute-start(bf16[256,768]{1,0:T(8,128)(2,1)} %collective-permute-done.5), channel_id=1, source_target_pairs={{1,0},{2,3},{5,4},{6,7},{9,8},{10,11},{13,12},{14,15},{17,16},{18,... | collective-permute-start | bytes 1179656 | tf_op jit(solution)/shard_map/ppermute | solution.py:279
  48.5 1.2 %collective-permute-start.9 = (bf16[256,768]{1,0:T(8,128)(2,1)}, bf16[256,768]{1,0:T(8,128)(2,1)S(1)}, u32[]{:S(2)}, u32[]{:S(2)}) collective-permute-start(bf16[256,768]{1,0:T(8,128)(2,1)} %collective-permute-done.4.refs_10_), channel_id=1, source_target_pairs={{0,16},{1,17},{2,18},{3,19},{4,20},{5,21},{6,22},{7,23},{8,24},{9,... | collective-permute-start | bytes 1179656 | tf_op jit(solution)/shard_map/ppermute | solution.py:279
  49.8 1.3 %collective-permute-start.18 = (bf16[256,768]{1,0:T(8,128)(2,1)}, bf16[256,768]{1,0:T(8,128)(2,1)S(1)}, u32[]{:S(2)}, u32[]{:S(2)}) collective-permute-start(bf16[256,768]{1,0:T(8,128)(2,1)} %collective-permute-done.15), channel_id=1, source_target_pairs={{1,0},{2,3},{5,4},{6,7},{9,8},{10,11},{13,12},{14,15},{17,16},{18,... | collective-permute-start | bytes 1179656 | tf_op jit(solution)/shard_map/ppermute | solution.py:279
  51.1 1.1 broadcast_select_fusion.2.refs_4_
  52.1 2.8 %collective-permute-done.7 = bf16[256,768]{1,0:T(8,128)(2,1)} collective-permute-done((bf16[256,768]{1,0:T(8,128)(2,1)}, bf16[256,768]{1,0:T(8,128)(2,1)}, u32[]{:S(2)}, u32[]{:S(2)}) %collective-permute-start.7) | collective-permute-done | bytes 393248 | tf_op jit(solution)/shard_map/ppermute | solution.py:279
  54.9 1.2 %collective-permute-start.19 = (bf16[256,768]{1,0:T(8,128)(2,1)S(1)}, bf16[256,768]{1,0:T(8,128)(2,1)S(1)}, u32[]{:S(2)}, u32[]{:S(2)}) collective-permute-start(bf16[256,768]{1,0:T(8,128)(2,1)S(1)} %broadcast_select_fusion.2.refs_4_), channel_id=1, source_target_pairs={{0,16},{1,17},{2,18},{3,19},{4,20},{5,21},{6,22},{7,23},{8,24},{9,... | collective-permute-start | bytes 1179656 | tf_op jit(solution)/shard_map/ppermute | solution.py:279
  56.1 3.5 %collective-permute-start.20 = (bf16[256,768]{1,0:T(8,128)(2,1)}, bf16[256,768]{1,0:T(8,128)(2,1)S(1)}, u32[]{:S(2)}, u32[]{:S(2)}) collective-permute-start(bf16[256,768]{1,0:T(8,128)(2,1)} %collective-permute-done.17.refs_7_), channel_id=1, source_target_pairs={{1,2},{2,1},{5,6},{6,5},{9,10},{10,9},{13,14},{14,13},{17,18},{18,... | collective-permute-start | bytes 1179656 | tf_op jit(solution)/shard_map/ppermute | solution.py:279
  59.6 1.3 %collective-permute-start.10 = (bf16[256,768]{1,0:T(8,128)(2,1)}, bf16[256,768]{1,0:T(8,128)(2,1)S(1)}, u32[]{:S(2)}, u32[]{:S(2)}) collective-permute-start(bf16[256,768]{1,0:T(8,128)(2,1)} %collective-permute-done.7), channel_id=1, source_target_pairs={{1,0},{2,3},{5,4},{6,7},{9,8},{10,11},{13,12},{14,15},{17,16},{18,... | collective-permute-start | bytes 1179656 | tf_op jit(solution)/shard_map/ppermute | solution.py:279
  61.0 1.1 broadcast_select_fusion.3.refs_11_
  62.0 0.3 collective-permute-start.11
  62.3 3.7 %collective-permute-done.19.refs_8_ = bf16[256,768]{1,0:T(8,128)(2,1)S(1)} collective-permute-done((bf16[256,768]{1,0:T(8,128)(2,1)S(1)}, bf16[256,768]{1,0:T(8,128)(2,1)S(1)}, u32[]{:S(2)}, u32[]{:S(2)}) %collective-permute-start.19) | collective-permute-done | bytes 393248 | tf_op jit(solution)/shard_map/ppermute | solution.py:279
  66.0 1.1 broadcast_select_fusion.1.refs_5_
  67.1 4.9 %shard_map.74 = (f32[256,768]{1,0:T(8,128)S(1)}, f32[256,768]{1,0:T(8,128)S(1)}, bf16[256,1024]{1,0:T(8,128)(2,1)S(1)}, bf16[256,1024]{1,0:T(8,128)(2,1)S(1)}) custom-call(s32[4]{0:T(128)S(1)} %copy-done.1, bf16[256,4096]{1,0:T(8,128)(2,1)S(1)} %bitcast.7, bf16[256,4096]{1,0:T(8,128)(2,1)} %collective-permute-done.3.refs_1_, ...), custom_call_target="tpu_custom_call" | custom-call | flops 2415919104 | bytes 4194304 | tf_op jit(solution)/shard_map/pallas_call | solution.py:317
  72.0 2.4 %collective-permute-done.11.refs_1_ = bf16[256,768]{1,0:T(8,128)(2,1)S(1)} collective-permute-done((bf16[256,768]{1,0:T(8,128)(2,1)S(1)}, bf16[256,768]{1,0:T(8,128)(2,1)S(1)}, u32[]{:S(2)}, u32[]{:S(2)}) %collective-permute-start.11) | collective-permute-done | bytes 393248 | tf_op jit(solution)/shard_map/ppermute | solution.py:279
  74.4 6.2 %collective-permute-start.24 = (bf16[256,4096]{1,0:T(8,128)(2,1)}, bf16[256,4096]{1,0:T(8,128)(2,1)S(1)}, u32[]{:S(2)}, u32[]{:S(2)}) collective-permute-start(bf16[256,4096]{1,0:T(8,128)(2,1)} %collective-permute-done.21.refs_0_), channel_id=1, source_target_pairs={{0,4},{1,5},{2,6},{3,7},{4,0},{5,1},{6,2},{7,3},{8,12},{9,13},{10,... | collective-permute-start | bytes 6291464 | tf_op jit(solution)/shard_map/ppermute | solution.py:279
  80.7 1.3 %collective-permute-start.22 = (bf16[256,256]{1,0:T(8,128)(2,1)S(1)}, bf16[256,256]{1,0:T(8,128)(2,1)S(1)}, u32[]{:S(2)}, u32[]{:S(2)}) collective-permute-start(bf16[256,256]{1,0:T(8,128)(2,1)S(1)} %slice.28), channel_id=1, source_target_pairs={{1,0},{2,3},{5,4},{6,7},{9,8},{10,11},{13,12},{14,15},{17,16},{18,... | collective-permute-start | bytes 393224 | tf_op jit(solution)/shard_map/ppermute | solution.py:279
  82.0 1.3 %collective-permute-start.26 = (bf16[256,512]{1,0:T(8,128)(2,1)S(1)}, bf16[256,512]{1,0:T(8,128)(2,1)S(1)}, u32[]{:S(2)}, u32[]{:S(2)}) collective-permute-start(bf16[256,512]{1,0:T(8,128)(2,1)S(1)} %slice.30), channel_id=1, source_target_pairs={{1,0},{2,3},{5,4},{6,7},{9,8},{10,11},{13,12},{14,15},{17,16},{18,... | collective-permute-start | bytes 786440 | tf_op jit(solution)/shard_map/ppermute | solution.py:279
  83.3 1.1 broadcast_select_fusion.refs_0_
  84.4 1.3 %collective-permute-start.23 = (bf16[256,256]{1,0:T(8,128)(2,1)S(1)}, bf16[256,256]{1,0:T(8,128)(2,1)S(1)}, u32[]{:S(2)}, u32[]{:S(2)}) collective-permute-start(bf16[256,256]{1,0:T(8,128)(2,1)S(1)} %slice.35), channel_id=1, source_target_pairs={{0,16},{1,17},{2,18},{3,19},{4,20},{5,21},{6,22},{7,23},{8,24},{9,... | collective-permute-start | bytes 393224 | tf_op jit(solution)/shard_map/ppermute | solution.py:279
  85.8 0.2 collective-permute-start.27
  86.0 4.9 %shard_map.75 = (f32[256,768]{1,0:T(8,128)S(1)}, f32[256,768]{1,0:T(8,128)S(1)}, bf16[256,1024]{1,0:T(8,128)(2,1)S(1)}, bf16[256,1024]{1,0:T(8,128)(2,1)S(1)}) custom-call(s32[4]{0:T(128)S(1)} %copy-done.1, bf16[256,4096]{1,0:T(8,128)(2,1)} %collective-permute-done.21.refs_0_, bf16[256,4096]{1,0:T(8,128)(2,1)S(1)} %collective-permute-done.24.refs_1_, ...), custom_call_target="tpu_custom_call" | custom-call | flops 2415919104 | bytes 4194304 | tf_op jit(solution)/shard_map/pallas_call | solution.py:317
  90.9 1.7 %shard_map.76 = (bf16[256,256]{1,0:T(8,128)(2,1)S(1)}, f32[128,256]{1,0:T(8,128)S(1)}, bf16[256,256]{1,0:T(8,128)(2,1)S(1)}, f32[128,256]{1,0:T(8,128)S(1)}, bf1...) custom-call(s32[4]{0:T(128)S(1)} %copy-done.1, ...), custom_call_target="tpu_custom_call" | custom-call | flops 536870912 | bytes 4194304 | tf_op jit(solution)/shard_map/pallas_call | solution.py:390
  92.6 1.3 %collective-permute-start.25 = (bf16[128,256]{1,0:T(8,128)(2,1)S(1)}, bf16[128,256]{1,0:T(8,128)(2,1)S(1)}, u32[]{:S(2)}, u32[]{:S(2)}) collective-permute-start(bf16[128,256]{1,0:T(8,128)(2,1)S(1)} %get-tuple-element.120), channel_id=1, source_target_pairs={{0,16},{1,17},{2,18},{3,19},{4,20},{5,21},{6,22},{7,23},{8,24},{9,... | collective-permute-start | bytes 196616 | tf_op jit(solution)/shard_map/ppermute | solution.py:279
  93.9 1.3 %collective-permute-done.27.refs_4_ = bf16[256,512]{1,0:T(8,128)(2,1)S(1)} collective-permute-done((bf16[256,512]{1,0:T(8,128)(2,1)S(1)}, bf16[256,512]{1,0:T(8,128)(2,1)S(1)}, u32[]{:S(2)}, u32[]{:S(2)}) %collective-permute-start.27) | collective-permute-done | bytes 262176 | tf_op jit(solution)/shard_map/ppermute | solution.py:279
  95.2 1.6 %shard_map.77 = (bf16[256,256]{1,0:T(8,128)(2,1)S(1)}, f32[256,256]{1,0:T(8,128)S(1)}, bf16[256,256]{1,0:T(8,128)(2,1)S(1)}, f32[256,256]{1,0:T(8,128)S(1)}) custom-call(s32[4]{0:T(128)S(1)} %copy-done.1, bf16[256,768]{1,0:T(8,128)(2,1)S(1)} %broadcast_select_fusion.refs_0_, bf16[256,768]{1,0:T(8,128)(2,1)S(1)} %collective-permute-done.11.refs_1_, ...), custom_call_target="tpu_custom_call" | custom-call | flops 134217728 | bytes 4194304 | tf_op jit(solution)/shard_map/pallas_call | solution.py:410
  96.8 1.2 %shard_map.78 = (bf16[256,256]{1,0:T(8,128)(2,1)S(1)}, bf16[256,256]{1,0:T(8,128)(2,1)S(1)}) custom-call(s32[4]{0:T(128)S(1)} %copy-done.1, f32[16]{0:T(128)S(1)} %copy-done.2, bf16[128,256]{1,0:T(8,128)(2,1)S(1)} %collective-permute-done.25.base_ref, f32[128,256]{1,0:T(8,128)S(1)} %get-tuple-element.126.refs_0_, f32[128,256]{1,0:T(8,128)S(1)} %get-tuple-element.127.refs_1_, ...), custom_call_target="tpu_custom_call" | custom-call | flops 201326592 | bytes 4194304 | tf_op jit(solution)/shard_map/pallas_call | solution.py:421
  98.0 0.3 collective-permute-start.28
  98.4 2.4 %collective-permute-start.30 = (bf16[256,256]{1,0:T(8,128)(2,1)S(1)}, bf16[256,256]{1,0:T(8,128)(2,1)S(1)}, u32[]{:S(2)}, u32[]{:S(2)}) collective-permute-start(bf16[256,256]{1,0:T(8,128)(2,1)S(1)} %get-tuple-element.133), channel_id=1, source_target_pairs={{0,12},{1,13},{2,14},{3,15},{4,8},{5,9},{6,10},{7,11},{8,4},{9,5},... | collective-permute-start | bytes 393224 | tf_op jit(solution)/shard_map/ppermute | solution.py:279
  100.7 1.8 %shard_map.79 = (bf16[256,256]{1,0:T(8,128)(2,1)S(1)}, f32[256,256]{1,0:T(8,128)S(1)}, bf16[256,256]{1,0:T(8,128)(2,1)S(1)}, f32[256,256]{1,0:T(8,128)S(1)}) custom-call(s32[4]{0:T(128)S(1)} %copy-done.1, bf16[256,768]{1,0:T(8,128)(2,1)S(1)} %broadcast_select_fusion.refs_0_, bf16[256,768]{1,0:T(8,128)(2,1)S(1)} %collective-permute-done.11.refs_1_, ...), custom_call_target="tpu_custom_call" | custom-call | flops 134217728 | bytes 4194304 | tf_op jit(solution)/shard_map/pallas_call | solution.py:410
  102.5 1.2 %shard_map.80 = (bf16[256,256]{1,0:T(8,128)(2,1)S(1)}, bf16[256,256]{1,0:T(8,128)(2,1)S(1)}) custom-call(s32[4]{0:T(128)S(1)} %copy-done.1, f32[16]{0:T(128)S(1)} %copy-done.2, bf16[128,256]{1,0:T(8,128)(2,1)S(1)} %collective-permute-done.25.base_ref, f32[128,256]{1,0:T(8,128)S(1)} %get-tuple-element.126.refs_0_, f32[128,256]{1,0:T(8,128)S(1)} %get-tuple-element.127.refs_1_, ...), custom_call_target="tpu_custom_call" | custom-call | flops 201326592 | bytes 4194304 | tf_op jit(solution)/shard_map/pallas_call | solution.py:421
  103.7 0.3 collective-permute-start.29
  104.0 0.6 collective-permute-start.31
  104.6 1.6 %shard_map.82 = (bf16[256,256]{1,0:T(8,128)(2,1)S(1)}, f32[256,256]{1,0:T(8,128)S(1)}, bf16[256,256]{1,0:T(8,128)(2,1)S(1)}, f32[256,256]{1,0:T(8,128)S(1)}) custom-call(s32[4]{0:T(128)S(1)} %copy-done.1, bf16[256,768]{1,0:T(8,128)(2,1)S(1)} %broadcast_select_fusion.refs_0_, bf16[256,768]{1,0:T(8,128)(2,1)S(1)} %collective-permute-done.11.refs_1_, ...), custom_call_target="tpu_custom_call" | custom-call | flops 134217728 | bytes 4194304 | tf_op jit(solution)/shard_map/pallas_call | solution.py:410
  106.2 1.6 %shard_map.83 = (bf16[256,256]{1,0:T(8,128)(2,1)S(1)}, f32[256,256]{1,0:T(8,128)S(1)}, bf16[256,256]{1,0:T(8,128)(2,1)S(1)}, f32[256,256]{1,0:T(8,128)S(1)}) custom-call(s32[4]{0:T(128)S(1)} %copy-done.1, bf16[256,768]{1,0:T(8,128)(2,1)S(1)} %broadcast_select_fusion.refs_0_, bf16[256,768]{1,0:T(8,128)(2,1)S(1)} %collective-permute-done.11.refs_1_, ...), custom_call_target="tpu_custom_call" | custom-call | flops 134217728 | bytes 4194304 | tf_op jit(solution)/shard_map/pallas_call | solution.py:410
  107.8 1.6 %shard_map.84 = (bf16[256,256]{1,0:T(8,128)(2,1)S(1)}, bf16[256,256]{1,0:T(8,128)(2,1)S(1)}, bf16[256,256]{1,0:T(8,128)(2,1)S(1)}, bf16[256,256]{1,0:T(8,128)(2,1)S(1)}) custom-call(s32[4]{0:T(128)S(1)} %copy-done.1, f32[16]{0:T(128)S(1)} %copy-done.2, bf16[128,256]{1,0:T(8,128)(2,1)S(1)} %collective-permute-done.25.base_ref, ...), custom_call_target="tpu_custom_call" | custom-call | flops 402653184 | bytes 4194304 | tf_op jit(solution)/shard_map/pallas_call | solution.py:421
  109.4 1.1 collective-permute-start.32
  110.5 0.1 collective-permute-start.33
  110.5 1.5 %collective-permute-done.31.refs_3_.refs_8_ = bf16[256,256]{1,0:T(8,128)(2,1)S(1)} collective-permute-done((bf16[256,256]{1,0:T(8,128)(2,1)S(1)}, bf16[256,256]{1,0:T(8,128)(2,1)S(1)}, u32[]{:S(2)}, u32[]{:S(2)}) %collective-permute-start.31) | collective-permute-done | bytes 131104 | tf_op jit(solution)/shard_map/ppermute | solution.py:279
  112.0 1.6 %shard_map.85 = bf16[256,2048]{1,0:T(8,128)(2,1)} custom-call(s32[4]{0:T(128)S(1)} %copy-done.1, f32[8,128]{1,0:T(8,128)S(1)} %shard_map.81.refs_0_, bf16[256,256]{1,0:T(8,128)(2,1)S(1)} %get-tuple-element.153.refs_1_, bf16[256,256]{1,0:T(8,128)(2,1)S(1)} %get-tuple-element.154.refs_2_, bf16[256,256]{1,0:T(8,128)(2,1)S(1)} %collective-permute-done.32.refs_3_, ...), custom_call_target="tpu_custom_call" | custom-call | bytes 4194304 | tf_op jit(solution)/shard_map/pallas_call | solution.py:444
  (48 shorter events, 0.2 us)
Async XLA Ops:
  0.0 16.7 %copy-start.3 = (bf16[1,256,4096]{2,1,0:T(8,128)(2,1)S(1)}, bf16[1,256,4096]{2,1,0:T(8,128)(2,1)}, u32[]{:S(2)}) copy-start(bf16[1,256,4096]{2,1,0:T(8,128)(2,1)} %param.7) | copy-start | bytes 6291460
  0.0 16.6 %collective-permute-start.3 = (bf16[256,4096]{1,0:T(8,128)(2,1)}, bf16[256,4096]{1,0:T(8,128)(2,1)}, u32[]{:S(2)}, u32[]{:S(2)}) collective-permute-start(bf16[256,4096]{1,0:T(8,128)(2,1)} %bitcast.5), channel_id=1, source_target_pairs={{0,4},{1,5},{2,6},{3,7},{4,0},{5,1},{6,2},{7,3},{8,12},{9,13},{10,... | collective-permute-start | bytes 6291464 | tf_op jit(solution)/shard_map/ppermute | solution.py:279
  4.1 2.8 %collective-permute-start = (bf16[144,768]{1,0:T(8,128)(2,1)}, bf16[144,768]{1,0:T(8,128)(2,1)S(1)}, u32[]{:S(2)}, u32[]{:S(2)}) collective-permute-start(bf16[144,768]{1,0:T(8,128)(2,1)} %get-tuple-element.82), channel_id=1, source_target_pairs={{0,4},{1,5},{2,6},{3,7},{4,0},{5,1},{6,2},{7,3},{8,12},{9,13},{10,... | collective-permute-start | bytes 663560 | tf_op jit(solution)/shard_map/ppermute | solution.py:279
  4.2 7.9 %collective-permute-start.2 = (bf16[144,768]{1,0:T(8,128)(2,1)}, bf16[144,768]{1,0:T(8,128)(2,1)S(1)}, u32[]{:S(2)}, u32[]{:S(2)}) collective-permute-start(bf16[144,768]{1,0:T(8,128)(2,1)} %get-tuple-element.84), channel_id=1, source_target_pairs={{0,12},{1,13},{2,14},{3,15},{4,8},{5,9},{6,10},{7,11},{8,4},{9,5},... | collective-permute-start | bytes 663560 | tf_op jit(solution)/shard_map/ppermute | solution.py:279
  5.7 10.9 %collective-permute-start.1 = (bf16[144,768]{1,0:T(8,128)(2,1)}, bf16[144,768]{1,0:T(8,128)(2,1)S(1)}, u32[]{:S(2)}, u32[]{:S(2)}) collective-permute-start(bf16[144,768]{1,0:T(8,128)(2,1)} %get-tuple-element.83), channel_id=1, source_target_pairs={{0,8},{1,9},{2,10},{3,11},{4,12},{5,13},{6,14},{7,15},{8,0},{9,1},... | collective-permute-start | bytes 663560 | tf_op jit(solution)/shard_map/ppermute | solution.py:279
  16.6 50.5 %copy-start.1 = (s32[4]{0:T(128)S(1)}, s32[4]{0:T(128)}, u32[]{:S(2)}) copy-start(s32[4]{0:T(128)} %pad_add_fusion.here_ref) | copy-start | bytes 52
  16.6 10.1 %collective-permute-start.12 = (bf16[256,768]{1,0:T(8,128)(2,1)S(1)}, bf16[256,768]{1,0:T(8,128)(2,1)}, u32[]{:S(2)}, u32[]{:S(2)}) collective-permute-start(bf16[256,768]{1,0:T(8,128)(2,1)S(1)} %pad_maximum_fusion.refs_2_), channel_id=1, source_target_pairs={{0,1},{1,0},{2,3},{3,2},{4,5},{5,4},{6,7},{7,6},{8,9},{9,8},{10,11... | collective-permute-start | bytes 1179656 | tf_op jit(solution)/shard_map/ppermute | solution.py:279
  16.7 55.3 %collective-permute-start.21 = (bf16[256,4096]{1,0:T(8,128)(2,1)S(1)}, bf16[256,4096]{1,0:T(8,128)(2,1)}, u32[]{:S(2)}, u32[]{:S(2)}) collective-permute-start(bf16[256,4096]{1,0:T(8,128)(2,1)S(1)} %bitcast.6), channel_id=1, source_target_pairs={{0,8},{1,9},{2,10},{3,11},{4,12},{5,13},{6,14},{7,15},{8,0},{9,1},... | collective-permute-start | bytes 6291464 | tf_op jit(solution)/shard_map/ppermute | solution.py:279
  18.1 12.6 %collective-permute-start.13 = (bf16[256,768]{1,0:T(8,128)(2,1)S(1)}, bf16[256,768]{1,0:T(8,128)(2,1)}, u32[]{:S(2)}, u32[]{:S(2)}) collective-permute-start(bf16[256,768]{1,0:T(8,128)(2,1)S(1)} %pad_maximum_fusion.refs_2_), channel_id=1, source_target_pairs={{1,2},{2,1},{5,6},{6,5},{9,10},{10,9},{13,14},{14,13},{17,18},{18,... | collective-permute-start | bytes 1179656 | tf_op jit(solution)/shard_map/ppermute | solution.py:279
  22.4 9.5 %collective-permute-start.14 = (bf16[256,768]{1,0:T(8,128)(2,1)S(1)}, bf16[256,768]{1,0:T(8,128)(2,1)S(1)}, u32[]{:S(2)}, u32[]{:S(2)}) collective-permute-start(bf16[256,768]{1,0:T(8,128)(2,1)S(1)} %pad_maximum_fusion.refs_2_), channel_id=1, source_target_pairs={{0,16},{1,17},{2,18},{3,19},{4,20},{5,21},{6,22},{7,23},{8,24},{9,... | collective-permute-start | bytes 1179656 | tf_op jit(solution)/shard_map/ppermute | solution.py:279
  23.7 12.0 %collective-permute-start.4 = (bf16[256,768]{1,0:T(8,128)(2,1)S(1)}, bf16[256,768]{1,0:T(8,128)(2,1)}, u32[]{:S(2)}, u32[]{:S(2)}) collective-permute-start(bf16[256,768]{1,0:T(8,128)(2,1)S(1)} %pad_maximum_fusion.1.refs_9_), channel_id=1, source_target_pairs={{0,1},{1,0},{2,3},{3,2},{4,5},{5,4},{6,7},{7,6},{8,9},{9,8},{10,11... | collective-permute-start | bytes 1179656 | tf_op jit(solution)/shard_map/ppermute | solution.py:279
  26.7 11.5 %collective-permute-start.5 = (bf16[256,768]{1,0:T(8,128)(2,1)S(1)}, bf16[256,768]{1,0:T(8,128)(2,1)}, u32[]{:S(2)}, u32[]{:S(2)}) collective-permute-start(bf16[256,768]{1,0:T(8,128)(2,1)S(1)} %pad_maximum_fusion.1.refs_9_), channel_id=1, source_target_pairs={{1,2},{2,1},{5,6},{6,5},{9,10},{10,9},{13,14},{14,13},{17,18},{18,... | collective-permute-start | bytes 1179656 | tf_op jit(solution)/shard_map/ppermute | solution.py:279
  30.6 8.6 %collective-permute-start.6 = (bf16[256,768]{1,0:T(8,128)(2,1)S(1)}, bf16[256,768]{1,0:T(8,128)(2,1)S(1)}, u32[]{:S(2)}, u32[]{:S(2)}) collective-permute-start(bf16[256,768]{1,0:T(8,128)(2,1)S(1)} %pad_maximum_fusion.1.refs_9_), channel_id=1, source_target_pairs={{0,16},{1,17},{2,18},{3,19},{4,20},{5,21},{6,22},{7,23},{8,24},{9,... | collective-permute-start | bytes 1179656 | tf_op jit(solution)/shard_map/ppermute | solution.py:279
  31.9 0.7 copy-start.4
  32.6 13.8 %collective-permute-start.15 = (bf16[256,768]{1,0:T(8,128)(2,1)}, bf16[256,768]{1,0:T(8,128)(2,1)}, u32[]{:S(2)}, u32[]{:S(2)}) collective-permute-start(bf16[256,768]{1,0:T(8,128)(2,1)} %collective-permute-done.12.refs_3_), channel_id=1, source_target_pairs={{1,2},{2,1},{5,6},{6,5},{9,10},{10,9},{13,14},{14,13},{17,18},{18,... | collective-permute-start | bytes 1179656 | tf_op jit(solution)/shard_map/ppermute | solution.py:279
  35.7 12.8 %collective-permute-start.16 = (bf16[256,768]{1,0:T(8,128)(2,1)}, bf16[256,768]{1,0:T(8,128)(2,1)}, u32[]{:S(2)}, u32[]{:S(2)}) collective-permute-start(bf16[256,768]{1,0:T(8,128)(2,1)} %collective-permute-done.13), channel_id=1, source_target_pairs={{1,0},{2,3},{5,4},{6,7},{9,8},{10,11},{13,12},{14,15},{17,16},{18,... | collective-permute-start | bytes 1179656 | tf_op jit(solution)/shard_map/ppermute | solution.py:279
  38.2 11.6 %collective-permute-start.17 = (bf16[256,768]{1,0:T(8,128)(2,1)}, bf16[256,768]{1,0:T(8,128)(2,1)}, u32[]{:S(2)}, u32[]{:S(2)}) collective-permute-start(bf16[256,768]{1,0:T(8,128)(2,1)} %collective-permute-done.12.refs_3_), channel_id=1, source_target_pairs={{0,16},{1,17},{2,18},{3,19},{4,20},{5,21},{6,22},{7,23},{8,24},{9,... | collective-permute-start | bytes 1179656 | tf_op jit(solution)/shard_map/ppermute | solution.py:279
  39.3 0.8 copy-start.6
  40.0 14.8 %collective-permute-start.7 = (bf16[256,768]{1,0:T(8,128)(2,1)}, bf16[256,768]{1,0:T(8,128)(2,1)}, u32[]{:S(2)}, u32[]{:S(2)}) collective-permute-start(bf16[256,768]{1,0:T(8,128)(2,1)} %collective-permute-done.4.refs_10_), channel_id=1, source_target_pairs={{1,2},{2,1},{5,6},{6,5},{9,10},{10,9},{13,14},{14,13},{17,18},{18,... | collective-permute-start | bytes 1179656 | tf_op jit(solution)/shard_map/ppermute | solution.py:279
  46.4 9.7 %collective-permute-start.8 = (bf16[256,768]{1,0:T(8,128)(2,1)}, bf16[256,768]{1,0:T(8,128)(2,1)}, u32[]{:S(2)}, u32[]{:S(2)}) collective-permute-start(bf16[256,768]{1,0:T(8,128)(2,1)} %collective-permute-done.5), channel_id=1, source_target_pairs={{1,0},{2,3},{5,4},{6,7},{9,8},{10,11},{13,12},{14,15},{17,16},{18,... | collective-permute-start | bytes 1179656 | tf_op jit(solution)/shard_map/ppermute | solution.py:279
  48.5 18.6 %copy-start.5 = (bf16[256,768]{1,0:T(8,128)(2,1)S(1)}, bf16[256,768]{1,0:T(8,128)(2,1)}, u32[]{:S(2)}) copy-start(bf16[256,768]{1,0:T(8,128)(2,1)} %copy-done.4) | copy-start | bytes 1179652
  48.5 18.6 %copy-start.7 = (bf16[256,768]{1,0:T(8,128)(2,1)S(1)}, bf16[256,768]{1,0:T(8,128)(2,1)}, u32[]{:S(2)}) copy-start(bf16[256,768]{1,0:T(8,128)(2,1)} %copy-done.6) | copy-start | bytes 1179652
  48.5 11.1 %collective-permute-start.9 = (bf16[256,768]{1,0:T(8,128)(2,1)}, bf16[256,768]{1,0:T(8,128)(2,1)S(1)}, u32[]{:S(2)}, u32[]{:S(2)}) collective-permute-start(bf16[256,768]{1,0:T(8,128)(2,1)} %collective-permute-done.4.refs_10_), channel_id=1, source_target_pairs={{0,16},{1,17},{2,18},{3,19},{4,20},{5,21},{6,22},{7,23},{8,24},{9,... | collective-permute-start | bytes 1179656 | tf_op jit(solution)/shard_map/ppermute | solution.py:279
  49.8 12.3 %collective-permute-start.18 = (bf16[256,768]{1,0:T(8,128)(2,1)}, bf16[256,768]{1,0:T(8,128)(2,1)S(1)}, u32[]{:S(2)}, u32[]{:S(2)}) collective-permute-start(bf16[256,768]{1,0:T(8,128)(2,1)} %collective-permute-done.15), channel_id=1, source_target_pairs={{1,0},{2,3},{5,4},{6,7},{9,8},{10,11},{13,12},{14,15},{17,16},{18,... | collective-permute-start | bytes 1179656 | tf_op jit(solution)/shard_map/ppermute | solution.py:279
  54.9 11.1 %collective-permute-start.19 = (bf16[256,768]{1,0:T(8,128)(2,1)S(1)}, bf16[256,768]{1,0:T(8,128)(2,1)S(1)}, u32[]{:S(2)}, u32[]{:S(2)}) collective-permute-start(bf16[256,768]{1,0:T(8,128)(2,1)S(1)} %broadcast_select_fusion.2.refs_4_), channel_id=1, source_target_pairs={{0,16},{1,17},{2,18},{3,19},{4,20},{5,21},{6,22},{7,23},{8,24},{9,... | collective-permute-start | bytes 1179656 | tf_op jit(solution)/shard_map/ppermute | solution.py:279
  56.1 9.9 %collective-permute-start.20 = (bf16[256,768]{1,0:T(8,128)(2,1)}, bf16[256,768]{1,0:T(8,128)(2,1)S(1)}, u32[]{:S(2)}, u32[]{:S(2)}) collective-permute-start(bf16[256,768]{1,0:T(8,128)(2,1)} %collective-permute-done.17.refs_7_), channel_id=1, source_target_pairs={{1,2},{2,1},{5,6},{6,5},{9,10},{10,9},{13,14},{14,13},{17,18},{18,... | collective-permute-start | bytes 1179656 | tf_op jit(solution)/shard_map/ppermute | solution.py:279
  59.6 12.4 %collective-permute-start.10 = (bf16[256,768]{1,0:T(8,128)(2,1)}, bf16[256,768]{1,0:T(8,128)(2,1)S(1)}, u32[]{:S(2)}, u32[]{:S(2)}) collective-permute-start(bf16[256,768]{1,0:T(8,128)(2,1)} %collective-permute-done.7), channel_id=1, source_target_pairs={{1,0},{2,3},{5,4},{6,7},{9,8},{10,11},{13,12},{14,15},{17,16},{18,... | collective-permute-start | bytes 1179656 | tf_op jit(solution)/shard_map/ppermute | solution.py:279
  62.0 12.4 %collective-permute-start.11 = (bf16[256,768]{1,0:T(8,128)(2,1)S(1)}, bf16[256,768]{1,0:T(8,128)(2,1)S(1)}, u32[]{:S(2)}, u32[]{:S(2)}) collective-permute-start(bf16[256,768]{1,0:T(8,128)(2,1)S(1)} %broadcast_select_fusion.3.refs_11_), channel_id=1, source_target_pairs={{0,16},{1,17},{2,18},{3,19},{4,20},{5,21},{6,22},{7,23},{8,24},{9,... | collective-permute-start | bytes 1179656 | tf_op jit(solution)/shard_map/ppermute | solution.py:279
  74.4 11.5 %collective-permute-start.24 = (bf16[256,4096]{1,0:T(8,128)(2,1)}, bf16[256,4096]{1,0:T(8,128)(2,1)S(1)}, u32[]{:S(2)}, u32[]{:S(2)}) collective-permute-start(bf16[256,4096]{1,0:T(8,128)(2,1)} %collective-permute-done.21.refs_0_), channel_id=1, source_target_pairs={{0,4},{1,5},{2,6},{3,7},{4,0},{5,1},{6,2},{7,3},{8,12},{9,13},{10,... | collective-permute-start | bytes 6291464 | tf_op jit(solution)/shard_map/ppermute | solution.py:279
  80.7 10.1 %collective-permute-start.22 = (bf16[256,256]{1,0:T(8,128)(2,1)S(1)}, bf16[256,256]{1,0:T(8,128)(2,1)S(1)}, u32[]{:S(2)}, u32[]{:S(2)}) collective-permute-start(bf16[256,256]{1,0:T(8,128)(2,1)S(1)} %slice.28), channel_id=1, source_target_pairs={{1,0},{2,3},{5,4},{6,7},{9,8},{10,11},{13,12},{14,15},{17,16},{18,... | collective-permute-start | bytes 393224 | tf_op jit(solution)/shard_map/ppermute | solution.py:279
  82.0 13.2 %collective-permute-start.26 = (bf16[256,512]{1,0:T(8,128)(2,1)S(1)}, bf16[256,512]{1,0:T(8,128)(2,1)S(1)}, u32[]{:S(2)}, u32[]{:S(2)}) collective-permute-start(bf16[256,512]{1,0:T(8,128)(2,1)S(1)} %slice.30), channel_id=1, source_target_pairs={{1,0},{2,3},{5,4},{6,7},{9,8},{10,11},{13,12},{14,15},{17,16},{18,... | collective-permute-start | bytes 786440 | tf_op jit(solution)/shard_map/ppermute | solution.py:279
  84.4 6.4 %copy-start = (bf16[144,768]{1,0:T(8,128)(2,1)S(1)}, bf16[144,768]{1,0:T(8,128)(2,1)}, u32[]{:S(2)}) copy-start(bf16[144,768]{1,0:T(8,128)(2,1)} %get-tuple-element.81.refs_13_.refs_8_.refs_5_) | copy-start | bytes 663556
  84.4 6.4 %collective-permute-start.23 = (bf16[256,256]{1,0:T(8,128)(2,1)S(1)}, bf16[256,256]{1,0:T(8,128)(2,1)S(1)}, u32[]{:S(2)}, u32[]{:S(2)}) collective-permute-start(bf16[256,256]{1,0:T(8,128)(2,1)S(1)} %slice.35), channel_id=1, source_target_pairs={{0,16},{1,17},{2,18},{3,19},{4,20},{5,21},{6,22},{7,23},{8,24},{9,... | collective-permute-start | bytes 393224 | tf_op jit(solution)/shard_map/ppermute | solution.py:279
  85.8 9.5 %collective-permute-start.27 = (bf16[256,512]{1,0:T(8,128)(2,1)S(1)}, bf16[256,512]{1,0:T(8,128)(2,1)S(1)}, u32[]{:S(2)}, u32[]{:S(2)}) collective-permute-start(bf16[256,512]{1,0:T(8,128)(2,1)S(1)} %slice.36), channel_id=1, source_target_pairs={{0,16},{1,17},{2,18},{3,19},{4,20},{5,21},{6,22},{7,23},{8,24},{9,... | collective-permute-start | bytes 786440 | tf_op jit(solution)/shard_map/ppermute | solution.py:279
  92.6 4.2 %collective-permute-start.25 = (bf16[128,256]{1,0:T(8,128)(2,1)S(1)}, bf16[128,256]{1,0:T(8,128)(2,1)S(1)}, u32[]{:S(2)}, u32[]{:S(2)}) collective-permute-start(bf16[128,256]{1,0:T(8,128)(2,1)S(1)} %get-tuple-element.120), channel_id=1, source_target_pairs={{0,16},{1,17},{2,18},{3,19},{4,20},{5,21},{6,22},{7,23},{8,24},{9,... | collective-permute-start | bytes 196616 | tf_op jit(solution)/shard_map/ppermute | solution.py:279
  95.2 1.6 %copy-start.2 = (f32[16]{0:T(128)S(1)}, f32[16]{0:T(128)}, u32[]{:S(2)}) copy-start(f32[16]{0:T(128)} %gate_ref.5) | copy-start | bytes 196
  98.0 12.4 %collective-permute-start.28 = (bf16[256,256]{1,0:T(8,128)(2,1)S(1)}, bf16[256,256]{1,0:T(8,128)(2,1)S(1)}, u32[]{:S(2)}, u32[]{:S(2)}) collective-permute-start(bf16[256,256]{1,0:T(8,128)(2,1)S(1)} %get-tuple-element.132), channel_id=1, source_target_pairs={{0,8},{1,9},{2,10},{3,11},{4,12},{5,13},{6,14},{7,15},{8,0},{9,1},... | collective-permute-start | bytes 393224 | tf_op jit(solution)/shard_map/ppermute | solution.py:279
  98.4 12.2 %collective-permute-start.30 = (bf16[256,256]{1,0:T(8,128)(2,1)S(1)}, bf16[256,256]{1,0:T(8,128)(2,1)S(1)}, u32[]{:S(2)}, u32[]{:S(2)}) collective-permute-start(bf16[256,256]{1,0:T(8,128)(2,1)S(1)} %get-tuple-element.133), channel_id=1, source_target_pairs={{0,12},{1,13},{2,14},{3,15},{4,8},{5,9},{6,10},{7,11},{8,4},{9,5},... | collective-permute-start | bytes 393224 | tf_op jit(solution)/shard_map/ppermute | solution.py:279
  103.7 6.9 %collective-permute-start.29 = (bf16[256,256]{1,0:T(8,128)(2,1)S(1)}, bf16[256,256]{1,0:T(8,128)(2,1)S(1)}, u32[]{:S(2)}, u32[]{:S(2)}) collective-permute-start(bf16[256,256]{1,0:T(8,128)(2,1)S(1)} %get-tuple-element.139), channel_id=1, source_target_pairs={{0,8},{1,9},{2,10},{3,11},{4,12},{5,13},{6,14},{7,15},{8,0},{9,1},... | collective-permute-start | bytes 393224 | tf_op jit(solution)/shard_map/ppermute | solution.py:279
  104.0 8.0 %collective-permute-start.31 = (bf16[256,256]{1,0:T(8,128)(2,1)S(1)}, bf16[256,256]{1,0:T(8,128)(2,1)S(1)}, u32[]{:S(2)}, u32[]{:S(2)}) collective-permute-start(bf16[256,256]{1,0:T(8,128)(2,1)S(1)} %get-tuple-element.140), channel_id=1, source_target_pairs={{0,12},{1,13},{2,14},{3,15},{4,8},{5,9},{6,10},{7,11},{8,4},{9,5},... | collective-permute-start | bytes 393224 | tf_op jit(solution)/shard_map/ppermute | solution.py:279
  109.4 2.7 %collective-permute-start.32 = (bf16[256,256]{1,0:T(8,128)(2,1)S(1)}, bf16[256,256]{1,0:T(8,128)(2,1)S(1)}, u32[]{:S(2)}, u32[]{:S(2)}) collective-permute-start(bf16[256,256]{1,0:T(8,128)(2,1)S(1)} %get-tuple-element.155), channel_id=1, source_target_pairs={{0,4},{1,5},{2,6},{3,7},{4,0},{5,1},{6,2},{7,3},{8,12},{9,13},{10,... | collective-permute-start | bytes 393224 | tf_op jit(solution)/shard_map/ppermute | solution.py:279
  110.5 1.6 %collective-permute-start.33 = (bf16[256,256]{1,0:T(8,128)(2,1)S(1)}, bf16[256,256]{1,0:T(8,128)(2,1)S(1)}, u32[]{:S(2)}, u32[]{:S(2)}) collective-permute-start(bf16[256,256]{1,0:T(8,128)(2,1)S(1)} %get-tuple-element.156), channel_id=1, source_target_pairs={{0,4},{1,5},{2,6},{3,7},{4,0},{5,1},{6,2},{7,3},{8,12},{9,13},{10,... | collective-permute-start | bytes 393224 | tf_op jit(solution)/shard_map/ppermute | solution.py:279
